TPU v7x, 32 devices: a whole 2x2x4 slice. The times are simulated.
32 devices in a mesh: ctx: 8 (over y, x, core), tp: 4 (over z).
Axes of the slice: x: 2, y: 2, z: 4, core: 2. Of those that a mesh axis runs over, the one named last changes fastest.
Arguments:
- tokens: bfloat16 [2048, 2048], P('ctx'), may hold values from -12 to 12
- feature_weight: bfloat16 [2048, 128], P(None, 'tp'), may hold values from -0.125 to 0.125
- window_weight: bfloat16 [2048, 1024], P(None, 'tp'), may hold values from -1 to 1
- value_weight: bfloat16 [2048, 512], P(None, 'tp'), may hold values from -0.125 to 0.125
- log_decay: float32 [2048, 4], P('ctx', 'tp'), may hold values from -1 to 0
- out_grad: bfloat16 [2048, 512], P('ctx', 'tp'), may hold values from -6 to 6
Outputs:
- attended: bfloat16 [2048, 512], P('ctx', 'tp')
- input_grad: bfloat16 [2048, 2048], P('ctx')
All inputs are finite; a program needn't handle non-finite values.
Results may differ from a plain program's by a relative error of at most 0.012.
The roundings to bfloat16 on the way count: a program that leaves them out, or rounds other values in their place, can miss the bound.
Values may be sent and summed in bfloat16 or wider, within the bound.
No kernel may reach another device: no remote copies, remote signals or barrier semaphores. Data moves between devices by JAX's collectives and lax.ppermute only.
A program may use at most 64 MiB of HBM per device.

v0:
```python
from functools import partial

import jax
import jax.numpy as jnp
from jax import lax
from jax.sharding import PartitionSpec as P

WINDOW = 1024


precise = lax.Precision.HIGHEST


def carried_in(part, axis, combine, identity):
    place = lax.axis_index(axis)
    gathered = jax.tree.map(lambda a: lax.all_gather(a, axis), part)
    state = jax.tree.map(lambda a, e: jnp.zeros_like(a) + jnp.asarray(e, a.dtype), part, identity)

    def one(step, state):
        return combine(
            state, jax.tree.map(lambda a: lax.dynamic_index_in_dim(a, step, 0, False), gathered)
        )

    return lax.fori_loop(0, place, one, state)


def shifted(value, axis, by):
    count = lax.axis_size(axis)
    pairs = [(i, i + by) for i in range(count) if 0 <= i + by < count]
    return lax.ppermute(value, axis, pairs)


def entering(value, axis, combine, identity):
    count, mine = (lax.axis_size(axis), lax.axis_index(axis))
    everything = jax.tree.map(
        lambda part, kind: lax.all_gather(part.astype(kind), axis),
        value,
        jax.tree.map(lambda a: jnp.bfloat16 if a.dtype == jnp.float32 else a.dtype, value),
    )
    start = jax.tree.map(
        lambda part, zero: jnp.broadcast_to(jnp.asarray(zero, part.dtype), part.shape),
        value,
        identity,
    )

    def step(k, before):
        at = count - 1 - k
        reached = at > mine
        new = combine(
            before, jax.tree.map(lambda part, own: part[at].astype(own.dtype), everything, value)
        )
        return jax.tree.map(lambda a, b: jnp.where(reached, a, b), new, before)

    return lax.fori_loop(0, count, step, start)


def feature_map(vectors):
    row_count = vectors.shape[0]
    feat_width = vectors.shape[1]
    square = (vectors[:, :, None] * vectors[:, None, :]).reshape(
        row_count, feat_width * feat_width
    ) * 0.5**0.5
    return jnp.concatenate([square, vectors, jnp.ones((row_count, 1), jnp.float32)], axis=1)


def linear_part(
    query_feat, query_cum, query_pos, key_feat, key_cum, key_pos, value_rows, state_num, state_den
):
    products = jnp.dot(query_feat, key_feat.T, precision=precise)
    kernel = 1.0 + products + 0.5 * products * products
    causal = key_pos[None, :] <= query_pos[:, None]
    decay_table = jnp.exp(jnp.where(causal, query_cum[:, None] - key_cum[None, :], -jnp.inf))
    weights = kernel * decay_table
    lifted = feature_map(query_feat)
    growth = jnp.exp(query_cum)
    numerator = jnp.dot(weights, value_rows, precision=precise) + growth[:, None] * jnp.dot(
        lifted, state_num, precision=precise
    )
    denominator = jnp.sum(weights, axis=1) + growth * jnp.dot(lifted, state_den, precision=precise)
    return numerator / denominator[:, None]


def window_part(queries, query_pos, key_rows, key_values, key_pos):
    head_dim = queries.shape[1]
    scores = jnp.dot(queries, key_rows.T, precision=precise) * head_dim ** (-0.5)
    allowed = (
        (key_pos[None, :] <= query_pos[:, None])
        & (query_pos[:, None] - key_pos[None, :] < WINDOW)
        & (key_pos[None, :] >= 0)
    )
    scores = jnp.where(allowed, scores, -jnp.inf)
    row_max = jnp.max(scores, axis=1, keepdims=True)
    exponent = jnp.exp(scores - row_max)
    return jnp.dot(exponent, key_values, precision=precise) / jnp.sum(
        exponent, axis=1, keepdims=True
    )


def combine_states(earlier, later):
    factor = jnp.exp(later[0])
    return (earlier[0] + later[0], factor * earlier[1] + later[1], factor * earlier[2] + later[2])


def local_state(feat_cols, val_cols, cumulative):
    feat_dim = feat_cols.shape[1] // 2
    key_feat = feat_cols[:, feat_dim:] * feat_dim ** (-0.25)
    tail_decay = jnp.exp(cumulative[-1] - cumulative)
    phi_keys = feature_map(key_feat) * tail_decay[:, None]
    return (jnp.dot(phi_keys.T, val_cols, precision=precise), jnp.sum(phi_keys, axis=0))


def local_output(
    feat_cols, win_cols, val_cols, halo_rows, state_num, state_den, cumulative, first_pos
):
    rows_here = feat_cols.shape[0]
    feat_dim = feat_cols.shape[1] // 2
    head_dim = val_cols.shape[1]
    feat_scale = feat_dim ** (-0.25)
    query_feat = feat_cols[:, :feat_dim] * feat_scale
    key_feat = feat_cols[:, feat_dim:] * feat_scale
    queries = win_cols[:, :head_dim]
    all_keys = jnp.concatenate([halo_rows[:, :head_dim], win_cols[:, head_dim:]], axis=0)
    all_values = jnp.concatenate([halo_rows[:, head_dim:], val_cols], axis=0)
    halo_span = halo_rows.shape[0]
    local_pos = jnp.arange(rows_here, dtype=jnp.int32)
    block_rows = min(rows_here, 512)
    linear = linear_part(
        query_feat,
        cumulative,
        local_pos,
        key_feat,
        cumulative,
        local_pos,
        val_cols,
        state_num,
        state_den,
    )
    key_pos = 0 - halo_span + jnp.arange(block_rows + halo_span, dtype=jnp.int32)
    windowed = window_part(
        queries, first_pos + local_pos, all_keys, all_values, first_pos + key_pos
    )
    pieces = [linear + windowed]
    return jnp.concatenate(pieces, axis=0)


def head_terms(grad_rows, feature_weight, window_weight, value_weight):
    return (
        jnp.dot(grad_rows[0], feature_weight.T, preferred_element_type=jnp.float32)
        + jnp.dot(grad_rows[1], window_weight.T, preferred_element_type=jnp.float32)
        + jnp.dot(grad_rows[2], value_weight.T, preferred_element_type=jnp.float32)
    )


def per_device(tokens, feature_weight, window_weight, value_weight, log_decay, out_grad):
    rows_here = tokens.shape[0]
    head_dim = value_weight.shape[1]
    features = jnp.dot(tokens, feature_weight, preferred_element_type=jnp.float32).astype(
        jnp.bfloat16
    )
    window = jnp.dot(tokens, window_weight, preferred_element_type=jnp.float32).astype(jnp.bfloat16)
    values = jnp.dot(tokens, value_weight, preferred_element_type=jnp.float32).astype(jnp.bfloat16)
    cumulative = jnp.cumsum(log_decay[:, 0])
    feat_cols = features.astype(jnp.float32)
    win_cols = window.astype(jnp.float32)
    val_cols = values.astype(jnp.float32)
    state_num, state_den = local_state(feat_cols, val_cols, cumulative)
    decay_total = cumulative[-1:]
    identity = (jnp.zeros((1,), jnp.float32), jnp.zeros_like(state_num), jnp.zeros_like(state_den))
    incoming = carried_in((decay_total, state_num, state_den), "ctx", combine_states, identity)
    pair_rows = jnp.concatenate([window[:, head_dim:], values], axis=1)
    blocks_back = WINDOW // rows_here
    fetched = [shifted(pair_rows, "ctx", distance) for distance in range(blocks_back, 0, -1)]
    halo_rows = jnp.concatenate(fetched, axis=0)
    first_pos = lax.axis_index("ctx") * rows_here
    output_fn = partial(local_output, cumulative=cumulative, first_pos=first_pos)
    result, pullback = jax.vjp(
        output_fn,
        feat_cols,
        win_cols,
        val_cols,
        halo_rows.astype(jnp.float32),
        incoming[1],
        incoming[2],
    )
    attended = result.astype(jnp.bfloat16)
    grad_feat, grad_win, grad_val, grad_halo, grad_num, grad_den = pullback(
        out_grad.astype(jnp.float32)
    )
    outgoing = entering((decay_total, grad_num, grad_den), "ctx", combine_states, identity)
    state_pull = jax.vjp(partial(local_state, cumulative=cumulative), feat_cols, val_cols)[1]
    more_feat, more_val = state_pull((outgoing[1], outgoing[2]))
    returned = jnp.zeros((rows_here, 2 * head_dim), jnp.float32)
    for distance in range(1, blocks_back + 1):
        offset = (blocks_back - distance) * rows_here
        returned = returned + shifted(grad_halo[offset : offset + rows_here], "ctx", -distance)
    grad_win = jnp.concatenate(
        [grad_win[:, :head_dim], grad_win[:, head_dim:] + returned[:, :head_dim]], axis=1
    )
    grad_val = grad_val + more_val + returned[:, head_dim:]
    grad_feat = grad_feat + more_feat
    grad_rows = (
        grad_feat.astype(jnp.bfloat16),
        grad_win.astype(jnp.bfloat16),
        grad_val.astype(jnp.bfloat16),
    )
    partial_sum = head_terms(grad_rows, feature_weight, window_weight, value_weight)
    input_grad = lax.psum(partial_sum, "tp").astype(jnp.bfloat16)
    return (attended, input_grad)


def solution(mesh):
    in_specs = (
        P("ctx", None),
        P(None, "tp"),
        P(None, "tp"),
        P(None, "tp"),
        P("ctx", "tp"),
        P("ctx", "tp"),
    )
    out_specs = (P("ctx", "tp"), P("ctx", None))
    return jax.shard_map(
        per_device, mesh=mesh, in_specs=in_specs, out_specs=out_specs, check_vma=False
    )
```

profile of v0, /device:TPU:0, one launch (start us, length us, event | category | flops | bytes accessed | tf_op | source)
XLA Modules:
  0.0 262.0 jit_solution(16762193563640875732)
XLA Ops:
  7.2 2.6 fusion.83
  11.0 4.9 %collective-permute-start = (bf16[256,256]{1,0:T(8,128)(2,1)S(1)}, bf16[256,256]{1,0:T(8,128)(2,1)S(1)}, u32[]{:S(2)}, u32[]{:S(2)}) collective-permute-start(bf16[256,256]{1,0:T(8,128)(2,1)S(1)} %pad_maximum_fusion.6), channel_id=1, source_target_pairs={{0,16},{4,20},{8,24},{12,28},{1,17},{5,21},{9,25},{13,29},{2,18},{... | collective-permute-start | bytes 393224 | tf_op jit(solution)/shard_map/ppermute | solution.py:30
  15.9 2.6 collective-permute-start.1
  18.5 2.1 collective-permute-start.2
  20.6 1.8 collective-permute-start.3
  24.3 1.3 fusion.81
  29.9 1.0 fusion.73
  32.5 24.0 %all-reduce.11 = (f32[8]{0:T(128)}, f32[2184]{0:T(1024)S(1)}) all-reduce(f32[8]{0:T(128)S(1)} %get-tuple-element.333, f32[2184]{0:T(1024)S(1)} %dynamic-update-slice.1), channel_id=2, replica_groups=mesh['ctx'=8,'tp'=4] {'ctx'}, use_global_device_ids=true, to_apply=%add.7 | all-reduce | flops 2192 | bytes 17536
  57.3 1.4 dynamic-update-slice.2
  59.7 1.1 fusion.82
  60.8 1.8 convert_reduce_fusion.1
  62.6 1.1 fusion.11
  65.2 1.3 fusion.70
  67.3 2.2 convolution_add_fusion.7
  70.1 2.8 %fusion.31 = (f32[256]{0:T(256)S(1)}, f32[256]{0:T(256)}, bf16[256,128]{0,1:T(8,128)(2,1)}) fusion(f32[256,128]{0,1:T(8,128)S(1)} %fusion.7, bf16[256,128]{0,1:T(8,128)(2,1)S(1)} %copy-done.9, f32[256]{0:T(256)S(1)} %get-tuple-element.312, f32[256]{0:T(256)S(1)} %copy-done.49, f32[256]{0:T(256)S(1)} %copy-done.35, f32[256]{0:T(256)S(1)} %get-tuple-element.313, ...), kind=kOutput, calls=%fused_computation.93 | convolution fusion | flops 504167936 | bytes 2235392 | tf_op jit(solution)/shard_map/jvp()/dot_general | solution.py:94
  73.6 1.1 convolution_add_fusion.4
  75.4 1.4 fusion.8
  76.8 34.8 %all-reduce.12 = (bf16[8]{0:T(256)(128)(2,1)S(1)}, bf16[2184]{0:T(1024)(128)(2,1)S(1)}) all-reduce(bf16[8]{0:T(256)(128)(2,1)} %copy-done.51, bf16[2184]{0:T(1024)(128)(2,1)S(1)} %dynamic-update-slice.3), channel_id=5, replica_groups=mesh['ctx'=8,'tp'=4] {'ctx'}, use_global_device_ids=true, to_apply=%add.9 | all-reduce | flops 2192 | bytes 8768
  111.7 10.4 %all-gather.7 = bf16[8,273,128]{2,1,0:T(8,128)(2,1)} all-gather(bf16[1,273,128]{2,1,0:T(8,128)(2,1)S(1)} %fusion.8), channel_id=6, replica_groups=mesh['ctx'=8,'tp'=4] {'ctx'}, dimensions={0}, use_global_device_ids=true | all-gather | bytes 628992 | tf_op jit(solution)/shard_map/all_gather | solution.py:36
  122.1 23.2 %while.33 = (s32[]{:T(128)}, f32[273,128]{1,0:T(8,128)S(1)}, f32[273]{0:T(512)S(1)}, s32[]{:T(128)}, bf16[8,1]{0,1:T(2,128)(2,1)S(1)}, /*index=5*/bf16[8,273,128...) while((s32[]{:T(128)}, f32[273,128]{1,0:T(8,128)S(1)}, ...), condition=%wide.region_12.13_spmd.clone, body=%wide.region_11.12_spmd.clone.sunk | while | flops 176093 | bytes 354557 | solution.py:54
  122.7 1.6 fusion.111
  125.6 1.6 fusion.111
  128.5 1.6 fusion.111
  131.4 1.6 fusion.111
  134.3 1.6 fusion.111
  137.2 1.6 fusion.111
  140.1 1.6 fusion.111
  143.0 1.6 fusion.111
  145.3 1.0 slice_multiply_fusion.1
  146.3 1.0 multiply_reduce_fusion.3
  147.4 1.3 fusion.26
  148.7 1.2 convolution_add_fusion.6
  150.5 1.6 fusion.84
  152.1 1.0 copy-done.4
  153.2 1.2 fusion.15
  154.5 1.2 slice-done
  156.7 1.3 collective-permute-start.4
  158.0 1.3 collective-permute-start.5
  159.3 1.3 collective-permute-start.6
  160.6 1.3 collective-permute-start.7
  162.2 1.6 fusion.10
  164.4 1.6 copy.24
  166.0 2.8 %fusion.14 = f32[256,128]{0,1:T(8,128)S(1)} fusion(f32[256,1280]{1,0:T(8,128)S(1)} %copy-done.5, pred[256,1280]{1,0:T(32,128)(4,1)} %get-tuple-element.311, f32[256]{0:T(256)} %copy-done.46, f32[256,128]{1,0:T(8,128)} %get-tuple-element.327, f32[1024,128]{1,0:T(8,128)S(1)} %copy-done.17, s32[1280]{0:T(1024)} %copy-done.38, s32[256]{0:T(256)} %iota_add_fusion, ...), kind=kOutput, calls=%fused_computation.50 | convolution fusion | flops 506429440 | bytes 2433280 | tf_op jit(solution)/shard_map/transpose(jvp())/dot_general | solution.py:85
  168.8 3.3 %collective-permute-done.5 = f32[256,256]{0,1:T(8,128)} collective-permute-done((f32[256,256]{0,1:T(8,128)}, f32[256,256]{0,1:T(8,128)}, u32[]{:S(2)}, u32[]{:S(2)}) %collective-permute-start.5) | collective-permute-done | bytes 262176 | tf_op jit(solution)/shard_map/ppermute | solution.py:30
  172.1 1.5 collective-permute-done.6
  173.7 2.5 collective-permute-done.7
  176.2 1.3 add_add_fusion
  179.9 75.3 %all-reduce.14 = bf16[256,2048]{1,0:T(8,128)(2,1)} all-reduce(f32[256,2048]{1,0:T(8,128)S(1)} %convolution_add_fusion.2), channel_id=1, replica_groups=mesh['ctx'=8,'tp'=4] {'tp'}, use_global_device_ids=true, to_apply=%region_18.19 | all-reduce | flops 524288 | bytes 3145728 | tf_op jit(solution)/shard_map/psum | solution.py:207
  (203 shorter events, 29.2 us)
Async XLA Ops:
  7.2 2.6 %copy-start = (bf16[2048,256]{1,0:T(8,128)(2,1)S(1)}, bf16[2048,256]{1,0:T(8,128)(2,1)}, u32[]{:S(2)}) copy-start(bf16[2048,256]{1,0:T(8,128)(2,1)} %param.12) | copy-start | bytes 3145732
  7.2 2.6 %copy-start.1 = (bf16[256,2048]{1,0:T(8,128)(2,1)S(1)}, bf16[256,2048]{1,0:T(8,128)(2,1)}, u32[]{:S(2)}) copy-start(bf16[256,2048]{1,0:T(8,128)(2,1)} %param.10) | copy-start | bytes 3145732
  7.2 57.9 %all-gather.10.cloned.1.call-start = ((), (), s32[]{:S(2)}) async-start(), calls=%async_computation | async-start | bytes 1290240 | tf_op jit(solution)/shard_map/all_gather | solution.py:16
  9.8 12.6 %copy-start.47 = (f32[256,1]{0,1:T(1,128)S(1)}, f32[256,1]{0,1:T(1,128)}, u32[]{:S(2)}) copy-start(f32[256,1]{0,1:T(1,128)} %param.14) | copy-start | bytes 3076
  9.8 13.8 %copy-start.54 = (u32[32]{0:T(128)S(1)}, u32[32]{0:T(128)}, u32[]{:S(2)}) copy-start(u32[32]{0:T(128)} %constant.116) | copy-start | bytes 388
  9.8 16.4 %copy-start.11 = (bf16[2048,32]{0,1:T(8,128)(2,1)S(1)}, bf16[2048,32]{0,1:T(8,128)(2,1)}, u32[]{:S(2)}) copy-start(bf16[2048,32]{0,1:T(8,128)(2,1)} %param.11) | copy-start | bytes 393220
  10.3 17.5 %copy-start.19 = (bf16[256,256]{1,0:T(8,128)(2,1)}, bf16[256,256]{1,0:T(8,128)(2,1)S(1)}, u32[]{:S(2)}) copy-start(bf16[256,256]{1,0:T(8,128)(2,1)S(1)} %convolution_convert_fusion) | copy-start | bytes 393220
  11.0 47.6 %collective-permute-start = (bf16[256,256]{1,0:T(8,128)(2,1)S(1)}, bf16[256,256]{1,0:T(8,128)(2,1)S(1)}, u32[]{:S(2)}, u32[]{:S(2)}) collective-permute-start(bf16[256,256]{1,0:T(8,128)(2,1)S(1)} %pad_maximum_fusion.6), channel_id=1, source_target_pairs={{0,16},{4,20},{8,24},{12,28},{1,17},{5,21},{9,25},{13,29},{2,18},{... | collective-permute-start | bytes 393224 | tf_op jit(solution)/shard_map/ppermute | solution.py:30
  15.9 42.7 %collective-permute-start.1 = (bf16[256,256]{1,0:T(8,128)(2,1)S(1)}, bf16[256,256]{1,0:T(8,128)(2,1)S(1)}, u32[]{:S(2)}, u32[]{:S(2)}) collective-permute-start(bf16[256,256]{1,0:T(8,128)(2,1)S(1)} %pad_maximum_fusion.6), channel_id=1, source_target_pairs={{0,12},{4,16},{8,20},{12,24},{16,28},{1,13},{5,17},{9,21},{13,25},... | collective-permute-start | bytes 393224 | tf_op jit(solution)/shard_map/ppermute | solution.py:30
  18.5 40.2 %collective-permute-start.2 = (bf16[256,256]{1,0:T(8,128)(2,1)S(1)}, bf16[256,256]{1,0:T(8,128)(2,1)S(1)}, u32[]{:S(2)}, u32[]{:S(2)}) collective-permute-start(bf16[256,256]{1,0:T(8,128)(2,1)S(1)} %pad_maximum_fusion.6), channel_id=1, source_target_pairs={{0,8},{4,12},{8,16},{12,20},{16,24},{20,28},{1,9},{5,13},{9,17},{1... | collective-permute-start | bytes 393224 | tf_op jit(solution)/shard_map/ppermute | solution.py:30
  20.6 38.0 %collective-permute-start.3 = (bf16[256,256]{1,0:T(8,128)(2,1)S(1)}, bf16[256,256]{1,0:T(8,128)(2,1)S(1)}, u32[]{:S(2)}, u32[]{:S(2)}) collective-permute-start(bf16[256,256]{1,0:T(8,128)(2,1)S(1)} %pad_maximum_fusion.6), channel_id=1, source_target_pairs={{0,4},{4,8},{8,12},{12,16},{16,20},{20,24},{24,28},{1,5},{5,9},{9,... | collective-permute-start | bytes 393224 | tf_op jit(solution)/shard_map/ppermute | solution.py:30
  23.6 32.8 %copy-start.32 = (f32[256]{0:T(256)}, f32[256]{0:T(256)S(1)}, u32[]{:S(2)}) copy-start(f32[256]{0:T(256)S(1)} %get-tuple-element.315) | copy-start | bytes 3076
  26.2 2.8 %copy-start.30 = (f32[256]{0:T(256)}, f32[256]{0:T(256)S(1)}, u32[]{:S(2)}) copy-start(f32[256]{0:T(256)S(1)} %subtract_exponential_fusion.3) | copy-start | bytes 3076
  26.6 4.2 %copy-start.22 = (f32[256,32]{0,1:T(8,128)}, f32[256,32]{0,1:T(8,128)S(1)}, u32[]{:S(2)}) copy-start(f32[256,32]{0,1:T(8,128)S(1)} %fusion.9) | copy-start | bytes 98308
  26.8 30.3 %copy-start.29 = (bf16[256,128]{1,0:T(8,128)(2,1)S(1)}, bf16[256,128]{1,0:T(8,128)(2,1)}, u32[]{:S(2)}) copy-start(bf16[256,128]{1,0:T(8,128)(2,1)} %param.15) | copy-start | bytes 196612
  29.0 27.4 %copy-start.55 = (f32[256,256]{0,1:T(8,128)}, f32[256,256]{0,1:T(8,128)S(1)}, u32[]{:S(2)}) copy-start(f32[256,256]{0,1:T(8,128)S(1)} %get-tuple-element.335) | copy-start | bytes 786436
  29.9 29.2 %copy-start.42 = (pred[1280]{0:T(1024)(128)(4,1)}, pred[1280]{0:T(1024)(128)(4,1)S(1)}, u32[]{:S(2)}) copy-start(pred[1280]{0:T(1024)(128)(4,1)S(1)} %broadcast_compare_fusion.1) | copy-start | bytes 3844
  57.2 5.4 %copy-start.8 = (bf16[256,128]{0,1:T(8,128)(2,1)}, bf16[256,128]{0,1:T(8,128)(2,1)S(1)}, u32[]{:S(2)}) copy-start(bf16[256,128]{0,1:T(8,128)(2,1)S(1)} %copy.18) | copy-start | bytes 196612
  60.8 2.9 %copy-start.36 = (f32[256]{0:T(256)}, f32[256]{0:T(256)S(1)}, u32[]{:S(2)}) copy-start(f32[256]{0:T(256)S(1)} %get-tuple-element.336) | copy-start | bytes 3076
  65.1 4.3 %copy-start.6 = (f32[256,16,16]{0,2,1:T(8,128)S(1)}, f32[256,16,16]{0,2,1:T(8,128)}, u32[]{:S(2)}) copy-start(f32[256,16,16]{0,2,1:T(8,128)} %multiply_multiply_fusion.2) | copy-start | bytes 786436
  65.1 4.3 %copy-start.25 = (f32[256,128]{0,1:T(8,128)S(1)}, f32[256,128]{0,1:T(8,128)}, u32[]{:S(2)}) copy-start(f32[256,128]{0,1:T(8,128)} %fusion.73) | copy-start | bytes 393220
  65.1 4.3 %copy-start.40 = (f32[256]{0:T(256)S(1)}, f32[256]{0:T(256)}, u32[]{:S(2)}) copy-start(f32[256]{0:T(256)} %get-tuple-element.314) | copy-start | bytes 3076
  65.2 4.9 %copy-start.9 = (bf16[256,128]{0,1:T(8,128)(2,1)S(1)}, bf16[256,128]{0,1:T(8,128)(2,1)}, u32[]{:S(2)}) copy-start(bf16[256,128]{0,1:T(8,128)(2,1)} %copy-done.8) | copy-start | bytes 196612
  65.2 4.9 %copy-start.13 = (f32[256,128]{1,0:T(8,128)S(1)}, f32[256,128]{1,0:T(8,128)}, u32[]{:S(2)}) copy-start(f32[256,128]{1,0:T(8,128)} %get-tuple-element.338) | copy-start | bytes 393220
  65.2 4.9 %copy-start.35 = (f32[256]{0:T(256)S(1)}, f32[256]{0:T(256)}, u32[]{:S(2)}) copy-start(f32[256]{0:T(256)} %copy-done.34) | copy-start | bytes 3076
  65.2 4.9 %copy-start.37 = (f32[256]{0:T(256)S(1)}, f32[256]{0:T(256)}, u32[]{:S(2)}) copy-start(f32[256]{0:T(256)} %copy-done.36) | copy-start | bytes 3076
  65.2 4.9 %copy-start.49 = (f32[256]{0:T(256)S(1)}, f32[256]{0:T(256)}, u32[]{:S(2)}) copy-start(f32[256]{0:T(256)} %multiply_divide_fusion) | copy-start | bytes 3076
  67.3 6.3 %copy-start.44 = (f32[256]{0:T(256)}, f32[256]{0:T(256)S(1)}, u32[]{:S(2)}) copy-start(f32[256]{0:T(256)S(1)} %get-tuple-element.313) | copy-start | bytes 3076
  70.1 2.9 %copy-start.33 = (f32[256]{0:T(256)S(1)}, f32[256]{0:T(256)}, u32[]{:S(2)}) copy-start(f32[256]{0:T(256)} %copy-done.32) | copy-start | bytes 3076
  122.1 25.3 %copy-start.10 = (bf16[256,128]{0,1:T(8,128)(2,1)S(1)}, bf16[256,128]{0,1:T(8,128)(2,1)}, u32[]{:S(2)}) copy-start(bf16[256,128]{0,1:T(8,128)(2,1)} %copy-done.8) | copy-start | bytes 196612
  122.1 25.3 %copy-start.45 = (f32[256]{0:T(256)S(1)}, f32[256]{0:T(256)}, u32[]{:S(2)}) copy-start(f32[256]{0:T(256)} %copy-done.44) | copy-start | bytes 3076
  122.1 25.3 %copy-start.50 = (f32[256]{0:T(256)S(1)}, f32[256]{0:T(256)}, u32[]{:S(2)}) copy-start(f32[256]{0:T(256)} %get-tuple-element.330) | copy-start | bytes 3076
  145.3 3.4 %copy-start.26 = (f32[256,128]{0,1:T(8,128)S(1)}, f32[256,128]{0,1:T(8,128)}, u32[]{:S(2)}) copy-start(f32[256,128]{0,1:T(8,128)} %convolution_add_fusion.7) | copy-start | bytes 393220
  145.3 3.4 %copy-start.31 = (f32[256]{0:T(256)S(1)}, f32[256]{0:T(256)}, u32[]{:S(2)}) copy-start(f32[256]{0:T(256)} %copy-done.30) | copy-start | bytes 3076
  150.4 2.7 %copy-start.18 = (pred[256,1280]{1,0:T(32,128)(4,1)S(1)}, pred[256,1280]{1,0:T(32,128)(4,1)}, u32[]{:S(2)}) copy-start(pred[256,1280]{1,0:T(32,128)(4,1)} %get-tuple-element.311) | copy-start | bytes 983044
  150.4 2.7 %copy-start.21 = (bf16[256,256]{1,0:T(8,128)(2,1)S(1)}, bf16[256,256]{1,0:T(8,128)(2,1)}, u32[]{:S(2)}) copy-start(bf16[256,256]{1,0:T(8,128)(2,1)} %copy-done.19) | copy-start | bytes 393220
  150.4 2.7 %copy-start.39 = (s32[1280]{0:T(1024)S(1)}, s32[1280]{0:T(1024)}, u32[]{:S(2)}) copy-start(s32[1280]{0:T(1024)} %copy-done.38) | copy-start | bytes 15364
  150.4 2.7 %copy-start.43 = (pred[1280]{0:T(1024)(128)(4,1)S(1)}, pred[1280]{0:T(1024)(128)(4,1)}, u32[]{:S(2)}) copy-start(pred[1280]{0:T(1024)(128)(4,1)} %copy-done.42) | copy-start | bytes 3844
  150.4 2.7 %copy-start.53 = (s32[256]{0:T(256)S(1)}, s32[256]{0:T(256)}, u32[]{:S(2)}) copy-start(s32[256]{0:T(256)} %iota_add_fusion) | copy-start | bytes 3076
  154.4 10.0 %copy-start.7 = (f32[1280,128]{0,1:T(8,128)}, f32[1280,128]{0,1:T(8,128)S(1)}, u32[]{:S(2)}) copy-start(f32[1280,128]{0,1:T(8,128)S(1)} %fusion.15) | copy-start | bytes 1966084
  155.7 6.2 %copy-start.23 = (f32[256,32]{0,1:T(8,128)S(1)}, f32[256,32]{0,1:T(8,128)}, u32[]{:S(2)}) copy-start(f32[256,32]{0,1:T(8,128)} %copy-done.22) | copy-start | bytes 98308
  155.7 10.3 %copy-start.5 = (f32[256,1280]{1,0:T(8,128)S(1)}, f32[256,1280]{1,0:T(8,128)}, u32[]{:S(2)}) copy-start(f32[256,1280]{1,0:T(8,128)} %copy-done.4) | copy-start | bytes 3932164
  155.7 10.3 %copy-start.17 = (f32[1024,128]{1,0:T(8,128)S(1)}, f32[1024,128]{1,0:T(8,128)}, u32[]{:S(2)}) copy-start(f32[1024,128]{1,0:T(8,128)} %copy-done.16) | copy-start | bytes 1572868
  156.7 12.1 %collective-permute-start.4 = (f32[256,256]{0,1:T(8,128)}, f32[256,256]{0,1:T(8,128)}, u32[]{:S(2)}, u32[]{:S(2)}) collective-permute-start(f32[256,256]{0,1:T(8,128)} %get-tuple-element.318), channel_id=1, source_target_pairs={{4,0},{8,4},{12,8},{16,12},{20,16},{24,20},{28,24},{5,1},{9,5},{13... | collective-permute-start | bytes 786440 | tf_op jit(solution)/shard_map/ppermute | solution.py:30
  158.0 14.1 %collective-permute-start.5 = (f32[256,256]{0,1:T(8,128)}, f32[256,256]{0,1:T(8,128)}, u32[]{:S(2)}, u32[]{:S(2)}) collective-permute-start(f32[256,256]{0,1:T(8,128)} %get-tuple-element.317), channel_id=1, source_target_pairs={{8,0},{12,4},{16,8},{20,12},{24,16},{28,20},{9,1},{13,5},{17,9},{2... | collective-permute-start | bytes 786440 | tf_op jit(solution)/shard_map/ppermute | solution.py:30
  159.3 14.4 %collective-permute-start.6 = (f32[256,256]{0,1:T(8,128)}, f32[256,256]{0,1:T(8,128)}, u32[]{:S(2)}, u32[]{:S(2)}) collective-permute-start(f32[256,256]{0,1:T(8,128)} %get-tuple-element.320), channel_id=1, source_target_pairs={{12,0},{16,4},{20,8},{24,12},{28,16},{13,1},{17,5},{21,9},{25,13},... | collective-permute-start | bytes 786440 | tf_op jit(solution)/shard_map/ppermute | solution.py:30
  160.6 15.6 %collective-permute-start.7 = (f32[256,256]{0,1:T(8,128)}, f32[256,256]{0,1:T(8,128)}, u32[]{:S(2)}, u32[]{:S(2)}) collective-permute-start(f32[256,256]{0,1:T(8,128)} %get-tuple-element.319), channel_id=1, source_target_pairs={{16,0},{20,4},{24,8},{28,12},{17,1},{21,5},{25,9},{29,13},{18,2},{... | collective-permute-start | bytes 786440 | tf_op jit(solution)/shard_map/ppermute | solution.py:30
  168.8 8.6 %slice-start.1 = ((f32[1280,128]{0,1:T(8,128)}), f32[256,128]{0,1:T(8,128)S(1)}, s32[]{:S(2)}) async-start(f32[1280,128]{0,1:T(8,128)} %copy-done.7), calls=%async_computation.2 | async-start | bytes 262144 | tf_op jit(solution)/shard_map/transpose(jvp())/split | solution.py:122
  (19 other events, 22.9 us)
Sparse Core Ops, SparseCore 0:
  27.9 24.1 all-gather.9
where the time goes:
time: 267 us; the launch traced here: 262 us
  blocking collectives  144 us (54%)
  other arithmetic  31.1 us (12%)
  matrix products  30.2 us (11%)
  starting transfers between devices  16.6 us (6%)
  local copies, waits for them, and re-layouts  16.5 us (6%)
  between operations  15.6 us (6%)
  waiting for transfers between devices  7.39 us (3%)
    psum x1, blocking collectives, per_device(): input_grad = lax.psum(partial_sum, 'tp').astype(jnp.bfloat16)  75.3 us
    unnamed x2, blocking collectives  58.8 us
    select_n x16, other arithmetic, step(): return jax.tree.map(lambda a, b: jnp.where(reached, a, b), new, before)  18.1 us
    ppermute x8, starting transfers between devices, shifted(): return lax.ppermute(value, axis, pairs)  16.5 us
    all_gather x1, blocking collectives, entering(): lax.all_gather(part.astype(kind), axis)  10.4 us
    unnamed x122, local copies, waits for them, and re-layouts  8.16 us
    ppermute x8, waiting for transfers between devices, shifted(): return lax.ppermute(value, axis, pairs)  7.37 us
    dot_general x3, matrix products, window_part(): jnp.dot(exponent, key_values, precision=precise)  5.52 us
  transfers between devices with their start and end apart: 9, of which 3 were waited for; matrix products, arithmetic and copies ran while one was open for 9% of the time, Pallas kernels for 0%

commit v1 on v0

v1 whole, which is shorter than its diff:
```python
from functools import partial

import jax
import jax.numpy as jnp
from jax import lax
from jax.experimental import pallas as pl
from jax.experimental.pallas import tpu as pltpu
from jax.sharding import Mesh
from jax.sharding import PartitionSpec as P

WINDOW = 1024
LANES = 128
MASKED = -1e30
CTX = ("chip", "core")
f32 = jnp.float32
bf16 = jnp.bfloat16


def nn(a, b):
    return lax.dot_general(a, b, (((1,), (0,)), ((), ())), preferred_element_type=f32)


def nt(a, b):
    return lax.dot_general(a, b, (((1,), (1,)), ((), ())), preferred_element_type=f32)


def wide(ref, at, start, count):
    view = ref if at is None else ref.at[at]
    return jnp.concatenate(
        [view[start : start + count, :], view[start + count : start + 2 * count, :]], axis=1
    )


def put_wide(ref, start, value):
    count = value.shape[0]
    for half in range(value.shape[1] // LANES):
        ref[start + half * count : start + (half + 1) * count, :] = value[
            :, half * LANES : (half + 1) * LANES
        ]


def cum_row(ref, at, start):
    view = ref if at is None else ref.at[at]
    tail = view[start : start + 16, :].astype(f32)
    first = tail[0:1] + tail[2:3] + tail[4:5]
    second = tail[1:2] + tail[3:4] + tail[5:6]
    return jnp.concatenate([first, second], axis=1)


def project_kernel(
    place_ref, tok_ref, fw_ref, ww_ref, vw_ref, ld_ref, do_ref,
    send_ref, own_ref, feat_ref, cum_ref, pack_ref,
):
    me, core = place_ref[0], place_ref[1]
    rows, dim = tok_ref.shape
    half = dim // 2
    dh = do_ref.shape[1]
    nf = fw_ref.shape[1] // 2
    count = send_ref.shape[0]
    tok = tok_ref[...]
    feat = nn(tok, fw_ref[...]).astype(bf16)
    window = nn(tok, ww_ref[...]).astype(bf16)
    values = nn(tok, vw_ref[...]).astype(bf16)
    feat_ref[...] = feat
    eye = (
        lax.broadcasted_iota(jnp.int32, (2 * nf, 2 * nf), 0)
        == lax.broadcasted_iota(jnp.int32, (2 * nf, 2 * nf), 1)
    ).astype(bf16)
    feat_t = nt(eye, feat).astype(bf16)
    at_row = lax.broadcasted_iota(jnp.int32, (rows, rows), 0)
    at_col = lax.broadcasted_iota(jnp.int32, (rows, rows), 1)
    ld = ld_ref[...]
    cum_r = jnp.sum(jnp.where(at_row <= at_col, ld, 0.0), axis=0, keepdims=True)
    ld_r = jnp.sum(jnp.where(at_row == at_col, ld, 0.0), axis=0, keepdims=True)
    cum_ref[...] = jnp.sum(jnp.where(at_col <= at_row, ld_r, 0.0), axis=1, keepdims=True)
    high = cum_r.astype(bf16)
    rest = cum_r - high.astype(f32)
    mid = rest.astype(bf16)
    low = (rest - mid.astype(f32)).astype(bf16)
    pieces = [high[:, :LANES], high[:, LANES:], mid[:, :LANES], mid[:, LANES:], low[:, :LANES], low[:, LANES:]]
    tail = jnp.concatenate(
        [p.astype(f32) for p in pieces] + [jnp.zeros((10, LANES), f32)], axis=0
    ).astype(bf16)
    feat_at = 2 * rows
    tail_at = feat_at + 2 * nf

    own_ref[0:rows, :] = window[:, dh:]
    own_ref[rows : 2 * rows, :] = values
    put_wide(own_ref, feat_at, feat_t[nf:, :])
    own_ref[tail_at : tail_at + 16, :] = tail

    def fill(j, carry):
        slot = send_ref.at[j]
        slot[tail_at : tail_at + 16, :] = tail

        @pl.when(j > me)
        def _():
            slot[0:rows, :] = window[:, dh:]
            slot[rows : 2 * rows, :] = values
            put_wide(slot, feat_at, feat_t[nf:, :])

        @pl.when(j <= me)
        def _():
            slot[0:rows, :] = window[:, :dh]
            slot[rows : 2 * rows, :] = do_ref[...]
            put_wide(slot, feat_at, feat_t[:nf, :])

        return carry

    lax.fori_loop(0, count, fill, 0)

    start = pl.multiple_of(core * half, half)
    pack_ref[0:half, :] = ww_ref[pl.ds(start, half), 0:dh]
    pack_ref[half : 2 * half, :] = ww_ref[pl.ds(start, half), dh : 2 * dh]
    pack_ref[2 * half : 3 * half, :] = vw_ref[pl.ds(start, half), :]
    fw_t = nt(eye, fw_ref[pl.ds(start, half), :]).astype(bf16)
    put_wide(pack_ref, 3 * half, fw_t)


def query_kernel(
    place_ref, recv_ref, own_ref, feat_ref, cum_ref,
    att_ref, stat_ref, dwq_ref, dqt_ref,
    p_ref,
):
    me = place_ref[0]
    rows, dh = att_ref.shape
    nf = feat_ref.shape[1] // 2
    back = WINDOW // rows
    feat_at = 2 * rows
    tail_at = feat_at + 2 * nf
    scale = dh ** (-0.5)
    feat_scale = nf ** (-0.5)
    wq = recv_ref[me, 0:rows, :]
    do = recv_ref[me, rows : 2 * rows, :]
    q = feat_ref[:, :nf]
    at_row = lax.broadcasted_iota(jnp.int32, (rows, rows), 0)
    at_col = lax.broadcasted_iota(jnp.int32, (rows, rows), 1)

    def keys(w):
        if w == back:
            return own_ref[0:rows, :]
        return recv_ref[jnp.maximum(me - back + w, 0), 0:rows, :]

    def vals(w):
        if w == back:
            return own_ref[rows : 2 * rows, :]
        return recv_ref[jnp.maximum(me - back + w, 0), rows : 2 * rows, :]

    top = jnp.full((rows, 1), MASKED, f32)
    for w in range(back + 1):
        s = nt(wq, keys(w)) * scale
        if w == back:
            ok = at_col <= at_row
        elif w == 0:
            ok = (at_col > at_row) & (me >= back)
        else:
            ok = (at_col >= 0) & (me >= back - w)
        s = jnp.where(ok, s, MASKED)
        p_ref[w] = s
        top = jnp.maximum(top, jnp.max(s, axis=1, keepdims=True))
    total = jnp.zeros((rows, 1), f32)
    out = jnp.zeros((rows, dh), f32)
    for w in range(back + 1):
        p = jnp.exp(p_ref[w] - top)
        p_ref[w] = p
        total += jnp.sum(p, axis=1, keepdims=True)
        out += nn(p.astype(bf16), vals(w))
    inv = 1.0 / total
    windowed = out * inv

    cum_c = cum_ref[...]
    growth = jnp.exp(cum_c)
    own_cum = cum_row(own_ref, None, tail_at)
    own_e = jnp.where(at_col <= at_row, jnp.exp(jnp.minimum(cum_c - own_cum, 0.0)), 0.0)

    def far_terms(j, between):
        cum = cum_row(recv_ref, j, tail_at)
        whole = cum[:, rows - 1 : rows]
        es = jnp.exp(between + whole - cum)
        x = nn(q, wide(recv_ref, j, feat_at, nf)) * feat_scale
        return es, x, between + whole

    def forward(step, carry):
        num, den, between = carry
        j = me - 1 - step
        es, x, between = far_terms(j, between)
        weight = (1.0 + x + 0.5 * x * x) * es
        den += jnp.sum(weight, axis=1, keepdims=True)
        num += nn(weight.astype(bf16), recv_ref[j, rows : 2 * rows, :])
        return num, den, between

    zero = jnp.zeros((1, 1), f32)
    num, den, _ = lax.fori_loop(
        0, me, forward, (jnp.zeros((rows, dh), f32), jnp.zeros((rows, 1), f32), zero)
    )
    own_x = nn(q, wide(own_ref, None, feat_at, nf)) * feat_scale
    weight = (1.0 + own_x + 0.5 * own_x * own_x) * own_e
    num = num * growth + nn(weight.astype(bf16), own_ref[rows : 2 * rows, :])
    den = den * growth + jnp.sum(weight, axis=1, keepdims=True)
    rden = 1.0 / den
    linear = num * rden
    att_ref[...] = (linear + windowed).astype(bf16)
    do_f = do.astype(f32)
    delta_w = jnp.sum(do_f * windowed, axis=1, keepdims=True)
    delta_l = jnp.sum(do_f * linear, axis=1, keepdims=True)
    lse = top + jnp.log(total)
    lane = lax.broadcasted_iota(jnp.int32, (rows, LANES), 1)
    sheet = jnp.where(lane == 0, lse, 0.0)
    sheet = jnp.where(lane == 1, delta_w, sheet)
    sheet = jnp.where(lane == 2, rden, sheet)
    sheet = jnp.where(lane == 3, delta_l, sheet)
    stat_ref[...] = jnp.transpose(sheet)[0:8, :]

    dwq = jnp.zeros((rows, dh), f32)
    for w in range(back + 1):
        dp = nt(do, vals(w))
        ds = (p_ref[w] * inv) * (dp - delta_w)
        dwq += nn(ds.astype(bf16), keys(w))
    dwq_ref[...] = (dwq * scale).astype(bf16)

    far_scale = growth * rden

    def backward(step, carry):
        dqt, between = carry
        j = me - 1 - step
        es, x, between = far_terms(j, between)
        dp = nt(do, recv_ref[j, rows : 2 * rows, :])
        dx = (dp - delta_l) * es * ((1.0 + x) * far_scale)
        dqt += nt(wide(recv_ref, j, feat_at, nf), dx.astype(bf16))
        return dqt, between

    dqt, _ = lax.fori_loop(0, me, backward, (jnp.zeros((nf, rows), f32), zero))
    dp = nt(do, own_ref[rows : 2 * rows, :])
    dx = (dp - delta_l) * own_e * ((1.0 + own_x) * rden)
    dqt += nt(wide(own_ref, None, feat_at, nf), dx.astype(bf16))
    dqt_ref[...] = (dqt * feat_scale).astype(bf16)


def key_kernel(
    place_ref, recv_ref, own_ref, feat_ref, cum_ref, stat_ref, dwq_ref, dqt_ref, grad_ref
):
    me = place_ref[0]
    count = recv_ref.shape[0]
    rows, dh = dwq_ref.shape
    nf = feat_ref.shape[1] // 2
    back = WINDOW // rows
    feat_at = 2 * rows
    tail_at = feat_at + 2 * nf
    scale = dh ** (-0.5)
    feat_scale = nf ** (-0.5)
    wk = own_ref[0:rows, :]
    v = own_ref[rows : 2 * rows, :]
    k = feat_ref[:, nf : 2 * nf]
    at_row = lax.broadcasted_iota(jnp.int32, (rows, rows), 0)
    at_col = lax.broadcasted_iota(jnp.int32, (rows, rows), 1)
    dwk = jnp.zeros((rows, dh), f32)
    dv = jnp.zeros((rows, dh), f32)
    for w in range(back + 1):
        j = jnp.minimum(me + w, count - 1)
        wq = recv_ref[j, 0:rows, :]
        do = recv_ref[j, rows : 2 * rows, :]
        if w == 0:
            ok = at_row <= at_col
        elif w == back:
            ok = (at_row > at_col) & (me + w < count)
        else:
            ok = (at_row >= 0) & (me + w < count)
        s = nt(wk, wq) * scale
        p = jnp.where(ok, jnp.exp(s - stat_ref[j, 0:1, :]), 0.0)
        ds = p * (nt(v, do) - stat_ref[j, 1:2, :])
        dv += nn(p.astype(bf16), do)
        dwk += nn(ds.astype(bf16), wq)

    cum_c = cum_ref[...]
    own_cum = cum_row(own_ref, None, tail_at)
    tail = jnp.exp(own_cum[:, rows - 1 : rows] - cum_c)

    def terms(j, e):
        qt = wide(recv_ref, j, feat_at, nf)
        do = recv_ref[j, rows : 2 * rows, :]
        x = nn(k, qt) * feat_scale
        weight = (1.0 + x + 0.5 * x * x) * e
        dx = (nt(v, do) - stat_ref[j, 3:4, :]) * e * (1.0 + x)
        return nn(weight.astype(bf16), do), nt(qt, dx.astype(bf16))

    own_e = jnp.where(at_row <= at_col, jnp.exp(jnp.minimum(own_cum - cum_c, 0.0)), 0.0)
    more_v, dkt = terms(me, own_e * stat_ref[me, 2:3, :])
    dv += more_v

    def far(j, carry):
        dv, dkt, between = carry
        cum = cum_row(recv_ref, j, tail_at)
        e = jnp.exp(between + cum) * stat_ref[j, 2:3, :] * tail
        more_v, more_k = terms(j, e)
        return dv + more_v, dkt + more_k, between + cum[:, rows - 1 : rows]

    dv, dkt, _ = lax.fori_loop(me + 1, count, far, (dv, dkt, jnp.zeros((1, 1), f32)))
    grad_ref[0:rows, :] = dwq_ref[...]
    grad_ref[rows : 2 * rows, :] = (dwk * scale).astype(bf16)
    grad_ref[2 * rows : 3 * rows, :] = dv.astype(bf16)
    dft = jnp.concatenate([dqt_ref[...], (dkt * feat_scale).astype(bf16)], axis=0)
    put_wide(grad_ref, 3 * rows, dft)


def merge_kernel(
    place_ref, grad_ref, mq_ref, mk_ref, mv_ref, mf_ref, oq_ref, ok_ref, ov_ref, of_ref,
    out_ref, cat_ref, feat_ref,
):
    heads = grad_ref.shape[0]
    rows = out_ref.shape[0]
    nf2 = mf_ref.shape[1] // (out_ref.shape[1] // LANES)
    step = pl.program_id(0)
    tiles = pl.num_programs(0) // 2

    @pl.when(step == 0)
    def _():
        for h in range(heads):
            for part in range(3):
                at = (3 * h + part) * LANES
                cat_ref[:, at : at + LANES] = grad_ref[h, part * rows : (part + 1) * rows, :]
        dft = jnp.concatenate([wide(grad_ref, h, 3 * rows, nf2) for h in range(heads)], axis=0)
        feat_ref[...] = jnp.transpose(dft.astype(f32)).astype(bf16)

    def product(q_ref, k_ref, v_ref, f_ref):
        weights = jnp.concatenate(
            [r[h] for h in range(heads) for r in (q_ref, k_ref, v_ref)], axis=1
        )
        feat_w = jnp.concatenate([wide(f_ref, h, 0, nf2) for h in range(heads)], axis=0)
        out = nt(cat_ref[...], weights) + nn(feat_ref[...], feat_w)
        out_ref[...] = out.astype(bf16)

    @pl.when(step < tiles)
    def _():
        product(mq_ref, mk_ref, mv_ref, mf_ref)

    @pl.when(step >= tiles)
    def _():
        product(oq_ref, ok_ref, ov_ref, of_ref)


VMEM = pl.BlockSpec(memory_space=pltpu.VMEM)
SMEM = pl.BlockSpec(memory_space=pltpu.SMEM)
params = pltpu.CompilerParams(vmem_limit_bytes=48 * 1024 * 1024)


def merge(place, grads, mine, other, dim):
    heads = grads.shape[0]
    rows = (grads.shape[1] * LANES) // (3 * LANES + 32)
    half = dim // 2
    tile = 256
    tiles = half // tile
    nf2 = (mine.shape[1] - 3 * half) * LANES // half
    frows = nf2 * tile // LANES

    def own_at(part):
        return lambda i, place: (0, part * tiles + jnp.minimum(i, tiles - 1), 0)

    def other_at(part):
        return lambda i, place: (0, part * tiles + jnp.maximum(i - tiles, 0), 0)

    first = 3 * half // frows
    big = (heads, tile, LANES)
    small = (heads, frows, LANES)
    specs = [pl.BlockSpec(grads.shape, lambda i, place: (0, 0, 0))]
    specs += [pl.BlockSpec(big, own_at(part)) for part in range(3)]
    specs += [pl.BlockSpec(small, lambda i, place: (0, first + jnp.minimum(i, tiles - 1), 0))]
    specs += [pl.BlockSpec(big, other_at(part)) for part in range(3)]
    specs += [pl.BlockSpec(small, lambda i, place: (0, first + jnp.maximum(i - tiles, 0), 0))]

    def out_at(i, place):
        core = place[1]
        return (0, jnp.where(i < tiles, core * tiles + i, (1 - core) * tiles + i - tiles))

    return pl.pallas_call(
        merge_kernel,
        out_shape=jax.ShapeDtypeStruct((rows, dim), bf16),
        grid_spec=pltpu.PrefetchScalarGridSpec(
            num_scalar_prefetch=1,
            grid=(2 * tiles,),
            in_specs=specs,
            out_specs=pl.BlockSpec((rows, tile), out_at),
            scratch_shapes=[
                pltpu.VMEM((rows, 3 * LANES * heads), bf16),
                pltpu.VMEM((rows, nf2 * heads), bf16),
            ],
        ),
        compiler_params=params,
        cost_estimate=pl.CostEstimate(
            flops=2 * rows * dim * heads * 416, bytes_accessed=heads * dim * 416 * 2, transcendentals=0
        ),
        name="head_sum",
    )(place, grads, mine, mine, mine, mine, other, other, other, other)


def per_device(tokens, feature_weight, window_weight, value_weight, log_decay, out_grad):
    rows, dim = tokens.shape
    nf2 = feature_weight.shape[1]
    nf = nf2 // 2
    dh = value_weight.shape[1]
    count = lax.axis_size(CTX)
    me = lax.axis_index(CTX)
    core = lax.axis_index("core")
    place = jnp.stack([me, core]).astype(jnp.int32)
    payload = 2 * rows + 2 * nf + 16
    pack = 3 * (dim // 2) + nf2 * (dim // 2) // LANES
    send, own, feat, cum, packed = pl.pallas_call(
        project_kernel,
        out_shape=(
            jax.ShapeDtypeStruct((count, payload, LANES), bf16),
            jax.ShapeDtypeStruct((payload, LANES), bf16),
            jax.ShapeDtypeStruct((rows, nf2), bf16),
            jax.ShapeDtypeStruct((rows, 1), f32),
            jax.ShapeDtypeStruct((pack, LANES), bf16),
        ),
        in_specs=[SMEM] + [VMEM] * 6,
        out_specs=[VMEM] * 5,
        compiler_params=params,
        cost_estimate=pl.CostEstimate(
            flops=2 * rows * dim * 416, bytes_accessed=4 * 1024 * 1024, transcendentals=0
        ),
        name="project",
    )(place, tokens, feature_weight, window_weight, value_weight, log_decay, out_grad)
    mine = lax.all_gather(packed, "tp")
    recv = lax.all_to_all(send, CTX, 0, 0, tiled=True)
    attended, stat, dwq, dqt = pl.pallas_call(
        query_kernel,
        out_shape=(
            jax.ShapeDtypeStruct((rows, dh), bf16),
            jax.ShapeDtypeStruct((8, rows), f32),
            jax.ShapeDtypeStruct((rows, dh), bf16),
            jax.ShapeDtypeStruct((nf, rows), bf16),
        ),
        in_specs=[SMEM] + [VMEM] * 4,
        out_specs=[VMEM] * 4,
        scratch_shapes=[pltpu.VMEM((WINDOW // rows + 1, rows, rows), f32)],
        compiler_params=params,
        cost_estimate=pl.CostEstimate(
            flops=10**9, bytes_accessed=2 * 1024 * 1024, transcendentals=10**6
        ),
        name="query_side",
    )(place, recv, own, feat, cum)
    stats = lax.all_gather(stat, CTX)
    grads = pl.pallas_call(
        key_kernel,
        out_shape=jax.ShapeDtypeStruct((3 * rows + nf2 * rows // LANES, LANES), bf16),
        in_specs=[SMEM] + [VMEM] * 7,
        out_specs=VMEM,
        compiler_params=params,
        cost_estimate=pl.CostEstimate(
            flops=10**9, bytes_accessed=2 * 1024 * 1024, transcendentals=10**6
        ),
        name="key_side",
    )(place, recv, own, feat, cum, stats, dwq, dqt)
    all_grads = lax.all_gather(grads, "tp")
    other = lax.ppermute(mine, "core", [(0, 1), (1, 0)])
    input_grad = merge(place, all_grads, mine, other, dim)
    return (attended, input_grad)


def solution(mesh):
    ctx, tp = mesh.devices.shape
    split = Mesh(mesh.devices.reshape(ctx // 2, 2, tp), ("chip", "core", "tp"))
    in_specs = (
        P(CTX, None),
        P(None, "tp"),
        P(None, "tp"),
        P(None, "tp"),
        P(CTX, "tp"),
        P(CTX, "tp"),
    )
    out_specs = (P(CTX, "tp"), P(CTX, None))
    return jax.shard_map(
        per_device, mesh=split, in_specs=in_specs, out_specs=out_specs, check_vma=False
    )
```

time: 267 us -> 161 us (0.60); the launches traced: 262 us -> 161 us
  blocking collectives: 144 us -> 49.7 us
  waiting for transfers between devices: 7.39 us -> 70.7 us
  other arithmetic: 31.1 us -> 0.08 us
  matrix products: 30.2 us -> 0 us
  Pallas kernels: 0 us -> 18.3 us
  starting transfers between devices: 16.6 us -> 0.04 us
  local copies, waits for them, and re-layouts: 16.5 us -> 8.1 us
    psum x1 -> x0, blocking collectives: 75.3 us -> none  [per_device(): input_grad = lax.psum(partial_sum, 'tp').astype(jnp.bfloat16)]
    all_gather x1, waiting for transfers between devices: 0.01 us -> 70.7 us  [per_device(): mine = lax.all_gather(packed, 'tp')]
    unnamed x2 -> x0, blocking collectives: 58.8 us -> none
    dot_general x26 -> x0, matrix products: 30.2 us -> none  [the longest x3 5.52 us: window_part(): jnp.dot(exponent, key_values, precision=precise)]
    all_to_all x0 -> x1, blocking collectives: none -> 20 us  [per_device(): recv = lax.all_to_all(send, CTX, 0, 0, tiled=True)]
    all_gather x1 -> x2, blocking collectives: 10.4 us -> 29.7 us  [the longest x1 18.4 us: per_device(): all_grads = lax.all_gather(grads, 'tp')]
    pallas_call x0 -> x4, Pallas kernels: none -> 18.3 us  [the longest x1 8.05 us: merge(): pl.pallas_call(merge_kernel, out_shape=jax.ShapeDtypeStruct((rows, dim),...]
    select_n x16 -> x0, other arithmetic: 18.1 us -> none  [step(): return jax.tree.map(lambda a, b: jnp.where(reached, a, b), new, before)]
  transfers between devices with their start and end apart: 9 -> 2, of which waited for: 3 -> 1; matrix products, arithmetic and copies ran while one was open for 9% -> 0% of each run, Pallas kernels for 0% -> 5%
where the time goes in v1:
time: 161 us
  waiting for transfers between devices  70.7 us (44%)
  blocking collectives  49.7 us (31%)
  Pallas kernels  18.3 us (11%)
  between operations  14.1 us (9%)
  local copies, waits for them, and re-layouts  8.1 us (5%)
    all_gather x1, waiting for transfers between devices, per_device(): mine = lax.all_gather(packed, 'tp')  70.7 us
    all_to_all x1, blocking collectives, per_device(): recv = lax.all_to_all(send, CTX, 0, 0, tiled=True)  20 us
    all_gather x1, blocking collectives, per_device(): all_grads = lax.all_gather(grads, 'tp')  18.4 us
    all_gather x1, blocking collectives, per_device(): stats = lax.all_gather(stat, CTX)  11.3 us
    unnamed x14, local copies, waits for them, and re-layouts  8.1 us
    pallas_call x1, Pallas kernels, merge(): pl.pallas_call(merge_kernel, out_shape=jax.ShapeDtypeStruct((rows, dim),...  8.05 us
    pallas_call x1, Pallas kernels, per_device(): pl.pallas_call(key_kernel, out_shape=jax.ShapeDtypeStruct((3 * rows + nf2...  4.55 us
  transfers between devices with their start and end apart: 2, of which 1 were waited for; matrix products, arithmetic and copies ran while one was open for 0% of the time, Pallas kernels for 5%

profile of v1, /device:TPU:0, one launch (start us, length us, event | category | flops | bytes accessed | tf_op | source)
XLA Modules:
  0.0 161.0 jit_solution(14864453726024304142)
XLA Ops:
  7.2 0.0 all-gather.5.cloned.1.call-start
  7.2 0.8 copy.9.ld_ref
  8.0 1.2 copy.8.fw_ref
  9.2 0.1 pad_add_fusion.place_ref
  9.3 0.0 copy-start.1
  9.3 1.2 copy-done.1
  10.5 0.0 copy-start.2
  10.5 1.2 copy-done.2
  11.8 0.0 copy-start.3
  11.8 1.0 copy-done.3
  12.8 0.0 copy-start.4
  12.8 0.8 copy-done.4
  13.6 2.8 %project.1 = (bf16[8,560,128]{2,1,0:T(8,128)(2,1)S(1)}, bf16[560,128]{1,0:T(8,128)(2,1)S(1)}, bf16[256,32]{1,0:T(8,128)(2,1)S(1)}, f32[256,1]{1,0:T(8,128)S(1)}, bf16[3328,128]{1,0:T(8,128)(2,1)}) custom-call(s32[2]{0:T(128)S(1)} %pad_add_fusion.place_ref, bf16[256,2048]{1,0:T(8,128)(2,1)S(1)} %copy-done.1, bf16[2048,32]{1,0:T(8,128)(2,1)S(1)} %copy.8.fw_ref, ...), custom_call_target="tpu_custom_call" | custom-call | flops 436207616 | bytes 4194304 | tf_op jit(solution)/shard_map/project/pallas_call | solution.py:406
  16.5 0.0 all-gather.5.cloned.1.call-update
  16.5 70.7 %all-gather.5.cloned.1.call-done = bf16[13312,128]{1,0:T(8,128)(2,1)} async-done(((bf16[3328,128]{1,0:T(8,128)(2,1)}), bf16[13312,128]{1,0:T(8,128)(2,1)}) %all-gather.5.cloned.1.call-update) | async-done | bytes 3407888 | tf_op jit(solution)/shard_map/all_gather | solution.py:423
  87.2 0.0 collective-permute-start
  87.2 20.0 %all_to_all.5.recv_ref = bf16[8,560,128]{2,1,0:T(8,128)(2,1)S(1)} all-to-all(bf16[8,560,128]{2,1,0:T(8,128)(2,1)S(1)} %get-tuple-element.11), channel_id=1, replica_groups=mesh['chip'=4,'core'=2,'tp'=4] {'chip','core'}, dimensions={0} | all-to-all | bytes 2293760 | tf_op jit(solution)/shard_map/all_to_all | solution.py:424
  107.1 0.0 copy-start
  107.1 2.9 %query_side.1 = (bf16[256,128]{1,0:T(8,128)(2,1)}, f32[8,256]{1,0:T(8,128)S(1)}, bf16[256,128]{1,0:T(8,128)(2,1)S(1)}, bf16[16,256]{1,0:T(8,128)(2,1)S(1)}) custom-call(s32[2]{0:T(128)S(1)} %pad_add_fusion.place_ref, bf16[8,560,128]{2,1,0:T(8,128)(2,1)S(1)} %all_to_all.5.recv_ref, bf16[560,128]{1,0:T(8,128)(2,1)S(1)} %get-tuple-element.12.own_ref, ...), custom_call_target="tpu_custom_call" | custom-call | flops 1000000000 | bytes 2097152 | tf_op jit(solution)/shard_map/query_side/pallas_call | solution.py:425
  110.0 11.3 %all-gather = f32[64,256]{1,0:T(8,128)S(1)} all-gather(f32[8,256]{1,0:T(8,128)S(1)} %get-tuple-element.16), channel_id=2, replica_groups=mesh['chip'=4,'core'=2,'tp'=4] {'chip','core'}, dimensions={0}, use_global_device_ids=true | all-gather | bytes 73728 | tf_op jit(solution)/shard_map/all_gather | solution.py:442
  121.3 4.6 %key_side.1 = bf16[832,128]{1,0:T(8,128)(2,1)S(1)} custom-call(s32[2]{0:T(128)S(1)} %pad_add_fusion.place_ref, bf16[8,560,128]{2,1,0:T(8,128)(2,1)S(1)} %all_to_all.5.recv_ref, bf16[560,128]{1,0:T(8,128)(2,1)S(1)} %get-tuple-element.12.own_ref, bf16[256,32]{1,0:T(8,128)(2,1)S(1)} %get-tuple-element.13.feat_ref, f32[256,1]{1,0:T(8,128)S(1)} %get-tuple-element.14.cum_ref, ...), custom_call_target="tpu_custom_call" | custom-call | flops 1000000000 | bytes 2097152 | tf_op jit(solution)/shard_map/key_side/pallas_call | solution.py:443
  125.9 18.4 %all-gather.1 = bf16[3328,128]{1,0:T(8,128)(2,1)S(1)} all-gather(bf16[832,128]{1,0:T(8,128)(2,1)S(1)} %key_side.1), channel_id=3, replica_groups=mesh['chip'=4,'core'=2,'tp'=4] {'tp'}, dimensions={0}, use_global_device_ids=true | all-gather | bytes 1064960 | tf_op jit(solution)/shard_map/all_gather | solution.py:454
  144.3 0.0 collective-permute-done.oq_ref.ok_ref.ov_ref.of_ref
  144.3 0.0 copy-start.5
  144.3 1.8 %copy-done.5 = bf16[4,3328,128]{2,1,0:T(8,128)(2,1)} copy-done((bf16[4,3328,128]{2,1,0:T(8,128)(2,1)}, bf16[4,3328,128]{2,1,0:T(8,128)(2,1)S(1)}, u32[]{:S(2)}) %copy-start.5) | copy-done | bytes 3407896
  146.1 0.0 copy-done
  146.1 8.0 %head_sum.1 = bf16[256,2048]{1,0:T(8,128)(2,1)} custom-call(s32[2]{0:T(128)S(1)} %pad_add_fusion.place_ref, bf16[4,832,128]{2,1,0:T(8,128)(2,1)S(1)} %bitcast.10, bf16[4,3328,128]{2,1,0:T(8,128)(2,1)S(1)} %bitcast.6, bf16[4,3328,128]{2,1,0:T(8,128)(2,1)S(1)} %bitcast.7, bf16[4,3328,128]{2,1,0:T(8,128)(2,1)S(1)} %bitcast.8, ...), custom_call_target="tpu_custom_call" | custom-call | flops 1744830464 | bytes 6815744 | tf_op jit(solution)/shard_map/head_sum/pallas_call | solution.py:374
Async XLA Ops:
  7.2 80.0 %all-gather.5.cloned.1.call-start = ((), (), s32[]{:S(2)}) async-start(), calls=%async_computation.1 | async-start | bytes 4259840 | tf_op jit(solution)/shard_map/all_gather | solution.py:423
  9.3 1.2 copy-start.1
  10.5 1.2 copy-start.2
  11.8 1.0 copy-start.3
  12.8 0.8 copy-start.4
  87.2 57.1 %collective-permute-start = (bf16[4,3328,128]{2,1,0:T(8,128)(2,1)}, bf16[4,3328,128]{2,1,0:T(8,128)(2,1)S(1)}, u32[]{:S(2)}, u32[]{:S(2)}) collective-permute-start(bf16[4,3328,128]{2,1,0:T(8,128)(2,1)} %bitcast.5), channel_id=1, source_target_pairs={{0,4},{4,0},{1,5},{5,1},{2,6},{6,2},{3,7},{7,3},{8,12},{12,8},{9,1... | collective-permute-start | bytes 10223624 | tf_op jit(solution)/shard_map/ppermute | solution.py:455
  107.1 38.9 %copy-start = (bf16[13312,128]{1,0:T(8,128)(2,1)S(1)}, bf16[13312,128]{1,0:T(8,128)(2,1)}, u32[]{:S(2)}) copy-start(bf16[13312,128]{1,0:T(8,128)(2,1)} %all-gather.5.cloned.1.call-done) | copy-start | bytes 10223620
  144.3 1.8 %copy-start.5 = (bf16[4,3328,128]{2,1,0:T(8,128)(2,1)}, bf16[4,3328,128]{2,1,0:T(8,128)(2,1)S(1)}, u32[]{:S(2)}) copy-start(bf16[4,3328,128]{2,1,0:T(8,128)(2,1)S(1)} %collective-permute-done.oq_ref.ok_ref.ov_ref.of_ref) | copy-start | bytes 10223620
Sparse Core Ops, SparseCore 0:
  16.6 70.5 all-gather.4

commit v2 on v1

v2 whole, which is shorter than its diff:
```python
import jax
import jax.numpy as jnp
from jax import lax
from jax.experimental import pallas as pl
from jax.experimental.pallas import tpu as pltpu
from jax.sharding import Mesh
from jax.sharding import PartitionSpec as P

WINDOW = 1024
LANES = 128
MASKED = -1e30
CTX = ("chip", "core")
CHUNKS = 4
f32 = jnp.float32
bf16 = jnp.bfloat16


def nn(a, b):
    return lax.dot_general(a, b, (((1,), (0,)), ((), ())), preferred_element_type=f32)


def nt(a, b):
    return lax.dot_general(a, b, (((1,), (1,)), ((), ())), preferred_element_type=f32)


def partner(me, d, count):
    assert count & (count - 1) == 0
    return jnp.bitwise_xor(me, d)


def wide(view, start, count):
    return jnp.concatenate(
        [view[start : start + count, :], view[start + count : start + 2 * count, :]], axis=1
    )


def put_wide(ref, start, value):
    count = value.shape[0]
    for half in range(value.shape[1] // LANES):
        ref[start + half * count : start + (half + 1) * count, :] = value[
            :, half * LANES : (half + 1) * LANES
        ]


def cum_row(view, start):
    tail = view[start : start + 16, :].astype(f32)
    first = tail[0:1] + tail[2:3] + tail[4:5]
    second = tail[1:2] + tail[3:4] + tail[5:6]
    return jnp.concatenate([first, second], axis=1)


def iotas(rows):
    return (
        lax.broadcasted_iota(jnp.int32, (rows, rows), 0),
        lax.broadcasted_iota(jnp.int32, (rows, rows), 1),
    )


def project_kernel(place_ref, tok_hbm, fw_hbm, ww_hbm, vw_hbm, ld_hbm, do_hbm, *rest):
    *sends, keys_ref, query_ref, feat_ref, cum_ref, pack_ref = rest[:-8]
    tok_ref, fw_ref, ww_ref, vw_ref, ld_ref, do_ref, sems, small = rest[-8:]
    me, piece = place_ref[0], place_ref[1]
    rows, dim = tok_ref.shape
    dh = do_ref.shape[1]
    nf = fw_ref.shape[0] // 2
    count = len(sends) + 1
    span = dim // CHUNKS
    copies = []
    for c in range(CHUNKS):
        part = pl.ds(c * span, span)
        copies.append([
            pltpu.make_async_copy(tok_hbm.at[:, part], tok_ref.at[:, part], sems.at[c, 0]),
            pltpu.make_async_copy(ww_hbm.at[part, :], ww_ref.at[part, :], sems.at[c, 1]),
            pltpu.make_async_copy(vw_hbm.at[part, :], vw_ref.at[part, :], sems.at[c, 2]),
            pltpu.make_async_copy(fw_hbm.at[:, part], fw_ref.at[:, part], sems.at[c, 3]),
        ])
    others = [
        pltpu.make_async_copy(ld_hbm, ld_ref, small.at[0]),
        pltpu.make_async_copy(do_hbm, do_ref, small.at[1]),
    ]
    for copy in copies[0] + others:
        copy.start()
    for group in copies[1:]:
        for copy in group:
            copy.start()
    for copy in others:
        copy.wait()
    at_row, at_col = iotas(rows)
    ld_r = ld_ref[...]
    ld_c = jnp.sum(jnp.where(at_row == at_col, ld_r, 0.0), axis=1, keepdims=True)
    cum_r = jnp.sum(jnp.where(at_row <= at_col, ld_c, 0.0), axis=0, keepdims=True)
    cum_ref[...] = jnp.sum(jnp.where(at_col <= at_row, ld_r, 0.0), axis=1, keepdims=True)
    high = cum_r.astype(bf16)
    left = cum_r - high.astype(f32)
    mid = left.astype(bf16)
    low = (left - mid.astype(f32)).astype(bf16)
    pieces = [t[:, h : h + LANES].astype(f32) for t in (high, mid, low) for h in range(0, rows, LANES)]
    tail = jnp.concatenate(pieces + [jnp.zeros((10, LANES), f32)], axis=0).astype(bf16)

    feat = jnp.zeros((rows, 2 * nf), f32)
    window = jnp.zeros((rows, 2 * dh), f32)
    values = jnp.zeros((rows, dh), f32)
    for c in range(CHUNKS):
        for copy in copies[c]:
            copy.wait()
        part = slice(c * span, (c + 1) * span)
        tok = tok_ref[:, part]
        feat += nt(tok, fw_ref[:, part])
        window += nn(tok, ww_ref[part, :])
        values += nn(tok, vw_ref[part, :])
    feat = feat.astype(bf16)
    window = window.astype(bf16)
    values = values.astype(bf16)
    feat_ref[...] = feat
    small_row, small_col = iotas(2 * nf)
    feat_t = nt((small_row == small_col).astype(bf16), feat).astype(bf16)
    feat_at = 2 * rows
    tail_at = feat_at + 2 * nf

    def put_keys(ref):
        ref[0:rows, :] = window[:, dh:]
        ref[rows : 2 * rows, :] = values
        put_wide(ref, feat_at, feat_t[nf:, :])
        ref[tail_at : tail_at + 16, :] = tail

    def put_query(ref):
        ref[0:rows, :] = window[:, :dh]
        ref[rows : 2 * rows, :] = do_ref[...]
        put_wide(ref, feat_at, feat_t[:nf, :])
        ref[tail_at : tail_at + 16, :] = tail

    put_keys(keys_ref)
    put_query(query_ref)
    for d in range(1, count):
        later = partner(me, d, count) > me
        ref = sends[d - 1]
        pl.when(later)(lambda ref=ref: put_keys(ref))
        pl.when(jnp.logical_not(later))(lambda ref=ref: put_query(ref))

    tile = pack_ref.shape[2]
    for p in range(pack_ref.shape[0]):
        at = pl.multiple_of((piece + p) * tile, tile)
        part = pl.ds(at, tile)
        pack_ref[p, 0 : 2 * dh, :] = jnp.transpose(ww_ref[part, :].astype(f32)).astype(bf16)
        pack_ref[p, 2 * dh : 3 * dh, :] = jnp.transpose(vw_ref[part, :].astype(f32)).astype(bf16)
        pack_ref[p, 3 * dh : 3 * dh + 2 * nf, :] = fw_ref[:, part]


def between(totals, low, high):
    at = lax.broadcasted_iota(jnp.int32, totals.shape, 0)
    return jnp.sum(jnp.where((at > low) & (at < high), totals, 0.0), axis=0, keepdims=True)


def over_partners(count, body, carry):
    if count <= 8:
        for d in range(1, count):
            carry = body(d, carry)
        return carry
    return lax.fori_loop(1, count, body, carry)


def query_kernel(count, place_ref, *rest):
    recvs = rest[: -10]
    (own_ref, query_ref, feat_ref, cum_ref, att_ref, stat_ref, sheet_ref, near_ref, p_ref,
     cums_ref) = rest[-10:]

    def recv(d):
        return recvs[d - 1] if len(recvs) > 1 else recvs[0].at[d - 1]

    me = place_ref[0]
    rows, dh = att_ref.shape
    nf = feat_ref.shape[1] // 2
    back = WINDOW // rows
    feat_at = 2 * rows
    tail_at = feat_at + 2 * nf
    scale = dh ** (-0.5)
    feat_scale = nf ** (-0.5)
    wq = query_ref[0:rows, :]
    do = query_ref[rows : 2 * rows, :]
    q = feat_ref[:, :nf]
    at_row, at_col = iotas(rows)
    own_cum = cum_row(own_ref, tail_at)
    cums_ref[pl.ds(me, 1), :] = own_cum
    near_ref[me] = own_ref[0 : 2 * rows, :]

    def gather(d, carry):
        j = partner(me, d, count)
        view = recv(d)
        near_ref[j] = view[0 : 2 * rows, :]
        cums_ref[pl.ds(j, 1), :] = cum_row(view, tail_at)
        return carry

    over_partners(count, gather, 0)

    def near(w):
        return near_ref.at[jnp.maximum(me - back + w, 0)]

    top = jnp.full((rows, LANES), MASKED, f32)
    for w in range(back + 1):
        keys = own_ref[0:rows, :] if w == back else near(w)[0:rows, :]
        s = nt(wq, keys) * scale
        if w == back:
            s = jnp.where(at_col <= at_row, s, MASKED)
        elif w == 0:
            s = jnp.where((at_col > at_row) & (me >= back), s, MASKED)
        else:
            s = jnp.where(me >= back - w, s, MASKED)
        p_ref[w] = s
        for h in range(0, rows, LANES):
            top = jnp.maximum(top, s[:, h : h + LANES])
    top = jnp.max(top, axis=1, keepdims=True)
    total = jnp.zeros((rows, LANES), f32)
    out = jnp.zeros((rows, dh), f32)
    for w in range(back + 1):
        p = jnp.exp(p_ref[w] - top)
        for h in range(0, rows, LANES):
            total += p[:, h : h + LANES]
        vals = own_ref[rows : 2 * rows, :] if w == back else near(w)[rows : 2 * rows, :]
        out += nn(p.astype(bf16), vals)
    total = jnp.sum(total, axis=1, keepdims=True)
    windowed = out * (1.0 / total)

    cum_c = cum_ref[...]
    growth = jnp.exp(cum_c)
    totals = cums_ref[:, rows - 1 : rows]

    def forward(d, carry):
        num, den = carry
        j = partner(me, d, count)
        view = recv(d)
        gap = between(totals, j - 1, me)
        es = jnp.where(j < me, jnp.exp(jnp.minimum(gap - cums_ref[pl.ds(j, 1), :], 0.0)), 0.0)
        x = nn(q, wide(view, feat_at, nf)) * feat_scale
        weight = (1.0 + x + 0.5 * x * x) * es
        for h in range(0, rows, LANES):
            den += weight[:, h : h + LANES]
        num += nn(weight.astype(bf16), view[rows : 2 * rows, :])
        return num, den

    num, den = over_partners(
        count, forward, (jnp.zeros((rows, dh), f32), jnp.zeros((rows, LANES), f32))
    )
    x = nn(q, wide(own_ref, feat_at, nf)) * feat_scale
    e = jnp.where(at_col <= at_row, jnp.exp(jnp.minimum(cum_c - own_cum, 0.0)), 0.0)
    weight = (1.0 + x + 0.5 * x * x) * e
    num = num * growth + nn(weight.astype(bf16), own_ref[rows : 2 * rows, :])
    den = den * growth
    for h in range(0, rows, LANES):
        den += weight[:, h : h + LANES]
    rden = 1.0 / jnp.sum(den, axis=1, keepdims=True)
    linear = num * rden
    att_ref[...] = (linear + windowed).astype(bf16)
    do_f = do.astype(f32)
    delta_w = jnp.sum(do_f * windowed, axis=1, keepdims=True)
    delta_l = jnp.sum(do_f * linear, axis=1, keepdims=True)
    lse = top + jnp.log(total)
    lane = lax.broadcasted_iota(jnp.int32, (rows, LANES), 1)
    sheet = jnp.where(lane == 0, lse, 0.0)
    sheet = jnp.where(lane == 1, delta_w, sheet)
    sheet = jnp.where(lane == 2, rden, sheet)
    sheet = jnp.where(lane == 3, delta_l, sheet)
    sheet = jnp.where(lane == 4, cum_c, sheet)
    sheet_ref[...] = sheet
    stat_ref[...] = jnp.transpose(sheet)[0:8, :]


def gradient_kernel(count, place_ref, *rest):
    recvs = rest[:-6]
    own_ref, query_ref, feat_ref, sheet_ref, stat_ref, grad_ref = rest[-6:]

    def recv(d):
        return recvs[d - 1] if len(recvs) > 1 else recvs[0].at[d - 1]

    me = place_ref[0]
    rows = feat_ref.shape[0]
    dh = LANES
    nf = feat_ref.shape[1] // 2
    feat_at = 2 * rows
    scale = dh ** (-0.5)
    feat_scale = nf ** (-0.5)
    at_row, at_col = iotas(rows)
    apart = at_row - at_col
    wq, wk = query_ref[0:rows, :], own_ref[0:rows, :]
    do, v = query_ref[rows : 2 * rows, :], own_ref[rows : 2 * rows, :]
    q, k = feat_ref[:, :nf], feat_ref[:, nf:]
    lse_c, dw_c = sheet_ref[:, 0:1], sheet_ref[:, 1:2]
    rden_c, dl_c, cum_c = sheet_ref[:, 2:3], sheet_ref[:, 3:4], sheet_ref[:, 4:5]
    totals = jnp.concatenate([stat_ref[j, 4:5, rows - 1 : rows] for j in range(count)], axis=0)
    own_cum = stat_ref[me, 4:5, :]
    growth_c = jnp.exp(cum_c) * rden_c
    tail_c = jnp.exp(own_cum[:, rows - 1 : rows] - cum_c)

    def pick(flag, a, b):
        return jnp.where(flag, a, b)

    s = nt(wq, wk) * scale
    causal = at_col <= at_row
    p = jnp.where(causal, jnp.exp(s - lse_c), 0.0)
    dp = nt(do, v)
    dwq = nn((p * (dp - dw_c)).astype(bf16), wk)
    x = nn(q, wide(own_ref, feat_at, nf)) * feat_scale
    e = jnp.where(causal, jnp.exp(jnp.minimum(cum_c - own_cum, 0.0)), 0.0) * rden_c
    dx = (dp - dl_c) * e * (1.0 + x)
    dqt = nt(wide(own_ref, feat_at, nf), dx.astype(bf16))

    s = nt(wk, wq) * scale
    causal = at_row <= at_col
    p = jnp.where(causal, jnp.exp(s - stat_ref[me, 0:1, :]), 0.0)
    dp = nt(v, do)
    dwk = nn((p * (dp - stat_ref[me, 1:2, :])).astype(bf16), wq)
    x = nn(k, wide(query_ref, feat_at, nf)) * feat_scale
    e = jnp.where(causal, jnp.exp(jnp.minimum(own_cum - cum_c, 0.0)), 0.0) * stat_ref[me, 2:3, :]
    dx = (dp - stat_ref[me, 3:4, :]) * e * (1.0 + x)
    dkt = nt(wide(query_ref, feat_at, nf), dx.astype(bf16))
    dv = nn((p + (1.0 + x + 0.5 * x * x) * e).astype(bf16), do)

    def step(d, carry):
        dwq, dqt, dwk, dkt, dv = carry
        j = partner(me, d, count)
        view = recv(d)
        mine = j < me
        sign = pick(mine, 1, -1)
        limit = WINDOW - jnp.abs(me - j) * rows
        rows_w = pick(mine, wq, wk)
        rows_v = pick(mine, do, v)
        rows_f = pick(mine, q, k)
        other_w = view[0:rows, :]
        other_v = view[rows : 2 * rows, :]
        other_f = wide(view, feat_at, nf)
        st = stat_ref[j]
        zero = jnp.zeros((1, rows), f32)
        cum = st[4:5, :]
        gap = between(totals, jnp.minimum(me, j), jnp.maximum(me, j))
        e_r = jnp.exp(jnp.minimum(gap + pick(mine, cum[:, rows - 1 : rows] - cum, cum), 0.0))
        e_r = e_r * pick(mine, 1.0, st[2:3, :])
        e_c = pick(mine, growth_c, tail_c)

        s = nt(rows_w, other_w) * scale
        p = jnp.exp(s - pick(mine, lse_c, 0.0) - pick(mine, zero, st[0:1, :]))
        p = jnp.where(apart * sign < limit, p, 0.0)
        dp = nt(rows_v, other_v)
        ds = p * (dp - pick(mine, dw_c, 0.0) - pick(mine, zero, st[1:2, :]))
        more_w = nn(ds.astype(bf16), other_w)
        x = nn(rows_f, other_f) * feat_scale
        e = e_r * e_c
        dx = (dp - pick(mine, dl_c, 0.0) - pick(mine, zero, st[3:4, :])) * e * (1.0 + x)
        more_f = nt(other_f, dx.astype(bf16))
        more_v = nn((p + (1.0 + x + 0.5 * x * x) * e).astype(bf16), other_v)
        dwq = dwq + pick(mine, more_w, 0.0)
        dwk = dwk + pick(mine, 0.0, more_w)
        dqt = dqt + pick(mine, more_f, 0.0)
        dkt = dkt + pick(mine, 0.0, more_f)
        dv = dv + pick(mine, 0.0, more_v)
        return dwq, dqt, dwk, dkt, dv

    dwq, dqt, dwk, dkt, dv = over_partners(count, step, (dwq, dqt, dwk, dkt, dv))
    grad_ref[0:rows, :] = (dwq * scale).astype(bf16)
    grad_ref[rows : 2 * rows, :] = (dwk * scale).astype(bf16)
    grad_ref[2 * rows : 3 * rows, :] = dv.astype(bf16)
    dft = (jnp.concatenate([dqt, dkt], axis=0) * feat_scale).astype(bf16)
    put_wide(grad_ref, 3 * rows, dft)


def merge_kernel(grad_ref, *rest):
    heads = grad_ref.shape[0]
    weights, out_ref, cat_ref, feat_ref = rest[:heads], rest[-3], rest[-2], rest[-1]
    rows = out_ref.shape[0]
    lanes = 3 * LANES
    nf2 = weights[0].shape[-2] - lanes

    @pl.when(pl.program_id(0) == 0)
    def _():
        for h in range(heads):
            for part in range(3):
                at = (3 * h + part) * LANES
                cat_ref[:, at : at + LANES] = grad_ref[h, part * rows : (part + 1) * rows, :]
        dft = jnp.concatenate([wide(grad_ref.at[h], 3 * rows, nf2) for h in range(heads)], axis=0)
        feat_ref[...] = jnp.transpose(dft.astype(f32)).astype(bf16)

    main = jnp.concatenate([w[0, 0, 0:lanes, :] for w in weights], axis=0)
    feats = jnp.concatenate([w[0, 0, lanes:, :] for w in weights], axis=0)
    out_ref[...] = (nn(cat_ref[...], main) + nn(feat_ref[...], feats)).astype(bf16)


VMEM = pl.BlockSpec(memory_space=pltpu.VMEM)
SMEM = pl.BlockSpec(memory_space=pltpu.SMEM)
ANY = pl.BlockSpec(memory_space=pl.ANY)
params = pltpu.CompilerParams(vmem_limit_bytes=48 * 1024 * 1024)


def cost(flops, nbytes, exps=0):
    return pl.CostEstimate(flops=flops, bytes_accessed=nbytes, transcendentals=exps)


def merge(grads, weights, by_head, rows, dim):
    heads = grads.shape[0]
    columns, tile = weights.shape[2:]
    pieces = dim // tile

    def at(h):
        return (lambda i: (h, i, 0, 0)) if by_head else (lambda i: (i, h, 0, 0))

    specs = [pl.BlockSpec(grads.shape, lambda i: (0, 0, 0))]
    specs += [pl.BlockSpec((1, 1, columns, tile), at(h)) for h in range(heads)]
    return pl.pallas_call(
        merge_kernel,
        out_shape=jax.ShapeDtypeStruct((rows, dim), bf16),
        grid=(pieces,),
        in_specs=specs,
        out_specs=pl.BlockSpec((rows, tile), lambda i: (0, i)),
        scratch_shapes=[
            pltpu.VMEM((rows, 3 * LANES * heads), bf16),
            pltpu.VMEM((rows, (columns - 3 * LANES) * heads), bf16),
        ],
        compiler_params=params,
        cost_estimate=cost(2 * rows * dim * heads * columns, heads * dim * columns * 2),
        name="head_sum",
    )(grads, *([weights] * heads))


def per_device(tokens, feature_weight, window_weight, value_weight, log_decay, out_grad):
    rows, dim = tokens.shape
    nf2 = feature_weight.shape[1]
    nf = nf2 // 2
    dh = value_weight.shape[1]
    columns = 3 * dh + nf2
    count = lax.axis_size(CTX)
    me = lax.axis_index(CTX)
    tile = 2 * LANES
    spread = count * tile == dim
    pieces = 1 if spread else dim // tile
    place = jnp.stack([me, me if spread else 0 * me]).astype(jnp.int32)
    payload = 2 * rows + 2 * nf + 16
    block = jax.ShapeDtypeStruct((payload, LANES), bf16)
    *sends, own, query, feat, cum, packed = pl.pallas_call(
        project_kernel,
        out_shape=[block] * (count + 1)
        + [
            jax.ShapeDtypeStruct((rows, nf2), bf16),
            jax.ShapeDtypeStruct((rows, 1), f32),
            jax.ShapeDtypeStruct((pieces, columns, tile), bf16),
        ],
        in_specs=[SMEM] + [ANY] * 6,
        out_specs=[VMEM] * (count + 4),
        scratch_shapes=[
            pltpu.VMEM((rows, dim), bf16),
            pltpu.VMEM((nf2, dim), bf16),
            pltpu.VMEM((dim, 2 * dh), bf16),
            pltpu.VMEM((dim, dh), bf16),
            pltpu.VMEM((1, rows), f32),
            pltpu.VMEM((rows, dh), bf16),
            pltpu.SemaphoreType.DMA((CHUNKS, 4)),
            pltpu.SemaphoreType.DMA((2,)),
        ],
        compiler_params=params,
        cost_estimate=cost(2 * rows * dim * columns, 4 * 1024 * 1024),
        name="project",
    )(place, tokens, feature_weight.T, window_weight, value_weight, log_decay.T, out_grad)
    if spread:
        weights = lax.all_gather(packed[0], CTX + ("tp",)).reshape(count, -1, columns, tile)
    else:
        weights = lax.all_gather(packed, "tp")

    recv = []
    for d in range(1, count):
        recv.append(lax.ppermute(sends[d - 1], CTX, [(i, i ^ d) for i in range(count)]))
    if count > 8:
        recv = [jnp.stack(recv)]

    attended, stat, sheet = pl.pallas_call(
        lambda *refs: query_kernel(count, *refs),
        out_shape=(
            jax.ShapeDtypeStruct((rows, dh), bf16),
            jax.ShapeDtypeStruct((8, rows), f32),
            jax.ShapeDtypeStruct((rows, LANES), f32),
        ),
        in_specs=[SMEM] + [VMEM] * (len(recv) + 4),
        out_specs=[VMEM] * 3,
        scratch_shapes=[
            pltpu.VMEM((count, 2 * rows, dh), bf16),
            pltpu.VMEM((WINDOW // rows + 1, rows, rows), f32),
            pltpu.VMEM((count, rows), f32),
        ],
        compiler_params=params,
        cost_estimate=cost(10**9, 2 * 1024 * 1024, 10**6),
        name="query_side",
    )(place, *recv, own, query, feat, cum)
    stats = lax.all_gather(stat, CTX)
    grads = pl.pallas_call(
        lambda *refs: gradient_kernel(count, *refs),
        out_shape=jax.ShapeDtypeStruct((3 * rows + nf2 * rows // LANES, LANES), bf16),
        in_specs=[SMEM] + [VMEM] * (len(recv) + 5),
        out_specs=VMEM,
        compiler_params=params,
        cost_estimate=cost(10**9, 2 * 1024 * 1024, 10**6),
        name="gradients",
    )(place, *recv, own, query, feat, sheet, stats)
    all_grads = lax.all_gather(grads, "tp")
    return (attended, merge(all_grads, weights, not spread, rows, dim))


def solution(mesh):
    ctx, tp = mesh.devices.shape
    split = Mesh(mesh.devices.reshape(ctx // 2, 2, tp), ("chip", "core", "tp"))
    in_specs = (
        P(CTX, None),
        P(None, "tp"),
        P(None, "tp"),
        P(None, "tp"),
        P(CTX, "tp"),
        P(CTX, "tp"),
    )
    out_specs = (P(CTX, "tp"), P(CTX, None))
    return jax.shard_map(
        per_device, mesh=split, in_specs=in_specs, out_specs=out_specs, check_vma=False
    )
```

time: 161 us -> 116 us (0.72)
  waiting for transfers between devices: 70.7 us -> 32.4 us
  blocking collectives: 49.7 us -> 34.3 us
  starting transfers between devices: 0.04 us -> 9.28 us
  local copies, waits for them, and re-layouts: 8.1 us -> 5.91 us
    all_gather x1, waiting for transfers between devices: 70.7 us -> 22.5 us  [per_device(): lax.all_gather(packed[0], CTX + ('tp',)).reshape(count, -1, columns, tile)]
    all_to_all x1 -> x0, blocking collectives: 20 us -> none  [per_device(): recv = lax.all_to_all(send, CTX, 0, 0, tiled=True)]
    ppermute x1 -> x7, waiting for transfers between devices: 0.01 us -> 9.92 us  [per_device(): lax.ppermute(sends[d - 1], CTX, [(i, i ^ d) for i in range(count)])]
    ppermute x1 -> x7, starting transfers between devices: 0.01 us -> 9.25 us  [per_device(): lax.ppermute(sends[d - 1], CTX, [(i, i ^ d) for i in range(count)])]
    all_gather x1, blocking collectives: 18.4 us -> 24.7 us  [per_device(): all_grads = lax.all_gather(grads, 'tp')]
    unnamed x14 -> x12, local copies, waits for them, and re-layouts: 8.1 us -> 5.91 us
    all_gather x1, blocking collectives: 11.3 us -> 9.67 us  [per_device(): stats = lax.all_gather(stat, CTX)]
  transfers between devices with their start and end apart: 2 -> 8, of which waited for: 1 -> 4; matrix products, arithmetic and copies ran while one was open for 0% -> 0% of each run, Pallas kernels for 5% -> 6%
where the time goes in v2:
time: 116 us; the launch traced here: 115 us
  blocking collectives  34.3 us (30%)
  waiting for transfers between devices  32.4 us (28%)
  Pallas kernels  19.3 us (17%)
  between operations  14.1 us (12%)
  starting transfers between devices  9.28 us (8%)
  local copies, waits for them, and re-layouts  5.91 us (5%)
    all_gather x1, blocking collectives, per_device(): all_grads = lax.all_gather(grads, 'tp')  24.7 us
    all_gather x1, waiting for transfers between devices, per_device(): lax.all_gather(packed[0], CTX + ('tp',)).reshape(count, -1, columns, tile)  22.5 us
    ppermute x7, waiting for transfers between devices, per_device(): lax.ppermute(sends[d - 1], CTX, [(i, i ^ d) for i in range(count)])  9.92 us
    all_gather x1, blocking collectives, per_device(): stats = lax.all_gather(stat, CTX)  9.67 us
    ppermute x7, starting transfers between devices, per_device(): lax.ppermute(sends[d - 1], CTX, [(i, i ^ d) for i in range(count)])  9.25 us
    pallas_call x1, Pallas kernels, merge(): pl.pallas_call(merge_kernel, out_shape=jax.ShapeDtypeStruct((rows, dim),...  8.02 us
    unnamed x12, local copies, waits for them, and re-layouts  5.91 us
    pallas_call x1, Pallas kernels, per_device(): pl.pallas_call(lambda *refs: gradient_kernel(count, *refs), out_shape=jax...  4.18 us
  transfers between devices with their start and end apart: 8, of which 4 were waited for; matrix products, arithmetic and copies ran while one was open for 0% of the time, Pallas kernels for 6%

profile of v2, /device:TPU:0, one launch (start us, length us, event | category | flops | bytes accessed | tf_op | source)
XLA Modules:
  0.0 115.3 jit_solution(2069060290839273364)
XLA Ops:
  7.2 0.0 all-gather.4.cloned.1.call-start
  7.2 0.1 pad_add_fusion.place_ref.refs_0_
  7.3 0.0 copy-start
  7.3 1.2 %copy-done = bf16[256,2048]{1,0:T(8,128)(2,1)S(1)} copy-done((bf16[256,2048]{1,0:T(8,128)(2,1)S(1)}, bf16[256,2048]{1,0:T(8,128)(2,1)}, u32[]{:S(2)}) %copy-start) | copy-done | bytes 1048600
  8.5 0.0 copy-start.1
  8.5 1.2 %copy-done.1 = bf16[2048,256]{1,0:T(8,128)(2,1)S(1)} copy-done((bf16[2048,256]{1,0:T(8,128)(2,1)S(1)}, bf16[2048,256]{1,0:T(8,128)(2,1)}, u32[]{:S(2)}) %copy-start.1) | copy-done | bytes 1048600
  9.7 0.0 copy-start.2
  9.7 1.0 copy-done.2
  10.8 0.0 copy-start.3
  10.8 0.9 copy-done.3
  11.7 0.0 copy-start.4
  11.7 0.8 copy-done.4
  12.5 0.0 copy-start.5
  12.5 0.7 copy-done.5
  13.2 4.1 %project.1 = (bf16[560,128]{1,0:T(8,128)(2,1)S(1)}, bf16[560,128]{1,0:T(8,128)(2,1)S(1)}, bf16[560,128]{1,0:T(8,128)(2,1)S(1)}, bf16[560,128]{1,0:T(8,128)(2,1)S...) custom-call(s32[2]{0:T(128)S(1)} %pad_add_fusion.place_ref.refs_0_, ...), custom_call_target="tpu_custom_call" | custom-call | flops 436207616 | bytes 4194304 | tf_op jit(solution)/shard_map/project/pallas_call | solution.py:435
  17.4 0.0 all-gather.4.cloned.1.call-update
  17.4 0.5 collective-permute-start
  17.9 2.5 %collective-permute-start.1 = (bf16[560,128]{1,0:T(8,128)(2,1)S(1)}, bf16[560,128]{1,0:T(8,128)(2,1)S(1)}, u32[]{:S(2)}, u32[]{:S(2)}) collective-permute-start(bf16[560,128]{1,0:T(8,128)(2,1)S(1)} %get-tuple-element.18), channel_id=1, source_target_pairs={{0,8},{4,12},{8,0},{12,4},{16,24},{20,28},{24,16},{28,20},{1,9},{5... | collective-permute-start | bytes 430088 | tf_op jit(solution)/shard_map/ppermute | solution.py:466
  20.5 0.1 collective-permute-start.2
  20.5 1.8 %collective-permute-start.3 = (bf16[560,128]{1,0:T(8,128)(2,1)S(1)}, bf16[560,128]{1,0:T(8,128)(2,1)S(1)}, u32[]{:S(2)}, u32[]{:S(2)}) collective-permute-start(bf16[560,128]{1,0:T(8,128)(2,1)S(1)} %get-tuple-element.20), channel_id=1, source_target_pairs={{0,16},{4,20},{8,24},{12,28},{16,0},{20,4},{24,8},{28,12},{1,17},{... | collective-permute-start | bytes 430088 | tf_op jit(solution)/shard_map/ppermute | solution.py:466
  22.3 0.0 collective-permute-start.4
  22.3 0.0 collective-permute-done.refs_1_
  22.3 2.6 %collective-permute-start.5 = (bf16[560,128]{1,0:T(8,128)(2,1)S(1)}, bf16[560,128]{1,0:T(8,128)(2,1)S(1)}, u32[]{:S(2)}, u32[]{:S(2)}) collective-permute-start(bf16[560,128]{1,0:T(8,128)(2,1)S(1)} %get-tuple-element.22), channel_id=1, source_target_pairs={{0,24},{4,28},{8,16},{12,20},{16,8},{20,12},{24,0},{28,4},{1,25},{... | collective-permute-start | bytes 430088 | tf_op jit(solution)/shard_map/ppermute | solution.py:466
  24.9 0.2 collective-permute-done.1.refs_2_
  25.1 1.7 %collective-permute-start.6 = (bf16[560,128]{1,0:T(8,128)(2,1)S(1)}, bf16[560,128]{1,0:T(8,128)(2,1)S(1)}, u32[]{:S(2)}, u32[]{:S(2)}) collective-permute-start(bf16[560,128]{1,0:T(8,128)(2,1)S(1)} %get-tuple-element.23), channel_id=1, source_target_pairs={{0,28},{4,24},{8,20},{12,16},{16,12},{20,8},{24,4},{28,0},{1,29},{... | collective-permute-start | bytes 430088 | tf_op jit(solution)/shard_map/ppermute | solution.py:466
  26.8 0.8 collective-permute-done.2.refs_3_
  27.6 0.0 collective-permute-done.3.refs_4_
  27.6 8.9 %collective-permute-done.4.refs_5_ = bf16[560,128]{1,0:T(8,128)(2,1)S(1)} collective-permute-done((bf16[560,128]{1,0:T(8,128)(2,1)S(1)}, bf16[560,128]{1,0:T(8,128)(2,1)S(1)}, u32[]{:S(2)}, u32[]{:S(2)}) %collective-permute-start.4) | collective-permute-done | bytes 143392 | tf_op jit(solution)/shard_map/ppermute | solution.py:466
  36.6 0.0 collective-permute-done.5.refs_6_
  36.6 0.0 collective-permute-done.6.refs_7_
  36.6 2.9 %query_side.1 = (bf16[256,128]{1,0:T(8,128)(2,1)}, f32[8,256]{1,0:T(8,128)S(1)}, f32[256,128]{1,0:T(8,128)S(1)}) custom-call(s32[2]{0:T(128)S(1)} %pad_add_fusion.place_ref.refs_0_, bf16[560,128]{1,0:T(8,128)(2,1)S(1)} %collective-permute-done.refs_1_, bf16[560,128]{1,0:T(8,128)(2,1)S(1)} %collective-permute-done.1.refs_2_, ...), custom_call_target="tpu_custom_call" | custom-call | flops 1000000000 | bytes 2097152 | tf_op jit(solution)/shard_map/query_side/pallas_call | solution.py:470
  39.5 9.7 %all-gather = f32[64,256]{1,0:T(8,128)S(1)} all-gather(f32[8,256]{1,0:T(8,128)S(1)} %get-tuple-element.30), channel_id=2, replica_groups=mesh['chip'=4,'core'=2,'tp'=4] {'chip','core'}, dimensions={0}, use_global_device_ids=true | all-gather | bytes 73728 | tf_op jit(solution)/shard_map/all_gather | solution.py:488
  49.1 4.2 %gradients.1 = bf16[832,128]{1,0:T(8,128)(2,1)S(1)} custom-call(s32[2]{0:T(128)S(1)} %pad_add_fusion.place_ref.refs_0_, bf16[560,128]{1,0:T(8,128)(2,1)S(1)} %collective-permute-done.refs_1_, bf16[560,128]{1,0:T(8,128)(2,1)S(1)} %collective-permute-done.1.refs_2_, bf16[560,128]{1,0:T(8,128)(2,1)S(1)} %collective-permute-done.2.refs_3_, ...), custom_call_target="tpu_custom_call" | custom-call | flops 1000000000 | bytes 2097152 | tf_op jit(solution)/shard_map/gradients/pallas_call | solution.py:489
  53.3 24.7 %all-gather.1 = bf16[3328,128]{1,0:T(8,128)(2,1)S(1)} all-gather(bf16[832,128]{1,0:T(8,128)(2,1)S(1)} %gradients.1), channel_id=3, replica_groups=mesh['chip'=4,'core'=2,'tp'=4] {'tp'}, dimensions={0}, use_global_device_ids=true | all-gather | bytes 1064960 | tf_op jit(solution)/shard_map/all_gather | solution.py:498
  78.0 22.5 %all-gather.4.cloned.1.call-done = bf16[32,416,256]{2,1,0:T(8,128)(2,1)} async-done(((bf16[1,416,256]{2,1,0:T(8,128)(2,1)}), bf16[32,416,256]{2,1,0:T(8,128)(2,1)}) %all-gather.4.cloned.1.call-update) | async-done | bytes 6815760 | tf_op jit(solution)/shard_map/all_gather | solution.py:460
  100.4 8.0 %head_sum.1 = bf16[256,2048]{1,0:T(8,128)(2,1)} custom-call(bf16[4,832,128]{2,1,0:T(8,128)(2,1)S(1)} %bitcast.6, bf16[8,4,416,256]{3,2,1,0:T(8,128)(2,1)} %bitcast.10, bf16[8,4,416,256]{3,2,1,0:T(8,128)(2,1)} %bitcast.11, bf16[8,4,416,256]{3,2,1,0:T(8,128)(2,1)} %bitcast.12, bf16[8,4,416,256]{3,2,1,0:T(8,128)(2,1)} %bitcast.13), custom_call_target="tpu_custom_call" | custom-call | flops 1744830464 | bytes 6815744 | tf_op jit(solution)/shard_map/head_sum/pallas_call | solution.py:405
Async XLA Ops:
  7.2 93.3 %all-gather.4.cloned.1.call-start = ((), (), s32[]{:S(2)}) async-start(), calls=%async_computation | async-start | bytes 7028736 | tf_op jit(solution)/shard_map/all_gather | solution.py:460
  7.3 1.2 %copy-start = (bf16[256,2048]{1,0:T(8,128)(2,1)S(1)}, bf16[256,2048]{1,0:T(8,128)(2,1)}, u32[]{:S(2)}) copy-start(bf16[256,2048]{1,0:T(8,128)(2,1)} %tok_hbm.1) | copy-start | bytes 3145732
  8.5 1.2 %copy-start.1 = (bf16[2048,256]{1,0:T(8,128)(2,1)S(1)}, bf16[2048,256]{1,0:T(8,128)(2,1)}, u32[]{:S(2)}) copy-start(bf16[2048,256]{1,0:T(8,128)(2,1)} %ww_hbm.1) | copy-start | bytes 3145732
  9.7 1.0 copy-start.2
  10.8 0.9 copy-start.3
  11.7 0.8 copy-start.4
  12.5 0.7 copy-start.5
  17.4 4.9 %collective-permute-start = (bf16[560,128]{1,0:T(8,128)(2,1)S(1)}, bf16[560,128]{1,0:T(8,128)(2,1)S(1)}, u32[]{:S(2)}, u32[]{:S(2)}) collective-permute-start(bf16[560,128]{1,0:T(8,128)(2,1)S(1)} %get-tuple-element.17), channel_id=1, source_target_pairs={{0,4},{4,0},{8,12},{12,8},{16,20},{20,16},{24,28},{28,24},{1,5},{5... | collective-permute-start | bytes 430088 | tf_op jit(solution)/shard_map/ppermute | solution.py:466
  17.9 7.2 %collective-permute-start.1 = (bf16[560,128]{1,0:T(8,128)(2,1)S(1)}, bf16[560,128]{1,0:T(8,128)(2,1)S(1)}, u32[]{:S(2)}, u32[]{:S(2)}) collective-permute-start(bf16[560,128]{1,0:T(8,128)(2,1)S(1)} %get-tuple-element.18), channel_id=1, source_target_pairs={{0,8},{4,12},{8,0},{12,4},{16,24},{20,28},{24,16},{28,20},{1,9},{5... | collective-permute-start | bytes 430088 | tf_op jit(solution)/shard_map/ppermute | solution.py:466
  20.5 7.2 %collective-permute-start.2 = (bf16[560,128]{1,0:T(8,128)(2,1)S(1)}, bf16[560,128]{1,0:T(8,128)(2,1)S(1)}, u32[]{:S(2)}, u32[]{:S(2)}) collective-permute-start(bf16[560,128]{1,0:T(8,128)(2,1)S(1)} %get-tuple-element.19), channel_id=1, source_target_pairs={{0,12},{4,8},{8,4},{12,0},{16,28},{20,24},{24,20},{28,16},{1,13},{... | collective-permute-start | bytes 430088 | tf_op jit(solution)/shard_map/ppermute | solution.py:466
  20.5 7.1 %collective-permute-start.3 = (bf16[560,128]{1,0:T(8,128)(2,1)S(1)}, bf16[560,128]{1,0:T(8,128)(2,1)S(1)}, u32[]{:S(2)}, u32[]{:S(2)}) collective-permute-start(bf16[560,128]{1,0:T(8,128)(2,1)S(1)} %get-tuple-element.20), channel_id=1, source_target_pairs={{0,16},{4,20},{8,24},{12,28},{16,0},{20,4},{24,8},{28,12},{1,17},{... | collective-permute-start | bytes 430088 | tf_op jit(solution)/shard_map/ppermute | solution.py:466
  22.3 14.2 %collective-permute-start.4 = (bf16[560,128]{1,0:T(8,128)(2,1)S(1)}, bf16[560,128]{1,0:T(8,128)(2,1)S(1)}, u32[]{:S(2)}, u32[]{:S(2)}) collective-permute-start(bf16[560,128]{1,0:T(8,128)(2,1)S(1)} %get-tuple-element.21), channel_id=1, source_target_pairs={{0,20},{4,16},{8,28},{12,24},{16,4},{20,0},{24,12},{28,8},{1,21},{... | collective-permute-start | bytes 430088 | tf_op jit(solution)/shard_map/ppermute | solution.py:466
  22.3 14.2 %collective-permute-start.5 = (bf16[560,128]{1,0:T(8,128)(2,1)S(1)}, bf16[560,128]{1,0:T(8,128)(2,1)S(1)}, u32[]{:S(2)}, u32[]{:S(2)}) collective-permute-start(bf16[560,128]{1,0:T(8,128)(2,1)S(1)} %get-tuple-element.22), channel_id=1, source_target_pairs={{0,24},{4,28},{8,16},{12,20},{16,8},{20,12},{24,0},{28,4},{1,25},{... | collective-permute-start | bytes 430088 | tf_op jit(solution)/shard_map/ppermute | solution.py:466
  25.1 11.5 %collective-permute-start.6 = (bf16[560,128]{1,0:T(8,128)(2,1)S(1)}, bf16[560,128]{1,0:T(8,128)(2,1)S(1)}, u32[]{:S(2)}, u32[]{:S(2)}) collective-permute-start(bf16[560,128]{1,0:T(8,128)(2,1)S(1)} %get-tuple-element.23), channel_id=1, source_target_pairs={{0,28},{4,24},{8,20},{12,16},{16,12},{20,8},{24,4},{28,0},{1,29},{... | collective-permute-start | bytes 430088 | tf_op jit(solution)/shard_map/ppermute | solution.py:466
Sparse Core Ops, SparseCore 0:
  17.5 82.8 all-gather.3

commit v3 on v2

--- a/solution.py
+++ b/solution.py
@@ -57,13 +57,12 @@
 
 
 def project_kernel(place_ref, tok_hbm, fw_hbm, ww_hbm, vw_hbm, ld_hbm, do_hbm, *rest):
-    *sends, keys_ref, query_ref, feat_ref, cum_ref, pack_ref = rest[:-8]
+    *sends, keys_ref, query_ref, feat_ref, cum_ref = rest[:-8]
     tok_ref, fw_ref, ww_ref, vw_ref, ld_ref, do_ref, sems, small = rest[-8:]
-    me, piece = place_ref[0], place_ref[1]
+    me = place_ref[0]
     rows, dim = tok_ref.shape
     dh = do_ref.shape[1]
     nf = fw_ref.shape[0] // 2
-    count = len(sends) + 1
     span = dim // CHUNKS
     copies = []
     for c in range(CHUNKS):
@@ -131,19 +130,49 @@
 
     put_keys(keys_ref)
     put_query(query_ref)
-    for d in range(1, count):
-        later = partner(me, d, count) > me
-        ref = sends[d - 1]
+    for at, ref in enumerate(sends):
+        later = jnp.bitwise_xor(me, max(2 * at, 1)) > me
         pl.when(later)(lambda ref=ref: put_keys(ref))
         pl.when(jnp.logical_not(later))(lambda ref=ref: put_query(ref))
 
-    tile = pack_ref.shape[2]
-    for p in range(pack_ref.shape[0]):
-        at = pl.multiple_of((piece + p) * tile, tile)
-        part = pl.ds(at, tile)
-        pack_ref[p, 0 : 2 * dh, :] = jnp.transpose(ww_ref[part, :].astype(f32)).astype(bf16)
-        pack_ref[p, 2 * dh : 3 * dh, :] = jnp.transpose(vw_ref[part, :].astype(f32)).astype(bf16)
-        pack_ref[p, 3 * dh : 3 * dh + 2 * nf, :] = fw_ref[:, part]
+
+def pack_kernel(place_ref, ww_hbm, vw_hbm, fw_hbm, pack_ref, ww_ref, vw_ref, fw_ref, sems):
+    pieces, height, tile = pack_ref.shape
+    dh = vw_ref.shape[1]
+    used = 3 * dh + fw_ref.shape[0]
+    part = pl.ds(pl.multiple_of(place_ref[1] * tile, tile), pieces * tile)
+    copies = [
+        pltpu.make_async_copy(ww_hbm.at[part, :], ww_ref, sems.at[0]),
+        pltpu.make_async_copy(vw_hbm.at[part, :], vw_ref, sems.at[1]),
+        pltpu.make_async_copy(fw_hbm.at[:, part], fw_ref, sems.at[2]),
+    ]
+    for copy in copies:
+        copy.start()
+    for copy in copies:
+        copy.wait()
+    for p in range(pieces):
+        at = slice(p * tile, (p + 1) * tile)
+        pack_ref[p, 0 : 2 * dh, :] = jnp.transpose(ww_ref[at, :].astype(f32)).astype(bf16)
+        pack_ref[p, 2 * dh : 3 * dh, :] = jnp.transpose(vw_ref[at, :].astype(f32)).astype(bf16)
+        pack_ref[p, 3 * dh : used, :] = fw_ref[:, at]
+        if height > used:
+            pack_ref[p, used:, :] = jnp.zeros((height - used, tile), bf16)
+
+
+def others_kernel(place_ref, pack_hbm, out_hbm, sems):
+    head = place_ref[3]
+    copies = [
+        pltpu.make_async_copy(
+            pack_hbm.at[jnp.bitwise_xor(head, t + 1), pl.ds(0, out_hbm.shape[1]), :],
+            out_hbm.at[t],
+            sems.at[t],
+        )
+        for t in range(out_hbm.shape[0])
+    ]
+    for copy in copies:
+        copy.start()
+    for copy in copies:
+        copy.wait()
 
 
 def between(totals, low, high):
@@ -361,52 +390,78 @@
     put_wide(grad_ref, 3 * rows, dft)
 
 
-def merge_kernel(grad_ref, *rest):
-    heads = grad_ref.shape[0]
-    weights, out_ref, cat_ref, feat_ref = rest[:heads], rest[-3], rest[-2], rest[-1]
-    rows = out_ref.shape[0]
+def gather_rows(grad_ref, order, cat_ref, feat_ref):
+    rows = cat_ref.shape[0]
+    nf2 = feat_ref.shape[1] // len(order)
+    for at, h in enumerate(order):
+        for part in range(3):
+            lane = (3 * at + part) * LANES
+            cat_ref[:, lane : lane + LANES] = grad_ref[h, part * rows : (part + 1) * rows, :]
+    dft = jnp.concatenate([wide(grad_ref.at[h], 3 * rows, nf2) for h in order], axis=0)
+    feat_ref[...] = jnp.transpose(dft.astype(f32)).astype(bf16)
+
+
+def merge_kernel(grad_ref, weight_ref, out_ref, cat_ref, feat_ref):
+    heads, pieces = weight_ref.shape[:2]
+    tile = weight_ref.shape[3]
     lanes = 3 * LANES
-    nf2 = weights[0].shape[-2] - lanes
 
     @pl.when(pl.program_id(0) == 0)
     def _():
-        for h in range(heads):
-            for part in range(3):
-                at = (3 * h + part) * LANES
-                cat_ref[:, at : at + LANES] = grad_ref[h, part * rows : (part + 1) * rows, :]
-        dft = jnp.concatenate([wide(grad_ref.at[h], 3 * rows, nf2) for h in range(heads)], axis=0)
-        feat_ref[...] = jnp.transpose(dft.astype(f32)).astype(bf16)
-
-    main = jnp.concatenate([w[0, 0, 0:lanes, :] for w in weights], axis=0)
-    feats = jnp.concatenate([w[0, 0, lanes:, :] for w in weights], axis=0)
-    out_ref[...] = (nn(cat_ref[...], main) + nn(feat_ref[...], feats)).astype(bf16)
+        gather_rows(grad_ref, range(heads), cat_ref, feat_ref)
+
+    for p in range(pieces):
+        main = jnp.concatenate([weight_ref[h, p, 0:lanes, :] for h in range(heads)], axis=0)
+        feats = jnp.concatenate([weight_ref[h, p, lanes:, :] for h in range(heads)], axis=0)
+        total = nn(cat_ref[...], main) + nn(feat_ref[...], feats)
+        out_ref[:, p * tile : (p + 1) * tile] = total.astype(bf16)
+
+
+def half_kernel(place_ref, grad_ref, weight_ref, ww_ref, vw_ref, fw_ref, *rest):
+    out_ref, cat_ref, feat_ref = rest[-3:]
+    head = place_ref[3]
+    pieces, heads, _, tile = weight_ref.shape
+    lanes = 3 * LANES
+
+    @pl.when(pl.program_id(0) == 0)
+    def _():
+        order = [head] + [jnp.bitwise_xor(head, t + 1) for t in range(heads)]
+        gather_rows(grad_ref, order, cat_ref, feat_ref)
+
+    nf2 = fw_ref.shape[0]
+    for p in range(pieces):
+        at = slice(p * tile, (p + 1) * tile)
+        main = jnp.concatenate([weight_ref[p, t, 0:lanes, :] for t in range(heads)], axis=0)
+        feats = jnp.concatenate(
+            [fw_ref[:, at]] + [weight_ref[p, t, lanes:, :] for t in range(heads)], axis=0
+        )
+        total = nn(cat_ref[:, lanes:], main) + nn(feat_ref[...], feats)
+        total += nt(cat_ref[:, 0 : 2 * LANES], ww_ref[at, :])
+        total += nt(cat_ref[:, 2 * LANES : lanes], vw_ref[at, :])
+        out_ref[:, at] = total.astype(bf16)
 
 
 VMEM = pl.BlockSpec(memory_space=pltpu.VMEM)
 SMEM = pl.BlockSpec(memory_space=pltpu.SMEM)
 ANY = pl.BlockSpec(memory_space=pl.ANY)
 params = pltpu.CompilerParams(vmem_limit_bytes=48 * 1024 * 1024)
+full = pltpu.CompilerParams(vmem_limit_bytes=60 * 1024 * 1024)
 
 
 def cost(flops, nbytes, exps=0):
     return pl.CostEstimate(flops=flops, bytes_accessed=nbytes, transcendentals=exps)
 
 
-def merge(grads, weights, by_head, rows, dim):
-    heads = grads.shape[0]
-    columns, tile = weights.shape[2:]
-    pieces = dim // tile
-
-    def at(h):
-        return (lambda i: (h, i, 0, 0)) if by_head else (lambda i: (i, h, 0, 0))
-
-    specs = [pl.BlockSpec(grads.shape, lambda i: (0, 0, 0))]
-    specs += [pl.BlockSpec((1, 1, columns, tile), at(h)) for h in range(heads)]
+def merge(grads, weights, rows, dim):
+    heads, pieces, columns, tile = weights.shape
     return pl.pallas_call(
         merge_kernel,
         out_shape=jax.ShapeDtypeStruct((rows, dim), bf16),
         grid=(pieces,),
-        in_specs=specs,
+        in_specs=[
+            pl.BlockSpec(grads.shape, lambda i: (0, 0, 0)),
+            pl.BlockSpec((heads, 1, columns, tile), lambda i: (0, i, 0, 0)),
+        ],
         out_specs=pl.BlockSpec((rows, tile), lambda i: (0, i)),
         scratch_shapes=[
             pltpu.VMEM((rows, 3 * LANES * heads), bf16),
@@ -415,7 +470,53 @@
         compiler_params=params,
         cost_estimate=cost(2 * rows * dim * heads * columns, heads * dim * columns * 2),
         name="head_sum",
-    )(grads, *([weights] * heads))
+    )(grads, weights)
+
+
+def merge_half(place, grads, weights, ww, vw, fw_t, own_half, before):
+    pieces, others, columns, tile = weights.shape
+    heads = others + 1
+    dim = ww.shape[0]
+    rows = grads.shape[1] * LANES // (3 * LANES + fw_t.shape[0])
+    group = 2
+    steps = pieces // group
+    span = group * tile
+
+    def at(i, place):
+        core = place[2]
+        return (core if own_half else 1 - core) * steps + i
+
+    in_specs = [
+        pl.BlockSpec(grads.shape, lambda i, place: (0, 0, 0)),
+        pl.BlockSpec((group, others, columns, tile), lambda i, place: (i, 0, 0, 0)),
+        pl.BlockSpec((span, ww.shape[1]), lambda i, place: (at(i, place), 0)),
+        pl.BlockSpec((span, vw.shape[1]), lambda i, place: (at(i, place), 0)),
+        pl.BlockSpec((fw_t.shape[0], span), lambda i, place: (0, at(i, place))),
+    ]
+    args = [place, grads, weights, ww, vw, fw_t]
+    aliases = {}
+    if before is not None:
+        in_specs.append(ANY)
+        aliases = {len(args): 0}
+        args.append(before)
+    return pl.pallas_call(
+        half_kernel,
+        out_shape=jax.ShapeDtypeStruct((rows, dim), bf16),
+        grid_spec=pltpu.PrefetchScalarGridSpec(
+            num_scalar_prefetch=1,
+            grid=(steps,),
+            in_specs=in_specs,
+            out_specs=pl.BlockSpec((rows, span), lambda i, place: (0, at(i, place))),
+            scratch_shapes=[
+                pltpu.VMEM((rows, 3 * LANES * heads), bf16),
+                pltpu.VMEM((rows, (columns - 3 * LANES) * heads), bf16),
+            ],
+        ),
+        input_output_aliases=aliases,
+        compiler_params=full,
+        cost_estimate=cost(rows * dim * heads * columns, heads * dim * columns),
+        name="half_sum",
+    )(*args)
 
 
 def per_device(tokens, feature_weight, window_weight, value_weight, log_decay, out_grad):
@@ -424,24 +525,44 @@
     nf = nf2 // 2
     dh = value_weight.shape[1]
     columns = 3 * dh + nf2
-    count = lax.axis_size(CTX)
+    chips, count = lax.axis_size("chip"), lax.axis_size(CTX)
+    heads = lax.axis_size("tp")
+    chip, core = lax.axis_index("chip"), lax.axis_index("core")
     me = lax.axis_index(CTX)
     tile = 2 * LANES
-    spread = count * tile == dim
-    pieces = 1 if spread else dim // tile
-    place = jnp.stack([me, me if spread else 0 * me]).astype(jnp.int32)
+    spread = count * tile == dim and heads == 4
+    pieces, height = (1, 4 * LANES) if spread else (dim // tile, columns)
+    piece = core * chips + chip if spread else 0 * me
+    place = jnp.stack([me, piece, core, lax.axis_index("tp")]).astype(jnp.int32)
+    fw_t = feature_weight.T
+    packed = pl.pallas_call(
+        pack_kernel,
+        out_shape=jax.ShapeDtypeStruct((pieces, height, tile), bf16),
+        in_specs=[SMEM] + [ANY] * 3,
+        out_specs=VMEM,
+        scratch_shapes=[
+            pltpu.VMEM((pieces * tile, 2 * dh), bf16),
+            pltpu.VMEM((pieces * tile, dh), bf16),
+            pltpu.VMEM((nf2, pieces * tile), bf16),
+            pltpu.SemaphoreType.DMA((3,)),
+        ],
+        compiler_params=full,
+        cost_estimate=cost(1, 2 * columns * tile * pieces * 2),
+        name="pack",
+    )(place, window_weight, value_weight, fw_t)
+    weights = lax.all_gather(packed[0] if spread else packed, "tp")
+
     payload = 2 * rows + 2 * nf + 16
     block = jax.ShapeDtypeStruct((payload, LANES), bf16)
-    *sends, own, query, feat, cum, packed = pl.pallas_call(
+    *sends, own, query, feat, cum = pl.pallas_call(
         project_kernel,
-        out_shape=[block] * (count + 1)
+        out_shape=[block] * (chips + 2)
         + [
             jax.ShapeDtypeStruct((rows, nf2), bf16),
             jax.ShapeDtypeStruct((rows, 1), f32),
-            jax.ShapeDtypeStruct((pieces, columns, tile), bf16),
         ],
         in_specs=[SMEM] + [ANY] * 6,
-        out_specs=[VMEM] * (count + 4),
+        out_specs=[VMEM] * (chips + 4),
         scratch_shapes=[
             pltpu.VMEM((rows, dim), bf16),
             pltpu.VMEM((nf2, dim), bf16),
@@ -452,18 +573,19 @@
             pltpu.SemaphoreType.DMA((CHUNKS, 4)),
             pltpu.SemaphoreType.DMA((2,)),
         ],
-        compiler_params=params,
+        compiler_params=full,
         cost_estimate=cost(2 * rows * dim * columns, 4 * 1024 * 1024),
         name="project",
-    )(place, tokens, feature_weight.T, window_weight, value_weight, log_decay.T, out_grad)
-    if spread:
-        weights = lax.all_gather(packed[0], CTX + ("tp",)).reshape(count, -1, columns, tile)
-    else:
-        weights = lax.all_gather(packed, "tp")
-
-    recv = []
-    for d in range(1, count):
-        recv.append(lax.ppermute(sends[d - 1], CTX, [(i, i ^ d) for i in range(count)]))
+    )(place, tokens, fw_t, window_weight, value_weight, log_decay.T, out_grad)
+
+    swap = [(0, 1), (1, 0)]
+    recv = {1: None}
+    for d in range(1, chips):
+        recv[2 * d] = lax.ppermute(sends[d], "chip", [(i, i ^ d) for i in range(chips)])
+    recv[1] = lax.ppermute(sends[0], "core", swap)
+    for d in range(1, chips):
+        recv[2 * d + 1] = lax.ppermute(recv[2 * d], "core", swap)
+    recv = [recv[d] for d in range(1, count)]
     if count > 8:
         recv = [jnp.stack(recv)]
 
@@ -485,6 +607,20 @@
         cost_estimate=cost(10**9, 2 * 1024 * 1024, 10**6),
         name="query_side",
     )(place, *recv, own, query, feat, cum)
+    if spread:
+        weights, _ = lax.optimization_barrier((weights, stat))
+        others = pl.pallas_call(
+            others_kernel,
+            out_shape=jax.ShapeDtypeStruct((heads - 1, columns, tile), bf16),
+            in_specs=[SMEM, ANY],
+            out_specs=ANY,
+            scratch_shapes=[pltpu.SemaphoreType.DMA((heads - 1,))],
+            compiler_params=full,
+            cost_estimate=cost(1, heads * columns * tile * 4),
+            name="others",
+        )(place, weights)
+        others, stat = lax.optimization_barrier((others, stat))
+        weights = lax.all_gather(others, "chip")
     stats = lax.all_gather(stat, CTX)
     grads = pl.pallas_call(
         lambda *refs: gradient_kernel(count, *refs),
@@ -495,8 +631,14 @@
         cost_estimate=cost(10**9, 2 * 1024 * 1024, 10**6),
         name="gradients",
     )(place, *recv, own, query, feat, sheet, stats)
-    all_grads = lax.all_gather(grads, "tp")
-    return (attended, merge(all_grads, weights, not spread, rows, dim))
+    grads = lax.all_gather(grads, "tp")
+    if not spread:
+        return (attended, merge(grads, weights, rows, dim))
+    weights, grads = lax.optimization_barrier((weights, grads))
+    swapped = lax.ppermute(weights, "core", swap)
+    total = merge_half(place, grads, weights, window_weight, value_weight, fw_t, True, None)
+    total = merge_half(place, grads, swapped, window_weight, value_weight, fw_t, False, total)
+    return (attended, total)
 
 
 def solution(mesh):

time: 116 us -> 120 us (1.034)
  Pallas kernels: 19.3 us -> 45.5 us
  waiting for transfers between devices: 32.4 us -> 20.4 us
  blocking collectives: 34.3 us -> 28.5 us
  starting transfers between devices: 9.28 us -> 5.14 us
    pallas_call x2 -> x5, Pallas kernels: 12.2 us -> 38.4 us  [the longest x1 21.1 us: per_device(): pl.pallas_call(others_kernel, out_shape=jax.ShapeDtypeStruct((heads - 1,...]
    all_gather x1 -> x2, waiting for transfers between devices: 22.5 us -> 12.2 us  [the longest x1 6.09 us: per_device(): weights = lax.all_gather(packed[0] if spread else packed, 'tp')]
    all_gather x1, blocking collectives: 24.7 us -> 19.3 us  [per_device(): grads = lax.all_gather(grads, 'tp')]
    ppermute x7 -> x8, starting transfers between devices: 9.25 us -> 5.06 us  [the longest x3 4.54 us: per_device(): lax.ppermute(sends[d], 'chip', [(i, i ^ d) for i in range(chips)])]
    ppermute x7 -> x8, waiting for transfers between devices: 9.92 us -> 8.23 us  [the longest x3 6.97 us: per_device(): lax.ppermute(sends[d], 'chip', [(i, i ^ d) for i in range(chips)])]
    unnamed x12 -> x20, local copies, waits for them, and re-layouts: 5.91 us -> 5.06 us
  transfers between devices with their start and end apart: 8 -> 10, of which waited for: 4 -> 7; matrix products, arithmetic and copies ran while one was open for 0% -> 0% of each run, Pallas kernels for 6% -> 14%
where the time goes in v3:
time: 120 us; the launch traced here: 119 us
  Pallas kernels  45.5 us (38%)
  blocking collectives  28.5 us (24%)
  waiting for transfers between devices  20.4 us (17%)
  between operations  14.1 us (12%)
  starting transfers between devices  5.14 us (4%)
  local copies, waits for them, and re-layouts  5.06 us (4%)
    pallas_call x1, Pallas kernels, per_device(): pl.pallas_call(others_kernel, out_shape=jax.ShapeDtypeStruct((heads - 1,...  21.1 us
    all_gather x1, blocking collectives, per_device(): grads = lax.all_gather(grads, 'tp')  19.3 us
    pallas_call x2, Pallas kernels, merge_half(): pl.pallas_call(half_kernel, out_shape=jax.ShapeDtypeStruct((rows, dim), b...  9.63 us
    all_gather x1, blocking collectives, per_device(): stats = lax.all_gather(stat, CTX)  9.19 us
    ppermute x3, waiting for transfers between devices, per_device(): lax.ppermute(sends[d], 'chip', [(i, i ^ d) for i in range(chips)])  6.97 us
    all_gather x1, waiting for transfers between devices, per_device(): weights = lax.all_gather(packed[0] if spread else packed, 'tp')  6.09 us
    all_gather x1, waiting for transfers between devices, per_device(): weights = lax.all_gather(others, 'chip')  6.07 us
    unnamed x20, local copies, waits for them, and re-layouts  5.06 us
  transfers between devices with their start and end apart: 10, of which 7 were waited for; matrix products, arithmetic and copies ran while one was open for 0% of the time, Pallas kernels for 14%

profile of v3, /device:TPU:0, one launch (start us, length us, event | category | flops | bytes accessed | tf_op | source)
XLA Modules:
  0.0 119.4 jit_solution(16199161798627744064)
XLA Ops:
  7.2 0.0 all-gather.6.cloned.1.call-start
  7.2 0.7 pad_add_fusion.place_ref.refs_0_
  7.9 0.0 copy-start
  7.9 2.6 %pack.1 = bf16[1,512,256]{2,1,0:T(8,128)(2,1)} custom-call(s32[4]{0:T(128)} %pad_add_fusion.place_ref.refs_0_, bf16[2048,256]{1,0:T(8,128)(2,1)} %ww_ref.3, bf16[2048,128]{1,0:T(8,128)(2,1)} %vw_ref.3, bf16[32,2048]{1,0:T(8,128)(2,1)} %bitcast.14), custom_call_target="tpu_custom_call" | custom-call | flops 1 | bytes 425984 | tf_op jit(solution)/shard_map/pack/pallas_call | solution.py:538
  10.5 0.0 all-gather.6.cloned.1.call-update
  10.5 0.0 all-gather.8.cloned.1.call-start
  10.5 5.0 %project.1 = (bf16[560,128]{1,0:T(8,128)(2,1)}, bf16[560,128]{1,0:T(8,128)(2,1)}, bf16[560,128]{1,0:T(8,128)(2,1)}, bf16[560,128]{1,0:T(8,128)(2,1)}, bf16[560,1...) custom-call(s32[4]{0:T(128)} %pad_add_fusion.place_ref.refs_0_, ...), custom_call_target="tpu_custom_call" | custom-call | flops 436207616 | bytes 4194304 | tf_op jit(solution)/shard_map/project/pallas_call | solution.py:557
  15.6 3.0 %collective-permute-start.1 = (bf16[560,128]{1,0:T(8,128)(2,1)}, bf16[560,128]{1,0:T(8,128)(2,1)S(1)}, u32[]{:S(2)}, u32[]{:S(2)}) collective-permute-start(bf16[560,128]{1,0:T(8,128)(2,1)} %get-tuple-element.19), channel_id=1, source_target_pairs={{0,8},{8,0},{16,24},{24,16},{1,9},{9,1},{17,25},{25,17},{2,10},{10... | collective-permute-start | bytes 430088 | tf_op jit(solution)/shard_map/ppermute | solution.py:584
  18.6 1.5 %collective-permute-start.3 = (bf16[560,128]{1,0:T(8,128)(2,1)}, bf16[560,128]{1,0:T(8,128)(2,1)S(1)}, u32[]{:S(2)}, u32[]{:S(2)}) collective-permute-start(bf16[560,128]{1,0:T(8,128)(2,1)} %get-tuple-element.20), channel_id=1, source_target_pairs={{0,16},{8,24},{16,0},{24,8},{1,17},{9,25},{17,1},{25,9},{2,18},{10... | collective-permute-start | bytes 430088 | tf_op jit(solution)/shard_map/ppermute | solution.py:584
  20.1 0.0 collective-permute-start.5
  20.1 0.0 collective-permute-start
  20.1 2.9 %collective-permute-done.1.refs_2_ = bf16[560,128]{1,0:T(8,128)(2,1)S(1)} collective-permute-done((bf16[560,128]{1,0:T(8,128)(2,1)}, bf16[560,128]{1,0:T(8,128)(2,1)S(1)}, u32[]{:S(2)}, u32[]{:S(2)}) %collective-permute-start.1) | collective-permute-done | bytes 143392 | tf_op jit(solution)/shard_map/ppermute | solution.py:584
  23.1 0.0 collective-permute-start.2
  23.1 4.0 %collective-permute-done.3.refs_4_ = bf16[560,128]{1,0:T(8,128)(2,1)S(1)} collective-permute-done((bf16[560,128]{1,0:T(8,128)(2,1)}, bf16[560,128]{1,0:T(8,128)(2,1)S(1)}, u32[]{:S(2)}, u32[]{:S(2)}) %collective-permute-start.3) | collective-permute-done | bytes 143392 | tf_op jit(solution)/shard_map/ppermute | solution.py:584
  27.1 0.0 collective-permute-start.4
  27.1 0.0 collective-permute-done.5.refs_6_
  27.1 0.5 collective-permute-start.6
  27.6 0.0 collective-permute-done.refs_1_
  27.6 0.0 collective-permute-done.2.refs_3_
  27.6 0.8 collective-permute-done.4.refs_5_
  28.5 0.2 collective-permute-done.6.refs_7_
  28.7 0.0 copy-done
  28.7 0.0 copy-start.2
  28.7 0.9 copy-done.2
  29.6 0.0 copy-start.4
  29.6 0.9 copy-done.4
  30.5 0.0 copy-start.6
  30.5 0.9 copy-done.6
  31.4 0.0 copy-start.7
  31.4 0.8 copy-done.7
  32.3 0.0 copy-start.1
  32.3 2.9 %query_side.1 = (bf16[256,128]{1,0:T(8,128)(2,1)}, f32[8,256]{1,0:T(8,128)S(1)}, f32[256,128]{1,0:T(8,128)S(1)}) custom-call(s32[4]{0:T(128)S(1)} %copy-done, bf16[560,128]{1,0:T(8,128)(2,1)S(1)} %collective-permute-done.refs_1_, bf16[560,128]{1,0:T(8,128)(2,1)S(1)} %collective-permute-done.1.refs_2_, bf16[560,128]{1,0:T(8,128)(2,1)S(1)} %collective-permute-done.2.refs_3_, ...), custom_call_target="tpu_custom_call" | custom-call | flops 1000000000 | bytes 2097152 | tf_op jit(solution)/shard_map/query_side/pallas_call | solution.py:592
  35.2 6.1 %all-gather.6.cloned.1.call-done.pack_hbm = bf16[4,512,256]{2,1,0:T(8,128)(2,1)} async-done(((bf16[1,512,256]{2,1,0:T(8,128)(2,1)}), bf16[4,512,256]{2,1,0:T(8,128)(2,1)}) %all-gather.6.cloned.1.call-update) | async-done | bytes 1048592 | tf_op jit(solution)/shard_map/all_gather | solution.py:553
  41.3 21.1 %others.1 = bf16[3,416,256]{2,1,0:T(8,128)(2,1)} custom-call(s32[4]{0:T(128)} %pad_add_fusion.place_ref.refs_0_, bf16[4,512,256]{2,1,0:T(8,128)(2,1)} %all-gather.6.cloned.1.call-done.pack_hbm), custom_call_target="tpu_custom_call" | custom-call | flops 1 | bytes 1703936 | tf_op jit(solution)/shard_map/others/pallas_call | solution.py:612
  62.4 0.0 all-gather.8.cloned.1.call-update
  62.5 9.2 %all-gather.1 = f32[64,256]{1,0:T(8,128)S(1)} all-gather(f32[8,256]{1,0:T(8,128)S(1)} %get-tuple-element.31), channel_id=3, replica_groups=mesh['chip'=4,'core'=2,'tp'=4] {'chip','core'}, dimensions={0}, use_global_device_ids=true | all-gather | bytes 73728 | tf_op jit(solution)/shard_map/all_gather | solution.py:624
  71.7 0.0 copy-done.1
  71.7 0.0 copy-done.3
  71.7 0.0 copy-done.5
  71.7 0.0 copy-done.8
  71.7 4.2 %gradients.1 = bf16[832,128]{1,0:T(8,128)(2,1)S(1)} custom-call(s32[4]{0:T(128)S(1)} %copy-done.1, bf16[560,128]{1,0:T(8,128)(2,1)S(1)} %collective-permute-done.refs_1_, bf16[560,128]{1,0:T(8,128)(2,1)S(1)} %collective-permute-done.1.refs_2_, bf16[560,128]{1,0:T(8,128)(2,1)S(1)} %collective-permute-done.2.refs_3_, ...), custom_call_target="tpu_custom_call" | custom-call | flops 1000000000 | bytes 2097152 | tf_op jit(solution)/shard_map/gradients/pallas_call | solution.py:625
  75.9 19.3 %all-gather.2 = bf16[3328,128]{1,0:T(8,128)(2,1)} all-gather(bf16[832,128]{1,0:T(8,128)(2,1)S(1)} %gradients.1), channel_id=4, replica_groups=mesh['chip'=4,'core'=2,'tp'=4] {'tp'}, dimensions={0}, use_global_device_ids=true | all-gather | bytes 1064960 | tf_op jit(solution)/shard_map/all_gather | solution.py:634
  95.1 6.1 %all-gather.8.cloned.1.call-done = bf16[12,416,256]{2,1,0:T(8,128)(2,1)} async-done(((bf16[3,416,256]{2,1,0:T(8,128)(2,1)}), bf16[12,416,256]{2,1,0:T(8,128)(2,1)}) %all-gather.8.cloned.1.call-update) | async-done | bytes 2555920 | tf_op jit(solution)/shard_map/all_gather | solution.py:623
  101.2 0.0 collective-permute-start.7
  101.2 4.8 %half_sum.2.rest_0_ = bf16[256,2048]{1,0:T(8,128)(2,1)} custom-call(s32[4]{0:T(128)} %pad_add_fusion.place_ref.refs_0_, bf16[4,832,128]{2,1,0:T(8,128)(2,1)} %bitcast.10, bf16[4,3,416,256]{3,2,1,0:T(8,128)(2,1)} %bitcast.13, bf16[2048,256]{1,0:T(8,128)(2,1)} %ww_ref.3, bf16[2048,128]{1,0:T(8,128)(2,1)} %vw_ref.3, bf16[32,2048]{1,0:T(8,128)(2,1)} %bitcast.16), custom_call_target="tpu_custom_call" | custom-call | flops 872415232 | bytes 3407872 | tf_op jit(solution)/shard_map/half_sum/pallas_call | solution.py:502
  106.0 0.2 collective-permute-done.7.weight_ref
  106.2 1.5 %copy-done.9 = bf16[4,3,416,256]{3,2,1,0:T(8,128)(2,1)} copy-done((bf16[4,3,416,256]{3,2,1,0:T(8,128)(2,1)}, bf16[4,3,416,256]{3,2,1,0:T(8,128)(2,1)S(1)}, u32[]{:S(2)}) %copy-start.9) | copy-done | bytes 2555928
  107.7 4.8 %half_sum.3 = bf16[256,2048]{1,0:T(8,128)(2,1)} custom-call(s32[4]{0:T(128)} %pad_add_fusion.place_ref.refs_0_, bf16[4,832,128]{2,1,0:T(8,128)(2,1)} %bitcast.11, bf16[4,3,416,256]{3,2,1,0:T(8,128)(2,1)} %copy-done.9, bf16[2048,256]{1,0:T(8,128)(2,1)} %ww_ref.3, bf16[2048,128]{1,0:T(8,128)(2,1)} %vw_ref.3, ...), custom_call_target="tpu_custom_call", output_to_operand_aliasing={{}: (6, {})} | custom-call | flops 872415232 | bytes 3407872 | tf_op jit(solution)/shard_map/half_sum/pallas_call | solution.py:502
  (4 shorter events, 0.0 us)
Async XLA Ops:
  7.2 34.1 %all-gather.6.cloned.1.call-start = ((), (), s32[]{:S(2)}) async-start(), calls=%async_computation | async-start | bytes 1310720 | tf_op jit(solution)/shard_map/all_gather | solution.py:553
  7.9 20.8 %copy-start = (s32[4]{0:T(128)S(1)}, s32[4]{0:T(128)}, u32[]{:S(2)}) copy-start(s32[4]{0:T(128)} %pad_add_fusion.place_ref.refs_0_) | copy-start | bytes 52
  10.5 90.7 %all-gather.8.cloned.1.call-start = ((), (), s32[]{:S(2)}) async-start(), calls=%async_computation.1 | async-start | bytes 3194880 | tf_op jit(solution)/shard_map/all_gather | solution.py:623
  15.6 7.5 %collective-permute-start.1 = (bf16[560,128]{1,0:T(8,128)(2,1)}, bf16[560,128]{1,0:T(8,128)(2,1)S(1)}, u32[]{:S(2)}, u32[]{:S(2)}) collective-permute-start(bf16[560,128]{1,0:T(8,128)(2,1)} %get-tuple-element.19), channel_id=1, source_target_pairs={{0,8},{8,0},{16,24},{24,16},{1,9},{9,1},{17,25},{25,17},{2,10},{10... | collective-permute-start | bytes 430088 | tf_op jit(solution)/shard_map/ppermute | solution.py:584
  18.6 8.5 %collective-permute-start.3 = (bf16[560,128]{1,0:T(8,128)(2,1)}, bf16[560,128]{1,0:T(8,128)(2,1)S(1)}, u32[]{:S(2)}, u32[]{:S(2)}) collective-permute-start(bf16[560,128]{1,0:T(8,128)(2,1)} %get-tuple-element.20), channel_id=1, source_target_pairs={{0,16},{8,24},{16,0},{24,8},{1,17},{9,25},{17,1},{25,9},{2,18},{10... | collective-permute-start | bytes 430088 | tf_op jit(solution)/shard_map/ppermute | solution.py:584
  20.1 7.0 %collective-permute-start.5 = (bf16[560,128]{1,0:T(8,128)(2,1)}, bf16[560,128]{1,0:T(8,128)(2,1)S(1)}, u32[]{:S(2)}, u32[]{:S(2)}) collective-permute-start(bf16[560,128]{1,0:T(8,128)(2,1)} %get-tuple-element.21), channel_id=1, source_target_pairs={{0,24},{8,16},{16,8},{24,0},{1,25},{9,17},{17,9},{25,1},{2,26},{10... | collective-permute-start | bytes 430088 | tf_op jit(solution)/shard_map/ppermute | solution.py:584
  20.1 7.5 %collective-permute-start = (bf16[560,128]{1,0:T(8,128)(2,1)}, bf16[560,128]{1,0:T(8,128)(2,1)S(1)}, u32[]{:S(2)}, u32[]{:S(2)}) collective-permute-start(bf16[560,128]{1,0:T(8,128)(2,1)} %get-tuple-element.18), channel_id=1, source_target_pairs={{0,4},{4,0},{1,5},{5,1},{2,6},{6,2},{3,7},{7,3},{8,12},{12,8},{9,1... | collective-permute-start | bytes 430088 | tf_op jit(solution)/shard_map/ppermute | solution.py:585
  23.1 4.5 %collective-permute-start.2 = (bf16[560,128]{1,0:T(8,128)(2,1)S(1)}, bf16[560,128]{1,0:T(8,128)(2,1)S(1)}, u32[]{:S(2)}, u32[]{:S(2)}) collective-permute-start(bf16[560,128]{1,0:T(8,128)(2,1)S(1)} %collective-permute-done.1.refs_2_), channel_id=1, source_target_pairs={{0,4},{4,0},{1,5},{5,1},{2,6},{6,2},{3,7},{7,3},{8,12},{12,8},{9,1... | collective-permute-start | bytes 430088 | tf_op jit(solution)/shard_map/ppermute | solution.py:587
  27.1 1.4 %collective-permute-start.4 = (bf16[560,128]{1,0:T(8,128)(2,1)S(1)}, bf16[560,128]{1,0:T(8,128)(2,1)S(1)}, u32[]{:S(2)}, u32[]{:S(2)}) collective-permute-start(bf16[560,128]{1,0:T(8,128)(2,1)S(1)} %collective-permute-done.3.refs_4_), channel_id=1, source_target_pairs={{0,4},{4,0},{1,5},{5,1},{2,6},{6,2},{3,7},{7,3},{8,12},{12,8},{9,1... | collective-permute-start | bytes 430088 | tf_op jit(solution)/shard_map/ppermute | solution.py:587
  27.1 1.6 %collective-permute-start.6 = (bf16[560,128]{1,0:T(8,128)(2,1)S(1)}, bf16[560,128]{1,0:T(8,128)(2,1)S(1)}, u32[]{:S(2)}, u32[]{:S(2)}) collective-permute-start(bf16[560,128]{1,0:T(8,128)(2,1)S(1)} %collective-permute-done.5.refs_6_), channel_id=1, source_target_pairs={{0,4},{4,0},{1,5},{5,1},{2,6},{6,2},{3,7},{7,3},{8,12},{12,8},{9,1... | collective-permute-start | bytes 430088 | tf_op jit(solution)/shard_map/ppermute | solution.py:587
  28.7 0.9 copy-start.2
  29.6 0.9 copy-start.4
  30.5 0.9 copy-start.6
  31.4 0.8 copy-start.7
  32.3 39.4 %copy-start.1 = (s32[4]{0:T(128)S(1)}, s32[4]{0:T(128)}, u32[]{:S(2)}) copy-start(s32[4]{0:T(128)} %pad_add_fusion.place_ref.refs_0_) | copy-start | bytes 52
  32.3 39.4 %copy-start.3 = (bf16[560,128]{1,0:T(8,128)(2,1)S(1)}, bf16[560,128]{1,0:T(8,128)(2,1)}, u32[]{:S(2)}) copy-start(bf16[560,128]{1,0:T(8,128)(2,1)} %get-tuple-element.22.refs_8_) | copy-start | bytes 430084
  32.3 39.4 %copy-start.5 = (bf16[560,128]{1,0:T(8,128)(2,1)S(1)}, bf16[560,128]{1,0:T(8,128)(2,1)}, u32[]{:S(2)}) copy-start(bf16[560,128]{1,0:T(8,128)(2,1)} %get-tuple-element.23.refs_9_) | copy-start | bytes 430084
  32.3 39.4 %copy-start.8 = (bf16[256,32]{1,0:T(8,128)(2,1)S(1)}, bf16[256,32]{1,0:T(8,128)(2,1)}, u32[]{:S(2)}) copy-start(bf16[256,32]{1,0:T(8,128)(2,1)} %get-tuple-element.24.refs_10_) | copy-start | bytes 49156
  101.2 5.0 %collective-permute-start.7 = (bf16[4,3,416,256]{3,2,1,0:T(8,128)(2,1)}, bf16[4,3,416,256]{3,2,1,0:T(8,128)(2,1)S(1)}, u32[]{:S(2)}, u32[]{:S(2)}) collective-permute-start(bf16[4,3,416,256]{3,2,1,0:T(8,128)(2,1)} %bitcast.12), channel_id=1, source_target_pairs={{0,4},{4,0},{1,5},{5,1},{2,6},{6,2},{3,7},{7,3},{8,12},{12,8},{9,1... | collective-permute-start | bytes 7667720 | tf_op jit(solution)/shard_map/ppermute | solution.py:638
  106.2 1.5 %copy-start.9 = (bf16[4,3,416,256]{3,2,1,0:T(8,128)(2,1)}, bf16[4,3,416,256]{3,2,1,0:T(8,128)(2,1)S(1)}, u32[]{:S(2)}) copy-start(bf16[4,3,416,256]{3,2,1,0:T(8,128)(2,1)S(1)} %collective-permute-done.7.weight_ref) | copy-start | bytes 7667716
Sparse Core Ops, SparseCore 0:
  10.6 30.6 all-gather.5
  62.6 38.5 all-gather.7

commit v4 on v3

--- a/solution.py
+++ b/solution.py
@@ -97,19 +97,17 @@
     tail = jnp.concatenate(pieces + [jnp.zeros((10, LANES), f32)], axis=0).astype(bf16)
 
     feat = jnp.zeros((rows, 2 * nf), f32)
-    window = jnp.zeros((rows, 2 * dh), f32)
-    values = jnp.zeros((rows, dh), f32)
+    main = jnp.zeros((rows, 3 * dh), f32)
     for c in range(CHUNKS):
         for copy in copies[c]:
             copy.wait()
         part = slice(c * span, (c + 1) * span)
         tok = tok_ref[:, part]
         feat += nt(tok, fw_ref[:, part])
-        window += nn(tok, ww_ref[part, :])
-        values += nn(tok, vw_ref[part, :])
+        main += nn(tok, jnp.concatenate([ww_ref[part, :], vw_ref[part, :]], axis=1))
     feat = feat.astype(bf16)
-    window = window.astype(bf16)
-    values = values.astype(bf16)
+    window = main[:, : 2 * dh].astype(bf16)
+    values = main[:, 2 * dh :].astype(bf16)
     feat_ref[...] = feat
     small_row, small_col = iotas(2 * nf)
     feat_t = nt((small_row == small_col).astype(bf16), feat).astype(bf16)
@@ -137,7 +135,7 @@
 
 
 def pack_kernel(place_ref, ww_hbm, vw_hbm, fw_hbm, pack_ref, ww_ref, vw_ref, fw_ref, sems):
-    pieces, height, tile = pack_ref.shape
+    pieces, _, tile = pack_ref.shape
     dh = vw_ref.shape[1]
     used = 3 * dh + fw_ref.shape[0]
     part = pl.ds(pl.multiple_of(place_ref[1] * tile, tile), pieces * tile)
@@ -155,24 +153,6 @@
         pack_ref[p, 0 : 2 * dh, :] = jnp.transpose(ww_ref[at, :].astype(f32)).astype(bf16)
         pack_ref[p, 2 * dh : 3 * dh, :] = jnp.transpose(vw_ref[at, :].astype(f32)).astype(bf16)
         pack_ref[p, 3 * dh : used, :] = fw_ref[:, at]
-        if height > used:
-            pack_ref[p, used:, :] = jnp.zeros((height - used, tile), bf16)
-
-
-def others_kernel(place_ref, pack_hbm, out_hbm, sems):
-    head = place_ref[3]
-    copies = [
-        pltpu.make_async_copy(
-            pack_hbm.at[jnp.bitwise_xor(head, t + 1), pl.ds(0, out_hbm.shape[1]), :],
-            out_hbm.at[t],
-            sems.at[t],
-        )
-        for t in range(out_hbm.shape[0])
-    ]
-    for copy in copies:
-        copy.start()
-    for copy in copies:
-        copy.wait()
 
 
 def between(totals, low, high):
@@ -390,60 +370,42 @@
     put_wide(grad_ref, 3 * rows, dft)
 
 
-def gather_rows(grad_ref, order, cat_ref, feat_ref):
+def merge_kernel(by_head, place_ref, grad_ref, weight_ref, *rest):
+    out_ref, cat_ref, feat_ref = rest[-3:]
+    heads = grad_ref.shape[0]
     rows = cat_ref.shape[0]
-    nf2 = feat_ref.shape[1] // len(order)
-    for at, h in enumerate(order):
-        for part in range(3):
-            lane = (3 * at + part) * LANES
-            cat_ref[:, lane : lane + LANES] = grad_ref[h, part * rows : (part + 1) * rows, :]
-    dft = jnp.concatenate([wide(grad_ref.at[h], 3 * rows, nf2) for h in order], axis=0)
-    feat_ref[...] = jnp.transpose(dft.astype(f32)).astype(bf16)
-
-
-def merge_kernel(grad_ref, weight_ref, out_ref, cat_ref, feat_ref):
-    heads, pieces = weight_ref.shape[:2]
-    tile = weight_ref.shape[3]
+    nf2 = feat_ref.shape[1] // heads
     lanes = 3 * LANES
 
     @pl.when(pl.program_id(0) == 0)
     def _():
-        gather_rows(grad_ref, range(heads), cat_ref, feat_ref)
-
-    for p in range(pieces):
-        main = jnp.concatenate([weight_ref[h, p, 0:lanes, :] for h in range(heads)], axis=0)
-        feats = jnp.concatenate([weight_ref[h, p, lanes:, :] for h in range(heads)], axis=0)
-        total = nn(cat_ref[...], main) + nn(feat_ref[...], feats)
-        out_ref[:, p * tile : (p + 1) * tile] = total.astype(bf16)
-
-
-def half_kernel(place_ref, grad_ref, weight_ref, ww_ref, vw_ref, fw_ref, *rest):
-    out_ref, cat_ref, feat_ref = rest[-3:]
-    head = place_ref[3]
-    pieces, heads, _, tile = weight_ref.shape
-    lanes = 3 * LANES
-
-    @pl.when(pl.program_id(0) == 0)
-    def _():
-        order = [head] + [jnp.bitwise_xor(head, t + 1) for t in range(heads)]
-        gather_rows(grad_ref, order, cat_ref, feat_ref)
-
-    nf2 = fw_ref.shape[0]
-    for p in range(pieces):
-        at = slice(p * tile, (p + 1) * tile)
-        main = jnp.concatenate([weight_ref[p, t, 0:lanes, :] for t in range(heads)], axis=0)
-        feats = jnp.concatenate(
-            [fw_ref[:, at]] + [weight_ref[p, t, lanes:, :] for t in range(heads)], axis=0
+        for h in range(heads):
+            for part in range(3):
+                at = h * lanes + part * LANES
+                cat_ref[:, at : at + LANES] = grad_ref[h, part * rows : (part + 1) * rows, :]
+        dft = jnp.concatenate([wide(grad_ref.at[h], 3 * rows, nf2) for h in range(heads)], axis=0)
+        feat_ref[...] = jnp.transpose(dft.astype(f32)).astype(bf16)
+
+    pieces = weight_ref.shape[1 if by_head else 0]
+
+    def stacked(part):
+        def one(h, p):
+            return weight_ref[(h, p) + part] if by_head else weight_ref[(p, h) + part]
+
+        return jnp.concatenate(
+            [jnp.concatenate([one(h, p) for h in range(heads)], axis=0) for p in range(pieces)],
+            axis=1,
         )
-        total = nn(cat_ref[:, lanes:], main) + nn(feat_ref[...], feats)
-        total += nt(cat_ref[:, 0 : 2 * LANES], ww_ref[at, :])
-        total += nt(cat_ref[:, 2 * LANES : lanes], vw_ref[at, :])
-        out_ref[:, at] = total.astype(bf16)
+
+    total = nn(cat_ref[...], stacked((slice(0, lanes), slice(None))))
+    total += nn(feat_ref[...], stacked((slice(lanes, None), slice(None))))
+    out_ref[...] = total.astype(bf16)
 
 
 VMEM = pl.BlockSpec(memory_space=pltpu.VMEM)
 SMEM = pl.BlockSpec(memory_space=pltpu.SMEM)
 ANY = pl.BlockSpec(memory_space=pl.ANY)
+HBM = pl.BlockSpec(memory_space=pltpu.HBM)
 params = pltpu.CompilerParams(vmem_limit_bytes=48 * 1024 * 1024)
 full = pltpu.CompilerParams(vmem_limit_bytes=60 * 1024 * 1024)
 
@@ -452,61 +414,39 @@
     return pl.CostEstimate(flops=flops, bytes_accessed=nbytes, transcendentals=exps)
 
 
-def merge(grads, weights, rows, dim):
-    heads, pieces, columns, tile = weights.shape
-    return pl.pallas_call(
-        merge_kernel,
-        out_shape=jax.ShapeDtypeStruct((rows, dim), bf16),
-        grid=(pieces,),
-        in_specs=[
-            pl.BlockSpec(grads.shape, lambda i: (0, 0, 0)),
-            pl.BlockSpec((heads, 1, columns, tile), lambda i: (0, i, 0, 0)),
-        ],
-        out_specs=pl.BlockSpec((rows, tile), lambda i: (0, i)),
-        scratch_shapes=[
-            pltpu.VMEM((rows, 3 * LANES * heads), bf16),
-            pltpu.VMEM((rows, (columns - 3 * LANES) * heads), bf16),
-        ],
-        compiler_params=params,
-        cost_estimate=cost(2 * rows * dim * heads * columns, heads * dim * columns * 2),
-        name="head_sum",
-    )(grads, weights)
-
-
-def merge_half(place, grads, weights, ww, vw, fw_t, own_half, before):
-    pieces, others, columns, tile = weights.shape
-    heads = others + 1
-    dim = ww.shape[0]
-    rows = grads.shape[1] * LANES // (3 * LANES + fw_t.shape[0])
-    group = 2
+def merge(place, grads, weights, by_head, group, rows, dim, half=None, before=None):
+    pieces, heads, columns, tile = weights.shape
+    block = (group, heads, columns, tile)
+    weight_at = lambda i, place: (i, 0, 0, 0)
+    if by_head:
+        pieces, heads = heads, pieces
+        block = (heads, group, columns, tile)
+        weight_at = lambda i, place: (0, i, 0, 0)
     steps = pieces // group
-    span = group * tile
 
     def at(i, place):
-        core = place[2]
-        return (core if own_half else 1 - core) * steps + i
+        if half is None:
+            return (0, i)
+        return (0, (place[2] if half == 0 else 1 - place[2]) * steps + i)
 
     in_specs = [
         pl.BlockSpec(grads.shape, lambda i, place: (0, 0, 0)),
-        pl.BlockSpec((group, others, columns, tile), lambda i, place: (i, 0, 0, 0)),
-        pl.BlockSpec((span, ww.shape[1]), lambda i, place: (at(i, place), 0)),
-        pl.BlockSpec((span, vw.shape[1]), lambda i, place: (at(i, place), 0)),
-        pl.BlockSpec((fw_t.shape[0], span), lambda i, place: (0, at(i, place))),
+        pl.BlockSpec(block, weight_at),
     ]
-    args = [place, grads, weights, ww, vw, fw_t]
+    args = [place, grads, weights]
     aliases = {}
     if before is not None:
         in_specs.append(ANY)
         aliases = {len(args): 0}
         args.append(before)
     return pl.pallas_call(
-        half_kernel,
+        lambda *refs: merge_kernel(by_head, *refs),
         out_shape=jax.ShapeDtypeStruct((rows, dim), bf16),
         grid_spec=pltpu.PrefetchScalarGridSpec(
             num_scalar_prefetch=1,
             grid=(steps,),
             in_specs=in_specs,
-            out_specs=pl.BlockSpec((rows, span), lambda i, place: (0, at(i, place))),
+            out_specs=pl.BlockSpec((rows, group * tile), at),
             scratch_shapes=[
                 pltpu.VMEM((rows, 3 * LANES * heads), bf16),
                 pltpu.VMEM((rows, (columns - 3 * LANES) * heads), bf16),
@@ -514,8 +454,8 @@
         ),
         input_output_aliases=aliases,
         compiler_params=full,
-        cost_estimate=cost(rows * dim * heads * columns, heads * dim * columns),
-        name="half_sum",
+        cost_estimate=cost(rows * pieces * tile * heads * columns, weights.size * 2),
+        name="head_sum",
     )(*args)
 
 
@@ -530,15 +470,15 @@
     chip, core = lax.axis_index("chip"), lax.axis_index("core")
     me = lax.axis_index(CTX)
     tile = 2 * LANES
-    spread = count * tile == dim and heads == 4
-    pieces, height = (1, 4 * LANES) if spread else (dim // tile, columns)
+    spread = count * tile == dim
+    pieces = 1 if spread else dim // tile
     piece = core * chips + chip if spread else 0 * me
     place = jnp.stack([me, piece, core, lax.axis_index("tp")]).astype(jnp.int32)
     fw_t = feature_weight.T
     packed = pl.pallas_call(
         pack_kernel,
-        out_shape=jax.ShapeDtypeStruct((pieces, height, tile), bf16),
-        in_specs=[SMEM] + [ANY] * 3,
+        out_shape=jax.ShapeDtypeStruct((pieces, columns, tile), bf16),
+        in_specs=[SMEM] + [HBM] * 3,
         out_specs=VMEM,
         scratch_shapes=[
             pltpu.VMEM((pieces * tile, 2 * dh), bf16),
@@ -550,7 +490,7 @@
         cost_estimate=cost(1, 2 * columns * tile * pieces * 2),
         name="pack",
     )(place, window_weight, value_weight, fw_t)
-    weights = lax.all_gather(packed[0] if spread else packed, "tp")
+    weights = lax.all_gather(packed[0], ("chip", "tp")) if spread else lax.all_gather(packed, "tp")
 
     payload = 2 * rows + 2 * nf + 16
     block = jax.ShapeDtypeStruct((payload, LANES), bf16)
@@ -561,7 +501,7 @@
             jax.ShapeDtypeStruct((rows, nf2), bf16),
             jax.ShapeDtypeStruct((rows, 1), f32),
         ],
-        in_specs=[SMEM] + [ANY] * 6,
+        in_specs=[SMEM] + [HBM] * 6,
         out_specs=[VMEM] * (chips + 4),
         scratch_shapes=[
             pltpu.VMEM((rows, dim), bf16),
@@ -573,7 +513,7 @@
             pltpu.SemaphoreType.DMA((CHUNKS, 4)),
             pltpu.SemaphoreType.DMA((2,)),
         ],
-        compiler_params=full,
+        compiler_params=params,
         cost_estimate=cost(2 * rows * dim * columns, 4 * 1024 * 1024),
         name="project",
     )(place, tokens, fw_t, window_weight, value_weight, log_decay.T, out_grad)
@@ -607,21 +547,7 @@
         cost_estimate=cost(10**9, 2 * 1024 * 1024, 10**6),
         name="query_side",
     )(place, *recv, own, query, feat, cum)
-    if spread:
-        weights, _ = lax.optimization_barrier((weights, stat))
-        others = pl.pallas_call(
-            others_kernel,
-            out_shape=jax.ShapeDtypeStruct((heads - 1, columns, tile), bf16),
-            in_specs=[SMEM, ANY],
-            out_specs=ANY,
-            scratch_shapes=[pltpu.SemaphoreType.DMA((heads - 1,))],
-            compiler_params=full,
-            cost_estimate=cost(1, heads * columns * tile * 4),
-            name="others",
-        )(place, weights)
-        others, stat = lax.optimization_barrier((others, stat))
-        weights = lax.all_gather(others, "chip")
-    stats = lax.all_gather(stat, CTX)
+    stats = lax.all_gather(lax.all_gather(stat, "core"), "chip").reshape(count, -1, rows)
     grads = pl.pallas_call(
         lambda *refs: gradient_kernel(count, *refs),
         out_shape=jax.ShapeDtypeStruct((3 * rows + nf2 * rows // LANES, LANES), bf16),
@@ -633,12 +559,12 @@
     )(place, *recv, own, query, feat, sheet, stats)
     grads = lax.all_gather(grads, "tp")
     if not spread:
-        return (attended, merge(grads, weights, rows, dim))
+        return (attended, merge(place, grads, weights, True, 1, rows, dim))
     weights, grads = lax.optimization_barrier((weights, grads))
+    weights = weights.reshape(chips, -1, columns, tile)
     swapped = lax.ppermute(weights, "core", swap)
-    total = merge_half(place, grads, weights, window_weight, value_weight, fw_t, True, None)
-    total = merge_half(place, grads, swapped, window_weight, value_weight, fw_t, False, total)
-    return (attended, total)
+    total = merge(place, grads, weights, False, 2, rows, dim, 0)
+    return (attended, merge(place, grads, swapped, False, 2, rows, dim, 1, total))
 
 
 def solution(mesh):

time: 120 us -> 109 us (0.908)
  Pallas kernels: 45.5 us -> 21.7 us
  blocking collectives: 28.5 us -> 35.3 us
  local copies, waits for them, and re-layouts: 5.06 us -> 8.28 us
  waiting for transfers between devices: 20.4 us -> 23.2 us
    pallas_call x4 -> x3, Pallas kernels: 33.3 us -> 11.3 us  [the longest x2 8.92 us: merge(): pl.pallas_call(lambda *refs: merge_kernel(by_head, *refs), out_shape=jax....]
    all_gather x1, blocking collectives: 19.3 us -> 25.3 us  [per_device(): grads = lax.all_gather(grads, 'tp')]
    unnamed x20 -> x16, local copies, waits for them, and re-layouts: 5.06 us -> 8.28 us
    pallas_call x1, Pallas kernels: 5.05 us -> 3.23 us  [per_device(): pl.pallas_call(project_kernel, out_shape=[block] * (chips + 2) + [jax.Sha...]
    ppermute x1, waiting for transfers between devices: 0.21 us -> 1.73 us  [per_device(): swapped = lax.ppermute(weights, 'core', swap)]
    ppermute x3, waiting for transfers between devices: 6.97 us -> 8.27 us  [per_device(): lax.ppermute(sends[d], 'chip', [(i, i ^ d) for i in range(chips)])]
    all_gather x1 -> x2, blocking collectives: 9.19 us -> 9.98 us  [the longest x1 8.18 us: per_device(): lax.all_gather(lax.all_gather(stat, 'core'), 'chip')]
    all_gather x2 -> x1, waiting for transfers between devices: 12.2 us -> 12.1 us  [per_device(): lax.all_gather(packed[0], ('chip', 'tp'))]
  transfers between devices with their start and end apart: 10 -> 9, of which waited for: 7 -> 6; matrix products, arithmetic and copies ran while one was open for 0% -> 0% of each run, Pallas kernels for 14% -> 14%
where the time goes in v4:
time: 109 us; the launch traced here: 108 us
  blocking collectives  35.3 us (32%)
  waiting for transfers between devices  23.2 us (21%)
  Pallas kernels  21.7 us (20%)
  between operations  14.1 us (13%)
  local copies, waits for them, and re-layouts  8.28 us (8%)
  starting transfers between devices  5.15 us (5%)
    all_gather x1, blocking collectives, per_device(): grads = lax.all_gather(grads, 'tp')  25.3 us
    all_gather x1, waiting for transfers between devices, per_device(): lax.all_gather(packed[0], ('chip', 'tp'))  12.1 us
    pallas_call x2, Pallas kernels, merge(): pl.pallas_call(lambda *refs: merge_kernel(by_head, *refs), out_shape=jax....  8.92 us
    unnamed x16, local copies, waits for them, and re-layouts  8.28 us
    ppermute x3, waiting for transfers between devices, per_device(): lax.ppermute(sends[d], 'chip', [(i, i ^ d) for i in range(chips)])  8.27 us
    all_gather x1, blocking collectives, per_device(): lax.all_gather(lax.all_gather(stat, 'core'), 'chip')  8.18 us
    ppermute x3, starting transfers between devices, per_device(): lax.ppermute(sends[d], 'chip', [(i, i ^ d) for i in range(chips)])  4.54 us
    pallas_call x1, Pallas kernels, per_device(): pl.pallas_call(lambda *refs: gradient_kernel(count, *refs), out_shape=jax...  4.22 us
  transfers between devices with their start and end apart: 9, of which 6 were waited for; matrix products, arithmetic and copies ran while one was open for 0% of the time, Pallas kernels for 14%

profile of v4, /device:TPU:0, one launch (start us, length us, event | category | flops | bytes accessed | tf_op | source)
XLA Modules:
  0.0 108.3 jit_solution(5798931695785379608)
XLA Ops:
  7.2 0.0 all-gather.5.cloned.1.call-start
  7.2 0.7 pad_add_fusion.place_ref.refs_0_
  7.9 2.4 %pack.1 = bf16[1,416,256]{2,1,0:T(8,128)(2,1)} custom-call(s32[4]{0:T(128)} %pad_add_fusion.place_ref.refs_0_, bf16[2048,256]{1,0:T(8,128)(2,1)} %ww_hbm.3, bf16[2048,128]{1,0:T(8,128)(2,1)} %vw_hbm.3, bf16[32,2048]{1,0:T(8,128)(2,1)} %bitcast.9), custom_call_target="tpu_custom_call" | custom-call | flops 1 | bytes 425984 | tf_op jit(solution)/shard_map/pack/pallas_call | solution.py:478
  10.3 0.0 all-gather.5.cloned.1.call-update
  10.3 0.0 copy-start
  10.3 1.2 %copy-done = bf16[2048,256]{1,0:T(8,128)(2,1)S(1)} copy-done((bf16[2048,256]{1,0:T(8,128)(2,1)S(1)}, bf16[2048,256]{1,0:T(8,128)(2,1)}, u32[]{:S(2)}) %copy-start) | copy-done | bytes 1048600
  11.6 0.0 copy-start.1
  11.6 1.0 copy-done.1
  12.6 0.0 copy-start.2
  12.6 1.2 %copy-done.2 = bf16[256,2048]{1,0:T(8,128)(2,1)S(1)} copy-done((bf16[256,2048]{1,0:T(8,128)(2,1)S(1)}, bf16[256,2048]{1,0:T(8,128)(2,1)}, u32[]{:S(2)}) %copy-start.2) | copy-done | bytes 1048600
  13.8 0.0 copy-start.3
  13.8 0.9 copy-done.3
  14.7 0.0 copy-start.4
  14.7 0.8 copy-done.4
  15.6 0.0 copy-start.5
  15.6 0.7 copy-done.5
  16.2 0.0 copy-start.6
  16.2 0.7 copy-done.6
  16.9 3.2 %project.1 = (bf16[560,128]{1,0:T(8,128)(2,1)S(1)}, bf16[560,128]{1,0:T(8,128)(2,1)S(1)}, bf16[560,128]{1,0:T(8,128)(2,1)S(1)}, bf16[560,128]{1,0:T(8,128)(2,1)S...) custom-call(s32[4]{0:T(128)S(1)} %copy-done.5, ...), custom_call_target="tpu_custom_call" | custom-call | flops 436207616 | bytes 4194304 | tf_op jit(solution)/shard_map/project/pallas_call | solution.py:497
  20.1 3.0 %collective-permute-start.1 = (bf16[560,128]{1,0:T(8,128)(2,1)S(1)}, bf16[560,128]{1,0:T(8,128)(2,1)S(1)}, u32[]{:S(2)}, u32[]{:S(2)}) collective-permute-start(bf16[560,128]{1,0:T(8,128)(2,1)S(1)} %get-tuple-element.16), channel_id=1, source_target_pairs={{0,8},{8,0},{16,24},{24,16},{1,9},{9,1},{17,25},{25,17},{2,10},{10... | collective-permute-start | bytes 430088 | tf_op jit(solution)/shard_map/ppermute | solution.py:524
  23.1 1.5 %collective-permute-start.3 = (bf16[560,128]{1,0:T(8,128)(2,1)S(1)}, bf16[560,128]{1,0:T(8,128)(2,1)S(1)}, u32[]{:S(2)}, u32[]{:S(2)}) collective-permute-start(bf16[560,128]{1,0:T(8,128)(2,1)S(1)} %get-tuple-element.17), channel_id=1, source_target_pairs={{0,16},{8,24},{16,0},{24,8},{1,17},{9,25},{17,1},{25,9},{2,18},{10... | collective-permute-start | bytes 430088 | tf_op jit(solution)/shard_map/ppermute | solution.py:524
  24.7 0.0 collective-permute-start.5
  24.7 0.0 collective-permute-start
  24.7 4.6 %collective-permute-done.1.refs_2_ = bf16[560,128]{1,0:T(8,128)(2,1)S(1)} collective-permute-done((bf16[560,128]{1,0:T(8,128)(2,1)S(1)}, bf16[560,128]{1,0:T(8,128)(2,1)S(1)}, u32[]{:S(2)}, u32[]{:S(2)}) %collective-permute-start.1) | collective-permute-done | bytes 143392 | tf_op jit(solution)/shard_map/ppermute | solution.py:524
  29.3 0.0 collective-permute-start.2
  29.3 3.7 %collective-permute-done.3.refs_4_ = bf16[560,128]{1,0:T(8,128)(2,1)S(1)} collective-permute-done((bf16[560,128]{1,0:T(8,128)(2,1)S(1)}, bf16[560,128]{1,0:T(8,128)(2,1)S(1)}, u32[]{:S(2)}, u32[]{:S(2)}) %collective-permute-start.3) | collective-permute-done | bytes 143392 | tf_op jit(solution)/shard_map/ppermute | solution.py:524
  33.0 0.0 collective-permute-start.4
  33.0 0.0 collective-permute-done.5.refs_6_
  33.0 0.5 collective-permute-start.6
  33.5 0.0 collective-permute-done.refs_1_
  33.5 0.0 collective-permute-done.2.refs_3_
  33.5 0.8 collective-permute-done.4.refs_5_
  34.3 0.2 collective-permute-done.6.refs_7_
  34.5 2.9 %query_side.1 = (bf16[256,128]{1,0:T(8,128)(2,1)}, f32[8,256]{1,0:T(8,128)S(1)}, f32[256,128]{1,0:T(8,128)S(1)}) custom-call(s32[4]{0:T(128)S(1)} %copy-done.5, bf16[560,128]{1,0:T(8,128)(2,1)S(1)} %collective-permute-done.refs_1_, bf16[560,128]{1,0:T(8,128)(2,1)S(1)} %collective-permute-done.1.refs_2_, bf16[560,128]{1,0:T(8,128)(2,1)S(1)} %collective-permute-done.2.refs_3_, ...), custom_call_target="tpu_custom_call" | custom-call | flops 1000000000 | bytes 2097152 | tf_op jit(solution)/shard_map/query_side/pallas_call | solution.py:532
  37.4 1.8 %all-gather = f32[16,256]{1,0:T(8,128)S(1)} all-gather(f32[8,256]{1,0:T(8,128)S(1)} %get-tuple-element.25), channel_id=2, replica_groups=mesh['chip'=4,'core'=2,'tp'=4] {'core'}, dimensions={0}, use_global_device_ids=true | all-gather | bytes 24576 | tf_op jit(solution)/shard_map/all_gather | solution.py:550
  39.2 8.2 %all-gather.1.refs_12_ = f32[8,8,256]{2,1,0:T(8,128)S(1)} all-gather(f32[2,8,256]{2,1,0:T(8,128)S(1)} %bitcast.16), channel_id=3, replica_groups=mesh['chip'=4,'core'=2,'tp'=4] {'chip'}, dimensions={0}, use_global_device_ids=true | all-gather | bytes 81920 | tf_op jit(solution)/shard_map/all_gather | solution.py:550
  47.4 4.2 %gradients.1 = bf16[832,128]{1,0:T(8,128)(2,1)S(1)} custom-call(s32[4]{0:T(128)S(1)} %copy-done.5, bf16[560,128]{1,0:T(8,128)(2,1)S(1)} %collective-permute-done.refs_1_, bf16[560,128]{1,0:T(8,128)(2,1)S(1)} %collective-permute-done.1.refs_2_, bf16[560,128]{1,0:T(8,128)(2,1)S(1)} %collective-permute-done.2.refs_3_, ...), custom_call_target="tpu_custom_call" | custom-call | flops 1000000000 | bytes 2097152 | tf_op jit(solution)/shard_map/gradients/pallas_call | solution.py:551
  51.6 25.3 %all-gather.2 = bf16[3328,128]{1,0:T(8,128)(2,1)} all-gather(bf16[832,128]{1,0:T(8,128)(2,1)S(1)} %gradients.1), channel_id=4, replica_groups=mesh['chip'=4,'core'=2,'tp'=4] {'tp'}, dimensions={0}, use_global_device_ids=true | all-gather | bytes 1064960 | tf_op jit(solution)/shard_map/all_gather | solution.py:560
  76.9 12.1 %all-gather.5.cloned.1.call-done = bf16[16,416,256]{2,1,0:T(8,128)(2,1)} async-done(((bf16[1,416,256]{2,1,0:T(8,128)(2,1)}), bf16[16,416,256]{2,1,0:T(8,128)(2,1)}) %all-gather.5.cloned.1.call-update) | async-done | bytes 3407888 | tf_op jit(solution)/shard_map/all_gather | solution.py:493
  89.0 0.1 collective-permute-start.7
  89.1 4.5 %head_sum.2.refs_3_ = bf16[256,2048]{1,0:T(8,128)(2,1)} custom-call(s32[4]{0:T(128)} %pad_add_fusion.place_ref.refs_0_, bf16[4,832,128]{2,1,0:T(8,128)(2,1)} %bitcast.12, bf16[4,4,416,256]{3,2,1,0:T(8,128)(2,1)} %bitcast.15), custom_call_target="tpu_custom_call" | custom-call | flops 436207616 | bytes 3407872 | tf_op jit(solution)/shard_map/head_sum/pallas_call | solution.py:442
  93.5 1.7 %collective-permute-done.7.refs_2_ = bf16[4,4,416,256]{3,2,1,0:T(8,128)(2,1)S(1)} collective-permute-done((bf16[4,4,416,256]{3,2,1,0:T(8,128)(2,1)}, bf16[4,4,416,256]{3,2,1,0:T(8,128)(2,1)S(1)}, u32[]{:S(2)}, u32[]{:S(2)}) %collective-permute-start.7) | collective-permute-done | bytes 3407904 | tf_op jit(solution)/shard_map/ppermute | solution.py:565
  95.3 0.0 copy-start.7
  95.3 1.7 %copy-done.7 = bf16[4,4,416,256]{3,2,1,0:T(8,128)(2,1)} copy-done((bf16[4,4,416,256]{3,2,1,0:T(8,128)(2,1)}, bf16[4,4,416,256]{3,2,1,0:T(8,128)(2,1)S(1)}, u32[]{:S(2)}) %copy-start.7) | copy-done | bytes 3407896
  97.0 4.5 %head_sum.3 = bf16[256,2048]{1,0:T(8,128)(2,1)} custom-call(s32[4]{0:T(128)} %pad_add_fusion.place_ref.refs_0_, bf16[4,832,128]{2,1,0:T(8,128)(2,1)} %bitcast.13, bf16[4,4,416,256]{3,2,1,0:T(8,128)(2,1)} %copy-done.7, bf16[256,2048]{1,0:T(8,128)(2,1)} %head_sum.2.refs_3_), custom_call_target="tpu_custom_call", output_to_operand_aliasing={{}: (3, {})} | custom-call | flops 436207616 | bytes 3407872 | tf_op jit(solution)/shard_map/head_sum/pallas_call | solution.py:442
Async XLA Ops:
  7.2 81.9 %all-gather.5.cloned.1.call-start = ((), (), s32[]{:S(2)}) async-start(), calls=%async_computation | async-start | bytes 3620864 | tf_op jit(solution)/shard_map/all_gather | solution.py:493
  10.3 1.2 %copy-start = (bf16[2048,256]{1,0:T(8,128)(2,1)S(1)}, bf16[2048,256]{1,0:T(8,128)(2,1)}, u32[]{:S(2)}) copy-start(bf16[2048,256]{1,0:T(8,128)(2,1)} %ww_hbm.3) | copy-start | bytes 3145732
  11.6 1.0 copy-start.1
  12.6 1.2 %copy-start.2 = (bf16[256,2048]{1,0:T(8,128)(2,1)S(1)}, bf16[256,2048]{1,0:T(8,128)(2,1)}, u32[]{:S(2)}) copy-start(bf16[256,2048]{1,0:T(8,128)(2,1)} %tok_hbm.1) | copy-start | bytes 3145732
  13.8 0.9 copy-start.3
  14.7 0.8 copy-start.4
  15.6 0.7 copy-start.5
  16.2 0.7 copy-start.6
  20.1 9.1 %collective-permute-start.1 = (bf16[560,128]{1,0:T(8,128)(2,1)S(1)}, bf16[560,128]{1,0:T(8,128)(2,1)S(1)}, u32[]{:S(2)}, u32[]{:S(2)}) collective-permute-start(bf16[560,128]{1,0:T(8,128)(2,1)S(1)} %get-tuple-element.16), channel_id=1, source_target_pairs={{0,8},{8,0},{16,24},{24,16},{1,9},{9,1},{17,25},{25,17},{2,10},{10... | collective-permute-start | bytes 430088 | tf_op jit(solution)/shard_map/ppermute | solution.py:524
  23.1 9.8 %collective-permute-start.3 = (bf16[560,128]{1,0:T(8,128)(2,1)S(1)}, bf16[560,128]{1,0:T(8,128)(2,1)S(1)}, u32[]{:S(2)}, u32[]{:S(2)}) collective-permute-start(bf16[560,128]{1,0:T(8,128)(2,1)S(1)} %get-tuple-element.17), channel_id=1, source_target_pairs={{0,16},{8,24},{16,0},{24,8},{1,17},{9,25},{17,1},{25,9},{2,18},{10... | collective-permute-start | bytes 430088 | tf_op jit(solution)/shard_map/ppermute | solution.py:524
  24.7 8.3 %collective-permute-start.5 = (bf16[560,128]{1,0:T(8,128)(2,1)S(1)}, bf16[560,128]{1,0:T(8,128)(2,1)S(1)}, u32[]{:S(2)}, u32[]{:S(2)}) collective-permute-start(bf16[560,128]{1,0:T(8,128)(2,1)S(1)} %get-tuple-element.18), channel_id=1, source_target_pairs={{0,24},{8,16},{16,8},{24,0},{1,25},{9,17},{17,9},{25,1},{2,26},{10... | collective-permute-start | bytes 430088 | tf_op jit(solution)/shard_map/ppermute | solution.py:524
  24.7 8.8 %collective-permute-start = (bf16[560,128]{1,0:T(8,128)(2,1)S(1)}, bf16[560,128]{1,0:T(8,128)(2,1)S(1)}, u32[]{:S(2)}, u32[]{:S(2)}) collective-permute-start(bf16[560,128]{1,0:T(8,128)(2,1)S(1)} %get-tuple-element.15), channel_id=1, source_target_pairs={{0,4},{4,0},{1,5},{5,1},{2,6},{6,2},{3,7},{7,3},{8,12},{12,8},{9,1... | collective-permute-start | bytes 430088 | tf_op jit(solution)/shard_map/ppermute | solution.py:525
  29.3 4.2 %collective-permute-start.2 = (bf16[560,128]{1,0:T(8,128)(2,1)S(1)}, bf16[560,128]{1,0:T(8,128)(2,1)S(1)}, u32[]{:S(2)}, u32[]{:S(2)}) collective-permute-start(bf16[560,128]{1,0:T(8,128)(2,1)S(1)} %collective-permute-done.1.refs_2_), channel_id=1, source_target_pairs={{0,4},{4,0},{1,5},{5,1},{2,6},{6,2},{3,7},{7,3},{8,12},{12,8},{9,1... | collective-permute-start | bytes 430088 | tf_op jit(solution)/shard_map/ppermute | solution.py:527
  33.0 1.4 %collective-permute-start.4 = (bf16[560,128]{1,0:T(8,128)(2,1)S(1)}, bf16[560,128]{1,0:T(8,128)(2,1)S(1)}, u32[]{:S(2)}, u32[]{:S(2)}) collective-permute-start(bf16[560,128]{1,0:T(8,128)(2,1)S(1)} %collective-permute-done.3.refs_4_), channel_id=1, source_target_pairs={{0,4},{4,0},{1,5},{5,1},{2,6},{6,2},{3,7},{7,3},{8,12},{12,8},{9,1... | collective-permute-start | bytes 430088 | tf_op jit(solution)/shard_map/ppermute | solution.py:527
  33.0 1.6 %collective-permute-start.6 = (bf16[560,128]{1,0:T(8,128)(2,1)S(1)}, bf16[560,128]{1,0:T(8,128)(2,1)S(1)}, u32[]{:S(2)}, u32[]{:S(2)}) collective-permute-start(bf16[560,128]{1,0:T(8,128)(2,1)S(1)} %collective-permute-done.5.refs_6_), channel_id=1, source_target_pairs={{0,4},{4,0},{1,5},{5,1},{2,6},{6,2},{3,7},{7,3},{8,12},{12,8},{9,1... | collective-permute-start | bytes 430088 | tf_op jit(solution)/shard_map/ppermute | solution.py:527
  89.0 6.2 %collective-permute-start.7 = (bf16[4,4,416,256]{3,2,1,0:T(8,128)(2,1)}, bf16[4,4,416,256]{3,2,1,0:T(8,128)(2,1)S(1)}, u32[]{:S(2)}, u32[]{:S(2)}) collective-permute-start(bf16[4,4,416,256]{3,2,1,0:T(8,128)(2,1)} %bitcast.14), channel_id=1, source_target_pairs={{0,4},{4,0},{1,5},{5,1},{2,6},{6,2},{3,7},{7,3},{8,12},{12,8},{9,1... | collective-permute-start | bytes 10223624 | tf_op jit(solution)/shard_map/ppermute | solution.py:565
  95.3 1.7 %copy-start.7 = (bf16[4,4,416,256]{3,2,1,0:T(8,128)(2,1)}, bf16[4,4,416,256]{3,2,1,0:T(8,128)(2,1)S(1)}, u32[]{:S(2)}) copy-start(bf16[4,4,416,256]{3,2,1,0:T(8,128)(2,1)S(1)} %collective-permute-done.7.refs_2_) | copy-start | bytes 10223620
Sparse Core Ops, SparseCore 0:
  11.3 77.6 all-gather.4

commit v5 on v2

--- a/solution.py
+++ b/solution.py
@@ -56,14 +56,17 @@
     )
 
 
-def project_kernel(place_ref, tok_hbm, fw_hbm, ww_hbm, vw_hbm, ld_hbm, do_hbm, *rest):
-    *sends, keys_ref, query_ref, feat_ref, cum_ref, pack_ref = rest[:-8]
+def block_index():
+    return lax.axis_index("chip") * lax.axis_size("core") + lax.axis_index("core")
+
+
+def project_kernel(tok_hbm, fw_hbm, ww_hbm, vw_hbm, ld_hbm, do_hbm, *rest):
+    *sends, keys_ref, query_ref, feat_ref, cum_ref = rest[:-8]
     tok_ref, fw_ref, ww_ref, vw_ref, ld_ref, do_ref, sems, small = rest[-8:]
-    me, piece = place_ref[0], place_ref[1]
+    me = block_index()
     rows, dim = tok_ref.shape
     dh = do_ref.shape[1]
     nf = fw_ref.shape[0] // 2
-    count = len(sends) + 1
     span = dim // CHUNKS
     copies = []
     for c in range(CHUNKS):
@@ -98,19 +101,17 @@
     tail = jnp.concatenate(pieces + [jnp.zeros((10, LANES), f32)], axis=0).astype(bf16)
 
     feat = jnp.zeros((rows, 2 * nf), f32)
-    window = jnp.zeros((rows, 2 * dh), f32)
-    values = jnp.zeros((rows, dh), f32)
+    main = jnp.zeros((rows, 3 * dh), f32)
     for c in range(CHUNKS):
         for copy in copies[c]:
             copy.wait()
         part = slice(c * span, (c + 1) * span)
         tok = tok_ref[:, part]
         feat += nt(tok, fw_ref[:, part])
-        window += nn(tok, ww_ref[part, :])
-        values += nn(tok, vw_ref[part, :])
+        main += nn(tok, jnp.concatenate([ww_ref[part, :], vw_ref[part, :]], axis=1))
     feat = feat.astype(bf16)
-    window = window.astype(bf16)
-    values = values.astype(bf16)
+    window = main[:, : 2 * dh].astype(bf16)
+    values = main[:, 2 * dh :].astype(bf16)
     feat_ref[...] = feat
     small_row, small_col = iotas(2 * nf)
     feat_t = nt((small_row == small_col).astype(bf16), feat).astype(bf16)
@@ -131,19 +132,36 @@
 
     put_keys(keys_ref)
     put_query(query_ref)
-    for d in range(1, count):
-        later = partner(me, d, count) > me
-        ref = sends[d - 1]
+    for at, ref in enumerate(sends):
+        later = jnp.bitwise_xor(me, max(2 * at, 1)) > me
         pl.when(later)(lambda ref=ref: put_keys(ref))
         pl.when(jnp.logical_not(later))(lambda ref=ref: put_query(ref))
 
-    tile = pack_ref.shape[2]
-    for p in range(pack_ref.shape[0]):
-        at = pl.multiple_of((piece + p) * tile, tile)
-        part = pl.ds(at, tile)
-        pack_ref[p, 0 : 2 * dh, :] = jnp.transpose(ww_ref[part, :].astype(f32)).astype(bf16)
-        pack_ref[p, 2 * dh : 3 * dh, :] = jnp.transpose(vw_ref[part, :].astype(f32)).astype(bf16)
-        pack_ref[p, 3 * dh : 3 * dh + 2 * nf, :] = fw_ref[:, part]
+
+def pack_kernel(ww_hbm, vw_hbm, fw_hbm, own_ref, *rest):
+    sends, sems = rest[:-1], rest[-1]
+    head, core = lax.axis_index("tp"), lax.axis_index("core")
+    nf2 = fw_hbm.shape[0]
+    tile = (own_ref.shape[1] * LANES) // (3 * LANES + nf2)
+    parts = [(own_ref.at[k], 2 * head + k) for k in range(2)]
+    parts += [(ref, 2 * jnp.bitwise_xor(head, t + 1) + core) for t, ref in enumerate(sends)]
+    copies = []
+    for n, (ref, piece) in enumerate(parts):
+        rows = pl.ds(pl.multiple_of(piece * tile, tile), tile)
+        moves = [
+            (ww_hbm.at[rows, pl.ds(0, LANES)], ref.at[pl.ds(0, tile), :]),
+            (ww_hbm.at[rows, pl.ds(LANES, LANES)], ref.at[pl.ds(tile, tile), :]),
+            (vw_hbm.at[rows, :], ref.at[pl.ds(2 * tile, tile), :]),
+        ]
+        for m in range(tile // LANES):
+            lanes = pl.ds(pl.multiple_of(piece * tile + m * LANES, LANES), LANES)
+            moves.append((fw_hbm.at[:, lanes], ref.at[pl.ds(3 * tile + m * nf2, nf2), :]))
+        for m, (src, dst) in enumerate(moves):
+            copies.append(pltpu.make_async_copy(src, dst, sems.at[n, m]))
+    for copy in copies:
+        copy.start()
+    for copy in copies:
+        copy.wait()
 
 
 def between(totals, low, high):
@@ -159,7 +177,7 @@
     return lax.fori_loop(1, count, body, carry)
 
 
-def query_kernel(count, place_ref, *rest):
+def query_kernel(count, *rest):
     recvs = rest[: -10]
     (own_ref, query_ref, feat_ref, cum_ref, att_ref, stat_ref, sheet_ref, near_ref, p_ref,
      cums_ref) = rest[-10:]
@@ -167,7 +185,7 @@
     def recv(d):
         return recvs[d - 1] if len(recvs) > 1 else recvs[0].at[d - 1]
 
-    me = place_ref[0]
+    me = block_index()
     rows, dh = att_ref.shape
     nf = feat_ref.shape[1] // 2
     back = WINDOW // rows
@@ -264,14 +282,18 @@
     stat_ref[...] = jnp.transpose(sheet)[0:8, :]
 
 
-def gradient_kernel(count, place_ref, *rest):
-    recvs = rest[:-6]
-    own_ref, query_ref, feat_ref, sheet_ref, stat_ref, grad_ref = rest[-6:]
+def gradient_kernel(count, *rest):
+    parts = len(rest) - 7 >> 1
+    recvs, stats = rest[:parts], rest[parts : 2 * parts]
+    own_ref, query_ref, feat_ref, sheet_ref, mine_ref, grad_ref, total_ref = rest[2 * parts :]
 
     def recv(d):
         return recvs[d - 1] if len(recvs) > 1 else recvs[0].at[d - 1]
 
-    me = place_ref[0]
+    def stat(d):
+        return stats[d - 1] if len(stats) > 1 else stats[0].at[d - 1]
+
+    me = block_index()
     rows = feat_ref.shape[0]
     dh = LANES
     nf = feat_ref.shape[1] // 2
@@ -285,8 +307,15 @@
     q, k = feat_ref[:, :nf], feat_ref[:, nf:]
     lse_c, dw_c = sheet_ref[:, 0:1], sheet_ref[:, 1:2]
     rden_c, dl_c, cum_c = sheet_ref[:, 2:3], sheet_ref[:, 3:4], sheet_ref[:, 4:5]
-    totals = jnp.concatenate([stat_ref[j, 4:5, rows - 1 : rows] for j in range(count)], axis=0)
-    own_cum = stat_ref[me, 4:5, :]
+    own_cum = mine_ref[4:5, :]
+    total_ref[pl.ds(me, 1), :] = own_cum[:, rows - LANES :]
+
+    def place(d, carry):
+        total_ref[pl.ds(partner(me, d, count), 1), :] = stat(d)[4:5, rows - LANES :]
+        return carry
+
+    over_partners(count, place, 0)
+    totals = total_ref[:, LANES - 1 :]
     growth_c = jnp.exp(cum_c) * rden_c
     tail_c = jnp.exp(own_cum[:, rows - 1 : rows] - cum_c)
 
@@ -305,12 +334,12 @@
 
     s = nt(wk, wq) * scale
     causal = at_row <= at_col
-    p = jnp.where(causal, jnp.exp(s - stat_ref[me, 0:1, :]), 0.0)
+    p = jnp.where(causal, jnp.exp(s - mine_ref[0:1, :]), 0.0)
     dp = nt(v, do)
-    dwk = nn((p * (dp - stat_ref[me, 1:2, :])).astype(bf16), wq)
+    dwk = nn((p * (dp - mine_ref[1:2, :])).astype(bf16), wq)
     x = nn(k, wide(query_ref, feat_at, nf)) * feat_scale
-    e = jnp.where(causal, jnp.exp(jnp.minimum(own_cum - cum_c, 0.0)), 0.0) * stat_ref[me, 2:3, :]
-    dx = (dp - stat_ref[me, 3:4, :]) * e * (1.0 + x)
+    e = jnp.where(causal, jnp.exp(jnp.minimum(own_cum - cum_c, 0.0)), 0.0) * mine_ref[2:3, :]
+    dx = (dp - mine_ref[3:4, :]) * e * (1.0 + x)
     dkt = nt(wide(query_ref, feat_at, nf), dx.astype(bf16))
     dv = nn((p + (1.0 + x + 0.5 * x * x) * e).astype(bf16), do)
 
@@ -327,7 +356,7 @@
         other_w = view[0:rows, :]
         other_v = view[rows : 2 * rows, :]
         other_f = wide(view, feat_at, nf)
-        st = stat_ref[j]
+        st = stat(d)
         zero = jnp.zeros((1, rows), f32)
         cum = st[4:5, :]
         gap = between(totals, jnp.minimum(me, j), jnp.maximum(me, j))
@@ -361,52 +390,92 @@
     put_wide(grad_ref, 3 * rows, dft)
 
 
-def merge_kernel(grad_ref, *rest):
+def gather_rows(grad_ref, order, cat_ref, feat_ref):
+    rows = cat_ref.shape[0]
+    nf2 = feat_ref.shape[1] // len(order)
+    for at, h in enumerate(order):
+        for part in range(3):
+            lane = (3 * at + part) * LANES
+            cat_ref[:, lane : lane + LANES] = grad_ref[h, part * rows : (part + 1) * rows, :]
+    dft = jnp.concatenate([wide(grad_ref.at[h], 3 * rows, nf2) for h in order], axis=0)
+    feat_ref[...] = jnp.transpose(dft.astype(f32)).astype(bf16)
+
+
+def share_kernel(grad_ref, own_ref, *rest):
     heads = grad_ref.shape[0]
-    weights, out_ref, cat_ref, feat_ref = rest[:heads], rest[-3], rest[-2], rest[-1]
-    rows = out_ref.shape[0]
+    near, far = rest[: heads - 1], rest[heads - 1 : 2 * heads - 2]
+    first_ref, second_ref, cat_ref, feat_ref = rest[-4:]
+    rows = cat_ref.shape[0]
+    tile = first_ref.shape[1]
+    nf2 = feat_ref.shape[1] // heads
+    head, core = lax.axis_index("tp"), lax.axis_index("core")
+    gather_rows(
+        grad_ref, [head] + [jnp.bitwise_xor(head, t) for t in range(1, heads)], cat_ref, feat_ref
+    )
+
+    def product(out_ref, views):
+        main = jnp.concatenate(
+            [v[m * tile : (m + 1) * tile, :] for v in views for m in range(3)], axis=1
+        )
+        feats = jnp.concatenate([wide(v, 3 * tile, nf2) for v in views], axis=0)
+        out_ref[...] = (nt(cat_ref[...], main) + nn(feat_ref[...], feats)).astype(bf16)
+
+    for flag, ours, theirs in ((0, first_ref, second_ref), (1, second_ref, first_ref)):
+
+        @pl.when(core == flag)
+        def _():
+            product(ours, [own_ref.at[flag], *near])
+            product(theirs, [own_ref.at[1 - flag], *far])
+
+
+def lay_kernel(first_ref, second_ref, out_ref):
+    shares, _, tile = first_ref.shape
+    for z in range(shares):
+        at = 2 * z * tile
+        out_ref[:, at : at + tile] = first_ref[z]
+        out_ref[:, at + tile : at + 2 * tile] = second_ref[z]
+
+
+def merge_kernel(grad_ref, weight_ref, out_ref, cat_ref, feat_ref):
+    heads = grad_ref.shape[0]
+    tile = out_ref.shape[1]
     lanes = 3 * LANES
-    nf2 = weights[0].shape[-2] - lanes
+    nf2 = feat_ref.shape[1] // heads
 
     @pl.when(pl.program_id(0) == 0)
     def _():
-        for h in range(heads):
-            for part in range(3):
-                at = (3 * h + part) * LANES
-                cat_ref[:, at : at + LANES] = grad_ref[h, part * rows : (part + 1) * rows, :]
-        dft = jnp.concatenate([wide(grad_ref.at[h], 3 * rows, nf2) for h in range(heads)], axis=0)
-        feat_ref[...] = jnp.transpose(dft.astype(f32)).astype(bf16)
-
-    main = jnp.concatenate([w[0, 0, 0:lanes, :] for w in weights], axis=0)
-    feats = jnp.concatenate([w[0, 0, lanes:, :] for w in weights], axis=0)
-    out_ref[...] = (nn(cat_ref[...], main) + nn(feat_ref[...], feats)).astype(bf16)
+        gather_rows(grad_ref, range(heads), cat_ref, feat_ref)
+
+    views = [weight_ref.at[h] for h in range(heads)]
+    main = jnp.concatenate([v[:, 0:lanes] for v in views], axis=1)
+    feats = jnp.concatenate([v[:, lanes:] for v in views], axis=1)
+    out_ref[...] = (nt(cat_ref[...], main) + nt(feat_ref[...], feats)).astype(bf16)
 
 
 VMEM = pl.BlockSpec(memory_space=pltpu.VMEM)
-SMEM = pl.BlockSpec(memory_space=pltpu.SMEM)
-ANY = pl.BlockSpec(memory_space=pl.ANY)
-params = pltpu.CompilerParams(vmem_limit_bytes=48 * 1024 * 1024)
+HBM = pl.BlockSpec(memory_space=pltpu.HBM)
+params = pltpu.CompilerParams(vmem_limit_bytes=32 * 1024 * 1024)
+
+
+def in_hbm(*arrays):
+    return [pltpu.with_memory_space_constraint(a, pltpu.HBM) for a in arrays]
 
 
 def cost(flops, nbytes, exps=0):
     return pl.CostEstimate(flops=flops, bytes_accessed=nbytes, transcendentals=exps)
 
 
-def merge(grads, weights, by_head, rows, dim):
-    heads = grads.shape[0]
-    columns, tile = weights.shape[2:]
-    pieces = dim // tile
-
-    def at(h):
-        return (lambda i: (h, i, 0, 0)) if by_head else (lambda i: (i, h, 0, 0))
-
-    specs = [pl.BlockSpec(grads.shape, lambda i: (0, 0, 0))]
-    specs += [pl.BlockSpec((1, 1, columns, tile), at(h)) for h in range(heads)]
+def merge(grads, weights, rows, dim):
+    heads, _, columns = weights.shape
+    tile = 2 * LANES
     return pl.pallas_call(
         merge_kernel,
         out_shape=jax.ShapeDtypeStruct((rows, dim), bf16),
-        grid=(pieces,),
-        in_specs=specs,
+        grid=(dim // tile,),
+        in_specs=[
+            pl.BlockSpec(grads.shape, lambda i: (0, 0, 0)),
+            pl.BlockSpec((heads, tile, columns), lambda i: (0, i, 0)),
+        ],
         out_specs=pl.BlockSpec((rows, tile), lambda i: (0, i)),
         scratch_shapes=[
             pltpu.VMEM((rows, 3 * LANES * heads), bf16),
@@ -415,7 +484,7 @@
         compiler_params=params,
         cost_estimate=cost(2 * rows * dim * heads * columns, heads * dim * columns * 2),
         name="head_sum",
-    )(grads, *([weights] * heads))
+    )(grads, weights)
 
 
 def per_device(tokens, feature_weight, window_weight, value_weight, log_decay, out_grad):
@@ -424,24 +493,21 @@
     nf = nf2 // 2
     dh = value_weight.shape[1]
     columns = 3 * dh + nf2
-    count = lax.axis_size(CTX)
-    me = lax.axis_index(CTX)
+    chips, count, heads = lax.axis_size("chip"), lax.axis_size(CTX), lax.axis_size("tp")
     tile = 2 * LANES
-    spread = count * tile == dim
-    pieces = 1 if spread else dim // tile
-    place = jnp.stack([me, me if spread else 0 * me]).astype(jnp.int32)
+    fw_t = feature_weight.T
+
     payload = 2 * rows + 2 * nf + 16
     block = jax.ShapeDtypeStruct((payload, LANES), bf16)
-    *sends, own, query, feat, cum, packed = pl.pallas_call(
+    *sends, own, query, feat, cum = pl.pallas_call(
         project_kernel,
-        out_shape=[block] * (count + 1)
+        out_shape=[block] * (chips + 2)
         + [
             jax.ShapeDtypeStruct((rows, nf2), bf16),
             jax.ShapeDtypeStruct((rows, 1), f32),
-            jax.ShapeDtypeStruct((pieces, columns, tile), bf16),
         ],
-        in_specs=[SMEM] + [ANY] * 6,
-        out_specs=[VMEM] * (count + 4),
+        in_specs=[HBM] * 6,
+        out_specs=[VMEM] * (chips + 4),
         scratch_shapes=[
             pltpu.VMEM((rows, dim), bf16),
             pltpu.VMEM((nf2, dim), bf16),
@@ -455,15 +521,36 @@
         compiler_params=params,
         cost_estimate=cost(2 * rows * dim * columns, 4 * 1024 * 1024),
         name="project",
-    )(place, tokens, feature_weight.T, window_weight, value_weight, log_decay.T, out_grad)
-    if spread:
-        weights = lax.all_gather(packed[0], CTX + ("tp",)).reshape(count, -1, columns, tile)
-    else:
-        weights = lax.all_gather(packed, "tp")
-
-    recv = []
-    for d in range(1, count):
-        recv.append(lax.ppermute(sends[d - 1], CTX, [(i, i ^ d) for i in range(count)]))
+    )(*in_hbm(tokens, fw_t, window_weight, value_weight, log_decay.T, out_grad))
+
+    shared = heads & (heads - 1) == 0 and 2 * tile * heads == dim
+    if shared:
+        sources, _ = lax.optimization_barrier(((window_weight, value_weight, fw_t), sends[0]))
+        area = 3 * tile + nf2 * tile // LANES
+        own_weights, *packed = pl.pallas_call(
+            pack_kernel,
+            out_shape=[jax.ShapeDtypeStruct((2, area, LANES), bf16)]
+            + [jax.ShapeDtypeStruct((area, LANES), bf16)] * (heads - 1),
+            in_specs=[HBM] * 3,
+            out_specs=[VMEM] * heads,
+            scratch_shapes=[pltpu.SemaphoreType.DMA((heads + 1, 3 + tile // LANES))],
+            compiler_params=params,
+            cost_estimate=cost(1, 2 * columns * tile * (heads + 1) * 2),
+            name="pack",
+        )(*in_hbm(*sources))
+        near = [
+            lax.ppermute(packed[t - 1], "tp", [(z, z ^ t) for z in range(heads)])
+            for t in range(1, heads)
+        ]
+
+    swap = [(0, 1), (1, 0)]
+    recv = {}
+    for d in range(1, chips):
+        recv[2 * d] = lax.ppermute(sends[d], "chip", [(i, i ^ d) for i in range(chips)])
+    recv[1] = lax.ppermute(sends[0], "core", swap)
+    for d in range(1, chips):
+        recv[2 * d + 1] = lax.ppermute(recv[2 * d], "core", swap)
+    recv = [recv[d] for d in range(1, count)]
     if count > 8:
         recv = [jnp.stack(recv)]
 
@@ -474,7 +561,7 @@
             jax.ShapeDtypeStruct((8, rows), f32),
             jax.ShapeDtypeStruct((rows, LANES), f32),
         ),
-        in_specs=[SMEM] + [VMEM] * (len(recv) + 4),
+        in_specs=[VMEM] * (len(recv) + 4),
         out_specs=[VMEM] * 3,
         scratch_shapes=[
             pltpu.VMEM((count, 2 * rows, dh), bf16),
@@ -484,19 +571,54 @@
         compiler_params=params,
         cost_estimate=cost(10**9, 2 * 1024 * 1024, 10**6),
         name="query_side",
-    )(place, *recv, own, query, feat, cum)
-    stats = lax.all_gather(stat, CTX)
+    )(*recv, own, query, feat, cum)
+    stats = [
+        lax.ppermute(stat, CTX, [(i, i ^ d) for i in range(count)]) for d in range(1, count)
+    ]
+    if count > 8:
+        stats = [jnp.stack(stats)]
     grads = pl.pallas_call(
         lambda *refs: gradient_kernel(count, *refs),
         out_shape=jax.ShapeDtypeStruct((3 * rows + nf2 * rows // LANES, LANES), bf16),
-        in_specs=[SMEM] + [VMEM] * (len(recv) + 5),
+        in_specs=[VMEM] * (2 * len(recv) + 5),
         out_specs=VMEM,
+        scratch_shapes=[pltpu.VMEM((count, LANES), f32)],
         compiler_params=params,
         cost_estimate=cost(10**9, 2 * 1024 * 1024, 10**6),
         name="gradients",
-    )(place, *recv, own, query, feat, sheet, stats)
-    all_grads = lax.all_gather(grads, "tp")
-    return (attended, merge(all_grads, weights, not spread, rows, dim))
+    )(*recv, *stats, own, query, feat, sheet, stat)
+    if not shared:
+        weights = jnp.concatenate([window_weight, value_weight, feature_weight], axis=1)
+        weights = lax.all_gather(weights, "tp")
+        return (attended, merge(lax.all_gather(grads, "tp"), weights, rows, dim))
+
+    near, grads = lax.optimization_barrier((near, grads))
+    far = [lax.ppermute(n, "core", swap) for n in near]
+    grads = lax.all_gather(grads, "tp")
+    tiles = pl.pallas_call(
+        share_kernel,
+        out_shape=[jax.ShapeDtypeStruct((rows, tile), bf16)] * 2,
+        in_specs=[VMEM] * (2 * heads),
+        out_specs=[VMEM] * 2,
+        scratch_shapes=[
+            pltpu.VMEM((rows, 3 * LANES * heads), bf16),
+            pltpu.VMEM((rows, nf2 * heads), bf16),
+        ],
+        compiler_params=params,
+        cost_estimate=cost(4 * rows * tile * heads * columns, 4 * heads * tile * columns),
+        name="share",
+    )(grads, own_weights, *near, *far)
+    first, second = [lax.all_gather(t, "tp") for t in tiles]
+    total = pl.pallas_call(
+        lay_kernel,
+        out_shape=jax.ShapeDtypeStruct((rows, dim), bf16),
+        in_specs=[VMEM] * 2,
+        out_specs=VMEM,
+        compiler_params=params,
+        cost_estimate=cost(1, 4 * rows * dim),
+        name="lay",
+    )(first, second)
+    return (attended, total)
 
 
 def solution(mesh):

time: 116 us -> 94.4 us (0.81)
  waiting for transfers between devices: 32.4 us -> 12.7 us
  blocking collectives: 34.3 us -> 51.4 us
  between operations: 14.1 us -> 0.72 us
  starting transfers between devices: 9.28 us -> 16.5 us
  Pallas kernels: 19.3 us -> 12.9 us
  local copies, waits for them, and re-layouts: 5.91 us -> 0 us
    all_gather x1 -> x0, waiting for transfers between devices: 22.5 us -> none  [per_device(): lax.all_gather(packed[0], CTX + ('tp',)).reshape(count, -1, columns, tile)]
    all_gather x2 -> x3, blocking collectives: 34.3 us -> 51.4 us  [the longest x2 31 us: per_device(): first, second = [lax.all_gather(t, 'tp') for t in tiles]]
    ppermute x7 -> x20, starting transfers between devices: 9.25 us -> 16.5 us  [the longest x7 6.3 us: per_device(): lax.ppermute(stat, CTX, [(i, i ^ d) for i in range(count)])]
    unnamed x12 -> x0, local copies, waits for them, and re-layouts: 5.91 us -> none
    pallas_call x2 -> x4, Pallas kernels: 12.2 us -> 6.81 us  [the longest x1 3.4 us: per_device(): pl.pallas_call(project_kernel, out_shape=[block] * (chips + 2) + [jax.Sha...]
    ppermute x7 -> x20, waiting for transfers between devices: 9.92 us -> 12.7 us  [the longest x3 6.76 us: per_device(): lax.ppermute(sends[d], 'chip', [(i, i ^ d) for i in range(chips)])]
  transfers between devices with their start and end apart: 8 -> 20, of which waited for: 4 -> 8; matrix products, arithmetic and copies ran while one was open for 0% -> 0% of each run, Pallas kernels for 6% -> 8%
where the time goes in v5:
time: 94.4 us; the launch traced here: 94.1 us
  blocking collectives  51.4 us (54%)
  starting transfers between devices  16.5 us (17%)
  Pallas kernels  12.9 us (14%)
  waiting for transfers between devices  12.7 us (13%)
    all_gather x2, blocking collectives, per_device(): first, second = [lax.all_gather(t, 'tp') for t in tiles]  31 us
    all_gather x1, blocking collectives, per_device(): grads = lax.all_gather(grads, 'tp')  20.4 us
    ppermute x3, waiting for transfers between devices, per_device(): lax.ppermute(sends[d], 'chip', [(i, i ^ d) for i in range(chips)])  6.76 us
    ppermute x7, starting transfers between devices, per_device(): lax.ppermute(stat, CTX, [(i, i ^ d) for i in range(count)])  6.3 us
    ppermute x7, waiting for transfers between devices, per_device(): lax.ppermute(stat, CTX, [(i, i ^ d) for i in range(count)])  5.9 us
    ppermute x3, starting transfers between devices, per_device(): lax.ppermute(sends[d], 'chip', [(i, i ^ d) for i in range(chips)])  4.54 us
    ppermute x3, starting transfers between devices, per_device(): lax.ppermute(packed[t - 1], 'tp', [(z, z ^ t) for z in range(heads)])  4.45 us
    pallas_call x1, Pallas kernels, per_device(): pl.pallas_call(lambda *refs: gradient_kernel(count, *refs), out_shape=jax...  3.67 us
  transfers between devices with their start and end apart: 20, of which 8 were waited for; matrix products, arithmetic and copies ran while one was open for 0% of the time, Pallas kernels for 8%

profile of v5, /device:TPU:0, one launch (start us, length us, event | category | flops | bytes accessed | tf_op | source)
XLA Modules:
  0.0 94.1 jit_solution(8152052229652489775)
XLA Ops:
  0.6 3.4 %project.1 = (bf16[560,128]{1,0:T(8,128)(2,1)S(1)}, bf16[560,128]{1,0:T(8,128)(2,1)S(1)}, bf16[560,128]{1,0:T(8,128)(2,1)S(1)}, bf16[560,128]{1,0:T(8,128)(2,1)S...) custom-call(bf16[256,2048]{1,0:T(8,128)(2,1)} %tok_hbm.1, ...), custom_call_target="tpu_custom_call" | custom-call | flops 436207616 | bytes 4194304 | tf_op jit(solution)/shard_map/project/pallas_call | solution.py:502
  4.0 3.0 %collective-permute-start.1 = (bf16[560,128]{1,0:T(8,128)(2,1)S(1)}, bf16[560,128]{1,0:T(8,128)(2,1)S(1)}, u32[]{:S(2)}, u32[]{:S(2)}) collective-permute-start(bf16[560,128]{1,0:T(8,128)(2,1)S(1)} %get-tuple-element.27), channel_id=1, source_target_pairs={{0,8},{8,0},{16,24},{24,16},{1,9},{9,1},{17,25},{25,17},{2,10},{10... | collective-permute-start | bytes 430088 | tf_op jit(solution)/shard_map/ppermute | solution.py:549
  7.0 1.5 %collective-permute-start.3 = (bf16[560,128]{1,0:T(8,128)(2,1)S(1)}, bf16[560,128]{1,0:T(8,128)(2,1)S(1)}, u32[]{:S(2)}, u32[]{:S(2)}) collective-permute-start(bf16[560,128]{1,0:T(8,128)(2,1)S(1)} %get-tuple-element.28), channel_id=1, source_target_pairs={{0,16},{8,24},{16,0},{24,8},{1,17},{9,25},{17,1},{25,9},{2,18},{10... | collective-permute-start | bytes 430088 | tf_op jit(solution)/shard_map/ppermute | solution.py:549
  8.6 0.0 collective-permute-start.5
  8.6 0.0 collective-permute-start
  8.6 2.6 %collective-permute-done.1.refs_1_ = bf16[560,128]{1,0:T(8,128)(2,1)S(1)} collective-permute-done((bf16[560,128]{1,0:T(8,128)(2,1)S(1)}, bf16[560,128]{1,0:T(8,128)(2,1)S(1)}, u32[]{:S(2)}, u32[]{:S(2)}) %collective-permute-start.1) | collective-permute-done | bytes 143392 | tf_op jit(solution)/shard_map/ppermute | solution.py:549
  11.2 0.0 collective-permute-start.2
  11.2 4.1 %collective-permute-done.3.refs_3_ = bf16[560,128]{1,0:T(8,128)(2,1)S(1)} collective-permute-done((bf16[560,128]{1,0:T(8,128)(2,1)S(1)}, bf16[560,128]{1,0:T(8,128)(2,1)S(1)}, u32[]{:S(2)}, u32[]{:S(2)}) %collective-permute-start.3) | collective-permute-done | bytes 143392 | tf_op jit(solution)/shard_map/ppermute | solution.py:549
  15.4 0.0 collective-permute-start.4
  15.4 0.0 collective-permute-done.5.refs_5_
  15.4 0.5 collective-permute-start.6
  15.9 1.5 %pack.1 = (bf16[2,832,128]{2,1,0:T(8,128)(2,1)S(1)}, bf16[832,128]{1,0:T(8,128)(2,1)S(1)}, bf16[832,128]{1,0:T(8,128)(2,1)S(1)}, bf16[832,128]{1,0:T(8,128)(2,1)S(1)}) custom-call(bf16[2048,256]{1,0:T(8,128)(2,1)} %ww_hbm.2, bf16[2048,128]{1,0:T(8,128)(2,1)} %vw_hbm.2, bf16[32,2048]{1,0:T(8,128)(2,1)} %bitcast.9), custom_call_target="tpu_custom_call" | custom-call | flops 1 | bytes 2129920 | tf_op jit(solution)/shard_map/pack/pallas_call | solution.py:530
  17.4 1.6 %collective-permute-start.7 = (bf16[832,128]{1,0:T(8,128)(2,1)S(1)}, bf16[832,128]{1,0:T(8,128)(2,1)S(1)}, u32[]{:S(2)}, u32[]{:S(2)}) collective-permute-start(bf16[832,128]{1,0:T(8,128)(2,1)S(1)} %get-tuple-element.38), channel_id=1, source_target_pairs={{0,1},{1,0},{2,3},{3,2},{4,5},{5,4},{6,7},{7,6},{8,9},{9,8},{10,11... | collective-permute-start | bytes 638984 | tf_op jit(solution)/shard_map/ppermute | solution.py:542
  19.0 0.0 collective-permute-done.refs_0_
  19.0 2.6 %collective-permute-start.8 = (bf16[832,128]{1,0:T(8,128)(2,1)S(1)}, bf16[832,128]{1,0:T(8,128)(2,1)S(1)}, u32[]{:S(2)}, u32[]{:S(2)}) collective-permute-start(bf16[832,128]{1,0:T(8,128)(2,1)S(1)} %get-tuple-element.39), channel_id=1, source_target_pairs={{0,2},{1,3},{2,0},{3,1},{4,6},{5,7},{6,4},{7,5},{8,10},{9,11},{10,... | collective-permute-start | bytes 638984 | tf_op jit(solution)/shard_map/ppermute | solution.py:542
  21.6 0.0 collective-permute-done.2.refs_2_
  21.6 0.2 collective-permute-start.9
  21.8 0.0 collective-permute-done.4.refs_4_
  21.8 0.0 collective-permute-done.6.refs_6_
  21.8 2.4 %query_side.1 = (bf16[256,128]{1,0:T(8,128)(2,1)}, f32[8,256]{1,0:T(8,128)S(1)}, f32[256,128]{1,0:T(8,128)S(1)}) custom-call(bf16[560,128]{1,0:T(8,128)(2,1)S(1)} %collective-permute-done.refs_0_, bf16[560,128]{1,0:T(8,128)(2,1)S(1)} %collective-permute-done.1.refs_1_, bf16[560,128]{1,0:T(8,128)(2,1)S(1)} %collective-permute-done.2.refs_2_, ...), custom_call_target="tpu_custom_call" | custom-call | flops 1000000000 | bytes 2097152 | tf_op jit(solution)/shard_map/query_side/pallas_call | solution.py:557
  24.2 0.3 collective-permute-start.16
  24.6 1.4 %collective-permute-start.15 = (f32[8,256]{1,0:T(8,128)S(1)}, f32[8,256]{1,0:T(8,128)S(1)}, u32[]{:S(2)}, u32[]{:S(2)}) collective-permute-start(f32[8,256]{1,0:T(8,128)S(1)} %get-tuple-element.41.refs_18_), channel_id=1, source_target_pairs={{0,24},{4,28},{8,16},{12,20},{16,8},{20,12},{24,0},{28,4},{1,25},{... | collective-permute-start | bytes 24584 | tf_op jit(solution)/shard_map/ppermute | solution.py:576
  26.0 2.2 %collective-permute-done.16.refs_13_ = f32[8,256]{1,0:T(8,128)S(1)} collective-permute-done((f32[8,256]{1,0:T(8,128)S(1)}, f32[8,256]{1,0:T(8,128)S(1)}, u32[]{:S(2)}, u32[]{:S(2)}) %collective-permute-start.16) | collective-permute-done | bytes 8224 | tf_op jit(solution)/shard_map/ppermute | solution.py:576
  28.2 0.7 collective-permute-start.14
  28.9 0.3 collective-permute-done.15.refs_12_
  29.1 1.2 %collective-permute-start.13 = (f32[8,256]{1,0:T(8,128)S(1)}, f32[8,256]{1,0:T(8,128)S(1)}, u32[]{:S(2)}, u32[]{:S(2)}) collective-permute-start(f32[8,256]{1,0:T(8,128)S(1)} %get-tuple-element.41.refs_18_), channel_id=1, source_target_pairs={{0,16},{4,20},{8,24},{12,28},{16,0},{20,4},{24,8},{28,12},{1,17},{... | collective-permute-start | bytes 24584 | tf_op jit(solution)/shard_map/ppermute | solution.py:576
  30.3 0.9 %collective-permute-done.14.refs_11_ = f32[8,256]{1,0:T(8,128)S(1)} collective-permute-done((f32[8,256]{1,0:T(8,128)S(1)}, f32[8,256]{1,0:T(8,128)S(1)}, u32[]{:S(2)}, u32[]{:S(2)}) %collective-permute-start.14) | collective-permute-done | bytes 8224 | tf_op jit(solution)/shard_map/ppermute | solution.py:576
  31.3 0.7 collective-permute-start.12
  31.9 0.8 collective-permute-done.13.refs_10_
  32.8 1.5 %collective-permute-start.11 = (f32[8,256]{1,0:T(8,128)S(1)}, f32[8,256]{1,0:T(8,128)S(1)}, u32[]{:S(2)}, u32[]{:S(2)}) collective-permute-start(f32[8,256]{1,0:T(8,128)S(1)} %get-tuple-element.41.refs_18_), channel_id=1, source_target_pairs={{0,8},{4,12},{8,0},{12,4},{16,24},{20,28},{24,16},{28,20},{1,9},{5... | collective-permute-start | bytes 24584 | tf_op jit(solution)/shard_map/ppermute | solution.py:576
  34.3 0.1 collective-permute-done.12.refs_9_
  34.4 0.5 collective-permute-start.10
  34.8 1.6 %collective-permute-done.11.refs_8_ = f32[8,256]{1,0:T(8,128)S(1)} collective-permute-done((f32[8,256]{1,0:T(8,128)S(1)}, f32[8,256]{1,0:T(8,128)S(1)}, u32[]{:S(2)}, u32[]{:S(2)}) %collective-permute-start.11) | collective-permute-done | bytes 8224 | tf_op jit(solution)/shard_map/ppermute | solution.py:576
  36.4 0.0 collective-permute-done.10.refs_7_
  36.4 3.7 %gradients.1 = bf16[832,128]{1,0:T(8,128)(2,1)S(1)} custom-call(bf16[560,128]{1,0:T(8,128)(2,1)S(1)} %collective-permute-done.refs_0_, bf16[560,128]{1,0:T(8,128)(2,1)S(1)} %collective-permute-done.1.refs_1_, bf16[560,128]{1,0:T(8,128)(2,1)S(1)} %collective-permute-done.2.refs_2_, bf16[560,128]{1,0:T(8,128)(2,1)S(1)} %collective-permute-done.3.refs_3_, ...), custom_call_target="tpu_custom_call" | custom-call | flops 1000000000 | bytes 2097152 | tf_op jit(solution)/shard_map/gradients/pallas_call | solution.py:580
  40.1 0.0 collective-permute-done.7.rest_0_
  40.1 0.0 collective-permute-done.8.rest_1_
  40.1 0.0 collective-permute-done.9.rest_2_
  40.1 0.1 collective-permute-start.17
  40.2 0.5 collective-permute-start.18
  40.7 0.1 collective-permute-start.19
  40.8 20.4 %all-gather = bf16[3328,128]{1,0:T(8,128)(2,1)S(1)} all-gather(bf16[832,128]{1,0:T(8,128)(2,1)S(1)} %gradients.1), channel_id=2, replica_groups=mesh['chip'=4,'core'=2,'tp'=4] {'tp'}, dimensions={0}, use_global_device_ids=true | all-gather | bytes 1064960 | tf_op jit(solution)/shard_map/all_gather | solution.py:597
  61.2 0.0 collective-permute-done.17.rest_3_
  61.2 0.0 collective-permute-done.18.rest_4_
  61.2 0.8 share.1
  62.0 15.4 %all-gather.1 = bf16[1024,256]{1,0:T(8,128)(2,1)S(1)} all-gather(bf16[256,256]{1,0:T(8,128)(2,1)S(1)} %get-tuple-element.48), channel_id=3, replica_groups=mesh['chip'=4,'core'=2,'tp'=4] {'tp'}, dimensions={0}, use_global_device_ids=true | all-gather | bytes 655360 | tf_op jit(solution)/shard_map/all_gather | solution.py:611
  77.5 15.6 %all-gather.2 = bf16[1024,256]{1,0:T(8,128)(2,1)S(1)} all-gather(bf16[256,256]{1,0:T(8,128)(2,1)S(1)} %get-tuple-element.49), channel_id=4, replica_groups=mesh['chip'=4,'core'=2,'tp'=4] {'tp'}, dimensions={0}, use_global_device_ids=true | all-gather | bytes 655360 | tf_op jit(solution)/shard_map/all_gather | solution.py:611
  93.0 1.1 %lay.1 = bf16[256,2048]{1,0:T(8,128)(2,1)} custom-call(bf16[4,256,256]{2,1,0:T(8,128)(2,1)S(1)} %bitcast.6, bf16[4,256,256]{2,1,0:T(8,128)(2,1)S(1)} %bitcast.7), custom_call_target="tpu_custom_call" | custom-call | flops 1 | bytes 2097152 | tf_op jit(solution)/shard_map/lay/pallas_call | solution.py:612
  (1 shorter events, 0.0 us)
Async XLA Ops:
  4.0 7.2 %collective-permute-start.1 = (bf16[560,128]{1,0:T(8,128)(2,1)S(1)}, bf16[560,128]{1,0:T(8,128)(2,1)S(1)}, u32[]{:S(2)}, u32[]{:S(2)}) collective-permute-start(bf16[560,128]{1,0:T(8,128)(2,1)S(1)} %get-tuple-element.27), channel_id=1, source_target_pairs={{0,8},{8,0},{16,24},{24,16},{1,9},{9,1},{17,25},{25,17},{2,10},{10... | collective-permute-start | bytes 430088 | tf_op jit(solution)/shard_map/ppermute | solution.py:549
  7.0 8.3 %collective-permute-start.3 = (bf16[560,128]{1,0:T(8,128)(2,1)S(1)}, bf16[560,128]{1,0:T(8,128)(2,1)S(1)}, u32[]{:S(2)}, u32[]{:S(2)}) collective-permute-start(bf16[560,128]{1,0:T(8,128)(2,1)S(1)} %get-tuple-element.28), channel_id=1, source_target_pairs={{0,16},{8,24},{16,0},{24,8},{1,17},{9,25},{17,1},{25,9},{2,18},{10... | collective-permute-start | bytes 430088 | tf_op jit(solution)/shard_map/ppermute | solution.py:549
  8.6 6.8 %collective-permute-start.5 = (bf16[560,128]{1,0:T(8,128)(2,1)S(1)}, bf16[560,128]{1,0:T(8,128)(2,1)S(1)}, u32[]{:S(2)}, u32[]{:S(2)}) collective-permute-start(bf16[560,128]{1,0:T(8,128)(2,1)S(1)} %get-tuple-element.29), channel_id=1, source_target_pairs={{0,24},{8,16},{16,8},{24,0},{1,25},{9,17},{17,9},{25,1},{2,26},{10... | collective-permute-start | bytes 430088 | tf_op jit(solution)/shard_map/ppermute | solution.py:549
  8.6 10.4 %collective-permute-start = (bf16[560,128]{1,0:T(8,128)(2,1)S(1)}, bf16[560,128]{1,0:T(8,128)(2,1)S(1)}, u32[]{:S(2)}, u32[]{:S(2)}) collective-permute-start(bf16[560,128]{1,0:T(8,128)(2,1)S(1)} %get-tuple-element.26), channel_id=1, source_target_pairs={{0,4},{4,0},{1,5},{5,1},{2,6},{6,2},{3,7},{7,3},{8,12},{12,8},{9,1... | collective-permute-start | bytes 430088 | tf_op jit(solution)/shard_map/ppermute | solution.py:550
  11.2 10.4 %collective-permute-start.2 = (bf16[560,128]{1,0:T(8,128)(2,1)S(1)}, bf16[560,128]{1,0:T(8,128)(2,1)S(1)}, u32[]{:S(2)}, u32[]{:S(2)}) collective-permute-start(bf16[560,128]{1,0:T(8,128)(2,1)S(1)} %collective-permute-done.1.refs_1_), channel_id=1, source_target_pairs={{0,4},{4,0},{1,5},{5,1},{2,6},{6,2},{3,7},{7,3},{8,12},{12,8},{9,1... | collective-permute-start | bytes 430088 | tf_op jit(solution)/shard_map/ppermute | solution.py:552
  15.4 6.5 %collective-permute-start.4 = (bf16[560,128]{1,0:T(8,128)(2,1)S(1)}, bf16[560,128]{1,0:T(8,128)(2,1)S(1)}, u32[]{:S(2)}, u32[]{:S(2)}) collective-permute-start(bf16[560,128]{1,0:T(8,128)(2,1)S(1)} %collective-permute-done.3.refs_3_), channel_id=1, source_target_pairs={{0,4},{4,0},{1,5},{5,1},{2,6},{6,2},{3,7},{7,3},{8,12},{12,8},{9,1... | collective-permute-start | bytes 430088 | tf_op jit(solution)/shard_map/ppermute | solution.py:552
  15.4 6.5 %collective-permute-start.6 = (bf16[560,128]{1,0:T(8,128)(2,1)S(1)}, bf16[560,128]{1,0:T(8,128)(2,1)S(1)}, u32[]{:S(2)}, u32[]{:S(2)}) collective-permute-start(bf16[560,128]{1,0:T(8,128)(2,1)S(1)} %collective-permute-done.5.refs_5_), channel_id=1, source_target_pairs={{0,4},{4,0},{1,5},{5,1},{2,6},{6,2},{3,7},{7,3},{8,12},{12,8},{9,1... | collective-permute-start | bytes 430088 | tf_op jit(solution)/shard_map/ppermute | solution.py:552
  17.4 22.7 %collective-permute-start.7 = (bf16[832,128]{1,0:T(8,128)(2,1)S(1)}, bf16[832,128]{1,0:T(8,128)(2,1)S(1)}, u32[]{:S(2)}, u32[]{:S(2)}) collective-permute-start(bf16[832,128]{1,0:T(8,128)(2,1)S(1)} %get-tuple-element.38), channel_id=1, source_target_pairs={{0,1},{1,0},{2,3},{3,2},{4,5},{5,4},{6,7},{7,6},{8,9},{9,8},{10,11... | collective-permute-start | bytes 638984 | tf_op jit(solution)/shard_map/ppermute | solution.py:542
  19.0 21.1 %collective-permute-start.8 = (bf16[832,128]{1,0:T(8,128)(2,1)S(1)}, bf16[832,128]{1,0:T(8,128)(2,1)S(1)}, u32[]{:S(2)}, u32[]{:S(2)}) collective-permute-start(bf16[832,128]{1,0:T(8,128)(2,1)S(1)} %get-tuple-element.39), channel_id=1, source_target_pairs={{0,2},{1,3},{2,0},{3,1},{4,6},{5,7},{6,4},{7,5},{8,10},{9,11},{10,... | collective-permute-start | bytes 638984 | tf_op jit(solution)/shard_map/ppermute | solution.py:542
  21.6 18.5 %collective-permute-start.9 = (bf16[832,128]{1,0:T(8,128)(2,1)S(1)}, bf16[832,128]{1,0:T(8,128)(2,1)S(1)}, u32[]{:S(2)}, u32[]{:S(2)}) collective-permute-start(bf16[832,128]{1,0:T(8,128)(2,1)S(1)} %get-tuple-element.40), channel_id=1, source_target_pairs={{0,3},{1,2},{2,1},{3,0},{4,7},{5,6},{6,5},{7,4},{8,11},{9,10},{10,... | collective-permute-start | bytes 638984 | tf_op jit(solution)/shard_map/ppermute | solution.py:542
  24.2 4.0 %collective-permute-start.16 = (f32[8,256]{1,0:T(8,128)S(1)}, f32[8,256]{1,0:T(8,128)S(1)}, u32[]{:S(2)}, u32[]{:S(2)}) collective-permute-start(f32[8,256]{1,0:T(8,128)S(1)} %get-tuple-element.41.refs_18_), channel_id=1, source_target_pairs={{0,28},{4,24},{8,20},{12,16},{16,12},{20,8},{24,4},{28,0},{1,29},{... | collective-permute-start | bytes 24584 | tf_op jit(solution)/shard_map/ppermute | solution.py:576
  24.6 4.5 %collective-permute-start.15 = (f32[8,256]{1,0:T(8,128)S(1)}, f32[8,256]{1,0:T(8,128)S(1)}, u32[]{:S(2)}, u32[]{:S(2)}) collective-permute-start(f32[8,256]{1,0:T(8,128)S(1)} %get-tuple-element.41.refs_18_), channel_id=1, source_target_pairs={{0,24},{4,28},{8,16},{12,20},{16,8},{20,12},{24,0},{28,4},{1,25},{... | collective-permute-start | bytes 24584 | tf_op jit(solution)/shard_map/ppermute | solution.py:576
  28.2 3.1 %collective-permute-start.14 = (f32[8,256]{1,0:T(8,128)S(1)}, f32[8,256]{1,0:T(8,128)S(1)}, u32[]{:S(2)}, u32[]{:S(2)}) collective-permute-start(f32[8,256]{1,0:T(8,128)S(1)} %get-tuple-element.41.refs_18_), channel_id=1, source_target_pairs={{0,20},{4,16},{8,28},{12,24},{16,4},{20,0},{24,12},{28,8},{1,21},{... | collective-permute-start | bytes 24584 | tf_op jit(solution)/shard_map/ppermute | solution.py:576
  29.1 3.7 %collective-permute-start.13 = (f32[8,256]{1,0:T(8,128)S(1)}, f32[8,256]{1,0:T(8,128)S(1)}, u32[]{:S(2)}, u32[]{:S(2)}) collective-permute-start(f32[8,256]{1,0:T(8,128)S(1)} %get-tuple-element.41.refs_18_), channel_id=1, source_target_pairs={{0,16},{4,20},{8,24},{12,28},{16,0},{20,4},{24,8},{28,12},{1,17},{... | collective-permute-start | bytes 24584 | tf_op jit(solution)/shard_map/ppermute | solution.py:576
  31.3 3.1 %collective-permute-start.12 = (f32[8,256]{1,0:T(8,128)S(1)}, f32[8,256]{1,0:T(8,128)S(1)}, u32[]{:S(2)}, u32[]{:S(2)}) collective-permute-start(f32[8,256]{1,0:T(8,128)S(1)} %get-tuple-element.41.refs_18_), channel_id=1, source_target_pairs={{0,12},{4,8},{8,4},{12,0},{16,28},{20,24},{24,20},{28,16},{1,13},{... | collective-permute-start | bytes 24584 | tf_op jit(solution)/shard_map/ppermute | solution.py:576
  32.8 3.7 %collective-permute-start.11 = (f32[8,256]{1,0:T(8,128)S(1)}, f32[8,256]{1,0:T(8,128)S(1)}, u32[]{:S(2)}, u32[]{:S(2)}) collective-permute-start(f32[8,256]{1,0:T(8,128)S(1)} %get-tuple-element.41.refs_18_), channel_id=1, source_target_pairs={{0,8},{4,12},{8,0},{12,4},{16,24},{20,28},{24,16},{28,20},{1,9},{5... | collective-permute-start | bytes 24584 | tf_op jit(solution)/shard_map/ppermute | solution.py:576
  34.4 2.1 %collective-permute-start.10 = (f32[8,256]{1,0:T(8,128)S(1)}, f32[8,256]{1,0:T(8,128)S(1)}, u32[]{:S(2)}, u32[]{:S(2)}) collective-permute-start(f32[8,256]{1,0:T(8,128)S(1)} %get-tuple-element.41.refs_18_), channel_id=1, source_target_pairs={{0,4},{4,0},{8,12},{12,8},{16,20},{20,16},{24,28},{28,24},{1,5},{5... | collective-permute-start | bytes 24584 | tf_op jit(solution)/shard_map/ppermute | solution.py:576
  40.1 21.1 %collective-permute-start.17 = (bf16[832,128]{1,0:T(8,128)(2,1)S(1)}, bf16[832,128]{1,0:T(8,128)(2,1)S(1)}, u32[]{:S(2)}, u32[]{:S(2)}) collective-permute-start(bf16[832,128]{1,0:T(8,128)(2,1)S(1)} %collective-permute-done.7.rest_0_), channel_id=1, source_target_pairs={{0,4},{4,0},{1,5},{5,1},{2,6},{6,2},{3,7},{7,3},{8,12},{12,8},{9,1... | collective-permute-start | bytes 638984 | tf_op jit(solution)/shard_map/ppermute | solution.py:596
  40.2 21.0 %collective-permute-start.18 = (bf16[832,128]{1,0:T(8,128)(2,1)S(1)}, bf16[832,128]{1,0:T(8,128)(2,1)S(1)}, u32[]{:S(2)}, u32[]{:S(2)}) collective-permute-start(bf16[832,128]{1,0:T(8,128)(2,1)S(1)} %collective-permute-done.8.rest_1_), channel_id=1, source_target_pairs={{0,4},{4,0},{1,5},{5,1},{2,6},{6,2},{3,7},{7,3},{8,12},{12,8},{9,1... | collective-permute-start | bytes 638984 | tf_op jit(solution)/shard_map/ppermute | solution.py:596
  40.7 20.5 %collective-permute-start.19 = (bf16[832,128]{1,0:T(8,128)(2,1)S(1)}, bf16[832,128]{1,0:T(8,128)(2,1)S(1)}, u32[]{:S(2)}, u32[]{:S(2)}) collective-permute-start(bf16[832,128]{1,0:T(8,128)(2,1)S(1)} %collective-permute-done.9.rest_2_), channel_id=1, source_target_pairs={{0,4},{4,0},{1,5},{5,1},{2,6},{6,2},{3,7},{7,3},{8,12},{12,8},{9,1... | collective-permute-start | bytes 638984 | tf_op jit(solution)/shard_map/ppermute | solution.py:596

commit v6 on v5

--- a/solution.py
+++ b/solution.py
@@ -141,27 +141,42 @@
 def pack_kernel(ww_hbm, vw_hbm, fw_hbm, own_ref, *rest):
     sends, sems = rest[:-1], rest[-1]
     head, core = lax.axis_index("tp"), lax.axis_index("core")
-    nf2 = fw_hbm.shape[0]
-    tile = (own_ref.shape[1] * LANES) // (3 * LANES + nf2)
-    parts = [(own_ref.at[k], 2 * head + k) for k in range(2)]
-    parts += [(ref, 2 * jnp.bitwise_xor(head, t + 1) + core) for t, ref in enumerate(sends)]
+    nf2, dim = fw_hbm.shape
+    common, share = columns_of(dim, len(sends) + 1)
+    parts = [(own_ref.at[k], head, k) for k in range(2)]
+    parts += [(ref, jnp.bitwise_xor(head, t + 1), core) for t, ref in enumerate(sends)]
     copies = []
-    for n, (ref, piece) in enumerate(parts):
-        rows = pl.ds(pl.multiple_of(piece * tile, tile), tile)
-        moves = [
-            (ww_hbm.at[rows, pl.ds(0, LANES)], ref.at[pl.ds(0, tile), :]),
-            (ww_hbm.at[rows, pl.ds(LANES, LANES)], ref.at[pl.ds(tile, tile), :]),
-            (vw_hbm.at[rows, :], ref.at[pl.ds(2 * tile, tile), :]),
-        ]
-        for m in range(tile // LANES):
-            lanes = pl.ds(pl.multiple_of(piece * tile + m * LANES, LANES), LANES)
-            moves.append((fw_hbm.at[:, lanes], ref.at[pl.ds(3 * tile + m * nf2, nf2), :]))
+    for n, (ref, to, k) in enumerate(parts):
+        first = k * common
+        rest_at = 2 * common + to * 2 * share
+        moves = []
+        for at, start, size, chunks in (
+            (0, first, common, first),
+            (area(common, nf2), rest_at + k * share, share, rest_at + k * LANES),
+        ):
+            rows = pl.ds(pl.multiple_of(start, 64), size)
+            moves += [
+                (ww_hbm.at[rows, pl.ds(0, LANES)], ref.at[pl.ds(at, size), :]),
+                (ww_hbm.at[rows, pl.ds(LANES, LANES)], ref.at[pl.ds(at + size, size), :]),
+                (vw_hbm.at[rows, :], ref.at[pl.ds(at + 2 * size, size), :]),
+            ]
+            for m in range(2):
+                lanes = pl.ds(pl.multiple_of(chunks + m * LANES, LANES), LANES)
+                moves.append((fw_hbm.at[:, lanes], ref.at[pl.ds(at + 3 * size + m * nf2, nf2), :]))
         for m, (src, dst) in enumerate(moves):
             copies.append(pltpu.make_async_copy(src, dst, sems.at[n, m]))
     for copy in copies:
         copy.start()
     for copy in copies:
         copy.wait()
+
+
+def columns_of(dim, heads):
+    return dim // 8, dim * 3 // 4 // heads // 2
+
+
+def area(size, nf2):
+    return 3 * size + 2 * nf2
 
 
 def between(totals, low, high):
@@ -283,15 +298,11 @@
 
 
 def gradient_kernel(count, *rest):
-    parts = len(rest) - 7 >> 1
-    recvs, stats = rest[:parts], rest[parts : 2 * parts]
-    own_ref, query_ref, feat_ref, sheet_ref, mine_ref, grad_ref, total_ref = rest[2 * parts :]
+    recvs = rest[:-6]
+    own_ref, query_ref, feat_ref, sheet_ref, stat_ref, grad_ref = rest[-6:]
 
     def recv(d):
         return recvs[d - 1] if len(recvs) > 1 else recvs[0].at[d - 1]
-
-    def stat(d):
-        return stats[d - 1] if len(stats) > 1 else stats[0].at[d - 1]
 
     me = block_index()
     rows = feat_ref.shape[0]
@@ -307,15 +318,9 @@
     q, k = feat_ref[:, :nf], feat_ref[:, nf:]
     lse_c, dw_c = sheet_ref[:, 0:1], sheet_ref[:, 1:2]
     rden_c, dl_c, cum_c = sheet_ref[:, 2:3], sheet_ref[:, 3:4], sheet_ref[:, 4:5]
+    mine_ref = stat_ref.at[me]
     own_cum = mine_ref[4:5, :]
-    total_ref[pl.ds(me, 1), :] = own_cum[:, rows - LANES :]
-
-    def place(d, carry):
-        total_ref[pl.ds(partner(me, d, count), 1), :] = stat(d)[4:5, rows - LANES :]
-        return carry
-
-    over_partners(count, place, 0)
-    totals = total_ref[:, LANES - 1 :]
+    totals = jnp.concatenate([stat_ref[j, 4:5, rows - 1 : rows] for j in range(count)], axis=0)
     growth_c = jnp.exp(cum_c) * rden_c
     tail_c = jnp.exp(own_cum[:, rows - 1 : rows] - cum_c)
 
@@ -356,7 +361,7 @@
         other_w = view[0:rows, :]
         other_v = view[rows : 2 * rows, :]
         other_f = wide(view, feat_at, nf)
-        st = stat(d)
+        st = stat_ref[j]
         zero = jnp.zeros((1, rows), f32)
         cum = st[4:5, :]
         gap = between(totals, jnp.minimum(me, j), jnp.maximum(me, j))
@@ -404,36 +409,55 @@
 def share_kernel(grad_ref, own_ref, *rest):
     heads = grad_ref.shape[0]
     near, far = rest[: heads - 1], rest[heads - 1 : 2 * heads - 2]
-    first_ref, second_ref, cat_ref, feat_ref = rest[-4:]
-    rows = cat_ref.shape[0]
-    tile = first_ref.shape[1]
+    common_ref, share_ref, cat_ref, feat_ref = rest[-4:]
     nf2 = feat_ref.shape[1] // heads
     head, core = lax.axis_index("tp"), lax.axis_index("core")
     gather_rows(
         grad_ref, [head] + [jnp.bitwise_xor(head, t) for t in range(1, heads)], cat_ref, feat_ref
     )
-
-    def product(out_ref, views):
+    common, share = common_ref.shape[1] // 2, share_ref.shape[1] // 2
+
+    def product(sides, at, size, chunks):
         main = jnp.concatenate(
-            [v[m * tile : (m + 1) * tile, :] for v in views for m in range(3)], axis=1
+            [
+                jnp.concatenate(
+                    [v[at + m * size : at + (m + 1) * size, :] for v in views for m in range(3)],
+                    axis=1,
+                )
+                for views in sides
+            ],
+            axis=0,
         )
-        feats = jnp.concatenate([wide(v, 3 * tile, nf2) for v in views], axis=0)
-        out_ref[...] = (nt(cat_ref[...], main) + nn(feat_ref[...], feats)).astype(bf16)
-
-    for flag, ours, theirs in ((0, first_ref, second_ref), (1, second_ref, first_ref)):
+        feats = jnp.concatenate(
+            [
+                jnp.concatenate(
+                    [
+                        sides[k][h][at + 3 * size + m * nf2 : at + 3 * size + (m + 1) * nf2, :]
+                        for k, m in chunks
+                    ],
+                    axis=1,
+                )
+                for h in range(heads)
+            ],
+            axis=0,
+        )
+        return (nt(cat_ref[...], main) + nn(feat_ref[...], feats)).astype(bf16)
+
+    for flag, zero, one in ((0, near, far), (1, far, near)):
 
         @pl.when(core == flag)
         def _():
-            product(ours, [own_ref.at[flag], *near])
-            product(theirs, [own_ref.at[1 - flag], *far])
-
-
-def lay_kernel(first_ref, second_ref, out_ref):
-    shares, _, tile = first_ref.shape
+            sides = [[own_ref.at[0], *zero], [own_ref.at[1], *one]]
+            share_ref[...] = product(sides, area(common, nf2), share, ((0, 0), (0, 1), (1, 1)))
+            common_ref[...] = product(sides, 0, common, ((0, 0), (0, 1), (1, 0), (1, 1)))
+
+
+def lay_kernel(common_ref, share_ref, out_ref):
+    first = common_ref.shape[1]
+    shares, _, width = share_ref.shape
+    out_ref[:, 0:first] = common_ref[...]
     for z in range(shares):
-        at = 2 * z * tile
-        out_ref[:, at : at + tile] = first_ref[z]
-        out_ref[:, at + tile : at + 2 * tile] = second_ref[z]
+        out_ref[:, first + z * width : first + (z + 1) * width] = share_ref[z]
 
 
 def merge_kernel(grad_ref, weight_ref, out_ref, cat_ref, feat_ref):
@@ -523,19 +547,20 @@
         name="project",
     )(*in_hbm(tokens, fw_t, window_weight, value_weight, log_decay.T, out_grad))
 
-    shared = heads & (heads - 1) == 0 and 2 * tile * heads == dim
+    common, share = columns_of(dim, heads)
+    shared = heads & (heads - 1) == 0 and common == 2 * LANES and share * 2 == 3 * LANES
     if shared:
         sources, _ = lax.optimization_barrier(((window_weight, value_weight, fw_t), sends[0]))
-        area = 3 * tile + nf2 * tile // LANES
+        height = area(common, nf2) + area(share, nf2)
         own_weights, *packed = pl.pallas_call(
             pack_kernel,
-            out_shape=[jax.ShapeDtypeStruct((2, area, LANES), bf16)]
-            + [jax.ShapeDtypeStruct((area, LANES), bf16)] * (heads - 1),
+            out_shape=[jax.ShapeDtypeStruct((2, height, LANES), bf16)]
+            + [jax.ShapeDtypeStruct((height, LANES), bf16)] * (heads - 1),
             in_specs=[HBM] * 3,
             out_specs=[VMEM] * heads,
-            scratch_shapes=[pltpu.SemaphoreType.DMA((heads + 1, 3 + tile // LANES))],
+            scratch_shapes=[pltpu.SemaphoreType.DMA((heads + 1, 10))],
             compiler_params=params,
-            cost_estimate=cost(1, 2 * columns * tile * (heads + 1) * 2),
+            cost_estimate=cost(1, 2 * height * LANES * (heads + 1) * 2),
             name="pack",
         )(*in_hbm(*sources))
         near = [
@@ -548,6 +573,8 @@
     for d in range(1, chips):
         recv[2 * d] = lax.ppermute(sends[d], "chip", [(i, i ^ d) for i in range(chips)])
     recv[1] = lax.ppermute(sends[0], "core", swap)
+    if shared:
+        recv, packed = lax.optimization_barrier((recv, packed))
     for d in range(1, chips):
         recv[2 * d + 1] = lax.ppermute(recv[2 * d], "core", swap)
     recv = [recv[d] for d in range(1, count)]
@@ -572,21 +599,16 @@
         cost_estimate=cost(10**9, 2 * 1024 * 1024, 10**6),
         name="query_side",
     )(*recv, own, query, feat, cum)
-    stats = [
-        lax.ppermute(stat, CTX, [(i, i ^ d) for i in range(count)]) for d in range(1, count)
-    ]
-    if count > 8:
-        stats = [jnp.stack(stats)]
+    stats = lax.all_gather(stat, CTX)
     grads = pl.pallas_call(
         lambda *refs: gradient_kernel(count, *refs),
         out_shape=jax.ShapeDtypeStruct((3 * rows + nf2 * rows // LANES, LANES), bf16),
-        in_specs=[VMEM] * (2 * len(recv) + 5),
+        in_specs=[VMEM] * (len(recv) + 5),
         out_specs=VMEM,
-        scratch_shapes=[pltpu.VMEM((count, LANES), f32)],
         compiler_params=params,
         cost_estimate=cost(10**9, 2 * 1024 * 1024, 10**6),
         name="gradients",
-    )(*recv, *stats, own, query, feat, sheet, stat)
+    )(*recv, own, query, feat, sheet, stats)
     if not shared:
         weights = jnp.concatenate([window_weight, value_weight, feature_weight], axis=1)
         weights = lax.all_gather(weights, "tp")
@@ -595,9 +617,12 @@
     near, grads = lax.optimization_barrier((near, grads))
     far = [lax.ppermute(n, "core", swap) for n in near]
     grads = lax.all_gather(grads, "tp")
-    tiles = pl.pallas_call(
+    first, rest = pl.pallas_call(
         share_kernel,
-        out_shape=[jax.ShapeDtypeStruct((rows, tile), bf16)] * 2,
+        out_shape=[
+            jax.ShapeDtypeStruct((rows, 2 * common), bf16),
+            jax.ShapeDtypeStruct((rows, 2 * share), bf16),
+        ],
         in_specs=[VMEM] * (2 * heads),
         out_specs=[VMEM] * 2,
         scratch_shapes=[
@@ -605,10 +630,11 @@
             pltpu.VMEM((rows, nf2 * heads), bf16),
         ],
         compiler_params=params,
-        cost_estimate=cost(4 * rows * tile * heads * columns, 4 * heads * tile * columns),
+        cost_estimate=cost(
+            4 * rows * (common + share) * heads * columns, 4 * heads * height * LANES
+        ),
         name="share",
     )(grads, own_weights, *near, *far)
-    first, second = [lax.all_gather(t, "tp") for t in tiles]
     total = pl.pallas_call(
         lay_kernel,
         out_shape=jax.ShapeDtypeStruct((rows, dim), bf16),
@@ -617,7 +643,7 @@
         compiler_params=params,
         cost_estimate=cost(1, 4 * rows * dim),
         name="lay",
-    )(first, second)
+    )(first, lax.all_gather(rest, "tp"))
     return (attended, total)
 
 

time: 94.4 us -> 92.3 us (0.978)
  starting transfers between devices: 16.5 us -> 10 us
  waiting for transfers between devices: 12.7 us -> 14.8 us
  blocking collectives: 51.4 us -> 52.7 us
  Pallas kernels: 12.9 us -> 13.9 us
    ppermute x3, waiting for transfers between devices: 0.01 us -> 9.01 us  [per_device(): lax.ppermute(packed[t - 1], 'tp', [(z, z ^ t) for z in range(heads)])]
    ppermute x7 -> x0, starting transfers between devices: 6.3 us -> none  [per_device(): lax.ppermute(stat, CTX, [(i, i ^ d) for i in range(count)])]
    ppermute x7 -> x0, waiting for transfers between devices: 5.9 us -> none  [per_device(): lax.ppermute(stat, CTX, [(i, i ^ d) for i in range(count)])]
    all_gather x1, blocking collectives: 20.4 us -> 25.4 us  [per_device(): grads = lax.all_gather(grads, 'tp')]
    all_gather x2, blocking collectives: 31 us -> 27.2 us  [the longest x1 18 us: per_device(): lax.all_gather(rest, 'tp')]
    ppermute x3, waiting for transfers between devices: 6.76 us -> 4.7 us  [per_device(): lax.ppermute(sends[d], 'chip', [(i, i ^ d) for i in range(chips)])]
    ppermute x3, waiting for transfers between devices: 0.01 us -> 1.06 us  [per_device(): recv[2 * d + 1] = lax.ppermute(recv[2 * d], 'core', swap)]
    pallas_call x2, Pallas kernels: 2.31 us -> 3.36 us  [the longest x1 2.06 us: per_device(): pl.pallas_call(pack_kernel, out_shape=[jax.ShapeDtypeStruct((2, height, L...]
  transfers between devices with their start and end apart: 20 -> 13, of which waited for: 8 -> 5; matrix products, arithmetic and copies ran while one was open for 0% -> 0% of each run, Pallas kernels for 8% -> 9%
where the time goes in v6:
time: 92.3 us; the launch traced here: 92.1 us
  blocking collectives  52.7 us (57%)
  waiting for transfers between devices  14.8 us (16%)
  Pallas kernels  13.9 us (15%)
  starting transfers between devices  10 us (11%)
    all_gather x1, blocking collectives, per_device(): grads = lax.all_gather(grads, 'tp')  25.4 us
    all_gather x1, blocking collectives, per_device(): lax.all_gather(rest, 'tp')  18 us
    all_gather x1, blocking collectives, per_device(): stats = lax.all_gather(stat, CTX)  9.24 us
    ppermute x3, waiting for transfers between devices, per_device(): lax.ppermute(packed[t - 1], 'tp', [(z, z ^ t) for z in range(heads)])  9.01 us
    ppermute x3, waiting for transfers between devices, per_device(): lax.ppermute(sends[d], 'chip', [(i, i ^ d) for i in range(chips)])  4.7 us
    ppermute x3, starting transfers between devices, per_device(): lax.ppermute(sends[d], 'chip', [(i, i ^ d) for i in range(chips)])  4.54 us
    ppermute x3, starting transfers between devices, per_device(): lax.ppermute(packed[t - 1], 'tp', [(z, z ^ t) for z in range(heads)])  4.45 us
    pallas_call x1, Pallas kernels, per_device(): pl.pallas_call(lambda *refs: gradient_kernel(count, *refs), out_shape=jax...  3.68 us
  transfers between devices with their start and end apart: 13, of which 5 were waited for; matrix products, arithmetic and copies ran while one was open for 0% of the time, Pallas kernels for 9%

profile of v6, /device:TPU:0, one launch (start us, length us, event | category | flops | bytes accessed | tf_op | source)
XLA Modules:
  0.0 92.1 jit_solution(11185617011035225594)
XLA Ops:
  0.6 3.4 %project.1 = (bf16[560,128]{1,0:T(8,128)(2,1)S(1)}, bf16[560,128]{1,0:T(8,128)(2,1)S(1)}, bf16[560,128]{1,0:T(8,128)(2,1)S(1)}, bf16[560,128]{1,0:T(8,128)(2,1)S...) custom-call(bf16[256,2048]{1,0:T(8,128)(2,1)} %tok_hbm.1, ...), custom_call_target="tpu_custom_call" | custom-call | flops 436207616 | bytes 4194304 | tf_op jit(solution)/shard_map/project/pallas_call | solution.py:526
  4.0 3.0 %collective-permute-start.1 = (bf16[560,128]{1,0:T(8,128)(2,1)S(1)}, bf16[560,128]{1,0:T(8,128)(2,1)S(1)}, u32[]{:S(2)}, u32[]{:S(2)}) collective-permute-start(bf16[560,128]{1,0:T(8,128)(2,1)S(1)} %get-tuple-element.31), channel_id=1, source_target_pairs={{0,8},{8,0},{16,24},{24,16},{1,9},{9,1},{17,25},{25,17},{2,10},{10... | collective-permute-start | bytes 430088 | tf_op jit(solution)/shard_map/ppermute | solution.py:574
  7.0 1.5 %collective-permute-start.2 = (bf16[560,128]{1,0:T(8,128)(2,1)S(1)}, bf16[560,128]{1,0:T(8,128)(2,1)S(1)}, u32[]{:S(2)}, u32[]{:S(2)}) collective-permute-start(bf16[560,128]{1,0:T(8,128)(2,1)S(1)} %get-tuple-element.32), channel_id=1, source_target_pairs={{0,16},{8,24},{16,0},{24,8},{1,17},{9,25},{17,1},{25,9},{2,18},{10... | collective-permute-start | bytes 430088 | tf_op jit(solution)/shard_map/ppermute | solution.py:574
  8.6 0.0 collective-permute-start.3
  8.6 0.0 collective-permute-start
  8.6 2.1 %pack.1 = (bf16[2,1472,128]{2,1,0:T(8,128)(2,1)S(1)}, bf16[1472,128]{1,0:T(8,128)(2,1)S(1)}, bf16[1472,128]{1,0:T(8,128)(2,1)S(1)}, bf16[1472,128]{1,0:T(8,128)(2,1)S(1)}) custom-call(bf16[2048,256]{1,0:T(8,128)(2,1)} %ww_hbm.2, bf16[2048,128]{1,0:T(8,128)(2,1)} %vw_hbm.2, bf16[32,2048]{1,0:T(8,128)(2,1)} %bitcast.9), custom_call_target="tpu_custom_call" | custom-call | flops 1 | bytes 3768320 | tf_op jit(solution)/shard_map/pack/pallas_call | solution.py:555
  10.7 0.6 collective-permute-done.1.refs_1_
  11.2 4.1 %collective-permute-done.2.refs_3_ = bf16[560,128]{1,0:T(8,128)(2,1)S(1)} collective-permute-done((bf16[560,128]{1,0:T(8,128)(2,1)S(1)}, bf16[560,128]{1,0:T(8,128)(2,1)S(1)}, u32[]{:S(2)}, u32[]{:S(2)}) %collective-permute-start.2) | collective-permute-done | bytes 143392 | tf_op jit(solution)/shard_map/ppermute | solution.py:574
  15.4 0.0 collective-permute-done.3.refs_5_
  15.4 0.0 collective-permute-done.refs_0_
  15.4 0.0 collective-permute-start.4
  15.4 1.6 %collective-permute-start.7 = (bf16[1472,128]{1,0:T(8,128)(2,1)S(1)}, bf16[1472,128]{1,0:T(8,128)(2,1)S(1)}, u32[]{:S(2)}, u32[]{:S(2)}) collective-permute-start(bf16[1472,128]{1,0:T(8,128)(2,1)S(1)} %get-tuple-element.37), channel_id=1, source_target_pairs={{0,1},{1,0},{2,3},{3,2},{4,5},{5,4},{6,7},{7,6},{8,9},{9,8},{10,11... | collective-permute-start | bytes 1130504 | tf_op jit(solution)/shard_map/ppermute | solution.py:567
  17.0 2.6 %collective-permute-start.8 = (bf16[1472,128]{1,0:T(8,128)(2,1)S(1)}, bf16[1472,128]{1,0:T(8,128)(2,1)S(1)}, u32[]{:S(2)}, u32[]{:S(2)}) collective-permute-start(bf16[1472,128]{1,0:T(8,128)(2,1)S(1)} %get-tuple-element.38), channel_id=1, source_target_pairs={{0,2},{1,3},{2,0},{3,1},{4,6},{5,7},{6,4},{7,5},{8,10},{9,11},{10,... | collective-permute-start | bytes 1130504 | tf_op jit(solution)/shard_map/ppermute | solution.py:567
  19.6 0.2 collective-permute-start.9
  19.8 0.0 collective-permute-start.5
  19.8 0.0 collective-permute-done.4.refs_2_
  19.8 0.5 collective-permute-start.6
  20.3 0.9 collective-permute-done.5.refs_4_
  21.2 0.2 collective-permute-done.6.refs_6_
  21.4 2.4 %query_side.1 = (bf16[256,128]{1,0:T(8,128)(2,1)}, f32[8,256]{1,0:T(8,128)S(1)}, f32[256,128]{1,0:T(8,128)S(1)}) custom-call(bf16[560,128]{1,0:T(8,128)(2,1)S(1)} %collective-permute-done.refs_0_, bf16[560,128]{1,0:T(8,128)(2,1)S(1)} %collective-permute-done.1.refs_1_, bf16[560,128]{1,0:T(8,128)(2,1)S(1)} %collective-permute-done.4.refs_2_, ...), custom_call_target="tpu_custom_call" | custom-call | flops 1000000000 | bytes 2097152 | tf_op jit(solution)/shard_map/query_side/pallas_call | solution.py:584
  23.8 9.2 %all-gather = f32[64,256]{1,0:T(8,128)S(1)} all-gather(f32[8,256]{1,0:T(8,128)S(1)} %get-tuple-element.50), channel_id=2, replica_groups=mesh['chip'=4,'core'=2,'tp'=4] {'chip','core'}, dimensions={0}, use_global_device_ids=true | all-gather | bytes 73728 | tf_op jit(solution)/shard_map/all_gather | solution.py:602
  33.0 3.7 %gradients.1 = bf16[832,128]{1,0:T(8,128)(2,1)S(1)} custom-call(bf16[560,128]{1,0:T(8,128)(2,1)S(1)} %collective-permute-done.refs_0_, bf16[560,128]{1,0:T(8,128)(2,1)S(1)} %collective-permute-done.1.refs_1_, bf16[560,128]{1,0:T(8,128)(2,1)S(1)} %collective-permute-done.4.refs_2_, bf16[560,128]{1,0:T(8,128)(2,1)S(1)} %collective-permute-done.2.refs_3_, ...), custom_call_target="tpu_custom_call" | custom-call | flops 1000000000 | bytes 2097152 | tf_op jit(solution)/shard_map/gradients/pallas_call | solution.py:603
  36.7 0.0 collective-permute-done.7.rest_0_
  36.7 9.0 %collective-permute-done.8.rest_1_ = bf16[1472,128]{1,0:T(8,128)(2,1)S(1)} collective-permute-done((bf16[1472,128]{1,0:T(8,128)(2,1)S(1)}, bf16[1472,128]{1,0:T(8,128)(2,1)S(1)}, u32[]{:S(2)}, u32[]{:S(2)}) %collective-permute-start.8) | collective-permute-done | bytes 376864 | tf_op jit(solution)/shard_map/ppermute | solution.py:567
  45.7 0.0 collective-permute-done.9.rest_2_
  45.7 0.0 collective-permute-start.10
  45.7 0.5 collective-permute-start.11
  46.2 0.0 collective-permute-start.12
  46.2 25.4 %all-gather.1 = bf16[3328,128]{1,0:T(8,128)(2,1)S(1)} all-gather(bf16[832,128]{1,0:T(8,128)(2,1)S(1)} %gradients.1), channel_id=3, replica_groups=mesh['chip'=4,'core'=2,'tp'=4] {'tp'}, dimensions={0}, use_global_device_ids=true | all-gather | bytes 1064960 | tf_op jit(solution)/shard_map/all_gather | solution.py:619
  71.7 0.0 collective-permute-done.10.rest_3_
  71.7 0.0 collective-permute-done.11.rest_4_
  71.7 0.0 collective-permute-done.12.rest_5_
  71.7 1.3 %share.1 = (bf16[256,512]{1,0:T(8,128)(2,1)S(1)}, bf16[256,384]{1,0:T(8,128)(2,1)S(1)}) custom-call(bf16[4,832,128]{2,1,0:T(8,128)(2,1)S(1)} %bitcast.5, bf16[2,1472,128]{2,1,0:T(8,128)(2,1)S(1)} %get-tuple-element.52.own_ref, bf16[1472,128]{1,0:T(8,128)(2,1)S(1)} %collective-permute-done.7.rest_0_, bf16[1472,128]{1,0:T(8,128)(2,1)S(1)} %collective-permute-done.8.rest_1_, ...), custom_call_target="tpu_custom_call" | custom-call | flops 763363328 | bytes 3014656 | tf_op jit(solution)/shard_map/share/pallas_call | solution.py:620
  73.0 18.0 %all-gather.2 = bf16[1024,384]{1,0:T(8,128)(2,1)S(1)} all-gather(bf16[256,384]{1,0:T(8,128)(2,1)S(1)} %get-tuple-element.57), channel_id=4, replica_groups=mesh['chip'=4,'core'=2,'tp'=4] {'tp'}, dimensions={0}, use_global_device_ids=true | all-gather | bytes 983040 | tf_op jit(solution)/shard_map/all_gather | solution.py:646
  91.0 1.1 %lay.1 = bf16[256,2048]{1,0:T(8,128)(2,1)} custom-call(bf16[256,512]{1,0:T(8,128)(2,1)S(1)} %get-tuple-element.56.common_ref, bf16[4,256,384]{2,1,0:T(8,128)(2,1)S(1)} %bitcast.6), custom_call_target="tpu_custom_call" | custom-call | flops 1 | bytes 2097152 | tf_op jit(solution)/shard_map/lay/pallas_call | solution.py:638
Async XLA Ops:
  4.0 7.2 %collective-permute-start.1 = (bf16[560,128]{1,0:T(8,128)(2,1)S(1)}, bf16[560,128]{1,0:T(8,128)(2,1)S(1)}, u32[]{:S(2)}, u32[]{:S(2)}) collective-permute-start(bf16[560,128]{1,0:T(8,128)(2,1)S(1)} %get-tuple-element.31), channel_id=1, source_target_pairs={{0,8},{8,0},{16,24},{24,16},{1,9},{9,1},{17,25},{25,17},{2,10},{10... | collective-permute-start | bytes 430088 | tf_op jit(solution)/shard_map/ppermute | solution.py:574
  7.0 8.3 %collective-permute-start.2 = (bf16[560,128]{1,0:T(8,128)(2,1)S(1)}, bf16[560,128]{1,0:T(8,128)(2,1)S(1)}, u32[]{:S(2)}, u32[]{:S(2)}) collective-permute-start(bf16[560,128]{1,0:T(8,128)(2,1)S(1)} %get-tuple-element.32), channel_id=1, source_target_pairs={{0,16},{8,24},{16,0},{24,8},{1,17},{9,25},{17,1},{25,9},{2,18},{10... | collective-permute-start | bytes 430088 | tf_op jit(solution)/shard_map/ppermute | solution.py:574
  8.6 6.8 %collective-permute-start.3 = (bf16[560,128]{1,0:T(8,128)(2,1)S(1)}, bf16[560,128]{1,0:T(8,128)(2,1)S(1)}, u32[]{:S(2)}, u32[]{:S(2)}) collective-permute-start(bf16[560,128]{1,0:T(8,128)(2,1)S(1)} %get-tuple-element.33), channel_id=1, source_target_pairs={{0,24},{8,16},{16,8},{24,0},{1,25},{9,17},{17,9},{25,1},{2,26},{10... | collective-permute-start | bytes 430088 | tf_op jit(solution)/shard_map/ppermute | solution.py:574
  8.6 6.8 %collective-permute-start = (bf16[560,128]{1,0:T(8,128)(2,1)S(1)}, bf16[560,128]{1,0:T(8,128)(2,1)S(1)}, u32[]{:S(2)}, u32[]{:S(2)}) collective-permute-start(bf16[560,128]{1,0:T(8,128)(2,1)S(1)} %get-tuple-element.30), channel_id=1, source_target_pairs={{0,4},{4,0},{1,5},{5,1},{2,6},{6,2},{3,7},{7,3},{8,12},{12,8},{9,1... | collective-permute-start | bytes 430088 | tf_op jit(solution)/shard_map/ppermute | solution.py:575
  15.4 4.5 %collective-permute-start.4 = (bf16[560,128]{1,0:T(8,128)(2,1)S(1)}, bf16[560,128]{1,0:T(8,128)(2,1)S(1)}, u32[]{:S(2)}, u32[]{:S(2)}) collective-permute-start(bf16[560,128]{1,0:T(8,128)(2,1)S(1)} %collective-permute-done.1.refs_1_), channel_id=1, source_target_pairs={{0,4},{4,0},{1,5},{5,1},{2,6},{6,2},{3,7},{7,3},{8,12},{12,8},{9,1... | collective-permute-start | bytes 430088 | tf_op jit(solution)/shard_map/ppermute | solution.py:579
  15.4 21.3 %collective-permute-start.7 = (bf16[1472,128]{1,0:T(8,128)(2,1)S(1)}, bf16[1472,128]{1,0:T(8,128)(2,1)S(1)}, u32[]{:S(2)}, u32[]{:S(2)}) collective-permute-start(bf16[1472,128]{1,0:T(8,128)(2,1)S(1)} %get-tuple-element.37), channel_id=1, source_target_pairs={{0,1},{1,0},{2,3},{3,2},{4,5},{5,4},{6,7},{7,6},{8,9},{9,8},{10,11... | collective-permute-start | bytes 1130504 | tf_op jit(solution)/shard_map/ppermute | solution.py:567
  17.0 28.7 %collective-permute-start.8 = (bf16[1472,128]{1,0:T(8,128)(2,1)S(1)}, bf16[1472,128]{1,0:T(8,128)(2,1)S(1)}, u32[]{:S(2)}, u32[]{:S(2)}) collective-permute-start(bf16[1472,128]{1,0:T(8,128)(2,1)S(1)} %get-tuple-element.38), channel_id=1, source_target_pairs={{0,2},{1,3},{2,0},{3,1},{4,6},{5,7},{6,4},{7,5},{8,10},{9,11},{10,... | collective-permute-start | bytes 1130504 | tf_op jit(solution)/shard_map/ppermute | solution.py:567
  19.6 26.1 %collective-permute-start.9 = (bf16[1472,128]{1,0:T(8,128)(2,1)S(1)}, bf16[1472,128]{1,0:T(8,128)(2,1)S(1)}, u32[]{:S(2)}, u32[]{:S(2)}) collective-permute-start(bf16[1472,128]{1,0:T(8,128)(2,1)S(1)} %get-tuple-element.39), channel_id=1, source_target_pairs={{0,3},{1,2},{2,1},{3,0},{4,7},{5,6},{6,5},{7,4},{8,11},{9,10},{10,... | collective-permute-start | bytes 1130504 | tf_op jit(solution)/shard_map/ppermute | solution.py:567
  19.8 1.4 %collective-permute-start.5 = (bf16[560,128]{1,0:T(8,128)(2,1)S(1)}, bf16[560,128]{1,0:T(8,128)(2,1)S(1)}, u32[]{:S(2)}, u32[]{:S(2)}) collective-permute-start(bf16[560,128]{1,0:T(8,128)(2,1)S(1)} %collective-permute-done.2.refs_3_), channel_id=1, source_target_pairs={{0,4},{4,0},{1,5},{5,1},{2,6},{6,2},{3,7},{7,3},{8,12},{12,8},{9,1... | collective-permute-start | bytes 430088 | tf_op jit(solution)/shard_map/ppermute | solution.py:579
  19.8 1.6 %collective-permute-start.6 = (bf16[560,128]{1,0:T(8,128)(2,1)S(1)}, bf16[560,128]{1,0:T(8,128)(2,1)S(1)}, u32[]{:S(2)}, u32[]{:S(2)}) collective-permute-start(bf16[560,128]{1,0:T(8,128)(2,1)S(1)} %collective-permute-done.3.refs_5_), channel_id=1, source_target_pairs={{0,4},{4,0},{1,5},{5,1},{2,6},{6,2},{3,7},{7,3},{8,12},{12,8},{9,1... | collective-permute-start | bytes 430088 | tf_op jit(solution)/shard_map/ppermute | solution.py:579
  45.7 26.0 %collective-permute-start.10 = (bf16[1472,128]{1,0:T(8,128)(2,1)S(1)}, bf16[1472,128]{1,0:T(8,128)(2,1)S(1)}, u32[]{:S(2)}, u32[]{:S(2)}) collective-permute-start(bf16[1472,128]{1,0:T(8,128)(2,1)S(1)} %collective-permute-done.7.rest_0_), channel_id=1, source_target_pairs={{0,4},{4,0},{1,5},{5,1},{2,6},{6,2},{3,7},{7,3},{8,12},{12,8},{9,1... | collective-permute-start | bytes 1130504 | tf_op jit(solution)/shard_map/ppermute | solution.py:618
  45.7 26.0 %collective-permute-start.11 = (bf16[1472,128]{1,0:T(8,128)(2,1)S(1)}, bf16[1472,128]{1,0:T(8,128)(2,1)S(1)}, u32[]{:S(2)}, u32[]{:S(2)}) collective-permute-start(bf16[1472,128]{1,0:T(8,128)(2,1)S(1)} %collective-permute-done.8.rest_1_), channel_id=1, source_target_pairs={{0,4},{4,0},{1,5},{5,1},{2,6},{6,2},{3,7},{7,3},{8,12},{12,8},{9,1... | collective-permute-start | bytes 1130504 | tf_op jit(solution)/shard_map/ppermute | solution.py:618
  46.2 25.5 %collective-permute-start.12 = (bf16[1472,128]{1,0:T(8,128)(2,1)S(1)}, bf16[1472,128]{1,0:T(8,128)(2,1)S(1)}, u32[]{:S(2)}, u32[]{:S(2)}) collective-permute-start(bf16[1472,128]{1,0:T(8,128)(2,1)S(1)} %collective-permute-done.9.rest_2_), channel_id=1, source_target_pairs={{0,4},{4,0},{1,5},{5,1},{2,6},{6,2},{3,7},{7,3},{8,12},{12,8},{9,1... | collective-permute-start | bytes 1130504 | tf_op jit(solution)/shard_map/ppermute | solution.py:618

commit v7 on v5

--- a/solution.py
+++ b/solution.py
@@ -60,9 +60,31 @@
     return lax.axis_index("chip") * lax.axis_size("core") + lax.axis_index("core")
 
 
-def project_kernel(tok_hbm, fw_hbm, ww_hbm, vw_hbm, ld_hbm, do_hbm, *rest):
-    *sends, keys_ref, query_ref, feat_ref, cum_ref = rest[:-8]
-    tok_ref, fw_ref, ww_ref, vw_ref, ld_ref, do_ref, sems, small = rest[-8:]
+def pack_copies(ww_hbm, vw_hbm, fw_hbm, own_ref, sends, sems):
+    head, core = lax.axis_index("tp"), lax.axis_index("core")
+    nf2 = fw_hbm.shape[0]
+    tile = own_ref.shape[1] * LANES // (3 * LANES + nf2)
+    parts = [(ref, 2 * jnp.bitwise_xor(head, t + 1) + core) for t, ref in enumerate(sends)]
+    parts += [(own_ref.at[k], 2 * head + k) for k in range(2)]
+    copies = []
+    for n, (ref, piece) in enumerate(parts):
+        rows = pl.ds(pl.multiple_of(piece * tile, tile), tile)
+        moves = [
+            (ww_hbm.at[rows, pl.ds(0, LANES)], ref.at[pl.ds(0, tile), :]),
+            (ww_hbm.at[rows, pl.ds(LANES, LANES)], ref.at[pl.ds(tile, tile), :]),
+            (vw_hbm.at[rows, :], ref.at[pl.ds(2 * tile, tile), :]),
+        ]
+        for m in range(tile // LANES):
+            lanes = pl.ds(pl.multiple_of(piece * tile + m * LANES, LANES), LANES)
+            moves.append((fw_hbm.at[:, lanes], ref.at[pl.ds(3 * tile + m * nf2, nf2), :]))
+        for m, (src, dst) in enumerate(moves):
+            copies.append(pltpu.make_async_copy(src, dst, sems.at[n, m]))
+    return copies
+
+
+def project_kernel(packs, tok_hbm, fw_hbm, ww_hbm, vw_hbm, ld_hbm, do_hbm, *rest):
+    *sends, keys_ref, query_ref, feat_ref, cum_ref = rest[packs:-9]
+    tok_ref, fw_ref, ww_ref, vw_ref, ld_ref, do_ref, sems, small, pack_sems = rest[-9:]
     me = block_index()
     rows, dim = tok_ref.shape
     dh = do_ref.shape[1]
@@ -86,6 +108,9 @@
     for group in copies[1:]:
         for copy in group:
             copy.start()
+    packing = pack_copies(ww_hbm, vw_hbm, fw_hbm, rest[0], rest[1:packs], pack_sems) if packs else []
+    for copy in packing:
+        copy.start()
     for copy in others:
         copy.wait()
     at_row, at_col = iotas(rows)
@@ -136,31 +161,7 @@
         later = jnp.bitwise_xor(me, max(2 * at, 1)) > me
         pl.when(later)(lambda ref=ref: put_keys(ref))
         pl.when(jnp.logical_not(later))(lambda ref=ref: put_query(ref))
-
-
-def pack_kernel(ww_hbm, vw_hbm, fw_hbm, own_ref, *rest):
-    sends, sems = rest[:-1], rest[-1]
-    head, core = lax.axis_index("tp"), lax.axis_index("core")
-    nf2 = fw_hbm.shape[0]
-    tile = (own_ref.shape[1] * LANES) // (3 * LANES + nf2)
-    parts = [(own_ref.at[k], 2 * head + k) for k in range(2)]
-    parts += [(ref, 2 * jnp.bitwise_xor(head, t + 1) + core) for t, ref in enumerate(sends)]
-    copies = []
-    for n, (ref, piece) in enumerate(parts):
-        rows = pl.ds(pl.multiple_of(piece * tile, tile), tile)
-        moves = [
-            (ww_hbm.at[rows, pl.ds(0, LANES)], ref.at[pl.ds(0, tile), :]),
-            (ww_hbm.at[rows, pl.ds(LANES, LANES)], ref.at[pl.ds(tile, tile), :]),
-            (vw_hbm.at[rows, :], ref.at[pl.ds(2 * tile, tile), :]),
-        ]
-        for m in range(tile // LANES):
-            lanes = pl.ds(pl.multiple_of(piece * tile + m * LANES, LANES), LANES)
-            moves.append((fw_hbm.at[:, lanes], ref.at[pl.ds(3 * tile + m * nf2, nf2), :]))
-        for m, (src, dst) in enumerate(moves):
-            copies.append(pltpu.make_async_copy(src, dst, sems.at[n, m]))
-    for copy in copies:
-        copy.start()
-    for copy in copies:
+    for copy in packing:
         copy.wait()
 
 
@@ -283,15 +284,11 @@
 
 
 def gradient_kernel(count, *rest):
-    parts = len(rest) - 7 >> 1
-    recvs, stats = rest[:parts], rest[parts : 2 * parts]
-    own_ref, query_ref, feat_ref, sheet_ref, mine_ref, grad_ref, total_ref = rest[2 * parts :]
+    recvs = rest[:-6]
+    own_ref, query_ref, feat_ref, sheet_ref, stat_ref, grad_ref = rest[-6:]
 
     def recv(d):
         return recvs[d - 1] if len(recvs) > 1 else recvs[0].at[d - 1]
-
-    def stat(d):
-        return stats[d - 1] if len(stats) > 1 else stats[0].at[d - 1]
 
     me = block_index()
     rows = feat_ref.shape[0]
@@ -307,15 +304,9 @@
     q, k = feat_ref[:, :nf], feat_ref[:, nf:]
     lse_c, dw_c = sheet_ref[:, 0:1], sheet_ref[:, 1:2]
     rden_c, dl_c, cum_c = sheet_ref[:, 2:3], sheet_ref[:, 3:4], sheet_ref[:, 4:5]
+    mine_ref = stat_ref.at[me]
     own_cum = mine_ref[4:5, :]
-    total_ref[pl.ds(me, 1), :] = own_cum[:, rows - LANES :]
-
-    def place(d, carry):
-        total_ref[pl.ds(partner(me, d, count), 1), :] = stat(d)[4:5, rows - LANES :]
-        return carry
-
-    over_partners(count, place, 0)
-    totals = total_ref[:, LANES - 1 :]
+    totals = jnp.concatenate([stat_ref[j, 4:5, rows - 1 : rows] for j in range(count)], axis=0)
     growth_c = jnp.exp(cum_c) * rden_c
     tail_c = jnp.exp(own_cum[:, rows - 1 : rows] - cum_c)
 
@@ -356,7 +347,7 @@
         other_w = view[0:rows, :]
         other_v = view[rows : 2 * rows, :]
         other_f = wide(view, feat_at, nf)
-        st = stat(d)
+        st = stat_ref[j]
         zero = jnp.zeros((1, rows), f32)
         cum = st[4:5, :]
         gap = between(totals, jnp.minimum(me, j), jnp.maximum(me, j))
@@ -404,36 +395,41 @@
 def share_kernel(grad_ref, own_ref, *rest):
     heads = grad_ref.shape[0]
     near, far = rest[: heads - 1], rest[heads - 1 : 2 * heads - 2]
-    first_ref, second_ref, cat_ref, feat_ref = rest[-4:]
-    rows = cat_ref.shape[0]
-    tile = first_ref.shape[1]
+    most_ref, last_ref, cat_ref, feat_ref = rest[-4:]
     nf2 = feat_ref.shape[1] // heads
     head, core = lax.axis_index("tp"), lax.axis_index("core")
     gather_rows(
         grad_ref, [head] + [jnp.bitwise_xor(head, t) for t in range(1, heads)], cat_ref, feat_ref
     )
-
-    def product(out_ref, views):
+    most = most_ref.shape[0]
+    tile = most_ref.shape[1] // 2
+
+    def product(k, views):
         main = jnp.concatenate(
             [v[m * tile : (m + 1) * tile, :] for v in views for m in range(3)], axis=1
         )
         feats = jnp.concatenate([wide(v, 3 * tile, nf2) for v in views], axis=0)
-        out_ref[...] = (nt(cat_ref[...], main) + nn(feat_ref[...], feats)).astype(bf16)
-
-    for flag, ours, theirs in ((0, first_ref, second_ref), (1, second_ref, first_ref)):
+        out = (nt(cat_ref[...], main) + nn(feat_ref[...], feats)).astype(bf16)
+        most_ref[:, k * tile : (k + 1) * tile] = out[:most]
+        last_ref[:, k * tile : (k + 1) * tile] = out[most:]
+
+    for flag, zero, one in ((0, near, far), (1, far, near)):
 
         @pl.when(core == flag)
         def _():
-            product(ours, [own_ref.at[flag], *near])
-            product(theirs, [own_ref.at[1 - flag], *far])
-
-
-def lay_kernel(first_ref, second_ref, out_ref):
-    shares, _, tile = first_ref.shape
+            product(0, [own_ref.at[0], *zero])
+            product(1, [own_ref.at[1], *one])
+
+
+def lay_kernel(most_ref, own_ref, *rest):
+    *lasts, out_ref = rest
+    shares, most, width = most_ref.shape
+    head = lax.axis_index("tp")
     for z in range(shares):
-        at = 2 * z * tile
-        out_ref[:, at : at + tile] = first_ref[z]
-        out_ref[:, at + tile : at + 2 * tile] = second_ref[z]
+        out_ref[0:most, z * width : (z + 1) * width] = most_ref[z]
+    for t, ref in enumerate([own_ref, *lasts]):
+        at = pl.multiple_of(jnp.bitwise_xor(head, t) * width, width)
+        out_ref[most:, pl.ds(at, width)] = ref[...]
 
 
 def merge_kernel(grad_ref, weight_ref, out_ref, cat_ref, feat_ref):
@@ -497,17 +493,25 @@
     tile = 2 * LANES
     fw_t = feature_weight.T
 
+    shared = heads & (heads - 1) == 0 and 2 * tile * heads == dim
+    height = 3 * tile + nf2 * tile // LANES
+    packs = []
+    if shared:
+        packs = [jax.ShapeDtypeStruct((2, height, LANES), bf16)]
+        packs += [jax.ShapeDtypeStruct((height, LANES), bf16)] * (heads - 1)
+
     payload = 2 * rows + 2 * nf + 16
     block = jax.ShapeDtypeStruct((payload, LANES), bf16)
-    *sends, own, query, feat, cum = pl.pallas_call(
-        project_kernel,
-        out_shape=[block] * (chips + 2)
+    outs = pl.pallas_call(
+        lambda *refs: project_kernel(len(packs), *refs),
+        out_shape=packs
+        + [block] * (chips + 2)
         + [
             jax.ShapeDtypeStruct((rows, nf2), bf16),
             jax.ShapeDtypeStruct((rows, 1), f32),
         ],
         in_specs=[HBM] * 6,
-        out_specs=[VMEM] * (chips + 4),
+        out_specs=[VMEM] * (len(packs) + chips + 4),
         scratch_shapes=[
             pltpu.VMEM((rows, dim), bf16),
             pltpu.VMEM((nf2, dim), bf16),
@@ -517,31 +521,18 @@
             pltpu.VMEM((rows, dh), bf16),
             pltpu.SemaphoreType.DMA((CHUNKS, 4)),
             pltpu.SemaphoreType.DMA((2,)),
+            pltpu.SemaphoreType.DMA((heads + 1, 3 + tile // LANES)),
         ],
         compiler_params=params,
         cost_estimate=cost(2 * rows * dim * columns, 4 * 1024 * 1024),
         name="project",
     )(*in_hbm(tokens, fw_t, window_weight, value_weight, log_decay.T, out_grad))
-
-    shared = heads & (heads - 1) == 0 and 2 * tile * heads == dim
-    if shared:
-        sources, _ = lax.optimization_barrier(((window_weight, value_weight, fw_t), sends[0]))
-        area = 3 * tile + nf2 * tile // LANES
-        own_weights, *packed = pl.pallas_call(
-            pack_kernel,
-            out_shape=[jax.ShapeDtypeStruct((2, area, LANES), bf16)]
-            + [jax.ShapeDtypeStruct((area, LANES), bf16)] * (heads - 1),
-            in_specs=[HBM] * 3,
-            out_specs=[VMEM] * heads,
-            scratch_shapes=[pltpu.SemaphoreType.DMA((heads + 1, 3 + tile // LANES))],
-            compiler_params=params,
-            cost_estimate=cost(1, 2 * columns * tile * (heads + 1) * 2),
-            name="pack",
-        )(*in_hbm(*sources))
-        near = [
-            lax.ppermute(packed[t - 1], "tp", [(z, z ^ t) for z in range(heads)])
-            for t in range(1, heads)
-        ]
+    packed, (*sends, own, query, feat, cum) = outs[: len(packs)], outs[len(packs) :]
+    near = [
+        lax.ppermute(p, "tp", [(z, z ^ t) for z in range(heads)])
+        for t, p in enumerate(packed)
+        if t
+    ]
 
     swap = [(0, 1), (1, 0)]
     recv = {}
@@ -572,21 +563,16 @@
         cost_estimate=cost(10**9, 2 * 1024 * 1024, 10**6),
         name="query_side",
     )(*recv, own, query, feat, cum)
-    stats = [
-        lax.ppermute(stat, CTX, [(i, i ^ d) for i in range(count)]) for d in range(1, count)
-    ]
-    if count > 8:
-        stats = [jnp.stack(stats)]
+    stats = lax.all_gather(stat, CTX)
     grads = pl.pallas_call(
         lambda *refs: gradient_kernel(count, *refs),
         out_shape=jax.ShapeDtypeStruct((3 * rows + nf2 * rows // LANES, LANES), bf16),
-        in_specs=[VMEM] * (2 * len(recv) + 5),
+        in_specs=[VMEM] * (len(recv) + 5),
         out_specs=VMEM,
-        scratch_shapes=[pltpu.VMEM((count, LANES), f32)],
         compiler_params=params,
         cost_estimate=cost(10**9, 2 * 1024 * 1024, 10**6),
         name="gradients",
-    )(*recv, *stats, own, query, feat, sheet, stat)
+    )(*recv, own, query, feat, sheet, stats)
     if not shared:
         weights = jnp.concatenate([window_weight, value_weight, feature_weight], axis=1)
         weights = lax.all_gather(weights, "tp")
@@ -595,9 +581,13 @@
     near, grads = lax.optimization_barrier((near, grads))
     far = [lax.ppermute(n, "core", swap) for n in near]
     grads = lax.all_gather(grads, "tp")
-    tiles = pl.pallas_call(
+    last = 16
+    sums, ends = pl.pallas_call(
         share_kernel,
-        out_shape=[jax.ShapeDtypeStruct((rows, tile), bf16)] * 2,
+        out_shape=[
+            jax.ShapeDtypeStruct((rows - last, 2 * tile), bf16),
+            jax.ShapeDtypeStruct((last, 2 * tile), bf16),
+        ],
         in_specs=[VMEM] * (2 * heads),
         out_specs=[VMEM] * 2,
         scratch_shapes=[
@@ -605,19 +595,21 @@
             pltpu.VMEM((rows, nf2 * heads), bf16),
         ],
         compiler_params=params,
-        cost_estimate=cost(4 * rows * tile * heads * columns, 4 * heads * tile * columns),
+        cost_estimate=cost(4 * rows * tile * heads * columns, 4 * heads * height * LANES),
         name="share",
-    )(grads, own_weights, *near, *far)
-    first, second = [lax.all_gather(t, "tp") for t in tiles]
+    )(grads, packed[0], *near, *far)
+    others = [
+        lax.ppermute(ends, "tp", [(z, z ^ t) for z in range(heads)]) for t in range(1, heads)
+    ]
     total = pl.pallas_call(
         lay_kernel,
         out_shape=jax.ShapeDtypeStruct((rows, dim), bf16),
-        in_specs=[VMEM] * 2,
+        in_specs=[VMEM] * (heads + 1),
         out_specs=VMEM,
         compiler_params=params,
         cost_estimate=cost(1, 4 * rows * dim),
         name="lay",
-    )(first, second)
+    )(lax.all_gather(sums, "tp"), ends, *others)
     return (attended, total)
 
 

time: 94.4 us -> 85 us (0.900)
  waiting for transfers between devices: 12.7 us -> 6.91 us
  starting transfers between devices: 16.5 us -> 14.7 us
    ppermute x10 -> x6, waiting for transfers between devices: 5.9 us -> 0.12 us  [the longest x3 0.12 us: per_device(): lax.ppermute(p, 'tp', [(z, z ^ t) for z in range(heads)])]
    ppermute x10 -> x6, starting transfers between devices: 10.8 us -> 8.84 us  [the longest x3 4.45 us: per_device(): lax.ppermute(ends, 'tp', [(z, z ^ t) for z in range(heads)])]
    all_gather x2, blocking collectives: 31 us -> 29.3 us  [the longest x1 20.1 us: per_device(): lax.all_gather(sums, 'tp')]
    pallas_call x3 -> x2, Pallas kernels: 5.72 us -> 4.96 us  [the longest x1 4.14 us: per_device(): pl.pallas_call(lambda *refs: project_kernel(len(packs), *refs), out_shape...]
  transfers between devices with their start and end apart: 20 -> 16, of which waited for: 8 -> 3; matrix products, arithmetic and copies ran while one was open for 0% -> 0% of each run, Pallas kernels for 8% -> 7%
where the time goes in v7:
time: 85 us; the launch traced here: 84.9 us
  blocking collectives  50.5 us (59%)
  starting transfers between devices  14.7 us (17%)
  Pallas kernels  12 us (14%)
  waiting for transfers between devices  6.91 us (8%)
    all_gather x1, blocking collectives, per_device(): grads = lax.all_gather(grads, 'tp')  21.2 us
    all_gather x1, blocking collectives, per_device(): lax.all_gather(sums, 'tp')  20.1 us
    all_gather x1, blocking collectives, per_device(): stats = lax.all_gather(stat, CTX)  9.22 us
    ppermute x3, waiting for transfers between devices, per_device(): lax.ppermute(sends[d], 'chip', [(i, i ^ d) for i in range(chips)])  6.77 us
    ppermute x3, starting transfers between devices, per_device(): lax.ppermute(sends[d], 'chip', [(i, i ^ d) for i in range(chips)])  4.54 us
    ppermute x3, starting transfers between devices, per_device(): lax.ppermute(ends, 'tp', [(z, z ^ t) for z in range(heads)])  4.45 us
    ppermute x3, starting transfers between devices, per_device(): lax.ppermute(p, 'tp', [(z, z ^ t) for z in range(heads)])  4.39 us
    pallas_call x1, Pallas kernels, per_device(): pl.pallas_call(lambda *refs: project_kernel(len(packs), *refs), out_shape...  4.14 us
  transfers between devices with their start and end apart: 16, of which 3 were waited for; matrix products, arithmetic and copies ran while one was open for 0% of the time, Pallas kernels for 7%

profile of v7, /device:TPU:0, one launch (start us, length us, event | category | flops | bytes accessed | tf_op | source)
XLA Modules:
  0.0 84.9 jit_solution(1717655483479200405)
XLA Ops:
  0.6 4.1 %project.1 = (bf16[2,832,128]{2,1,0:T(8,128)(2,1)S(1)}, bf16[832,128]{1,0:T(8,128)(2,1)S(1)}, bf16[832,128]{1,0:T(8,128)(2,1)S(1)}, bf16[832,128]{1,0:T(8,128)(2...) custom-call(bf16[256,2048]{1,0:T(8,128)(2,1)} %refs_0_.1, ...), custom_call_target="tpu_custom_call" | custom-call | flops 436207616 | bytes 4194304 | tf_op jit(solution)/shard_map/project/pallas_call | solution.py:505
  4.8 3.0 %collective-permute-start.1 = (bf16[560,128]{1,0:T(8,128)(2,1)S(1)}, bf16[560,128]{1,0:T(8,128)(2,1)S(1)}, u32[]{:S(2)}, u32[]{:S(2)}) collective-permute-start(bf16[560,128]{1,0:T(8,128)(2,1)S(1)} %get-tuple-element.24), channel_id=1, source_target_pairs={{0,8},{8,0},{16,24},{24,16},{1,9},{9,1},{17,25},{25,17},{2,10},{10... | collective-permute-start | bytes 430088 | tf_op jit(solution)/shard_map/ppermute | solution.py:540
  7.8 1.5 %collective-permute-start.3 = (bf16[560,128]{1,0:T(8,128)(2,1)S(1)}, bf16[560,128]{1,0:T(8,128)(2,1)S(1)}, u32[]{:S(2)}, u32[]{:S(2)}) collective-permute-start(bf16[560,128]{1,0:T(8,128)(2,1)S(1)} %get-tuple-element.25), channel_id=1, source_target_pairs={{0,16},{8,24},{16,0},{24,8},{1,17},{9,25},{17,1},{25,9},{2,18},{10... | collective-permute-start | bytes 430088 | tf_op jit(solution)/shard_map/ppermute | solution.py:540
  9.3 0.0 collective-permute-start.5
  9.3 0.0 collective-permute-start
  9.3 2.6 %collective-permute-done.1.refs_1_ = bf16[560,128]{1,0:T(8,128)(2,1)S(1)} collective-permute-done((bf16[560,128]{1,0:T(8,128)(2,1)S(1)}, bf16[560,128]{1,0:T(8,128)(2,1)S(1)}, u32[]{:S(2)}, u32[]{:S(2)}) %collective-permute-start.1) | collective-permute-done | bytes 143392 | tf_op jit(solution)/shard_map/ppermute | solution.py:540
  11.9 0.0 collective-permute-start.2
  11.9 4.1 %collective-permute-done.3.refs_3_ = bf16[560,128]{1,0:T(8,128)(2,1)S(1)} collective-permute-done((bf16[560,128]{1,0:T(8,128)(2,1)S(1)}, bf16[560,128]{1,0:T(8,128)(2,1)S(1)}, u32[]{:S(2)}, u32[]{:S(2)}) %collective-permute-start.3) | collective-permute-done | bytes 143392 | tf_op jit(solution)/shard_map/ppermute | solution.py:540
  16.1 0.0 collective-permute-start.4
  16.1 0.0 collective-permute-done.5.refs_5_
  16.1 0.5 collective-permute-start.6
  16.6 1.6 %collective-permute-start.7 = (bf16[832,128]{1,0:T(8,128)(2,1)S(1)}, bf16[832,128]{1,0:T(8,128)(2,1)S(1)}, u32[]{:S(2)}, u32[]{:S(2)}) collective-permute-start(bf16[832,128]{1,0:T(8,128)(2,1)S(1)} %get-tuple-element.32), channel_id=1, source_target_pairs={{0,1},{1,0},{2,3},{3,2},{4,5},{5,4},{6,7},{7,6},{8,9},{9,8},{10,11... | collective-permute-start | bytes 638984 | tf_op jit(solution)/shard_map/ppermute | solution.py:532
  18.2 0.0 collective-permute-done.refs_0_
  18.2 2.6 %collective-permute-start.8 = (bf16[832,128]{1,0:T(8,128)(2,1)S(1)}, bf16[832,128]{1,0:T(8,128)(2,1)S(1)}, u32[]{:S(2)}, u32[]{:S(2)}) collective-permute-start(bf16[832,128]{1,0:T(8,128)(2,1)S(1)} %get-tuple-element.33), channel_id=1, source_target_pairs={{0,2},{1,3},{2,0},{3,1},{4,6},{5,7},{6,4},{7,5},{8,10},{9,11},{10,... | collective-permute-start | bytes 638984 | tf_op jit(solution)/shard_map/ppermute | solution.py:532
  20.8 0.0 collective-permute-done.2.refs_2_
  20.8 0.2 collective-permute-start.9
  21.0 0.0 collective-permute-done.4.refs_4_
  21.0 0.0 collective-permute-done.6.refs_6_
  21.0 2.4 %query_side.1 = (bf16[256,128]{1,0:T(8,128)(2,1)}, f32[8,256]{1,0:T(8,128)S(1)}, f32[256,128]{1,0:T(8,128)S(1)}) custom-call(bf16[560,128]{1,0:T(8,128)(2,1)S(1)} %collective-permute-done.refs_0_, bf16[560,128]{1,0:T(8,128)(2,1)S(1)} %collective-permute-done.1.refs_1_, bf16[560,128]{1,0:T(8,128)(2,1)S(1)} %collective-permute-done.2.refs_2_, ...), custom_call_target="tpu_custom_call" | custom-call | flops 1000000000 | bytes 2097152 | tf_op jit(solution)/shard_map/query_side/pallas_call | solution.py:548
  23.4 9.2 %all-gather = f32[64,256]{1,0:T(8,128)S(1)} all-gather(f32[8,256]{1,0:T(8,128)S(1)} %get-tuple-element.36), channel_id=2, replica_groups=mesh['chip'=4,'core'=2,'tp'=4] {'chip','core'}, dimensions={0}, use_global_device_ids=true | all-gather | bytes 73728 | tf_op jit(solution)/shard_map/all_gather | solution.py:566
  32.6 3.6 %gradients.1 = bf16[832,128]{1,0:T(8,128)(2,1)S(1)} custom-call(bf16[560,128]{1,0:T(8,128)(2,1)S(1)} %collective-permute-done.refs_0_, bf16[560,128]{1,0:T(8,128)(2,1)S(1)} %collective-permute-done.1.refs_1_, bf16[560,128]{1,0:T(8,128)(2,1)S(1)} %collective-permute-done.2.refs_2_, bf16[560,128]{1,0:T(8,128)(2,1)S(1)} %collective-permute-done.3.refs_3_, ...), custom_call_target="tpu_custom_call" | custom-call | flops 1000000000 | bytes 2097152 | tf_op jit(solution)/shard_map/gradients/pallas_call | solution.py:567
  36.3 0.0 collective-permute-done.7.rest_0_
  36.3 0.1 collective-permute-done.8.rest_1_
  36.4 0.0 collective-permute-done.9.rest_2_
  36.4 0.3 collective-permute-start.10
  36.7 0.2 collective-permute-start.11
  36.9 0.3 collective-permute-start.12
  37.2 21.2 %all-gather.1 = bf16[3328,128]{1,0:T(8,128)(2,1)S(1)} all-gather(bf16[832,128]{1,0:T(8,128)(2,1)S(1)} %gradients.1), channel_id=3, replica_groups=mesh['chip'=4,'core'=2,'tp'=4] {'tp'}, dimensions={0}, use_global_device_ids=true | all-gather | bytes 1064960 | tf_op jit(solution)/shard_map/all_gather | solution.py:583
  58.4 0.0 collective-permute-done.10.rest_3_
  58.4 0.0 collective-permute-done.11.rest_4_
  58.4 0.0 collective-permute-done.12.rest_5_
  58.4 0.8 share.1
  59.2 1.7 %collective-permute-start.15 = (bf16[16,512]{1,0:T(8,128)(2,1)S(1)}, bf16[16,512]{1,0:T(8,128)(2,1)S(1)}, u32[]{:S(2)}, u32[]{:S(2)}) collective-permute-start(bf16[16,512]{1,0:T(8,128)(2,1)S(1)} %get-tuple-element.43.own_ref), channel_id=1, source_target_pairs={{0,3},{1,2},{2,1},{3,0},{4,7},{5,6},{6,5},{7,4},{8,11},{9,10},{10,... | collective-permute-start | bytes 49160 | tf_op jit(solution)/shard_map/ppermute | solution.py:602
  61.0 0.0 collective-permute-start.14
  61.0 2.7 %collective-permute-start.13 = (bf16[16,512]{1,0:T(8,128)(2,1)S(1)}, bf16[16,512]{1,0:T(8,128)(2,1)S(1)}, u32[]{:S(2)}, u32[]{:S(2)}) collective-permute-start(bf16[16,512]{1,0:T(8,128)(2,1)S(1)} %get-tuple-element.43.own_ref), channel_id=1, source_target_pairs={{0,1},{1,0},{2,3},{3,2},{4,5},{5,4},{6,7},{7,6},{8,9},{9,8},{10,11... | collective-permute-start | bytes 49160 | tf_op jit(solution)/shard_map/ppermute | solution.py:602
  63.7 20.1 %all-gather.2 = bf16[960,512]{1,0:T(8,128)(2,1)S(1)} all-gather(bf16[240,512]{1,0:T(8,128)(2,1)S(1)} %get-tuple-element.42), channel_id=4, replica_groups=mesh['chip'=4,'core'=2,'tp'=4] {'tp'}, dimensions={0}, use_global_device_ids=true | all-gather | bytes 1228800 | tf_op jit(solution)/shard_map/all_gather | solution.py:612
  83.8 0.0 collective-permute-done.15.rest_2_
  83.8 0.0 collective-permute-done.14.rest_1_
  83.8 0.0 collective-permute-done.13.rest_0_
  83.8 1.0 %lay.1 = bf16[256,2048]{1,0:T(8,128)(2,1)} custom-call(bf16[4,240,512]{2,1,0:T(8,128)(2,1)S(1)} %bitcast.5, bf16[16,512]{1,0:T(8,128)(2,1)S(1)} %get-tuple-element.43.own_ref, bf16[16,512]{1,0:T(8,128)(2,1)S(1)} %collective-permute-done.13.rest_0_, bf16[16,512]{1,0:T(8,128)(2,1)S(1)} %collective-permute-done.14.rest_1_, ...), custom_call_target="tpu_custom_call" | custom-call | flops 1 | bytes 2097152 | tf_op jit(solution)/shard_map/lay/pallas_call | solution.py:604
Async XLA Ops:
  4.8 7.2 %collective-permute-start.1 = (bf16[560,128]{1,0:T(8,128)(2,1)S(1)}, bf16[560,128]{1,0:T(8,128)(2,1)S(1)}, u32[]{:S(2)}, u32[]{:S(2)}) collective-permute-start(bf16[560,128]{1,0:T(8,128)(2,1)S(1)} %get-tuple-element.24), channel_id=1, source_target_pairs={{0,8},{8,0},{16,24},{24,16},{1,9},{9,1},{17,25},{25,17},{2,10},{10... | collective-permute-start | bytes 430088 | tf_op jit(solution)/shard_map/ppermute | solution.py:540
  7.8 8.3 %collective-permute-start.3 = (bf16[560,128]{1,0:T(8,128)(2,1)S(1)}, bf16[560,128]{1,0:T(8,128)(2,1)S(1)}, u32[]{:S(2)}, u32[]{:S(2)}) collective-permute-start(bf16[560,128]{1,0:T(8,128)(2,1)S(1)} %get-tuple-element.25), channel_id=1, source_target_pairs={{0,16},{8,24},{16,0},{24,8},{1,17},{9,25},{17,1},{25,9},{2,18},{10... | collective-permute-start | bytes 430088 | tf_op jit(solution)/shard_map/ppermute | solution.py:540
  9.3 6.8 %collective-permute-start.5 = (bf16[560,128]{1,0:T(8,128)(2,1)S(1)}, bf16[560,128]{1,0:T(8,128)(2,1)S(1)}, u32[]{:S(2)}, u32[]{:S(2)}) collective-permute-start(bf16[560,128]{1,0:T(8,128)(2,1)S(1)} %get-tuple-element.26), channel_id=1, source_target_pairs={{0,24},{8,16},{16,8},{24,0},{1,25},{9,17},{17,9},{25,1},{2,26},{10... | collective-permute-start | bytes 430088 | tf_op jit(solution)/shard_map/ppermute | solution.py:540
  9.3 8.9 %collective-permute-start = (bf16[560,128]{1,0:T(8,128)(2,1)S(1)}, bf16[560,128]{1,0:T(8,128)(2,1)S(1)}, u32[]{:S(2)}, u32[]{:S(2)}) collective-permute-start(bf16[560,128]{1,0:T(8,128)(2,1)S(1)} %get-tuple-element.23), channel_id=1, source_target_pairs={{0,4},{4,0},{1,5},{5,1},{2,6},{6,2},{3,7},{7,3},{8,12},{12,8},{9,1... | collective-permute-start | bytes 430088 | tf_op jit(solution)/shard_map/ppermute | solution.py:541
  11.9 8.8 %collective-permute-start.2 = (bf16[560,128]{1,0:T(8,128)(2,1)S(1)}, bf16[560,128]{1,0:T(8,128)(2,1)S(1)}, u32[]{:S(2)}, u32[]{:S(2)}) collective-permute-start(bf16[560,128]{1,0:T(8,128)(2,1)S(1)} %collective-permute-done.1.refs_1_), channel_id=1, source_target_pairs={{0,4},{4,0},{1,5},{5,1},{2,6},{6,2},{3,7},{7,3},{8,12},{12,8},{9,1... | collective-permute-start | bytes 430088 | tf_op jit(solution)/shard_map/ppermute | solution.py:543
  16.1 4.9 %collective-permute-start.4 = (bf16[560,128]{1,0:T(8,128)(2,1)S(1)}, bf16[560,128]{1,0:T(8,128)(2,1)S(1)}, u32[]{:S(2)}, u32[]{:S(2)}) collective-permute-start(bf16[560,128]{1,0:T(8,128)(2,1)S(1)} %collective-permute-done.3.refs_3_), channel_id=1, source_target_pairs={{0,4},{4,0},{1,5},{5,1},{2,6},{6,2},{3,7},{7,3},{8,12},{12,8},{9,1... | collective-permute-start | bytes 430088 | tf_op jit(solution)/shard_map/ppermute | solution.py:543
  16.1 4.9 %collective-permute-start.6 = (bf16[560,128]{1,0:T(8,128)(2,1)S(1)}, bf16[560,128]{1,0:T(8,128)(2,1)S(1)}, u32[]{:S(2)}, u32[]{:S(2)}) collective-permute-start(bf16[560,128]{1,0:T(8,128)(2,1)S(1)} %collective-permute-done.5.refs_5_), channel_id=1, source_target_pairs={{0,4},{4,0},{1,5},{5,1},{2,6},{6,2},{3,7},{7,3},{8,12},{12,8},{9,1... | collective-permute-start | bytes 430088 | tf_op jit(solution)/shard_map/ppermute | solution.py:543
  16.6 19.6 %collective-permute-start.7 = (bf16[832,128]{1,0:T(8,128)(2,1)S(1)}, bf16[832,128]{1,0:T(8,128)(2,1)S(1)}, u32[]{:S(2)}, u32[]{:S(2)}) collective-permute-start(bf16[832,128]{1,0:T(8,128)(2,1)S(1)} %get-tuple-element.32), channel_id=1, source_target_pairs={{0,1},{1,0},{2,3},{3,2},{4,5},{5,4},{6,7},{7,6},{8,9},{9,8},{10,11... | collective-permute-start | bytes 638984 | tf_op jit(solution)/shard_map/ppermute | solution.py:532
  18.2 18.2 %collective-permute-start.8 = (bf16[832,128]{1,0:T(8,128)(2,1)S(1)}, bf16[832,128]{1,0:T(8,128)(2,1)S(1)}, u32[]{:S(2)}, u32[]{:S(2)}) collective-permute-start(bf16[832,128]{1,0:T(8,128)(2,1)S(1)} %get-tuple-element.33), channel_id=1, source_target_pairs={{0,2},{1,3},{2,0},{3,1},{4,6},{5,7},{6,4},{7,5},{8,10},{9,11},{10,... | collective-permute-start | bytes 638984 | tf_op jit(solution)/shard_map/ppermute | solution.py:532
  20.8 15.6 %collective-permute-start.9 = (bf16[832,128]{1,0:T(8,128)(2,1)S(1)}, bf16[832,128]{1,0:T(8,128)(2,1)S(1)}, u32[]{:S(2)}, u32[]{:S(2)}) collective-permute-start(bf16[832,128]{1,0:T(8,128)(2,1)S(1)} %get-tuple-element.34), channel_id=1, source_target_pairs={{0,3},{1,2},{2,1},{3,0},{4,7},{5,6},{6,5},{7,4},{8,11},{9,10},{10,... | collective-permute-start | bytes 638984 | tf_op jit(solution)/shard_map/ppermute | solution.py:532
  36.4 22.0 %collective-permute-start.10 = (bf16[832,128]{1,0:T(8,128)(2,1)S(1)}, bf16[832,128]{1,0:T(8,128)(2,1)S(1)}, u32[]{:S(2)}, u32[]{:S(2)}) collective-permute-start(bf16[832,128]{1,0:T(8,128)(2,1)S(1)} %collective-permute-done.7.rest_0_), channel_id=1, source_target_pairs={{0,4},{4,0},{1,5},{5,1},{2,6},{6,2},{3,7},{7,3},{8,12},{12,8},{9,1... | collective-permute-start | bytes 638984 | tf_op jit(solution)/shard_map/ppermute | solution.py:582
  36.7 21.7 %collective-permute-start.11 = (bf16[832,128]{1,0:T(8,128)(2,1)S(1)}, bf16[832,128]{1,0:T(8,128)(2,1)S(1)}, u32[]{:S(2)}, u32[]{:S(2)}) collective-permute-start(bf16[832,128]{1,0:T(8,128)(2,1)S(1)} %collective-permute-done.8.rest_1_), channel_id=1, source_target_pairs={{0,4},{4,0},{1,5},{5,1},{2,6},{6,2},{3,7},{7,3},{8,12},{12,8},{9,1... | collective-permute-start | bytes 638984 | tf_op jit(solution)/shard_map/ppermute | solution.py:582
  36.9 21.5 %collective-permute-start.12 = (bf16[832,128]{1,0:T(8,128)(2,1)S(1)}, bf16[832,128]{1,0:T(8,128)(2,1)S(1)}, u32[]{:S(2)}, u32[]{:S(2)}) collective-permute-start(bf16[832,128]{1,0:T(8,128)(2,1)S(1)} %collective-permute-done.9.rest_2_), channel_id=1, source_target_pairs={{0,4},{4,0},{1,5},{5,1},{2,6},{6,2},{3,7},{7,3},{8,12},{12,8},{9,1... | collective-permute-start | bytes 638984 | tf_op jit(solution)/shard_map/ppermute | solution.py:582
  59.2 24.6 %collective-permute-start.15 = (bf16[16,512]{1,0:T(8,128)(2,1)S(1)}, bf16[16,512]{1,0:T(8,128)(2,1)S(1)}, u32[]{:S(2)}, u32[]{:S(2)}) collective-permute-start(bf16[16,512]{1,0:T(8,128)(2,1)S(1)} %get-tuple-element.43.own_ref), channel_id=1, source_target_pairs={{0,3},{1,2},{2,1},{3,0},{4,7},{5,6},{6,5},{7,4},{8,11},{9,10},{10,... | collective-permute-start | bytes 49160 | tf_op jit(solution)/shard_map/ppermute | solution.py:602
  61.0 22.8 %collective-permute-start.14 = (bf16[16,512]{1,0:T(8,128)(2,1)S(1)}, bf16[16,512]{1,0:T(8,128)(2,1)S(1)}, u32[]{:S(2)}, u32[]{:S(2)}) collective-permute-start(bf16[16,512]{1,0:T(8,128)(2,1)S(1)} %get-tuple-element.43.own_ref), channel_id=1, source_target_pairs={{0,2},{1,3},{2,0},{3,1},{4,6},{5,7},{6,4},{7,5},{8,10},{9,11},{10,... | collective-permute-start | bytes 49160 | tf_op jit(solution)/shard_map/ppermute | solution.py:602
  61.0 22.8 %collective-permute-start.13 = (bf16[16,512]{1,0:T(8,128)(2,1)S(1)}, bf16[16,512]{1,0:T(8,128)(2,1)S(1)}, u32[]{:S(2)}, u32[]{:S(2)}) collective-permute-start(bf16[16,512]{1,0:T(8,128)(2,1)S(1)} %get-tuple-element.43.own_ref), channel_id=1, source_target_pairs={{0,1},{1,0},{2,3},{3,2},{4,5},{5,4},{6,7},{7,6},{8,9},{9,8},{10,11... | collective-permute-start | bytes 49160 | tf_op jit(solution)/shard_map/ppermute | solution.py:602

commit v8 on v7

--- a/solution.py
+++ b/solution.py
@@ -1,3 +1,5 @@
+from functools import partial
+
 import jax
 import jax.numpy as jnp
 from jax import lax
@@ -9,7 +11,6 @@
 WINDOW = 1024
 LANES = 128
 MASKED = -1e30
-CTX = ("chip", "core")
 CHUNKS = 4
 f32 = jnp.float32
 bf16 = jnp.bfloat16
@@ -56,36 +57,17 @@
     )
 
 
-def block_index():
-    return lax.axis_index("chip") * lax.axis_size("core") + lax.axis_index("core")
-
-
-def pack_copies(ww_hbm, vw_hbm, fw_hbm, own_ref, sends, sems):
-    head, core = lax.axis_index("tp"), lax.axis_index("core")
-    nf2 = fw_hbm.shape[0]
-    tile = own_ref.shape[1] * LANES // (3 * LANES + nf2)
-    parts = [(ref, 2 * jnp.bitwise_xor(head, t + 1) + core) for t, ref in enumerate(sends)]
-    parts += [(own_ref.at[k], 2 * head + k) for k in range(2)]
-    copies = []
-    for n, (ref, piece) in enumerate(parts):
-        rows = pl.ds(pl.multiple_of(piece * tile, tile), tile)
-        moves = [
-            (ww_hbm.at[rows, pl.ds(0, LANES)], ref.at[pl.ds(0, tile), :]),
-            (ww_hbm.at[rows, pl.ds(LANES, LANES)], ref.at[pl.ds(tile, tile), :]),
-            (vw_hbm.at[rows, :], ref.at[pl.ds(2 * tile, tile), :]),
-        ]
-        for m in range(tile // LANES):
-            lanes = pl.ds(pl.multiple_of(piece * tile + m * LANES, LANES), LANES)
-            moves.append((fw_hbm.at[:, lanes], ref.at[pl.ds(3 * tile + m * nf2, nf2), :]))
-        for m, (src, dst) in enumerate(moves):
-            copies.append(pltpu.make_async_copy(src, dst, sems.at[n, m]))
-    return copies
-
-
-def project_kernel(packs, tok_hbm, fw_hbm, ww_hbm, vw_hbm, ld_hbm, do_hbm, *rest):
-    *sends, keys_ref, query_ref, feat_ref, cum_ref = rest[packs:-9]
-    tok_ref, fw_ref, ww_ref, vw_ref, ld_ref, do_ref, sems, small, pack_sems = rest[-9:]
-    me = block_index()
+def block_index(ctx):
+    place = 0
+    for name in ctx:
+        place = place * lax.axis_size(name) + lax.axis_index(name)
+    return place
+
+
+def project_kernel(ctx, tok_hbm, fw_hbm, ww_hbm, vw_hbm, ld_hbm, do_hbm, *rest):
+    *sends, keys_ref, query_ref, feat_ref, cum_ref, ww_ref, vw_ref, fw_ref = rest[:-5]
+    tok_ref, ld_ref, do_ref, sems, small = rest[-5:]
+    me = block_index(ctx)
     rows, dim = tok_ref.shape
     dh = do_ref.shape[1]
     nf = fw_ref.shape[0] // 2
@@ -108,9 +90,6 @@
     for group in copies[1:]:
         for copy in group:
             copy.start()
-    packing = pack_copies(ww_hbm, vw_hbm, fw_hbm, rest[0], rest[1:packs], pack_sems) if packs else []
-    for copy in packing:
-        copy.start()
     for copy in others:
         copy.wait()
     at_row, at_col = iotas(rows)
@@ -161,9 +140,6 @@
         later = jnp.bitwise_xor(me, max(2 * at, 1)) > me
         pl.when(later)(lambda ref=ref: put_keys(ref))
         pl.when(jnp.logical_not(later))(lambda ref=ref: put_query(ref))
-    for copy in packing:
-        copy.wait()
-
 
 def between(totals, low, high):
     at = lax.broadcasted_iota(jnp.int32, totals.shape, 0)
@@ -178,7 +154,7 @@
     return lax.fori_loop(1, count, body, carry)
 
 
-def query_kernel(count, *rest):
+def query_kernel(ctx, count, *rest):
     recvs = rest[: -10]
     (own_ref, query_ref, feat_ref, cum_ref, att_ref, stat_ref, sheet_ref, near_ref, p_ref,
      cums_ref) = rest[-10:]
@@ -186,7 +162,7 @@
     def recv(d):
         return recvs[d - 1] if len(recvs) > 1 else recvs[0].at[d - 1]
 
-    me = block_index()
+    me = block_index(ctx)
     rows, dh = att_ref.shape
     nf = feat_ref.shape[1] // 2
     back = WINDOW // rows
@@ -283,14 +259,14 @@
     stat_ref[...] = jnp.transpose(sheet)[0:8, :]
 
 
-def gradient_kernel(count, *rest):
-    recvs = rest[:-6]
-    own_ref, query_ref, feat_ref, sheet_ref, stat_ref, grad_ref = rest[-6:]
+def gradient_kernel(ctx, count, recvs, *rest):
+    recvs = rest[:recvs]
+    own_ref, query_ref, feat_ref, sheet_ref, stat_ref, *rest = rest[len(recvs) :]
 
     def recv(d):
         return recvs[d - 1] if len(recvs) > 1 else recvs[0].at[d - 1]
 
-    me = block_index()
+    me = block_index(ctx)
     rows = feat_ref.shape[0]
     dh = LANES
     nf = feat_ref.shape[1] // 2
@@ -374,11 +350,38 @@
         return dwq, dqt, dwk, dkt, dv
 
     dwq, dqt, dwk, dkt, dv = over_partners(count, step, (dwq, dqt, dwk, dkt, dv))
-    grad_ref[0:rows, :] = (dwq * scale).astype(bf16)
-    grad_ref[rows : 2 * rows, :] = (dwk * scale).astype(bf16)
-    grad_ref[2 * rows : 3 * rows, :] = dv.astype(bf16)
+    dwq, dwk = (dwq * scale).astype(bf16), (dwk * scale).astype(bf16)
+    dv = dv.astype(bf16)
     dft = (jnp.concatenate([dqt, dkt], axis=0) * feat_scale).astype(bf16)
-    put_wide(grad_ref, 3 * rows, dft)
+    if len(rest) == 1:
+        grad_ref = rest[0]
+        grad_ref[0:rows, :] = dwq
+        grad_ref[rows : 2 * rows, :] = dwk
+        grad_ref[2 * rows : 3 * rows, :] = dv
+        put_wide(grad_ref, 3 * rows, dft)
+        return
+
+    ww_ref, vw_ref, fw_ref, part_ref, *sends = rest
+    head = lax.axis_index("tp")
+    share = part_ref.shape[1]
+    dw = jnp.concatenate([dwq, dwk], axis=1)
+    padded = jnp.concatenate([dft.astype(f32), jnp.zeros((LANES - 2 * nf, rows), f32)], axis=0)
+    df = jnp.transpose(padded)[:, : 2 * nf].astype(bf16)
+    for t, ref in enumerate([part_ref, *sends]):
+        part = pl.ds(pl.multiple_of(jnp.bitwise_xor(head, t) * share, share), share)
+        product = nt(dw, ww_ref[part, :]) + nt(dv, vw_ref[part, :]) + nn(df, fw_ref[:, part])
+        ref[...] = product.astype(ref.dtype)
+
+
+def add_kernel(part_ref, *rest):
+    *others, most_ref, last_ref = rest
+    total = part_ref[...]
+    for ref in others:
+        total += ref[...].astype(f32)
+    most = most_ref.shape[0]
+    total = total.astype(bf16)
+    most_ref[...] = total[:most]
+    last_ref[...] = total[most:]
 
 
 def gather_rows(grad_ref, order, cat_ref, feat_ref):
@@ -390,35 +393,6 @@
             cat_ref[:, lane : lane + LANES] = grad_ref[h, part * rows : (part + 1) * rows, :]
     dft = jnp.concatenate([wide(grad_ref.at[h], 3 * rows, nf2) for h in order], axis=0)
     feat_ref[...] = jnp.transpose(dft.astype(f32)).astype(bf16)
-
-
-def share_kernel(grad_ref, own_ref, *rest):
-    heads = grad_ref.shape[0]
-    near, far = rest[: heads - 1], rest[heads - 1 : 2 * heads - 2]
-    most_ref, last_ref, cat_ref, feat_ref = rest[-4:]
-    nf2 = feat_ref.shape[1] // heads
-    head, core = lax.axis_index("tp"), lax.axis_index("core")
-    gather_rows(
-        grad_ref, [head] + [jnp.bitwise_xor(head, t) for t in range(1, heads)], cat_ref, feat_ref
-    )
-    most = most_ref.shape[0]
-    tile = most_ref.shape[1] // 2
-
-    def product(k, views):
-        main = jnp.concatenate(
-            [v[m * tile : (m + 1) * tile, :] for v in views for m in range(3)], axis=1
-        )
-        feats = jnp.concatenate([wide(v, 3 * tile, nf2) for v in views], axis=0)
-        out = (nt(cat_ref[...], main) + nn(feat_ref[...], feats)).astype(bf16)
-        most_ref[:, k * tile : (k + 1) * tile] = out[:most]
-        last_ref[:, k * tile : (k + 1) * tile] = out[most:]
-
-    for flag, zero, one in ((0, near, far), (1, far, near)):
-
-        @pl.when(core == flag)
-        def _():
-            product(0, [own_ref.at[0], *zero])
-            product(1, [own_ref.at[1], *one])
 
 
 def lay_kernel(most_ref, own_ref, *rest):
@@ -483,61 +457,45 @@
     )(grads, weights)
 
 
-def per_device(tokens, feature_weight, window_weight, value_weight, log_decay, out_grad):
+def per_device(ctx, tokens, feature_weight, window_weight, value_weight, log_decay, out_grad):
     rows, dim = tokens.shape
     nf2 = feature_weight.shape[1]
     nf = nf2 // 2
     dh = value_weight.shape[1]
     columns = 3 * dh + nf2
-    chips, count, heads = lax.axis_size("chip"), lax.axis_size(CTX), lax.axis_size("tp")
-    tile = 2 * LANES
+    chips, count, heads = lax.axis_size(ctx[:-1]), lax.axis_size(ctx), lax.axis_size("tp")
     fw_t = feature_weight.T
-
-    shared = heads & (heads - 1) == 0 and 2 * tile * heads == dim
-    height = 3 * tile + nf2 * tile // LANES
-    packs = []
-    if shared:
-        packs = [jax.ShapeDtypeStruct((2, height, LANES), bf16)]
-        packs += [jax.ShapeDtypeStruct((height, LANES), bf16)] * (heads - 1)
 
     payload = 2 * rows + 2 * nf + 16
     block = jax.ShapeDtypeStruct((payload, LANES), bf16)
-    outs = pl.pallas_call(
-        lambda *refs: project_kernel(len(packs), *refs),
-        out_shape=packs
-        + [block] * (chips + 2)
+    *sends, own, query, feat, cum, ww, vw, fw = pl.pallas_call(
+        partial(project_kernel, ctx),
+        out_shape=[block] * (chips + 2)
         + [
             jax.ShapeDtypeStruct((rows, nf2), bf16),
             jax.ShapeDtypeStruct((rows, 1), f32),
+            jax.ShapeDtypeStruct((dim, 2 * dh), bf16),
+            jax.ShapeDtypeStruct((dim, dh), bf16),
+            jax.ShapeDtypeStruct((nf2, dim), bf16),
         ],
         in_specs=[HBM] * 6,
-        out_specs=[VMEM] * (len(packs) + chips + 4),
+        out_specs=[VMEM] * (chips + 7),
         scratch_shapes=[
             pltpu.VMEM((rows, dim), bf16),
-            pltpu.VMEM((nf2, dim), bf16),
-            pltpu.VMEM((dim, 2 * dh), bf16),
-            pltpu.VMEM((dim, dh), bf16),
             pltpu.VMEM((1, rows), f32),
             pltpu.VMEM((rows, dh), bf16),
             pltpu.SemaphoreType.DMA((CHUNKS, 4)),
             pltpu.SemaphoreType.DMA((2,)),
-            pltpu.SemaphoreType.DMA((heads + 1, 3 + tile // LANES)),
         ],
         compiler_params=params,
         cost_estimate=cost(2 * rows * dim * columns, 4 * 1024 * 1024),
         name="project",
     )(*in_hbm(tokens, fw_t, window_weight, value_weight, log_decay.T, out_grad))
-    packed, (*sends, own, query, feat, cum) = outs[: len(packs)], outs[len(packs) :]
-    near = [
-        lax.ppermute(p, "tp", [(z, z ^ t) for z in range(heads)])
-        for t, p in enumerate(packed)
-        if t
-    ]
 
     swap = [(0, 1), (1, 0)]
     recv = {}
     for d in range(1, chips):
-        recv[2 * d] = lax.ppermute(sends[d], "chip", [(i, i ^ d) for i in range(chips)])
+        recv[2 * d] = lax.ppermute(sends[d], ctx[:-1], [(i, i ^ d) for i in range(chips)])
     recv[1] = lax.ppermute(sends[0], "core", swap)
     for d in range(1, chips):
         recv[2 * d + 1] = lax.ppermute(recv[2 * d], "core", swap)
@@ -546,7 +504,7 @@
         recv = [jnp.stack(recv)]
 
     attended, stat, sheet = pl.pallas_call(
-        lambda *refs: query_kernel(count, *refs),
+        lambda *refs: query_kernel(ctx, count, *refs),
         out_shape=(
             jax.ShapeDtypeStruct((rows, dh), bf16),
             jax.ShapeDtypeStruct((8, rows), f32),
@@ -563,44 +521,54 @@
         cost_estimate=cost(10**9, 2 * 1024 * 1024, 10**6),
         name="query_side",
     )(*recv, own, query, feat, cum)
-    stats = lax.all_gather(stat, CTX)
+    stats = stat
+    for name in reversed(ctx):
+        stats = lax.all_gather(stats, name, tiled=True)
+    stats = stats.reshape(count, -1, rows)
+
+    share = dim // heads
+    shared = heads & (heads - 1) == 0 and share % LANES == 0
+    args = [*recv, own, query, feat, sheet, stats]
+    if shared:
+        args += [ww, vw, fw]
+        out_shape = [jax.ShapeDtypeStruct((rows, share), f32)]
+        out_shape += [jax.ShapeDtypeStruct((rows, share), bf16)] * (heads - 1)
+    else:
+        out_shape = [jax.ShapeDtypeStruct((3 * rows + nf2 * rows // LANES, LANES), bf16)]
     grads = pl.pallas_call(
-        lambda *refs: gradient_kernel(count, *refs),
-        out_shape=jax.ShapeDtypeStruct((3 * rows + nf2 * rows // LANES, LANES), bf16),
-        in_specs=[VMEM] * (len(recv) + 5),
-        out_specs=VMEM,
+        lambda *refs: gradient_kernel(ctx, count, len(recv), *refs),
+        out_shape=out_shape,
+        in_specs=[VMEM] * len(args),
+        out_specs=[VMEM] * len(out_shape),
         compiler_params=params,
         cost_estimate=cost(10**9, 2 * 1024 * 1024, 10**6),
         name="gradients",
-    )(*recv, own, query, feat, sheet, stats)
+    )(*args)
     if not shared:
         weights = jnp.concatenate([window_weight, value_weight, feature_weight], axis=1)
         weights = lax.all_gather(weights, "tp")
-        return (attended, merge(lax.all_gather(grads, "tp"), weights, rows, dim))
-
-    near, grads = lax.optimization_barrier((near, grads))
-    far = [lax.ppermute(n, "core", swap) for n in near]
-    grads = lax.all_gather(grads, "tp")
+        return (attended, merge(lax.all_gather(grads[0], "tp"), weights, rows, dim))
+
+    def passed_on(parts):
+        return [
+            lax.ppermute(parts[t], "tp", [(z, z ^ t) for z in range(heads)])
+            for t in range(heads - 1, 0, -1)
+        ][::-1]
+
     last = 16
     sums, ends = pl.pallas_call(
-        share_kernel,
+        add_kernel,
         out_shape=[
-            jax.ShapeDtypeStruct((rows - last, 2 * tile), bf16),
-            jax.ShapeDtypeStruct((last, 2 * tile), bf16),
+            jax.ShapeDtypeStruct((rows - last, share), bf16),
+            jax.ShapeDtypeStruct((last, share), bf16),
         ],
-        in_specs=[VMEM] * (2 * heads),
+        in_specs=[VMEM] * heads,
         out_specs=[VMEM] * 2,
-        scratch_shapes=[
-            pltpu.VMEM((rows, 3 * LANES * heads), bf16),
-            pltpu.VMEM((rows, nf2 * heads), bf16),
-        ],
         compiler_params=params,
-        cost_estimate=cost(4 * rows * tile * heads * columns, 4 * heads * height * LANES),
-        name="share",
-    )(grads, packed[0], *near, *far)
-    others = [
-        lax.ppermute(ends, "tp", [(z, z ^ t) for z in range(heads)]) for t in range(1, heads)
-    ]
+        cost_estimate=cost(rows * share * heads, 2 * rows * share * heads),
+        name="add",
+    )(grads[0], *passed_on(grads))
+    others = passed_on([ends] * heads)
     total = pl.pallas_call(
         lay_kernel,
         out_shape=jax.ShapeDtypeStruct((rows, dim), bf16),
@@ -614,17 +582,24 @@
 
 
 def solution(mesh):
-    ctx, tp = mesh.devices.shape
-    split = Mesh(mesh.devices.reshape(ctx // 2, 2, tp), ("chip", "core", "tp"))
+    blocks, tp = mesh.devices.shape
+    bits = blocks.bit_length() - 1
+    assert blocks == 2**bits
+    ctx = tuple(f"half{i}" for i in range(bits - 1)) + ("core",)
+    split = Mesh(mesh.devices.reshape((2,) * bits + (tp,)), (*ctx, "tp"))
     in_specs = (
-        P(CTX, None),
+        P(ctx, None),
         P(None, "tp"),
         P(None, "tp"),
         P(None, "tp"),
-        P(CTX, "tp"),
-        P(CTX, "tp"),
+        P(ctx, "tp"),
+        P(ctx, "tp"),
     )
-    out_specs = (P(CTX, "tp"), P(CTX, None))
+    out_specs = (P(ctx, "tp"), P(ctx, None))
     return jax.shard_map(
-        per_device, mesh=split, in_specs=in_specs, out_specs=out_specs, check_vma=False
+        partial(per_device, ctx),
+        mesh=split,
+        in_specs=in_specs,
+        out_specs=out_specs,
+        check_vma=False,
     )

time: 85 us -> 83.9 us (0.987)
  blocking collectives: 50.5 us -> 30.9 us
  waiting for transfers between devices: 6.91 us -> 26.1 us
    all_gather x2 -> x3, blocking collectives: 30.4 us -> 10.8 us  [per_device(): stats = lax.all_gather(stats, name, tiled=True)]
    ppermute x12 -> x9, waiting for transfers between devices: 6.9 us -> 25.1 us  [the longest x6 18.3 us: passed_on(): lax.ppermute(parts[t], 'tp', [(z, z ^ t) for z in range(heads)])]
    ppermute x3, waiting for transfers between devices: 0.01 us -> 1.05 us  [per_device(): recv[2 * d + 1] = lax.ppermute(recv[2 * d], 'core', swap)]
    ppermute x12 -> x9, starting transfers between devices: 14.2 us -> 14 us  [the longest x6 9.47 us: passed_on(): lax.ppermute(parts[t], 'tp', [(z, z ^ t) for z in range(heads)])]
  transfers between devices with their start and end apart: 16 -> 13, of which waited for: 3 -> 6; matrix products, arithmetic and copies ran while one was open for 0% -> 0% of each run, Pallas kernels for 7% -> 0%
where the time goes in v8:
time: 83.9 us; the launch traced here: 83.7 us
  blocking collectives  30.9 us (37%)
  waiting for transfers between devices  26.1 us (31%)
  starting transfers between devices  14.5 us (17%)
  Pallas kernels  11.5 us (14%)
    all_gather x1, blocking collectives, per_device(): lax.all_gather(sums, 'tp')  20.1 us
    ppermute x6, waiting for transfers between devices, passed_on(): lax.ppermute(parts[t], 'tp', [(z, z ^ t) for z in range(heads)])  18.3 us
    all_gather x3, blocking collectives, per_device(): stats = lax.all_gather(stats, name, tiled=True)  10.8 us
    ppermute x6, starting transfers between devices, passed_on(): lax.ppermute(parts[t], 'tp', [(z, z ^ t) for z in range(heads)])  9.47 us
    ppermute x3, waiting for transfers between devices, per_device(): lax.ppermute(sends[d], ctx[:-1], [(i, i ^ d) for i in range(chips)])  6.77 us
    pallas_call x1, Pallas kernels, per_device(): pl.pallas_call(lambda *refs: gradient_kernel(ctx, count, len(recv), *refs...  4.56 us
    ppermute x3, starting transfers between devices, per_device(): lax.ppermute(sends[d], ctx[:-1], [(i, i ^ d) for i in range(chips)])  4.54 us
    pallas_call x1, Pallas kernels, per_device(): pl.pallas_call(partial(project_kernel, ctx), out_shape=[block] * (chips +...  3.41 us
  transfers between devices with their start and end apart: 13, of which 6 were waited for; matrix products, arithmetic and copies ran while one was open for 0% of the time, Pallas kernels for 0%

profile of v8, /device:TPU:0, one launch (start us, length us, event | category | flops | bytes accessed | tf_op | source)
XLA Modules:
  0.0 83.7 jit_solution(12335708525971322097)
XLA Ops:
  0.6 3.4 %project.1 = (bf16[560,128]{1,0:T(8,128)(2,1)S(1)}, bf16[560,128]{1,0:T(8,128)(2,1)S(1)}, bf16[560,128]{1,0:T(8,128)(2,1)S(1)}, bf16[560,128]{1,0:T(8,128)(2,1)S...) custom-call(bf16[256,2048]{1,0:T(8,128)(2,1)} %tok_hbm.1, ...), custom_call_target="tpu_custom_call" | custom-call | flops 436207616 | bytes 4194304 | tf_op jit(solution)/shard_map/project/pallas_call | solution.py:471
  4.1 3.0 %collective-permute-start.1 = (bf16[560,128]{1,0:T(8,128)(2,1)S(1)}, bf16[560,128]{1,0:T(8,128)(2,1)S(1)}, u32[]{:S(2)}, u32[]{:S(2)}) collective-permute-start(bf16[560,128]{1,0:T(8,128)(2,1)S(1)} %get-tuple-element.23), channel_id=1, source_target_pairs={{0,8},{8,0},{16,24},{24,16},{1,9},{9,1},{17,25},{25,17},{2,10},{10... | collective-permute-start | bytes 430088 | tf_op jit(solution)/shard_map/ppermute | solution.py:498
  7.1 1.5 %collective-permute-start.3 = (bf16[560,128]{1,0:T(8,128)(2,1)S(1)}, bf16[560,128]{1,0:T(8,128)(2,1)S(1)}, u32[]{:S(2)}, u32[]{:S(2)}) collective-permute-start(bf16[560,128]{1,0:T(8,128)(2,1)S(1)} %get-tuple-element.24), channel_id=1, source_target_pairs={{0,16},{8,24},{16,0},{24,8},{1,17},{9,25},{17,1},{25,9},{2,18},{10... | collective-permute-start | bytes 430088 | tf_op jit(solution)/shard_map/ppermute | solution.py:498
  8.6 0.0 collective-permute-start.5
  8.6 0.0 collective-permute-start
  8.6 2.6 %collective-permute-done.1.refs_1_ = bf16[560,128]{1,0:T(8,128)(2,1)S(1)} collective-permute-done((bf16[560,128]{1,0:T(8,128)(2,1)S(1)}, bf16[560,128]{1,0:T(8,128)(2,1)S(1)}, u32[]{:S(2)}, u32[]{:S(2)}) %collective-permute-start.1) | collective-permute-done | bytes 143392 | tf_op jit(solution)/shard_map/ppermute | solution.py:498
  11.2 0.0 collective-permute-start.2
  11.2 4.1 %collective-permute-done.3.refs_3_ = bf16[560,128]{1,0:T(8,128)(2,1)S(1)} collective-permute-done((bf16[560,128]{1,0:T(8,128)(2,1)S(1)}, bf16[560,128]{1,0:T(8,128)(2,1)S(1)}, u32[]{:S(2)}, u32[]{:S(2)}) %collective-permute-start.3) | collective-permute-done | bytes 143392 | tf_op jit(solution)/shard_map/ppermute | solution.py:498
  15.4 0.0 collective-permute-start.4
  15.4 0.0 collective-permute-done.5.refs_5_
  15.4 0.5 collective-permute-start.6
  15.9 0.0 collective-permute-done.refs_0_
  15.9 0.0 collective-permute-done.2.refs_2_
  15.9 0.8 %collective-permute-done.4.refs_4_ = bf16[560,128]{1,0:T(8,128)(2,1)S(1)} collective-permute-done((bf16[560,128]{1,0:T(8,128)(2,1)S(1)}, bf16[560,128]{1,0:T(8,128)(2,1)S(1)}, u32[]{:S(2)}, u32[]{:S(2)}) %collective-permute-start.4) | collective-permute-done | bytes 143392 | tf_op jit(solution)/shard_map/ppermute | solution.py:501
  16.7 0.2 collective-permute-done.6.refs_6_
  16.9 2.4 %query_side.1 = (bf16[256,128]{1,0:T(8,128)(2,1)}, f32[8,256]{1,0:T(8,128)S(1)}, f32[256,128]{1,0:T(8,128)S(1)}) custom-call(bf16[560,128]{1,0:T(8,128)(2,1)S(1)} %collective-permute-done.refs_0_, bf16[560,128]{1,0:T(8,128)(2,1)S(1)} %collective-permute-done.1.refs_1_, bf16[560,128]{1,0:T(8,128)(2,1)S(1)} %collective-permute-done.2.refs_2_, ...), custom_call_target="tpu_custom_call" | custom-call | flops 1000000000 | bytes 2097152 | tf_op jit(solution)/shard_map/query_side/pallas_call | solution.py:506
  19.3 1.8 %all_gather.15 = f32[16,256]{1,0:T(8,128)S(1)} all-gather(f32[8,256]{1,0:T(8,128)S(1)} %get-tuple-element.32), channel_id=1, replica_groups=mesh['half0'=2,'half1'=2,'core'=2,'tp'=4] {'core'}, dimensions={0}, use_global_device_ids=true | all-gather | bytes 24576 | tf_op jit(solution)/shard_map/all_gather | solution.py:526
  21.1 4.4 %all_gather.16 = f32[32,256]{1,0:T(8,128)S(1)} all-gather(f32[16,256]{1,0:T(8,128)S(1)} %all_gather.15), channel_id=1, replica_groups=mesh['half0'=2,'half1'=2,'core'=2,'tp'=4] {'half1'}, dimensions={0}, use_global_device_ids=true | all-gather | bytes 49152 | tf_op jit(solution)/shard_map/all_gather | solution.py:526
  25.5 4.6 %all_gather.17 = f32[64,256]{1,0:T(8,128)S(1)} all-gather(f32[32,256]{1,0:T(8,128)S(1)} %all_gather.16), channel_id=1, replica_groups=mesh['half0'=2,'half1'=2,'core'=2,'tp'=4] {'half0'}, dimensions={0}, use_global_device_ids=true | all-gather | bytes 98304 | tf_op jit(solution)/shard_map/all_gather | solution.py:526
  30.1 4.6 %gradients.1 = (f32[256,512]{1,0:T(8,128)S(1)}, bf16[256,512]{1,0:T(8,128)(2,1)S(1)}, bf16[256,512]{1,0:T(8,128)(2,1)S(1)}, bf16[256,512]{1,0:T(8,128)(2,1)S(1)}) custom-call(bf16[560,128]{1,0:T(8,128)(2,1)S(1)} %collective-permute-done.refs_0_, bf16[560,128]{1,0:T(8,128)(2,1)S(1)} %collective-permute-done.1.refs_1_, ...), custom_call_target="tpu_custom_call" | custom-call | flops 1000000000 | bytes 2097152 | tf_op jit(solution)/shard_map/gradients/pallas_call | solution.py:538
  34.7 1.6 %collective-permute-start.7 = (bf16[256,512]{1,0:T(8,128)(2,1)S(1)}, bf16[256,512]{1,0:T(8,128)(2,1)S(1)}, u32[]{:S(2)}, u32[]{:S(2)}) collective-permute-start(bf16[256,512]{1,0:T(8,128)(2,1)S(1)} %get-tuple-element.37), channel_id=1, source_target_pairs={{0,1},{1,0},{2,3},{3,2},{4,5},{5,4},{6,7},{7,6},{8,9},{9,8},{10,11... | collective-permute-start | bytes 786440 | tf_op jit(solution)/shard_map/ppermute | solution.py:554
  36.3 2.6 %collective-permute-start.8 = (bf16[256,512]{1,0:T(8,128)(2,1)S(1)}, bf16[256,512]{1,0:T(8,128)(2,1)S(1)}, u32[]{:S(2)}, u32[]{:S(2)}) collective-permute-start(bf16[256,512]{1,0:T(8,128)(2,1)S(1)} %get-tuple-element.38), channel_id=1, source_target_pairs={{0,2},{1,3},{2,0},{3,1},{4,6},{5,7},{6,4},{7,5},{8,10},{9,11},{10,... | collective-permute-start | bytes 786440 | tf_op jit(solution)/shard_map/ppermute | solution.py:554
  38.9 0.2 collective-permute-start.9
  39.1 5.6 %collective-permute-done.7.rest_0_ = bf16[256,512]{1,0:T(8,128)(2,1)S(1)} collective-permute-done((bf16[256,512]{1,0:T(8,128)(2,1)S(1)}, bf16[256,512]{1,0:T(8,128)(2,1)S(1)}, u32[]{:S(2)}, u32[]{:S(2)}) %collective-permute-start.7) | collective-permute-done | bytes 262176 | tf_op jit(solution)/shard_map/ppermute | solution.py:554
  44.7 12.7 %collective-permute-done.8.rest_1_ = bf16[256,512]{1,0:T(8,128)(2,1)S(1)} collective-permute-done((bf16[256,512]{1,0:T(8,128)(2,1)S(1)}, bf16[256,512]{1,0:T(8,128)(2,1)S(1)}, u32[]{:S(2)}, u32[]{:S(2)}) %collective-permute-start.8) | collective-permute-done | bytes 262176 | tf_op jit(solution)/shard_map/ppermute | solution.py:554
  57.4 0.0 collective-permute-done.9.rest_2_
  57.4 0.1 add.1
  57.6 2.0 %collective-permute-start.12 = (bf16[16,512]{1,0:T(8,128)(2,1)S(1)}, bf16[16,512]{1,0:T(8,128)(2,1)S(1)}, u32[]{:S(2)}, u32[]{:S(2)}) collective-permute-start(bf16[16,512]{1,0:T(8,128)(2,1)S(1)} %get-tuple-element.41.own_ref), channel_id=1, source_target_pairs={{0,3},{1,2},{2,1},{3,0},{4,7},{5,6},{6,5},{7,4},{8,11},{9,10},{10,... | collective-permute-start | bytes 49160 | tf_op jit(solution)/shard_map/ppermute | solution.py:554
  59.6 2.9 %collective-permute-start.11 = (bf16[16,512]{1,0:T(8,128)(2,1)S(1)}, bf16[16,512]{1,0:T(8,128)(2,1)S(1)}, u32[]{:S(2)}, u32[]{:S(2)}) collective-permute-start(bf16[16,512]{1,0:T(8,128)(2,1)S(1)} %get-tuple-element.41.own_ref), channel_id=1, source_target_pairs={{0,2},{1,3},{2,0},{3,1},{4,6},{5,7},{6,4},{7,5},{8,10},{9,11},{10,... | collective-permute-start | bytes 49160 | tf_op jit(solution)/shard_map/ppermute | solution.py:554
  62.5 0.1 collective-permute-start.10
  62.6 20.1 %all-gather = bf16[960,512]{1,0:T(8,128)(2,1)S(1)} all-gather(bf16[240,512]{1,0:T(8,128)(2,1)S(1)} %get-tuple-element.40), channel_id=2, replica_groups=mesh['half0'=2,'half1'=2,'core'=2,'tp'=4] {'tp'}, dimensions={0}, use_global_device_ids=true | all-gather | bytes 1228800 | tf_op jit(solution)/shard_map/all_gather | solution.py:580
  82.7 0.0 collective-permute-done.12.rest_2_
  82.7 0.0 collective-permute-done.11.rest_1_
  82.7 0.0 collective-permute-done.10.rest_0_
  82.7 1.0 %lay.1 = bf16[256,2048]{1,0:T(8,128)(2,1)} custom-call(bf16[4,240,512]{2,1,0:T(8,128)(2,1)S(1)} %bitcast.4, bf16[16,512]{1,0:T(8,128)(2,1)S(1)} %get-tuple-element.41.own_ref, bf16[16,512]{1,0:T(8,128)(2,1)S(1)} %collective-permute-done.10.rest_0_, bf16[16,512]{1,0:T(8,128)(2,1)S(1)} %collective-permute-done.11.rest_1_, ...), custom_call_target="tpu_custom_call" | custom-call | flops 1 | bytes 2097152 | tf_op jit(solution)/shard_map/lay/pallas_call | solution.py:572
Async XLA Ops:
  4.1 7.2 %collective-permute-start.1 = (bf16[560,128]{1,0:T(8,128)(2,1)S(1)}, bf16[560,128]{1,0:T(8,128)(2,1)S(1)}, u32[]{:S(2)}, u32[]{:S(2)}) collective-permute-start(bf16[560,128]{1,0:T(8,128)(2,1)S(1)} %get-tuple-element.23), channel_id=1, source_target_pairs={{0,8},{8,0},{16,24},{24,16},{1,9},{9,1},{17,25},{25,17},{2,10},{10... | collective-permute-start | bytes 430088 | tf_op jit(solution)/shard_map/ppermute | solution.py:498
  7.1 8.3 %collective-permute-start.3 = (bf16[560,128]{1,0:T(8,128)(2,1)S(1)}, bf16[560,128]{1,0:T(8,128)(2,1)S(1)}, u32[]{:S(2)}, u32[]{:S(2)}) collective-permute-start(bf16[560,128]{1,0:T(8,128)(2,1)S(1)} %get-tuple-element.24), channel_id=1, source_target_pairs={{0,16},{8,24},{16,0},{24,8},{1,17},{9,25},{17,1},{25,9},{2,18},{10... | collective-permute-start | bytes 430088 | tf_op jit(solution)/shard_map/ppermute | solution.py:498
  8.6 6.8 %collective-permute-start.5 = (bf16[560,128]{1,0:T(8,128)(2,1)S(1)}, bf16[560,128]{1,0:T(8,128)(2,1)S(1)}, u32[]{:S(2)}, u32[]{:S(2)}) collective-permute-start(bf16[560,128]{1,0:T(8,128)(2,1)S(1)} %get-tuple-element.25), channel_id=1, source_target_pairs={{0,24},{8,16},{16,8},{24,0},{1,25},{9,17},{17,9},{25,1},{2,26},{10... | collective-permute-start | bytes 430088 | tf_op jit(solution)/shard_map/ppermute | solution.py:498
  8.6 7.3 %collective-permute-start = (bf16[560,128]{1,0:T(8,128)(2,1)S(1)}, bf16[560,128]{1,0:T(8,128)(2,1)S(1)}, u32[]{:S(2)}, u32[]{:S(2)}) collective-permute-start(bf16[560,128]{1,0:T(8,128)(2,1)S(1)} %get-tuple-element.22), channel_id=1, source_target_pairs={{0,4},{4,0},{1,5},{5,1},{2,6},{6,2},{3,7},{7,3},{8,12},{12,8},{9,1... | collective-permute-start | bytes 430088 | tf_op jit(solution)/shard_map/ppermute | solution.py:499
  11.2 4.7 %collective-permute-start.2 = (bf16[560,128]{1,0:T(8,128)(2,1)S(1)}, bf16[560,128]{1,0:T(8,128)(2,1)S(1)}, u32[]{:S(2)}, u32[]{:S(2)}) collective-permute-start(bf16[560,128]{1,0:T(8,128)(2,1)S(1)} %collective-permute-done.1.refs_1_), channel_id=1, source_target_pairs={{0,4},{4,0},{1,5},{5,1},{2,6},{6,2},{3,7},{7,3},{8,12},{12,8},{9,1... | collective-permute-start | bytes 430088 | tf_op jit(solution)/shard_map/ppermute | solution.py:501
  15.4 1.4 %collective-permute-start.4 = (bf16[560,128]{1,0:T(8,128)(2,1)S(1)}, bf16[560,128]{1,0:T(8,128)(2,1)S(1)}, u32[]{:S(2)}, u32[]{:S(2)}) collective-permute-start(bf16[560,128]{1,0:T(8,128)(2,1)S(1)} %collective-permute-done.3.refs_3_), channel_id=1, source_target_pairs={{0,4},{4,0},{1,5},{5,1},{2,6},{6,2},{3,7},{7,3},{8,12},{12,8},{9,1... | collective-permute-start | bytes 430088 | tf_op jit(solution)/shard_map/ppermute | solution.py:501
  15.4 1.6 %collective-permute-start.6 = (bf16[560,128]{1,0:T(8,128)(2,1)S(1)}, bf16[560,128]{1,0:T(8,128)(2,1)S(1)}, u32[]{:S(2)}, u32[]{:S(2)}) collective-permute-start(bf16[560,128]{1,0:T(8,128)(2,1)S(1)} %collective-permute-done.5.refs_5_), channel_id=1, source_target_pairs={{0,4},{4,0},{1,5},{5,1},{2,6},{6,2},{3,7},{7,3},{8,12},{12,8},{9,1... | collective-permute-start | bytes 430088 | tf_op jit(solution)/shard_map/ppermute | solution.py:501
  34.7 10.0 %collective-permute-start.7 = (bf16[256,512]{1,0:T(8,128)(2,1)S(1)}, bf16[256,512]{1,0:T(8,128)(2,1)S(1)}, u32[]{:S(2)}, u32[]{:S(2)}) collective-permute-start(bf16[256,512]{1,0:T(8,128)(2,1)S(1)} %get-tuple-element.37), channel_id=1, source_target_pairs={{0,1},{1,0},{2,3},{3,2},{4,5},{5,4},{6,7},{7,6},{8,9},{9,8},{10,11... | collective-permute-start | bytes 786440 | tf_op jit(solution)/shard_map/ppermute | solution.py:554
  36.3 21.1 %collective-permute-start.8 = (bf16[256,512]{1,0:T(8,128)(2,1)S(1)}, bf16[256,512]{1,0:T(8,128)(2,1)S(1)}, u32[]{:S(2)}, u32[]{:S(2)}) collective-permute-start(bf16[256,512]{1,0:T(8,128)(2,1)S(1)} %get-tuple-element.38), channel_id=1, source_target_pairs={{0,2},{1,3},{2,0},{3,1},{4,6},{5,7},{6,4},{7,5},{8,10},{9,11},{10,... | collective-permute-start | bytes 786440 | tf_op jit(solution)/shard_map/ppermute | solution.py:554
  38.9 18.5 %collective-permute-start.9 = (bf16[256,512]{1,0:T(8,128)(2,1)S(1)}, bf16[256,512]{1,0:T(8,128)(2,1)S(1)}, u32[]{:S(2)}, u32[]{:S(2)}) collective-permute-start(bf16[256,512]{1,0:T(8,128)(2,1)S(1)} %get-tuple-element.39), channel_id=1, source_target_pairs={{0,3},{1,2},{2,1},{3,0},{4,7},{5,6},{6,5},{7,4},{8,11},{9,10},{10,... | collective-permute-start | bytes 786440 | tf_op jit(solution)/shard_map/ppermute | solution.py:554
  57.6 25.1 %collective-permute-start.12 = (bf16[16,512]{1,0:T(8,128)(2,1)S(1)}, bf16[16,512]{1,0:T(8,128)(2,1)S(1)}, u32[]{:S(2)}, u32[]{:S(2)}) collective-permute-start(bf16[16,512]{1,0:T(8,128)(2,1)S(1)} %get-tuple-element.41.own_ref), channel_id=1, source_target_pairs={{0,3},{1,2},{2,1},{3,0},{4,7},{5,6},{6,5},{7,4},{8,11},{9,10},{10,... | collective-permute-start | bytes 49160 | tf_op jit(solution)/shard_map/ppermute | solution.py:554
  59.6 23.1 %collective-permute-start.11 = (bf16[16,512]{1,0:T(8,128)(2,1)S(1)}, bf16[16,512]{1,0:T(8,128)(2,1)S(1)}, u32[]{:S(2)}, u32[]{:S(2)}) collective-permute-start(bf16[16,512]{1,0:T(8,128)(2,1)S(1)} %get-tuple-element.41.own_ref), channel_id=1, source_target_pairs={{0,2},{1,3},{2,0},{3,1},{4,6},{5,7},{6,4},{7,5},{8,10},{9,11},{10,... | collective-permute-start | bytes 49160 | tf_op jit(solution)/shard_map/ppermute | solution.py:554
  62.5 20.2 %collective-permute-start.10 = (bf16[16,512]{1,0:T(8,128)(2,1)S(1)}, bf16[16,512]{1,0:T(8,128)(2,1)S(1)}, u32[]{:S(2)}, u32[]{:S(2)}) collective-permute-start(bf16[16,512]{1,0:T(8,128)(2,1)S(1)} %get-tuple-element.41.own_ref), channel_id=1, source_target_pairs={{0,1},{1,0},{2,3},{3,2},{4,5},{5,4},{6,7},{7,6},{8,9},{9,8},{10,11... | collective-permute-start | bytes 49160 | tf_op jit(solution)/shard_map/ppermute | solution.py:554

commit v9 on v8

--- a/solution.py
+++ b/solution.py
@@ -85,11 +85,11 @@
         pltpu.make_async_copy(ld_hbm, ld_ref, small.at[0]),
         pltpu.make_async_copy(do_hbm, do_ref, small.at[1]),
     ]
-    for copy in copies[0] + others:
+    for copy in others:
         copy.start()
-    for group in copies[1:]:
-        for copy in group:
-            copy.start()
+    for group in copies:
+        for at, copy in enumerate(group):
+            copy.start(priority=min(at, 1))
     for copy in others:
         copy.wait()
     at_row, at_col = iotas(rows)
@@ -259,9 +259,10 @@
     stat_ref[...] = jnp.transpose(sheet)[0:8, :]
 
 
-def gradient_kernel(ctx, count, recvs, *rest):
-    recvs = rest[:recvs]
-    own_ref, query_ref, feat_ref, sheet_ref, stat_ref, *rest = rest[len(recvs) :]
+def gradient_kernel(ctx, count, recvs, stats, *rest):
+    recvs, rest = rest[:recvs], rest[recvs:]
+    stats, rest = rest[:stats], rest[stats:]
+    own_ref, query_ref, feat_ref, sheet_ref, *rest, total_ref = rest
 
     def recv(d):
         return recvs[d - 1] if len(recvs) > 1 else recvs[0].at[d - 1]
@@ -280,9 +281,22 @@
     q, k = feat_ref[:, :nf], feat_ref[:, nf:]
     lse_c, dw_c = sheet_ref[:, 0:1], sheet_ref[:, 1:2]
     rden_c, dl_c, cum_c = sheet_ref[:, 2:3], sheet_ref[:, 3:4], sheet_ref[:, 4:5]
-    mine_ref = stat_ref.at[me]
+    def stat(d):
+        if len(stats) == 1:
+            return stats[0].at[pl.ds(pl.multiple_of(8 * d, 8), 8)]
+        at = d.bit_length()
+        return stats[at].at[pl.ds(8 * (d - (1 << at >> 1)), 8)]
+
+    mine_ref = stat(0)
     own_cum = mine_ref[4:5, :]
-    totals = jnp.concatenate([stat_ref[j, 4:5, rows - 1 : rows] for j in range(count)], axis=0)
+    total_ref[pl.ds(me, 1), :] = own_cum[:, rows - LANES :]
+
+    def place(d, carry):
+        total_ref[pl.ds(partner(me, d, count), 1), :] = stat(d)[4:5, rows - LANES :]
+        return carry
+
+    over_partners(count, place, 0)
+    totals = total_ref[:, LANES - 1 :]
     growth_c = jnp.exp(cum_c) * rden_c
     tail_c = jnp.exp(own_cum[:, rows - 1 : rows] - cum_c)
 
@@ -323,7 +337,7 @@
         other_w = view[0:rows, :]
         other_v = view[rows : 2 * rows, :]
         other_f = wide(view, feat_at, nf)
-        st = stat_ref[j]
+        st = stat(d)
         zero = jnp.zeros((1, rows), f32)
         cum = st[4:5, :]
         gap = between(totals, jnp.minimum(me, j), jnp.maximum(me, j))
@@ -361,27 +375,42 @@
         put_wide(grad_ref, 3 * rows, dft)
         return
 
-    ww_ref, vw_ref, fw_ref, part_ref, *sends = rest
+    ww_ref, vw_ref, fw_ref, *parts = rest
     head = lax.axis_index("tp")
-    share = part_ref.shape[1]
+    half, share = parts[0].shape
     dw = jnp.concatenate([dwq, dwk], axis=1)
     padded = jnp.concatenate([dft.astype(f32), jnp.zeros((LANES - 2 * nf, rows), f32)], axis=0)
     df = jnp.transpose(padded)[:, : 2 * nf].astype(bf16)
-    for t, ref in enumerate([part_ref, *sends]):
+    for t in range(len(parts) // 2):
         part = pl.ds(pl.multiple_of(jnp.bitwise_xor(head, t) * share, share), share)
         product = nt(dw, ww_ref[part, :]) + nt(dv, vw_ref[part, :]) + nn(df, fw_ref[:, part])
-        ref[...] = product.astype(ref.dtype)
+        for h in range(2):
+            ref = parts[2 * t + h]
+            ref[...] = product[h * half : (h + 1) * half].astype(ref.dtype)
 
 
 def add_kernel(part_ref, *rest):
-    *others, most_ref, last_ref = rest
+    *others, out_ref = rest
     total = part_ref[...]
     for ref in others:
         total += ref[...].astype(f32)
-    most = most_ref.shape[0]
-    total = total.astype(bf16)
-    most_ref[...] = total[:most]
-    last_ref[...] = total[most:]
+    out_ref[...] = total.astype(bf16)
+
+
+def lay_kernel(half, sums_ref, *rest):
+    out_ref, sems = rest[-2:]
+    shares, rows, width = sums_ref.shape
+    at = pl.ds(half * rows, rows)
+    copies = [
+        pltpu.make_async_copy(
+            sums_ref.at[z], out_ref.at[at, pl.ds(z * width, width)], sems.at[z]
+        )
+        for z in range(shares)
+    ]
+    for copy in copies:
+        copy.start()
+    for copy in copies:
+        copy.wait()
 
 
 def gather_rows(grad_ref, order, cat_ref, feat_ref):
@@ -395,17 +424,6 @@
     feat_ref[...] = jnp.transpose(dft.astype(f32)).astype(bf16)
 
 
-def lay_kernel(most_ref, own_ref, *rest):
-    *lasts, out_ref = rest
-    shares, most, width = most_ref.shape
-    head = lax.axis_index("tp")
-    for z in range(shares):
-        out_ref[0:most, z * width : (z + 1) * width] = most_ref[z]
-    for t, ref in enumerate([own_ref, *lasts]):
-        at = pl.multiple_of(jnp.bitwise_xor(head, t) * width, width)
-        out_ref[most:, pl.ds(at, width)] = ref[...]
-
-
 def merge_kernel(grad_ref, weight_ref, out_ref, cat_ref, feat_ref):
     heads = grad_ref.shape[0]
     tile = out_ref.shape[1]
@@ -424,6 +442,7 @@
 
 VMEM = pl.BlockSpec(memory_space=pltpu.VMEM)
 HBM = pl.BlockSpec(memory_space=pltpu.HBM)
+ANY = pl.BlockSpec(memory_space=pl.ANY)
 params = pltpu.CompilerParams(vmem_limit_bytes=32 * 1024 * 1024)
 
 
@@ -521,25 +540,28 @@
         cost_estimate=cost(10**9, 2 * 1024 * 1024, 10**6),
         name="query_side",
     )(*recv, own, query, feat, cum)
-    stats = stat
+    stats = [stat]
     for name in reversed(ctx):
-        stats = lax.all_gather(stats, name, tiled=True)
-    stats = stats.reshape(count, -1, rows)
+        held = stats[0] if len(stats) == 1 else jnp.concatenate(stats, axis=0)
+        stats.append(lax.ppermute(held, name, swap))
+    if count > 8:
+        stats = [jnp.concatenate(stats, axis=0)]
 
     share = dim // heads
     shared = heads & (heads - 1) == 0 and share % LANES == 0
-    args = [*recv, own, query, feat, sheet, stats]
+    args = [*recv, *stats, own, query, feat, sheet]
     if shared:
         args += [ww, vw, fw]
-        out_shape = [jax.ShapeDtypeStruct((rows, share), f32)]
-        out_shape += [jax.ShapeDtypeStruct((rows, share), bf16)] * (heads - 1)
+        out_shape = [jax.ShapeDtypeStruct((rows // 2, share), f32)] * 2
+        out_shape += [jax.ShapeDtypeStruct((rows // 2, share), bf16)] * (2 * heads - 2)
     else:
         out_shape = [jax.ShapeDtypeStruct((3 * rows + nf2 * rows // LANES, LANES), bf16)]
     grads = pl.pallas_call(
-        lambda *refs: gradient_kernel(ctx, count, len(recv), *refs),
+        lambda *refs: gradient_kernel(ctx, count, len(recv), len(stats), *refs),
         out_shape=out_shape,
         in_specs=[VMEM] * len(args),
         out_specs=[VMEM] * len(out_shape),
+        scratch_shapes=[pltpu.VMEM((count, LANES), f32)],
         compiler_params=params,
         cost_estimate=cost(10**9, 2 * 1024 * 1024, 10**6),
         name="gradients",
@@ -549,36 +571,37 @@
         weights = lax.all_gather(weights, "tp")
         return (attended, merge(lax.all_gather(grads[0], "tp"), weights, rows, dim))
 
-    def passed_on(parts):
-        return [
-            lax.ppermute(parts[t], "tp", [(z, z ^ t) for z in range(heads)])
+    def sum_of(half):
+        others = [
+            lax.ppermute(grads[2 * t + half], "tp", [(z, z ^ t) for z in range(heads)])
             for t in range(heads - 1, 0, -1)
-        ][::-1]
-
-    last = 16
-    sums, ends = pl.pallas_call(
-        add_kernel,
-        out_shape=[
-            jax.ShapeDtypeStruct((rows - last, share), bf16),
-            jax.ShapeDtypeStruct((last, share), bf16),
-        ],
-        in_specs=[VMEM] * heads,
-        out_specs=[VMEM] * 2,
-        compiler_params=params,
-        cost_estimate=cost(rows * share * heads, 2 * rows * share * heads),
-        name="add",
-    )(grads[0], *passed_on(grads))
-    others = passed_on([ends] * heads)
-    total = pl.pallas_call(
-        lay_kernel,
-        out_shape=jax.ShapeDtypeStruct((rows, dim), bf16),
-        in_specs=[VMEM] * (heads + 1),
-        out_specs=VMEM,
-        compiler_params=params,
-        cost_estimate=cost(1, 4 * rows * dim),
-        name="lay",
-    )(lax.all_gather(sums, "tp"), ends, *others)
-    return (attended, total)
+        ]
+        return pl.pallas_call(
+            add_kernel,
+            out_shape=jax.ShapeDtypeStruct((rows // 2, share), bf16),
+            in_specs=[VMEM] * heads,
+            out_specs=VMEM,
+            compiler_params=params,
+            cost_estimate=cost(rows * share * heads, 2 * rows * share * heads),
+            name="add",
+        )(grads[half], *others)
+
+    def lay(half, sums, before):
+        return pl.pallas_call(
+            partial(lay_kernel, half),
+            out_shape=jax.ShapeDtypeStruct((rows, dim), bf16),
+            in_specs=[VMEM] + [ANY] * len(before),
+            out_specs=ANY,
+            scratch_shapes=[pltpu.SemaphoreType.DMA((heads,))],
+            input_output_aliases={1: 0} if before else {},
+            compiler_params=params,
+            cost_estimate=cost(1, 2 * rows * dim),
+            name="lay",
+        )(sums, *before)
+
+    halves = [sum_of(half) for half in range(2)]
+    first = lay(0, lax.all_gather(halves[0], "tp"), [])
+    return (attended, lay(1, lax.all_gather(halves[1], "tp"), [first]))
 
 
 def solution(mesh):

time: 83.9 us -> 85.5 us (1.019)
  starting transfers between devices: 14.5 us -> 23 us
  waiting for transfers between devices: 26.1 us -> 18.2 us
    ppermute x6 -> x9, starting transfers between devices: 9.47 us -> 18 us  [the longest x6 15.1 us: sum_of(): lax.ppermute(grads[2 * t + half], 'tp', [(z, z ^ t) for z in range(heads)])]
    ppermute x6 -> x9, waiting for transfers between devices: 18.3 us -> 10.4 us  [the longest x3 5.98 us: per_device(): stats.append(lax.ppermute(held, name, swap))]
    all_gather x4 -> x2, blocking collectives: 30.9 us -> 31.7 us  [the longest x1 16.2 us: per_device(): first = lay(0, lax.all_gather(halves[0], 'tp'), [])]
    pallas_call x3 -> x5, Pallas kernels: 5.74 us -> 6.33 us  [the longest x1 4.55 us: per_device(): pl.pallas_call(lambda *refs: gradient_kernel(ctx, count, len(recv), len(s...]
  transfers between devices with their start and end apart: 13 -> 16, of which waited for: 6 -> 8; matrix products, arithmetic and copies ran while one was open for 0% -> 0% of each run, Pallas kernels for 0% -> 0%
where the time goes in v9:
time: 85.5 us; the launch traced here: 85.4 us
  blocking collectives  31.7 us (37%)
  starting transfers between devices  23 us (27%)
  waiting for transfers between devices  18.2 us (21%)
  Pallas kernels  11.7 us (14%)
    all_gather x1, blocking collectives, per_device(): first = lay(0, lax.all_gather(halves[0], 'tp'), [])  16.2 us
    all_gather x1, blocking collectives, per_device(): return (attended, lay(1, lax.all_gather(halves[1], 'tp'), [first]))  15.5 us
    ppermute x6, starting transfers between devices, sum_of(): lax.ppermute(grads[2 * t + half], 'tp', [(z, z ^ t) for z in range(heads)])  15.1 us
    ppermute x3, waiting for transfers between devices, per_device(): lax.ppermute(sends[d], ctx[:-1], [(i, i ^ d) for i in range(chips)])  6.77 us
    ppermute x3, waiting for transfers between devices, per_device(): stats.append(lax.ppermute(held, name, swap))  5.98 us
    pallas_call x1, Pallas kernels, per_device(): pl.pallas_call(lambda *refs: gradient_kernel(ctx, count, len(recv), len(s...  4.55 us
    ppermute x3, starting transfers between devices, per_device(): lax.ppermute(sends[d], ctx[:-1], [(i, i ^ d) for i in range(chips)])  4.54 us
    ppermute x6, waiting for transfers between devices, sum_of(): lax.ppermute(grads[2 * t + half], 'tp', [(z, z ^ t) for z in range(heads)])  4.42 us
  transfers between devices with their start and end apart: 16, of which 8 were waited for; matrix products, arithmetic and copies ran while one was open for 0% of the time, Pallas kernels for 0%

profile of v9, /device:TPU:0, one launch (start us, length us, event | category | flops | bytes accessed | tf_op | source)
XLA Modules:
  0.0 85.4 jit_solution(9151579692451241191)
XLA Ops:
  0.6 3.0 %project.1 = (bf16[560,128]{1,0:T(8,128)(2,1)S(1)}, bf16[560,128]{1,0:T(8,128)(2,1)S(1)}, bf16[560,128]{1,0:T(8,128)(2,1)S(1)}, bf16[560,128]{1,0:T(8,128)(2,1)S...) custom-call(bf16[256,2048]{1,0:T(8,128)(2,1)} %tok_hbm.1, ...), custom_call_target="tpu_custom_call" | custom-call | flops 436207616 | bytes 4194304 | tf_op jit(solution)/shard_map/project/pallas_call | solution.py:490
  3.7 3.0 %collective-permute-start.1 = (bf16[560,128]{1,0:T(8,128)(2,1)S(1)}, bf16[560,128]{1,0:T(8,128)(2,1)S(1)}, u32[]{:S(2)}, u32[]{:S(2)}) collective-permute-start(bf16[560,128]{1,0:T(8,128)(2,1)S(1)} %get-tuple-element.25), channel_id=1, source_target_pairs={{0,8},{8,0},{16,24},{24,16},{1,9},{9,1},{17,25},{25,17},{2,10},{10... | collective-permute-start | bytes 430088 | tf_op jit(solution)/shard_map/ppermute | solution.py:517
  6.7 1.5 %collective-permute-start.3 = (bf16[560,128]{1,0:T(8,128)(2,1)S(1)}, bf16[560,128]{1,0:T(8,128)(2,1)S(1)}, u32[]{:S(2)}, u32[]{:S(2)}) collective-permute-start(bf16[560,128]{1,0:T(8,128)(2,1)S(1)} %get-tuple-element.26), channel_id=1, source_target_pairs={{0,16},{8,24},{16,0},{24,8},{1,17},{9,25},{17,1},{25,9},{2,18},{10... | collective-permute-start | bytes 430088 | tf_op jit(solution)/shard_map/ppermute | solution.py:517
  8.2 0.0 collective-permute-start.5
  8.2 0.0 collective-permute-start
  8.2 2.6 %collective-permute-done.1.refs_1_ = bf16[560,128]{1,0:T(8,128)(2,1)S(1)} collective-permute-done((bf16[560,128]{1,0:T(8,128)(2,1)S(1)}, bf16[560,128]{1,0:T(8,128)(2,1)S(1)}, u32[]{:S(2)}, u32[]{:S(2)}) %collective-permute-start.1) | collective-permute-done | bytes 143392 | tf_op jit(solution)/shard_map/ppermute | solution.py:517
  10.8 0.0 collective-permute-start.2
  10.8 4.2 %collective-permute-done.3.refs_3_ = bf16[560,128]{1,0:T(8,128)(2,1)S(1)} collective-permute-done((bf16[560,128]{1,0:T(8,128)(2,1)S(1)}, bf16[560,128]{1,0:T(8,128)(2,1)S(1)}, u32[]{:S(2)}, u32[]{:S(2)}) %collective-permute-start.3) | collective-permute-done | bytes 143392 | tf_op jit(solution)/shard_map/ppermute | solution.py:517
  15.0 0.0 collective-permute-start.4
  15.0 0.0 collective-permute-done.5.refs_5_
  15.0 0.5 collective-permute-start.6
  15.5 0.0 collective-permute-done.refs_0_
  15.5 0.0 collective-permute-done.2.refs_2_
  15.5 0.8 collective-permute-done.4.refs_4_
  16.3 0.2 collective-permute-done.6.refs_6_
  16.6 2.4 %query_side.1 = (bf16[256,128]{1,0:T(8,128)(2,1)}, f32[8,256]{1,0:T(8,128)S(1)}, f32[256,128]{1,0:T(8,128)S(1)}) custom-call(bf16[560,128]{1,0:T(8,128)(2,1)S(1)} %collective-permute-done.refs_0_, bf16[560,128]{1,0:T(8,128)(2,1)S(1)} %collective-permute-done.1.refs_1_, bf16[560,128]{1,0:T(8,128)(2,1)S(1)} %collective-permute-done.2.refs_2_, ...), custom_call_target="tpu_custom_call" | custom-call | flops 1000000000 | bytes 2097152 | tf_op jit(solution)/shard_map/query_side/pallas_call | solution.py:525
  18.9 0.3 collective-permute-start.7
  19.2 0.9 %collective-permute-done.7.refs_8_ = f32[8,256]{1,0:T(8,128)S(1)} collective-permute-done((f32[8,256]{1,0:T(8,128)S(1)}, f32[8,256]{1,0:T(8,128)S(1)}, u32[]{:S(2)}, u32[]{:S(2)}) %collective-permute-start.7) | collective-permute-done | bytes 8224 | tf_op jit(solution)/shard_map/ppermute | solution.py:546
  20.1 1.0 %collective-permute-start.8 = (f32[16,256]{1,0:T(8,128)S(1)}, f32[16,256]{1,0:T(8,128)S(1)}, u32[]{:S(2)}, u32[]{:S(2)}) collective-permute-start(f32[16,256]{1,0:T(8,128)S(1)} %pad_maximum_fusion.1), channel_id=1, source_target_pairs={{0,8},{8,0},{1,9},{9,1},{2,10},{10,2},{3,11},{11,3},{4,12},{12,4},... | collective-permute-start | bytes 49160 | tf_op jit(solution)/shard_map/ppermute | solution.py:546
  21.1 2.7 %collective-permute-done.8.refs_9_ = f32[16,256]{1,0:T(8,128)S(1)} collective-permute-done((f32[16,256]{1,0:T(8,128)S(1)}, f32[16,256]{1,0:T(8,128)S(1)}, u32[]{:S(2)}, u32[]{:S(2)}) %collective-permute-start.8) | collective-permute-done | bytes 16416 | tf_op jit(solution)/shard_map/ppermute | solution.py:546
  23.9 1.5 %collective-permute-start.9 = (f32[32,256]{1,0:T(8,128)S(1)}, f32[32,256]{1,0:T(8,128)S(1)}, u32[]{:S(2)}, u32[]{:S(2)}) collective-permute-start(f32[32,256]{1,0:T(8,128)S(1)} %pad_maximum_fusion), channel_id=1, source_target_pairs={{0,16},{16,0},{1,17},{17,1},{2,18},{18,2},{3,19},{19,3},{4,20},{20... | collective-permute-start | bytes 98312 | tf_op jit(solution)/shard_map/ppermute | solution.py:546
  25.4 2.4 %collective-permute-done.9.refs_10_ = f32[32,256]{1,0:T(8,128)S(1)} collective-permute-done((f32[32,256]{1,0:T(8,128)S(1)}, f32[32,256]{1,0:T(8,128)S(1)}, u32[]{:S(2)}, u32[]{:S(2)}) %collective-permute-start.9) | collective-permute-done | bytes 32800 | tf_op jit(solution)/shard_map/ppermute | solution.py:546
  27.8 4.6 %gradients.1 = (f32[128,512]{1,0:T(8,128)S(1)}, f32[128,512]{1,0:T(8,128)S(1)}, bf16[128,512]{1,0:T(8,128)(2,1)S(1)}, bf16[128,512]{1,0:T(8,128)(2,1)S(1)}, bf16...) custom-call(bf16[560,128]{1,0:T(8,128)(2,1)S(1)} %collective-permute, ...), custom_call_target="tpu_custom_call" | custom-call | flops 1000000000 | bytes 2097152 | tf_op jit(solution)/shard_map/gradients/pallas_call | solution.py:559
  32.3 3.7 %collective-permute-start.13 = (bf16[128,512]{1,0:T(8,128)(2,1)S(1)}, bf16[128,512]{1,0:T(8,128)(2,1)S(1)}, u32[]{:S(2)}, u32[]{:S(2)}) collective-permute-start(bf16[128,512]{1,0:T(8,128)(2,1)S(1)} %get-tuple-element.43), channel_id=1, source_target_pairs={{0,3},{1,2},{2,1},{3,0},{4,7},{5,6},{6,5},{7,4},{8,11},{9,10},{10,... | collective-permute-start | bytes 393224 | tf_op jit(solution)/shard_map/ppermute | solution.py:576
  36.0 0.0 collective-permute-start.14
  36.0 0.8 collective-permute-start.15
  36.8 3.6 %collective-permute-start.10 = (bf16[128,512]{1,0:T(8,128)(2,1)S(1)}, bf16[128,512]{1,0:T(8,128)(2,1)S(1)}, u32[]{:S(2)}, u32[]{:S(2)}) collective-permute-start(bf16[128,512]{1,0:T(8,128)(2,1)S(1)} %get-tuple-element.39), channel_id=1, source_target_pairs={{0,3},{1,2},{2,1},{3,0},{4,7},{5,6},{6,5},{7,4},{8,11},{9,10},{10,... | collective-permute-start | bytes 393224 | tf_op jit(solution)/shard_map/ppermute | solution.py:576
  40.4 0.0 collective-permute-start.11
  40.4 0.0 collective-permute-done.13.rest_0_
  40.4 7.1 %collective-permute-start.12 = (bf16[128,512]{1,0:T(8,128)(2,1)S(1)}, bf16[128,512]{1,0:T(8,128)(2,1)S(1)}, u32[]{:S(2)}, u32[]{:S(2)}) collective-permute-start(bf16[128,512]{1,0:T(8,128)(2,1)S(1)} %get-tuple-element.41), channel_id=1, source_target_pairs={{0,1},{1,0},{2,3},{3,2},{4,5},{5,4},{6,7},{7,6},{8,9},{9,8},{10,11... | collective-permute-start | bytes 393224 | tf_op jit(solution)/shard_map/ppermute | solution.py:576
  47.5 4.4 %collective-permute-done.14.rest_1_ = bf16[128,512]{1,0:T(8,128)(2,1)S(1)} collective-permute-done((bf16[128,512]{1,0:T(8,128)(2,1)S(1)}, bf16[128,512]{1,0:T(8,128)(2,1)S(1)}, u32[]{:S(2)}, u32[]{:S(2)}) %collective-permute-start.14) | collective-permute-done | bytes 131104 | tf_op jit(solution)/shard_map/ppermute | solution.py:576
  51.9 0.0 collective-permute-done.15.rest_2_
  51.9 0.1 add.3
  52.0 16.2 %all-gather.1 = bf16[512,512]{1,0:T(8,128)(2,1)S(1)} all-gather(bf16[128,512]{1,0:T(8,128)(2,1)S(1)} %add.3), channel_id=3, replica_groups=mesh['half0'=2,'half1'=2,'core'=2,'tp'=4] {'tp'}, dimensions={0}, use_global_device_ids=true | all-gather | bytes 655360 | tf_op jit(solution)/shard_map/all_gather | solution.py:603
  68.2 0.0 collective-permute-done.10.rest_0_
  68.2 0.0 collective-permute-done.11.rest_1_
  68.2 0.0 collective-permute-done.12.rest_2_
  68.2 0.1 add.2
  68.2 15.5 %all-gather = bf16[512,512]{1,0:T(8,128)(2,1)S(1)} all-gather(bf16[128,512]{1,0:T(8,128)(2,1)S(1)} %add.2), channel_id=2, replica_groups=mesh['half0'=2,'half1'=2,'core'=2,'tp'=4] {'tp'}, dimensions={0}, use_global_device_ids=true | all-gather | bytes 655360 | tf_op jit(solution)/shard_map/all_gather | solution.py:604
  83.7 0.8 lay.2.rest_0_
  84.5 0.8 lay.3
  (2 shorter events, 0.0 us)
Async XLA Ops:
  3.7 7.2 %collective-permute-start.1 = (bf16[560,128]{1,0:T(8,128)(2,1)S(1)}, bf16[560,128]{1,0:T(8,128)(2,1)S(1)}, u32[]{:S(2)}, u32[]{:S(2)}) collective-permute-start(bf16[560,128]{1,0:T(8,128)(2,1)S(1)} %get-tuple-element.25), channel_id=1, source_target_pairs={{0,8},{8,0},{16,24},{24,16},{1,9},{9,1},{17,25},{25,17},{2,10},{10... | collective-permute-start | bytes 430088 | tf_op jit(solution)/shard_map/ppermute | solution.py:517
  6.7 8.3 %collective-permute-start.3 = (bf16[560,128]{1,0:T(8,128)(2,1)S(1)}, bf16[560,128]{1,0:T(8,128)(2,1)S(1)}, u32[]{:S(2)}, u32[]{:S(2)}) collective-permute-start(bf16[560,128]{1,0:T(8,128)(2,1)S(1)} %get-tuple-element.26), channel_id=1, source_target_pairs={{0,16},{8,24},{16,0},{24,8},{1,17},{9,25},{17,1},{25,9},{2,18},{10... | collective-permute-start | bytes 430088 | tf_op jit(solution)/shard_map/ppermute | solution.py:517
  8.2 6.8 %collective-permute-start.5 = (bf16[560,128]{1,0:T(8,128)(2,1)S(1)}, bf16[560,128]{1,0:T(8,128)(2,1)S(1)}, u32[]{:S(2)}, u32[]{:S(2)}) collective-permute-start(bf16[560,128]{1,0:T(8,128)(2,1)S(1)} %get-tuple-element.27), channel_id=1, source_target_pairs={{0,24},{8,16},{16,8},{24,0},{1,25},{9,17},{17,9},{25,1},{2,26},{10... | collective-permute-start | bytes 430088 | tf_op jit(solution)/shard_map/ppermute | solution.py:517
  8.2 7.3 %collective-permute-start = (bf16[560,128]{1,0:T(8,128)(2,1)S(1)}, bf16[560,128]{1,0:T(8,128)(2,1)S(1)}, u32[]{:S(2)}, u32[]{:S(2)}) collective-permute-start(bf16[560,128]{1,0:T(8,128)(2,1)S(1)} %get-tuple-element.24), channel_id=1, source_target_pairs={{0,4},{4,0},{1,5},{5,1},{2,6},{6,2},{3,7},{7,3},{8,12},{12,8},{9,1... | collective-permute-start | bytes 430088 | tf_op jit(solution)/shard_map/ppermute | solution.py:518
  10.8 4.7 %collective-permute-start.2 = (bf16[560,128]{1,0:T(8,128)(2,1)S(1)}, bf16[560,128]{1,0:T(8,128)(2,1)S(1)}, u32[]{:S(2)}, u32[]{:S(2)}) collective-permute-start(bf16[560,128]{1,0:T(8,128)(2,1)S(1)} %collective-permute-done.1.refs_1_), channel_id=1, source_target_pairs={{0,4},{4,0},{1,5},{5,1},{2,6},{6,2},{3,7},{7,3},{8,12},{12,8},{9,1... | collective-permute-start | bytes 430088 | tf_op jit(solution)/shard_map/ppermute | solution.py:520
  15.0 1.4 %collective-permute-start.4 = (bf16[560,128]{1,0:T(8,128)(2,1)S(1)}, bf16[560,128]{1,0:T(8,128)(2,1)S(1)}, u32[]{:S(2)}, u32[]{:S(2)}) collective-permute-start(bf16[560,128]{1,0:T(8,128)(2,1)S(1)} %collective-permute-done.3.refs_3_), channel_id=1, source_target_pairs={{0,4},{4,0},{1,5},{5,1},{2,6},{6,2},{3,7},{7,3},{8,12},{12,8},{9,1... | collective-permute-start | bytes 430088 | tf_op jit(solution)/shard_map/ppermute | solution.py:520
  15.0 1.6 %collective-permute-start.6 = (bf16[560,128]{1,0:T(8,128)(2,1)S(1)}, bf16[560,128]{1,0:T(8,128)(2,1)S(1)}, u32[]{:S(2)}, u32[]{:S(2)}) collective-permute-start(bf16[560,128]{1,0:T(8,128)(2,1)S(1)} %collective-permute-done.5.refs_5_), channel_id=1, source_target_pairs={{0,4},{4,0},{1,5},{5,1},{2,6},{6,2},{3,7},{7,3},{8,12},{12,8},{9,1... | collective-permute-start | bytes 430088 | tf_op jit(solution)/shard_map/ppermute | solution.py:520
  18.9 1.2 %collective-permute-start.7 = (f32[8,256]{1,0:T(8,128)S(1)}, f32[8,256]{1,0:T(8,128)S(1)}, u32[]{:S(2)}, u32[]{:S(2)}) collective-permute-start(f32[8,256]{1,0:T(8,128)S(1)} %get-tuple-element.33.refs_7_), channel_id=1, source_target_pairs={{0,4},{4,0},{1,5},{5,1},{2,6},{6,2},{3,7},{7,3},{8,12},{12,8},{9,1... | collective-permute-start | bytes 24584 | tf_op jit(solution)/shard_map/ppermute | solution.py:546
  20.1 3.7 %collective-permute-start.8 = (f32[16,256]{1,0:T(8,128)S(1)}, f32[16,256]{1,0:T(8,128)S(1)}, u32[]{:S(2)}, u32[]{:S(2)}) collective-permute-start(f32[16,256]{1,0:T(8,128)S(1)} %pad_maximum_fusion.1), channel_id=1, source_target_pairs={{0,8},{8,0},{1,9},{9,1},{2,10},{10,2},{3,11},{11,3},{4,12},{12,4},... | collective-permute-start | bytes 49160 | tf_op jit(solution)/shard_map/ppermute | solution.py:546
  23.9 3.9 %collective-permute-start.9 = (f32[32,256]{1,0:T(8,128)S(1)}, f32[32,256]{1,0:T(8,128)S(1)}, u32[]{:S(2)}, u32[]{:S(2)}) collective-permute-start(f32[32,256]{1,0:T(8,128)S(1)} %pad_maximum_fusion), channel_id=1, source_target_pairs={{0,16},{16,0},{1,17},{17,1},{2,18},{18,2},{3,19},{19,3},{4,20},{20... | collective-permute-start | bytes 98312 | tf_op jit(solution)/shard_map/ppermute | solution.py:546
  32.3 8.1 %collective-permute-start.13 = (bf16[128,512]{1,0:T(8,128)(2,1)S(1)}, bf16[128,512]{1,0:T(8,128)(2,1)S(1)}, u32[]{:S(2)}, u32[]{:S(2)}) collective-permute-start(bf16[128,512]{1,0:T(8,128)(2,1)S(1)} %get-tuple-element.43), channel_id=1, source_target_pairs={{0,3},{1,2},{2,1},{3,0},{4,7},{5,6},{6,5},{7,4},{8,11},{9,10},{10,... | collective-permute-start | bytes 393224 | tf_op jit(solution)/shard_map/ppermute | solution.py:576
  36.0 15.9 %collective-permute-start.14 = (bf16[128,512]{1,0:T(8,128)(2,1)S(1)}, bf16[128,512]{1,0:T(8,128)(2,1)S(1)}, u32[]{:S(2)}, u32[]{:S(2)}) collective-permute-start(bf16[128,512]{1,0:T(8,128)(2,1)S(1)} %get-tuple-element.44), channel_id=1, source_target_pairs={{0,2},{1,3},{2,0},{3,1},{4,6},{5,7},{6,4},{7,5},{8,10},{9,11},{10,... | collective-permute-start | bytes 393224 | tf_op jit(solution)/shard_map/ppermute | solution.py:576
  36.0 15.9 %collective-permute-start.15 = (bf16[128,512]{1,0:T(8,128)(2,1)S(1)}, bf16[128,512]{1,0:T(8,128)(2,1)S(1)}, u32[]{:S(2)}, u32[]{:S(2)}) collective-permute-start(bf16[128,512]{1,0:T(8,128)(2,1)S(1)} %get-tuple-element.45), channel_id=1, source_target_pairs={{0,1},{1,0},{2,3},{3,2},{4,5},{5,4},{6,7},{7,6},{8,9},{9,8},{10,11... | collective-permute-start | bytes 393224 | tf_op jit(solution)/shard_map/ppermute | solution.py:576
  36.8 31.4 %collective-permute-start.10 = (bf16[128,512]{1,0:T(8,128)(2,1)S(1)}, bf16[128,512]{1,0:T(8,128)(2,1)S(1)}, u32[]{:S(2)}, u32[]{:S(2)}) collective-permute-start(bf16[128,512]{1,0:T(8,128)(2,1)S(1)} %get-tuple-element.39), channel_id=1, source_target_pairs={{0,3},{1,2},{2,1},{3,0},{4,7},{5,6},{6,5},{7,4},{8,11},{9,10},{10,... | collective-permute-start | bytes 393224 | tf_op jit(solution)/shard_map/ppermute | solution.py:576
  40.4 27.8 %collective-permute-start.11 = (bf16[128,512]{1,0:T(8,128)(2,1)S(1)}, bf16[128,512]{1,0:T(8,128)(2,1)S(1)}, u32[]{:S(2)}, u32[]{:S(2)}) collective-permute-start(bf16[128,512]{1,0:T(8,128)(2,1)S(1)} %get-tuple-element.40), channel_id=1, source_target_pairs={{0,2},{1,3},{2,0},{3,1},{4,6},{5,7},{6,4},{7,5},{8,10},{9,11},{10,... | collective-permute-start | bytes 393224 | tf_op jit(solution)/shard_map/ppermute | solution.py:576
  40.4 27.8 %collective-permute-start.12 = (bf16[128,512]{1,0:T(8,128)(2,1)S(1)}, bf16[128,512]{1,0:T(8,128)(2,1)S(1)}, u32[]{:S(2)}, u32[]{:S(2)}) collective-permute-start(bf16[128,512]{1,0:T(8,128)(2,1)S(1)} %get-tuple-element.41), channel_id=1, source_target_pairs={{0,1},{1,0},{2,3},{3,2},{4,5},{5,4},{6,7},{7,6},{8,9},{9,8},{10,11... | collective-permute-start | bytes 393224 | tf_op jit(solution)/shard_map/ppermute | solution.py:576

commit v10 on v9

--- a/solution.py
+++ b/solution.py
@@ -141,6 +141,45 @@
         pl.when(later)(lambda ref=ref: put_keys(ref))
         pl.when(jnp.logical_not(later))(lambda ref=ref: put_query(ref))
 
+def pack_kernel(ctx, ww_hbm, vw_hbm, fw_hbm, out_ref, sems):
+    nf2, dim = fw_hbm.shape
+    tile = 2 * LANES
+    at = pl.multiple_of(block_index(ctx) * tile, tile)
+    rows = pl.ds(at, tile)
+    moves = [
+        (ww_hbm.at[rows, pl.ds(0, LANES)], out_ref.at[pl.ds(0, tile), :]),
+        (ww_hbm.at[rows, pl.ds(LANES, LANES)], out_ref.at[pl.ds(tile, tile), :]),
+        (vw_hbm.at[rows, :], out_ref.at[pl.ds(2 * tile, tile), :]),
+    ]
+    for m in range(2):
+        lanes = pl.ds(pl.multiple_of(at + m * LANES, LANES), LANES)
+        moves.append((fw_hbm.at[:, lanes], out_ref.at[pl.ds(3 * tile + m * nf2, nf2), :]))
+    copies = [
+        pltpu.make_async_copy(src, dst, sems.at[n]) for n, (src, dst) in enumerate(moves)
+    ]
+    for copy in copies:
+        copy.start()
+    used = 3 * tile + 2 * nf2
+    out_ref[used:, :] = jnp.zeros((out_ref.shape[0] - used, LANES), bf16)
+    for copy in copies:
+        copy.wait()
+
+
+def others_kernel(pack_hbm, out_ref, sems):
+    head = lax.axis_index("tp")
+    others, used, _ = out_ref.shape
+    copies = [
+        pltpu.make_async_copy(
+            pack_hbm.at[jnp.bitwise_xor(head, t + 1), pl.ds(0, used), :], out_ref.at[t], sems.at[t]
+        )
+        for t in range(others)
+    ]
+    for copy in copies:
+        copy.start()
+    for copy in copies:
+        copy.wait()
+
+
 def between(totals, low, high):
     at = lax.broadcasted_iota(jnp.int32, totals.shape, 0)
     return jnp.sum(jnp.where((at > low) & (at < high), totals, 0.0), axis=0, keepdims=True)
@@ -367,50 +406,11 @@
     dwq, dwk = (dwq * scale).astype(bf16), (dwk * scale).astype(bf16)
     dv = dv.astype(bf16)
     dft = (jnp.concatenate([dqt, dkt], axis=0) * feat_scale).astype(bf16)
-    if len(rest) == 1:
-        grad_ref = rest[0]
-        grad_ref[0:rows, :] = dwq
-        grad_ref[rows : 2 * rows, :] = dwk
-        grad_ref[2 * rows : 3 * rows, :] = dv
-        put_wide(grad_ref, 3 * rows, dft)
-        return
-
-    ww_ref, vw_ref, fw_ref, *parts = rest
-    head = lax.axis_index("tp")
-    half, share = parts[0].shape
-    dw = jnp.concatenate([dwq, dwk], axis=1)
-    padded = jnp.concatenate([dft.astype(f32), jnp.zeros((LANES - 2 * nf, rows), f32)], axis=0)
-    df = jnp.transpose(padded)[:, : 2 * nf].astype(bf16)
-    for t in range(len(parts) // 2):
-        part = pl.ds(pl.multiple_of(jnp.bitwise_xor(head, t) * share, share), share)
-        product = nt(dw, ww_ref[part, :]) + nt(dv, vw_ref[part, :]) + nn(df, fw_ref[:, part])
-        for h in range(2):
-            ref = parts[2 * t + h]
-            ref[...] = product[h * half : (h + 1) * half].astype(ref.dtype)
-
-
-def add_kernel(part_ref, *rest):
-    *others, out_ref = rest
-    total = part_ref[...]
-    for ref in others:
-        total += ref[...].astype(f32)
-    out_ref[...] = total.astype(bf16)
-
-
-def lay_kernel(half, sums_ref, *rest):
-    out_ref, sems = rest[-2:]
-    shares, rows, width = sums_ref.shape
-    at = pl.ds(half * rows, rows)
-    copies = [
-        pltpu.make_async_copy(
-            sums_ref.at[z], out_ref.at[at, pl.ds(z * width, width)], sems.at[z]
-        )
-        for z in range(shares)
-    ]
-    for copy in copies:
-        copy.start()
-    for copy in copies:
-        copy.wait()
+    (grad_ref,) = rest
+    grad_ref[0:rows, :] = dwq
+    grad_ref[rows : 2 * rows, :] = dwk
+    grad_ref[2 * rows : 3 * rows, :] = dv
+    put_wide(grad_ref, 3 * rows, dft)
 
 
 def gather_rows(grad_ref, order, cat_ref, feat_ref):
@@ -422,6 +422,34 @@
             cat_ref[:, lane : lane + LANES] = grad_ref[h, part * rows : (part + 1) * rows, :]
     dft = jnp.concatenate([wide(grad_ref.at[h], 3 * rows, nf2) for h in order], axis=0)
     feat_ref[...] = jnp.transpose(dft.astype(f32)).astype(bf16)
+
+
+def columns_kernel(ctx, side, grad_ref, ww_ref, vw_ref, fw_ref, *rest):
+    pieces = rest[: ww_ref.shape[0] // (4 * LANES)]
+    out_ref, cat_ref, feat_ref, tile_ref, sems = rest[-5:]
+    heads = grad_ref.shape[0]
+    nf2 = fw_ref.shape[0]
+    tile = 2 * LANES
+    head, me = lax.axis_index("tp"), block_index(ctx)
+    gather_rows(
+        grad_ref, [head] + [jnp.bitwise_xor(head, t) for t in range(1, heads)], cat_ref, feat_ref
+    )
+    copies = []
+    for d, ref in enumerate(pieces):
+        at = pl.multiple_of(jnp.bitwise_xor(me, 2 * d + side) * tile, tile)
+        part = pl.ds(at, tile)
+        main = [ww_ref[part, :], vw_ref[part, :]]
+        main += [
+            ref[t, m * tile : (m + 1) * tile, :] for t in range(heads - 1) for m in range(3)
+        ]
+        feats = [fw_ref[:, part]] + [wide(ref.at[t], 3 * tile, nf2) for t in range(heads - 1)]
+        total = nt(cat_ref[...], jnp.concatenate(main, axis=1))
+        total += nn(feat_ref[...], jnp.concatenate(feats, axis=0))
+        tile_ref[d] = total.astype(bf16)
+        copies.append(pltpu.make_async_copy(tile_ref.at[d], out_ref.at[:, part], sems.at[d]))
+        copies[-1].start()
+    for copy in copies:
+        copy.wait()
 
 
 def merge_kernel(grad_ref, weight_ref, out_ref, cat_ref, feat_ref):
@@ -484,6 +512,20 @@
     columns = 3 * dh + nf2
     chips, count, heads = lax.axis_size(ctx[:-1]), lax.axis_size(ctx), lax.axis_size("tp")
     fw_t = feature_weight.T
+    tile = 2 * LANES
+    spread = heads == 4 and count * tile == dim and count == 8
+    if spread:
+        packed = pl.pallas_call(
+            partial(pack_kernel, ctx),
+            out_shape=jax.ShapeDtypeStruct((4 * tile, LANES), bf16),
+            in_specs=[HBM] * 3,
+            out_specs=VMEM,
+            scratch_shapes=[pltpu.SemaphoreType.DMA((5,))],
+            compiler_params=params,
+            cost_estimate=cost(1, 4 * columns * tile),
+            name="pack",
+        )(*in_hbm(window_weight, value_weight, fw_t))
+        weights = lax.all_gather(packed, "tp")
 
     payload = 2 * rows + 2 * nf + 16
     block = jax.ShapeDtypeStruct((payload, LANES), bf16)
@@ -547,61 +589,62 @@
     if count > 8:
         stats = [jnp.concatenate(stats, axis=0)]
 
-    share = dim // heads
-    shared = heads & (heads - 1) == 0 and share % LANES == 0
-    args = [*recv, *stats, own, query, feat, sheet]
-    if shared:
-        args += [ww, vw, fw]
-        out_shape = [jax.ShapeDtypeStruct((rows // 2, share), f32)] * 2
-        out_shape += [jax.ShapeDtypeStruct((rows // 2, share), bf16)] * (2 * heads - 2)
-    else:
-        out_shape = [jax.ShapeDtypeStruct((3 * rows + nf2 * rows // LANES, LANES), bf16)]
     grads = pl.pallas_call(
         lambda *refs: gradient_kernel(ctx, count, len(recv), len(stats), *refs),
-        out_shape=out_shape,
-        in_specs=[VMEM] * len(args),
-        out_specs=[VMEM] * len(out_shape),
+        out_shape=jax.ShapeDtypeStruct((3 * rows + nf2 * rows // LANES, LANES), bf16),
+        in_specs=[VMEM] * (len(recv) + len(stats) + 4),
+        out_specs=VMEM,
         scratch_shapes=[pltpu.VMEM((count, LANES), f32)],
         compiler_params=params,
         cost_estimate=cost(10**9, 2 * 1024 * 1024, 10**6),
         name="gradients",
-    )(*args)
-    if not shared:
+    )(*recv, *stats, own, query, feat, sheet)
+    if not spread:
         weights = jnp.concatenate([window_weight, value_weight, feature_weight], axis=1)
         weights = lax.all_gather(weights, "tp")
-        return (attended, merge(lax.all_gather(grads[0], "tp"), weights, rows, dim))
-
-    def sum_of(half):
-        others = [
-            lax.ppermute(grads[2 * t + half], "tp", [(z, z ^ t) for z in range(heads)])
-            for t in range(heads - 1, 0, -1)
-        ]
+        return (attended, merge(lax.all_gather(grads, "tp"), weights, rows, dim))
+
+    weights, grads = lax.optimization_barrier((weights, grads))
+    pieces = [
+        pl.pallas_call(
+            others_kernel,
+            out_shape=jax.ShapeDtypeStruct((heads - 1, columns * tile // LANES, LANES), bf16),
+            in_specs=[HBM],
+            out_specs=VMEM,
+            scratch_shapes=[pltpu.SemaphoreType.DMA((heads - 1,))],
+            compiler_params=params,
+            cost_estimate=cost(1, heads * columns * tile * 4),
+            name="others",
+        )(*in_hbm(weights))
+    ]
+    pieces[0], grads = lax.optimization_barrier((pieces[0], grads))
+    for d in range(1, chips):
+        pieces.append(
+            lax.ppermute(pieces[0], ctx[:-1], [(i, i ^ d) for i in range(chips)])
+        )
+    grads = lax.all_gather(grads, "tp")
+    swapped = [lax.ppermute(p, "core", swap) for p in pieces]
+
+    def columns_of(side, pieces, before):
         return pl.pallas_call(
-            add_kernel,
-            out_shape=jax.ShapeDtypeStruct((rows // 2, share), bf16),
-            in_specs=[VMEM] * heads,
-            out_specs=VMEM,
+            partial(columns_kernel, ctx, side),
+            out_shape=jax.ShapeDtypeStruct((rows, dim), bf16),
+            in_specs=[VMEM] * (4 + chips) + [ANY] * len(before),
+            out_specs=ANY,
+            scratch_shapes=[
+                pltpu.VMEM((rows, 3 * LANES * heads), bf16),
+                pltpu.VMEM((rows, nf2 * heads), bf16),
+                pltpu.VMEM((chips, rows, tile), bf16),
+                pltpu.SemaphoreType.DMA((chips,)),
+            ],
+            input_output_aliases={4 + chips: 0} if before else {},
             compiler_params=params,
-            cost_estimate=cost(rows * share * heads, 2 * rows * share * heads),
-            name="add",
-        )(grads[half], *others)
-
-    def lay(half, sums, before):
-        return pl.pallas_call(
-            partial(lay_kernel, half),
-            out_shape=jax.ShapeDtypeStruct((rows, dim), bf16),
-            in_specs=[VMEM] + [ANY] * len(before),
-            out_specs=ANY,
-            scratch_shapes=[pltpu.SemaphoreType.DMA((heads,))],
-            input_output_aliases={1: 0} if before else {},
-            compiler_params=params,
-            cost_estimate=cost(1, 2 * rows * dim),
-            name="lay",
-        )(sums, *before)
-
-    halves = [sum_of(half) for half in range(2)]
-    first = lay(0, lax.all_gather(halves[0], "tp"), [])
-    return (attended, lay(1, lax.all_gather(halves[1], "tp"), [first]))
+            cost_estimate=cost(rows * dim * heads * columns, heads * dim * columns),
+            name="columns",
+        )(grads, ww, vw, fw, *pieces, *before)
+
+    first = columns_of(0, pieces, [])
+    return (attended, columns_of(1, swapped, [first]))
 
 
 def solution(mesh):

time: 85.5 us -> 104 us (1.22)
  waiting for transfers between devices: 18.2 us -> 42.2 us
  between operations: 0.69 us -> 14.1 us
  blocking collectives: 31.7 us -> 19.2 us
  starting transfers between devices: 23 us -> 12 us
  Pallas kernels: 11.7 us -> 15.7 us
    ppermute x6 -> x7, waiting for transfers between devices: 4.42 us -> 27.4 us  [the longest x3 27.4 us: per_device(): lax.ppermute(pieces[0], ctx[:-1], [(i, i ^ d) for i in range(chips)])]
    all_gather x2 -> x1, blocking collectives: 31.7 us -> 19.2 us  [per_device(): grads = lax.all_gather(grads, 'tp')]
    ppermute x6 -> x7, starting transfers between devices: 15.1 us -> 4.07 us  [the longest x3 3.55 us: per_device(): lax.ppermute(pieces[0], ctx[:-1], [(i, i ^ d) for i in range(chips)])]
    pallas_call x4, Pallas kernels: 1.78 us -> 6.64 us  [the longest x2 3.81 us: columns_of(): pl.pallas_call(partial(columns_kernel, ctx, side), out_shape=jax.ShapeDty...]
    all_gather x0 -> x1, waiting for transfers between devices: none -> 1.07 us  [per_device(): weights = lax.all_gather(packed, 'tp')]
  transfers between devices with their start and end apart: 16 -> 18, of which waited for: 8 -> 10; matrix products, arithmetic and copies ran while one was open for 0% -> 0% of each run, Pallas kernels for 0% -> 11%
where the time goes in v10:
time: 104 us; the launch traced here: 103 us
  waiting for transfers between devices  42.2 us (41%)
  blocking collectives  19.2 us (18%)
  Pallas kernels  15.7 us (15%)
  between operations  14.1 us (14%)
  starting transfers between devices  12 us (12%)
    ppermute x3, waiting for transfers between devices, per_device(): lax.ppermute(pieces[0], ctx[:-1], [(i, i ^ d) for i in range(chips)])  27.4 us
    all_gather x1, blocking collectives, per_device(): grads = lax.all_gather(grads, 'tp')  19.2 us
    ppermute x3, waiting for transfers between devices, per_device(): lax.ppermute(sends[d], ctx[:-1], [(i, i ^ d) for i in range(chips)])  6.76 us
    ppermute x3, waiting for transfers between devices, per_device(): stats.append(lax.ppermute(held, name, swap))  5.96 us
    ppermute x3, starting transfers between devices, per_device(): lax.ppermute(sends[d], ctx[:-1], [(i, i ^ d) for i in range(chips)])  4.55 us
    pallas_call x2, Pallas kernels, columns_of(): pl.pallas_call(partial(columns_kernel, ctx, side), out_shape=jax.ShapeDty...  3.81 us
    pallas_call x1, Pallas kernels, per_device(): pl.pallas_call(lambda *refs: gradient_kernel(ctx, count, len(recv), len(s...  3.68 us
    ppermute x3, starting transfers between devices, per_device(): lax.ppermute(pieces[0], ctx[:-1], [(i, i ^ d) for i in range(chips)])  3.55 us
  transfers between devices with their start and end apart: 18, of which 10 were waited for; matrix products, arithmetic and copies ran while one was open for 0% of the time, Pallas kernels for 11%

profile of v10, /device:TPU:0, one launch (start us, length us, event | category | flops | bytes accessed | tf_op | source)
XLA Modules:
  0.0 103.3 jit_solution(1566774643703531886)
XLA Ops:
  7.2 0.0 all-gather.4.cloned.1.call-start
  7.2 1.7 %pack.1 = bf16[1024,128]{1,0:T(8,128)(2,1)} custom-call(bf16[2048,256]{1,0:T(8,128)(2,1)} %ww_hbm.3, bf16[2048,128]{1,0:T(8,128)(2,1)} %vw_hbm.3, bf16[32,2048]{1,0:T(8,128)(2,1)} %bitcast.7), custom_call_target="tpu_custom_call" | custom-call | flops 1 | bytes 425984 | tf_op jit(solution)/shard_map/pack/pallas_call | solution.py:518
  8.9 0.0 all-gather.4.cloned.1.call-update
  8.9 3.0 %project.1 = (bf16[560,128]{1,0:T(8,128)(2,1)S(1)}, bf16[560,128]{1,0:T(8,128)(2,1)S(1)}, bf16[560,128]{1,0:T(8,128)(2,1)S(1)}, bf16[560,128]{1,0:T(8,128)(2,1)S...) custom-call(bf16[256,2048]{1,0:T(8,128)(2,1)} %tok_hbm.1, ...), custom_call_target="tpu_custom_call" | custom-call | flops 436207616 | bytes 4194304 | tf_op jit(solution)/shard_map/project/pallas_call | solution.py:532
  11.9 3.0 %collective-permute-start.1 = (bf16[560,128]{1,0:T(8,128)(2,1)S(1)}, bf16[560,128]{1,0:T(8,128)(2,1)S(1)}, u32[]{:S(2)}, u32[]{:S(2)}) collective-permute-start(bf16[560,128]{1,0:T(8,128)(2,1)S(1)} %get-tuple-element.21), channel_id=1, source_target_pairs={{0,8},{8,0},{16,24},{24,16},{1,9},{9,1},{17,25},{25,17},{2,10},{10... | collective-permute-start | bytes 430088 | tf_op jit(solution)/shard_map/ppermute | solution.py:559
  14.9 1.5 %collective-permute-start.3 = (bf16[560,128]{1,0:T(8,128)(2,1)S(1)}, bf16[560,128]{1,0:T(8,128)(2,1)S(1)}, u32[]{:S(2)}, u32[]{:S(2)}) collective-permute-start(bf16[560,128]{1,0:T(8,128)(2,1)S(1)} %get-tuple-element.22), channel_id=1, source_target_pairs={{0,16},{8,24},{16,0},{24,8},{1,17},{9,25},{17,1},{25,9},{2,18},{10... | collective-permute-start | bytes 430088 | tf_op jit(solution)/shard_map/ppermute | solution.py:559
  16.5 0.0 collective-permute-start.5
  16.5 0.0 collective-permute-start
  16.5 2.6 %collective-permute-done.1.refs_1_ = bf16[560,128]{1,0:T(8,128)(2,1)S(1)} collective-permute-done((bf16[560,128]{1,0:T(8,128)(2,1)S(1)}, bf16[560,128]{1,0:T(8,128)(2,1)S(1)}, u32[]{:S(2)}, u32[]{:S(2)}) %collective-permute-start.1) | collective-permute-done | bytes 143392 | tf_op jit(solution)/shard_map/ppermute | solution.py:559
  19.1 0.0 collective-permute-start.2
  19.1 4.1 %collective-permute-done.3.refs_3_ = bf16[560,128]{1,0:T(8,128)(2,1)S(1)} collective-permute-done((bf16[560,128]{1,0:T(8,128)(2,1)S(1)}, bf16[560,128]{1,0:T(8,128)(2,1)S(1)}, u32[]{:S(2)}, u32[]{:S(2)}) %collective-permute-start.3) | collective-permute-done | bytes 143392 | tf_op jit(solution)/shard_map/ppermute | solution.py:559
  23.3 0.0 collective-permute-start.4
  23.3 0.0 collective-permute-done.5.refs_5_
  23.3 0.5 collective-permute-start.6
  23.8 0.0 collective-permute-done.refs_0_
  23.8 0.0 collective-permute-done.2.refs_2_
  23.8 0.8 collective-permute-done.4.refs_4_
  24.6 0.2 collective-permute-done.6.refs_6_
  24.8 2.4 %query_side.1 = (bf16[256,128]{1,0:T(8,128)(2,1)}, f32[8,256]{1,0:T(8,128)S(1)}, f32[256,128]{1,0:T(8,128)S(1)}) custom-call(bf16[560,128]{1,0:T(8,128)(2,1)S(1)} %collective-permute-done.refs_0_, bf16[560,128]{1,0:T(8,128)(2,1)S(1)} %collective-permute-done.1.refs_1_, bf16[560,128]{1,0:T(8,128)(2,1)S(1)} %collective-permute-done.2.refs_2_, ...), custom_call_target="tpu_custom_call" | custom-call | flops 1000000000 | bytes 2097152 | tf_op jit(solution)/shard_map/query_side/pallas_call | solution.py:567
  27.2 0.3 collective-permute-start.7
  27.5 0.9 collective-permute-done.7.refs_8_
  28.4 1.0 %collective-permute-start.8 = (f32[16,256]{1,0:T(8,128)S(1)}, f32[16,256]{1,0:T(8,128)S(1)}, u32[]{:S(2)}, u32[]{:S(2)}) collective-permute-start(f32[16,256]{1,0:T(8,128)S(1)} %pad_maximum_fusion.1), channel_id=1, source_target_pairs={{0,8},{8,0},{1,9},{9,1},{2,10},{10,2},{3,11},{11,3},{4,12},{12,4},... | collective-permute-start | bytes 49160 | tf_op jit(solution)/shard_map/ppermute | solution.py:588
  29.4 2.7 %collective-permute-done.8.refs_9_ = f32[16,256]{1,0:T(8,128)S(1)} collective-permute-done((f32[16,256]{1,0:T(8,128)S(1)}, f32[16,256]{1,0:T(8,128)S(1)}, u32[]{:S(2)}, u32[]{:S(2)}) %collective-permute-start.8) | collective-permute-done | bytes 16416 | tf_op jit(solution)/shard_map/ppermute | solution.py:588
  32.1 1.5 %collective-permute-start.9 = (f32[32,256]{1,0:T(8,128)S(1)}, f32[32,256]{1,0:T(8,128)S(1)}, u32[]{:S(2)}, u32[]{:S(2)}) collective-permute-start(f32[32,256]{1,0:T(8,128)S(1)} %pad_maximum_fusion), channel_id=1, source_target_pairs={{0,16},{16,0},{1,17},{17,1},{2,18},{18,2},{3,19},{19,3},{4,20},{20... | collective-permute-start | bytes 98312 | tf_op jit(solution)/shard_map/ppermute | solution.py:588
  33.7 2.4 %collective-permute-done.9.refs_10_ = f32[32,256]{1,0:T(8,128)S(1)} collective-permute-done((f32[32,256]{1,0:T(8,128)S(1)}, f32[32,256]{1,0:T(8,128)S(1)}, u32[]{:S(2)}, u32[]{:S(2)}) %collective-permute-start.9) | collective-permute-done | bytes 32800 | tf_op jit(solution)/shard_map/ppermute | solution.py:588
  36.0 3.7 %gradients.1 = bf16[832,128]{1,0:T(8,128)(2,1)S(1)} custom-call(bf16[560,128]{1,0:T(8,128)(2,1)S(1)} %collective-permute-done.refs_0_, bf16[560,128]{1,0:T(8,128)(2,1)S(1)} %collective-permute-done.1.refs_1_, bf16[560,128]{1,0:T(8,128)(2,1)S(1)} %collective-permute-done.2.refs_2_, bf16[560,128]{1,0:T(8,128)(2,1)S(1)} %collective-permute-done.3.refs_3_, ...), custom_call_target="tpu_custom_call" | custom-call | flops 1000000000 | bytes 2097152 | tf_op jit(solution)/shard_map/gradients/pallas_call | solution.py:592
  39.7 1.1 %all-gather.4.cloned.1.call-done = bf16[4096,128]{1,0:T(8,128)(2,1)} async-done(((bf16[1024,128]{1,0:T(8,128)(2,1)}), bf16[4096,128]{1,0:T(8,128)(2,1)}) %all-gather.4.cloned.1.call-update) | async-done | bytes 1048592 | tf_op jit(solution)/shard_map/all_gather | solution.py:528
  40.8 1.2 %others.1.rest_0_ = bf16[3,832,128]{2,1,0:T(8,128)(2,1)S(1)} custom-call(bf16[4,1024,128]{2,1,0:T(8,128)(2,1)} %bitcast.6), custom_call_target="tpu_custom_call" | custom-call | flops 1 | bytes 1703936 | tf_op jit(solution)/shard_map/others/pallas_call | solution.py:609
  42.0 1.5 %collective-permute-start.11 = (bf16[3,832,128]{2,1,0:T(8,128)(2,1)S(1)}, bf16[3,832,128]{2,1,0:T(8,128)(2,1)S(1)}, u32[]{:S(2)}, u32[]{:S(2)}) collective-permute-start(bf16[3,832,128]{2,1,0:T(8,128)(2,1)S(1)} %others.1.rest_0_), channel_id=1, source_target_pairs={{0,8},{8,0},{16,24},{24,16},{1,9},{9,1},{17,25},{25,17},{2,10},{10... | collective-permute-start | bytes 1916936 | tf_op jit(solution)/shard_map/ppermute | solution.py:623
  43.5 1.5 %collective-permute-start.13 = (bf16[3,832,128]{2,1,0:T(8,128)(2,1)S(1)}, bf16[3,832,128]{2,1,0:T(8,128)(2,1)S(1)}, u32[]{:S(2)}, u32[]{:S(2)}) collective-permute-start(bf16[3,832,128]{2,1,0:T(8,128)(2,1)S(1)} %others.1.rest_0_), channel_id=1, source_target_pairs={{0,16},{8,24},{16,0},{24,8},{1,17},{9,25},{17,1},{25,9},{2,18},{10... | collective-permute-start | bytes 1916936 | tf_op jit(solution)/shard_map/ppermute | solution.py:623
  45.0 0.5 collective-permute-start.15
  45.5 0.0 collective-permute-start.10
  45.5 13.8 %collective-permute-done.11.rest_1_ = bf16[3,832,128]{2,1,0:T(8,128)(2,1)S(1)} collective-permute-done((bf16[3,832,128]{2,1,0:T(8,128)(2,1)S(1)}, bf16[3,832,128]{2,1,0:T(8,128)(2,1)S(1)}, u32[]{:S(2)}, u32[]{:S(2)}) %collective-permute-start.11) | collective-permute-done | bytes 639008 | tf_op jit(solution)/shard_map/ppermute | solution.py:623
  59.3 0.0 collective-permute-start.12
  59.3 13.6 %collective-permute-done.13.rest_2_ = bf16[3,832,128]{2,1,0:T(8,128)(2,1)S(1)} collective-permute-done((bf16[3,832,128]{2,1,0:T(8,128)(2,1)S(1)}, bf16[3,832,128]{2,1,0:T(8,128)(2,1)S(1)}, u32[]{:S(2)}, u32[]{:S(2)}) %collective-permute-start.13) | collective-permute-done | bytes 639008 | tf_op jit(solution)/shard_map/ppermute | solution.py:623
  72.9 0.0 collective-permute-start.14
  72.9 0.0 collective-permute-done.15.rest_3_
  72.9 0.5 collective-permute-start.16
  73.4 19.2 %all-gather.1 = bf16[3328,128]{1,0:T(8,128)(2,1)S(1)} all-gather(bf16[832,128]{1,0:T(8,128)(2,1)S(1)} %gradients.1), channel_id=3, replica_groups=mesh['half0'=2,'half1'=2,'core'=2,'tp'=4] {'tp'}, dimensions={0}, use_global_device_ids=true | all-gather | bytes 1064960 | tf_op jit(solution)/shard_map/all_gather | solution.py:625
  92.6 1.9 %columns.2.rest_4_ = bf16[256,2048]{1,0:T(8,128)(2,1)} custom-call(bf16[4,832,128]{2,1,0:T(8,128)(2,1)S(1)} %bitcast.4, bf16[2048,256]{1,0:T(8,128)(2,1)S(1)} %get-tuple-element.34.ww_ref, bf16[2048,128]{1,0:T(8,128)(2,1)S(1)} %get-tuple-element.35.vw_ref, bf16[32,2048]{1,0:T(8,128)(2,1)S(1)} %get-tuple-element.36.fw_ref, ...), custom_call_target="tpu_custom_call" | custom-call | flops 872415232 | bytes 3407872 | tf_op jit(solution)/shard_map/columns/pallas_call | solution.py:629
  94.5 0.0 collective-permute-done.10.rest_0_
  94.5 0.0 collective-permute-done.12.rest_1_
  94.5 0.0 collective-permute-done.14.rest_2_
  94.5 0.0 collective-permute-done.16.rest_3_
  94.5 1.9 %columns.3 = bf16[256,2048]{1,0:T(8,128)(2,1)} custom-call(bf16[4,832,128]{2,1,0:T(8,128)(2,1)S(1)} %bitcast.5, bf16[2048,256]{1,0:T(8,128)(2,1)S(1)} %get-tuple-element.34.ww_ref, bf16[2048,128]{1,0:T(8,128)(2,1)S(1)} %get-tuple-element.35.vw_ref, bf16[32,2048]{1,0:T(8,128)(2,1)S(1)} %get-tuple-element.36.fw_ref, ...), custom_call_target="tpu_custom_call", output_to_operand_aliasing={{}: (8, {})} | custom-call | flops 872415232 | bytes 3407872 | tf_op jit(solution)/shard_map/columns/pallas_call | solution.py:629
  (2 shorter events, 0.0 us)
Async XLA Ops:
  7.2 33.6 %all-gather.4.cloned.1.call-start = ((), (), s32[]{:S(2)}) async-start(), calls=%async_computation | async-start | bytes 1310720 | tf_op jit(solution)/shard_map/all_gather | solution.py:528
  11.9 7.2 %collective-permute-start.1 = (bf16[560,128]{1,0:T(8,128)(2,1)S(1)}, bf16[560,128]{1,0:T(8,128)(2,1)S(1)}, u32[]{:S(2)}, u32[]{:S(2)}) collective-permute-start(bf16[560,128]{1,0:T(8,128)(2,1)S(1)} %get-tuple-element.21), channel_id=1, source_target_pairs={{0,8},{8,0},{16,24},{24,16},{1,9},{9,1},{17,25},{25,17},{2,10},{10... | collective-permute-start | bytes 430088 | tf_op jit(solution)/shard_map/ppermute | solution.py:559
  14.9 8.3 %collective-permute-start.3 = (bf16[560,128]{1,0:T(8,128)(2,1)S(1)}, bf16[560,128]{1,0:T(8,128)(2,1)S(1)}, u32[]{:S(2)}, u32[]{:S(2)}) collective-permute-start(bf16[560,128]{1,0:T(8,128)(2,1)S(1)} %get-tuple-element.22), channel_id=1, source_target_pairs={{0,16},{8,24},{16,0},{24,8},{1,17},{9,25},{17,1},{25,9},{2,18},{10... | collective-permute-start | bytes 430088 | tf_op jit(solution)/shard_map/ppermute | solution.py:559
  16.5 6.8 %collective-permute-start.5 = (bf16[560,128]{1,0:T(8,128)(2,1)S(1)}, bf16[560,128]{1,0:T(8,128)(2,1)S(1)}, u32[]{:S(2)}, u32[]{:S(2)}) collective-permute-start(bf16[560,128]{1,0:T(8,128)(2,1)S(1)} %get-tuple-element.23), channel_id=1, source_target_pairs={{0,24},{8,16},{16,8},{24,0},{1,25},{9,17},{17,9},{25,1},{2,26},{10... | collective-permute-start | bytes 430088 | tf_op jit(solution)/shard_map/ppermute | solution.py:559
  16.5 7.3 %collective-permute-start = (bf16[560,128]{1,0:T(8,128)(2,1)S(1)}, bf16[560,128]{1,0:T(8,128)(2,1)S(1)}, u32[]{:S(2)}, u32[]{:S(2)}) collective-permute-start(bf16[560,128]{1,0:T(8,128)(2,1)S(1)} %get-tuple-element.20), channel_id=1, source_target_pairs={{0,4},{4,0},{1,5},{5,1},{2,6},{6,2},{3,7},{7,3},{8,12},{12,8},{9,1... | collective-permute-start | bytes 430088 | tf_op jit(solution)/shard_map/ppermute | solution.py:560
  19.1 4.7 %collective-permute-start.2 = (bf16[560,128]{1,0:T(8,128)(2,1)S(1)}, bf16[560,128]{1,0:T(8,128)(2,1)S(1)}, u32[]{:S(2)}, u32[]{:S(2)}) collective-permute-start(bf16[560,128]{1,0:T(8,128)(2,1)S(1)} %collective-permute-done.1.refs_1_), channel_id=1, source_target_pairs={{0,4},{4,0},{1,5},{5,1},{2,6},{6,2},{3,7},{7,3},{8,12},{12,8},{9,1... | collective-permute-start | bytes 430088 | tf_op jit(solution)/shard_map/ppermute | solution.py:562
  23.3 1.4 %collective-permute-start.4 = (bf16[560,128]{1,0:T(8,128)(2,1)S(1)}, bf16[560,128]{1,0:T(8,128)(2,1)S(1)}, u32[]{:S(2)}, u32[]{:S(2)}) collective-permute-start(bf16[560,128]{1,0:T(8,128)(2,1)S(1)} %collective-permute-done.3.refs_3_), channel_id=1, source_target_pairs={{0,4},{4,0},{1,5},{5,1},{2,6},{6,2},{3,7},{7,3},{8,12},{12,8},{9,1... | collective-permute-start | bytes 430088 | tf_op jit(solution)/shard_map/ppermute | solution.py:562
  23.3 1.6 %collective-permute-start.6 = (bf16[560,128]{1,0:T(8,128)(2,1)S(1)}, bf16[560,128]{1,0:T(8,128)(2,1)S(1)}, u32[]{:S(2)}, u32[]{:S(2)}) collective-permute-start(bf16[560,128]{1,0:T(8,128)(2,1)S(1)} %collective-permute-done.5.refs_5_), channel_id=1, source_target_pairs={{0,4},{4,0},{1,5},{5,1},{2,6},{6,2},{3,7},{7,3},{8,12},{12,8},{9,1... | collective-permute-start | bytes 430088 | tf_op jit(solution)/shard_map/ppermute | solution.py:562
  27.2 1.2 %collective-permute-start.7 = (f32[8,256]{1,0:T(8,128)S(1)}, f32[8,256]{1,0:T(8,128)S(1)}, u32[]{:S(2)}, u32[]{:S(2)}) collective-permute-start(f32[8,256]{1,0:T(8,128)S(1)} %get-tuple-element.29.refs_7_), channel_id=1, source_target_pairs={{0,4},{4,0},{1,5},{5,1},{2,6},{6,2},{3,7},{7,3},{8,12},{12,8},{9,1... | collective-permute-start | bytes 24584 | tf_op jit(solution)/shard_map/ppermute | solution.py:588
  28.4 3.7 %collective-permute-start.8 = (f32[16,256]{1,0:T(8,128)S(1)}, f32[16,256]{1,0:T(8,128)S(1)}, u32[]{:S(2)}, u32[]{:S(2)}) collective-permute-start(f32[16,256]{1,0:T(8,128)S(1)} %pad_maximum_fusion.1), channel_id=1, source_target_pairs={{0,8},{8,0},{1,9},{9,1},{2,10},{10,2},{3,11},{11,3},{4,12},{12,4},... | collective-permute-start | bytes 49160 | tf_op jit(solution)/shard_map/ppermute | solution.py:588
  32.1 3.9 %collective-permute-start.9 = (f32[32,256]{1,0:T(8,128)S(1)}, f32[32,256]{1,0:T(8,128)S(1)}, u32[]{:S(2)}, u32[]{:S(2)}) collective-permute-start(f32[32,256]{1,0:T(8,128)S(1)} %pad_maximum_fusion), channel_id=1, source_target_pairs={{0,16},{16,0},{1,17},{17,1},{2,18},{18,2},{3,19},{19,3},{4,20},{20... | collective-permute-start | bytes 98312 | tf_op jit(solution)/shard_map/ppermute | solution.py:588
  42.0 17.4 %collective-permute-start.11 = (bf16[3,832,128]{2,1,0:T(8,128)(2,1)S(1)}, bf16[3,832,128]{2,1,0:T(8,128)(2,1)S(1)}, u32[]{:S(2)}, u32[]{:S(2)}) collective-permute-start(bf16[3,832,128]{2,1,0:T(8,128)(2,1)S(1)} %others.1.rest_0_), channel_id=1, source_target_pairs={{0,8},{8,0},{16,24},{24,16},{1,9},{9,1},{17,25},{25,17},{2,10},{10... | collective-permute-start | bytes 1916936 | tf_op jit(solution)/shard_map/ppermute | solution.py:623
  43.5 29.4 %collective-permute-start.13 = (bf16[3,832,128]{2,1,0:T(8,128)(2,1)S(1)}, bf16[3,832,128]{2,1,0:T(8,128)(2,1)S(1)}, u32[]{:S(2)}, u32[]{:S(2)}) collective-permute-start(bf16[3,832,128]{2,1,0:T(8,128)(2,1)S(1)} %others.1.rest_0_), channel_id=1, source_target_pairs={{0,16},{8,24},{16,0},{24,8},{1,17},{9,25},{17,1},{25,9},{2,18},{10... | collective-permute-start | bytes 1916936 | tf_op jit(solution)/shard_map/ppermute | solution.py:623
  45.0 27.9 %collective-permute-start.15 = (bf16[3,832,128]{2,1,0:T(8,128)(2,1)S(1)}, bf16[3,832,128]{2,1,0:T(8,128)(2,1)S(1)}, u32[]{:S(2)}, u32[]{:S(2)}) collective-permute-start(bf16[3,832,128]{2,1,0:T(8,128)(2,1)S(1)} %others.1.rest_0_), channel_id=1, source_target_pairs={{0,24},{8,16},{16,8},{24,0},{1,25},{9,17},{17,9},{25,1},{2,26},{10... | collective-permute-start | bytes 1916936 | tf_op jit(solution)/shard_map/ppermute | solution.py:623
  45.5 49.0 %collective-permute-start.10 = (bf16[3,832,128]{2,1,0:T(8,128)(2,1)S(1)}, bf16[3,832,128]{2,1,0:T(8,128)(2,1)S(1)}, u32[]{:S(2)}, u32[]{:S(2)}) collective-permute-start(bf16[3,832,128]{2,1,0:T(8,128)(2,1)S(1)} %others.1.rest_0_), channel_id=1, source_target_pairs={{0,4},{4,0},{1,5},{5,1},{2,6},{6,2},{3,7},{7,3},{8,12},{12,8},{9,1... | collective-permute-start | bytes 1916936 | tf_op jit(solution)/shard_map/ppermute | solution.py:626
  59.3 35.2 %collective-permute-start.12 = (bf16[3,832,128]{2,1,0:T(8,128)(2,1)S(1)}, bf16[3,832,128]{2,1,0:T(8,128)(2,1)S(1)}, u32[]{:S(2)}, u32[]{:S(2)}) collective-permute-start(bf16[3,832,128]{2,1,0:T(8,128)(2,1)S(1)} %collective-permute-done.11.rest_1_), channel_id=1, source_target_pairs={{0,4},{4,0},{1,5},{5,1},{2,6},{6,2},{3,7},{7,3},{8,12},{12,8},{9,1... | collective-permute-start | bytes 1916936 | tf_op jit(solution)/shard_map/ppermute | solution.py:626
  72.9 21.6 %collective-permute-start.14 = (bf16[3,832,128]{2,1,0:T(8,128)(2,1)S(1)}, bf16[3,832,128]{2,1,0:T(8,128)(2,1)S(1)}, u32[]{:S(2)}, u32[]{:S(2)}) collective-permute-start(bf16[3,832,128]{2,1,0:T(8,128)(2,1)S(1)} %collective-permute-done.13.rest_2_), channel_id=1, source_target_pairs={{0,4},{4,0},{1,5},{5,1},{2,6},{6,2},{3,7},{7,3},{8,12},{12,8},{9,1... | collective-permute-start | bytes 1916936 | tf_op jit(solution)/shard_map/ppermute | solution.py:626
  72.9 21.6 %collective-permute-start.16 = (bf16[3,832,128]{2,1,0:T(8,128)(2,1)S(1)}, bf16[3,832,128]{2,1,0:T(8,128)(2,1)S(1)}, u32[]{:S(2)}, u32[]{:S(2)}) collective-permute-start(bf16[3,832,128]{2,1,0:T(8,128)(2,1)S(1)} %collective-permute-done.15.rest_3_), channel_id=1, source_target_pairs={{0,4},{4,0},{1,5},{5,1},{2,6},{6,2},{3,7},{7,3},{8,12},{12,8},{9,1... | collective-permute-start | bytes 1916936 | tf_op jit(solution)/shard_map/ppermute | solution.py:626
Sparse Core Ops, SparseCore 0:
  10.1 30.6 all-gather.3

commit v11 on v10

--- a/solution.py
+++ b/solution.py
@@ -159,25 +159,14 @@
     ]
     for copy in copies:
         copy.start()
-    used = 3 * tile + 2 * nf2
-    out_ref[used:, :] = jnp.zeros((out_ref.shape[0] - used, LANES), bf16)
     for copy in copies:
         copy.wait()
 
 
-def others_kernel(pack_hbm, out_ref, sems):
-    head = lax.axis_index("tp")
-    others, used, _ = out_ref.shape
-    copies = [
-        pltpu.make_async_copy(
-            pack_hbm.at[jnp.bitwise_xor(head, t + 1), pl.ds(0, used), :], out_ref.at[t], sems.at[t]
-        )
-        for t in range(others)
-    ]
-    for copy in copies:
-        copy.start()
-    for copy in copies:
-        copy.wait()
+def stack_kernel(*refs):
+    *parts, out_ref = refs
+    for t, ref in enumerate(parts):
+        out_ref[t] = ref[...]
 
 
 def between(totals, low, high):
@@ -517,7 +506,7 @@
     if spread:
         packed = pl.pallas_call(
             partial(pack_kernel, ctx),
-            out_shape=jax.ShapeDtypeStruct((4 * tile, LANES), bf16),
+            out_shape=jax.ShapeDtypeStruct((columns * tile // LANES, LANES), bf16),
             in_specs=[HBM] * 3,
             out_specs=VMEM,
             scratch_shapes=[pltpu.SemaphoreType.DMA((5,))],
@@ -525,7 +514,25 @@
             cost_estimate=cost(1, 4 * columns * tile),
             name="pack",
         )(*in_hbm(window_weight, value_weight, fw_t))
-        weights = lax.all_gather(packed, "tp")
+        near = [
+            lax.ppermute(packed, "tp", [(z, z ^ t) for z in range(heads)])
+            for t in range(1, heads)
+        ]
+        pieces = [
+            pl.pallas_call(
+                stack_kernel,
+                out_shape=jax.ShapeDtypeStruct((heads - 1, *packed.shape), bf16),
+                in_specs=[VMEM] * (heads - 1),
+                out_specs=VMEM,
+                compiler_params=params,
+                cost_estimate=cost(1, 4 * packed.size * heads),
+                name="stack",
+            )(*near)
+        ]
+        for d in range(1, chips):
+            pieces.append(
+                lax.ppermute(pieces[0], ctx[:-1], [(i, i ^ d) for i in range(chips)])
+            )
 
     payload = 2 * rows + 2 * nf + 16
     block = jax.ShapeDtypeStruct((payload, LANES), bf16)
@@ -549,7 +556,7 @@
             pltpu.SemaphoreType.DMA((2,)),
         ],
         compiler_params=params,
-        cost_estimate=cost(2 * rows * dim * columns, 4 * 1024 * 1024),
+        cost_estimate=cost(1, 1024),
         name="project",
     )(*in_hbm(tokens, fw_t, window_weight, value_weight, log_decay.T, out_grad))
 
@@ -579,7 +586,7 @@
             pltpu.VMEM((count, rows), f32),
         ],
         compiler_params=params,
-        cost_estimate=cost(10**9, 2 * 1024 * 1024, 10**6),
+        cost_estimate=cost(1, 1024),
         name="query_side",
     )(*recv, own, query, feat, cum)
     stats = [stat]
@@ -596,7 +603,7 @@
         out_specs=VMEM,
         scratch_shapes=[pltpu.VMEM((count, LANES), f32)],
         compiler_params=params,
-        cost_estimate=cost(10**9, 2 * 1024 * 1024, 10**6),
+        cost_estimate=cost(1, 1024),
         name="gradients",
     )(*recv, *stats, own, query, feat, sheet)
     if not spread:
@@ -604,25 +611,8 @@
         weights = lax.all_gather(weights, "tp")
         return (attended, merge(lax.all_gather(grads, "tp"), weights, rows, dim))
 
-    weights, grads = lax.optimization_barrier((weights, grads))
-    pieces = [
-        pl.pallas_call(
-            others_kernel,
-            out_shape=jax.ShapeDtypeStruct((heads - 1, columns * tile // LANES, LANES), bf16),
-            in_specs=[HBM],
-            out_specs=VMEM,
-            scratch_shapes=[pltpu.SemaphoreType.DMA((heads - 1,))],
-            compiler_params=params,
-            cost_estimate=cost(1, heads * columns * tile * 4),
-            name="others",
-        )(*in_hbm(weights))
-    ]
-    pieces[0], grads = lax.optimization_barrier((pieces[0], grads))
-    for d in range(1, chips):
-        pieces.append(
-            lax.ppermute(pieces[0], ctx[:-1], [(i, i ^ d) for i in range(chips)])
-        )
     grads = lax.all_gather(grads, "tp")
+    pieces, grads = lax.optimization_barrier((pieces, grads))
     swapped = [lax.ppermute(p, "core", swap) for p in pieces]
 
     def columns_of(side, pieces, before):

time: 104 us -> 92.5 us (0.89)
  between operations: 14.1 us -> 0.71 us
  starting transfers between devices: 12 us -> 16.4 us
  Pallas kernels: 15.7 us -> 13.9 us
    ppermute x3, waiting for transfers between devices: 27.4 us -> 0.01 us  [per_device(): lax.ppermute(pieces[0], ctx[:-1], [(i, i ^ d) for i in range(chips)])]
    ppermute x3, waiting for transfers between devices: 5.96 us -> 27.3 us  [per_device(): stats.append(lax.ppermute(held, name, swap))]
    ppermute x0 -> x3, waiting for transfers between devices: none -> 6.88 us  [per_device(): lax.ppermute(packed, 'tp', [(z, z ^ t) for z in range(heads)])]
    ppermute x0 -> x3, starting transfers between devices: none -> 4.67 us  [per_device(): lax.ppermute(packed, 'tp', [(z, z ^ t) for z in range(heads)])]
    ppermute x4, waiting for transfers between devices: 0.01 us -> 1.87 us  [per_device(): swapped = [lax.ppermute(p, 'core', swap) for p in pieces]]
    ppermute x3, starting transfers between devices: 2.87 us -> 1.56 us  [per_device(): stats.append(lax.ppermute(held, name, swap))]
    pallas_call x1, Pallas kernels: 1.16 us -> 0.04 us  [per_device(): pl.pallas_call(stack_kernel, out_shape=jax.ShapeDtypeStruct((heads - 1, *...]
    all_gather x1 -> x0, waiting for transfers between devices: 1.07 us -> none  [per_device(): weights = lax.all_gather(packed, 'tp')]
  transfers between devices with their start and end apart: 18 -> 20, of which waited for: 10 -> 7; matrix products, arithmetic and copies ran while one was open for 0% -> 0% of each run, Pallas kernels for 11% -> 10%
where the time goes in v11:
time: 92.5 us; the launch traced here: 92.3 us
  waiting for transfers between devices  41.8 us (45%)
  blocking collectives  19.5 us (21%)
  starting transfers between devices  16.4 us (18%)
  Pallas kernels  13.9 us (15%)
    ppermute x3, waiting for transfers between devices, per_device(): stats.append(lax.ppermute(held, name, swap))  27.3 us
    all_gather x1, blocking collectives, per_device(): grads = lax.all_gather(grads, 'tp')  19.5 us
    ppermute x3, waiting for transfers between devices, per_device(): lax.ppermute(packed, 'tp', [(z, z ^ t) for z in range(heads)])  6.88 us
    ppermute x3, waiting for transfers between devices, per_device(): lax.ppermute(sends[d], ctx[:-1], [(i, i ^ d) for i in range(chips)])  5.73 us
    ppermute x3, starting transfers between devices, per_device(): lax.ppermute(sends[d], ctx[:-1], [(i, i ^ d) for i in range(chips)])  5 us
    ppermute x3, starting transfers between devices, per_device(): lax.ppermute(packed, 'tp', [(z, z ^ t) for z in range(heads)])  4.67 us
    pallas_call x2, Pallas kernels, columns_of(): pl.pallas_call(partial(columns_kernel, ctx, side), out_shape=jax.ShapeDty...  3.8 us
    pallas_call x1, Pallas kernels, per_device(): pl.pallas_call(lambda *refs: gradient_kernel(ctx, count, len(recv), len(s...  3.66 us
  transfers between devices with their start and end apart: 20, of which 7 were waited for; matrix products, arithmetic and copies ran while one was open for 0% of the time, Pallas kernels for 10%

profile of v11, /device:TPU:0, one launch (start us, length us, event | category | flops | bytes accessed | tf_op | source)
XLA Modules:
  0.0 92.3 jit_solution(3754864249561822350)
XLA Ops:
  0.6 3.0 %project.1 = (bf16[560,128]{1,0:T(8,128)(2,1)S(1)}, bf16[560,128]{1,0:T(8,128)(2,1)S(1)}, bf16[560,128]{1,0:T(8,128)(2,1)S(1)}, bf16[560,128]{1,0:T(8,128)(2,1)S...) custom-call(bf16[256,2048]{1,0:T(8,128)(2,1)} %tok_hbm.1, ...), custom_call_target="tpu_custom_call" | custom-call | flops 1 | bytes 1024 | tf_op jit(solution)/shard_map/project/pallas_call | solution.py:539
  3.7 3.0 %collective-permute-start.1 = (bf16[560,128]{1,0:T(8,128)(2,1)S(1)}, bf16[560,128]{1,0:T(8,128)(2,1)S(1)}, u32[]{:S(2)}, u32[]{:S(2)}) collective-permute-start(bf16[560,128]{1,0:T(8,128)(2,1)S(1)} %get-tuple-element.22), channel_id=1, source_target_pairs={{0,8},{8,0},{16,24},{24,16},{1,9},{9,1},{17,25},{25,17},{2,10},{10... | collective-permute-start | bytes 430088 | tf_op jit(solution)/shard_map/ppermute | solution.py:566
  6.7 0.9 %pack.1 = bf16[832,128]{1,0:T(8,128)(2,1)S(1)} custom-call(bf16[2048,256]{1,0:T(8,128)(2,1)} %ww_hbm.3, bf16[2048,128]{1,0:T(8,128)(2,1)} %vw_hbm.3, bf16[32,2048]{1,0:T(8,128)(2,1)} %bitcast.6), custom_call_target="tpu_custom_call" | custom-call | flops 1 | bytes 425984 | tf_op jit(solution)/shard_map/pack/pallas_call | solution.py:507
  7.6 1.6 %collective-permute-start.7 = (bf16[832,128]{1,0:T(8,128)(2,1)S(1)}, bf16[832,128]{1,0:T(8,128)(2,1)S(1)}, u32[]{:S(2)}, u32[]{:S(2)}) collective-permute-start(bf16[832,128]{1,0:T(8,128)(2,1)S(1)} %pack.1), channel_id=1, source_target_pairs={{0,1},{1,0},{2,3},{3,2},{4,5},{5,4},{6,7},{7,6},{8,9},{9,8},{10,11... | collective-permute-start | bytes 638984 | tf_op jit(solution)/shard_map/ppermute | solution.py:518
  9.3 2.6 %collective-permute-start.8 = (bf16[832,128]{1,0:T(8,128)(2,1)S(1)}, bf16[832,128]{1,0:T(8,128)(2,1)S(1)}, u32[]{:S(2)}, u32[]{:S(2)}) collective-permute-start(bf16[832,128]{1,0:T(8,128)(2,1)S(1)} %pack.1), channel_id=1, source_target_pairs={{0,2},{1,3},{2,0},{3,1},{4,6},{5,7},{6,4},{7,5},{8,10},{9,11},{10,... | collective-permute-start | bytes 638984 | tf_op jit(solution)/shard_map/ppermute | solution.py:518
  11.8 1.5 %collective-permute-start.3 = (bf16[560,128]{1,0:T(8,128)(2,1)S(1)}, bf16[560,128]{1,0:T(8,128)(2,1)S(1)}, u32[]{:S(2)}, u32[]{:S(2)}) collective-permute-start(bf16[560,128]{1,0:T(8,128)(2,1)S(1)} %get-tuple-element.23), channel_id=1, source_target_pairs={{0,16},{8,24},{16,0},{24,8},{1,17},{9,25},{17,1},{25,9},{2,18},{10... | collective-permute-start | bytes 430088 | tf_op jit(solution)/shard_map/ppermute | solution.py:566
  13.4 0.5 collective-permute-start.5
  13.8 0.0 collective-permute-done.1.refs_1_
  13.8 0.4 collective-permute-start.9
  14.3 5.7 %collective-permute-done.3.refs_3_ = bf16[560,128]{1,0:T(8,128)(2,1)S(1)} collective-permute-done((bf16[560,128]{1,0:T(8,128)(2,1)S(1)}, bf16[560,128]{1,0:T(8,128)(2,1)S(1)}, u32[]{:S(2)}, u32[]{:S(2)}) %collective-permute-start.3) | collective-permute-done | bytes 143392 | tf_op jit(solution)/shard_map/ppermute | solution.py:566
  20.0 0.0 collective-permute-start
  20.0 0.0 collective-permute-done.5.refs_5_
  20.0 0.5 collective-permute-start.2
  20.5 0.0 collective-permute-done.7.refs_0_
  20.5 0.1 collective-permute-start.4
  20.6 6.9 %collective-permute-done.8.refs_1_ = bf16[832,128]{1,0:T(8,128)(2,1)S(1)} collective-permute-done((bf16[832,128]{1,0:T(8,128)(2,1)S(1)}, bf16[832,128]{1,0:T(8,128)(2,1)S(1)}, u32[]{:S(2)}, u32[]{:S(2)}) %collective-permute-start.8) | collective-permute-done | bytes 213024 | tf_op jit(solution)/shard_map/ppermute | solution.py:518
  27.5 0.0 collective-permute-start.6
  27.5 0.0 collective-permute-done.9.refs_2_
  27.5 0.1 collective-permute-start.10
  27.7 0.0 collective-permute-done.refs_0_
  27.7 1.5 %collective-permute-start.11 = (bf16[3,832,128]{2,1,0:T(8,128)(2,1)S(1)}, bf16[3,832,128]{2,1,0:T(8,128)(2,1)S(1)}, u32[]{:S(2)}, u32[]{:S(2)}) collective-permute-start(bf16[3,832,128]{2,1,0:T(8,128)(2,1)S(1)} %stack.1.rest_0_), channel_id=1, source_target_pairs={{0,16},{8,24},{16,0},{24,8},{1,17},{9,25},{17,1},{25,9},{2,18},{10... | collective-permute-start | bytes 1916936 | tf_op jit(solution)/shard_map/ppermute | solution.py:534
  29.2 0.0 collective-permute-done.2.refs_2_
  29.2 1.9 %collective-permute-start.12 = (bf16[3,832,128]{2,1,0:T(8,128)(2,1)S(1)}, bf16[3,832,128]{2,1,0:T(8,128)(2,1)S(1)}, u32[]{:S(2)}, u32[]{:S(2)}) collective-permute-start(bf16[3,832,128]{2,1,0:T(8,128)(2,1)S(1)} %stack.1.rest_0_), channel_id=1, source_target_pairs={{0,24},{8,16},{16,8},{24,0},{1,25},{9,17},{17,9},{25,1},{2,26},{10... | collective-permute-start | bytes 1916936 | tf_op jit(solution)/shard_map/ppermute | solution.py:534
  31.1 0.0 collective-permute-done.4.refs_4_
  31.1 0.0 collective-permute-done.6.refs_6_
  31.1 2.4 %query_side.1 = (bf16[256,128]{1,0:T(8,128)(2,1)}, f32[8,256]{1,0:T(8,128)S(1)}, f32[256,128]{1,0:T(8,128)S(1)}) custom-call(bf16[560,128]{1,0:T(8,128)(2,1)S(1)} %collective-permute-done.refs_0_, bf16[560,128]{1,0:T(8,128)(2,1)S(1)} %collective-permute-done.1.refs_1_, bf16[560,128]{1,0:T(8,128)(2,1)S(1)} %collective-permute-done.2.refs_2_, ...), custom_call_target="tpu_custom_call" | custom-call | flops 1 | bytes 1024 | tf_op jit(solution)/shard_map/query_side/pallas_call | solution.py:574
  33.5 0.0 collective-permute-start.13
  33.5 1.2 %collective-permute-done.13.refs_8_ = f32[8,256]{1,0:T(8,128)S(1)} collective-permute-done((f32[8,256]{1,0:T(8,128)S(1)}, f32[8,256]{1,0:T(8,128)S(1)}, u32[]{:S(2)}, u32[]{:S(2)}) %collective-permute-start.13) | collective-permute-done | bytes 8224 | tf_op jit(solution)/shard_map/ppermute | solution.py:595
  34.7 0.1 collective-permute-start.14
  34.8 23.7 %collective-permute-done.14.refs_9_ = f32[16,256]{1,0:T(8,128)S(1)} collective-permute-done((f32[16,256]{1,0:T(8,128)S(1)}, f32[16,256]{1,0:T(8,128)S(1)}, u32[]{:S(2)}, u32[]{:S(2)}) %collective-permute-start.14) | collective-permute-done | bytes 16416 | tf_op jit(solution)/shard_map/ppermute | solution.py:595
  58.5 1.5 %collective-permute-start.15 = (f32[32,256]{1,0:T(8,128)S(1)}, f32[32,256]{1,0:T(8,128)S(1)}, u32[]{:S(2)}, u32[]{:S(2)}) collective-permute-start(f32[32,256]{1,0:T(8,128)S(1)} %pad_maximum_fusion), channel_id=1, source_target_pairs={{0,16},{16,0},{1,17},{17,1},{2,18},{18,2},{3,19},{19,3},{4,20},{20... | collective-permute-start | bytes 98312 | tf_op jit(solution)/shard_map/ppermute | solution.py:595
  60.0 2.4 %collective-permute-done.15.refs_10_ = f32[32,256]{1,0:T(8,128)S(1)} collective-permute-done((f32[32,256]{1,0:T(8,128)S(1)}, f32[32,256]{1,0:T(8,128)S(1)}, u32[]{:S(2)}, u32[]{:S(2)}) %collective-permute-start.15) | collective-permute-done | bytes 32800 | tf_op jit(solution)/shard_map/ppermute | solution.py:595
  62.4 3.7 %gradients.1 = bf16[832,128]{1,0:T(8,128)(2,1)S(1)} custom-call(bf16[560,128]{1,0:T(8,128)(2,1)S(1)} %collective-permute-done.refs_0_, bf16[560,128]{1,0:T(8,128)(2,1)S(1)} %collective-permute-done.1.refs_1_, bf16[560,128]{1,0:T(8,128)(2,1)S(1)} %collective-permute-done.2.refs_2_, bf16[560,128]{1,0:T(8,128)(2,1)S(1)} %collective-permute-done.3.refs_3_, ...), custom_call_target="tpu_custom_call" | custom-call | flops 1 | bytes 1024 | tf_op jit(solution)/shard_map/gradients/pallas_call | solution.py:599
  66.1 19.5 %all-gather = bf16[3328,128]{1,0:T(8,128)(2,1)S(1)} all-gather(bf16[832,128]{1,0:T(8,128)(2,1)S(1)} %gradients.1), channel_id=2, replica_groups=mesh['half0'=2,'half1'=2,'core'=2,'tp'=4] {'tp'}, dimensions={0}, use_global_device_ids=true | all-gather | bytes 1064960 | tf_op jit(solution)/shard_map/all_gather | solution.py:614
  85.5 0.0 collective-permute-done.10.rest_1_
  85.5 0.0 collective-permute-done.11.rest_2_
  85.5 0.0 collective-permute-done.12.rest_3_
  85.5 0.1 collective-permute-start.16
  85.6 0.5 collective-permute-start.17
  86.1 0.1 collective-permute-start.18
  86.2 0.4 collective-permute-start.19
  86.6 1.9 %columns.2.rest_4_ = bf16[256,2048]{1,0:T(8,128)(2,1)} custom-call(bf16[4,832,128]{2,1,0:T(8,128)(2,1)S(1)} %bitcast.3, bf16[2048,256]{1,0:T(8,128)(2,1)S(1)} %get-tuple-element.33.ww_ref, bf16[2048,128]{1,0:T(8,128)(2,1)S(1)} %get-tuple-element.34.vw_ref, bf16[32,2048]{1,0:T(8,128)(2,1)S(1)} %get-tuple-element.35.fw_ref, ...), custom_call_target="tpu_custom_call" | custom-call | flops 872415232 | bytes 3407872 | tf_op jit(solution)/shard_map/columns/pallas_call | solution.py:619
  88.5 0.0 collective-permute-done.16.rest_0_
  88.5 0.0 collective-permute-done.17.rest_1_
  88.6 0.9 collective-permute-done.18.rest_2_
  89.5 0.9 collective-permute-done.19.rest_3_
  90.4 1.9 %columns.3 = bf16[256,2048]{1,0:T(8,128)(2,1)} custom-call(bf16[4,832,128]{2,1,0:T(8,128)(2,1)S(1)} %bitcast.4, bf16[2048,256]{1,0:T(8,128)(2,1)S(1)} %get-tuple-element.33.ww_ref, bf16[2048,128]{1,0:T(8,128)(2,1)S(1)} %get-tuple-element.34.vw_ref, bf16[32,2048]{1,0:T(8,128)(2,1)S(1)} %get-tuple-element.35.fw_ref, ...), custom_call_target="tpu_custom_call", output_to_operand_aliasing={{}: (8, {})} | custom-call | flops 872415232 | bytes 3407872 | tf_op jit(solution)/shard_map/columns/pallas_call | solution.py:619
  (3 shorter events, 0.0 us)
Async XLA Ops:
  3.7 10.2 %collective-permute-start.1 = (bf16[560,128]{1,0:T(8,128)(2,1)S(1)}, bf16[560,128]{1,0:T(8,128)(2,1)S(1)}, u32[]{:S(2)}, u32[]{:S(2)}) collective-permute-start(bf16[560,128]{1,0:T(8,128)(2,1)S(1)} %get-tuple-element.22), channel_id=1, source_target_pairs={{0,8},{8,0},{16,24},{24,16},{1,9},{9,1},{17,25},{25,17},{2,10},{10... | collective-permute-start | bytes 430088 | tf_op jit(solution)/shard_map/ppermute | solution.py:566
  7.6 12.9 %collective-permute-start.7 = (bf16[832,128]{1,0:T(8,128)(2,1)S(1)}, bf16[832,128]{1,0:T(8,128)(2,1)S(1)}, u32[]{:S(2)}, u32[]{:S(2)}) collective-permute-start(bf16[832,128]{1,0:T(8,128)(2,1)S(1)} %pack.1), channel_id=1, source_target_pairs={{0,1},{1,0},{2,3},{3,2},{4,5},{5,4},{6,7},{7,6},{8,9},{9,8},{10,11... | collective-permute-start | bytes 638984 | tf_op jit(solution)/shard_map/ppermute | solution.py:518
  9.3 18.2 %collective-permute-start.8 = (bf16[832,128]{1,0:T(8,128)(2,1)S(1)}, bf16[832,128]{1,0:T(8,128)(2,1)S(1)}, u32[]{:S(2)}, u32[]{:S(2)}) collective-permute-start(bf16[832,128]{1,0:T(8,128)(2,1)S(1)} %pack.1), channel_id=1, source_target_pairs={{0,2},{1,3},{2,0},{3,1},{4,6},{5,7},{6,4},{7,5},{8,10},{9,11},{10,... | collective-permute-start | bytes 638984 | tf_op jit(solution)/shard_map/ppermute | solution.py:518
  11.8 8.2 %collective-permute-start.3 = (bf16[560,128]{1,0:T(8,128)(2,1)S(1)}, bf16[560,128]{1,0:T(8,128)(2,1)S(1)}, u32[]{:S(2)}, u32[]{:S(2)}) collective-permute-start(bf16[560,128]{1,0:T(8,128)(2,1)S(1)} %get-tuple-element.23), channel_id=1, source_target_pairs={{0,16},{8,24},{16,0},{24,8},{1,17},{9,25},{17,1},{25,9},{2,18},{10... | collective-permute-start | bytes 430088 | tf_op jit(solution)/shard_map/ppermute | solution.py:566
  13.4 6.7 %collective-permute-start.5 = (bf16[560,128]{1,0:T(8,128)(2,1)S(1)}, bf16[560,128]{1,0:T(8,128)(2,1)S(1)}, u32[]{:S(2)}, u32[]{:S(2)}) collective-permute-start(bf16[560,128]{1,0:T(8,128)(2,1)S(1)} %get-tuple-element.24), channel_id=1, source_target_pairs={{0,24},{8,16},{16,8},{24,0},{1,25},{9,17},{17,9},{25,1},{2,26},{10... | collective-permute-start | bytes 430088 | tf_op jit(solution)/shard_map/ppermute | solution.py:566
  13.8 13.6 %collective-permute-start.9 = (bf16[832,128]{1,0:T(8,128)(2,1)S(1)}, bf16[832,128]{1,0:T(8,128)(2,1)S(1)}, u32[]{:S(2)}, u32[]{:S(2)}) collective-permute-start(bf16[832,128]{1,0:T(8,128)(2,1)S(1)} %pack.1), channel_id=1, source_target_pairs={{0,3},{1,2},{2,1},{3,0},{4,7},{5,6},{6,5},{7,4},{8,11},{9,10},{10,... | collective-permute-start | bytes 638984 | tf_op jit(solution)/shard_map/ppermute | solution.py:518
  20.0 7.7 %collective-permute-start = (bf16[560,128]{1,0:T(8,128)(2,1)S(1)}, bf16[560,128]{1,0:T(8,128)(2,1)S(1)}, u32[]{:S(2)}, u32[]{:S(2)}) collective-permute-start(bf16[560,128]{1,0:T(8,128)(2,1)S(1)} %get-tuple-element.21), channel_id=1, source_target_pairs={{0,4},{4,0},{1,5},{5,1},{2,6},{6,2},{3,7},{7,3},{8,12},{12,8},{9,1... | collective-permute-start | bytes 430088 | tf_op jit(solution)/shard_map/ppermute | solution.py:567
  20.0 9.2 %collective-permute-start.2 = (bf16[560,128]{1,0:T(8,128)(2,1)S(1)}, bf16[560,128]{1,0:T(8,128)(2,1)S(1)}, u32[]{:S(2)}, u32[]{:S(2)}) collective-permute-start(bf16[560,128]{1,0:T(8,128)(2,1)S(1)} %collective-permute-done.1.refs_1_), channel_id=1, source_target_pairs={{0,4},{4,0},{1,5},{5,1},{2,6},{6,2},{3,7},{7,3},{8,12},{12,8},{9,1... | collective-permute-start | bytes 430088 | tf_op jit(solution)/shard_map/ppermute | solution.py:569
  20.5 10.6 %collective-permute-start.4 = (bf16[560,128]{1,0:T(8,128)(2,1)S(1)}, bf16[560,128]{1,0:T(8,128)(2,1)S(1)}, u32[]{:S(2)}, u32[]{:S(2)}) collective-permute-start(bf16[560,128]{1,0:T(8,128)(2,1)S(1)} %collective-permute-done.3.refs_3_), channel_id=1, source_target_pairs={{0,4},{4,0},{1,5},{5,1},{2,6},{6,2},{3,7},{7,3},{8,12},{12,8},{9,1... | collective-permute-start | bytes 430088 | tf_op jit(solution)/shard_map/ppermute | solution.py:569
  27.5 3.6 %collective-permute-start.6 = (bf16[560,128]{1,0:T(8,128)(2,1)S(1)}, bf16[560,128]{1,0:T(8,128)(2,1)S(1)}, u32[]{:S(2)}, u32[]{:S(2)}) collective-permute-start(bf16[560,128]{1,0:T(8,128)(2,1)S(1)} %collective-permute-done.5.refs_5_), channel_id=1, source_target_pairs={{0,4},{4,0},{1,5},{5,1},{2,6},{6,2},{3,7},{7,3},{8,12},{12,8},{9,1... | collective-permute-start | bytes 430088 | tf_op jit(solution)/shard_map/ppermute | solution.py:569
  27.5 58.0 %collective-permute-start.10 = (bf16[3,832,128]{2,1,0:T(8,128)(2,1)S(1)}, bf16[3,832,128]{2,1,0:T(8,128)(2,1)S(1)}, u32[]{:S(2)}, u32[]{:S(2)}) collective-permute-start(bf16[3,832,128]{2,1,0:T(8,128)(2,1)S(1)} %stack.1.rest_0_), channel_id=1, source_target_pairs={{0,8},{8,0},{16,24},{24,16},{1,9},{9,1},{17,25},{25,17},{2,10},{10... | collective-permute-start | bytes 1916936 | tf_op jit(solution)/shard_map/ppermute | solution.py:534
  27.7 57.9 %collective-permute-start.11 = (bf16[3,832,128]{2,1,0:T(8,128)(2,1)S(1)}, bf16[3,832,128]{2,1,0:T(8,128)(2,1)S(1)}, u32[]{:S(2)}, u32[]{:S(2)}) collective-permute-start(bf16[3,832,128]{2,1,0:T(8,128)(2,1)S(1)} %stack.1.rest_0_), channel_id=1, source_target_pairs={{0,16},{8,24},{16,0},{24,8},{1,17},{9,25},{17,1},{25,9},{2,18},{10... | collective-permute-start | bytes 1916936 | tf_op jit(solution)/shard_map/ppermute | solution.py:534
  29.2 56.3 %collective-permute-start.12 = (bf16[3,832,128]{2,1,0:T(8,128)(2,1)S(1)}, bf16[3,832,128]{2,1,0:T(8,128)(2,1)S(1)}, u32[]{:S(2)}, u32[]{:S(2)}) collective-permute-start(bf16[3,832,128]{2,1,0:T(8,128)(2,1)S(1)} %stack.1.rest_0_), channel_id=1, source_target_pairs={{0,24},{8,16},{16,8},{24,0},{1,25},{9,17},{17,9},{25,1},{2,26},{10... | collective-permute-start | bytes 1916936 | tf_op jit(solution)/shard_map/ppermute | solution.py:534
  33.5 1.2 %collective-permute-start.13 = (f32[8,256]{1,0:T(8,128)S(1)}, f32[8,256]{1,0:T(8,128)S(1)}, u32[]{:S(2)}, u32[]{:S(2)}) collective-permute-start(f32[8,256]{1,0:T(8,128)S(1)} %get-tuple-element.30.refs_7_), channel_id=1, source_target_pairs={{0,4},{4,0},{1,5},{5,1},{2,6},{6,2},{3,7},{7,3},{8,12},{12,8},{9,1... | collective-permute-start | bytes 24584 | tf_op jit(solution)/shard_map/ppermute | solution.py:595
  34.7 23.8 %collective-permute-start.14 = (f32[16,256]{1,0:T(8,128)S(1)}, f32[16,256]{1,0:T(8,128)S(1)}, u32[]{:S(2)}, u32[]{:S(2)}) collective-permute-start(f32[16,256]{1,0:T(8,128)S(1)} %pad_maximum_fusion.1), channel_id=1, source_target_pairs={{0,8},{8,0},{1,9},{9,1},{2,10},{10,2},{3,11},{11,3},{4,12},{12,4},... | collective-permute-start | bytes 49160 | tf_op jit(solution)/shard_map/ppermute | solution.py:595
  58.5 3.9 %collective-permute-start.15 = (f32[32,256]{1,0:T(8,128)S(1)}, f32[32,256]{1,0:T(8,128)S(1)}, u32[]{:S(2)}, u32[]{:S(2)}) collective-permute-start(f32[32,256]{1,0:T(8,128)S(1)} %pad_maximum_fusion), channel_id=1, source_target_pairs={{0,16},{16,0},{1,17},{17,1},{2,18},{18,2},{3,19},{19,3},{4,20},{20... | collective-permute-start | bytes 98312 | tf_op jit(solution)/shard_map/ppermute | solution.py:595
  85.5 3.0 %collective-permute-start.16 = (bf16[3,832,128]{2,1,0:T(8,128)(2,1)S(1)}, bf16[3,832,128]{2,1,0:T(8,128)(2,1)S(1)}, u32[]{:S(2)}, u32[]{:S(2)}) collective-permute-start(bf16[3,832,128]{2,1,0:T(8,128)(2,1)S(1)} %stack.1.rest_0_), channel_id=1, source_target_pairs={{0,4},{4,0},{1,5},{5,1},{2,6},{6,2},{3,7},{7,3},{8,12},{12,8},{9,1... | collective-permute-start | bytes 1916936 | tf_op jit(solution)/shard_map/ppermute | solution.py:616
  85.6 3.0 %collective-permute-start.17 = (bf16[3,832,128]{2,1,0:T(8,128)(2,1)S(1)}, bf16[3,832,128]{2,1,0:T(8,128)(2,1)S(1)}, u32[]{:S(2)}, u32[]{:S(2)}) collective-permute-start(bf16[3,832,128]{2,1,0:T(8,128)(2,1)S(1)} %collective-permute-done.10.rest_1_), channel_id=1, source_target_pairs={{0,4},{4,0},{1,5},{5,1},{2,6},{6,2},{3,7},{7,3},{8,12},{12,8},{9,1... | collective-permute-start | bytes 1916936 | tf_op jit(solution)/shard_map/ppermute | solution.py:616
  86.1 3.4 %collective-permute-start.18 = (bf16[3,832,128]{2,1,0:T(8,128)(2,1)S(1)}, bf16[3,832,128]{2,1,0:T(8,128)(2,1)S(1)}, u32[]{:S(2)}, u32[]{:S(2)}) collective-permute-start(bf16[3,832,128]{2,1,0:T(8,128)(2,1)S(1)} %collective-permute-done.11.rest_2_), channel_id=1, source_target_pairs={{0,4},{4,0},{1,5},{5,1},{2,6},{6,2},{3,7},{7,3},{8,12},{12,8},{9,1... | collective-permute-start | bytes 1916936 | tf_op jit(solution)/shard_map/ppermute | solution.py:616
  86.2 4.2 %collective-permute-start.19 = (bf16[3,832,128]{2,1,0:T(8,128)(2,1)S(1)}, bf16[3,832,128]{2,1,0:T(8,128)(2,1)S(1)}, u32[]{:S(2)}, u32[]{:S(2)}) collective-permute-start(bf16[3,832,128]{2,1,0:T(8,128)(2,1)S(1)} %collective-permute-done.12.rest_3_), channel_id=1, source_target_pairs={{0,4},{4,0},{1,5},{5,1},{2,6},{6,2},{3,7},{7,3},{8,12},{12,8},{9,1... | collective-permute-start | bytes 1916936 | tf_op jit(solution)/shard_map/ppermute | solution.py:616

commit v12 on v11

--- a/solution.py
+++ b/solution.py
@@ -64,9 +64,25 @@
     return place
 
 
-def project_kernel(ctx, tok_hbm, fw_hbm, ww_hbm, vw_hbm, ld_hbm, do_hbm, *rest):
-    *sends, keys_ref, query_ref, feat_ref, cum_ref, ww_ref, vw_ref, fw_ref = rest[:-5]
-    tok_ref, ld_ref, do_ref, sems, small = rest[-5:]
+def pack_copies(ctx, ww_hbm, vw_hbm, fw_hbm, out_ref, sems):
+    nf2 = fw_hbm.shape[0]
+    tile = 2 * LANES
+    at = pl.multiple_of(block_index(ctx) * tile, tile)
+    rows = pl.ds(at, tile)
+    moves = [
+        (ww_hbm.at[rows, pl.ds(0, LANES)], out_ref.at[pl.ds(0, tile), :]),
+        (ww_hbm.at[rows, pl.ds(LANES, LANES)], out_ref.at[pl.ds(tile, tile), :]),
+        (vw_hbm.at[rows, :], out_ref.at[pl.ds(2 * tile, tile), :]),
+    ]
+    for m in range(2):
+        lanes = pl.ds(pl.multiple_of(at + m * LANES, LANES), LANES)
+        moves.append((fw_hbm.at[:, lanes], out_ref.at[pl.ds(3 * tile + m * nf2, nf2), :]))
+    return [pltpu.make_async_copy(src, dst, sems.at[n]) for n, (src, dst) in enumerate(moves)]
+
+
+def project_kernel(ctx, packs, tok_hbm, fw_hbm, ww_hbm, vw_hbm, ld_hbm, do_hbm, *rest):
+    *sends, keys_ref, query_ref, feat_ref, cum_ref, ww_ref, vw_ref, fw_ref = rest[packs:-6]
+    tok_ref, ld_ref, do_ref, sems, small, pack_sems = rest[-6:]
     me = block_index(ctx)
     rows, dim = tok_ref.shape
     dh = do_ref.shape[1]
@@ -90,6 +106,9 @@
     for group in copies:
         for at, copy in enumerate(group):
             copy.start(priority=min(at, 1))
+    packing = pack_copies(ctx, ww_hbm, vw_hbm, fw_hbm, rest[0], pack_sems) if packs else []
+    for copy in packing:
+        copy.start()
     for copy in others:
         copy.wait()
     at_row, at_col = iotas(rows)
@@ -140,28 +159,8 @@
         later = jnp.bitwise_xor(me, max(2 * at, 1)) > me
         pl.when(later)(lambda ref=ref: put_keys(ref))
         pl.when(jnp.logical_not(later))(lambda ref=ref: put_query(ref))
-
-def pack_kernel(ctx, ww_hbm, vw_hbm, fw_hbm, out_ref, sems):
-    nf2, dim = fw_hbm.shape
-    tile = 2 * LANES
-    at = pl.multiple_of(block_index(ctx) * tile, tile)
-    rows = pl.ds(at, tile)
-    moves = [
-        (ww_hbm.at[rows, pl.ds(0, LANES)], out_ref.at[pl.ds(0, tile), :]),
-        (ww_hbm.at[rows, pl.ds(LANES, LANES)], out_ref.at[pl.ds(tile, tile), :]),
-        (vw_hbm.at[rows, :], out_ref.at[pl.ds(2 * tile, tile), :]),
-    ]
-    for m in range(2):
-        lanes = pl.ds(pl.multiple_of(at + m * LANES, LANES), LANES)
-        moves.append((fw_hbm.at[:, lanes], out_ref.at[pl.ds(3 * tile + m * nf2, nf2), :]))
-    copies = [
-        pltpu.make_async_copy(src, dst, sems.at[n]) for n, (src, dst) in enumerate(moves)
-    ]
-    for copy in copies:
-        copy.start()
-    for copy in copies:
+    for copy in packing:
         copy.wait()
-
 
 def stack_kernel(*refs):
     *parts, out_ref = refs
@@ -503,42 +502,16 @@
     fw_t = feature_weight.T
     tile = 2 * LANES
     spread = heads == 4 and count * tile == dim and count == 8
+    packs = []
     if spread:
-        packed = pl.pallas_call(
-            partial(pack_kernel, ctx),
-            out_shape=jax.ShapeDtypeStruct((columns * tile // LANES, LANES), bf16),
-            in_specs=[HBM] * 3,
-            out_specs=VMEM,
-            scratch_shapes=[pltpu.SemaphoreType.DMA((5,))],
-            compiler_params=params,
-            cost_estimate=cost(1, 4 * columns * tile),
-            name="pack",
-        )(*in_hbm(window_weight, value_weight, fw_t))
-        near = [
-            lax.ppermute(packed, "tp", [(z, z ^ t) for z in range(heads)])
-            for t in range(1, heads)
-        ]
-        pieces = [
-            pl.pallas_call(
-                stack_kernel,
-                out_shape=jax.ShapeDtypeStruct((heads - 1, *packed.shape), bf16),
-                in_specs=[VMEM] * (heads - 1),
-                out_specs=VMEM,
-                compiler_params=params,
-                cost_estimate=cost(1, 4 * packed.size * heads),
-                name="stack",
-            )(*near)
-        ]
-        for d in range(1, chips):
-            pieces.append(
-                lax.ppermute(pieces[0], ctx[:-1], [(i, i ^ d) for i in range(chips)])
-            )
+        packs = [jax.ShapeDtypeStruct((columns * tile // LANES, LANES), bf16)]
 
     payload = 2 * rows + 2 * nf + 16
     block = jax.ShapeDtypeStruct((payload, LANES), bf16)
-    *sends, own, query, feat, cum, ww, vw, fw = pl.pallas_call(
-        partial(project_kernel, ctx),
-        out_shape=[block] * (chips + 2)
+    outs = pl.pallas_call(
+        partial(project_kernel, ctx, len(packs)),
+        out_shape=packs
+        + [block] * (chips + 2)
         + [
             jax.ShapeDtypeStruct((rows, nf2), bf16),
             jax.ShapeDtypeStruct((rows, 1), f32),
@@ -547,18 +520,20 @@
             jax.ShapeDtypeStruct((nf2, dim), bf16),
         ],
         in_specs=[HBM] * 6,
-        out_specs=[VMEM] * (chips + 7),
+        out_specs=[VMEM] * (len(packs) + chips + 7),
         scratch_shapes=[
             pltpu.VMEM((rows, dim), bf16),
             pltpu.VMEM((1, rows), f32),
             pltpu.VMEM((rows, dh), bf16),
             pltpu.SemaphoreType.DMA((CHUNKS, 4)),
             pltpu.SemaphoreType.DMA((2,)),
+            pltpu.SemaphoreType.DMA((5,)),
         ],
         compiler_params=params,
         cost_estimate=cost(1, 1024),
         name="project",
     )(*in_hbm(tokens, fw_t, window_weight, value_weight, log_decay.T, out_grad))
+    *sends, own, query, feat, cum, ww, vw, fw = outs[len(packs) :]
 
     swap = [(0, 1), (1, 0)]
     recv = {}
@@ -570,6 +545,13 @@
     recv = [recv[d] for d in range(1, count)]
     if count > 8:
         recv = [jnp.stack(recv)]
+
+    if spread:
+        near = [
+            lax.ppermute(outs[0], "tp", [(z, z ^ t) for z in range(heads)])
+            for t in range(1, heads)
+        ]
+        near[:2], own = lax.optimization_barrier((near[:2], own))
 
     attended, stat, sheet = pl.pallas_call(
         lambda *refs: query_kernel(ctx, count, *refs),
@@ -596,6 +578,26 @@
     if count > 8:
         stats = [jnp.concatenate(stats, axis=0)]
 
+    if spread:
+        near, stats = lax.optimization_barrier((near, stats))
+        pieces = [
+            pl.pallas_call(
+                stack_kernel,
+                out_shape=jax.ShapeDtypeStruct((heads - 1, *packs[0].shape), bf16),
+                in_specs=[VMEM] * (heads - 1),
+                out_specs=VMEM,
+                compiler_params=params,
+                cost_estimate=cost(1, 1024),
+                name="stack",
+            )(*near)
+        ]
+        for d in range(1, chips):
+            pieces.append(
+                lax.ppermute(pieces[0], ctx[:-1], [(i, i ^ d) for i in range(chips)])
+            )
+        first, sheet = lax.optimization_barrier((pieces[0], sheet))
+        pieces[0] = first
+
     grads = pl.pallas_call(
         lambda *refs: gradient_kernel(ctx, count, len(recv), len(stats), *refs),
         out_shape=jax.ShapeDtypeStruct((3 * rows + nf2 * rows // LANES, LANES), bf16),

time: 92.5 us -> 71.6 us (0.77)
  waiting for transfers between devices: 41.8 us -> 18.9 us
  starting transfers between devices: 16.4 us -> 19.9 us
    ppermute x3, waiting for transfers between devices: 27.3 us -> 2.84 us  [per_device(): stats.append(lax.ppermute(held, name, swap))]
    ppermute x3, waiting for transfers between devices: 0.01 us -> 4.21 us  [per_device(): lax.ppermute(pieces[0], ctx[:-1], [(i, i ^ d) for i in range(chips)])]
    ppermute x3, starting transfers between devices: 4.67 us -> 8.19 us  [per_device(): lax.ppermute(outs[0], 'tp', [(z, z ^ t) for z in range(heads)])]
    ppermute x3, waiting for transfers between devices: 5.73 us -> 3.57 us  [per_device(): lax.ppermute(sends[d], ctx[:-1], [(i, i ^ d) for i in range(chips)])]
    ppermute x3, starting transfers between devices: 5 us -> 3.49 us  [per_device(): lax.ppermute(sends[d], ctx[:-1], [(i, i ^ d) for i in range(chips)])]
    ppermute x3, starting transfers between devices: 1.56 us -> 3.03 us  [per_device(): stats.append(lax.ppermute(held, name, swap))]
    pallas_call x2 -> x1, Pallas kernels: 3.97 us -> 3.14 us  [per_device(): pl.pallas_call(partial(project_kernel, ctx, len(packs)), out_shape=packs...]
  transfers between devices with their start and end apart: 20 -> 20, of which waited for: 7 -> 8; matrix products, arithmetic and copies ran while one was open for 0% -> 0% of each run, Pallas kernels for 10% -> 8%
where the time goes in v12:
time: 71.6 us; the launch traced here: 71.4 us
  starting transfers between devices  19.9 us (28%)
  waiting for transfers between devices  18.9 us (26%)
  blocking collectives  18.9 us (26%)
  Pallas kernels  13 us (18%)
    all_gather x1, blocking collectives, per_device(): grads = lax.all_gather(grads, 'tp')  18.9 us
    ppermute x3, starting transfers between devices, per_device(): lax.ppermute(outs[0], 'tp', [(z, z ^ t) for z in range(heads)])  8.19 us
    ppermute x3, waiting for transfers between devices, per_device(): lax.ppermute(outs[0], 'tp', [(z, z ^ t) for z in range(heads)])  6.39 us
    ppermute x3, waiting for transfers between devices, per_device(): lax.ppermute(pieces[0], ctx[:-1], [(i, i ^ d) for i in range(chips)])  4.21 us
    pallas_call x2, Pallas kernels, columns_of(): pl.pallas_call(partial(columns_kernel, ctx, side), out_shape=jax.ShapeDty...  3.81 us
    pallas_call x1, Pallas kernels, per_device(): pl.pallas_call(lambda *refs: gradient_kernel(ctx, count, len(recv), len(s...  3.62 us
    ppermute x3, waiting for transfers between devices, per_device(): lax.ppermute(sends[d], ctx[:-1], [(i, i ^ d) for i in range(chips)])  3.57 us
    ppermute x3, starting transfers between devices, per_device(): lax.ppermute(pieces[0], ctx[:-1], [(i, i ^ d) for i in range(chips)])  3.55 us
  transfers between devices with their start and end apart: 20, of which 8 were waited for; matrix products, arithmetic and copies ran while one was open for 0% of the time, Pallas kernels for 8%

profile of v12, /device:TPU:0, one launch (start us, length us, event | category | flops | bytes accessed | tf_op | source)
XLA Modules:
  0.0 71.4 jit_solution(4849747583420082250)
XLA Ops:
  0.6 3.1 %project.1 = (bf16[832,128]{1,0:T(8,128)(2,1)S(1)}, bf16[560,128]{1,0:T(8,128)(2,1)S(1)}, bf16[560,128]{1,0:T(8,128)(2,1)S(1)}, bf16[560,128]{1,0:T(8,128)(2,1)S...) custom-call(bf16[256,2048]{1,0:T(8,128)(2,1)} %tok_hbm.1, ...), custom_call_target="tpu_custom_call" | custom-call | flops 1 | bytes 1024 | tf_op jit(solution)/shard_map/project/pallas_call | solution.py:511
  3.8 3.1 %collective-permute-start.7 = (bf16[832,128]{1,0:T(8,128)(2,1)S(1)}, bf16[832,128]{1,0:T(8,128)(2,1)S(1)}, u32[]{:S(2)}, u32[]{:S(2)}) collective-permute-start(bf16[832,128]{1,0:T(8,128)(2,1)S(1)} %get-tuple-element.38), channel_id=1, source_target_pairs={{0,1},{1,0},{2,3},{3,2},{4,5},{5,4},{6,7},{7,6},{8,9},{9,8},{10,11... | collective-permute-start | bytes 638984 | tf_op jit(solution)/shard_map/ppermute | solution.py:551
  6.9 1.5 %collective-permute-start.1 = (bf16[560,128]{1,0:T(8,128)(2,1)S(1)}, bf16[560,128]{1,0:T(8,128)(2,1)S(1)}, u32[]{:S(2)}, u32[]{:S(2)}) collective-permute-start(bf16[560,128]{1,0:T(8,128)(2,1)S(1)} %get-tuple-element.35), channel_id=1, source_target_pairs={{0,8},{8,0},{16,24},{24,16},{1,9},{9,1},{17,25},{25,17},{2,10},{10... | collective-permute-start | bytes 430088 | tf_op jit(solution)/shard_map/ppermute | solution.py:541
  8.4 1.5 %collective-permute-start.3 = (bf16[560,128]{1,0:T(8,128)(2,1)S(1)}, bf16[560,128]{1,0:T(8,128)(2,1)S(1)}, u32[]{:S(2)}, u32[]{:S(2)}) collective-permute-start(bf16[560,128]{1,0:T(8,128)(2,1)S(1)} %get-tuple-element.36), channel_id=1, source_target_pairs={{0,16},{8,24},{16,0},{24,8},{1,17},{9,25},{17,1},{25,9},{2,18},{10... | collective-permute-start | bytes 430088 | tf_op jit(solution)/shard_map/ppermute | solution.py:541
  9.9 0.5 collective-permute-start.5
  10.4 2.6 %collective-permute-start.8 = (bf16[832,128]{1,0:T(8,128)(2,1)S(1)}, bf16[832,128]{1,0:T(8,128)(2,1)S(1)}, u32[]{:S(2)}, u32[]{:S(2)}) collective-permute-start(bf16[832,128]{1,0:T(8,128)(2,1)S(1)} %get-tuple-element.38), channel_id=1, source_target_pairs={{0,2},{1,3},{2,0},{3,1},{4,6},{5,7},{6,4},{7,5},{8,10},{9,11},{10,... | collective-permute-start | bytes 638984 | tf_op jit(solution)/shard_map/ppermute | solution.py:551
  13.0 0.0 collective-permute-done.1.refs_1_
  13.0 0.0 collective-permute-start
  13.0 3.6 %collective-permute-done.3.refs_3_ = bf16[560,128]{1,0:T(8,128)(2,1)S(1)} collective-permute-done((bf16[560,128]{1,0:T(8,128)(2,1)S(1)}, bf16[560,128]{1,0:T(8,128)(2,1)S(1)}, u32[]{:S(2)}, u32[]{:S(2)}) %collective-permute-start.3) | collective-permute-done | bytes 143392 | tf_op jit(solution)/shard_map/ppermute | solution.py:541
  16.5 0.0 collective-permute-start.2
  16.5 0.0 collective-permute-done.5.refs_5_
  16.5 0.5 collective-permute-start.4
  17.0 0.0 collective-permute-done.7.refs_0_
  17.0 0.1 collective-permute-start.6
  17.1 4.6 %collective-permute-done.8.refs_1_ = bf16[832,128]{1,0:T(8,128)(2,1)S(1)} collective-permute-done((bf16[832,128]{1,0:T(8,128)(2,1)S(1)}, bf16[832,128]{1,0:T(8,128)(2,1)S(1)}, u32[]{:S(2)}, u32[]{:S(2)}) %collective-permute-start.8) | collective-permute-done | bytes 213024 | tf_op jit(solution)/shard_map/ppermute | solution.py:551
  21.7 0.0 collective-permute-done.refs_0_
  21.7 0.0 collective-permute-done.2.refs_2_
  21.7 0.0 collective-permute-done.4.refs_4_
  21.7 0.0 collective-permute-done.6.refs_6_
  21.7 2.4 %query_side.1 = (bf16[256,128]{1,0:T(8,128)(2,1)}, f32[8,256]{1,0:T(8,128)S(1)}, f32[256,128]{1,0:T(8,128)S(1)}) custom-call(bf16[560,128]{1,0:T(8,128)(2,1)S(1)} %collective-permute-done.refs_0_, bf16[560,128]{1,0:T(8,128)(2,1)S(1)} %collective-permute-done.1.refs_1_, bf16[560,128]{1,0:T(8,128)(2,1)S(1)} %collective-permute-done.2.refs_2_, ...), custom_call_target="tpu_custom_call" | custom-call | flops 1 | bytes 1024 | tf_op jit(solution)/shard_map/query_side/pallas_call | solution.py:556
  24.1 0.0 collective-permute-start.10
  24.1 2.5 %collective-permute-start.9 = (bf16[832,128]{1,0:T(8,128)(2,1)S(1)}, bf16[832,128]{1,0:T(8,128)(2,1)S(1)}, u32[]{:S(2)}, u32[]{:S(2)}) collective-permute-start(bf16[832,128]{1,0:T(8,128)(2,1)S(1)} %get-tuple-element.38), channel_id=1, source_target_pairs={{0,3},{1,2},{2,1},{3,0},{4,7},{5,6},{6,5},{7,4},{8,11},{9,10},{10,... | collective-permute-start | bytes 638984 | tf_op jit(solution)/shard_map/ppermute | solution.py:551
  26.6 0.0 collective-permute-done.10.refs_8_
  26.7 1.5 %collective-permute-start.11 = (f32[16,256]{1,0:T(8,128)S(1)}, f32[16,256]{1,0:T(8,128)S(1)}, u32[]{:S(2)}, u32[]{:S(2)}) collective-permute-start(f32[16,256]{1,0:T(8,128)S(1)} %pad_maximum_fusion.1), channel_id=1, source_target_pairs={{0,8},{8,0},{1,9},{9,1},{2,10},{10,2},{3,11},{11,3},{4,12},{12,4},... | collective-permute-start | bytes 49160 | tf_op jit(solution)/shard_map/ppermute | solution.py:577
  28.2 2.2 %collective-permute-done.11.refs_9_ = f32[16,256]{1,0:T(8,128)S(1)} collective-permute-done((f32[16,256]{1,0:T(8,128)S(1)}, f32[16,256]{1,0:T(8,128)S(1)}, u32[]{:S(2)}, u32[]{:S(2)}) %collective-permute-start.11) | collective-permute-done | bytes 16416 | tf_op jit(solution)/shard_map/ppermute | solution.py:577
  30.4 1.5 %collective-permute-start.12 = (f32[32,256]{1,0:T(8,128)S(1)}, f32[32,256]{1,0:T(8,128)S(1)}, u32[]{:S(2)}, u32[]{:S(2)}) collective-permute-start(f32[32,256]{1,0:T(8,128)S(1)} %pad_maximum_fusion), channel_id=1, source_target_pairs={{0,16},{16,0},{1,17},{17,1},{2,18},{18,2},{3,19},{19,3},{4,20},{20... | collective-permute-start | bytes 98312 | tf_op jit(solution)/shard_map/ppermute | solution.py:577
  31.9 1.8 %collective-permute-done.9.refs_2_ = bf16[832,128]{1,0:T(8,128)(2,1)S(1)} collective-permute-done((bf16[832,128]{1,0:T(8,128)(2,1)S(1)}, bf16[832,128]{1,0:T(8,128)(2,1)S(1)}, u32[]{:S(2)}, u32[]{:S(2)}) %collective-permute-start.9) | collective-permute-done | bytes 213024 | tf_op jit(solution)/shard_map/ppermute | solution.py:551
  33.7 0.6 collective-permute-done.12.refs_10_
  34.4 1.6 %collective-permute-start.13 = (bf16[3,832,128]{2,1,0:T(8,128)(2,1)S(1)}, bf16[3,832,128]{2,1,0:T(8,128)(2,1)S(1)}, u32[]{:S(2)}, u32[]{:S(2)}) collective-permute-start(bf16[3,832,128]{2,1,0:T(8,128)(2,1)S(1)} %stack.1.rest_0_), channel_id=1, source_target_pairs={{0,8},{8,0},{16,24},{24,16},{1,9},{9,1},{17,25},{25,17},{2,10},{10... | collective-permute-start | bytes 1916936 | tf_op jit(solution)/shard_map/ppermute | solution.py:596
  35.9 1.5 %collective-permute-start.14 = (bf16[3,832,128]{2,1,0:T(8,128)(2,1)S(1)}, bf16[3,832,128]{2,1,0:T(8,128)(2,1)S(1)}, u32[]{:S(2)}, u32[]{:S(2)}) collective-permute-start(bf16[3,832,128]{2,1,0:T(8,128)(2,1)S(1)} %stack.1.rest_0_), channel_id=1, source_target_pairs={{0,16},{8,24},{16,0},{24,8},{1,17},{9,25},{17,1},{25,9},{2,18},{10... | collective-permute-start | bytes 1916936 | tf_op jit(solution)/shard_map/ppermute | solution.py:596
  37.4 0.5 collective-permute-start.15
  37.9 3.6 %gradients.1 = bf16[832,128]{1,0:T(8,128)(2,1)S(1)} custom-call(bf16[560,128]{1,0:T(8,128)(2,1)S(1)} %collective-permute-done.refs_0_, bf16[560,128]{1,0:T(8,128)(2,1)S(1)} %collective-permute-done.1.refs_1_, bf16[560,128]{1,0:T(8,128)(2,1)S(1)} %collective-permute-done.2.refs_2_, bf16[560,128]{1,0:T(8,128)(2,1)S(1)} %collective-permute-done.3.refs_3_, ...), custom_call_target="tpu_custom_call" | custom-call | flops 1 | bytes 1024 | tf_op jit(solution)/shard_map/gradients/pallas_call | solution.py:601
  41.5 18.9 %all-gather = bf16[3328,128]{1,0:T(8,128)(2,1)S(1)} all-gather(bf16[832,128]{1,0:T(8,128)(2,1)S(1)} %gradients.1), channel_id=2, replica_groups=mesh['half0'=2,'half1'=2,'core'=2,'tp'=4] {'tp'}, dimensions={0}, use_global_device_ids=true | all-gather | bytes 1064960 | tf_op jit(solution)/shard_map/all_gather | solution.py:616
  60.5 0.0 collective-permute-done.13.rest_1_
  60.5 4.2 %collective-permute-done.14.rest_2_ = bf16[3,832,128]{2,1,0:T(8,128)(2,1)S(1)} collective-permute-done((bf16[3,832,128]{2,1,0:T(8,128)(2,1)S(1)}, bf16[3,832,128]{2,1,0:T(8,128)(2,1)S(1)}, u32[]{:S(2)}, u32[]{:S(2)}) %collective-permute-start.14) | collective-permute-done | bytes 639008 | tf_op jit(solution)/shard_map/ppermute | solution.py:596
  64.7 0.0 collective-permute-done.15.rest_3_
  64.7 0.0 collective-permute-start.16
  64.7 0.5 collective-permute-start.17
  65.2 0.0 collective-permute-start.18
  65.2 0.5 collective-permute-start.19
  65.7 1.9 %columns.2.rest_4_ = bf16[256,2048]{1,0:T(8,128)(2,1)} custom-call(bf16[4,832,128]{2,1,0:T(8,128)(2,1)S(1)} %bitcast.3, bf16[2048,256]{1,0:T(8,128)(2,1)S(1)} %get-tuple-element.59.ww_ref, bf16[2048,128]{1,0:T(8,128)(2,1)S(1)} %get-tuple-element.60.vw_ref, bf16[32,2048]{1,0:T(8,128)(2,1)S(1)} %get-tuple-element.61.fw_ref, ...), custom_call_target="tpu_custom_call" | custom-call | flops 872415232 | bytes 3407872 | tf_op jit(solution)/shard_map/columns/pallas_call | solution.py:621
  67.6 0.0 collective-permute-done.16.rest_0_
  67.6 0.0 collective-permute-done.17.rest_1_
  67.7 0.9 %collective-permute-done.18.rest_2_ = bf16[3,832,128]{2,1,0:T(8,128)(2,1)S(1)} collective-permute-done((bf16[3,832,128]{2,1,0:T(8,128)(2,1)S(1)}, bf16[3,832,128]{2,1,0:T(8,128)(2,1)S(1)}, u32[]{:S(2)}, u32[]{:S(2)}) %collective-permute-start.18) | collective-permute-done | bytes 639008 | tf_op jit(solution)/shard_map/ppermute | solution.py:618
  68.6 0.9 %collective-permute-done.19.rest_3_ = bf16[3,832,128]{2,1,0:T(8,128)(2,1)S(1)} collective-permute-done((bf16[3,832,128]{2,1,0:T(8,128)(2,1)S(1)}, bf16[3,832,128]{2,1,0:T(8,128)(2,1)S(1)}, u32[]{:S(2)}, u32[]{:S(2)}) %collective-permute-start.19) | collective-permute-done | bytes 639008 | tf_op jit(solution)/shard_map/ppermute | solution.py:618
  69.5 1.9 %columns.3 = bf16[256,2048]{1,0:T(8,128)(2,1)} custom-call(bf16[4,832,128]{2,1,0:T(8,128)(2,1)S(1)} %bitcast.4, bf16[2048,256]{1,0:T(8,128)(2,1)S(1)} %get-tuple-element.59.ww_ref, bf16[2048,128]{1,0:T(8,128)(2,1)S(1)} %get-tuple-element.60.vw_ref, bf16[32,2048]{1,0:T(8,128)(2,1)S(1)} %get-tuple-element.61.fw_ref, ...), custom_call_target="tpu_custom_call", output_to_operand_aliasing={{}: (8, {})} | custom-call | flops 872415232 | bytes 3407872 | tf_op jit(solution)/shard_map/columns/pallas_call | solution.py:621
  (3 shorter events, 0.0 us)
Async XLA Ops:
  3.8 13.3 %collective-permute-start.7 = (bf16[832,128]{1,0:T(8,128)(2,1)S(1)}, bf16[832,128]{1,0:T(8,128)(2,1)S(1)}, u32[]{:S(2)}, u32[]{:S(2)}) collective-permute-start(bf16[832,128]{1,0:T(8,128)(2,1)S(1)} %get-tuple-element.38), channel_id=1, source_target_pairs={{0,1},{1,0},{2,3},{3,2},{4,5},{5,4},{6,7},{7,6},{8,9},{9,8},{10,11... | collective-permute-start | bytes 638984 | tf_op jit(solution)/shard_map/ppermute | solution.py:551
  6.9 6.1 %collective-permute-start.1 = (bf16[560,128]{1,0:T(8,128)(2,1)S(1)}, bf16[560,128]{1,0:T(8,128)(2,1)S(1)}, u32[]{:S(2)}, u32[]{:S(2)}) collective-permute-start(bf16[560,128]{1,0:T(8,128)(2,1)S(1)} %get-tuple-element.35), channel_id=1, source_target_pairs={{0,8},{8,0},{16,24},{24,16},{1,9},{9,1},{17,25},{25,17},{2,10},{10... | collective-permute-start | bytes 430088 | tf_op jit(solution)/shard_map/ppermute | solution.py:541
  8.4 8.2 %collective-permute-start.3 = (bf16[560,128]{1,0:T(8,128)(2,1)S(1)}, bf16[560,128]{1,0:T(8,128)(2,1)S(1)}, u32[]{:S(2)}, u32[]{:S(2)}) collective-permute-start(bf16[560,128]{1,0:T(8,128)(2,1)S(1)} %get-tuple-element.36), channel_id=1, source_target_pairs={{0,16},{8,24},{16,0},{24,8},{1,17},{9,25},{17,1},{25,9},{2,18},{10... | collective-permute-start | bytes 430088 | tf_op jit(solution)/shard_map/ppermute | solution.py:541
  9.9 6.7 %collective-permute-start.5 = (bf16[560,128]{1,0:T(8,128)(2,1)S(1)}, bf16[560,128]{1,0:T(8,128)(2,1)S(1)}, u32[]{:S(2)}, u32[]{:S(2)}) collective-permute-start(bf16[560,128]{1,0:T(8,128)(2,1)S(1)} %get-tuple-element.37), channel_id=1, source_target_pairs={{0,24},{8,16},{16,8},{24,0},{1,25},{9,17},{17,9},{25,1},{2,26},{10... | collective-permute-start | bytes 430088 | tf_op jit(solution)/shard_map/ppermute | solution.py:541
  10.4 11.4 %collective-permute-start.8 = (bf16[832,128]{1,0:T(8,128)(2,1)S(1)}, bf16[832,128]{1,0:T(8,128)(2,1)S(1)}, u32[]{:S(2)}, u32[]{:S(2)}) collective-permute-start(bf16[832,128]{1,0:T(8,128)(2,1)S(1)} %get-tuple-element.38), channel_id=1, source_target_pairs={{0,2},{1,3},{2,0},{3,1},{4,6},{5,7},{6,4},{7,5},{8,10},{9,11},{10,... | collective-permute-start | bytes 638984 | tf_op jit(solution)/shard_map/ppermute | solution.py:551
  13.0 8.8 %collective-permute-start = (bf16[560,128]{1,0:T(8,128)(2,1)S(1)}, bf16[560,128]{1,0:T(8,128)(2,1)S(1)}, u32[]{:S(2)}, u32[]{:S(2)}) collective-permute-start(bf16[560,128]{1,0:T(8,128)(2,1)S(1)} %get-tuple-element.34), channel_id=1, source_target_pairs={{0,4},{4,0},{1,5},{5,1},{2,6},{6,2},{3,7},{7,3},{8,12},{12,8},{9,1... | collective-permute-start | bytes 430088 | tf_op jit(solution)/shard_map/ppermute | solution.py:542
  16.5 5.2 %collective-permute-start.2 = (bf16[560,128]{1,0:T(8,128)(2,1)S(1)}, bf16[560,128]{1,0:T(8,128)(2,1)S(1)}, u32[]{:S(2)}, u32[]{:S(2)}) collective-permute-start(bf16[560,128]{1,0:T(8,128)(2,1)S(1)} %collective-permute-done.1.refs_1_), channel_id=1, source_target_pairs={{0,4},{4,0},{1,5},{5,1},{2,6},{6,2},{3,7},{7,3},{8,12},{12,8},{9,1... | collective-permute-start | bytes 430088 | tf_op jit(solution)/shard_map/ppermute | solution.py:544
  16.5 5.2 %collective-permute-start.4 = (bf16[560,128]{1,0:T(8,128)(2,1)S(1)}, bf16[560,128]{1,0:T(8,128)(2,1)S(1)}, u32[]{:S(2)}, u32[]{:S(2)}) collective-permute-start(bf16[560,128]{1,0:T(8,128)(2,1)S(1)} %collective-permute-done.3.refs_3_), channel_id=1, source_target_pairs={{0,4},{4,0},{1,5},{5,1},{2,6},{6,2},{3,7},{7,3},{8,12},{12,8},{9,1... | collective-permute-start | bytes 430088 | tf_op jit(solution)/shard_map/ppermute | solution.py:544
  17.0 4.7 %collective-permute-start.6 = (bf16[560,128]{1,0:T(8,128)(2,1)S(1)}, bf16[560,128]{1,0:T(8,128)(2,1)S(1)}, u32[]{:S(2)}, u32[]{:S(2)}) collective-permute-start(bf16[560,128]{1,0:T(8,128)(2,1)S(1)} %collective-permute-done.5.refs_5_), channel_id=1, source_target_pairs={{0,4},{4,0},{1,5},{5,1},{2,6},{6,2},{3,7},{7,3},{8,12},{12,8},{9,1... | collective-permute-start | bytes 430088 | tf_op jit(solution)/shard_map/ppermute | solution.py:544
  24.1 2.5 %collective-permute-start.10 = (f32[8,256]{1,0:T(8,128)S(1)}, f32[8,256]{1,0:T(8,128)S(1)}, u32[]{:S(2)}, u32[]{:S(2)}) collective-permute-start(f32[8,256]{1,0:T(8,128)S(1)} %get-tuple-element.53.refs_7_), channel_id=1, source_target_pairs={{0,4},{4,0},{1,5},{5,1},{2,6},{6,2},{3,7},{7,3},{8,12},{12,8},{9,1... | collective-permute-start | bytes 24584 | tf_op jit(solution)/shard_map/ppermute | solution.py:577
  24.1 9.6 %collective-permute-start.9 = (bf16[832,128]{1,0:T(8,128)(2,1)S(1)}, bf16[832,128]{1,0:T(8,128)(2,1)S(1)}, u32[]{:S(2)}, u32[]{:S(2)}) collective-permute-start(bf16[832,128]{1,0:T(8,128)(2,1)S(1)} %get-tuple-element.38), channel_id=1, source_target_pairs={{0,3},{1,2},{2,1},{3,0},{4,7},{5,6},{6,5},{7,4},{8,11},{9,10},{10,... | collective-permute-start | bytes 638984 | tf_op jit(solution)/shard_map/ppermute | solution.py:551
  26.7 3.7 %collective-permute-start.11 = (f32[16,256]{1,0:T(8,128)S(1)}, f32[16,256]{1,0:T(8,128)S(1)}, u32[]{:S(2)}, u32[]{:S(2)}) collective-permute-start(f32[16,256]{1,0:T(8,128)S(1)} %pad_maximum_fusion.1), channel_id=1, source_target_pairs={{0,8},{8,0},{1,9},{9,1},{2,10},{10,2},{3,11},{11,3},{4,12},{12,4},... | collective-permute-start | bytes 49160 | tf_op jit(solution)/shard_map/ppermute | solution.py:577
  30.4 3.9 %collective-permute-start.12 = (f32[32,256]{1,0:T(8,128)S(1)}, f32[32,256]{1,0:T(8,128)S(1)}, u32[]{:S(2)}, u32[]{:S(2)}) collective-permute-start(f32[32,256]{1,0:T(8,128)S(1)} %pad_maximum_fusion), channel_id=1, source_target_pairs={{0,16},{16,0},{1,17},{17,1},{2,18},{18,2},{3,19},{19,3},{4,20},{20... | collective-permute-start | bytes 98312 | tf_op jit(solution)/shard_map/ppermute | solution.py:577
  34.4 26.1 %collective-permute-start.13 = (bf16[3,832,128]{2,1,0:T(8,128)(2,1)S(1)}, bf16[3,832,128]{2,1,0:T(8,128)(2,1)S(1)}, u32[]{:S(2)}, u32[]{:S(2)}) collective-permute-start(bf16[3,832,128]{2,1,0:T(8,128)(2,1)S(1)} %stack.1.rest_0_), channel_id=1, source_target_pairs={{0,8},{8,0},{16,24},{24,16},{1,9},{9,1},{17,25},{25,17},{2,10},{10... | collective-permute-start | bytes 1916936 | tf_op jit(solution)/shard_map/ppermute | solution.py:596
  35.9 28.7 %collective-permute-start.14 = (bf16[3,832,128]{2,1,0:T(8,128)(2,1)S(1)}, bf16[3,832,128]{2,1,0:T(8,128)(2,1)S(1)}, u32[]{:S(2)}, u32[]{:S(2)}) collective-permute-start(bf16[3,832,128]{2,1,0:T(8,128)(2,1)S(1)} %stack.1.rest_0_), channel_id=1, source_target_pairs={{0,16},{8,24},{16,0},{24,8},{1,17},{9,25},{17,1},{25,9},{2,18},{10... | collective-permute-start | bytes 1916936 | tf_op jit(solution)/shard_map/ppermute | solution.py:596
  37.4 27.2 %collective-permute-start.15 = (bf16[3,832,128]{2,1,0:T(8,128)(2,1)S(1)}, bf16[3,832,128]{2,1,0:T(8,128)(2,1)S(1)}, u32[]{:S(2)}, u32[]{:S(2)}) collective-permute-start(bf16[3,832,128]{2,1,0:T(8,128)(2,1)S(1)} %stack.1.rest_0_), channel_id=1, source_target_pairs={{0,24},{8,16},{16,8},{24,0},{1,25},{9,17},{17,9},{25,1},{2,26},{10... | collective-permute-start | bytes 1916936 | tf_op jit(solution)/shard_map/ppermute | solution.py:596
  64.7 2.9 %collective-permute-start.16 = (bf16[3,832,128]{2,1,0:T(8,128)(2,1)S(1)}, bf16[3,832,128]{2,1,0:T(8,128)(2,1)S(1)}, u32[]{:S(2)}, u32[]{:S(2)}) collective-permute-start(bf16[3,832,128]{2,1,0:T(8,128)(2,1)S(1)} %stack.1.rest_0_), channel_id=1, source_target_pairs={{0,4},{4,0},{1,5},{5,1},{2,6},{6,2},{3,7},{7,3},{8,12},{12,8},{9,1... | collective-permute-start | bytes 1916936 | tf_op jit(solution)/shard_map/ppermute | solution.py:618
  64.7 3.0 %collective-permute-start.17 = (bf16[3,832,128]{2,1,0:T(8,128)(2,1)S(1)}, bf16[3,832,128]{2,1,0:T(8,128)(2,1)S(1)}, u32[]{:S(2)}, u32[]{:S(2)}) collective-permute-start(bf16[3,832,128]{2,1,0:T(8,128)(2,1)S(1)} %collective-permute-done.13.rest_1_), channel_id=1, source_target_pairs={{0,4},{4,0},{1,5},{5,1},{2,6},{6,2},{3,7},{7,3},{8,12},{12,8},{9,1... | collective-permute-start | bytes 1916936 | tf_op jit(solution)/shard_map/ppermute | solution.py:618
  65.2 3.4 %collective-permute-start.18 = (bf16[3,832,128]{2,1,0:T(8,128)(2,1)S(1)}, bf16[3,832,128]{2,1,0:T(8,128)(2,1)S(1)}, u32[]{:S(2)}, u32[]{:S(2)}) collective-permute-start(bf16[3,832,128]{2,1,0:T(8,128)(2,1)S(1)} %collective-permute-done.14.rest_2_), channel_id=1, source_target_pairs={{0,4},{4,0},{1,5},{5,1},{2,6},{6,2},{3,7},{7,3},{8,12},{12,8},{9,1... | collective-permute-start | bytes 1916936 | tf_op jit(solution)/shard_map/ppermute | solution.py:618
  65.2 4.3 %collective-permute-start.19 = (bf16[3,832,128]{2,1,0:T(8,128)(2,1)S(1)}, bf16[3,832,128]{2,1,0:T(8,128)(2,1)S(1)}, u32[]{:S(2)}, u32[]{:S(2)}) collective-permute-start(bf16[3,832,128]{2,1,0:T(8,128)(2,1)S(1)} %collective-permute-done.15.rest_3_), channel_id=1, source_target_pairs={{0,4},{4,0},{1,5},{5,1},{2,6},{6,2},{3,7},{7,3},{8,12},{12,8},{9,1... | collective-permute-start | bytes 1916936 | tf_op jit(solution)/shard_map/ppermute | solution.py:618

commit v13 on v12

--- a/solution.py
+++ b/solution.py
@@ -412,20 +412,23 @@
     feat_ref[...] = jnp.transpose(dft.astype(f32)).astype(bf16)
 
 
-def columns_kernel(ctx, side, grad_ref, ww_ref, vw_ref, fw_ref, *rest):
-    pieces = rest[: ww_ref.shape[0] // (4 * LANES)]
-    out_ref, cat_ref, feat_ref, tile_ref, sems = rest[-5:]
+def cat_kernel(grad_ref, cat_ref, feat_ref):
     heads = grad_ref.shape[0]
+    head = lax.axis_index("tp")
+    order = [head] + [jnp.bitwise_xor(head, t) for t in range(1, heads)]
+    gather_rows(grad_ref, order, cat_ref, feat_ref)
+
+
+def columns_kernel(ctx, distances, cat_ref, feat_ref, ww_ref, vw_ref, fw_ref, *rest):
+    pieces = rest[: len(distances)]
+    out_ref, tile_ref, sems = rest[-3:]
     nf2 = fw_ref.shape[0]
+    heads = feat_ref.shape[1] // nf2
     tile = 2 * LANES
-    head, me = lax.axis_index("tp"), block_index(ctx)
-    gather_rows(
-        grad_ref, [head] + [jnp.bitwise_xor(head, t) for t in range(1, heads)], cat_ref, feat_ref
-    )
+    me = block_index(ctx)
     copies = []
-    for d, ref in enumerate(pieces):
-        at = pl.multiple_of(jnp.bitwise_xor(me, 2 * d + side) * tile, tile)
-        part = pl.ds(at, tile)
+    for n, (e, ref) in enumerate(zip(distances, pieces)):
+        part = pl.ds(pl.multiple_of(jnp.bitwise_xor(me, e) * tile, tile), tile)
         main = [ww_ref[part, :], vw_ref[part, :]]
         main += [
             ref[t, m * tile : (m + 1) * tile, :] for t in range(heads - 1) for m in range(3)
@@ -433,8 +436,8 @@
         feats = [fw_ref[:, part]] + [wide(ref.at[t], 3 * tile, nf2) for t in range(heads - 1)]
         total = nt(cat_ref[...], jnp.concatenate(main, axis=1))
         total += nn(feat_ref[...], jnp.concatenate(feats, axis=0))
-        tile_ref[d] = total.astype(bf16)
-        copies.append(pltpu.make_async_copy(tile_ref.at[d], out_ref.at[:, part], sems.at[d]))
+        tile_ref[n] = total.astype(bf16)
+        copies.append(pltpu.make_async_copy(tile_ref.at[n], out_ref.at[:, part], sems.at[n]))
         copies[-1].start()
     for copy in copies:
         copy.wait()
@@ -551,7 +554,7 @@
             lax.ppermute(outs[0], "tp", [(z, z ^ t) for z in range(heads)])
             for t in range(1, heads)
         ]
-        near[:2], own = lax.optimization_barrier((near[:2], own))
+        near[1], own = lax.optimization_barrier((near[1], own))
 
     attended, stat, sheet = pl.pallas_call(
         lambda *refs: query_kernel(ctx, count, *refs),
@@ -573,6 +576,8 @@
     )(*recv, own, query, feat, cum)
     stats = [stat]
     for name in reversed(ctx):
+        if spread and len(stats) == 2:
+            near, stats = lax.optimization_barrier((near, stats))
         held = stats[0] if len(stats) == 1 else jnp.concatenate(stats, axis=0)
         stats.append(lax.ppermute(held, name, swap))
     if count > 8:
@@ -613,30 +618,51 @@
         weights = lax.all_gather(weights, "tp")
         return (attended, merge(lax.all_gather(grads, "tp"), weights, rows, dim))
 
+    swapped = {0: lax.ppermute(pieces[0], "core", swap)}
+    swapped[0], grads = lax.optimization_barrier((swapped[0], grads))
     grads = lax.all_gather(grads, "tp")
-    pieces, grads = lax.optimization_barrier((pieces, grads))
-    swapped = [lax.ppermute(p, "core", swap) for p in pieces]
-
-    def columns_of(side, pieces, before):
-        return pl.pallas_call(
-            partial(columns_kernel, ctx, side),
-            out_shape=jax.ShapeDtypeStruct((rows, dim), bf16),
-            in_specs=[VMEM] * (4 + chips) + [ANY] * len(before),
-            out_specs=ANY,
-            scratch_shapes=[
-                pltpu.VMEM((rows, 3 * LANES * heads), bf16),
-                pltpu.VMEM((rows, nf2 * heads), bf16),
-                pltpu.VMEM((chips, rows, tile), bf16),
-                pltpu.SemaphoreType.DMA((chips,)),
-            ],
-            input_output_aliases={4 + chips: 0} if before else {},
-            compiler_params=params,
-            cost_estimate=cost(rows * dim * heads * columns, heads * dim * columns),
-            name="columns",
-        )(grads, ww, vw, fw, *pieces, *before)
-
-    first = columns_of(0, pieces, [])
-    return (attended, columns_of(1, swapped, [first]))
+    cat, feats = pl.pallas_call(
+        cat_kernel,
+        out_shape=[
+            jax.ShapeDtypeStruct((rows, 3 * LANES * heads), bf16),
+            jax.ShapeDtypeStruct((rows, nf2 * heads), bf16),
+        ],
+        in_specs=[VMEM],
+        out_specs=[VMEM] * 2,
+        compiler_params=params,
+        cost_estimate=cost(1, 1024),
+        name="cat",
+    )(grads)
+    total = []
+    groups = [(0, 1)]
+    for d in range(1, chips):
+        groups.append((2 * d - 1, 2 * d) if d > 1 else (2 * d,))
+    groups.append((2 * chips - 1,))
+    for d, distances in enumerate(groups):
+        if 0 < d < chips:
+            if d < 3:
+                late = slice(d, d + 1 if d == 1 else chips)
+                pieces[late], total = lax.optimization_barrier((pieces[late], total))
+            swapped[d] = lax.ppermute(pieces[d], "core", swap)
+        parts = [(swapped if e % 2 else pieces)[e // 2] for e in distances]
+        args = [cat, feats, ww, vw, fw, *parts, *total]
+        total = [
+            pl.pallas_call(
+                partial(columns_kernel, ctx, distances),
+                out_shape=jax.ShapeDtypeStruct((rows, dim), bf16),
+                in_specs=[VMEM] * (5 + len(parts)) + [ANY] * len(total),
+                out_specs=ANY,
+                scratch_shapes=[
+                    pltpu.VMEM((len(parts), rows, tile), bf16),
+                    pltpu.SemaphoreType.DMA((len(parts),)),
+                ],
+                input_output_aliases={len(args) - 1: 0} if total else {},
+                compiler_params=params,
+                cost_estimate=cost(1, 1024),
+                name="columns",
+            )(*args)
+        ]
+    return (attended, total[0])
 
 
 def solution(mesh):

time: 71.6 us -> 73.8 us (1.031)
  Pallas kernels: 13 us -> 15.7 us
  blocking collectives: 18.9 us -> 19.8 us
  starting transfers between devices: 19.9 us -> 19.1 us
    pallas_call x2 -> x6, Pallas kernels: 3.81 us -> 6.48 us  [the longest x5 6.27 us: per_device(): pl.pallas_call(partial(columns_kernel, ctx, distances), out_shape=jax.Sha...]
    ppermute x3, waiting for transfers between devices: 2.84 us -> 4.97 us  [per_device(): stats.append(lax.ppermute(held, name, swap))]
    ppermute x3, waiting for transfers between devices: 6.39 us -> 4.29 us  [per_device(): lax.ppermute(outs[0], 'tp', [(z, z ^ t) for z in range(heads)])]
    ppermute x4, waiting for transfers between devices: 1.88 us -> 0.2 us  [the longest x3 0.19 us: per_device(): swapped[d] = lax.ppermute(pieces[d], 'core', swap)]
    ppermute x3, waiting for transfers between devices: 0.01 us -> 1.36 us  [per_device(): recv[2 * d + 1] = lax.ppermute(recv[2 * d], 'core', swap)]
    ppermute x3, starting transfers between devices: 8.19 us -> 7.04 us  [per_device(): lax.ppermute(outs[0], 'tp', [(z, z ^ t) for z in range(heads)])]
    all_gather x1, blocking collectives: 18.9 us -> 19.8 us  [per_device(): grads = lax.all_gather(grads, 'tp')]
    ppermute x3, starting transfers between devices: 3.03 us -> 3.85 us  [per_device(): stats.append(lax.ppermute(held, name, swap))]
  transfers between devices with their start and end apart: 20 -> 20, of which waited for: 8 -> 10; matrix products, arithmetic and copies ran while one was open for 0% -> 0% of each run, Pallas kernels for 8% -> 15%
where the time goes in v13:
time: 73.8 us; the launch traced here: 73.7 us
  blocking collectives  19.8 us (27%)
  starting transfers between devices  19.1 us (26%)
  waiting for transfers between devices  18.3 us (25%)
  Pallas kernels  15.7 us (21%)
  between operations  0.75 us (1%)
    all_gather x1, blocking collectives, per_device(): grads = lax.all_gather(grads, 'tp')  19.8 us
    ppermute x3, starting transfers between devices, per_device(): lax.ppermute(outs[0], 'tp', [(z, z ^ t) for z in range(heads)])  7.04 us
    pallas_call x5, Pallas kernels, per_device(): pl.pallas_call(partial(columns_kernel, ctx, distances), out_shape=jax.Sha...  6.27 us
    ppermute x3, waiting for transfers between devices, per_device(): stats.append(lax.ppermute(held, name, swap))  4.97 us
    ppermute x3, waiting for transfers between devices, per_device(): lax.ppermute(outs[0], 'tp', [(z, z ^ t) for z in range(heads)])  4.29 us
    ppermute x3, waiting for transfers between devices, per_device(): lax.ppermute(sends[d], ctx[:-1], [(i, i ^ d) for i in range(chips)])  4.03 us
    ppermute x3, starting transfers between devices, per_device(): stats.append(lax.ppermute(held, name, swap))  3.85 us
    pallas_call x1, Pallas kernels, per_device(): pl.pallas_call(lambda *refs: gradient_kernel(ctx, count, len(recv), len(s...  3.6 us
  transfers between devices with their start and end apart: 20, of which 10 were waited for; matrix products, arithmetic and copies ran while one was open for 0% of the time, Pallas kernels for 15%

profile of v13, /device:TPU:0, one launch (start us, length us, event | category | flops | bytes accessed | tf_op | source)
XLA Modules:
  0.0 73.7 jit_solution(2396834595436584138)
XLA Ops:
  0.6 3.1 %project.1 = (bf16[832,128]{1,0:T(8,128)(2,1)S(1)}, bf16[560,128]{1,0:T(8,128)(2,1)S(1)}, bf16[560,128]{1,0:T(8,128)(2,1)S(1)}, bf16[560,128]{1,0:T(8,128)(2,1)S...) custom-call(bf16[256,2048]{1,0:T(8,128)(2,1)} %tok_hbm.1, ...), custom_call_target="tpu_custom_call" | custom-call | flops 1 | bytes 1024 | tf_op jit(solution)/shard_map/project/pallas_call | solution.py:514
  3.8 4.1 %collective-permute-start.7 = (bf16[832,128]{1,0:T(8,128)(2,1)S(1)}, bf16[832,128]{1,0:T(8,128)(2,1)S(1)}, u32[]{:S(2)}, u32[]{:S(2)}) collective-permute-start(bf16[832,128]{1,0:T(8,128)(2,1)S(1)} %get-tuple-element.46), channel_id=1, source_target_pairs={{0,2},{1,3},{2,0},{3,1},{4,6},{5,7},{6,4},{7,5},{8,10},{9,11},{10,... | collective-permute-start | bytes 638984 | tf_op jit(solution)/shard_map/ppermute | solution.py:554
  7.9 0.0 collective-permute-start
  7.9 1.5 %collective-permute-start.1 = (bf16[560,128]{1,0:T(8,128)(2,1)S(1)}, bf16[560,128]{1,0:T(8,128)(2,1)S(1)}, u32[]{:S(2)}, u32[]{:S(2)}) collective-permute-start(bf16[560,128]{1,0:T(8,128)(2,1)S(1)} %get-tuple-element.43), channel_id=1, source_target_pairs={{0,8},{8,0},{16,24},{24,16},{1,9},{9,1},{17,25},{25,17},{2,10},{10... | collective-permute-start | bytes 430088 | tf_op jit(solution)/shard_map/ppermute | solution.py:544
  9.4 1.5 %collective-permute-start.3 = (bf16[560,128]{1,0:T(8,128)(2,1)S(1)}, bf16[560,128]{1,0:T(8,128)(2,1)S(1)}, u32[]{:S(2)}, u32[]{:S(2)}) collective-permute-start(bf16[560,128]{1,0:T(8,128)(2,1)S(1)} %get-tuple-element.44), channel_id=1, source_target_pairs={{0,16},{8,24},{16,0},{24,8},{1,17},{9,25},{17,1},{25,9},{2,18},{10... | collective-permute-start | bytes 430088 | tf_op jit(solution)/shard_map/ppermute | solution.py:544
  10.9 0.5 collective-permute-start.5
  11.4 0.0 collective-permute-done.refs_0_
  11.4 1.4 %collective-permute-start.9 = (bf16[832,128]{1,0:T(8,128)(2,1)S(1)}, bf16[832,128]{1,0:T(8,128)(2,1)S(1)}, u32[]{:S(2)}, u32[]{:S(2)}) collective-permute-start(bf16[832,128]{1,0:T(8,128)(2,1)S(1)} %get-tuple-element.46), channel_id=1, source_target_pairs={{0,3},{1,2},{2,1},{3,0},{4,7},{5,6},{6,5},{7,4},{8,11},{9,10},{10,... | collective-permute-start | bytes 638984 | tf_op jit(solution)/shard_map/ppermute | solution.py:554
  12.7 1.7 %collective-permute-done.1.refs_1_ = bf16[560,128]{1,0:T(8,128)(2,1)S(1)} collective-permute-done((bf16[560,128]{1,0:T(8,128)(2,1)S(1)}, bf16[560,128]{1,0:T(8,128)(2,1)S(1)}, u32[]{:S(2)}, u32[]{:S(2)}) %collective-permute-start.1) | collective-permute-done | bytes 143392 | tf_op jit(solution)/shard_map/ppermute | solution.py:544
  14.4 1.6 %collective-permute-start.8 = (bf16[832,128]{1,0:T(8,128)(2,1)S(1)}, bf16[832,128]{1,0:T(8,128)(2,1)S(1)}, u32[]{:S(2)}, u32[]{:S(2)}) collective-permute-start(bf16[832,128]{1,0:T(8,128)(2,1)S(1)} %get-tuple-element.46), channel_id=1, source_target_pairs={{0,1},{1,0},{2,3},{3,2},{4,5},{5,4},{6,7},{7,6},{8,9},{9,8},{10,11... | collective-permute-start | bytes 638984 | tf_op jit(solution)/shard_map/ppermute | solution.py:554
  16.0 2.3 %collective-permute-done.3.refs_3_ = bf16[560,128]{1,0:T(8,128)(2,1)S(1)} collective-permute-done((bf16[560,128]{1,0:T(8,128)(2,1)S(1)}, bf16[560,128]{1,0:T(8,128)(2,1)S(1)}, u32[]{:S(2)}, u32[]{:S(2)}) %collective-permute-start.3) | collective-permute-done | bytes 143392 | tf_op jit(solution)/shard_map/ppermute | solution.py:544
  18.3 0.0 collective-permute-start.2
  18.3 0.0 collective-permute-done.5.refs_5_
  18.3 0.5 collective-permute-start.4
  18.9 4.3 %collective-permute-done.7.refs_1_ = bf16[832,128]{1,0:T(8,128)(2,1)S(1)} collective-permute-done((bf16[832,128]{1,0:T(8,128)(2,1)S(1)}, bf16[832,128]{1,0:T(8,128)(2,1)S(1)}, u32[]{:S(2)}, u32[]{:S(2)}) %collective-permute-start.7) | collective-permute-done | bytes 213024 | tf_op jit(solution)/shard_map/ppermute | solution.py:554
  23.1 0.0 collective-permute-start.6
  23.1 0.0 collective-permute-done.2.refs_2_
  23.1 0.0 collective-permute-done.4.refs_4_
  23.2 1.4 %collective-permute-done.6.refs_6_ = bf16[560,128]{1,0:T(8,128)(2,1)S(1)} collective-permute-done((bf16[560,128]{1,0:T(8,128)(2,1)S(1)}, bf16[560,128]{1,0:T(8,128)(2,1)S(1)}, u32[]{:S(2)}, u32[]{:S(2)}) %collective-permute-start.6) | collective-permute-done | bytes 143392 | tf_op jit(solution)/shard_map/ppermute | solution.py:547
  24.5 2.4 %query_side.1 = (bf16[256,128]{1,0:T(8,128)(2,1)}, f32[8,256]{1,0:T(8,128)S(1)}, f32[256,128]{1,0:T(8,128)S(1)}) custom-call(bf16[560,128]{1,0:T(8,128)(2,1)S(1)} %collective-permute-done.refs_0_, bf16[560,128]{1,0:T(8,128)(2,1)S(1)} %collective-permute-done.1.refs_1_, bf16[560,128]{1,0:T(8,128)(2,1)S(1)} %collective-permute-done.2.refs_2_, ...), custom_call_target="tpu_custom_call" | custom-call | flops 1 | bytes 1024 | tf_op jit(solution)/shard_map/query_side/pallas_call | solution.py:559
  26.9 0.1 collective-permute-start.10
  27.0 0.0 collective-permute-done.9.refs_2_
  27.0 0.0 collective-permute-done.8.refs_0_
  27.0 1.0 %collective-permute-done.10.refs_8_ = f32[8,256]{1,0:T(8,128)S(1)} collective-permute-done((f32[8,256]{1,0:T(8,128)S(1)}, f32[8,256]{1,0:T(8,128)S(1)}, u32[]{:S(2)}, u32[]{:S(2)}) %collective-permute-start.10) | collective-permute-done | bytes 8224 | tf_op jit(solution)/shard_map/ppermute | solution.py:582
  28.1 1.8 %collective-permute-start.11 = (f32[16,256]{1,0:T(8,128)S(1)}, f32[16,256]{1,0:T(8,128)S(1)}, u32[]{:S(2)}, u32[]{:S(2)}) collective-permute-start(f32[16,256]{1,0:T(8,128)S(1)} %pad_maximum_fusion.1), channel_id=1, source_target_pairs={{0,8},{8,0},{1,9},{9,1},{2,10},{10,2},{3,11},{11,3},{4,12},{12,4},... | collective-permute-start | bytes 49160 | tf_op jit(solution)/shard_map/ppermute | solution.py:582
  29.9 1.9 %collective-permute-done.11.refs_9_ = f32[16,256]{1,0:T(8,128)S(1)} collective-permute-done((f32[16,256]{1,0:T(8,128)S(1)}, f32[16,256]{1,0:T(8,128)S(1)}, u32[]{:S(2)}, u32[]{:S(2)}) %collective-permute-start.11) | collective-permute-done | bytes 16416 | tf_op jit(solution)/shard_map/ppermute | solution.py:582
  31.8 1.9 %collective-permute-start.12 = (f32[32,256]{1,0:T(8,128)S(1)}, f32[32,256]{1,0:T(8,128)S(1)}, u32[]{:S(2)}, u32[]{:S(2)}) collective-permute-start(f32[32,256]{1,0:T(8,128)S(1)} %pad_maximum_fusion), channel_id=1, source_target_pairs={{0,16},{16,0},{1,17},{17,1},{2,18},{18,2},{3,19},{19,3},{4,20},{20... | collective-permute-start | bytes 98312 | tf_op jit(solution)/shard_map/ppermute | solution.py:582
  33.7 2.0 %collective-permute-done.12.refs_10_ = f32[32,256]{1,0:T(8,128)S(1)} collective-permute-done((f32[32,256]{1,0:T(8,128)S(1)}, f32[32,256]{1,0:T(8,128)S(1)}, u32[]{:S(2)}, u32[]{:S(2)}) %collective-permute-start.12) | collective-permute-done | bytes 32800 | tf_op jit(solution)/shard_map/ppermute | solution.py:582
  35.8 0.1 collective-permute-start.13
  35.9 1.9 %collective-permute-start.16 = (bf16[3,832,128]{2,1,0:T(8,128)(2,1)S(1)}, bf16[3,832,128]{2,1,0:T(8,128)(2,1)S(1)}, u32[]{:S(2)}, u32[]{:S(2)}) collective-permute-start(bf16[3,832,128]{2,1,0:T(8,128)(2,1)S(1)} %stack.1.rest_0_), channel_id=1, source_target_pairs={{0,8},{8,0},{16,24},{24,16},{1,9},{9,1},{17,25},{25,17},{2,10},{10... | collective-permute-start | bytes 1916936 | tf_op jit(solution)/shard_map/ppermute | solution.py:601
  37.8 1.5 %collective-permute-start.15 = (bf16[3,832,128]{2,1,0:T(8,128)(2,1)S(1)}, bf16[3,832,128]{2,1,0:T(8,128)(2,1)S(1)}, u32[]{:S(2)}, u32[]{:S(2)}) collective-permute-start(bf16[3,832,128]{2,1,0:T(8,128)(2,1)S(1)} %stack.1.rest_0_), channel_id=1, source_target_pairs={{0,24},{8,16},{16,8},{24,0},{1,25},{9,17},{17,9},{25,1},{2,26},{10... | collective-permute-start | bytes 1916936 | tf_op jit(solution)/shard_map/ppermute | solution.py:601
  39.3 0.2 collective-permute-start.14
  39.4 3.6 %gradients.1 = bf16[832,128]{1,0:T(8,128)(2,1)S(1)} custom-call(bf16[560,128]{1,0:T(8,128)(2,1)S(1)} %collective-permute-done.refs_0_, bf16[560,128]{1,0:T(8,128)(2,1)S(1)} %collective-permute-done.1.refs_1_, bf16[560,128]{1,0:T(8,128)(2,1)S(1)} %collective-permute-done.2.refs_2_, bf16[560,128]{1,0:T(8,128)(2,1)S(1)} %collective-permute-done.3.refs_3_, ...), custom_call_target="tpu_custom_call" | custom-call | flops 1 | bytes 1024 | tf_op jit(solution)/shard_map/gradients/pallas_call | solution.py:606
  43.0 0.0 collective-permute-done.13.rest_1_
  43.0 19.8 %all-gather = bf16[3328,128]{1,0:T(8,128)(2,1)S(1)} all-gather(bf16[832,128]{1,0:T(8,128)(2,1)S(1)} %gradients.1), channel_id=2, replica_groups=mesh['half0'=2,'half1'=2,'core'=2,'tp'=4] {'tp'}, dimensions={0}, use_global_device_ids=true | all-gather | bytes 1064960 | tf_op jit(solution)/shard_map/all_gather | solution.py:623
  62.8 0.2 cat.1
  63.1 1.4 %columns.5.rest_1_ = bf16[256,2048]{1,0:T(8,128)(2,1)} custom-call(bf16[256,1536]{1,0:T(8,128)(2,1)S(1)} %get-tuple-element.71.cat_ref, bf16[256,128]{1,0:T(8,128)(2,1)S(1)} %get-tuple-element.72.feat_ref, bf16[2048,256]{1,0:T(8,128)(2,1)S(1)} %get-tuple-element.73.ww_ref, bf16[2048,128]{1,0:T(8,128)(2,1)S(1)} %get-tuple-element.74.vw_ref, ...), custom_call_target="tpu_custom_call" | custom-call | flops 1 | bytes 1024 | tf_op jit(solution)/shard_map/columns/pallas_call | solution.py:650
  64.4 0.0 collective-permute-done.16.rest_0_
  64.4 0.1 collective-permute-start.19
  64.5 1.1 %columns.6.rest_2_ = bf16[256,2048]{1,0:T(8,128)(2,1)} custom-call(bf16[256,1536]{1,0:T(8,128)(2,1)S(1)} %get-tuple-element.71.cat_ref, bf16[256,128]{1,0:T(8,128)(2,1)S(1)} %get-tuple-element.72.feat_ref, bf16[2048,256]{1,0:T(8,128)(2,1)S(1)} %get-tuple-element.73.ww_ref, ...), custom_call_target="tpu_custom_call", output_to_operand_aliasing={{}: (6, {})} | custom-call | flops 1 | bytes 1024 | tf_op jit(solution)/shard_map/columns/pallas_call | solution.py:650
  65.6 2.1 %collective-permute-done.15.rest_1_ = bf16[3,832,128]{2,1,0:T(8,128)(2,1)S(1)} collective-permute-done((bf16[3,832,128]{2,1,0:T(8,128)(2,1)S(1)}, bf16[3,832,128]{2,1,0:T(8,128)(2,1)S(1)}, u32[]{:S(2)}, u32[]{:S(2)}) %collective-permute-start.15) | collective-permute-done | bytes 639008 | tf_op jit(solution)/shard_map/ppermute | solution.py:601
  67.8 1.4 %collective-permute-done.14.rest_1_ = bf16[3,832,128]{2,1,0:T(8,128)(2,1)S(1)} collective-permute-done((bf16[3,832,128]{2,1,0:T(8,128)(2,1)S(1)}, bf16[3,832,128]{2,1,0:T(8,128)(2,1)S(1)}, u32[]{:S(2)}, u32[]{:S(2)}) %collective-permute-start.14) | collective-permute-done | bytes 639008 | tf_op jit(solution)/shard_map/ppermute | solution.py:601
  69.1 0.5 collective-permute-start.17
  69.6 0.0 collective-permute-done.19.rest_0_
  69.6 1.4 %columns.7.rest_2_ = bf16[256,2048]{1,0:T(8,128)(2,1)} custom-call(bf16[256,1536]{1,0:T(8,128)(2,1)S(1)} %get-tuple-element.71.cat_ref, bf16[256,128]{1,0:T(8,128)(2,1)S(1)} %get-tuple-element.72.feat_ref, bf16[2048,256]{1,0:T(8,128)(2,1)S(1)} %get-tuple-element.73.ww_ref, ...), custom_call_target="tpu_custom_call", output_to_operand_aliasing={{}: (7, {})} | custom-call | flops 1 | bytes 1024 | tf_op jit(solution)/shard_map/columns/pallas_call | solution.py:650
  71.0 0.2 collective-permute-done.18.rest_0_
  71.2 1.4 %columns.8.rest_1_ = bf16[256,2048]{1,0:T(8,128)(2,1)} custom-call(bf16[256,1536]{1,0:T(8,128)(2,1)S(1)} %get-tuple-element.71.cat_ref, bf16[256,128]{1,0:T(8,128)(2,1)S(1)} %get-tuple-element.72.feat_ref, bf16[2048,256]{1,0:T(8,128)(2,1)S(1)} %get-tuple-element.73.ww_ref, ...), custom_call_target="tpu_custom_call", output_to_operand_aliasing={{}: (7, {})} | custom-call | flops 1 | bytes 1024 | tf_op jit(solution)/shard_map/columns/pallas_call | solution.py:650
  72.6 1.1 %columns.9 = bf16[256,2048]{1,0:T(8,128)(2,1)} custom-call(bf16[256,1536]{1,0:T(8,128)(2,1)S(1)} %get-tuple-element.71.cat_ref, bf16[256,128]{1,0:T(8,128)(2,1)S(1)} %get-tuple-element.72.feat_ref, bf16[2048,256]{1,0:T(8,128)(2,1)S(1)} %get-tuple-element.73.ww_ref, bf16[2048,128]{1,0:T(8,128)(2,1)S(1)} %get-tuple-element.74.vw_ref, ...), custom_call_target="tpu_custom_call", output_to_operand_aliasing={{}: (6, {})} | custom-call | flops 1 | bytes 1024 | tf_op jit(solution)/shard_map/columns/pallas_call | solution.py:650
  (5 shorter events, 0.1 us)
Async XLA Ops:
  3.8 19.4 %collective-permute-start.7 = (bf16[832,128]{1,0:T(8,128)(2,1)S(1)}, bf16[832,128]{1,0:T(8,128)(2,1)S(1)}, u32[]{:S(2)}, u32[]{:S(2)}) collective-permute-start(bf16[832,128]{1,0:T(8,128)(2,1)S(1)} %get-tuple-element.46), channel_id=1, source_target_pairs={{0,2},{1,3},{2,0},{3,1},{4,6},{5,7},{6,4},{7,5},{8,10},{9,11},{10,... | collective-permute-start | bytes 638984 | tf_op jit(solution)/shard_map/ppermute | solution.py:554
  7.9 3.5 %collective-permute-start = (bf16[560,128]{1,0:T(8,128)(2,1)S(1)}, bf16[560,128]{1,0:T(8,128)(2,1)S(1)}, u32[]{:S(2)}, u32[]{:S(2)}) collective-permute-start(bf16[560,128]{1,0:T(8,128)(2,1)S(1)} %get-tuple-element.42), channel_id=1, source_target_pairs={{0,4},{4,0},{1,5},{5,1},{2,6},{6,2},{3,7},{7,3},{8,12},{12,8},{9,1... | collective-permute-start | bytes 430088 | tf_op jit(solution)/shard_map/ppermute | solution.py:545
  7.9 6.6 %collective-permute-start.1 = (bf16[560,128]{1,0:T(8,128)(2,1)S(1)}, bf16[560,128]{1,0:T(8,128)(2,1)S(1)}, u32[]{:S(2)}, u32[]{:S(2)}) collective-permute-start(bf16[560,128]{1,0:T(8,128)(2,1)S(1)} %get-tuple-element.43), channel_id=1, source_target_pairs={{0,8},{8,0},{16,24},{24,16},{1,9},{9,1},{17,25},{25,17},{2,10},{10... | collective-permute-start | bytes 430088 | tf_op jit(solution)/shard_map/ppermute | solution.py:544
  9.4 9.0 %collective-permute-start.3 = (bf16[560,128]{1,0:T(8,128)(2,1)S(1)}, bf16[560,128]{1,0:T(8,128)(2,1)S(1)}, u32[]{:S(2)}, u32[]{:S(2)}) collective-permute-start(bf16[560,128]{1,0:T(8,128)(2,1)S(1)} %get-tuple-element.44), channel_id=1, source_target_pairs={{0,16},{8,24},{16,0},{24,8},{1,17},{9,25},{17,1},{25,9},{2,18},{10... | collective-permute-start | bytes 430088 | tf_op jit(solution)/shard_map/ppermute | solution.py:544
  10.9 7.5 %collective-permute-start.5 = (bf16[560,128]{1,0:T(8,128)(2,1)S(1)}, bf16[560,128]{1,0:T(8,128)(2,1)S(1)}, u32[]{:S(2)}, u32[]{:S(2)}) collective-permute-start(bf16[560,128]{1,0:T(8,128)(2,1)S(1)} %get-tuple-element.45), channel_id=1, source_target_pairs={{0,24},{8,16},{16,8},{24,0},{1,25},{9,17},{17,9},{25,1},{2,26},{10... | collective-permute-start | bytes 430088 | tf_op jit(solution)/shard_map/ppermute | solution.py:544
  11.4 15.7 %collective-permute-start.9 = (bf16[832,128]{1,0:T(8,128)(2,1)S(1)}, bf16[832,128]{1,0:T(8,128)(2,1)S(1)}, u32[]{:S(2)}, u32[]{:S(2)}) collective-permute-start(bf16[832,128]{1,0:T(8,128)(2,1)S(1)} %get-tuple-element.46), channel_id=1, source_target_pairs={{0,3},{1,2},{2,1},{3,0},{4,7},{5,6},{6,5},{7,4},{8,11},{9,10},{10,... | collective-permute-start | bytes 638984 | tf_op jit(solution)/shard_map/ppermute | solution.py:554
  14.4 12.6 %collective-permute-start.8 = (bf16[832,128]{1,0:T(8,128)(2,1)S(1)}, bf16[832,128]{1,0:T(8,128)(2,1)S(1)}, u32[]{:S(2)}, u32[]{:S(2)}) collective-permute-start(bf16[832,128]{1,0:T(8,128)(2,1)S(1)} %get-tuple-element.46), channel_id=1, source_target_pairs={{0,1},{1,0},{2,3},{3,2},{4,5},{5,4},{6,7},{7,6},{8,9},{9,8},{10,11... | collective-permute-start | bytes 638984 | tf_op jit(solution)/shard_map/ppermute | solution.py:554
  18.3 4.8 %collective-permute-start.2 = (bf16[560,128]{1,0:T(8,128)(2,1)S(1)}, bf16[560,128]{1,0:T(8,128)(2,1)S(1)}, u32[]{:S(2)}, u32[]{:S(2)}) collective-permute-start(bf16[560,128]{1,0:T(8,128)(2,1)S(1)} %collective-permute-done.1.refs_1_), channel_id=1, source_target_pairs={{0,4},{4,0},{1,5},{5,1},{2,6},{6,2},{3,7},{7,3},{8,12},{12,8},{9,1... | collective-permute-start | bytes 430088 | tf_op jit(solution)/shard_map/ppermute | solution.py:547
  18.3 4.8 %collective-permute-start.4 = (bf16[560,128]{1,0:T(8,128)(2,1)S(1)}, bf16[560,128]{1,0:T(8,128)(2,1)S(1)}, u32[]{:S(2)}, u32[]{:S(2)}) collective-permute-start(bf16[560,128]{1,0:T(8,128)(2,1)S(1)} %collective-permute-done.3.refs_3_), channel_id=1, source_target_pairs={{0,4},{4,0},{1,5},{5,1},{2,6},{6,2},{3,7},{7,3},{8,12},{12,8},{9,1... | collective-permute-start | bytes 430088 | tf_op jit(solution)/shard_map/ppermute | solution.py:547
  23.1 1.4 %collective-permute-start.6 = (bf16[560,128]{1,0:T(8,128)(2,1)S(1)}, bf16[560,128]{1,0:T(8,128)(2,1)S(1)}, u32[]{:S(2)}, u32[]{:S(2)}) collective-permute-start(bf16[560,128]{1,0:T(8,128)(2,1)S(1)} %collective-permute-done.5.refs_5_), channel_id=1, source_target_pairs={{0,4},{4,0},{1,5},{5,1},{2,6},{6,2},{3,7},{7,3},{8,12},{12,8},{9,1... | collective-permute-start | bytes 430088 | tf_op jit(solution)/shard_map/ppermute | solution.py:547
  26.9 1.2 %collective-permute-start.10 = (f32[8,256]{1,0:T(8,128)S(1)}, f32[8,256]{1,0:T(8,128)S(1)}, u32[]{:S(2)}, u32[]{:S(2)}) collective-permute-start(f32[8,256]{1,0:T(8,128)S(1)} %get-tuple-element.65.refs_7_), channel_id=1, source_target_pairs={{0,4},{4,0},{1,5},{5,1},{2,6},{6,2},{3,7},{7,3},{8,12},{12,8},{9,1... | collective-permute-start | bytes 24584 | tf_op jit(solution)/shard_map/ppermute | solution.py:582
  28.1 3.7 %collective-permute-start.11 = (f32[16,256]{1,0:T(8,128)S(1)}, f32[16,256]{1,0:T(8,128)S(1)}, u32[]{:S(2)}, u32[]{:S(2)}) collective-permute-start(f32[16,256]{1,0:T(8,128)S(1)} %pad_maximum_fusion.1), channel_id=1, source_target_pairs={{0,8},{8,0},{1,9},{9,1},{2,10},{10,2},{3,11},{11,3},{4,12},{12,4},... | collective-permute-start | bytes 49160 | tf_op jit(solution)/shard_map/ppermute | solution.py:582
  31.8 3.9 %collective-permute-start.12 = (f32[32,256]{1,0:T(8,128)S(1)}, f32[32,256]{1,0:T(8,128)S(1)}, u32[]{:S(2)}, u32[]{:S(2)}) collective-permute-start(f32[32,256]{1,0:T(8,128)S(1)} %pad_maximum_fusion), channel_id=1, source_target_pairs={{0,16},{16,0},{1,17},{17,1},{2,18},{18,2},{3,19},{19,3},{4,20},{20... | collective-permute-start | bytes 98312 | tf_op jit(solution)/shard_map/ppermute | solution.py:582
  35.8 7.2 %collective-permute-start.13 = (bf16[3,832,128]{2,1,0:T(8,128)(2,1)S(1)}, bf16[3,832,128]{2,1,0:T(8,128)(2,1)S(1)}, u32[]{:S(2)}, u32[]{:S(2)}) collective-permute-start(bf16[3,832,128]{2,1,0:T(8,128)(2,1)S(1)} %stack.1.rest_0_), channel_id=1, source_target_pairs={{0,4},{4,0},{1,5},{5,1},{2,6},{6,2},{3,7},{7,3},{8,12},{12,8},{9,1... | collective-permute-start | bytes 1916936 | tf_op jit(solution)/shard_map/ppermute | solution.py:621
  35.9 28.6 %collective-permute-start.16 = (bf16[3,832,128]{2,1,0:T(8,128)(2,1)S(1)}, bf16[3,832,128]{2,1,0:T(8,128)(2,1)S(1)}, u32[]{:S(2)}, u32[]{:S(2)}) collective-permute-start(bf16[3,832,128]{2,1,0:T(8,128)(2,1)S(1)} %stack.1.rest_0_), channel_id=1, source_target_pairs={{0,8},{8,0},{16,24},{24,16},{1,9},{9,1},{17,25},{25,17},{2,10},{10... | collective-permute-start | bytes 1916936 | tf_op jit(solution)/shard_map/ppermute | solution.py:601
  37.8 30.0 %collective-permute-start.15 = (bf16[3,832,128]{2,1,0:T(8,128)(2,1)S(1)}, bf16[3,832,128]{2,1,0:T(8,128)(2,1)S(1)}, u32[]{:S(2)}, u32[]{:S(2)}) collective-permute-start(bf16[3,832,128]{2,1,0:T(8,128)(2,1)S(1)} %stack.1.rest_0_), channel_id=1, source_target_pairs={{0,24},{8,16},{16,8},{24,0},{1,25},{9,17},{17,9},{25,1},{2,26},{10... | collective-permute-start | bytes 1916936 | tf_op jit(solution)/shard_map/ppermute | solution.py:601
  39.3 29.9 %collective-permute-start.14 = (bf16[3,832,128]{2,1,0:T(8,128)(2,1)S(1)}, bf16[3,832,128]{2,1,0:T(8,128)(2,1)S(1)}, u32[]{:S(2)}, u32[]{:S(2)}) collective-permute-start(bf16[3,832,128]{2,1,0:T(8,128)(2,1)S(1)} %stack.1.rest_0_), channel_id=1, source_target_pairs={{0,16},{8,24},{16,0},{24,8},{1,17},{9,25},{17,1},{25,9},{2,18},{10... | collective-permute-start | bytes 1916936 | tf_op jit(solution)/shard_map/ppermute | solution.py:601
  64.4 5.2 %collective-permute-start.19 = (bf16[3,832,128]{2,1,0:T(8,128)(2,1)S(1)}, bf16[3,832,128]{2,1,0:T(8,128)(2,1)S(1)}, u32[]{:S(2)}, u32[]{:S(2)}) collective-permute-start(bf16[3,832,128]{2,1,0:T(8,128)(2,1)S(1)} %collective-permute-done.16.rest_0_), channel_id=1, source_target_pairs={{0,4},{4,0},{1,5},{5,1},{2,6},{6,2},{3,7},{7,3},{8,12},{12,8},{9,1... | collective-permute-start | bytes 1916936 | tf_op jit(solution)/shard_map/ppermute | solution.py:646
  69.1 2.1 %collective-permute-start.18 = (bf16[3,832,128]{2,1,0:T(8,128)(2,1)S(1)}, bf16[3,832,128]{2,1,0:T(8,128)(2,1)S(1)}, u32[]{:S(2)}, u32[]{:S(2)}) collective-permute-start(bf16[3,832,128]{2,1,0:T(8,128)(2,1)S(1)} %collective-permute-done.14.rest_1_), channel_id=1, source_target_pairs={{0,4},{4,0},{1,5},{5,1},{2,6},{6,2},{3,7},{7,3},{8,12},{12,8},{9,1... | collective-permute-start | bytes 1916936 | tf_op jit(solution)/shard_map/ppermute | solution.py:646
  69.1 3.4 %collective-permute-start.17 = (bf16[3,832,128]{2,1,0:T(8,128)(2,1)S(1)}, bf16[3,832,128]{2,1,0:T(8,128)(2,1)S(1)}, u32[]{:S(2)}, u32[]{:S(2)}) collective-permute-start(bf16[3,832,128]{2,1,0:T(8,128)(2,1)S(1)} %collective-permute-done.15.rest_1_), channel_id=1, source_target_pairs={{0,4},{4,0},{1,5},{5,1},{2,6},{6,2},{3,7},{7,3},{8,12},{12,8},{9,1... | collective-permute-start | bytes 1916936 | tf_op jit(solution)/shard_map/ppermute | solution.py:646

commit v14 on v13

--- a/solution.py
+++ b/solution.py
@@ -554,7 +554,6 @@
             lax.ppermute(outs[0], "tp", [(z, z ^ t) for z in range(heads)])
             for t in range(1, heads)
         ]
-        near[1], own = lax.optimization_barrier((near[1], own))
 
     attended, stat, sheet = pl.pallas_call(
         lambda *refs: query_kernel(ctx, count, *refs),
@@ -634,16 +633,14 @@
         name="cat",
     )(grads)
     total = []
-    groups = [(0, 1)]
-    for d in range(1, chips):
-        groups.append((2 * d - 1, 2 * d) if d > 1 else (2 * d,))
-    groups.append((2 * chips - 1,))
-    for d, distances in enumerate(groups):
-        if 0 < d < chips:
-            if d < 3:
-                late = slice(d, d + 1 if d == 1 else chips)
-                pieces[late], total = lax.optimization_barrier((pieces[late], total))
-            swapped[d] = lax.ppermute(pieces[d], "core", swap)
+    for distances in ((0, 1), (2,), (3, 4, 6), (5, 7)):
+        if distances == (2,):
+            pieces[1], total = lax.optimization_barrier((pieces[1], total))
+            swapped[1] = lax.ppermute(pieces[1], "core", swap)
+        if distances == (3, 4, 6):
+            pieces[2:], total = lax.optimization_barrier((pieces[2:], total))
+            for d in range(2, chips):
+                swapped[d] = lax.ppermute(pieces[d], "core", swap)
         parts = [(swapped if e % 2 else pieces)[e // 2] for e in distances]
         args = [cat, feats, ww, vw, fw, *parts, *total]
         total = [

time: 73.8 us -> 78.9 us (1.069)
  waiting for transfers between devices: 18.3 us -> 24.8 us
  Pallas kernels: 15.7 us -> 14.9 us
    ppermute x3, waiting for transfers between devices: 4.29 us -> 11.3 us  [per_device(): lax.ppermute(outs[0], 'tp', [(z, z ^ t) for z in range(heads)])]
    ppermute x3, starting transfers between devices: 7.04 us -> 5.29 us  [per_device(): lax.ppermute(outs[0], 'tp', [(z, z ^ t) for z in range(heads)])]
    ppermute x3, starting transfers between devices: 3.49 us -> 4.64 us  [per_device(): lax.ppermute(sends[d], ctx[:-1], [(i, i ^ d) for i in range(chips)])]
    ppermute x3, waiting for transfers between devices: 4.97 us -> 4.12 us  [per_device(): stats.append(lax.ppermute(held, name, swap))]
    pallas_call x5 -> x4, Pallas kernels: 6.27 us -> 5.43 us  [per_device(): pl.pallas_call(partial(columns_kernel, ctx, distances), out_shape=jax.Sha...]
  transfers between devices with their start and end apart: 20 -> 20, of which waited for: 10 -> 10; matrix products, arithmetic and copies ran while one was open for 0% -> 0% of each run, Pallas kernels for 15% -> 13%
where the time goes in v14:
time: 78.9 us; the launch traced here: 78.7 us
  waiting for transfers between devices  24.8 us (31%)
  blocking collectives  19.5 us (25%)
  starting transfers between devices  18.8 us (24%)
  Pallas kernels  14.9 us (19%)
    all_gather x1, blocking collectives, per_device(): grads = lax.all_gather(grads, 'tp')  19.5 us
    ppermute x3, waiting for transfers between devices, per_device(): lax.ppermute(outs[0], 'tp', [(z, z ^ t) for z in range(heads)])  11.3 us
    pallas_call x4, Pallas kernels, per_device(): pl.pallas_call(partial(columns_kernel, ctx, distances), out_shape=jax.Sha...  5.43 us
    ppermute x3, starting transfers between devices, per_device(): lax.ppermute(outs[0], 'tp', [(z, z ^ t) for z in range(heads)])  5.29 us
    ppermute x3, starting transfers between devices, per_device(): lax.ppermute(sends[d], ctx[:-1], [(i, i ^ d) for i in range(chips)])  4.64 us
    ppermute x3, waiting for transfers between devices, per_device(): stats.append(lax.ppermute(held, name, swap))  4.12 us
    ppermute x3, starting transfers between devices, per_device(): stats.append(lax.ppermute(held, name, swap))  4.04 us
    ppermute x3, waiting for transfers between devices, per_device(): lax.ppermute(sends[d], ctx[:-1], [(i, i ^ d) for i in range(chips)])  3.88 us
  transfers between devices with their start and end apart: 20, of which 10 were waited for; matrix products, arithmetic and copies ran while one was open for 0% of the time, Pallas kernels for 13%

profile of v14, /device:TPU:0, one launch (start us, length us, event | category | flops | bytes accessed | tf_op | source)
XLA Modules:
  0.0 78.7 jit_solution(11975335158950966593)
XLA Ops:
  0.6 3.1 %project.1 = (bf16[832,128]{1,0:T(8,128)(2,1)S(1)}, bf16[560,128]{1,0:T(8,128)(2,1)S(1)}, bf16[560,128]{1,0:T(8,128)(2,1)S(1)}, bf16[560,128]{1,0:T(8,128)(2,1)S...) custom-call(bf16[256,2048]{1,0:T(8,128)(2,1)} %tok_hbm.1, ...), custom_call_target="tpu_custom_call" | custom-call | flops 1 | bytes 1024 | tf_op jit(solution)/shard_map/project/pallas_call | solution.py:514
  3.8 3.0 %collective-permute-start.1 = (bf16[560,128]{1,0:T(8,128)(2,1)S(1)}, bf16[560,128]{1,0:T(8,128)(2,1)S(1)}, u32[]{:S(2)}, u32[]{:S(2)}) collective-permute-start(bf16[560,128]{1,0:T(8,128)(2,1)S(1)} %get-tuple-element.41), channel_id=1, source_target_pairs={{0,8},{8,0},{16,24},{24,16},{1,9},{9,1},{17,25},{25,17},{2,10},{10... | collective-permute-start | bytes 430088 | tf_op jit(solution)/shard_map/ppermute | solution.py:544
  6.8 0.0 collective-permute-start
  6.8 1.5 %collective-permute-start.3 = (bf16[560,128]{1,0:T(8,128)(2,1)S(1)}, bf16[560,128]{1,0:T(8,128)(2,1)S(1)}, u32[]{:S(2)}, u32[]{:S(2)}) collective-permute-start(bf16[560,128]{1,0:T(8,128)(2,1)S(1)} %get-tuple-element.42), channel_id=1, source_target_pairs={{0,16},{8,24},{16,0},{24,8},{1,17},{9,25},{17,1},{25,9},{2,18},{10... | collective-permute-start | bytes 430088 | tf_op jit(solution)/shard_map/ppermute | solution.py:544
  8.3 0.1 collective-permute-start.5
  8.4 2.3 %collective-permute-done.1.refs_1_ = bf16[560,128]{1,0:T(8,128)(2,1)S(1)} collective-permute-done((bf16[560,128]{1,0:T(8,128)(2,1)S(1)}, bf16[560,128]{1,0:T(8,128)(2,1)S(1)}, u32[]{:S(2)}, u32[]{:S(2)}) %collective-permute-start.1) | collective-permute-done | bytes 143392 | tf_op jit(solution)/shard_map/ppermute | solution.py:544
  10.7 0.0 collective-permute-start.2
  10.7 3.7 %collective-permute-start.9 = (bf16[832,128]{1,0:T(8,128)(2,1)S(1)}, bf16[832,128]{1,0:T(8,128)(2,1)S(1)}, u32[]{:S(2)}, u32[]{:S(2)}) collective-permute-start(bf16[832,128]{1,0:T(8,128)(2,1)S(1)} %get-tuple-element.49), channel_id=1, source_target_pairs={{0,3},{1,2},{2,1},{3,0},{4,7},{5,6},{6,5},{7,4},{8,11},{9,10},{10,... | collective-permute-start | bytes 638984 | tf_op jit(solution)/shard_map/ppermute | solution.py:554
  14.4 0.0 collective-permute-done.refs_0_
  14.4 0.0 collective-permute-start.8
  14.4 1.6 %collective-permute-done.3.refs_3_ = bf16[560,128]{1,0:T(8,128)(2,1)S(1)} collective-permute-done((bf16[560,128]{1,0:T(8,128)(2,1)S(1)}, bf16[560,128]{1,0:T(8,128)(2,1)S(1)}, u32[]{:S(2)}, u32[]{:S(2)}) %collective-permute-start.3) | collective-permute-done | bytes 143392 | tf_op jit(solution)/shard_map/ppermute | solution.py:544
  16.0 1.6 %collective-permute-start.7 = (bf16[832,128]{1,0:T(8,128)(2,1)S(1)}, bf16[832,128]{1,0:T(8,128)(2,1)S(1)}, u32[]{:S(2)}, u32[]{:S(2)}) collective-permute-start(bf16[832,128]{1,0:T(8,128)(2,1)S(1)} %get-tuple-element.49), channel_id=1, source_target_pairs={{0,1},{1,0},{2,3},{3,2},{4,5},{5,4},{6,7},{7,6},{8,9},{9,8},{10,11... | collective-permute-start | bytes 638984 | tf_op jit(solution)/shard_map/ppermute | solution.py:554
  17.6 0.0 collective-permute-done.5.refs_5_
  17.6 0.0 collective-permute-start.4
  17.6 0.0 collective-permute-done.2.refs_2_
  17.6 0.5 collective-permute-start.6
  18.1 0.9 %collective-permute-done.4.refs_4_ = bf16[560,128]{1,0:T(8,128)(2,1)S(1)} collective-permute-done((bf16[560,128]{1,0:T(8,128)(2,1)S(1)}, bf16[560,128]{1,0:T(8,128)(2,1)S(1)}, u32[]{:S(2)}, u32[]{:S(2)}) %collective-permute-start.4) | collective-permute-done | bytes 143392 | tf_op jit(solution)/shard_map/ppermute | solution.py:547
  19.0 0.2 collective-permute-done.6.refs_6_
  19.2 2.4 %query_side.1 = (bf16[256,128]{1,0:T(8,128)(2,1)}, f32[8,256]{1,0:T(8,128)S(1)}, f32[256,128]{1,0:T(8,128)S(1)}) custom-call(bf16[560,128]{1,0:T(8,128)(2,1)S(1)} %collective-permute-done.refs_0_, bf16[560,128]{1,0:T(8,128)(2,1)S(1)} %collective-permute-done.1.refs_1_, bf16[560,128]{1,0:T(8,128)(2,1)S(1)} %collective-permute-done.2.refs_2_, ...), custom_call_target="tpu_custom_call" | custom-call | flops 1 | bytes 1024 | tf_op jit(solution)/shard_map/query_side/pallas_call | solution.py:558
  21.6 0.3 collective-permute-start.10
  21.9 0.0 collective-permute-done.9.refs_2_
  21.9 11.3 %collective-permute-done.8.refs_1_ = bf16[832,128]{1,0:T(8,128)(2,1)S(1)} collective-permute-done((bf16[832,128]{1,0:T(8,128)(2,1)S(1)}, bf16[832,128]{1,0:T(8,128)(2,1)S(1)}, u32[]{:S(2)}, u32[]{:S(2)}) %collective-permute-start.8) | collective-permute-done | bytes 213024 | tf_op jit(solution)/shard_map/ppermute | solution.py:554
  33.2 0.0 collective-permute-done.7.refs_0_
  33.2 0.0 collective-permute-done.10.refs_8_
  33.2 2.2 %collective-permute-start.11 = (f32[16,256]{1,0:T(8,128)S(1)}, f32[16,256]{1,0:T(8,128)S(1)}, u32[]{:S(2)}, u32[]{:S(2)}) collective-permute-start(f32[16,256]{1,0:T(8,128)S(1)} %pad_maximum_fusion.1), channel_id=1, source_target_pairs={{0,8},{8,0},{1,9},{9,1},{2,10},{10,2},{3,11},{11,3},{4,12},{12,4},... | collective-permute-start | bytes 49160 | tf_op jit(solution)/shard_map/ppermute | solution.py:581
  35.4 1.7 %collective-permute-done.11.refs_9_ = f32[16,256]{1,0:T(8,128)S(1)} collective-permute-done((f32[16,256]{1,0:T(8,128)S(1)}, f32[16,256]{1,0:T(8,128)S(1)}, u32[]{:S(2)}, u32[]{:S(2)}) %collective-permute-start.11) | collective-permute-done | bytes 16416 | tf_op jit(solution)/shard_map/ppermute | solution.py:581
  37.1 1.5 %collective-permute-start.12 = (f32[32,256]{1,0:T(8,128)S(1)}, f32[32,256]{1,0:T(8,128)S(1)}, u32[]{:S(2)}, u32[]{:S(2)}) collective-permute-start(f32[32,256]{1,0:T(8,128)S(1)} %pad_maximum_fusion), channel_id=1, source_target_pairs={{0,16},{16,0},{1,17},{17,1},{2,18},{18,2},{3,19},{19,3},{4,20},{20... | collective-permute-start | bytes 98312 | tf_op jit(solution)/shard_map/ppermute | solution.py:581
  38.7 2.4 %collective-permute-done.12.refs_10_ = f32[32,256]{1,0:T(8,128)S(1)} collective-permute-done((f32[32,256]{1,0:T(8,128)S(1)}, f32[32,256]{1,0:T(8,128)S(1)}, u32[]{:S(2)}, u32[]{:S(2)}) %collective-permute-start.12) | collective-permute-done | bytes 32800 | tf_op jit(solution)/shard_map/ppermute | solution.py:581
  41.1 0.1 collective-permute-start.13
  41.2 2.1 %collective-permute-start.16 = (bf16[3,832,128]{2,1,0:T(8,128)(2,1)S(1)}, bf16[3,832,128]{2,1,0:T(8,128)(2,1)S(1)}, u32[]{:S(2)}, u32[]{:S(2)}) collective-permute-start(bf16[3,832,128]{2,1,0:T(8,128)(2,1)S(1)} %stack.1.rest_0_), channel_id=1, source_target_pairs={{0,8},{8,0},{16,24},{24,16},{1,9},{9,1},{17,25},{25,17},{2,10},{10... | collective-permute-start | bytes 1916936 | tf_op jit(solution)/shard_map/ppermute | solution.py:600
  43.3 1.0 %collective-permute-start.15 = (bf16[3,832,128]{2,1,0:T(8,128)(2,1)S(1)}, bf16[3,832,128]{2,1,0:T(8,128)(2,1)S(1)}, u32[]{:S(2)}, u32[]{:S(2)}) collective-permute-start(bf16[3,832,128]{2,1,0:T(8,128)(2,1)S(1)} %stack.1.rest_0_), channel_id=1, source_target_pairs={{0,24},{8,16},{16,8},{24,0},{1,25},{9,17},{17,9},{25,1},{2,26},{10... | collective-permute-start | bytes 1916936 | tf_op jit(solution)/shard_map/ppermute | solution.py:600
  44.3 0.5 collective-permute-start.14
  44.8 3.7 %gradients.1 = bf16[832,128]{1,0:T(8,128)(2,1)S(1)} custom-call(bf16[560,128]{1,0:T(8,128)(2,1)S(1)} %collective-permute-done.refs_0_, bf16[560,128]{1,0:T(8,128)(2,1)S(1)} %collective-permute-done.1.refs_1_, bf16[560,128]{1,0:T(8,128)(2,1)S(1)} %collective-permute-done.2.refs_2_, bf16[560,128]{1,0:T(8,128)(2,1)S(1)} %collective-permute-done.3.refs_3_, ...), custom_call_target="tpu_custom_call" | custom-call | flops 1 | bytes 1024 | tf_op jit(solution)/shard_map/gradients/pallas_call | solution.py:605
  48.5 0.0 collective-permute-done.13.rest_1_
  48.5 19.5 %all-gather = bf16[3328,128]{1,0:T(8,128)(2,1)S(1)} all-gather(bf16[832,128]{1,0:T(8,128)(2,1)S(1)} %gradients.1), channel_id=2, replica_groups=mesh['half0'=2,'half1'=2,'core'=2,'tp'=4] {'tp'}, dimensions={0}, use_global_device_ids=true | all-gather | bytes 1064960 | tf_op jit(solution)/shard_map/all_gather | solution.py:622
  68.0 0.2 cat.1
  68.2 1.4 %columns.4.rest_1_ = bf16[256,2048]{1,0:T(8,128)(2,1)} custom-call(bf16[256,1536]{1,0:T(8,128)(2,1)S(1)} %get-tuple-element.67.cat_ref, bf16[256,128]{1,0:T(8,128)(2,1)S(1)} %get-tuple-element.68.feat_ref, bf16[2048,256]{1,0:T(8,128)(2,1)S(1)} %get-tuple-element.69.ww_ref, bf16[2048,128]{1,0:T(8,128)(2,1)S(1)} %get-tuple-element.70.vw_ref, ...), custom_call_target="tpu_custom_call" | custom-call | flops 1 | bytes 1024 | tf_op jit(solution)/shard_map/columns/pallas_call | solution.py:647
  69.6 0.0 collective-permute-done.16.rest_0_
  69.6 0.1 collective-permute-start.19
  69.7 1.1 %columns.5.rest_3_ = bf16[256,2048]{1,0:T(8,128)(2,1)} custom-call(bf16[256,1536]{1,0:T(8,128)(2,1)S(1)} %get-tuple-element.67.cat_ref, bf16[256,128]{1,0:T(8,128)(2,1)S(1)} %get-tuple-element.68.feat_ref, bf16[2048,256]{1,0:T(8,128)(2,1)S(1)} %get-tuple-element.69.ww_ref, ...), custom_call_target="tpu_custom_call", output_to_operand_aliasing={{}: (6, {})} | custom-call | flops 1 | bytes 1024 | tf_op jit(solution)/shard_map/columns/pallas_call | solution.py:647
  70.8 2.2 %collective-permute-done.15.rest_2_ = bf16[3,832,128]{2,1,0:T(8,128)(2,1)S(1)} collective-permute-done((bf16[3,832,128]{2,1,0:T(8,128)(2,1)S(1)}, bf16[3,832,128]{2,1,0:T(8,128)(2,1)S(1)}, u32[]{:S(2)}, u32[]{:S(2)}) %collective-permute-start.15) | collective-permute-done | bytes 639008 | tf_op jit(solution)/shard_map/ppermute | solution.py:600
  73.0 1.4 %collective-permute-done.14.rest_1_ = bf16[3,832,128]{2,1,0:T(8,128)(2,1)S(1)} collective-permute-done((bf16[3,832,128]{2,1,0:T(8,128)(2,1)S(1)}, bf16[3,832,128]{2,1,0:T(8,128)(2,1)S(1)}, u32[]{:S(2)}, u32[]{:S(2)}) %collective-permute-start.14) | collective-permute-done | bytes 639008 | tf_op jit(solution)/shard_map/ppermute | solution.py:600
  74.4 0.5 collective-permute-start.18
  74.9 0.0 collective-permute-done.19.rest_0_
  74.9 1.6 %columns.6.rest_2_ = bf16[256,2048]{1,0:T(8,128)(2,1)} custom-call(bf16[256,1536]{1,0:T(8,128)(2,1)S(1)} %get-tuple-element.67.cat_ref, bf16[256,128]{1,0:T(8,128)(2,1)S(1)} %get-tuple-element.68.feat_ref, bf16[2048,256]{1,0:T(8,128)(2,1)S(1)} %get-tuple-element.69.ww_ref, ...), custom_call_target="tpu_custom_call", output_to_operand_aliasing={{}: (8, {})} | custom-call | flops 1 | bytes 1024 | tf_op jit(solution)/shard_map/columns/pallas_call | solution.py:647
  76.5 0.0 collective-permute-done.17.rest_0_
  76.5 0.9 %collective-permute-done.18.rest_1_ = bf16[3,832,128]{2,1,0:T(8,128)(2,1)S(1)} collective-permute-done((bf16[3,832,128]{2,1,0:T(8,128)(2,1)S(1)}, bf16[3,832,128]{2,1,0:T(8,128)(2,1)S(1)}, u32[]{:S(2)}, u32[]{:S(2)}) %collective-permute-start.18) | collective-permute-done | bytes 639008 | tf_op jit(solution)/shard_map/ppermute | solution.py:643
  77.3 1.4 %columns.7 = bf16[256,2048]{1,0:T(8,128)(2,1)} custom-call(bf16[256,1536]{1,0:T(8,128)(2,1)S(1)} %get-tuple-element.67.cat_ref, bf16[256,128]{1,0:T(8,128)(2,1)S(1)} %get-tuple-element.68.feat_ref, bf16[2048,256]{1,0:T(8,128)(2,1)S(1)} %get-tuple-element.69.ww_ref, bf16[2048,128]{1,0:T(8,128)(2,1)S(1)} %get-tuple-element.70.vw_ref, ...), custom_call_target="tpu_custom_call", output_to_operand_aliasing={{}: (7, {})} | custom-call | flops 1 | bytes 1024 | tf_op jit(solution)/shard_map/columns/pallas_call | solution.py:647
  (4 shorter events, 0.0 us)
Async XLA Ops:
  3.8 6.9 %collective-permute-start.1 = (bf16[560,128]{1,0:T(8,128)(2,1)S(1)}, bf16[560,128]{1,0:T(8,128)(2,1)S(1)}, u32[]{:S(2)}, u32[]{:S(2)}) collective-permute-start(bf16[560,128]{1,0:T(8,128)(2,1)S(1)} %get-tuple-element.41), channel_id=1, source_target_pairs={{0,8},{8,0},{16,24},{24,16},{1,9},{9,1},{17,25},{25,17},{2,10},{10... | collective-permute-start | bytes 430088 | tf_op jit(solution)/shard_map/ppermute | solution.py:544
  6.8 7.6 %collective-permute-start = (bf16[560,128]{1,0:T(8,128)(2,1)S(1)}, bf16[560,128]{1,0:T(8,128)(2,1)S(1)}, u32[]{:S(2)}, u32[]{:S(2)}) collective-permute-start(bf16[560,128]{1,0:T(8,128)(2,1)S(1)} %get-tuple-element.40), channel_id=1, source_target_pairs={{0,4},{4,0},{1,5},{5,1},{2,6},{6,2},{3,7},{7,3},{8,12},{12,8},{9,1... | collective-permute-start | bytes 430088 | tf_op jit(solution)/shard_map/ppermute | solution.py:545
  6.8 9.2 %collective-permute-start.3 = (bf16[560,128]{1,0:T(8,128)(2,1)S(1)}, bf16[560,128]{1,0:T(8,128)(2,1)S(1)}, u32[]{:S(2)}, u32[]{:S(2)}) collective-permute-start(bf16[560,128]{1,0:T(8,128)(2,1)S(1)} %get-tuple-element.42), channel_id=1, source_target_pairs={{0,16},{8,24},{16,0},{24,8},{1,17},{9,25},{17,1},{25,9},{2,18},{10... | collective-permute-start | bytes 430088 | tf_op jit(solution)/shard_map/ppermute | solution.py:544
  8.3 9.3 %collective-permute-start.5 = (bf16[560,128]{1,0:T(8,128)(2,1)S(1)}, bf16[560,128]{1,0:T(8,128)(2,1)S(1)}, u32[]{:S(2)}, u32[]{:S(2)}) collective-permute-start(bf16[560,128]{1,0:T(8,128)(2,1)S(1)} %get-tuple-element.43), channel_id=1, source_target_pairs={{0,24},{8,16},{16,8},{24,0},{1,25},{9,17},{17,9},{25,1},{2,26},{10... | collective-permute-start | bytes 430088 | tf_op jit(solution)/shard_map/ppermute | solution.py:544
  10.7 6.9 %collective-permute-start.2 = (bf16[560,128]{1,0:T(8,128)(2,1)S(1)}, bf16[560,128]{1,0:T(8,128)(2,1)S(1)}, u32[]{:S(2)}, u32[]{:S(2)}) collective-permute-start(bf16[560,128]{1,0:T(8,128)(2,1)S(1)} %collective-permute-done.1.refs_1_), channel_id=1, source_target_pairs={{0,4},{4,0},{1,5},{5,1},{2,6},{6,2},{3,7},{7,3},{8,12},{12,8},{9,1... | collective-permute-start | bytes 430088 | tf_op jit(solution)/shard_map/ppermute | solution.py:547
  10.7 11.2 %collective-permute-start.9 = (bf16[832,128]{1,0:T(8,128)(2,1)S(1)}, bf16[832,128]{1,0:T(8,128)(2,1)S(1)}, u32[]{:S(2)}, u32[]{:S(2)}) collective-permute-start(bf16[832,128]{1,0:T(8,128)(2,1)S(1)} %get-tuple-element.49), channel_id=1, source_target_pairs={{0,3},{1,2},{2,1},{3,0},{4,7},{5,6},{6,5},{7,4},{8,11},{9,10},{10,... | collective-permute-start | bytes 638984 | tf_op jit(solution)/shard_map/ppermute | solution.py:554
  14.4 18.8 %collective-permute-start.8 = (bf16[832,128]{1,0:T(8,128)(2,1)S(1)}, bf16[832,128]{1,0:T(8,128)(2,1)S(1)}, u32[]{:S(2)}, u32[]{:S(2)}) collective-permute-start(bf16[832,128]{1,0:T(8,128)(2,1)S(1)} %get-tuple-element.49), channel_id=1, source_target_pairs={{0,2},{1,3},{2,0},{3,1},{4,6},{5,7},{6,4},{7,5},{8,10},{9,11},{10,... | collective-permute-start | bytes 638984 | tf_op jit(solution)/shard_map/ppermute | solution.py:554
  16.0 17.2 %collective-permute-start.7 = (bf16[832,128]{1,0:T(8,128)(2,1)S(1)}, bf16[832,128]{1,0:T(8,128)(2,1)S(1)}, u32[]{:S(2)}, u32[]{:S(2)}) collective-permute-start(bf16[832,128]{1,0:T(8,128)(2,1)S(1)} %get-tuple-element.49), channel_id=1, source_target_pairs={{0,1},{1,0},{2,3},{3,2},{4,5},{5,4},{6,7},{7,6},{8,9},{9,8},{10,11... | collective-permute-start | bytes 638984 | tf_op jit(solution)/shard_map/ppermute | solution.py:554
  17.6 1.4 %collective-permute-start.4 = (bf16[560,128]{1,0:T(8,128)(2,1)S(1)}, bf16[560,128]{1,0:T(8,128)(2,1)S(1)}, u32[]{:S(2)}, u32[]{:S(2)}) collective-permute-start(bf16[560,128]{1,0:T(8,128)(2,1)S(1)} %collective-permute-done.3.refs_3_), channel_id=1, source_target_pairs={{0,4},{4,0},{1,5},{5,1},{2,6},{6,2},{3,7},{7,3},{8,12},{12,8},{9,1... | collective-permute-start | bytes 430088 | tf_op jit(solution)/shard_map/ppermute | solution.py:547
  17.6 1.6 %collective-permute-start.6 = (bf16[560,128]{1,0:T(8,128)(2,1)S(1)}, bf16[560,128]{1,0:T(8,128)(2,1)S(1)}, u32[]{:S(2)}, u32[]{:S(2)}) collective-permute-start(bf16[560,128]{1,0:T(8,128)(2,1)S(1)} %collective-permute-done.5.refs_5_), channel_id=1, source_target_pairs={{0,4},{4,0},{1,5},{5,1},{2,6},{6,2},{3,7},{7,3},{8,12},{12,8},{9,1... | collective-permute-start | bytes 430088 | tf_op jit(solution)/shard_map/ppermute | solution.py:547
  21.6 11.6 %collective-permute-start.10 = (f32[8,256]{1,0:T(8,128)S(1)}, f32[8,256]{1,0:T(8,128)S(1)}, u32[]{:S(2)}, u32[]{:S(2)}) collective-permute-start(f32[8,256]{1,0:T(8,128)S(1)} %get-tuple-element.61.refs_7_), channel_id=1, source_target_pairs={{0,4},{4,0},{1,5},{5,1},{2,6},{6,2},{3,7},{7,3},{8,12},{12,8},{9,1... | collective-permute-start | bytes 24584 | tf_op jit(solution)/shard_map/ppermute | solution.py:581
  33.2 3.9 %collective-permute-start.11 = (f32[16,256]{1,0:T(8,128)S(1)}, f32[16,256]{1,0:T(8,128)S(1)}, u32[]{:S(2)}, u32[]{:S(2)}) collective-permute-start(f32[16,256]{1,0:T(8,128)S(1)} %pad_maximum_fusion.1), channel_id=1, source_target_pairs={{0,8},{8,0},{1,9},{9,1},{2,10},{10,2},{3,11},{11,3},{4,12},{12,4},... | collective-permute-start | bytes 49160 | tf_op jit(solution)/shard_map/ppermute | solution.py:581
  37.1 3.9 %collective-permute-start.12 = (f32[32,256]{1,0:T(8,128)S(1)}, f32[32,256]{1,0:T(8,128)S(1)}, u32[]{:S(2)}, u32[]{:S(2)}) collective-permute-start(f32[32,256]{1,0:T(8,128)S(1)} %pad_maximum_fusion), channel_id=1, source_target_pairs={{0,16},{16,0},{1,17},{17,1},{2,18},{18,2},{3,19},{19,3},{4,20},{20... | collective-permute-start | bytes 98312 | tf_op jit(solution)/shard_map/ppermute | solution.py:581
  41.1 7.4 %collective-permute-start.13 = (bf16[3,832,128]{2,1,0:T(8,128)(2,1)S(1)}, bf16[3,832,128]{2,1,0:T(8,128)(2,1)S(1)}, u32[]{:S(2)}, u32[]{:S(2)}) collective-permute-start(bf16[3,832,128]{2,1,0:T(8,128)(2,1)S(1)} %stack.1.rest_0_), channel_id=1, source_target_pairs={{0,4},{4,0},{1,5},{5,1},{2,6},{6,2},{3,7},{7,3},{8,12},{12,8},{9,1... | collective-permute-start | bytes 1916936 | tf_op jit(solution)/shard_map/ppermute | solution.py:620
  41.2 28.4 %collective-permute-start.16 = (bf16[3,832,128]{2,1,0:T(8,128)(2,1)S(1)}, bf16[3,832,128]{2,1,0:T(8,128)(2,1)S(1)}, u32[]{:S(2)}, u32[]{:S(2)}) collective-permute-start(bf16[3,832,128]{2,1,0:T(8,128)(2,1)S(1)} %stack.1.rest_0_), channel_id=1, source_target_pairs={{0,8},{8,0},{16,24},{24,16},{1,9},{9,1},{17,25},{25,17},{2,10},{10... | collective-permute-start | bytes 1916936 | tf_op jit(solution)/shard_map/ppermute | solution.py:600
  43.3 29.7 %collective-permute-start.15 = (bf16[3,832,128]{2,1,0:T(8,128)(2,1)S(1)}, bf16[3,832,128]{2,1,0:T(8,128)(2,1)S(1)}, u32[]{:S(2)}, u32[]{:S(2)}) collective-permute-start(bf16[3,832,128]{2,1,0:T(8,128)(2,1)S(1)} %stack.1.rest_0_), channel_id=1, source_target_pairs={{0,24},{8,16},{16,8},{24,0},{1,25},{9,17},{17,9},{25,1},{2,26},{10... | collective-permute-start | bytes 1916936 | tf_op jit(solution)/shard_map/ppermute | solution.py:600
  44.3 30.1 %collective-permute-start.14 = (bf16[3,832,128]{2,1,0:T(8,128)(2,1)S(1)}, bf16[3,832,128]{2,1,0:T(8,128)(2,1)S(1)}, u32[]{:S(2)}, u32[]{:S(2)}) collective-permute-start(bf16[3,832,128]{2,1,0:T(8,128)(2,1)S(1)} %stack.1.rest_0_), channel_id=1, source_target_pairs={{0,16},{8,24},{16,0},{24,8},{1,17},{9,25},{17,1},{25,9},{2,18},{10... | collective-permute-start | bytes 1916936 | tf_op jit(solution)/shard_map/ppermute | solution.py:600
  69.6 5.3 %collective-permute-start.19 = (bf16[3,832,128]{2,1,0:T(8,128)(2,1)S(1)}, bf16[3,832,128]{2,1,0:T(8,128)(2,1)S(1)}, u32[]{:S(2)}, u32[]{:S(2)}) collective-permute-start(bf16[3,832,128]{2,1,0:T(8,128)(2,1)S(1)} %collective-permute-done.16.rest_0_), channel_id=1, source_target_pairs={{0,4},{4,0},{1,5},{5,1},{2,6},{6,2},{3,7},{7,3},{8,12},{12,8},{9,1... | collective-permute-start | bytes 1916936 | tf_op jit(solution)/shard_map/ppermute | solution.py:639
  74.4 2.1 %collective-permute-start.17 = (bf16[3,832,128]{2,1,0:T(8,128)(2,1)S(1)}, bf16[3,832,128]{2,1,0:T(8,128)(2,1)S(1)}, u32[]{:S(2)}, u32[]{:S(2)}) collective-permute-start(bf16[3,832,128]{2,1,0:T(8,128)(2,1)S(1)} %collective-permute-done.14.rest_1_), channel_id=1, source_target_pairs={{0,4},{4,0},{1,5},{5,1},{2,6},{6,2},{3,7},{7,3},{8,12},{12,8},{9,1... | collective-permute-start | bytes 1916936 | tf_op jit(solution)/shard_map/ppermute | solution.py:643
  74.4 3.0 %collective-permute-start.18 = (bf16[3,832,128]{2,1,0:T(8,128)(2,1)S(1)}, bf16[3,832,128]{2,1,0:T(8,128)(2,1)S(1)}, u32[]{:S(2)}, u32[]{:S(2)}) collective-permute-start(bf16[3,832,128]{2,1,0:T(8,128)(2,1)S(1)} %collective-permute-done.15.rest_2_), channel_id=1, source_target_pairs={{0,4},{4,0},{1,5},{5,1},{2,6},{6,2},{3,7},{7,3},{8,12},{12,8},{9,1... | collective-permute-start | bytes 1916936 | tf_op jit(solution)/shard_map/ppermute | solution.py:643

commit v15 on v14

--- a/solution.py
+++ b/solution.py
@@ -64,10 +64,10 @@
     return place
 
 
-def pack_copies(ctx, ww_hbm, vw_hbm, fw_hbm, out_ref, sems):
+def pack_copies(ctx, distance, ww_hbm, vw_hbm, fw_hbm, out_ref, sems):
     nf2 = fw_hbm.shape[0]
     tile = 2 * LANES
-    at = pl.multiple_of(block_index(ctx) * tile, tile)
+    at = pl.multiple_of(jnp.bitwise_xor(block_index(ctx), distance) * tile, tile)
     rows = pl.ds(at, tile)
     moves = [
         (ww_hbm.at[rows, pl.ds(0, LANES)], out_ref.at[pl.ds(0, tile), :]),
@@ -106,7 +106,7 @@
     for group in copies:
         for at, copy in enumerate(group):
             copy.start(priority=min(at, 1))
-    packing = pack_copies(ctx, ww_hbm, vw_hbm, fw_hbm, rest[0], pack_sems) if packs else []
+    packing = pack_copies(ctx, 0, ww_hbm, vw_hbm, fw_hbm, rest[0], pack_sems) if packs else []
     for copy in packing:
         copy.start()
     for copy in others:
@@ -181,10 +181,19 @@
     return lax.fori_loop(1, count, body, carry)
 
 
-def query_kernel(ctx, count, *rest):
-    recvs = rest[: -10]
-    (own_ref, query_ref, feat_ref, cum_ref, att_ref, stat_ref, sheet_ref, near_ref, p_ref,
-     cums_ref) = rest[-10:]
+def query_kernel(ctx, count, recvs, *rest):
+    recvs, rest = rest[:recvs], rest[recvs:]
+    own_ref, query_ref, feat_ref, cum_ref, *rest = rest
+    near_ref, p_ref, cums_ref, sems = rest[-4:]
+    packing = []
+    if len(rest) > 7:
+        *weights, pack_ref = rest[:3] + rest[6:7]
+        rest = rest[3:]
+        for n in range(pack_ref.shape[0]):
+            packing += pack_copies(ctx, 2 * n, *weights, pack_ref.at[n], sems.at[n])
+    for copy in packing:
+        copy.start()
+    att_ref, stat_ref, sheet_ref = rest[:3]
 
     def recv(d):
         return recvs[d - 1] if len(recvs) > 1 else recvs[0].at[d - 1]
@@ -284,12 +293,13 @@
     sheet = jnp.where(lane == 4, cum_c, sheet)
     sheet_ref[...] = sheet
     stat_ref[...] = jnp.transpose(sheet)[0:8, :]
-
-
-def gradient_kernel(ctx, count, recvs, stats, *rest):
+    for copy in packing:
+        copy.wait()
+
+
+def gradient_kernel(ctx, count, recvs, *rest):
     recvs, rest = rest[:recvs], rest[recvs:]
-    stats, rest = rest[:stats], rest[stats:]
-    own_ref, query_ref, feat_ref, sheet_ref, *rest, total_ref = rest
+    own_ref, query_ref, feat_ref, sheet_ref, stat_ref, *rest, total_ref = rest
 
     def recv(d):
         return recvs[d - 1] if len(recvs) > 1 else recvs[0].at[d - 1]
@@ -309,10 +319,7 @@
     lse_c, dw_c = sheet_ref[:, 0:1], sheet_ref[:, 1:2]
     rden_c, dl_c, cum_c = sheet_ref[:, 2:3], sheet_ref[:, 3:4], sheet_ref[:, 4:5]
     def stat(d):
-        if len(stats) == 1:
-            return stats[0].at[pl.ds(pl.multiple_of(8 * d, 8), 8)]
-        at = d.bit_length()
-        return stats[at].at[pl.ds(8 * (d - (1 << at >> 1)), 8)]
+        return stat_ref.at[partner(me, d, count)]
 
     mine_ref = stat(0)
     own_cum = mine_ref[4:5, :]
@@ -420,7 +427,7 @@
 
 
 def columns_kernel(ctx, distances, cat_ref, feat_ref, ww_ref, vw_ref, fw_ref, *rest):
-    pieces = rest[: len(distances)]
+    pieces, firsts = rest[: len(distances)], rest[len(distances) : len(distances) + 2]
     out_ref, tile_ref, sems = rest[-3:]
     nf2 = fw_ref.shape[0]
     heads = feat_ref.shape[1] // nf2
@@ -429,11 +436,10 @@
     copies = []
     for n, (e, ref) in enumerate(zip(distances, pieces)):
         part = pl.ds(pl.multiple_of(jnp.bitwise_xor(me, e) * tile, tile), tile)
+        views = [firsts[e % 2].at[e // 2]] + [ref.at[t] for t in range(heads - 2)]
         main = [ww_ref[part, :], vw_ref[part, :]]
-        main += [
-            ref[t, m * tile : (m + 1) * tile, :] for t in range(heads - 1) for m in range(3)
-        ]
-        feats = [fw_ref[:, part]] + [wide(ref.at[t], 3 * tile, nf2) for t in range(heads - 1)]
+        main += [v[m * tile : (m + 1) * tile, :] for v in views for m in range(3)]
+        feats = [fw_ref[:, part]] + [wide(v, 3 * tile, nf2) for v in views]
         total = nt(cat_ref[...], jnp.concatenate(main, axis=1))
         total += nn(feat_ref[...], jnp.concatenate(feats, axis=0))
         tile_ref[n] = total.astype(bf16)
@@ -549,46 +555,46 @@
     if count > 8:
         recv = [jnp.stack(recv)]
 
+    first_pack, first_args = [], []
     if spread:
-        near = [
-            lax.ppermute(outs[0], "tp", [(z, z ^ t) for z in range(heads)])
-            for t in range(1, heads)
-        ]
-
-    attended, stat, sheet = pl.pallas_call(
-        lambda *refs: query_kernel(ctx, count, *refs),
-        out_shape=(
+        across = lax.ppermute(outs[0], "tp", [(z, z ^ 2) for z in range(heads)])
+        across, own = lax.optimization_barrier((across, own))
+        near = [across, lax.ppermute(across, "tp", [(z, z ^ 1) for z in range(heads)])]
+        first_pack = [jax.ShapeDtypeStruct((chips, *packs[0].shape), bf16)]
+        first_args = in_hbm(window_weight, value_weight, fw_t)
+
+    attended, stat, sheet, *first = pl.pallas_call(
+        lambda *refs: query_kernel(ctx, count, len(recv), *refs),
+        out_shape=[
             jax.ShapeDtypeStruct((rows, dh), bf16),
             jax.ShapeDtypeStruct((8, rows), f32),
             jax.ShapeDtypeStruct((rows, LANES), f32),
-        ),
-        in_specs=[VMEM] * (len(recv) + 4),
-        out_specs=[VMEM] * 3,
+            *first_pack,
+        ],
+        in_specs=[VMEM] * (len(recv) + 4) + [HBM] * len(first_args),
+        out_specs=[VMEM] * (3 + len(first_pack)),
         scratch_shapes=[
             pltpu.VMEM((count, 2 * rows, dh), bf16),
             pltpu.VMEM((WINDOW // rows + 1, rows, rows), f32),
             pltpu.VMEM((count, rows), f32),
+            pltpu.SemaphoreType.DMA((chips, 5)),
         ],
         compiler_params=params,
         cost_estimate=cost(1, 1024),
         name="query_side",
-    )(*recv, own, query, feat, cum)
-    stats = [stat]
-    for name in reversed(ctx):
-        if spread and len(stats) == 2:
-            near, stats = lax.optimization_barrier((near, stats))
-        held = stats[0] if len(stats) == 1 else jnp.concatenate(stats, axis=0)
-        stats.append(lax.ppermute(held, name, swap))
-    if count > 8:
-        stats = [jnp.concatenate(stats, axis=0)]
-
+    )(*recv, own, query, feat, cum, *first_args)
     if spread:
+        near, stat, first = lax.optimization_barrier((near, stat, first))
+    stats = lax.all_gather(stat, ctx)
+
+    if spread:
+        first = lax.ppermute(first[0], "tp", [(z, z ^ 1) for z in range(heads)])
         near, stats = lax.optimization_barrier((near, stats))
         pieces = [
             pl.pallas_call(
                 stack_kernel,
-                out_shape=jax.ShapeDtypeStruct((heads - 1, *packs[0].shape), bf16),
-                in_specs=[VMEM] * (heads - 1),
+                out_shape=jax.ShapeDtypeStruct((heads - 2, *packs[0].shape), bf16),
+                in_specs=[VMEM] * (heads - 2),
                 out_specs=VMEM,
                 compiler_params=params,
                 cost_estimate=cost(1, 1024),
@@ -599,26 +605,26 @@
             pieces.append(
                 lax.ppermute(pieces[0], ctx[:-1], [(i, i ^ d) for i in range(chips)])
             )
-        first, sheet = lax.optimization_barrier((pieces[0], sheet))
-        pieces[0] = first
+        pieces[0], sheet = lax.optimization_barrier((pieces[0], sheet))
 
     grads = pl.pallas_call(
-        lambda *refs: gradient_kernel(ctx, count, len(recv), len(stats), *refs),
+        lambda *refs: gradient_kernel(ctx, count, len(recv), *refs),
         out_shape=jax.ShapeDtypeStruct((3 * rows + nf2 * rows // LANES, LANES), bf16),
-        in_specs=[VMEM] * (len(recv) + len(stats) + 4),
+        in_specs=[VMEM] * (len(recv) + 5),
         out_specs=VMEM,
         scratch_shapes=[pltpu.VMEM((count, LANES), f32)],
         compiler_params=params,
         cost_estimate=cost(1, 1024),
         name="gradients",
-    )(*recv, *stats, own, query, feat, sheet)
+    )(*recv, own, query, feat, sheet, stats)
     if not spread:
         weights = jnp.concatenate([window_weight, value_weight, feature_weight], axis=1)
         weights = lax.all_gather(weights, "tp")
         return (attended, merge(lax.all_gather(grads, "tp"), weights, rows, dim))
 
-    swapped = {0: lax.ppermute(pieces[0], "core", swap)}
-    swapped[0], grads = lax.optimization_barrier((swapped[0], grads))
+    first, grads = lax.optimization_barrier((first, grads))
+    swapped = [lax.ppermute(pieces[0], "core", swap)]
+    firsts = [first, lax.ppermute(first, "core", swap)]
     grads = lax.all_gather(grads, "tp")
     cat, feats = pl.pallas_call(
         cat_kernel,
@@ -632,22 +638,18 @@
         cost_estimate=cost(1, 1024),
         name="cat",
     )(grads)
+    pieces, _ = lax.optimization_barrier((pieces, cat))
+    swapped += [lax.ppermute(p, "core", swap) for p in pieces[1:]]
+
     total = []
-    for distances in ((0, 1), (2,), (3, 4, 6), (5, 7)):
-        if distances == (2,):
-            pieces[1], total = lax.optimization_barrier((pieces[1], total))
-            swapped[1] = lax.ppermute(pieces[1], "core", swap)
-        if distances == (3, 4, 6):
-            pieces[2:], total = lax.optimization_barrier((pieces[2:], total))
-            for d in range(2, chips):
-                swapped[d] = lax.ppermute(pieces[d], "core", swap)
+    for distances in ((0, 1, 2, 4, 6), (3, 5, 7)):
         parts = [(swapped if e % 2 else pieces)[e // 2] for e in distances]
-        args = [cat, feats, ww, vw, fw, *parts, *total]
+        args = [cat, feats, ww, vw, fw, *parts, *firsts, *total]
         total = [
             pl.pallas_call(
                 partial(columns_kernel, ctx, distances),
                 out_shape=jax.ShapeDtypeStruct((rows, dim), bf16),
-                in_specs=[VMEM] * (5 + len(parts)) + [ANY] * len(total),
+                in_specs=[VMEM] * (7 + len(parts)) + [ANY] * len(total),
                 out_specs=ANY,
                 scratch_shapes=[
                     pltpu.VMEM((len(parts), rows, tile), bf16),

time: 78.9 us -> 71.1 us (0.901)
  waiting for transfers between devices: 24.8 us -> 11.1 us
  blocking collectives: 19.5 us -> 29.4 us
  starting transfers between devices: 18.8 us -> 15.5 us
  Pallas kernels: 14.9 us -> 14.1 us
    all_gather x0 -> x1, blocking collectives: none -> 9.22 us  [per_device(): stats = lax.all_gather(stat, ctx)]
    ppermute x10 -> x8, waiting for transfers between devices: 16.3 us -> 10 us  [the longest x1 6.35 us: per_device(): across = lax.ppermute(outs[0], 'tp', [(z, z ^ 2) for z in range(heads)])]
    ppermute x3, waiting for transfers between devices: 3.88 us -> 0.01 us  [per_device(): lax.ppermute(sends[d], ctx[:-1], [(i, i ^ d) for i in range(chips)])]
    ppermute x3, waiting for transfers between devices: 3.59 us -> 0.01 us  [per_device(): lax.ppermute(pieces[0], ctx[:-1], [(i, i ^ d) for i in range(chips)])]
    ppermute x10 -> x8, starting transfers between devices: 9.98 us -> 7.42 us  [the longest x1 4.1 us: per_device(): across = lax.ppermute(outs[0], 'tp', [(z, z ^ 2) for z in range(heads)])]
    pallas_call x4 -> x2, Pallas kernels: 5.43 us -> 3.69 us  [per_device(): pl.pallas_call(partial(columns_kernel, ctx, distances), out_shape=jax.Sha...]
    ppermute x3, starting transfers between devices: 4.64 us -> 3.49 us  [per_device(): lax.ppermute(sends[d], ctx[:-1], [(i, i ^ d) for i in range(chips)])]
    pallas_call x3, Pallas kernels: 6.08 us -> 7.09 us  [the longest x1 3.59 us: per_device(): pl.pallas_call(lambda *refs: gradient_kernel(ctx, count, len(recv), *refs...]
  transfers between devices with their start and end apart: 20 -> 18, of which waited for: 10 -> 8; matrix products, arithmetic and copies ran while one was open for 0% -> 0% of each run, Pallas kernels for 13% -> 13%
where the time goes in v15:
time: 71.1 us; the launch traced here: 70.8 us
  blocking collectives  29.4 us (41%)
  starting transfers between devices  15.5 us (22%)
  Pallas kernels  14.1 us (20%)
  waiting for transfers between devices  11.1 us (16%)
  between operations  0.73 us (1%)
    all_gather x1, blocking collectives, per_device(): grads = lax.all_gather(grads, 'tp')  20.2 us
    all_gather x1, blocking collectives, per_device(): stats = lax.all_gather(stat, ctx)  9.22 us
    ppermute x1, waiting for transfers between devices, per_device(): across = lax.ppermute(outs[0], 'tp', [(z, z ^ 2) for z in range(heads)])  6.35 us
    ppermute x1, starting transfers between devices, per_device(): across = lax.ppermute(outs[0], 'tp', [(z, z ^ 2) for z in range(heads)])  4.1 us
    pallas_call x2, Pallas kernels, per_device(): pl.pallas_call(partial(columns_kernel, ctx, distances), out_shape=jax.Sha...  3.69 us
    pallas_call x1, Pallas kernels, per_device(): pl.pallas_call(lambda *refs: gradient_kernel(ctx, count, len(recv), *refs...  3.59 us
    ppermute x3, starting transfers between devices, per_device(): lax.ppermute(pieces[0], ctx[:-1], [(i, i ^ d) for i in range(chips)])  3.55 us
    ppermute x3, starting transfers between devices, per_device(): lax.ppermute(sends[d], ctx[:-1], [(i, i ^ d) for i in range(chips)])  3.49 us
  transfers between devices with their start and end apart: 18, of which 8 were waited for; matrix products, arithmetic and copies ran while one was open for 0% of the time, Pallas kernels for 13%

profile of v15, /device:TPU:0, one launch (start us, length us, event | category | flops | bytes accessed | tf_op | source)
XLA Modules:
  0.0 70.8 jit_solution(17133343164340367469)
XLA Ops:
  0.6 3.1 %project.1 = (bf16[832,128]{1,0:T(8,128)(2,1)S(1)}, bf16[560,128]{1,0:T(8,128)(2,1)S(1)}, bf16[560,128]{1,0:T(8,128)(2,1)S(1)}, bf16[560,128]{1,0:T(8,128)(2,1)S...) custom-call(bf16[256,2048]{1,0:T(8,128)(2,1)} %tok_hbm.1, ...), custom_call_target="tpu_custom_call" | custom-call | flops 1 | bytes 1024 | tf_op jit(solution)/shard_map/project/pallas_call | solution.py:520
  3.8 4.1 %collective-permute-start.7 = (bf16[832,128]{1,0:T(8,128)(2,1)S(1)}, bf16[832,128]{1,0:T(8,128)(2,1)S(1)}, u32[]{:S(2)}, u32[]{:S(2)}) collective-permute-start(bf16[832,128]{1,0:T(8,128)(2,1)S(1)} %get-tuple-element.41), channel_id=1, source_target_pairs={{0,2},{1,3},{2,0},{3,1},{4,6},{5,7},{6,4},{7,5},{8,10},{9,11},{10,... | collective-permute-start | bytes 638984 | tf_op jit(solution)/shard_map/ppermute | solution.py:560
  7.9 1.5 %collective-permute-start.1 = (bf16[560,128]{1,0:T(8,128)(2,1)S(1)}, bf16[560,128]{1,0:T(8,128)(2,1)S(1)}, u32[]{:S(2)}, u32[]{:S(2)}) collective-permute-start(bf16[560,128]{1,0:T(8,128)(2,1)S(1)} %get-tuple-element.38), channel_id=1, source_target_pairs={{0,8},{8,0},{16,24},{24,16},{1,9},{9,1},{17,25},{25,17},{2,10},{10... | collective-permute-start | bytes 430088 | tf_op jit(solution)/shard_map/ppermute | solution.py:550
  9.4 1.5 %collective-permute-start.3 = (bf16[560,128]{1,0:T(8,128)(2,1)S(1)}, bf16[560,128]{1,0:T(8,128)(2,1)S(1)}, u32[]{:S(2)}, u32[]{:S(2)}) collective-permute-start(bf16[560,128]{1,0:T(8,128)(2,1)S(1)} %get-tuple-element.39), channel_id=1, source_target_pairs={{0,16},{8,24},{16,0},{24,8},{1,17},{9,25},{17,1},{25,9},{2,18},{10... | collective-permute-start | bytes 430088 | tf_op jit(solution)/shard_map/ppermute | solution.py:550
  10.9 0.5 collective-permute-start.5
  11.4 6.3 %collective-permute-done.7.refs_0_ = bf16[832,128]{1,0:T(8,128)(2,1)S(1)} collective-permute-done((bf16[832,128]{1,0:T(8,128)(2,1)S(1)}, bf16[832,128]{1,0:T(8,128)(2,1)S(1)}, u32[]{:S(2)}, u32[]{:S(2)}) %collective-permute-start.7) | collective-permute-done | bytes 213024 | tf_op jit(solution)/shard_map/ppermute | solution.py:560
  17.7 0.7 %collective-permute-start.8 = (bf16[832,128]{1,0:T(8,128)(2,1)S(1)}, bf16[832,128]{1,0:T(8,128)(2,1)S(1)}, u32[]{:S(2)}, u32[]{:S(2)}) collective-permute-start(bf16[832,128]{1,0:T(8,128)(2,1)S(1)} %collective-permute-done.7.refs_0_), channel_id=1, source_target_pairs={{0,1},{1,0},{2,3},{3,2},{4,5},{5,4},{6,7},{7,6},{8,9},{9,8},{10,11... | collective-permute-start | bytes 638984 | tf_op jit(solution)/shard_map/ppermute | solution.py:562
  18.4 0.0 collective-permute-start
  18.4 0.0 collective-permute-done.1.refs_1_
  18.5 0.5 collective-permute-start.2
  19.0 0.0 collective-permute-done.3.refs_3_
  19.0 0.1 collective-permute-start.4
  19.0 0.0 collective-permute-done.5.refs_5_
  19.0 0.4 collective-permute-start.6
  19.5 0.3 collective-permute-done.refs_0_
  19.8 0.2 collective-permute-done.2.refs_2_
  20.0 0.3 collective-permute-done.4.refs_4_
  20.3 0.2 collective-permute-done.6.refs_6_
  20.5 3.5 %query_side.1 = (bf16[256,128]{1,0:T(8,128)(2,1)}, f32[8,256]{1,0:T(8,128)S(1)}, f32[256,128]{1,0:T(8,128)S(1)}, bf16[4,832,128]{2,1,0:T(8,128)(2,1)S(1)}) custom-call(bf16[560,128]{1,0:T(8,128)(2,1)S(1)} %collective-permute-done.refs_0_, bf16[560,128]{1,0:T(8,128)(2,1)S(1)} %collective-permute-done.1.refs_1_, ...), custom_call_target="tpu_custom_call" | custom-call | flops 1 | bytes 1024 | tf_op jit(solution)/shard_map/query_side/pallas_call | solution.py:566
  24.0 0.2 collective-permute-done.8.refs_1_
  24.2 1.4 %collective-permute-start.9 = (bf16[4,832,128]{2,1,0:T(8,128)(2,1)S(1)}, bf16[4,832,128]{2,1,0:T(8,128)(2,1)S(1)}, u32[]{:S(2)}, u32[]{:S(2)}) collective-permute-start(bf16[4,832,128]{2,1,0:T(8,128)(2,1)S(1)} %get-tuple-element.51), channel_id=1, source_target_pairs={{0,1},{1,0},{2,3},{3,2},{4,5},{5,4},{6,7},{7,6},{8,9},{9,8},{10,11... | collective-permute-start | bytes 2555912 | tf_op jit(solution)/shard_map/ppermute | solution.py:591
  25.6 9.2 %all-gather = f32[64,256]{1,0:T(8,128)S(1)} all-gather(f32[8,256]{1,0:T(8,128)S(1)} %get-tuple-element.54), channel_id=2, replica_groups=mesh['half0'=2,'half1'=2,'core'=2,'tp'=4] {'half0','half1','core'}, dimensions={0}, use_global_device_ids=true | all-gather | bytes 73728 | tf_op jit(solution)/shard_map/all_gather | solution.py:588
  34.9 1.6 %collective-permute-start.10 = (bf16[2,832,128]{2,1,0:T(8,128)(2,1)S(1)}, bf16[2,832,128]{2,1,0:T(8,128)(2,1)S(1)}, u32[]{:S(2)}, u32[]{:S(2)}) collective-permute-start(bf16[2,832,128]{2,1,0:T(8,128)(2,1)S(1)} %stack.1.rest_0_), channel_id=1, source_target_pairs={{0,8},{8,0},{16,24},{24,16},{1,9},{9,1},{17,25},{25,17},{2,10},{10... | collective-permute-start | bytes 1277960 | tf_op jit(solution)/shard_map/ppermute | solution.py:606
  36.4 0.5 collective-permute-start.11
  37.0 1.5 %collective-permute-start.12 = (bf16[2,832,128]{2,1,0:T(8,128)(2,1)S(1)}, bf16[2,832,128]{2,1,0:T(8,128)(2,1)S(1)}, u32[]{:S(2)}, u32[]{:S(2)}) collective-permute-start(bf16[2,832,128]{2,1,0:T(8,128)(2,1)S(1)} %stack.1.rest_0_), channel_id=1, source_target_pairs={{0,24},{8,16},{16,8},{24,0},{1,25},{9,17},{17,9},{25,1},{2,26},{10... | collective-permute-start | bytes 1277960 | tf_op jit(solution)/shard_map/ppermute | solution.py:606
  38.4 3.6 %gradients.1 = bf16[832,128]{1,0:T(8,128)(2,1)S(1)} custom-call(bf16[560,128]{1,0:T(8,128)(2,1)S(1)} %collective-permute-done.refs_0_, bf16[560,128]{1,0:T(8,128)(2,1)S(1)} %collective-permute-done.1.refs_1_, bf16[560,128]{1,0:T(8,128)(2,1)S(1)} %collective-permute-done.2.refs_2_, bf16[560,128]{1,0:T(8,128)(2,1)S(1)} %collective-permute-done.3.refs_3_, ...), custom_call_target="tpu_custom_call" | custom-call | flops 1 | bytes 1024 | tf_op jit(solution)/shard_map/gradients/pallas_call | solution.py:610
  42.0 3.2 %collective-permute-done.9.rest_5_.rest_3_ = bf16[4,832,128]{2,1,0:T(8,128)(2,1)S(1)} collective-permute-done((bf16[4,832,128]{2,1,0:T(8,128)(2,1)S(1)}, bf16[4,832,128]{2,1,0:T(8,128)(2,1)S(1)}, u32[]{:S(2)}, u32[]{:S(2)}) %collective-permute-start.9) | collective-permute-done | bytes 852000 | tf_op jit(solution)/shard_map/ppermute | solution.py:591
  45.3 0.0 collective-permute-start.16
  45.3 0.5 collective-permute-start.17
  45.8 20.2 %all-gather.1 = bf16[3328,128]{1,0:T(8,128)(2,1)S(1)} all-gather(bf16[832,128]{1,0:T(8,128)(2,1)S(1)} %gradients.1), channel_id=3, replica_groups=mesh['half0'=2,'half1'=2,'core'=2,'tp'=4] {'tp'}, dimensions={0}, use_global_device_ids=true | all-gather | bytes 1064960 | tf_op jit(solution)/shard_map/all_gather | solution.py:628
  65.9 0.2 cat.1
  66.1 0.0 collective-permute-done.10.rest_2_
  66.2 0.0 collective-permute-done.11.rest_3_
  66.2 0.0 collective-permute-done.12.rest_4_
  66.2 0.1 collective-permute-start.13
  66.3 0.5 collective-permute-start.14
  66.8 0.1 collective-permute-start.15
  66.8 0.0 collective-permute-done.17.rest_1_
  66.8 0.0 collective-permute-done.16.rest_6_.rest_4_
  66.8 2.1 %columns.2.rest_5_ = bf16[256,2048]{1,0:T(8,128)(2,1)} custom-call(bf16[256,1536]{1,0:T(8,128)(2,1)S(1)} %get-tuple-element.61.cat_ref, bf16[256,128]{1,0:T(8,128)(2,1)S(1)} %get-tuple-element.62.feat_ref, bf16[2048,256]{1,0:T(8,128)(2,1)S(1)} %get-tuple-element.63.ww_ref, bf16[2048,128]{1,0:T(8,128)(2,1)S(1)} %get-tuple-element.64.vw_ref, ...), custom_call_target="tpu_custom_call" | custom-call | flops 1 | bytes 1024 | tf_op jit(solution)/shard_map/columns/pallas_call | solution.py:649
  68.9 0.0 collective-permute-done.13.rest_0_
  69.0 0.0 collective-permute-done.14.rest_1_
  69.0 0.3 collective-permute-done.15.rest_2_
  69.2 1.6 %columns.3 = bf16[256,2048]{1,0:T(8,128)(2,1)} custom-call(bf16[256,1536]{1,0:T(8,128)(2,1)S(1)} %get-tuple-element.61.cat_ref, bf16[256,128]{1,0:T(8,128)(2,1)S(1)} %get-tuple-element.62.feat_ref, bf16[2048,256]{1,0:T(8,128)(2,1)S(1)} %get-tuple-element.63.ww_ref, bf16[2048,128]{1,0:T(8,128)(2,1)S(1)} %get-tuple-element.64.vw_ref, ...), custom_call_target="tpu_custom_call", output_to_operand_aliasing={{}: (10, {})} | custom-call | flops 1 | bytes 1024 | tf_op jit(solution)/shard_map/columns/pallas_call | solution.py:649
  (1 shorter events, 0.0 us)
Async XLA Ops:
  3.8 13.9 %collective-permute-start.7 = (bf16[832,128]{1,0:T(8,128)(2,1)S(1)}, bf16[832,128]{1,0:T(8,128)(2,1)S(1)}, u32[]{:S(2)}, u32[]{:S(2)}) collective-permute-start(bf16[832,128]{1,0:T(8,128)(2,1)S(1)} %get-tuple-element.41), channel_id=1, source_target_pairs={{0,2},{1,3},{2,0},{3,1},{4,6},{5,7},{6,4},{7,5},{8,10},{9,11},{10,... | collective-permute-start | bytes 638984 | tf_op jit(solution)/shard_map/ppermute | solution.py:560
  7.9 10.6 %collective-permute-start.1 = (bf16[560,128]{1,0:T(8,128)(2,1)S(1)}, bf16[560,128]{1,0:T(8,128)(2,1)S(1)}, u32[]{:S(2)}, u32[]{:S(2)}) collective-permute-start(bf16[560,128]{1,0:T(8,128)(2,1)S(1)} %get-tuple-element.38), channel_id=1, source_target_pairs={{0,8},{8,0},{16,24},{24,16},{1,9},{9,1},{17,25},{25,17},{2,10},{10... | collective-permute-start | bytes 430088 | tf_op jit(solution)/shard_map/ppermute | solution.py:550
  9.4 9.6 %collective-permute-start.3 = (bf16[560,128]{1,0:T(8,128)(2,1)S(1)}, bf16[560,128]{1,0:T(8,128)(2,1)S(1)}, u32[]{:S(2)}, u32[]{:S(2)}) collective-permute-start(bf16[560,128]{1,0:T(8,128)(2,1)S(1)} %get-tuple-element.39), channel_id=1, source_target_pairs={{0,16},{8,24},{16,0},{24,8},{1,17},{9,25},{17,1},{25,9},{2,18},{10... | collective-permute-start | bytes 430088 | tf_op jit(solution)/shard_map/ppermute | solution.py:550
  10.9 8.1 %collective-permute-start.5 = (bf16[560,128]{1,0:T(8,128)(2,1)S(1)}, bf16[560,128]{1,0:T(8,128)(2,1)S(1)}, u32[]{:S(2)}, u32[]{:S(2)}) collective-permute-start(bf16[560,128]{1,0:T(8,128)(2,1)S(1)} %get-tuple-element.40), channel_id=1, source_target_pairs={{0,24},{8,16},{16,8},{24,0},{1,25},{9,17},{17,9},{25,1},{2,26},{10... | collective-permute-start | bytes 430088 | tf_op jit(solution)/shard_map/ppermute | solution.py:550
  17.7 6.5 %collective-permute-start.8 = (bf16[832,128]{1,0:T(8,128)(2,1)S(1)}, bf16[832,128]{1,0:T(8,128)(2,1)S(1)}, u32[]{:S(2)}, u32[]{:S(2)}) collective-permute-start(bf16[832,128]{1,0:T(8,128)(2,1)S(1)} %collective-permute-done.7.refs_0_), channel_id=1, source_target_pairs={{0,1},{1,0},{2,3},{3,2},{4,5},{5,4},{6,7},{7,6},{8,9},{9,8},{10,11... | collective-permute-start | bytes 638984 | tf_op jit(solution)/shard_map/ppermute | solution.py:562
  18.4 1.4 %collective-permute-start = (bf16[560,128]{1,0:T(8,128)(2,1)S(1)}, bf16[560,128]{1,0:T(8,128)(2,1)S(1)}, u32[]{:S(2)}, u32[]{:S(2)}) collective-permute-start(bf16[560,128]{1,0:T(8,128)(2,1)S(1)} %get-tuple-element.37), channel_id=1, source_target_pairs={{0,4},{4,0},{1,5},{5,1},{2,6},{6,2},{3,7},{7,3},{8,12},{12,8},{9,1... | collective-permute-start | bytes 430088 | tf_op jit(solution)/shard_map/ppermute | solution.py:551
  18.5 1.6 %collective-permute-start.2 = (bf16[560,128]{1,0:T(8,128)(2,1)S(1)}, bf16[560,128]{1,0:T(8,128)(2,1)S(1)}, u32[]{:S(2)}, u32[]{:S(2)}) collective-permute-start(bf16[560,128]{1,0:T(8,128)(2,1)S(1)} %collective-permute-done.1.refs_1_), channel_id=1, source_target_pairs={{0,4},{4,0},{1,5},{5,1},{2,6},{6,2},{3,7},{7,3},{8,12},{12,8},{9,1... | collective-permute-start | bytes 430088 | tf_op jit(solution)/shard_map/ppermute | solution.py:553
  19.0 1.4 %collective-permute-start.4 = (bf16[560,128]{1,0:T(8,128)(2,1)S(1)}, bf16[560,128]{1,0:T(8,128)(2,1)S(1)}, u32[]{:S(2)}, u32[]{:S(2)}) collective-permute-start(bf16[560,128]{1,0:T(8,128)(2,1)S(1)} %collective-permute-done.3.refs_3_), channel_id=1, source_target_pairs={{0,4},{4,0},{1,5},{5,1},{2,6},{6,2},{3,7},{7,3},{8,12},{12,8},{9,1... | collective-permute-start | bytes 430088 | tf_op jit(solution)/shard_map/ppermute | solution.py:553
  19.0 1.5 %collective-permute-start.6 = (bf16[560,128]{1,0:T(8,128)(2,1)S(1)}, bf16[560,128]{1,0:T(8,128)(2,1)S(1)}, u32[]{:S(2)}, u32[]{:S(2)}) collective-permute-start(bf16[560,128]{1,0:T(8,128)(2,1)S(1)} %collective-permute-done.5.refs_5_), channel_id=1, source_target_pairs={{0,4},{4,0},{1,5},{5,1},{2,6},{6,2},{3,7},{7,3},{8,12},{12,8},{9,1... | collective-permute-start | bytes 430088 | tf_op jit(solution)/shard_map/ppermute | solution.py:553
  24.2 21.1 %collective-permute-start.9 = (bf16[4,832,128]{2,1,0:T(8,128)(2,1)S(1)}, bf16[4,832,128]{2,1,0:T(8,128)(2,1)S(1)}, u32[]{:S(2)}, u32[]{:S(2)}) collective-permute-start(bf16[4,832,128]{2,1,0:T(8,128)(2,1)S(1)} %get-tuple-element.51), channel_id=1, source_target_pairs={{0,1},{1,0},{2,3},{3,2},{4,5},{5,4},{6,7},{7,6},{8,9},{9,8},{10,11... | collective-permute-start | bytes 2555912 | tf_op jit(solution)/shard_map/ppermute | solution.py:591
  34.9 31.3 %collective-permute-start.10 = (bf16[2,832,128]{2,1,0:T(8,128)(2,1)S(1)}, bf16[2,832,128]{2,1,0:T(8,128)(2,1)S(1)}, u32[]{:S(2)}, u32[]{:S(2)}) collective-permute-start(bf16[2,832,128]{2,1,0:T(8,128)(2,1)S(1)} %stack.1.rest_0_), channel_id=1, source_target_pairs={{0,8},{8,0},{16,24},{24,16},{1,9},{9,1},{17,25},{25,17},{2,10},{10... | collective-permute-start | bytes 1277960 | tf_op jit(solution)/shard_map/ppermute | solution.py:606
  36.4 29.7 %collective-permute-start.11 = (bf16[2,832,128]{2,1,0:T(8,128)(2,1)S(1)}, bf16[2,832,128]{2,1,0:T(8,128)(2,1)S(1)}, u32[]{:S(2)}, u32[]{:S(2)}) collective-permute-start(bf16[2,832,128]{2,1,0:T(8,128)(2,1)S(1)} %stack.1.rest_0_), channel_id=1, source_target_pairs={{0,16},{8,24},{16,0},{24,8},{1,17},{9,25},{17,1},{25,9},{2,18},{10... | collective-permute-start | bytes 1277960 | tf_op jit(solution)/shard_map/ppermute | solution.py:606
  37.0 29.2 %collective-permute-start.12 = (bf16[2,832,128]{2,1,0:T(8,128)(2,1)S(1)}, bf16[2,832,128]{2,1,0:T(8,128)(2,1)S(1)}, u32[]{:S(2)}, u32[]{:S(2)}) collective-permute-start(bf16[2,832,128]{2,1,0:T(8,128)(2,1)S(1)} %stack.1.rest_0_), channel_id=1, source_target_pairs={{0,24},{8,16},{16,8},{24,0},{1,25},{9,17},{17,9},{25,1},{2,26},{10... | collective-permute-start | bytes 1277960 | tf_op jit(solution)/shard_map/ppermute | solution.py:606
  45.3 21.6 %collective-permute-start.16 = (bf16[4,832,128]{2,1,0:T(8,128)(2,1)S(1)}, bf16[4,832,128]{2,1,0:T(8,128)(2,1)S(1)}, u32[]{:S(2)}, u32[]{:S(2)}) collective-permute-start(bf16[4,832,128]{2,1,0:T(8,128)(2,1)S(1)} %collective-permute-done.9.rest_5_.rest_3_), channel_id=1, source_target_pairs={{0,4},{4,0},{1,5},{5,1},{2,6},{6,2},{3,7},{7,3},{8,12},{12,8},{9,1... | collective-permute-start | bytes 2555912 | tf_op jit(solution)/shard_map/ppermute | solution.py:627
  45.3 21.6 %collective-permute-start.17 = (bf16[2,832,128]{2,1,0:T(8,128)(2,1)S(1)}, bf16[2,832,128]{2,1,0:T(8,128)(2,1)S(1)}, u32[]{:S(2)}, u32[]{:S(2)}) collective-permute-start(bf16[2,832,128]{2,1,0:T(8,128)(2,1)S(1)} %stack.1.rest_0_), channel_id=1, source_target_pairs={{0,4},{4,0},{1,5},{5,1},{2,6},{6,2},{3,7},{7,3},{8,12},{12,8},{9,1... | collective-permute-start | bytes 1277960 | tf_op jit(solution)/shard_map/ppermute | solution.py:626
  66.2 2.8 %collective-permute-start.13 = (bf16[2,832,128]{2,1,0:T(8,128)(2,1)S(1)}, bf16[2,832,128]{2,1,0:T(8,128)(2,1)S(1)}, u32[]{:S(2)}, u32[]{:S(2)}) collective-permute-start(bf16[2,832,128]{2,1,0:T(8,128)(2,1)S(1)} %collective-permute-done.10.rest_2_), channel_id=1, source_target_pairs={{0,4},{4,0},{1,5},{5,1},{2,6},{6,2},{3,7},{7,3},{8,12},{12,8},{9,1... | collective-permute-start | bytes 1277960 | tf_op jit(solution)/shard_map/ppermute | solution.py:642
  66.3 2.7 %collective-permute-start.14 = (bf16[2,832,128]{2,1,0:T(8,128)(2,1)S(1)}, bf16[2,832,128]{2,1,0:T(8,128)(2,1)S(1)}, u32[]{:S(2)}, u32[]{:S(2)}) collective-permute-start(bf16[2,832,128]{2,1,0:T(8,128)(2,1)S(1)} %collective-permute-done.11.rest_3_), channel_id=1, source_target_pairs={{0,4},{4,0},{1,5},{5,1},{2,6},{6,2},{3,7},{7,3},{8,12},{12,8},{9,1... | collective-permute-start | bytes 1277960 | tf_op jit(solution)/shard_map/ppermute | solution.py:642
  66.8 2.5 %collective-permute-start.15 = (bf16[2,832,128]{2,1,0:T(8,128)(2,1)S(1)}, bf16[2,832,128]{2,1,0:T(8,128)(2,1)S(1)}, u32[]{:S(2)}, u32[]{:S(2)}) collective-permute-start(bf16[2,832,128]{2,1,0:T(8,128)(2,1)S(1)} %collective-permute-done.12.rest_4_), channel_id=1, source_target_pairs={{0,4},{4,0},{1,5},{5,1},{2,6},{6,2},{3,7},{7,3},{8,12},{12,8},{9,1... | collective-permute-start | bytes 1277960 | tf_op jit(solution)/shard_map/ppermute | solution.py:642

commit v16 on v15

--- a/solution.py
+++ b/solution.py
@@ -64,25 +64,20 @@
     return place
 
 
-def pack_copies(ctx, distance, ww_hbm, vw_hbm, fw_hbm, out_ref, sems):
-    nf2 = fw_hbm.shape[0]
+def pack(me, ww_ref, vw_ref, fw_ref, out_ref):
+    nf2 = fw_ref.shape[0]
     tile = 2 * LANES
-    at = pl.multiple_of(jnp.bitwise_xor(block_index(ctx), distance) * tile, tile)
+    at = pl.multiple_of(me * tile, tile)
     rows = pl.ds(at, tile)
-    moves = [
-        (ww_hbm.at[rows, pl.ds(0, LANES)], out_ref.at[pl.ds(0, tile), :]),
-        (ww_hbm.at[rows, pl.ds(LANES, LANES)], out_ref.at[pl.ds(tile, tile), :]),
-        (vw_hbm.at[rows, :], out_ref.at[pl.ds(2 * tile, tile), :]),
-    ]
-    for m in range(2):
-        lanes = pl.ds(pl.multiple_of(at + m * LANES, LANES), LANES)
-        moves.append((fw_hbm.at[:, lanes], out_ref.at[pl.ds(3 * tile + m * nf2, nf2), :]))
-    return [pltpu.make_async_copy(src, dst, sems.at[n]) for n, (src, dst) in enumerate(moves)]
+    out_ref[0:tile, :] = ww_ref[rows, 0:LANES]
+    out_ref[tile : 2 * tile, :] = ww_ref[rows, LANES:]
+    out_ref[2 * tile : 3 * tile, :] = vw_ref[rows, :]
+    put_wide(out_ref, 3 * tile, fw_ref[:, rows])
 
 
 def project_kernel(ctx, packs, tok_hbm, fw_hbm, ww_hbm, vw_hbm, ld_hbm, do_hbm, *rest):
-    *sends, keys_ref, query_ref, feat_ref, cum_ref, ww_ref, vw_ref, fw_ref = rest[packs:-6]
-    tok_ref, ld_ref, do_ref, sems, small, pack_sems = rest[-6:]
+    *sends, keys_ref, query_ref, feat_ref, cum_ref, ww_ref, vw_ref, fw_ref = rest[packs:-5]
+    tok_ref, ld_ref, do_ref, sems, small = rest[-5:]
     me = block_index(ctx)
     rows, dim = tok_ref.shape
     dh = do_ref.shape[1]
@@ -106,9 +101,6 @@
     for group in copies:
         for at, copy in enumerate(group):
             copy.start(priority=min(at, 1))
-    packing = pack_copies(ctx, 0, ww_hbm, vw_hbm, fw_hbm, rest[0], pack_sems) if packs else []
-    for copy in packing:
-        copy.start()
     for copy in others:
         copy.wait()
     at_row, at_col = iotas(rows)
@@ -159,8 +151,8 @@
         later = jnp.bitwise_xor(me, max(2 * at, 1)) > me
         pl.when(later)(lambda ref=ref: put_keys(ref))
         pl.when(jnp.logical_not(later))(lambda ref=ref: put_query(ref))
-    for copy in packing:
-        copy.wait()
+    for ref in rest[:packs]:
+        pack(me, ww_ref, vw_ref, fw_ref, ref)
 
 def stack_kernel(*refs):
     *parts, out_ref = refs
@@ -184,15 +176,13 @@
 def query_kernel(ctx, count, recvs, *rest):
     recvs, rest = rest[:recvs], rest[recvs:]
     own_ref, query_ref, feat_ref, cum_ref, *rest = rest
-    near_ref, p_ref, cums_ref, sems = rest[-4:]
-    packing = []
-    if len(rest) > 7:
+    near_ref, p_ref, cums_ref = rest[-3:]
+    me = block_index(ctx)
+    if len(rest) > 6:
         *weights, pack_ref = rest[:3] + rest[6:7]
         rest = rest[3:]
         for n in range(pack_ref.shape[0]):
-            packing += pack_copies(ctx, 2 * n, *weights, pack_ref.at[n], sems.at[n])
-    for copy in packing:
-        copy.start()
+            pack(jnp.bitwise_xor(me, 2 * n), *weights, pack_ref.at[n])
     att_ref, stat_ref, sheet_ref = rest[:3]
 
     def recv(d):
@@ -293,13 +283,12 @@
     sheet = jnp.where(lane == 4, cum_c, sheet)
     sheet_ref[...] = sheet
     stat_ref[...] = jnp.transpose(sheet)[0:8, :]
-    for copy in packing:
-        copy.wait()
-
-
-def gradient_kernel(ctx, count, recvs, *rest):
+
+
+def gradient_kernel(ctx, count, recvs, stats, *rest):
     recvs, rest = rest[:recvs], rest[recvs:]
-    own_ref, query_ref, feat_ref, sheet_ref, stat_ref, *rest, total_ref = rest
+    stats, rest = rest[:stats], rest[stats:]
+    own_ref, query_ref, feat_ref, sheet_ref, *rest, total_ref = rest
 
     def recv(d):
         return recvs[d - 1] if len(recvs) > 1 else recvs[0].at[d - 1]
@@ -319,7 +308,10 @@
     lse_c, dw_c = sheet_ref[:, 0:1], sheet_ref[:, 1:2]
     rden_c, dl_c, cum_c = sheet_ref[:, 2:3], sheet_ref[:, 3:4], sheet_ref[:, 4:5]
     def stat(d):
-        return stat_ref.at[partner(me, d, count)]
+        if len(stats) == 1:
+            return stats[0].at[pl.ds(pl.multiple_of(8 * d, 8), 8)]
+        at = d.bit_length()
+        return stats[at].at[pl.ds(8 * (d - (1 << at >> 1)), 8)]
 
     mine_ref = stat(0)
     own_cum = mine_ref[4:5, :]
@@ -536,7 +528,6 @@
             pltpu.VMEM((rows, dh), bf16),
             pltpu.SemaphoreType.DMA((CHUNKS, 4)),
             pltpu.SemaphoreType.DMA((2,)),
-            pltpu.SemaphoreType.DMA((5,)),
         ],
         compiler_params=params,
         cost_estimate=cost(1, 1024),
@@ -549,7 +540,11 @@
     for d in range(1, chips):
         recv[2 * d] = lax.ppermute(sends[d], ctx[:-1], [(i, i ^ d) for i in range(chips)])
     recv[1] = lax.ppermute(sends[0], "core", swap)
+    if spread:
+        across = lax.ppermute(outs[0], "tp", [(z, z ^ 2) for z in range(heads)])
     for d in range(1, chips):
+        if spread and d == chips - 1:
+            across, recv[2 * d] = lax.optimization_barrier((across, recv[2 * d]))
         recv[2 * d + 1] = lax.ppermute(recv[2 * d], "core", swap)
     recv = [recv[d] for d in range(1, count)]
     if count > 8:
@@ -557,11 +552,10 @@
 
     first_pack, first_args = [], []
     if spread:
-        across = lax.ppermute(outs[0], "tp", [(z, z ^ 2) for z in range(heads)])
-        across, own = lax.optimization_barrier((across, own))
+        across, recv = lax.optimization_barrier((across, recv))
         near = [across, lax.ppermute(across, "tp", [(z, z ^ 1) for z in range(heads)])]
         first_pack = [jax.ShapeDtypeStruct((chips, *packs[0].shape), bf16)]
-        first_args = in_hbm(window_weight, value_weight, fw_t)
+        first_args = [ww, vw, fw]
 
     attended, stat, sheet, *first = pl.pallas_call(
         lambda *refs: query_kernel(ctx, count, len(recv), *refs),
@@ -571,13 +565,12 @@
             jax.ShapeDtypeStruct((rows, LANES), f32),
             *first_pack,
         ],
-        in_specs=[VMEM] * (len(recv) + 4) + [HBM] * len(first_args),
+        in_specs=[VMEM] * (len(recv) + 4 + len(first_args)),
         out_specs=[VMEM] * (3 + len(first_pack)),
         scratch_shapes=[
             pltpu.VMEM((count, 2 * rows, dh), bf16),
             pltpu.VMEM((WINDOW // rows + 1, rows, rows), f32),
             pltpu.VMEM((count, rows), f32),
-            pltpu.SemaphoreType.DMA((chips, 5)),
         ],
         compiler_params=params,
         cost_estimate=cost(1, 1024),
@@ -585,7 +578,12 @@
     )(*recv, own, query, feat, cum, *first_args)
     if spread:
         near, stat, first = lax.optimization_barrier((near, stat, first))
-    stats = lax.all_gather(stat, ctx)
+    stats = [stat]
+    for name in reversed(ctx):
+        held = stats[0] if len(stats) == 1 else jnp.concatenate(stats, axis=0)
+        stats.append(lax.ppermute(held, name, swap))
+    if count > 8:
+        stats = [jnp.concatenate(stats, axis=0)]
 
     if spread:
         first = lax.ppermute(first[0], "tp", [(z, z ^ 1) for z in range(heads)])
@@ -608,15 +606,15 @@
         pieces[0], sheet = lax.optimization_barrier((pieces[0], sheet))
 
     grads = pl.pallas_call(
-        lambda *refs: gradient_kernel(ctx, count, len(recv), *refs),
+        lambda *refs: gradient_kernel(ctx, count, len(recv), len(stats), *refs),
         out_shape=jax.ShapeDtypeStruct((3 * rows + nf2 * rows // LANES, LANES), bf16),
-        in_specs=[VMEM] * (len(recv) + 5),
+        in_specs=[VMEM] * (len(recv) + len(stats) + 4),
         out_specs=VMEM,
         scratch_shapes=[pltpu.VMEM((count, LANES), f32)],
         compiler_params=params,
         cost_estimate=cost(1, 1024),
         name="gradients",
-    )(*recv, own, query, feat, sheet, stats)
+    )(*recv, *stats, own, query, feat, sheet)
     if not spread:
         weights = jnp.concatenate([window_weight, value_weight, feature_weight], axis=1)
         weights = lax.all_gather(weights, "tp")

time: 71.1 us -> 72.5 us (1.020)
  waiting for transfers between devices: 11.1 us -> 20.5 us
  blocking collectives: 29.4 us -> 20.1 us
  starting transfers between devices: 15.5 us -> 17.9 us
  Pallas kernels: 14.1 us -> 13.1 us
    all_gather x1 -> x0, blocking collectives: 9.22 us -> none  [per_device(): stats = lax.all_gather(stat, ctx)]
    ppermute x0 -> x3, waiting for transfers between devices: none -> 6.73 us  [per_device(): stats.append(lax.ppermute(held, name, swap))]
    ppermute x1, waiting for transfers between devices: 6.35 us -> 0.16 us  [per_device(): across = lax.ppermute(outs[0], 'tp', [(z, z ^ 2) for z in range(heads)])]
    ppermute x3, waiting for transfers between devices: 0.01 us -> 6.17 us  [per_device(): lax.ppermute(sends[d], ctx[:-1], [(i, i ^ d) for i in range(chips)])]
    ppermute x1, waiting for transfers between devices: 0.17 us -> 3.39 us  [per_device(): lax.ppermute(across, 'tp', [(z, z ^ 1) for z in range(heads)])]
    ppermute x0 -> x3, starting transfers between devices: none -> 2.09 us  [per_device(): stats.append(lax.ppermute(held, name, swap))]
    pallas_call x1, Pallas kernels: 3.48 us -> 2.49 us  [per_device(): pl.pallas_call(lambda *refs: query_kernel(ctx, count, len(recv), *refs),...]
    ppermute x1, starting transfers between devices: 0.72 us -> 1.59 us  [per_device(): lax.ppermute(across, 'tp', [(z, z ^ 1) for z in range(heads)])]
  transfers between devices with their start and end apart: 18 -> 21, of which waited for: 8 -> 11; matrix products, arithmetic and copies ran while one was open for 0% -> 0% of each run, Pallas kernels for 13% -> 12%
where the time goes in v16:
time: 72.5 us; the launch traced here: 72.4 us
  waiting for transfers between devices  20.5 us (28%)
  blocking collectives  20.1 us (28%)
  starting transfers between devices  17.9 us (25%)
  Pallas kernels  13.1 us (18%)
  between operations  0.73 us (1%)
    all_gather x1, blocking collectives, per_device(): grads = lax.all_gather(grads, 'tp')  20.1 us
    ppermute x3, waiting for transfers between devices, per_device(): stats.append(lax.ppermute(held, name, swap))  6.73 us
    ppermute x3, waiting for transfers between devices, per_device(): lax.ppermute(sends[d], ctx[:-1], [(i, i ^ d) for i in range(chips)])  6.17 us
    ppermute x1, starting transfers between devices, per_device(): across = lax.ppermute(outs[0], 'tp', [(z, z ^ 2) for z in range(heads)])  4.1 us
    pallas_call x2, Pallas kernels, per_device(): pl.pallas_call(partial(columns_kernel, ctx, distances), out_shape=jax.Sha...  3.68 us
    pallas_call x1, Pallas kernels, per_device(): pl.pallas_call(lambda *refs: gradient_kernel(ctx, count, len(recv), len(s...  3.67 us
    ppermute x3, starting transfers between devices, per_device(): lax.ppermute(pieces[0], ctx[:-1], [(i, i ^ d) for i in range(chips)])  3.55 us
    ppermute x3, starting transfers between devices, per_device(): lax.ppermute(sends[d], ctx[:-1], [(i, i ^ d) for i in range(chips)])  3.49 us
  transfers between devices with their start and end apart: 21, of which 11 were waited for; matrix products, arithmetic and copies ran while one was open for 0% of the time, Pallas kernels for 12%

profile of v16, /device:TPU:0, one launch (start us, length us, event | category | flops | bytes accessed | tf_op | source)
XLA Modules:
  0.0 72.4 jit_solution(16963790229744361088)
XLA Ops:
  0.6 3.0 %project.1 = (bf16[832,128]{1,0:T(8,128)(2,1)S(1)}, bf16[560,128]{1,0:T(8,128)(2,1)S(1)}, bf16[560,128]{1,0:T(8,128)(2,1)S(1)}, bf16[560,128]{1,0:T(8,128)(2,1)S...) custom-call(bf16[256,2048]{1,0:T(8,128)(2,1)} %tok_hbm.1, ...), custom_call_target="tpu_custom_call" | custom-call | flops 1 | bytes 1024 | tf_op jit(solution)/shard_map/project/pallas_call | solution.py:512
  3.7 4.1 %collective-permute-start = (bf16[832,128]{1,0:T(8,128)(2,1)S(1)}, bf16[832,128]{1,0:T(8,128)(2,1)S(1)}, u32[]{:S(2)}, u32[]{:S(2)}) collective-permute-start(bf16[832,128]{1,0:T(8,128)(2,1)S(1)} %get-tuple-element.48), channel_id=1, source_target_pairs={{0,2},{1,3},{2,0},{3,1},{4,6},{5,7},{6,4},{7,5},{8,10},{9,11},{10,... | collective-permute-start | bytes 638984 | tf_op jit(solution)/shard_map/ppermute | solution.py:544
  7.8 1.5 %collective-permute-start.3 = (bf16[560,128]{1,0:T(8,128)(2,1)S(1)}, bf16[560,128]{1,0:T(8,128)(2,1)S(1)}, u32[]{:S(2)}, u32[]{:S(2)}) collective-permute-start(bf16[560,128]{1,0:T(8,128)(2,1)S(1)} %get-tuple-element.52), channel_id=1, source_target_pairs={{0,8},{8,0},{16,24},{24,16},{1,9},{9,1},{17,25},{25,17},{2,10},{10... | collective-permute-start | bytes 430088 | tf_op jit(solution)/shard_map/ppermute | solution.py:541
  9.3 1.5 %collective-permute-start.5 = (bf16[560,128]{1,0:T(8,128)(2,1)S(1)}, bf16[560,128]{1,0:T(8,128)(2,1)S(1)}, u32[]{:S(2)}, u32[]{:S(2)}) collective-permute-start(bf16[560,128]{1,0:T(8,128)(2,1)S(1)} %get-tuple-element.53), channel_id=1, source_target_pairs={{0,16},{8,24},{16,0},{24,8},{1,17},{9,25},{17,1},{25,9},{2,18},{10... | collective-permute-start | bytes 430088 | tf_op jit(solution)/shard_map/ppermute | solution.py:541
  10.8 0.5 collective-permute-start.1
  11.3 0.0 collective-permute-start.2
  11.3 2.4 %collective-permute-done.3.refs_1_ = bf16[560,128]{1,0:T(8,128)(2,1)S(1)} collective-permute-done((bf16[560,128]{1,0:T(8,128)(2,1)S(1)}, bf16[560,128]{1,0:T(8,128)(2,1)S(1)}, u32[]{:S(2)}, u32[]{:S(2)}) %collective-permute-start.3) | collective-permute-done | bytes 143392 | tf_op jit(solution)/shard_map/ppermute | solution.py:541
  13.7 0.0 collective-permute-start.4
  13.7 3.8 %collective-permute-done.5.refs_3_ = bf16[560,128]{1,0:T(8,128)(2,1)S(1)} collective-permute-done((bf16[560,128]{1,0:T(8,128)(2,1)S(1)}, bf16[560,128]{1,0:T(8,128)(2,1)S(1)}, u32[]{:S(2)}, u32[]{:S(2)}) %collective-permute-start.5) | collective-permute-done | bytes 143392 | tf_op jit(solution)/shard_map/ppermute | solution.py:541
  17.4 0.0 collective-permute-start.6
  17.5 0.0 collective-permute-done.1.refs_5_
  17.5 0.2 collective-permute-done.refs_0_
  17.6 0.4 collective-permute-start.7
  18.0 0.0 collective-permute-done.2.refs_0_
  18.0 0.0 collective-permute-done.4.refs_2_
  18.0 0.8 %collective-permute-done.6.refs_4_ = bf16[560,128]{1,0:T(8,128)(2,1)S(1)} collective-permute-done((bf16[560,128]{1,0:T(8,128)(2,1)S(1)}, bf16[560,128]{1,0:T(8,128)(2,1)S(1)}, u32[]{:S(2)}, u32[]{:S(2)}) %collective-permute-start.6) | collective-permute-done | bytes 143392 | tf_op jit(solution)/shard_map/ppermute | solution.py:548
  18.8 0.2 collective-permute-done.7.refs_6_
  19.0 1.6 %collective-permute-start.8 = (bf16[832,128]{1,0:T(8,128)(2,1)S(1)}, bf16[832,128]{1,0:T(8,128)(2,1)S(1)}, u32[]{:S(2)}, u32[]{:S(2)}) collective-permute-start(bf16[832,128]{1,0:T(8,128)(2,1)S(1)} %collective-permute-done.refs_0_), channel_id=1, source_target_pairs={{0,1},{1,0},{2,3},{3,2},{4,5},{5,4},{6,7},{7,6},{8,9},{9,8},{10,11... | collective-permute-start | bytes 638984 | tf_op jit(solution)/shard_map/ppermute | solution.py:556
  20.6 2.5 %query_side.1 = (bf16[256,128]{1,0:T(8,128)(2,1)}, f32[8,256]{1,0:T(8,128)S(1)}, f32[256,128]{1,0:T(8,128)S(1)}, bf16[4,832,128]{2,1,0:T(8,128)(2,1)S(1)}) custom-call(bf16[560,128]{1,0:T(8,128)(2,1)S(1)} %collective-permute-done.2.refs_0_, bf16[560,128]{1,0:T(8,128)(2,1)S(1)} %collective-permute-done.3.refs_1_, ...), custom_call_target="tpu_custom_call" | custom-call | flops 1 | bytes 1024 | tf_op jit(solution)/shard_map/query_side/pallas_call | solution.py:560
  23.1 3.4 %collective-permute-done.8.refs_1_ = bf16[832,128]{1,0:T(8,128)(2,1)S(1)} collective-permute-done((bf16[832,128]{1,0:T(8,128)(2,1)S(1)}, bf16[832,128]{1,0:T(8,128)(2,1)S(1)}, u32[]{:S(2)}, u32[]{:S(2)}) %collective-permute-start.8) | collective-permute-done | bytes 213024 | tf_op jit(solution)/shard_map/ppermute | solution.py:556
  26.5 1.6 %collective-permute-start.9 = (bf16[4,832,128]{2,1,0:T(8,128)(2,1)S(1)}, bf16[4,832,128]{2,1,0:T(8,128)(2,1)S(1)}, u32[]{:S(2)}, u32[]{:S(2)}) collective-permute-start(bf16[4,832,128]{2,1,0:T(8,128)(2,1)S(1)} %get-tuple-element.73), channel_id=1, source_target_pairs={{0,1},{1,0},{2,3},{3,2},{4,5},{5,4},{6,7},{7,6},{8,9},{9,8},{10,11... | collective-permute-start | bytes 2555912 | tf_op jit(solution)/shard_map/ppermute | solution.py:589
  28.1 0.0 collective-permute-start.10
  28.1 1.2 %collective-permute-done.10.refs_8_ = f32[8,256]{1,0:T(8,128)S(1)} collective-permute-done((f32[8,256]{1,0:T(8,128)S(1)}, f32[8,256]{1,0:T(8,128)S(1)}, u32[]{:S(2)}, u32[]{:S(2)}) %collective-permute-start.10) | collective-permute-done | bytes 8224 | tf_op jit(solution)/shard_map/ppermute | solution.py:584
  29.3 0.7 collective-permute-start.11
  30.0 3.0 %collective-permute-done.11.refs_9_ = f32[16,256]{1,0:T(8,128)S(1)} collective-permute-done((f32[16,256]{1,0:T(8,128)S(1)}, f32[16,256]{1,0:T(8,128)S(1)}, u32[]{:S(2)}, u32[]{:S(2)}) %collective-permute-start.11) | collective-permute-done | bytes 16416 | tf_op jit(solution)/shard_map/ppermute | solution.py:584
  33.0 1.4 %collective-permute-start.12 = (f32[32,256]{1,0:T(8,128)S(1)}, f32[32,256]{1,0:T(8,128)S(1)}, u32[]{:S(2)}, u32[]{:S(2)}) collective-permute-start(f32[32,256]{1,0:T(8,128)S(1)} %pad_maximum_fusion), channel_id=1, source_target_pairs={{0,16},{16,0},{1,17},{17,1},{2,18},{18,2},{3,19},{19,3},{4,20},{20... | collective-permute-start | bytes 98312 | tf_op jit(solution)/shard_map/ppermute | solution.py:584
  34.4 2.5 %collective-permute-done.12.refs_10_ = f32[32,256]{1,0:T(8,128)S(1)} collective-permute-done((f32[32,256]{1,0:T(8,128)S(1)}, f32[32,256]{1,0:T(8,128)S(1)}, u32[]{:S(2)}, u32[]{:S(2)}) %collective-permute-start.12) | collective-permute-done | bytes 32800 | tf_op jit(solution)/shard_map/ppermute | solution.py:584
  36.9 0.8 %collective-permute-start.13 = (bf16[2,832,128]{2,1,0:T(8,128)(2,1)S(1)}, bf16[2,832,128]{2,1,0:T(8,128)(2,1)S(1)}, u32[]{:S(2)}, u32[]{:S(2)}) collective-permute-start(bf16[2,832,128]{2,1,0:T(8,128)(2,1)S(1)} %stack.1.rest_0_), channel_id=1, source_target_pairs={{0,8},{8,0},{16,24},{24,16},{1,9},{9,1},{17,25},{25,17},{2,10},{10... | collective-permute-start | bytes 1277960 | tf_op jit(solution)/shard_map/ppermute | solution.py:604
  37.7 1.2 %collective-permute-start.14 = (bf16[2,832,128]{2,1,0:T(8,128)(2,1)S(1)}, bf16[2,832,128]{2,1,0:T(8,128)(2,1)S(1)}, u32[]{:S(2)}, u32[]{:S(2)}) collective-permute-start(bf16[2,832,128]{2,1,0:T(8,128)(2,1)S(1)} %stack.1.rest_0_), channel_id=1, source_target_pairs={{0,16},{8,24},{16,0},{24,8},{1,17},{9,25},{17,1},{25,9},{2,18},{10... | collective-permute-start | bytes 1277960 | tf_op jit(solution)/shard_map/ppermute | solution.py:604
  39.0 1.5 %collective-permute-start.15 = (bf16[2,832,128]{2,1,0:T(8,128)(2,1)S(1)}, bf16[2,832,128]{2,1,0:T(8,128)(2,1)S(1)}, u32[]{:S(2)}, u32[]{:S(2)}) collective-permute-start(bf16[2,832,128]{2,1,0:T(8,128)(2,1)S(1)} %stack.1.rest_0_), channel_id=1, source_target_pairs={{0,24},{8,16},{16,8},{24,0},{1,25},{9,17},{17,9},{25,1},{2,26},{10... | collective-permute-start | bytes 1277960 | tf_op jit(solution)/shard_map/ppermute | solution.py:604
  40.5 3.7 %gradients.1 = bf16[832,128]{1,0:T(8,128)(2,1)S(1)} custom-call(bf16[560,128]{1,0:T(8,128)(2,1)S(1)} %collective-permute-done.2.refs_0_, bf16[560,128]{1,0:T(8,128)(2,1)S(1)} %collective-permute-done.3.refs_1_, bf16[560,128]{1,0:T(8,128)(2,1)S(1)} %collective-permute-done.4.refs_2_, bf16[560,128]{1,0:T(8,128)(2,1)S(1)} %collective-permute-done.5.refs_3_, ...), custom_call_target="tpu_custom_call" | custom-call | flops 1 | bytes 1024 | tf_op jit(solution)/shard_map/gradients/pallas_call | solution.py:608
  44.2 2.7 %collective-permute-done.9.rest_5_.rest_3_ = bf16[4,832,128]{2,1,0:T(8,128)(2,1)S(1)} collective-permute-done((bf16[4,832,128]{2,1,0:T(8,128)(2,1)S(1)}, bf16[4,832,128]{2,1,0:T(8,128)(2,1)S(1)}, u32[]{:S(2)}, u32[]{:S(2)}) %collective-permute-start.9) | collective-permute-done | bytes 852000 | tf_op jit(solution)/shard_map/ppermute | solution.py:589
  46.9 0.0 collective-permute-start.19
  46.9 0.5 collective-permute-start.20
  47.4 20.1 %all-gather = bf16[3328,128]{1,0:T(8,128)(2,1)S(1)} all-gather(bf16[832,128]{1,0:T(8,128)(2,1)S(1)} %gradients.1), channel_id=2, replica_groups=mesh['half0'=2,'half1'=2,'core'=2,'tp'=4] {'tp'}, dimensions={0}, use_global_device_ids=true | all-gather | bytes 1064960 | tf_op jit(solution)/shard_map/all_gather | solution.py:626
  67.5 0.2 cat.1
  67.7 0.0 collective-permute-done.13.rest_2_
  67.7 0.0 collective-permute-done.14.rest_3_
  67.7 0.0 collective-permute-done.15.rest_4_
  67.7 0.1 collective-permute-start.16
  67.8 0.5 collective-permute-start.17
  68.3 0.1 collective-permute-start.18
  68.4 0.0 collective-permute-done.20.rest_1_
  68.4 0.0 collective-permute-done.19.rest_6_.rest_4_
  68.4 2.1 %columns.2.rest_5_ = bf16[256,2048]{1,0:T(8,128)(2,1)} custom-call(bf16[256,1536]{1,0:T(8,128)(2,1)S(1)} %get-tuple-element.86.cat_ref, bf16[256,128]{1,0:T(8,128)(2,1)S(1)} %get-tuple-element.87.feat_ref, bf16[2048,256]{1,0:T(8,128)(2,1)S(1)} %get-tuple-element.66.refs_11_.ww_ref, bf16[2048,128]{1,0:T(8,128)(2,1)S(1)} %get-tuple-element.67.refs_12_.vw_ref, ...), custom_call_target="tpu_custom_call" | custom-call | flops 1 | bytes 1024 | tf_op jit(solution)/shard_map/columns/pallas_call | solution.py:647
  70.5 0.0 collective-permute-done.16.rest_0_
  70.5 0.3 collective-permute-done.18.rest_2_
  70.8 1.6 %columns.3 = bf16[256,2048]{1,0:T(8,128)(2,1)} custom-call(bf16[256,1536]{1,0:T(8,128)(2,1)S(1)} %get-tuple-element.86.cat_ref, bf16[256,128]{1,0:T(8,128)(2,1)S(1)} %get-tuple-element.87.feat_ref, bf16[2048,256]{1,0:T(8,128)(2,1)S(1)} %get-tuple-element.66.refs_11_.ww_ref, ...), custom_call_target="tpu_custom_call", output_to_operand_aliasing={{}: (10, {})} | custom-call | flops 1 | bytes 1024 | tf_op jit(solution)/shard_map/columns/pallas_call | solution.py:647
  (4 shorter events, 0.0 us)
Async XLA Ops:
  3.7 13.9 %collective-permute-start = (bf16[832,128]{1,0:T(8,128)(2,1)S(1)}, bf16[832,128]{1,0:T(8,128)(2,1)S(1)}, u32[]{:S(2)}, u32[]{:S(2)}) collective-permute-start(bf16[832,128]{1,0:T(8,128)(2,1)S(1)} %get-tuple-element.48), channel_id=1, source_target_pairs={{0,2},{1,3},{2,0},{3,1},{4,6},{5,7},{6,4},{7,5},{8,10},{9,11},{10,... | collective-permute-start | bytes 638984 | tf_op jit(solution)/shard_map/ppermute | solution.py:544
  7.8 5.9 %collective-permute-start.3 = (bf16[560,128]{1,0:T(8,128)(2,1)S(1)}, bf16[560,128]{1,0:T(8,128)(2,1)S(1)}, u32[]{:S(2)}, u32[]{:S(2)}) collective-permute-start(bf16[560,128]{1,0:T(8,128)(2,1)S(1)} %get-tuple-element.52), channel_id=1, source_target_pairs={{0,8},{8,0},{16,24},{24,16},{1,9},{9,1},{17,25},{25,17},{2,10},{10... | collective-permute-start | bytes 430088 | tf_op jit(solution)/shard_map/ppermute | solution.py:541
  9.3 8.2 %collective-permute-start.5 = (bf16[560,128]{1,0:T(8,128)(2,1)S(1)}, bf16[560,128]{1,0:T(8,128)(2,1)S(1)}, u32[]{:S(2)}, u32[]{:S(2)}) collective-permute-start(bf16[560,128]{1,0:T(8,128)(2,1)S(1)} %get-tuple-element.53), channel_id=1, source_target_pairs={{0,16},{8,24},{16,0},{24,8},{1,17},{9,25},{17,1},{25,9},{2,18},{10... | collective-permute-start | bytes 430088 | tf_op jit(solution)/shard_map/ppermute | solution.py:541
  10.8 6.7 %collective-permute-start.1 = (bf16[560,128]{1,0:T(8,128)(2,1)S(1)}, bf16[560,128]{1,0:T(8,128)(2,1)S(1)}, u32[]{:S(2)}, u32[]{:S(2)}) collective-permute-start(bf16[560,128]{1,0:T(8,128)(2,1)S(1)} %get-tuple-element.49), channel_id=1, source_target_pairs={{0,24},{8,16},{16,8},{24,0},{1,25},{9,17},{17,9},{25,1},{2,26},{10... | collective-permute-start | bytes 430088 | tf_op jit(solution)/shard_map/ppermute | solution.py:541
  11.3 6.7 %collective-permute-start.2 = (bf16[560,128]{1,0:T(8,128)(2,1)S(1)}, bf16[560,128]{1,0:T(8,128)(2,1)S(1)}, u32[]{:S(2)}, u32[]{:S(2)}) collective-permute-start(bf16[560,128]{1,0:T(8,128)(2,1)S(1)} %get-tuple-element.51), channel_id=1, source_target_pairs={{0,4},{4,0},{1,5},{5,1},{2,6},{6,2},{3,7},{7,3},{8,12},{12,8},{9,1... | collective-permute-start | bytes 430088 | tf_op jit(solution)/shard_map/ppermute | solution.py:542
  13.7 4.3 %collective-permute-start.4 = (bf16[560,128]{1,0:T(8,128)(2,1)S(1)}, bf16[560,128]{1,0:T(8,128)(2,1)S(1)}, u32[]{:S(2)}, u32[]{:S(2)}) collective-permute-start(bf16[560,128]{1,0:T(8,128)(2,1)S(1)} %collective-permute-done.3.refs_1_), channel_id=1, source_target_pairs={{0,4},{4,0},{1,5},{5,1},{2,6},{6,2},{3,7},{7,3},{8,12},{12,8},{9,1... | collective-permute-start | bytes 430088 | tf_op jit(solution)/shard_map/ppermute | solution.py:548
  17.4 1.4 %collective-permute-start.6 = (bf16[560,128]{1,0:T(8,128)(2,1)S(1)}, bf16[560,128]{1,0:T(8,128)(2,1)S(1)}, u32[]{:S(2)}, u32[]{:S(2)}) collective-permute-start(bf16[560,128]{1,0:T(8,128)(2,1)S(1)} %collective-permute-done.5.refs_3_), channel_id=1, source_target_pairs={{0,4},{4,0},{1,5},{5,1},{2,6},{6,2},{3,7},{7,3},{8,12},{12,8},{9,1... | collective-permute-start | bytes 430088 | tf_op jit(solution)/shard_map/ppermute | solution.py:548
  17.6 1.4 %collective-permute-start.7 = (bf16[560,128]{1,0:T(8,128)(2,1)S(1)}, bf16[560,128]{1,0:T(8,128)(2,1)S(1)}, u32[]{:S(2)}, u32[]{:S(2)}) collective-permute-start(bf16[560,128]{1,0:T(8,128)(2,1)S(1)} %collective-permute-done.1.refs_5_), channel_id=1, source_target_pairs={{0,4},{4,0},{1,5},{5,1},{2,6},{6,2},{3,7},{7,3},{8,12},{12,8},{9,1... | collective-permute-start | bytes 430088 | tf_op jit(solution)/shard_map/ppermute | solution.py:548
  19.0 7.5 %collective-permute-start.8 = (bf16[832,128]{1,0:T(8,128)(2,1)S(1)}, bf16[832,128]{1,0:T(8,128)(2,1)S(1)}, u32[]{:S(2)}, u32[]{:S(2)}) collective-permute-start(bf16[832,128]{1,0:T(8,128)(2,1)S(1)} %collective-permute-done.refs_0_), channel_id=1, source_target_pairs={{0,1},{1,0},{2,3},{3,2},{4,5},{5,4},{6,7},{7,6},{8,9},{9,8},{10,11... | collective-permute-start | bytes 638984 | tf_op jit(solution)/shard_map/ppermute | solution.py:556
  26.5 20.4 %collective-permute-start.9 = (bf16[4,832,128]{2,1,0:T(8,128)(2,1)S(1)}, bf16[4,832,128]{2,1,0:T(8,128)(2,1)S(1)}, u32[]{:S(2)}, u32[]{:S(2)}) collective-permute-start(bf16[4,832,128]{2,1,0:T(8,128)(2,1)S(1)} %get-tuple-element.73), channel_id=1, source_target_pairs={{0,1},{1,0},{2,3},{3,2},{4,5},{5,4},{6,7},{7,6},{8,9},{9,8},{10,11... | collective-permute-start | bytes 2555912 | tf_op jit(solution)/shard_map/ppermute | solution.py:589
  28.1 1.2 %collective-permute-start.10 = (f32[8,256]{1,0:T(8,128)S(1)}, f32[8,256]{1,0:T(8,128)S(1)}, u32[]{:S(2)}, u32[]{:S(2)}) collective-permute-start(f32[8,256]{1,0:T(8,128)S(1)} %get-tuple-element.77.refs_7_), channel_id=1, source_target_pairs={{0,4},{4,0},{1,5},{5,1},{2,6},{6,2},{3,7},{7,3},{8,12},{12,8},{9,1... | collective-permute-start | bytes 24584 | tf_op jit(solution)/shard_map/ppermute | solution.py:584
  29.3 3.7 %collective-permute-start.11 = (f32[16,256]{1,0:T(8,128)S(1)}, f32[16,256]{1,0:T(8,128)S(1)}, u32[]{:S(2)}, u32[]{:S(2)}) collective-permute-start(f32[16,256]{1,0:T(8,128)S(1)} %pad_maximum_fusion.1), channel_id=1, source_target_pairs={{0,8},{8,0},{1,9},{9,1},{2,10},{10,2},{3,11},{11,3},{4,12},{12,4},... | collective-permute-start | bytes 49160 | tf_op jit(solution)/shard_map/ppermute | solution.py:584
  33.0 3.9 %collective-permute-start.12 = (f32[32,256]{1,0:T(8,128)S(1)}, f32[32,256]{1,0:T(8,128)S(1)}, u32[]{:S(2)}, u32[]{:S(2)}) collective-permute-start(f32[32,256]{1,0:T(8,128)S(1)} %pad_maximum_fusion), channel_id=1, source_target_pairs={{0,16},{16,0},{1,17},{17,1},{2,18},{18,2},{3,19},{19,3},{4,20},{20... | collective-permute-start | bytes 98312 | tf_op jit(solution)/shard_map/ppermute | solution.py:584
  36.9 30.7 %collective-permute-start.13 = (bf16[2,832,128]{2,1,0:T(8,128)(2,1)S(1)}, bf16[2,832,128]{2,1,0:T(8,128)(2,1)S(1)}, u32[]{:S(2)}, u32[]{:S(2)}) collective-permute-start(bf16[2,832,128]{2,1,0:T(8,128)(2,1)S(1)} %stack.1.rest_0_), channel_id=1, source_target_pairs={{0,8},{8,0},{16,24},{24,16},{1,9},{9,1},{17,25},{25,17},{2,10},{10... | collective-permute-start | bytes 1277960 | tf_op jit(solution)/shard_map/ppermute | solution.py:604
  37.7 30.0 %collective-permute-start.14 = (bf16[2,832,128]{2,1,0:T(8,128)(2,1)S(1)}, bf16[2,832,128]{2,1,0:T(8,128)(2,1)S(1)}, u32[]{:S(2)}, u32[]{:S(2)}) collective-permute-start(bf16[2,832,128]{2,1,0:T(8,128)(2,1)S(1)} %stack.1.rest_0_), channel_id=1, source_target_pairs={{0,16},{8,24},{16,0},{24,8},{1,17},{9,25},{17,1},{25,9},{2,18},{10... | collective-permute-start | bytes 1277960 | tf_op jit(solution)/shard_map/ppermute | solution.py:604
  39.0 28.7 %collective-permute-start.15 = (bf16[2,832,128]{2,1,0:T(8,128)(2,1)S(1)}, bf16[2,832,128]{2,1,0:T(8,128)(2,1)S(1)}, u32[]{:S(2)}, u32[]{:S(2)}) collective-permute-start(bf16[2,832,128]{2,1,0:T(8,128)(2,1)S(1)} %stack.1.rest_0_), channel_id=1, source_target_pairs={{0,24},{8,16},{16,8},{24,0},{1,25},{9,17},{17,9},{25,1},{2,26},{10... | collective-permute-start | bytes 1277960 | tf_op jit(solution)/shard_map/ppermute | solution.py:604
  46.9 21.5 %collective-permute-start.19 = (bf16[4,832,128]{2,1,0:T(8,128)(2,1)S(1)}, bf16[4,832,128]{2,1,0:T(8,128)(2,1)S(1)}, u32[]{:S(2)}, u32[]{:S(2)}) collective-permute-start(bf16[4,832,128]{2,1,0:T(8,128)(2,1)S(1)} %collective-permute-done.9.rest_5_.rest_3_), channel_id=1, source_target_pairs={{0,4},{4,0},{1,5},{5,1},{2,6},{6,2},{3,7},{7,3},{8,12},{12,8},{9,1... | collective-permute-start | bytes 2555912 | tf_op jit(solution)/shard_map/ppermute | solution.py:625
  46.9 21.5 %collective-permute-start.20 = (bf16[2,832,128]{2,1,0:T(8,128)(2,1)S(1)}, bf16[2,832,128]{2,1,0:T(8,128)(2,1)S(1)}, u32[]{:S(2)}, u32[]{:S(2)}) collective-permute-start(bf16[2,832,128]{2,1,0:T(8,128)(2,1)S(1)} %stack.1.rest_0_), channel_id=1, source_target_pairs={{0,4},{4,0},{1,5},{5,1},{2,6},{6,2},{3,7},{7,3},{8,12},{12,8},{9,1... | collective-permute-start | bytes 1277960 | tf_op jit(solution)/shard_map/ppermute | solution.py:624
  67.7 2.8 %collective-permute-start.16 = (bf16[2,832,128]{2,1,0:T(8,128)(2,1)S(1)}, bf16[2,832,128]{2,1,0:T(8,128)(2,1)S(1)}, u32[]{:S(2)}, u32[]{:S(2)}) collective-permute-start(bf16[2,832,128]{2,1,0:T(8,128)(2,1)S(1)} %collective-permute-done.13.rest_2_), channel_id=1, source_target_pairs={{0,4},{4,0},{1,5},{5,1},{2,6},{6,2},{3,7},{7,3},{8,12},{12,8},{9,1... | collective-permute-start | bytes 1277960 | tf_op jit(solution)/shard_map/ppermute | solution.py:640
  67.8 2.7 %collective-permute-start.17 = (bf16[2,832,128]{2,1,0:T(8,128)(2,1)S(1)}, bf16[2,832,128]{2,1,0:T(8,128)(2,1)S(1)}, u32[]{:S(2)}, u32[]{:S(2)}) collective-permute-start(bf16[2,832,128]{2,1,0:T(8,128)(2,1)S(1)} %collective-permute-done.14.rest_3_), channel_id=1, source_target_pairs={{0,4},{4,0},{1,5},{5,1},{2,6},{6,2},{3,7},{7,3},{8,12},{12,8},{9,1... | collective-permute-start | bytes 1277960 | tf_op jit(solution)/shard_map/ppermute | solution.py:640
  68.3 2.5 %collective-permute-start.18 = (bf16[2,832,128]{2,1,0:T(8,128)(2,1)S(1)}, bf16[2,832,128]{2,1,0:T(8,128)(2,1)S(1)}, u32[]{:S(2)}, u32[]{:S(2)}) collective-permute-start(bf16[2,832,128]{2,1,0:T(8,128)(2,1)S(1)} %collective-permute-done.15.rest_4_), channel_id=1, source_target_pairs={{0,4},{4,0},{1,5},{5,1},{2,6},{6,2},{3,7},{7,3},{8,12},{12,8},{9,1... | collective-permute-start | bytes 1277960 | tf_op jit(solution)/shard_map/ppermute | solution.py:640

commit v17 on v16

--- a/solution.py
+++ b/solution.py
@@ -151,8 +151,11 @@
         later = jnp.bitwise_xor(me, max(2 * at, 1)) > me
         pl.when(later)(lambda ref=ref: put_keys(ref))
         pl.when(jnp.logical_not(later))(lambda ref=ref: put_query(ref))
-    for ref in rest[:packs]:
-        pack(me, ww_ref, vw_ref, fw_ref, ref)
+    if packs:
+        own_pack, first_pack = rest[:packs]
+        pack(me, ww_ref, vw_ref, fw_ref, own_pack)
+        for n in range(first_pack.shape[0]):
+            pack(jnp.bitwise_xor(me, 2 * n), ww_ref, vw_ref, fw_ref, first_pack.at[n])
 
 def stack_kernel(*refs):
     *parts, out_ref = refs
@@ -177,12 +180,6 @@
     recvs, rest = rest[:recvs], rest[recvs:]
     own_ref, query_ref, feat_ref, cum_ref, *rest = rest
     near_ref, p_ref, cums_ref = rest[-3:]
-    me = block_index(ctx)
-    if len(rest) > 6:
-        *weights, pack_ref = rest[:3] + rest[6:7]
-        rest = rest[3:]
-        for n in range(pack_ref.shape[0]):
-            pack(jnp.bitwise_xor(me, 2 * n), *weights, pack_ref.at[n])
     att_ref, stat_ref, sheet_ref = rest[:3]
 
     def recv(d):
@@ -506,6 +503,7 @@
     packs = []
     if spread:
         packs = [jax.ShapeDtypeStruct((columns * tile // LANES, LANES), bf16)]
+        packs += [jax.ShapeDtypeStruct((chips, *packs[0].shape), bf16)]
 
     payload = 2 * rows + 2 * nf + 16
     block = jax.ShapeDtypeStruct((payload, LANES), bf16)
@@ -550,23 +548,19 @@
     if count > 8:
         recv = [jnp.stack(recv)]
 
-    first_pack, first_args = [], []
     if spread:
         across, recv = lax.optimization_barrier((across, recv))
         near = [across, lax.ppermute(across, "tp", [(z, z ^ 1) for z in range(heads)])]
-        first_pack = [jax.ShapeDtypeStruct((chips, *packs[0].shape), bf16)]
-        first_args = [ww, vw, fw]
-
-    attended, stat, sheet, *first = pl.pallas_call(
+
+    attended, stat, sheet = pl.pallas_call(
         lambda *refs: query_kernel(ctx, count, len(recv), *refs),
         out_shape=[
             jax.ShapeDtypeStruct((rows, dh), bf16),
             jax.ShapeDtypeStruct((8, rows), f32),
             jax.ShapeDtypeStruct((rows, LANES), f32),
-            *first_pack,
         ],
-        in_specs=[VMEM] * (len(recv) + 4 + len(first_args)),
-        out_specs=[VMEM] * (3 + len(first_pack)),
+        in_specs=[VMEM] * (len(recv) + 4),
+        out_specs=[VMEM] * 3,
         scratch_shapes=[
             pltpu.VMEM((count, 2 * rows, dh), bf16),
             pltpu.VMEM((WINDOW // rows + 1, rows, rows), f32),
@@ -575,9 +569,7 @@
         compiler_params=params,
         cost_estimate=cost(1, 1024),
         name="query_side",
-    )(*recv, own, query, feat, cum, *first_args)
-    if spread:
-        near, stat, first = lax.optimization_barrier((near, stat, first))
+    )(*recv, own, query, feat, cum)
     stats = [stat]
     for name in reversed(ctx):
         held = stats[0] if len(stats) == 1 else jnp.concatenate(stats, axis=0)
@@ -586,7 +578,7 @@
         stats = [jnp.concatenate(stats, axis=0)]
 
     if spread:
-        first = lax.ppermute(first[0], "tp", [(z, z ^ 1) for z in range(heads)])
+        first = lax.ppermute(outs[1], "tp", [(z, z ^ 1) for z in range(heads)])
         near, stats = lax.optimization_barrier((near, stats))
         pieces = [
             pl.pallas_call(

time: 72.5 us -> 76.2 us (1.051)
  starting transfers between devices: 17.9 us -> 21.1 us
  waiting for transfers between devices: 20.5 us -> 22.5 us
  blocking collectives: 20.1 us -> 18.5 us
    ppermute x1, waiting for transfers between devices: 0.16 us -> 10.7 us  [per_device(): across = lax.ppermute(outs[0], 'tp', [(z, z ^ 2) for z in range(heads)])]
    ppermute x1, waiting for transfers between devices: 3.39 us -> 0.01 us  [per_device(): lax.ppermute(across, 'tp', [(z, z ^ 1) for z in range(heads)])]
    ppermute x1, waiting for transfers between devices: 2.67 us -> 0.01 us  [per_device(): first = lax.ppermute(outs[1], 'tp', [(z, z ^ 1) for z in range(heads)])]
    ppermute x3, waiting for transfers between devices: 6.73 us -> 4.64 us  [per_device(): stats.append(lax.ppermute(held, name, swap))]
    ppermute x1, starting transfers between devices: 1.59 us -> 3.51 us  [per_device(): lax.ppermute(across, 'tp', [(z, z ^ 1) for z in range(heads)])]
    all_gather x1, blocking collectives: 20.1 us -> 18.5 us  [per_device(): grads = lax.all_gather(grads, 'tp')]
    ppermute x1, starting transfers between devices: 4.1 us -> 2.59 us  [per_device(): across = lax.ppermute(outs[0], 'tp', [(z, z ^ 2) for z in range(heads)])]
    ppermute x1, starting transfers between devices: 1.59 us -> 3.08 us  [per_device(): first = lax.ppermute(outs[1], 'tp', [(z, z ^ 1) for z in range(heads)])]
  transfers between devices with their start and end apart: 21 -> 21, of which waited for: 11 -> 7; matrix products, arithmetic and copies ran while one was open for 0% -> 0% of each run, Pallas kernels for 12% -> 11%
where the time goes in v17:
time: 76.2 us; the launch traced here: 76 us
  waiting for transfers between devices  22.5 us (30%)
  starting transfers between devices  21.1 us (28%)
  blocking collectives  18.5 us (24%)
  Pallas kernels  13.1 us (17%)
    all_gather x1, blocking collectives, per_device(): grads = lax.all_gather(grads, 'tp')  18.5 us
    ppermute x1, waiting for transfers between devices, per_device(): across = lax.ppermute(outs[0], 'tp', [(z, z ^ 2) for z in range(heads)])  10.7 us
    ppermute x3, waiting for transfers between devices, per_device(): lax.ppermute(sends[d], ctx[:-1], [(i, i ^ d) for i in range(chips)])  5.49 us
    ppermute x3, waiting for transfers between devices, per_device(): stats.append(lax.ppermute(held, name, swap))  4.64 us
    pallas_call x2, Pallas kernels, per_device(): pl.pallas_call(partial(columns_kernel, ctx, distances), out_shape=jax.Sha...  3.68 us
    pallas_call x1, Pallas kernels, per_device(): pl.pallas_call(lambda *refs: gradient_kernel(ctx, count, len(recv), len(s...  3.66 us
    ppermute x3, starting transfers between devices, per_device(): lax.ppermute(pieces[0], ctx[:-1], [(i, i ^ d) for i in range(chips)])  3.55 us
    ppermute x1, starting transfers between devices, per_device(): lax.ppermute(across, 'tp', [(z, z ^ 1) for z in range(heads)])  3.51 us
  transfers between devices with their start and end apart: 21, of which 7 were waited for; matrix products, arithmetic and copies ran while one was open for 0% of the time, Pallas kernels for 11%

profile of v17, /device:TPU:0, one launch (start us, length us, event | category | flops | bytes accessed | tf_op | source)
XLA Modules:
  0.0 76.0 jit_solution(7055688561141045140)
XLA Ops:
  0.6 3.2 %project.1 = (bf16[832,128]{1,0:T(8,128)(2,1)S(1)}, bf16[4,832,128]{2,1,0:T(8,128)(2,1)S(1)}, bf16[560,128]{1,0:T(8,128)(2,1)S(1)}, bf16[560,128]{1,0:T(8,128)(2...) custom-call(bf16[256,2048]{1,0:T(8,128)(2,1)} %tok_hbm.1, ...), custom_call_target="tpu_custom_call" | custom-call | flops 1 | bytes 1024 | tf_op jit(solution)/shard_map/project/pallas_call | solution.py:510
  3.8 3.1 %collective-permute-start.8 = (bf16[4,832,128]{2,1,0:T(8,128)(2,1)S(1)}, bf16[4,832,128]{2,1,0:T(8,128)(2,1)S(1)}, u32[]{:S(2)}, u32[]{:S(2)}) collective-permute-start(bf16[4,832,128]{2,1,0:T(8,128)(2,1)S(1)} %get-tuple-element.63), channel_id=1, source_target_pairs={{0,1},{1,0},{2,3},{3,2},{4,5},{5,4},{6,7},{7,6},{8,9},{9,8},{10,11... | collective-permute-start | bytes 2555912 | tf_op jit(solution)/shard_map/ppermute | solution.py:581
  6.9 2.6 %collective-permute-start = (bf16[832,128]{1,0:T(8,128)(2,1)S(1)}, bf16[832,128]{1,0:T(8,128)(2,1)S(1)}, u32[]{:S(2)}, u32[]{:S(2)}) collective-permute-start(bf16[832,128]{1,0:T(8,128)(2,1)S(1)} %get-tuple-element.44), channel_id=1, source_target_pairs={{0,2},{1,3},{2,0},{3,1},{4,6},{5,7},{6,4},{7,5},{8,10},{9,11},{10,... | collective-permute-start | bytes 638984 | tf_op jit(solution)/shard_map/ppermute | solution.py:542
  9.5 2.4 %collective-permute-start.1 = (bf16[560,128]{1,0:T(8,128)(2,1)S(1)}, bf16[560,128]{1,0:T(8,128)(2,1)S(1)}, u32[]{:S(2)}, u32[]{:S(2)}) collective-permute-start(bf16[560,128]{1,0:T(8,128)(2,1)S(1)} %get-tuple-element.45), channel_id=1, source_target_pairs={{0,24},{8,16},{16,8},{24,0},{1,25},{9,17},{17,9},{25,1},{2,26},{10... | collective-permute-start | bytes 430088 | tf_op jit(solution)/shard_map/ppermute | solution.py:539
  11.9 0.5 collective-permute-start.3
  12.5 0.5 collective-permute-start.5
  13.0 3.9 %collective-permute-done.1.refs_5_ = bf16[560,128]{1,0:T(8,128)(2,1)S(1)} collective-permute-done((bf16[560,128]{1,0:T(8,128)(2,1)S(1)}, bf16[560,128]{1,0:T(8,128)(2,1)S(1)}, u32[]{:S(2)}, u32[]{:S(2)}) %collective-permute-start.1) | collective-permute-done | bytes 143392 | tf_op jit(solution)/shard_map/ppermute | solution.py:539
  16.9 0.0 collective-permute-start.2
  16.9 1.6 %collective-permute-done.3.refs_1_ = bf16[560,128]{1,0:T(8,128)(2,1)S(1)} collective-permute-done((bf16[560,128]{1,0:T(8,128)(2,1)S(1)}, bf16[560,128]{1,0:T(8,128)(2,1)S(1)}, u32[]{:S(2)}, u32[]{:S(2)}) %collective-permute-start.3) | collective-permute-done | bytes 143392 | tf_op jit(solution)/shard_map/ppermute | solution.py:539
  18.5 0.0 collective-permute-start.4
  18.5 0.0 collective-permute-done.5.refs_3_
  18.5 0.5 collective-permute-start.6
  19.0 10.7 %collective-permute-done.refs_0_ = bf16[832,128]{1,0:T(8,128)(2,1)S(1)} collective-permute-done((bf16[832,128]{1,0:T(8,128)(2,1)S(1)}, bf16[832,128]{1,0:T(8,128)(2,1)S(1)}, u32[]{:S(2)}, u32[]{:S(2)}) %collective-permute-start) | collective-permute-done | bytes 213024 | tf_op jit(solution)/shard_map/ppermute | solution.py:542
  29.7 0.0 collective-permute-start.7
  29.7 0.0 collective-permute-done.2.refs_0_
  29.7 0.0 collective-permute-done.4.refs_2_
  29.7 0.0 collective-permute-done.6.refs_4_
  29.7 1.3 %collective-permute-done.7.refs_6_ = bf16[560,128]{1,0:T(8,128)(2,1)S(1)} collective-permute-done((bf16[560,128]{1,0:T(8,128)(2,1)S(1)}, bf16[560,128]{1,0:T(8,128)(2,1)S(1)}, u32[]{:S(2)}, u32[]{:S(2)}) %collective-permute-start.7) | collective-permute-done | bytes 143392 | tf_op jit(solution)/shard_map/ppermute | solution.py:546
  31.0 2.4 %query_side.1 = (bf16[256,128]{1,0:T(8,128)(2,1)}, f32[8,256]{1,0:T(8,128)S(1)}, f32[256,128]{1,0:T(8,128)S(1)}) custom-call(bf16[560,128]{1,0:T(8,128)(2,1)S(1)} %collective-permute-done.2.refs_0_, bf16[560,128]{1,0:T(8,128)(2,1)S(1)} %collective-permute-done.3.refs_1_, bf16[560,128]{1,0:T(8,128)(2,1)S(1)} %collective-permute-done.4.refs_2_, ...), custom_call_target="tpu_custom_call" | custom-call | flops 1 | bytes 1024 | tf_op jit(solution)/shard_map/query_side/pallas_call | solution.py:555
  33.4 0.1 collective-permute-start.10
  33.6 3.5 %collective-permute-start.9 = (bf16[832,128]{1,0:T(8,128)(2,1)S(1)}, bf16[832,128]{1,0:T(8,128)(2,1)S(1)}, u32[]{:S(2)}, u32[]{:S(2)}) collective-permute-start(bf16[832,128]{1,0:T(8,128)(2,1)S(1)} %collective-permute-done.refs_0_), channel_id=1, source_target_pairs={{0,1},{1,0},{2,3},{3,2},{4,5},{5,4},{6,7},{7,6},{8,9},{9,8},{10,11... | collective-permute-start | bytes 638984 | tf_op jit(solution)/shard_map/ppermute | solution.py:553
  37.1 0.0 collective-permute-done.10.refs_8_
  37.1 1.5 %collective-permute-start.11 = (f32[16,256]{1,0:T(8,128)S(1)}, f32[16,256]{1,0:T(8,128)S(1)}, u32[]{:S(2)}, u32[]{:S(2)}) collective-permute-start(f32[16,256]{1,0:T(8,128)S(1)} %pad_maximum_fusion.1), channel_id=1, source_target_pairs={{0,8},{8,0},{1,9},{9,1},{2,10},{10,2},{3,11},{11,3},{4,12},{12,4},... | collective-permute-start | bytes 49160 | tf_op jit(solution)/shard_map/ppermute | solution.py:576
  38.6 2.2 %collective-permute-done.11.refs_9_ = f32[16,256]{1,0:T(8,128)S(1)} collective-permute-done((f32[16,256]{1,0:T(8,128)S(1)}, f32[16,256]{1,0:T(8,128)S(1)}, u32[]{:S(2)}, u32[]{:S(2)}) %collective-permute-start.11) | collective-permute-done | bytes 16416 | tf_op jit(solution)/shard_map/ppermute | solution.py:576
  40.8 1.5 %collective-permute-start.12 = (f32[32,256]{1,0:T(8,128)S(1)}, f32[32,256]{1,0:T(8,128)S(1)}, u32[]{:S(2)}, u32[]{:S(2)}) collective-permute-start(f32[32,256]{1,0:T(8,128)S(1)} %pad_maximum_fusion), channel_id=1, source_target_pairs={{0,16},{16,0},{1,17},{17,1},{2,18},{18,2},{3,19},{19,3},{4,20},{20... | collective-permute-start | bytes 98312 | tf_op jit(solution)/shard_map/ppermute | solution.py:576
  42.4 2.4 %collective-permute-done.12.refs_10_ = f32[32,256]{1,0:T(8,128)S(1)} collective-permute-done((f32[32,256]{1,0:T(8,128)S(1)}, f32[32,256]{1,0:T(8,128)S(1)}, u32[]{:S(2)}, u32[]{:S(2)}) %collective-permute-start.12) | collective-permute-done | bytes 32800 | tf_op jit(solution)/shard_map/ppermute | solution.py:576
  44.8 0.0 collective-permute-done.9.refs_1_
  44.8 1.6 %collective-permute-start.13 = (bf16[2,832,128]{2,1,0:T(8,128)(2,1)S(1)}, bf16[2,832,128]{2,1,0:T(8,128)(2,1)S(1)}, u32[]{:S(2)}, u32[]{:S(2)}) collective-permute-start(bf16[2,832,128]{2,1,0:T(8,128)(2,1)S(1)} %stack.1.rest_0_), channel_id=1, source_target_pairs={{0,8},{8,0},{16,24},{24,16},{1,9},{9,1},{17,25},{25,17},{2,10},{10... | collective-permute-start | bytes 1277960 | tf_op jit(solution)/shard_map/ppermute | solution.py:596
  46.4 1.5 %collective-permute-start.14 = (bf16[2,832,128]{2,1,0:T(8,128)(2,1)S(1)}, bf16[2,832,128]{2,1,0:T(8,128)(2,1)S(1)}, u32[]{:S(2)}, u32[]{:S(2)}) collective-permute-start(bf16[2,832,128]{2,1,0:T(8,128)(2,1)S(1)} %stack.1.rest_0_), channel_id=1, source_target_pairs={{0,16},{8,24},{16,0},{24,8},{1,17},{9,25},{17,1},{25,9},{2,18},{10... | collective-permute-start | bytes 1277960 | tf_op jit(solution)/shard_map/ppermute | solution.py:596
  47.9 0.5 collective-permute-start.15
  48.3 3.7 %gradients.1 = bf16[832,128]{1,0:T(8,128)(2,1)S(1)} custom-call(bf16[560,128]{1,0:T(8,128)(2,1)S(1)} %collective-permute-done.2.refs_0_, bf16[560,128]{1,0:T(8,128)(2,1)S(1)} %collective-permute-done.3.refs_1_, bf16[560,128]{1,0:T(8,128)(2,1)S(1)} %collective-permute-done.4.refs_2_, bf16[560,128]{1,0:T(8,128)(2,1)S(1)} %collective-permute-done.5.refs_3_, ...), custom_call_target="tpu_custom_call" | custom-call | flops 1 | bytes 1024 | tf_op jit(solution)/shard_map/gradients/pallas_call | solution.py:600
  52.0 0.0 collective-permute-done.8.rest_5_.rest_3_
  52.0 0.1 collective-permute-start.19
  52.1 0.5 collective-permute-start.20
  52.6 18.5 %all-gather = bf16[3328,128]{1,0:T(8,128)(2,1)S(1)} all-gather(bf16[832,128]{1,0:T(8,128)(2,1)S(1)} %gradients.1), channel_id=2, replica_groups=mesh['half0'=2,'half1'=2,'core'=2,'tp'=4] {'tp'}, dimensions={0}, use_global_device_ids=true | all-gather | bytes 1064960 | tf_op jit(solution)/shard_map/all_gather | solution.py:618
  71.1 0.2 cat.1
  71.3 0.0 collective-permute-done.13.rest_2_
  71.3 0.0 collective-permute-done.14.rest_3_
  71.3 0.0 collective-permute-done.15.rest_4_
  71.4 0.1 collective-permute-start.16
  71.4 0.5 collective-permute-start.17
  71.9 0.1 collective-permute-start.18
  72.0 0.0 collective-permute-done.20.rest_1_
  72.0 0.0 collective-permute-done.19.rest_6_.rest_4_
  72.0 2.1 %columns.2.rest_5_ = bf16[256,2048]{1,0:T(8,128)(2,1)} custom-call(bf16[256,1536]{1,0:T(8,128)(2,1)S(1)} %get-tuple-element.75.cat_ref, bf16[256,128]{1,0:T(8,128)(2,1)S(1)} %get-tuple-element.76.feat_ref, bf16[2048,256]{1,0:T(8,128)(2,1)S(1)} %get-tuple-element.77.ww_ref, bf16[2048,128]{1,0:T(8,128)(2,1)S(1)} %get-tuple-element.78.vw_ref, ...), custom_call_target="tpu_custom_call" | custom-call | flops 1 | bytes 1024 | tf_op jit(solution)/shard_map/columns/pallas_call | solution.py:639
  74.1 0.0 collective-permute-done.16.rest_0_
  74.1 0.3 collective-permute-done.18.rest_2_
  74.4 1.6 %columns.3 = bf16[256,2048]{1,0:T(8,128)(2,1)} custom-call(bf16[256,1536]{1,0:T(8,128)(2,1)S(1)} %get-tuple-element.75.cat_ref, bf16[256,128]{1,0:T(8,128)(2,1)S(1)} %get-tuple-element.76.feat_ref, bf16[2048,256]{1,0:T(8,128)(2,1)S(1)} %get-tuple-element.77.ww_ref, bf16[2048,128]{1,0:T(8,128)(2,1)S(1)} %get-tuple-element.78.vw_ref, ...), custom_call_target="tpu_custom_call", output_to_operand_aliasing={{}: (10, {})} | custom-call | flops 1 | bytes 1024 | tf_op jit(solution)/shard_map/columns/pallas_call | solution.py:639
  (4 shorter events, 0.0 us)
Async XLA Ops:
  3.8 48.2 %collective-permute-start.8 = (bf16[4,832,128]{2,1,0:T(8,128)(2,1)S(1)}, bf16[4,832,128]{2,1,0:T(8,128)(2,1)S(1)}, u32[]{:S(2)}, u32[]{:S(2)}) collective-permute-start(bf16[4,832,128]{2,1,0:T(8,128)(2,1)S(1)} %get-tuple-element.63), channel_id=1, source_target_pairs={{0,1},{1,0},{2,3},{3,2},{4,5},{5,4},{6,7},{7,6},{8,9},{9,8},{10,11... | collective-permute-start | bytes 2555912 | tf_op jit(solution)/shard_map/ppermute | solution.py:581
  6.9 22.8 %collective-permute-start = (bf16[832,128]{1,0:T(8,128)(2,1)S(1)}, bf16[832,128]{1,0:T(8,128)(2,1)S(1)}, u32[]{:S(2)}, u32[]{:S(2)}) collective-permute-start(bf16[832,128]{1,0:T(8,128)(2,1)S(1)} %get-tuple-element.44), channel_id=1, source_target_pairs={{0,2},{1,3},{2,0},{3,1},{4,6},{5,7},{6,4},{7,5},{8,10},{9,11},{10,... | collective-permute-start | bytes 638984 | tf_op jit(solution)/shard_map/ppermute | solution.py:542
  9.5 7.4 %collective-permute-start.1 = (bf16[560,128]{1,0:T(8,128)(2,1)S(1)}, bf16[560,128]{1,0:T(8,128)(2,1)S(1)}, u32[]{:S(2)}, u32[]{:S(2)}) collective-permute-start(bf16[560,128]{1,0:T(8,128)(2,1)S(1)} %get-tuple-element.45), channel_id=1, source_target_pairs={{0,24},{8,16},{16,8},{24,0},{1,25},{9,17},{17,9},{25,1},{2,26},{10... | collective-permute-start | bytes 430088 | tf_op jit(solution)/shard_map/ppermute | solution.py:539
  11.9 6.5 %collective-permute-start.3 = (bf16[560,128]{1,0:T(8,128)(2,1)S(1)}, bf16[560,128]{1,0:T(8,128)(2,1)S(1)}, u32[]{:S(2)}, u32[]{:S(2)}) collective-permute-start(bf16[560,128]{1,0:T(8,128)(2,1)S(1)} %get-tuple-element.48), channel_id=1, source_target_pairs={{0,8},{8,0},{16,24},{24,16},{1,9},{9,1},{17,25},{25,17},{2,10},{10... | collective-permute-start | bytes 430088 | tf_op jit(solution)/shard_map/ppermute | solution.py:539
  12.5 6.0 %collective-permute-start.5 = (bf16[560,128]{1,0:T(8,128)(2,1)S(1)}, bf16[560,128]{1,0:T(8,128)(2,1)S(1)}, u32[]{:S(2)}, u32[]{:S(2)}) collective-permute-start(bf16[560,128]{1,0:T(8,128)(2,1)S(1)} %get-tuple-element.49), channel_id=1, source_target_pairs={{0,16},{8,24},{16,0},{24,8},{1,17},{9,25},{17,1},{25,9},{2,18},{10... | collective-permute-start | bytes 430088 | tf_op jit(solution)/shard_map/ppermute | solution.py:539
  16.9 12.8 %collective-permute-start.2 = (bf16[560,128]{1,0:T(8,128)(2,1)S(1)}, bf16[560,128]{1,0:T(8,128)(2,1)S(1)}, u32[]{:S(2)}, u32[]{:S(2)}) collective-permute-start(bf16[560,128]{1,0:T(8,128)(2,1)S(1)} %get-tuple-element.47), channel_id=1, source_target_pairs={{0,4},{4,0},{1,5},{5,1},{2,6},{6,2},{3,7},{7,3},{8,12},{12,8},{9,1... | collective-permute-start | bytes 430088 | tf_op jit(solution)/shard_map/ppermute | solution.py:540
  18.5 11.2 %collective-permute-start.4 = (bf16[560,128]{1,0:T(8,128)(2,1)S(1)}, bf16[560,128]{1,0:T(8,128)(2,1)S(1)}, u32[]{:S(2)}, u32[]{:S(2)}) collective-permute-start(bf16[560,128]{1,0:T(8,128)(2,1)S(1)} %collective-permute-done.3.refs_1_), channel_id=1, source_target_pairs={{0,4},{4,0},{1,5},{5,1},{2,6},{6,2},{3,7},{7,3},{8,12},{12,8},{9,1... | collective-permute-start | bytes 430088 | tf_op jit(solution)/shard_map/ppermute | solution.py:546
  18.5 11.2 %collective-permute-start.6 = (bf16[560,128]{1,0:T(8,128)(2,1)S(1)}, bf16[560,128]{1,0:T(8,128)(2,1)S(1)}, u32[]{:S(2)}, u32[]{:S(2)}) collective-permute-start(bf16[560,128]{1,0:T(8,128)(2,1)S(1)} %collective-permute-done.5.refs_3_), channel_id=1, source_target_pairs={{0,4},{4,0},{1,5},{5,1},{2,6},{6,2},{3,7},{7,3},{8,12},{12,8},{9,1... | collective-permute-start | bytes 430088 | tf_op jit(solution)/shard_map/ppermute | solution.py:546
  29.7 1.4 %collective-permute-start.7 = (bf16[560,128]{1,0:T(8,128)(2,1)S(1)}, bf16[560,128]{1,0:T(8,128)(2,1)S(1)}, u32[]{:S(2)}, u32[]{:S(2)}) collective-permute-start(bf16[560,128]{1,0:T(8,128)(2,1)S(1)} %collective-permute-done.1.refs_5_), channel_id=1, source_target_pairs={{0,4},{4,0},{1,5},{5,1},{2,6},{6,2},{3,7},{7,3},{8,12},{12,8},{9,1... | collective-permute-start | bytes 430088 | tf_op jit(solution)/shard_map/ppermute | solution.py:546
  33.4 3.7 %collective-permute-start.10 = (f32[8,256]{1,0:T(8,128)S(1)}, f32[8,256]{1,0:T(8,128)S(1)}, u32[]{:S(2)}, u32[]{:S(2)}) collective-permute-start(f32[8,256]{1,0:T(8,128)S(1)} %get-tuple-element.66.refs_7_), channel_id=1, source_target_pairs={{0,4},{4,0},{1,5},{5,1},{2,6},{6,2},{3,7},{7,3},{8,12},{12,8},{9,1... | collective-permute-start | bytes 24584 | tf_op jit(solution)/shard_map/ppermute | solution.py:576
  33.6 11.2 %collective-permute-start.9 = (bf16[832,128]{1,0:T(8,128)(2,1)S(1)}, bf16[832,128]{1,0:T(8,128)(2,1)S(1)}, u32[]{:S(2)}, u32[]{:S(2)}) collective-permute-start(bf16[832,128]{1,0:T(8,128)(2,1)S(1)} %collective-permute-done.refs_0_), channel_id=1, source_target_pairs={{0,1},{1,0},{2,3},{3,2},{4,5},{5,4},{6,7},{7,6},{8,9},{9,8},{10,11... | collective-permute-start | bytes 638984 | tf_op jit(solution)/shard_map/ppermute | solution.py:553
  37.1 3.7 %collective-permute-start.11 = (f32[16,256]{1,0:T(8,128)S(1)}, f32[16,256]{1,0:T(8,128)S(1)}, u32[]{:S(2)}, u32[]{:S(2)}) collective-permute-start(f32[16,256]{1,0:T(8,128)S(1)} %pad_maximum_fusion.1), channel_id=1, source_target_pairs={{0,8},{8,0},{1,9},{9,1},{2,10},{10,2},{3,11},{11,3},{4,12},{12,4},... | collective-permute-start | bytes 49160 | tf_op jit(solution)/shard_map/ppermute | solution.py:576
  40.8 3.9 %collective-permute-start.12 = (f32[32,256]{1,0:T(8,128)S(1)}, f32[32,256]{1,0:T(8,128)S(1)}, u32[]{:S(2)}, u32[]{:S(2)}) collective-permute-start(f32[32,256]{1,0:T(8,128)S(1)} %pad_maximum_fusion), channel_id=1, source_target_pairs={{0,16},{16,0},{1,17},{17,1},{2,18},{18,2},{3,19},{19,3},{4,20},{20... | collective-permute-start | bytes 98312 | tf_op jit(solution)/shard_map/ppermute | solution.py:576
  44.8 26.5 %collective-permute-start.13 = (bf16[2,832,128]{2,1,0:T(8,128)(2,1)S(1)}, bf16[2,832,128]{2,1,0:T(8,128)(2,1)S(1)}, u32[]{:S(2)}, u32[]{:S(2)}) collective-permute-start(bf16[2,832,128]{2,1,0:T(8,128)(2,1)S(1)} %stack.1.rest_0_), channel_id=1, source_target_pairs={{0,8},{8,0},{16,24},{24,16},{1,9},{9,1},{17,25},{25,17},{2,10},{10... | collective-permute-start | bytes 1277960 | tf_op jit(solution)/shard_map/ppermute | solution.py:596
  46.4 25.0 %collective-permute-start.14 = (bf16[2,832,128]{2,1,0:T(8,128)(2,1)S(1)}, bf16[2,832,128]{2,1,0:T(8,128)(2,1)S(1)}, u32[]{:S(2)}, u32[]{:S(2)}) collective-permute-start(bf16[2,832,128]{2,1,0:T(8,128)(2,1)S(1)} %stack.1.rest_0_), channel_id=1, source_target_pairs={{0,16},{8,24},{16,0},{24,8},{1,17},{9,25},{17,1},{25,9},{2,18},{10... | collective-permute-start | bytes 1277960 | tf_op jit(solution)/shard_map/ppermute | solution.py:596
  47.9 23.5 %collective-permute-start.15 = (bf16[2,832,128]{2,1,0:T(8,128)(2,1)S(1)}, bf16[2,832,128]{2,1,0:T(8,128)(2,1)S(1)}, u32[]{:S(2)}, u32[]{:S(2)}) collective-permute-start(bf16[2,832,128]{2,1,0:T(8,128)(2,1)S(1)} %stack.1.rest_0_), channel_id=1, source_target_pairs={{0,24},{8,16},{16,8},{24,0},{1,25},{9,17},{17,9},{25,1},{2,26},{10... | collective-permute-start | bytes 1277960 | tf_op jit(solution)/shard_map/ppermute | solution.py:596
  52.0 20.0 %collective-permute-start.19 = (bf16[4,832,128]{2,1,0:T(8,128)(2,1)S(1)}, bf16[4,832,128]{2,1,0:T(8,128)(2,1)S(1)}, u32[]{:S(2)}, u32[]{:S(2)}) collective-permute-start(bf16[4,832,128]{2,1,0:T(8,128)(2,1)S(1)} %collective-permute-done.8.rest_5_.rest_3_), channel_id=1, source_target_pairs={{0,4},{4,0},{1,5},{5,1},{2,6},{6,2},{3,7},{7,3},{8,12},{12,8},{9,1... | collective-permute-start | bytes 2555912 | tf_op jit(solution)/shard_map/ppermute | solution.py:617
  52.1 19.9 %collective-permute-start.20 = (bf16[2,832,128]{2,1,0:T(8,128)(2,1)S(1)}, bf16[2,832,128]{2,1,0:T(8,128)(2,1)S(1)}, u32[]{:S(2)}, u32[]{:S(2)}) collective-permute-start(bf16[2,832,128]{2,1,0:T(8,128)(2,1)S(1)} %stack.1.rest_0_), channel_id=1, source_target_pairs={{0,4},{4,0},{1,5},{5,1},{2,6},{6,2},{3,7},{7,3},{8,12},{12,8},{9,1... | collective-permute-start | bytes 1277960 | tf_op jit(solution)/shard_map/ppermute | solution.py:616
  71.4 2.8 %collective-permute-start.16 = (bf16[2,832,128]{2,1,0:T(8,128)(2,1)S(1)}, bf16[2,832,128]{2,1,0:T(8,128)(2,1)S(1)}, u32[]{:S(2)}, u32[]{:S(2)}) collective-permute-start(bf16[2,832,128]{2,1,0:T(8,128)(2,1)S(1)} %collective-permute-done.13.rest_2_), channel_id=1, source_target_pairs={{0,4},{4,0},{1,5},{5,1},{2,6},{6,2},{3,7},{7,3},{8,12},{12,8},{9,1... | collective-permute-start | bytes 1277960 | tf_op jit(solution)/shard_map/ppermute | solution.py:632
  71.4 2.7 %collective-permute-start.17 = (bf16[2,832,128]{2,1,0:T(8,128)(2,1)S(1)}, bf16[2,832,128]{2,1,0:T(8,128)(2,1)S(1)}, u32[]{:S(2)}, u32[]{:S(2)}) collective-permute-start(bf16[2,832,128]{2,1,0:T(8,128)(2,1)S(1)} %collective-permute-done.14.rest_3_), channel_id=1, source_target_pairs={{0,4},{4,0},{1,5},{5,1},{2,6},{6,2},{3,7},{7,3},{8,12},{12,8},{9,1... | collective-permute-start | bytes 1277960 | tf_op jit(solution)/shard_map/ppermute | solution.py:632
  71.9 2.5 %collective-permute-start.18 = (bf16[2,832,128]{2,1,0:T(8,128)(2,1)S(1)}, bf16[2,832,128]{2,1,0:T(8,128)(2,1)S(1)}, u32[]{:S(2)}, u32[]{:S(2)}) collective-permute-start(bf16[2,832,128]{2,1,0:T(8,128)(2,1)S(1)} %collective-permute-done.15.rest_4_), channel_id=1, source_target_pairs={{0,4},{4,0},{1,5},{5,1},{2,6},{6,2},{3,7},{7,3},{8,12},{12,8},{9,1... | collective-permute-start | bytes 1277960 | tf_op jit(solution)/shard_map/ppermute | solution.py:632

commit v18 on v17

--- a/solution.py
+++ b/solution.py
@@ -152,10 +152,12 @@
         pl.when(later)(lambda ref=ref: put_keys(ref))
         pl.when(jnp.logical_not(later))(lambda ref=ref: put_query(ref))
     if packs:
-        own_pack, first_pack = rest[:packs]
+        own_pack, *first_packs = rest[:packs]
         pack(me, ww_ref, vw_ref, fw_ref, own_pack)
-        for n in range(first_pack.shape[0]):
-            pack(jnp.bitwise_xor(me, 2 * n), ww_ref, vw_ref, fw_ref, first_pack.at[n])
+        for n, ref in enumerate(first_packs):
+            for d in range(2):
+                piece = jnp.bitwise_xor(me, 4 * n + 2 * d)
+                pack(piece, ww_ref, vw_ref, fw_ref, ref.at[d])
 
 def stack_kernel(*refs):
     *parts, out_ref = refs
@@ -416,7 +418,7 @@
 
 
 def columns_kernel(ctx, distances, cat_ref, feat_ref, ww_ref, vw_ref, fw_ref, *rest):
-    pieces, firsts = rest[: len(distances)], rest[len(distances) : len(distances) + 2]
+    pieces, firsts = rest[: len(distances)], rest[len(distances) : len(distances) + 4]
     out_ref, tile_ref, sems = rest[-3:]
     nf2 = fw_ref.shape[0]
     heads = feat_ref.shape[1] // nf2
@@ -425,7 +427,8 @@
     copies = []
     for n, (e, ref) in enumerate(zip(distances, pieces)):
         part = pl.ds(pl.multiple_of(jnp.bitwise_xor(me, e) * tile, tile), tile)
-        views = [firsts[e % 2].at[e // 2]] + [ref.at[t] for t in range(heads - 2)]
+        views = [firsts[2 * (e % 2) + e // 4].at[e // 2 % 2]]
+        views += [ref.at[t] for t in range(heads - 2)]
         main = [ww_ref[part, :], vw_ref[part, :]]
         main += [v[m * tile : (m + 1) * tile, :] for v in views for m in range(3)]
         feats = [fw_ref[:, part]] + [wide(v, 3 * tile, nf2) for v in views]
@@ -503,7 +506,7 @@
     packs = []
     if spread:
         packs = [jax.ShapeDtypeStruct((columns * tile // LANES, LANES), bf16)]
-        packs += [jax.ShapeDtypeStruct((chips, *packs[0].shape), bf16)]
+        packs += [jax.ShapeDtypeStruct((2, *packs[0].shape), bf16)] * (chips // 2)
 
     payload = 2 * rows + 2 * nf + 16
     block = jax.ShapeDtypeStruct((payload, LANES), bf16)
@@ -549,7 +552,7 @@
         recv = [jnp.stack(recv)]
 
     if spread:
-        across, recv = lax.optimization_barrier((across, recv))
+        across, recv, sent = lax.optimization_barrier((across, recv, outs[1]))
         near = [across, lax.ppermute(across, "tp", [(z, z ^ 1) for z in range(heads)])]
 
     attended, stat, sheet = pl.pallas_call(
@@ -578,7 +581,8 @@
         stats = [jnp.concatenate(stats, axis=0)]
 
     if spread:
-        first = lax.ppermute(outs[1], "tp", [(z, z ^ 1) for z in range(heads)])
+        later, stats = lax.optimization_barrier((outs[2], stats))
+        first = [lax.ppermute(p, "tp", [(z, z ^ 1) for z in range(heads)]) for p in (sent, later)]
         near, stats = lax.optimization_barrier((near, stats))
         pieces = [
             pl.pallas_call(
@@ -612,9 +616,9 @@
         weights = lax.all_gather(weights, "tp")
         return (attended, merge(lax.all_gather(grads, "tp"), weights, rows, dim))
 
-    first, grads = lax.optimization_barrier((first, grads))
+    first[0], grads = lax.optimization_barrier((first[0], grads))
     swapped = [lax.ppermute(pieces[0], "core", swap)]
-    firsts = [first, lax.ppermute(first, "core", swap)]
+    firsts = [lax.ppermute(first[0], "core", swap)]
     grads = lax.all_gather(grads, "tp")
     cat, feats = pl.pallas_call(
         cat_kernel,
@@ -628,18 +632,19 @@
         cost_estimate=cost(1, 1024),
         name="cat",
     )(grads)
-    pieces, _ = lax.optimization_barrier((pieces, cat))
+    pieces, first[1], _ = lax.optimization_barrier((pieces, first[1], cat))
+    firsts = [*first, *firsts, lax.ppermute(first[1], "core", swap)]
     swapped += [lax.ppermute(p, "core", swap) for p in pieces[1:]]
 
     total = []
     for distances in ((0, 1, 2, 4, 6), (3, 5, 7)):
         parts = [(swapped if e % 2 else pieces)[e // 2] for e in distances]
-        args = [cat, feats, ww, vw, fw, *parts, *firsts, *total]
+        args = [cat, feats, ww, vw, fw, *parts, *firsts[:3], firsts[3 if total else 2], *total]
         total = [
             pl.pallas_call(
                 partial(columns_kernel, ctx, distances),
                 out_shape=jax.ShapeDtypeStruct((rows, dim), bf16),
-                in_specs=[VMEM] * (7 + len(parts)) + [ANY] * len(total),
+                in_specs=[VMEM] * (9 + len(parts)) + [ANY] * len(total),
                 out_specs=ANY,
                 scratch_shapes=[
                     pltpu.VMEM((len(parts), rows, tile), bf16),

time: 76.2 us -> 70.3 us (0.923)
  waiting for transfers between devices: 22.5 us -> 17.9 us
  starting transfers between devices: 21.1 us -> 17.9 us
  blocking collectives: 18.5 us -> 20.4 us
    ppermute x1, waiting for transfers between devices: 10.7 us -> 0.17 us  [per_device(): across = lax.ppermute(outs[0], 'tp', [(z, z ^ 2) for z in range(heads)])]
    ppermute x1, waiting for transfers between devices: 0.01 us -> 3.51 us  [per_device(): lax.ppermute(across, 'tp', [(z, z ^ 1) for z in range(heads)])]
    ppermute x1, starting transfers between devices: 3.51 us -> 0.44 us  [per_device(): lax.ppermute(across, 'tp', [(z, z ^ 1) for z in range(heads)])]
    all_gather x1, blocking collectives: 18.5 us -> 20.4 us  [per_device(): grads = lax.all_gather(grads, 'tp')]
    ppermute x1, starting transfers between devices: 2.59 us -> 4.11 us  [per_device(): across = lax.ppermute(outs[0], 'tp', [(z, z ^ 2) for z in range(heads)])]
    ppermute x3, waiting for transfers between devices: 4.64 us -> 6.06 us  [per_device(): stats.append(lax.ppermute(held, name, swap))]
    ppermute x2 -> x4, waiting for transfers between devices: 0.01 us -> 0.9 us  [the longest x1 0.59 us: per_device(): firsts = [lax.ppermute(first[0], 'core', swap)]]
    ppermute x3, starting transfers between devices: 3.16 us -> 2.32 us  [per_device(): stats.append(lax.ppermute(held, name, swap))]
  transfers between devices with their start and end apart: 21 -> 23, of which waited for: 7 -> 11; matrix products, arithmetic and copies ran while one was open for 0% -> 0% of each run, Pallas kernels for 11% -> 12%
where the time goes in v18:
time: 70.3 us; the launch traced here: 70.1 us
  blocking collectives  20.4 us (29%)
  starting transfers between devices  17.9 us (25%)
  waiting for transfers between devices  17.9 us (25%)
  Pallas kernels  13.1 us (19%)
  between operations  0.74 us (1%)
    all_gather x1, blocking collectives, per_device(): grads = lax.all_gather(grads, 'tp')  20.4 us
    ppermute x3, waiting for transfers between devices, per_device(): lax.ppermute(sends[d], ctx[:-1], [(i, i ^ d) for i in range(chips)])  6.15 us
    ppermute x3, waiting for transfers between devices, per_device(): stats.append(lax.ppermute(held, name, swap))  6.06 us
    ppermute x1, starting transfers between devices, per_device(): across = lax.ppermute(outs[0], 'tp', [(z, z ^ 2) for z in range(heads)])  4.11 us
    pallas_call x2, Pallas kernels, per_device(): pl.pallas_call(partial(columns_kernel, ctx, distances), out_shape=jax.Sha...  3.69 us
    pallas_call x1, Pallas kernels, per_device(): pl.pallas_call(lambda *refs: gradient_kernel(ctx, count, len(recv), len(s...  3.64 us
    ppermute x3, starting transfers between devices, per_device(): lax.ppermute(pieces[0], ctx[:-1], [(i, i ^ d) for i in range(chips)])  3.55 us
    ppermute x1, waiting for transfers between devices, per_device(): lax.ppermute(across, 'tp', [(z, z ^ 1) for z in range(heads)])  3.51 us
  transfers between devices with their start and end apart: 23, of which 11 were waited for; matrix products, arithmetic and copies ran while one was open for 0% of the time, Pallas kernels for 12%

profile of v18, /device:TPU:0, one launch (start us, length us, event | category | flops | bytes accessed | tf_op | source)
XLA Modules:
  0.0 70.1 jit_solution(16855733936889238971)
XLA Ops:
  0.6 3.2 %project.1 = (bf16[832,128]{1,0:T(8,128)(2,1)S(1)}, bf16[2,832,128]{2,1,0:T(8,128)(2,1)S(1)}, bf16[2,832,128]{2,1,0:T(8,128)(2,1)S(1)}, bf16[560,128]{1,0:T(8,12...) custom-call(bf16[256,2048]{1,0:T(8,128)(2,1)} %tok_hbm.1, ...), custom_call_target="tpu_custom_call" | custom-call | flops 1 | bytes 1024 | tf_op jit(solution)/shard_map/project/pallas_call | solution.py:513
  3.8 4.1 %collective-permute-start = (bf16[832,128]{1,0:T(8,128)(2,1)S(1)}, bf16[832,128]{1,0:T(8,128)(2,1)S(1)}, u32[]{:S(2)}, u32[]{:S(2)}) collective-permute-start(bf16[832,128]{1,0:T(8,128)(2,1)S(1)} %get-tuple-element.52), channel_id=1, source_target_pairs={{0,2},{1,3},{2,0},{3,1},{4,6},{5,7},{6,4},{7,5},{8,10},{9,11},{10,... | collective-permute-start | bytes 638984 | tf_op jit(solution)/shard_map/ppermute | solution.py:545
  7.9 1.5 %collective-permute-start.3 = (bf16[560,128]{1,0:T(8,128)(2,1)S(1)}, bf16[560,128]{1,0:T(8,128)(2,1)S(1)}, u32[]{:S(2)}, u32[]{:S(2)}) collective-permute-start(bf16[560,128]{1,0:T(8,128)(2,1)S(1)} %get-tuple-element.56), channel_id=1, source_target_pairs={{0,8},{8,0},{16,24},{24,16},{1,9},{9,1},{17,25},{25,17},{2,10},{10... | collective-permute-start | bytes 430088 | tf_op jit(solution)/shard_map/ppermute | solution.py:542
  9.4 1.5 %collective-permute-start.5 = (bf16[560,128]{1,0:T(8,128)(2,1)S(1)}, bf16[560,128]{1,0:T(8,128)(2,1)S(1)}, u32[]{:S(2)}, u32[]{:S(2)}) collective-permute-start(bf16[560,128]{1,0:T(8,128)(2,1)S(1)} %get-tuple-element.57), channel_id=1, source_target_pairs={{0,16},{8,24},{16,0},{24,8},{1,17},{9,25},{17,1},{25,9},{2,18},{10... | collective-permute-start | bytes 430088 | tf_op jit(solution)/shard_map/ppermute | solution.py:542
  10.9 0.5 collective-permute-start.1
  11.4 0.0 collective-permute-start.2
  11.4 2.4 %collective-permute-done.3.refs_1_ = bf16[560,128]{1,0:T(8,128)(2,1)S(1)} collective-permute-done((bf16[560,128]{1,0:T(8,128)(2,1)S(1)}, bf16[560,128]{1,0:T(8,128)(2,1)S(1)}, u32[]{:S(2)}, u32[]{:S(2)}) %collective-permute-start.3) | collective-permute-done | bytes 143392 | tf_op jit(solution)/shard_map/ppermute | solution.py:542
  13.8 0.0 collective-permute-start.4
  13.8 3.7 %collective-permute-done.5.refs_3_ = bf16[560,128]{1,0:T(8,128)(2,1)S(1)} collective-permute-done((bf16[560,128]{1,0:T(8,128)(2,1)S(1)}, bf16[560,128]{1,0:T(8,128)(2,1)S(1)}, u32[]{:S(2)}, u32[]{:S(2)}) %collective-permute-start.5) | collective-permute-done | bytes 143392 | tf_op jit(solution)/shard_map/ppermute | solution.py:542
  17.6 0.2 collective-permute-done.refs_0_
  17.7 0.3 collective-permute-start.7
  18.1 0.0 collective-permute-done.2.refs_0_
  18.1 0.0 collective-permute-done.4.refs_2_
  18.1 0.8 %collective-permute-done.6.refs_4_ = bf16[560,128]{1,0:T(8,128)(2,1)S(1)} collective-permute-done((bf16[560,128]{1,0:T(8,128)(2,1)S(1)}, bf16[560,128]{1,0:T(8,128)(2,1)S(1)}, u32[]{:S(2)}, u32[]{:S(2)}) %collective-permute-start.6) | collective-permute-done | bytes 143392 | tf_op jit(solution)/shard_map/ppermute | solution.py:549
  18.9 0.2 collective-permute-done.7.refs_6_
  19.1 1.6 %collective-permute-start.8 = (bf16[2,832,128]{2,1,0:T(8,128)(2,1)S(1)}, bf16[2,832,128]{2,1,0:T(8,128)(2,1)S(1)}, u32[]{:S(2)}, u32[]{:S(2)}) collective-permute-start(bf16[2,832,128]{2,1,0:T(8,128)(2,1)S(1)} %get-tuple-element.72), channel_id=1, source_target_pairs={{0,1},{1,0},{2,3},{3,2},{4,5},{5,4},{6,7},{7,6},{8,9},{9,8},{10,11... | collective-permute-start | bytes 1277960 | tf_op jit(solution)/shard_map/ppermute | solution.py:585
  20.7 2.4 %query_side.1 = (bf16[256,128]{1,0:T(8,128)(2,1)}, f32[8,256]{1,0:T(8,128)S(1)}, f32[256,128]{1,0:T(8,128)S(1)}) custom-call(bf16[560,128]{1,0:T(8,128)(2,1)S(1)} %collective-permute-done.2.refs_0_, bf16[560,128]{1,0:T(8,128)(2,1)S(1)} %collective-permute-done.3.refs_1_, bf16[560,128]{1,0:T(8,128)(2,1)S(1)} %collective-permute-done.4.refs_2_, ...), custom_call_target="tpu_custom_call" | custom-call | flops 1 | bytes 1024 | tf_op jit(solution)/shard_map/query_side/pallas_call | solution.py:558
  23.1 0.0 collective-permute-start.10
  23.1 0.4 collective-permute-start.9
  23.6 0.7 collective-permute-done.10.refs_8_
  24.3 0.9 %collective-permute-start.11 = (f32[16,256]{1,0:T(8,128)S(1)}, f32[16,256]{1,0:T(8,128)S(1)}, u32[]{:S(2)}, u32[]{:S(2)}) collective-permute-start(f32[16,256]{1,0:T(8,128)S(1)} %pad_maximum_fusion.1), channel_id=1, source_target_pairs={{0,8},{8,0},{1,9},{9,1},{2,10},{10,2},{3,11},{11,3},{4,12},{12,4},... | collective-permute-start | bytes 49160 | tf_op jit(solution)/shard_map/ppermute | solution.py:579
  25.2 2.8 %collective-permute-done.11.refs_9_ = f32[16,256]{1,0:T(8,128)S(1)} collective-permute-done((f32[16,256]{1,0:T(8,128)S(1)}, f32[16,256]{1,0:T(8,128)S(1)}, u32[]{:S(2)}, u32[]{:S(2)}) %collective-permute-start.11) | collective-permute-done | bytes 16416 | tf_op jit(solution)/shard_map/ppermute | solution.py:579
  28.0 1.4 %collective-permute-start.12 = (f32[32,256]{1,0:T(8,128)S(1)}, f32[32,256]{1,0:T(8,128)S(1)}, u32[]{:S(2)}, u32[]{:S(2)}) collective-permute-start(f32[32,256]{1,0:T(8,128)S(1)} %pad_maximum_fusion), channel_id=1, source_target_pairs={{0,16},{16,0},{1,17},{17,1},{2,18},{18,2},{3,19},{19,3},{4,20},{20... | collective-permute-start | bytes 98312 | tf_op jit(solution)/shard_map/ppermute | solution.py:579
  29.4 2.5 %collective-permute-done.12.refs_10_ = f32[32,256]{1,0:T(8,128)S(1)} collective-permute-done((f32[32,256]{1,0:T(8,128)S(1)}, f32[32,256]{1,0:T(8,128)S(1)}, u32[]{:S(2)}, u32[]{:S(2)}) %collective-permute-start.12) | collective-permute-done | bytes 32800 | tf_op jit(solution)/shard_map/ppermute | solution.py:579
  31.9 0.9 %collective-permute-start.16 = (bf16[2,832,128]{2,1,0:T(8,128)(2,1)S(1)}, bf16[2,832,128]{2,1,0:T(8,128)(2,1)S(1)}, u32[]{:S(2)}, u32[]{:S(2)}) collective-permute-start(bf16[2,832,128]{2,1,0:T(8,128)(2,1)S(1)} %get-tuple-element.95), channel_id=1, source_target_pairs={{0,1},{1,0},{2,3},{3,2},{4,5},{5,4},{6,7},{7,6},{8,9},{9,8},{10,11... | collective-permute-start | bytes 1277960 | tf_op jit(solution)/shard_map/ppermute | solution.py:585
  32.8 3.5 %collective-permute-done.9.refs_1_ = bf16[832,128]{1,0:T(8,128)(2,1)S(1)} collective-permute-done((bf16[832,128]{1,0:T(8,128)(2,1)S(1)}, bf16[832,128]{1,0:T(8,128)(2,1)S(1)}, u32[]{:S(2)}, u32[]{:S(2)}) %collective-permute-start.9) | collective-permute-done | bytes 213024 | tf_op jit(solution)/shard_map/ppermute | solution.py:556
  36.4 2.6 %collective-permute-start.15 = (bf16[2,832,128]{2,1,0:T(8,128)(2,1)S(1)}, bf16[2,832,128]{2,1,0:T(8,128)(2,1)S(1)}, u32[]{:S(2)}, u32[]{:S(2)}) collective-permute-start(bf16[2,832,128]{2,1,0:T(8,128)(2,1)S(1)} %stack.1.rest_0_), channel_id=1, source_target_pairs={{0,24},{8,16},{16,8},{24,0},{1,25},{9,17},{17,9},{25,1},{2,26},{10... | collective-permute-start | bytes 1277960 | tf_op jit(solution)/shard_map/ppermute | solution.py:600
  38.9 0.5 collective-permute-start.14
  39.4 0.5 collective-permute-start.13
  39.9 0.0 collective-permute-done.8.rest_5_.rest_3_
  39.9 0.0 collective-permute-start.22
  39.9 3.6 %gradients.1 = bf16[832,128]{1,0:T(8,128)(2,1)S(1)} custom-call(bf16[560,128]{1,0:T(8,128)(2,1)S(1)} %collective-permute-done.2.refs_0_, bf16[560,128]{1,0:T(8,128)(2,1)S(1)} %collective-permute-done.3.refs_1_, bf16[560,128]{1,0:T(8,128)(2,1)S(1)} %collective-permute-done.4.refs_2_, bf16[560,128]{1,0:T(8,128)(2,1)S(1)} %collective-permute-done.5.refs_3_, ...), custom_call_target="tpu_custom_call" | custom-call | flops 1 | bytes 1024 | tf_op jit(solution)/shard_map/gradients/pallas_call | solution.py:604
  43.6 20.4 %all-gather = bf16[3328,128]{1,0:T(8,128)(2,1)S(1)} all-gather(bf16[832,128]{1,0:T(8,128)(2,1)S(1)} %gradients.1), channel_id=2, replica_groups=mesh['half0'=2,'half1'=2,'core'=2,'tp'=4] {'tp'}, dimensions={0}, use_global_device_ids=true | all-gather | bytes 1064960 | tf_op jit(solution)/shard_map/all_gather | solution.py:622
  64.0 0.2 cat.1
  64.2 0.0 collective-permute-done.16.rest_6_.rest_4_
  64.2 0.1 collective-permute-start.20
  64.3 0.0 collective-permute-done.13.rest_2_
  64.3 0.5 collective-permute-start.17
  64.9 0.1 collective-permute-start.18
  65.0 0.4 collective-permute-start.19
  65.4 0.0 collective-permute-done.22.rest_1_
  65.4 0.1 collective-permute-start.21
  65.5 0.6 collective-permute-done.20.rest_7_.rest_8_.rest_5_
  66.1 2.1 %columns.2.rest_7_ = bf16[256,2048]{1,0:T(8,128)(2,1)} custom-call(bf16[256,1536]{1,0:T(8,128)(2,1)S(1)} %get-tuple-element.89.cat_ref, bf16[256,128]{1,0:T(8,128)(2,1)S(1)} %get-tuple-element.90.feat_ref, bf16[2048,256]{1,0:T(8,128)(2,1)S(1)} %get-tuple-element.91.ww_ref, bf16[2048,128]{1,0:T(8,128)(2,1)S(1)} %get-tuple-element.92.vw_ref, ...), custom_call_target="tpu_custom_call" | custom-call | flops 1 | bytes 1024 | tf_op jit(solution)/shard_map/columns/pallas_call | solution.py:644
  68.2 0.0 collective-permute-done.17.rest_0_
  68.2 0.0 collective-permute-done.19.rest_2_
  68.2 0.3 collective-permute-done.21.rest_6_
  68.5 1.6 %columns.3 = bf16[256,2048]{1,0:T(8,128)(2,1)} custom-call(bf16[256,1536]{1,0:T(8,128)(2,1)S(1)} %get-tuple-element.89.cat_ref, bf16[256,128]{1,0:T(8,128)(2,1)S(1)} %get-tuple-element.90.feat_ref, bf16[2048,256]{1,0:T(8,128)(2,1)S(1)} %get-tuple-element.91.ww_ref, bf16[2048,128]{1,0:T(8,128)(2,1)S(1)} %get-tuple-element.92.vw_ref, ...), custom_call_target="tpu_custom_call", output_to_operand_aliasing={{}: (12, {})} | custom-call | flops 1 | bytes 1024 | tf_op jit(solution)/shard_map/columns/pallas_call | solution.py:644
  (8 shorter events, 0.0 us)
Async XLA Ops:
  3.8 13.9 %collective-permute-start = (bf16[832,128]{1,0:T(8,128)(2,1)S(1)}, bf16[832,128]{1,0:T(8,128)(2,1)S(1)}, u32[]{:S(2)}, u32[]{:S(2)}) collective-permute-start(bf16[832,128]{1,0:T(8,128)(2,1)S(1)} %get-tuple-element.52), channel_id=1, source_target_pairs={{0,2},{1,3},{2,0},{3,1},{4,6},{5,7},{6,4},{7,5},{8,10},{9,11},{10,... | collective-permute-start | bytes 638984 | tf_op jit(solution)/shard_map/ppermute | solution.py:545
  7.9 5.9 %collective-permute-start.3 = (bf16[560,128]{1,0:T(8,128)(2,1)S(1)}, bf16[560,128]{1,0:T(8,128)(2,1)S(1)}, u32[]{:S(2)}, u32[]{:S(2)}) collective-permute-start(bf16[560,128]{1,0:T(8,128)(2,1)S(1)} %get-tuple-element.56), channel_id=1, source_target_pairs={{0,8},{8,0},{16,24},{24,16},{1,9},{9,1},{17,25},{25,17},{2,10},{10... | collective-permute-start | bytes 430088 | tf_op jit(solution)/shard_map/ppermute | solution.py:542
  9.4 8.2 %collective-permute-start.5 = (bf16[560,128]{1,0:T(8,128)(2,1)S(1)}, bf16[560,128]{1,0:T(8,128)(2,1)S(1)}, u32[]{:S(2)}, u32[]{:S(2)}) collective-permute-start(bf16[560,128]{1,0:T(8,128)(2,1)S(1)} %get-tuple-element.57), channel_id=1, source_target_pairs={{0,16},{8,24},{16,0},{24,8},{1,17},{9,25},{17,1},{25,9},{2,18},{10... | collective-permute-start | bytes 430088 | tf_op jit(solution)/shard_map/ppermute | solution.py:542
  10.9 6.7 %collective-permute-start.1 = (bf16[560,128]{1,0:T(8,128)(2,1)S(1)}, bf16[560,128]{1,0:T(8,128)(2,1)S(1)}, u32[]{:S(2)}, u32[]{:S(2)}) collective-permute-start(bf16[560,128]{1,0:T(8,128)(2,1)S(1)} %get-tuple-element.53), channel_id=1, source_target_pairs={{0,24},{8,16},{16,8},{24,0},{1,25},{9,17},{17,9},{25,1},{2,26},{10... | collective-permute-start | bytes 430088 | tf_op jit(solution)/shard_map/ppermute | solution.py:542
  11.4 6.7 %collective-permute-start.2 = (bf16[560,128]{1,0:T(8,128)(2,1)S(1)}, bf16[560,128]{1,0:T(8,128)(2,1)S(1)}, u32[]{:S(2)}, u32[]{:S(2)}) collective-permute-start(bf16[560,128]{1,0:T(8,128)(2,1)S(1)} %get-tuple-element.55), channel_id=1, source_target_pairs={{0,4},{4,0},{1,5},{5,1},{2,6},{6,2},{3,7},{7,3},{8,12},{12,8},{9,1... | collective-permute-start | bytes 430088 | tf_op jit(solution)/shard_map/ppermute | solution.py:543
  13.8 4.3 %collective-permute-start.4 = (bf16[560,128]{1,0:T(8,128)(2,1)S(1)}, bf16[560,128]{1,0:T(8,128)(2,1)S(1)}, u32[]{:S(2)}, u32[]{:S(2)}) collective-permute-start(bf16[560,128]{1,0:T(8,128)(2,1)S(1)} %collective-permute-done.3.refs_1_), channel_id=1, source_target_pairs={{0,4},{4,0},{1,5},{5,1},{2,6},{6,2},{3,7},{7,3},{8,12},{12,8},{9,1... | collective-permute-start | bytes 430088 | tf_op jit(solution)/shard_map/ppermute | solution.py:549
  17.6 1.4 %collective-permute-start.6 = (bf16[560,128]{1,0:T(8,128)(2,1)S(1)}, bf16[560,128]{1,0:T(8,128)(2,1)S(1)}, u32[]{:S(2)}, u32[]{:S(2)}) collective-permute-start(bf16[560,128]{1,0:T(8,128)(2,1)S(1)} %collective-permute-done.5.refs_3_), channel_id=1, source_target_pairs={{0,4},{4,0},{1,5},{5,1},{2,6},{6,2},{3,7},{7,3},{8,12},{12,8},{9,1... | collective-permute-start | bytes 430088 | tf_op jit(solution)/shard_map/ppermute | solution.py:549
  17.7 1.4 %collective-permute-start.7 = (bf16[560,128]{1,0:T(8,128)(2,1)S(1)}, bf16[560,128]{1,0:T(8,128)(2,1)S(1)}, u32[]{:S(2)}, u32[]{:S(2)}) collective-permute-start(bf16[560,128]{1,0:T(8,128)(2,1)S(1)} %collective-permute-done.1.refs_5_), channel_id=1, source_target_pairs={{0,4},{4,0},{1,5},{5,1},{2,6},{6,2},{3,7},{7,3},{8,12},{12,8},{9,1... | collective-permute-start | bytes 430088 | tf_op jit(solution)/shard_map/ppermute | solution.py:549
  19.1 20.8 %collective-permute-start.8 = (bf16[2,832,128]{2,1,0:T(8,128)(2,1)S(1)}, bf16[2,832,128]{2,1,0:T(8,128)(2,1)S(1)}, u32[]{:S(2)}, u32[]{:S(2)}) collective-permute-start(bf16[2,832,128]{2,1,0:T(8,128)(2,1)S(1)} %get-tuple-element.72), channel_id=1, source_target_pairs={{0,1},{1,0},{2,3},{3,2},{4,5},{5,4},{6,7},{7,6},{8,9},{9,8},{10,11... | collective-permute-start | bytes 1277960 | tf_op jit(solution)/shard_map/ppermute | solution.py:585
  23.1 1.2 %collective-permute-start.10 = (f32[8,256]{1,0:T(8,128)S(1)}, f32[8,256]{1,0:T(8,128)S(1)}, u32[]{:S(2)}, u32[]{:S(2)}) collective-permute-start(f32[8,256]{1,0:T(8,128)S(1)} %get-tuple-element.80.refs_7_), channel_id=1, source_target_pairs={{0,4},{4,0},{1,5},{5,1},{2,6},{6,2},{3,7},{7,3},{8,12},{12,8},{9,1... | collective-permute-start | bytes 24584 | tf_op jit(solution)/shard_map/ppermute | solution.py:579
  23.1 13.2 %collective-permute-start.9 = (bf16[832,128]{1,0:T(8,128)(2,1)S(1)}, bf16[832,128]{1,0:T(8,128)(2,1)S(1)}, u32[]{:S(2)}, u32[]{:S(2)}) collective-permute-start(bf16[832,128]{1,0:T(8,128)(2,1)S(1)} %collective-permute-done.refs_0_), channel_id=1, source_target_pairs={{0,1},{1,0},{2,3},{3,2},{4,5},{5,4},{6,7},{7,6},{8,9},{9,8},{10,11... | collective-permute-start | bytes 638984 | tf_op jit(solution)/shard_map/ppermute | solution.py:556
  24.3 3.7 %collective-permute-start.11 = (f32[16,256]{1,0:T(8,128)S(1)}, f32[16,256]{1,0:T(8,128)S(1)}, u32[]{:S(2)}, u32[]{:S(2)}) collective-permute-start(f32[16,256]{1,0:T(8,128)S(1)} %pad_maximum_fusion.1), channel_id=1, source_target_pairs={{0,8},{8,0},{1,9},{9,1},{2,10},{10,2},{3,11},{11,3},{4,12},{12,4},... | collective-permute-start | bytes 49160 | tf_op jit(solution)/shard_map/ppermute | solution.py:579
  28.0 3.9 %collective-permute-start.12 = (f32[32,256]{1,0:T(8,128)S(1)}, f32[32,256]{1,0:T(8,128)S(1)}, u32[]{:S(2)}, u32[]{:S(2)}) collective-permute-start(f32[32,256]{1,0:T(8,128)S(1)} %pad_maximum_fusion), channel_id=1, source_target_pairs={{0,16},{16,0},{1,17},{17,1},{2,18},{18,2},{3,19},{19,3},{4,20},{20... | collective-permute-start | bytes 98312 | tf_op jit(solution)/shard_map/ppermute | solution.py:579
  31.9 32.3 %collective-permute-start.16 = (bf16[2,832,128]{2,1,0:T(8,128)(2,1)S(1)}, bf16[2,832,128]{2,1,0:T(8,128)(2,1)S(1)}, u32[]{:S(2)}, u32[]{:S(2)}) collective-permute-start(bf16[2,832,128]{2,1,0:T(8,128)(2,1)S(1)} %get-tuple-element.95), channel_id=1, source_target_pairs={{0,1},{1,0},{2,3},{3,2},{4,5},{5,4},{6,7},{7,6},{8,9},{9,8},{10,11... | collective-permute-start | bytes 1277960 | tf_op jit(solution)/shard_map/ppermute | solution.py:585
  36.4 27.9 %collective-permute-start.15 = (bf16[2,832,128]{2,1,0:T(8,128)(2,1)S(1)}, bf16[2,832,128]{2,1,0:T(8,128)(2,1)S(1)}, u32[]{:S(2)}, u32[]{:S(2)}) collective-permute-start(bf16[2,832,128]{2,1,0:T(8,128)(2,1)S(1)} %stack.1.rest_0_), channel_id=1, source_target_pairs={{0,24},{8,16},{16,8},{24,0},{1,25},{9,17},{17,9},{25,1},{2,26},{10... | collective-permute-start | bytes 1277960 | tf_op jit(solution)/shard_map/ppermute | solution.py:600
  38.9 25.4 %collective-permute-start.14 = (bf16[2,832,128]{2,1,0:T(8,128)(2,1)S(1)}, bf16[2,832,128]{2,1,0:T(8,128)(2,1)S(1)}, u32[]{:S(2)}, u32[]{:S(2)}) collective-permute-start(bf16[2,832,128]{2,1,0:T(8,128)(2,1)S(1)} %stack.1.rest_0_), channel_id=1, source_target_pairs={{0,16},{8,24},{16,0},{24,8},{1,17},{9,25},{17,1},{25,9},{2,18},{10... | collective-permute-start | bytes 1277960 | tf_op jit(solution)/shard_map/ppermute | solution.py:600
  39.4 24.9 %collective-permute-start.13 = (bf16[2,832,128]{2,1,0:T(8,128)(2,1)S(1)}, bf16[2,832,128]{2,1,0:T(8,128)(2,1)S(1)}, u32[]{:S(2)}, u32[]{:S(2)}) collective-permute-start(bf16[2,832,128]{2,1,0:T(8,128)(2,1)S(1)} %stack.1.rest_0_), channel_id=1, source_target_pairs={{0,8},{8,0},{16,24},{24,16},{1,9},{9,1},{17,25},{25,17},{2,10},{10... | collective-permute-start | bytes 1277960 | tf_op jit(solution)/shard_map/ppermute | solution.py:600
  39.9 25.5 %collective-permute-start.22 = (bf16[2,832,128]{2,1,0:T(8,128)(2,1)S(1)}, bf16[2,832,128]{2,1,0:T(8,128)(2,1)S(1)}, u32[]{:S(2)}, u32[]{:S(2)}) collective-permute-start(bf16[2,832,128]{2,1,0:T(8,128)(2,1)S(1)} %stack.1.rest_0_), channel_id=1, source_target_pairs={{0,4},{4,0},{1,5},{5,1},{2,6},{6,2},{3,7},{7,3},{8,12},{12,8},{9,1... | collective-permute-start | bytes 1277960 | tf_op jit(solution)/shard_map/ppermute | solution.py:620
  64.2 1.8 %collective-permute-start.20 = (bf16[2,832,128]{2,1,0:T(8,128)(2,1)S(1)}, bf16[2,832,128]{2,1,0:T(8,128)(2,1)S(1)}, u32[]{:S(2)}, u32[]{:S(2)}) collective-permute-start(bf16[2,832,128]{2,1,0:T(8,128)(2,1)S(1)} %collective-permute-done.8.rest_5_.rest_3_), channel_id=1, source_target_pairs={{0,4},{4,0},{1,5},{5,1},{2,6},{6,2},{3,7},{7,3},{8,12},{12,8},{9,1... | collective-permute-start | bytes 1277960 | tf_op jit(solution)/shard_map/ppermute | solution.py:621
  64.3 3.8 %collective-permute-start.17 = (bf16[2,832,128]{2,1,0:T(8,128)(2,1)S(1)}, bf16[2,832,128]{2,1,0:T(8,128)(2,1)S(1)}, u32[]{:S(2)}, u32[]{:S(2)}) collective-permute-start(bf16[2,832,128]{2,1,0:T(8,128)(2,1)S(1)} %collective-permute-done.13.rest_2_), channel_id=1, source_target_pairs={{0,4},{4,0},{1,5},{5,1},{2,6},{6,2},{3,7},{7,3},{8,12},{12,8},{9,1... | collective-permute-start | bytes 1277960 | tf_op jit(solution)/shard_map/ppermute | solution.py:637
  64.9 3.3 %collective-permute-start.18 = (bf16[2,832,128]{2,1,0:T(8,128)(2,1)S(1)}, bf16[2,832,128]{2,1,0:T(8,128)(2,1)S(1)}, u32[]{:S(2)}, u32[]{:S(2)}) collective-permute-start(bf16[2,832,128]{2,1,0:T(8,128)(2,1)S(1)} %collective-permute-done.14.rest_3_), channel_id=1, source_target_pairs={{0,4},{4,0},{1,5},{5,1},{2,6},{6,2},{3,7},{7,3},{8,12},{12,8},{9,1... | collective-permute-start | bytes 1277960 | tf_op jit(solution)/shard_map/ppermute | solution.py:637
  65.0 3.2 %collective-permute-start.19 = (bf16[2,832,128]{2,1,0:T(8,128)(2,1)S(1)}, bf16[2,832,128]{2,1,0:T(8,128)(2,1)S(1)}, u32[]{:S(2)}, u32[]{:S(2)}) collective-permute-start(bf16[2,832,128]{2,1,0:T(8,128)(2,1)S(1)} %collective-permute-done.15.rest_4_), channel_id=1, source_target_pairs={{0,4},{4,0},{1,5},{5,1},{2,6},{6,2},{3,7},{7,3},{8,12},{12,8},{9,1... | collective-permute-start | bytes 1277960 | tf_op jit(solution)/shard_map/ppermute | solution.py:637
  65.4 3.1 %collective-permute-start.21 = (bf16[2,832,128]{2,1,0:T(8,128)(2,1)S(1)}, bf16[2,832,128]{2,1,0:T(8,128)(2,1)S(1)}, u32[]{:S(2)}, u32[]{:S(2)}) collective-permute-start(bf16[2,832,128]{2,1,0:T(8,128)(2,1)S(1)} %collective-permute-done.16.rest_6_.rest_4_), channel_id=1, source_target_pairs={{0,4},{4,0},{1,5},{5,1},{2,6},{6,2},{3,7},{7,3},{8,12},{12,8},{9,1... | collective-permute-start | bytes 1277960 | tf_op jit(solution)/shard_map/ppermute | solution.py:636

commit v19 on v18

--- a/solution.py
+++ b/solution.py
@@ -545,14 +545,13 @@
         across = lax.ppermute(outs[0], "tp", [(z, z ^ 2) for z in range(heads)])
     for d in range(1, chips):
         if spread and d == chips - 1:
-            across, recv[2 * d] = lax.optimization_barrier((across, recv[2 * d]))
+            across, recv = lax.optimization_barrier((across, recv))
         recv[2 * d + 1] = lax.ppermute(recv[2 * d], "core", swap)
     recv = [recv[d] for d in range(1, count)]
     if count > 8:
         recv = [jnp.stack(recv)]
 
     if spread:
-        across, recv, sent = lax.optimization_barrier((across, recv, outs[1]))
         near = [across, lax.ppermute(across, "tp", [(z, z ^ 1) for z in range(heads)])]
 
     attended, stat, sheet = pl.pallas_call(
@@ -575,6 +574,8 @@
     )(*recv, own, query, feat, cum)
     stats = [stat]
     for name in reversed(ctx):
+        if spread and len(stats) == 2:
+            near, sent, stats = lax.optimization_barrier((near, outs[1], stats))
         held = stats[0] if len(stats) == 1 else jnp.concatenate(stats, axis=0)
         stats.append(lax.ppermute(held, name, swap))
     if count > 8:

time: 70.3 us -> 71.2 us (1.013)
  starting transfers between devices: 17.9 us -> 16.3 us
  blocking collectives: 20.4 us -> 21.7 us
  waiting for transfers between devices: 17.9 us -> 19.2 us
    ppermute x1, waiting for transfers between devices: 3.51 us -> 0.51 us  [per_device(): lax.ppermute(across, 'tp', [(z, z ^ 1) for z in range(heads)])]
    ppermute x1, waiting for transfers between devices: 0.17 us -> 2.25 us  [per_device(): across = lax.ppermute(outs[0], 'tp', [(z, z ^ 2) for z in range(heads)])]
    ppermute x3, waiting for transfers between devices: 6.06 us -> 7.8 us  [per_device(): stats.append(lax.ppermute(held, name, swap))]
    ppermute x1, starting transfers between devices: 4.11 us -> 2.59 us  [per_device(): across = lax.ppermute(outs[0], 'tp', [(z, z ^ 2) for z in range(heads)])]
    ppermute x3, starting transfers between devices: 3.49 us -> 5.01 us  [per_device(): lax.ppermute(sends[d], ctx[:-1], [(i, i ^ d) for i in range(chips)])]
    all_gather x1, blocking collectives: 20.4 us -> 21.7 us  [per_device(): grads = lax.all_gather(grads, 'tp')]
    ppermute x3, starting transfers between devices: 2.32 us -> 1.19 us  [per_device(): stats.append(lax.ppermute(held, name, swap))]
where the time goes in v19:
time: 71.2 us; the launch traced here: 71 us
  blocking collectives  21.7 us (30%)
  waiting for transfers between devices  19.2 us (27%)
  starting transfers between devices  16.3 us (23%)
  Pallas kernels  13.1 us (18%)
  between operations  0.74 us (1%)
    all_gather x1, blocking collectives, per_device(): grads = lax.all_gather(grads, 'tp')  21.7 us
    ppermute x3, waiting for transfers between devices, per_device(): stats.append(lax.ppermute(held, name, swap))  7.8 us
    ppermute x3, waiting for transfers between devices, per_device(): lax.ppermute(sends[d], ctx[:-1], [(i, i ^ d) for i in range(chips)])  6.12 us
    ppermute x3, starting transfers between devices, per_device(): lax.ppermute(sends[d], ctx[:-1], [(i, i ^ d) for i in range(chips)])  5.01 us
    pallas_call x2, Pallas kernels, per_device(): pl.pallas_call(partial(columns_kernel, ctx, distances), out_shape=jax.Sha...  3.69 us
    pallas_call x1, Pallas kernels, per_device(): pl.pallas_call(lambda *refs: gradient_kernel(ctx, count, len(recv), len(s...  3.63 us
    ppermute x3, starting transfers between devices, per_device(): lax.ppermute(pieces[0], ctx[:-1], [(i, i ^ d) for i in range(chips)])  3.55 us
    pallas_call x1, Pallas kernels, per_device(): pl.pallas_call(partial(project_kernel, ctx, len(packs)), out_shape=packs...  3.16 us
  transfers between devices with their start and end apart: 23, of which 11 were waited for; matrix products, arithmetic and copies ran while one was open for 0% of the time, Pallas kernels for 12%

profile of v19, /device:TPU:0, one launch (start us, length us, event | category | flops | bytes accessed | tf_op | source)
XLA Modules:
  0.0 71.0 jit_solution(9980863912036035616)
XLA Ops:
  0.6 3.2 %project.1 = (bf16[832,128]{1,0:T(8,128)(2,1)S(1)}, bf16[2,832,128]{2,1,0:T(8,128)(2,1)S(1)}, bf16[2,832,128]{2,1,0:T(8,128)(2,1)S(1)}, bf16[560,128]{1,0:T(8,12...) custom-call(bf16[256,2048]{1,0:T(8,128)(2,1)} %tok_hbm.1, ...), custom_call_target="tpu_custom_call" | custom-call | flops 1 | bytes 1024 | tf_op jit(solution)/shard_map/project/pallas_call | solution.py:513
  3.8 3.0 %collective-permute-start.2 = (bf16[560,128]{1,0:T(8,128)(2,1)S(1)}, bf16[560,128]{1,0:T(8,128)(2,1)S(1)}, u32[]{:S(2)}, u32[]{:S(2)}) collective-permute-start(bf16[560,128]{1,0:T(8,128)(2,1)S(1)} %get-tuple-element.55), channel_id=1, source_target_pairs={{0,8},{8,0},{16,24},{24,16},{1,9},{9,1},{17,25},{25,17},{2,10},{10... | collective-permute-start | bytes 430088 | tf_op jit(solution)/shard_map/ppermute | solution.py:542
  6.8 1.5 %collective-permute-start.4 = (bf16[560,128]{1,0:T(8,128)(2,1)S(1)}, bf16[560,128]{1,0:T(8,128)(2,1)S(1)}, u32[]{:S(2)}, u32[]{:S(2)}) collective-permute-start(bf16[560,128]{1,0:T(8,128)(2,1)S(1)} %get-tuple-element.56), channel_id=1, source_target_pairs={{0,16},{8,24},{16,0},{24,8},{1,17},{9,25},{17,1},{25,9},{2,18},{10... | collective-permute-start | bytes 430088 | tf_op jit(solution)/shard_map/ppermute | solution.py:542
  8.3 2.6 %collective-permute-start = (bf16[832,128]{1,0:T(8,128)(2,1)S(1)}, bf16[832,128]{1,0:T(8,128)(2,1)S(1)}, u32[]{:S(2)}, u32[]{:S(2)}) collective-permute-start(bf16[832,128]{1,0:T(8,128)(2,1)S(1)} %get-tuple-element.53), channel_id=1, source_target_pairs={{0,2},{1,3},{2,0},{3,1},{4,6},{5,7},{6,4},{7,5},{8,10},{9,11},{10,... | collective-permute-start | bytes 638984 | tf_op jit(solution)/shard_map/ppermute | solution.py:545
  10.9 0.0 collective-permute-start.1
  10.9 0.5 collective-permute-start.6
  11.4 0.0 collective-permute-done.2.refs_1_
  11.4 0.2 collective-permute-start.3
  11.6 0.4 collective-permute-done.4.refs_3_
  12.0 0.0 collective-permute-start.5
  12.0 0.2 collective-permute-done.1.refs_0_
  12.3 5.7 %collective-permute-done.6.refs_5_ = bf16[560,128]{1,0:T(8,128)(2,1)S(1)} collective-permute-done((bf16[560,128]{1,0:T(8,128)(2,1)S(1)}, bf16[560,128]{1,0:T(8,128)(2,1)S(1)}, u32[]{:S(2)}, u32[]{:S(2)}) %collective-permute-start.6) | collective-permute-done | bytes 143392 | tf_op jit(solution)/shard_map/ppermute | solution.py:542
  18.0 2.2 %collective-permute-done.refs_0_ = bf16[832,128]{1,0:T(8,128)(2,1)S(1)} collective-permute-done((bf16[832,128]{1,0:T(8,128)(2,1)S(1)}, bf16[832,128]{1,0:T(8,128)(2,1)S(1)}, u32[]{:S(2)}, u32[]{:S(2)}) %collective-permute-start) | collective-permute-done | bytes 213024 | tf_op jit(solution)/shard_map/ppermute | solution.py:545
  20.2 0.0 collective-permute-done.3.refs_2_
  20.2 0.0 collective-permute-done.5.refs_4_
  20.2 0.7 collective-permute-start.8
  20.9 0.0 collective-permute-start.7
  20.9 1.4 %collective-permute-done.7.refs_6_ = bf16[560,128]{1,0:T(8,128)(2,1)S(1)} collective-permute-done((bf16[560,128]{1,0:T(8,128)(2,1)S(1)}, bf16[560,128]{1,0:T(8,128)(2,1)S(1)}, u32[]{:S(2)}, u32[]{:S(2)}) %collective-permute-start.7) | collective-permute-done | bytes 143392 | tf_op jit(solution)/shard_map/ppermute | solution.py:549
  22.3 2.4 %query_side.1 = (bf16[256,128]{1,0:T(8,128)(2,1)}, f32[8,256]{1,0:T(8,128)S(1)}, f32[256,128]{1,0:T(8,128)S(1)}) custom-call(bf16[560,128]{1,0:T(8,128)(2,1)S(1)} %collective-permute-done.1.refs_0_, bf16[560,128]{1,0:T(8,128)(2,1)S(1)} %collective-permute-done.2.refs_1_, bf16[560,128]{1,0:T(8,128)(2,1)S(1)} %collective-permute-done.3.refs_2_, ...), custom_call_target="tpu_custom_call" | custom-call | flops 1 | bytes 1024 | tf_op jit(solution)/shard_map/query_side/pallas_call | solution.py:557
  24.7 0.1 collective-permute-start.9
  24.8 1.0 %collective-permute-done.9.refs_8_ = f32[8,256]{1,0:T(8,128)S(1)} collective-permute-done((f32[8,256]{1,0:T(8,128)S(1)}, f32[8,256]{1,0:T(8,128)S(1)}, u32[]{:S(2)}, u32[]{:S(2)}) %collective-permute-start.9) | collective-permute-done | bytes 8224 | tf_op jit(solution)/shard_map/ppermute | solution.py:580
  25.8 0.5 collective-permute-done.8.refs_1_
  26.4 1.7 %collective-permute-start.10 = (bf16[2,832,128]{2,1,0:T(8,128)(2,1)S(1)}, bf16[2,832,128]{2,1,0:T(8,128)(2,1)S(1)}, u32[]{:S(2)}, u32[]{:S(2)}) collective-permute-start(bf16[2,832,128]{2,1,0:T(8,128)(2,1)S(1)} %get-tuple-element.72), channel_id=1, source_target_pairs={{0,1},{1,0},{2,3},{3,2},{4,5},{5,4},{6,7},{7,6},{8,9},{9,8},{10,11... | collective-permute-start | bytes 1277960 | tf_op jit(solution)/shard_map/ppermute | solution.py:586
  28.1 0.5 collective-permute-start.11
  28.6 3.2 %collective-permute-done.11.refs_9_ = f32[16,256]{1,0:T(8,128)S(1)} collective-permute-done((f32[16,256]{1,0:T(8,128)S(1)}, f32[16,256]{1,0:T(8,128)S(1)}, u32[]{:S(2)}, u32[]{:S(2)}) %collective-permute-start.11) | collective-permute-done | bytes 16416 | tf_op jit(solution)/shard_map/ppermute | solution.py:580
  31.8 0.5 collective-permute-start.12
  32.3 3.6 %collective-permute-done.12.refs_10_ = f32[32,256]{1,0:T(8,128)S(1)} collective-permute-done((f32[32,256]{1,0:T(8,128)S(1)}, f32[32,256]{1,0:T(8,128)S(1)}, u32[]{:S(2)}, u32[]{:S(2)}) %collective-permute-start.12) | collective-permute-done | bytes 32800 | tf_op jit(solution)/shard_map/ppermute | solution.py:580
  36.0 0.4 collective-permute-start.15
  36.3 1.5 %collective-permute-start.14 = (bf16[2,832,128]{2,1,0:T(8,128)(2,1)S(1)}, bf16[2,832,128]{2,1,0:T(8,128)(2,1)S(1)}, u32[]{:S(2)}, u32[]{:S(2)}) collective-permute-start(bf16[2,832,128]{2,1,0:T(8,128)(2,1)S(1)} %stack.1.rest_0_), channel_id=1, source_target_pairs={{0,16},{8,24},{16,0},{24,8},{1,17},{9,25},{17,1},{25,9},{2,18},{10... | collective-permute-start | bytes 1277960 | tf_op jit(solution)/shard_map/ppermute | solution.py:601
  37.9 1.7 %collective-permute-start.13 = (bf16[2,832,128]{2,1,0:T(8,128)(2,1)S(1)}, bf16[2,832,128]{2,1,0:T(8,128)(2,1)S(1)}, u32[]{:S(2)}, u32[]{:S(2)}) collective-permute-start(bf16[2,832,128]{2,1,0:T(8,128)(2,1)S(1)} %stack.1.rest_0_), channel_id=1, source_target_pairs={{0,8},{8,0},{16,24},{24,16},{1,9},{9,1},{17,25},{25,17},{2,10},{10... | collective-permute-start | bytes 1277960 | tf_op jit(solution)/shard_map/ppermute | solution.py:601
  39.5 0.1 collective-permute-start.16
  39.6 0.0 collective-permute-done.10.rest_5_.rest_3_
  39.6 0.0 collective-permute-start.22
  39.6 3.6 %gradients.1 = bf16[832,128]{1,0:T(8,128)(2,1)S(1)} custom-call(bf16[560,128]{1,0:T(8,128)(2,1)S(1)} %collective-permute-done.1.refs_0_, bf16[560,128]{1,0:T(8,128)(2,1)S(1)} %collective-permute-done.2.refs_1_, bf16[560,128]{1,0:T(8,128)(2,1)S(1)} %collective-permute-done.3.refs_2_, bf16[560,128]{1,0:T(8,128)(2,1)S(1)} %collective-permute-done.4.refs_3_, ...), custom_call_target="tpu_custom_call" | custom-call | flops 1 | bytes 1024 | tf_op jit(solution)/shard_map/gradients/pallas_call | solution.py:605
  43.3 21.7 %all-gather = bf16[3328,128]{1,0:T(8,128)(2,1)S(1)} all-gather(bf16[832,128]{1,0:T(8,128)(2,1)S(1)} %gradients.1), channel_id=2, replica_groups=mesh['half0'=2,'half1'=2,'core'=2,'tp'=4] {'tp'}, dimensions={0}, use_global_device_ids=true | all-gather | bytes 1064960 | tf_op jit(solution)/shard_map/all_gather | solution.py:623
  65.0 0.2 cat.1
  65.2 0.1 collective-permute-start.20
  65.2 0.0 collective-permute-done.14.rest_3_
  65.3 0.5 collective-permute-start.17
  65.8 0.1 collective-permute-start.18
  65.9 0.4 collective-permute-start.19
  66.3 0.1 collective-permute-start.21
  66.4 0.6 collective-permute-done.20.rest_7_.rest_8_.rest_5_
  67.0 2.1 %columns.2.rest_7_ = bf16[256,2048]{1,0:T(8,128)(2,1)} custom-call(bf16[256,1536]{1,0:T(8,128)(2,1)S(1)} %get-tuple-element.91.cat_ref, bf16[256,128]{1,0:T(8,128)(2,1)S(1)} %get-tuple-element.92.feat_ref, bf16[2048,256]{1,0:T(8,128)(2,1)S(1)} %get-tuple-element.93.ww_ref, bf16[2048,128]{1,0:T(8,128)(2,1)S(1)} %get-tuple-element.94.vw_ref, ...), custom_call_target="tpu_custom_call" | custom-call | flops 1 | bytes 1024 | tf_op jit(solution)/shard_map/columns/pallas_call | solution.py:645
  69.1 0.0 collective-permute-done.17.rest_0_
  69.1 0.0 collective-permute-done.18.rest_1_
  69.1 0.3 collective-permute-done.21.rest_6_
  69.4 1.6 %columns.3 = bf16[256,2048]{1,0:T(8,128)(2,1)} custom-call(bf16[256,1536]{1,0:T(8,128)(2,1)S(1)} %get-tuple-element.91.cat_ref, bf16[256,128]{1,0:T(8,128)(2,1)S(1)} %get-tuple-element.92.feat_ref, bf16[2048,256]{1,0:T(8,128)(2,1)S(1)} %get-tuple-element.93.ww_ref, bf16[2048,128]{1,0:T(8,128)(2,1)S(1)} %get-tuple-element.94.vw_ref, ...), custom_call_target="tpu_custom_call", output_to_operand_aliasing={{}: (12, {})} | custom-call | flops 1 | bytes 1024 | tf_op jit(solution)/shard_map/columns/pallas_call | solution.py:645
  (8 shorter events, 0.0 us)
Async XLA Ops:
  3.8 7.6 %collective-permute-start.2 = (bf16[560,128]{1,0:T(8,128)(2,1)S(1)}, bf16[560,128]{1,0:T(8,128)(2,1)S(1)}, u32[]{:S(2)}, u32[]{:S(2)}) collective-permute-start(bf16[560,128]{1,0:T(8,128)(2,1)S(1)} %get-tuple-element.55), channel_id=1, source_target_pairs={{0,8},{8,0},{16,24},{24,16},{1,9},{9,1},{17,25},{25,17},{2,10},{10... | collective-permute-start | bytes 430088 | tf_op jit(solution)/shard_map/ppermute | solution.py:542
  6.8 5.2 %collective-permute-start.4 = (bf16[560,128]{1,0:T(8,128)(2,1)S(1)}, bf16[560,128]{1,0:T(8,128)(2,1)S(1)}, u32[]{:S(2)}, u32[]{:S(2)}) collective-permute-start(bf16[560,128]{1,0:T(8,128)(2,1)S(1)} %get-tuple-element.56), channel_id=1, source_target_pairs={{0,16},{8,24},{16,0},{24,8},{1,17},{9,25},{17,1},{25,9},{2,18},{10... | collective-permute-start | bytes 430088 | tf_op jit(solution)/shard_map/ppermute | solution.py:542
  8.3 11.9 %collective-permute-start = (bf16[832,128]{1,0:T(8,128)(2,1)S(1)}, bf16[832,128]{1,0:T(8,128)(2,1)S(1)}, u32[]{:S(2)}, u32[]{:S(2)}) collective-permute-start(bf16[832,128]{1,0:T(8,128)(2,1)S(1)} %get-tuple-element.53), channel_id=1, source_target_pairs={{0,2},{1,3},{2,0},{3,1},{4,6},{5,7},{6,4},{7,5},{8,10},{9,11},{10,... | collective-permute-start | bytes 638984 | tf_op jit(solution)/shard_map/ppermute | solution.py:545
  10.9 1.4 %collective-permute-start.1 = (bf16[560,128]{1,0:T(8,128)(2,1)S(1)}, bf16[560,128]{1,0:T(8,128)(2,1)S(1)}, u32[]{:S(2)}, u32[]{:S(2)}) collective-permute-start(bf16[560,128]{1,0:T(8,128)(2,1)S(1)} %get-tuple-element.54), channel_id=1, source_target_pairs={{0,4},{4,0},{1,5},{5,1},{2,6},{6,2},{3,7},{7,3},{8,12},{12,8},{9,1... | collective-permute-start | bytes 430088 | tf_op jit(solution)/shard_map/ppermute | solution.py:543
  10.9 7.1 %collective-permute-start.6 = (bf16[560,128]{1,0:T(8,128)(2,1)S(1)}, bf16[560,128]{1,0:T(8,128)(2,1)S(1)}, u32[]{:S(2)}, u32[]{:S(2)}) collective-permute-start(bf16[560,128]{1,0:T(8,128)(2,1)S(1)} %get-tuple-element.57), channel_id=1, source_target_pairs={{0,24},{8,16},{16,8},{24,0},{1,25},{9,17},{17,9},{25,1},{2,26},{10... | collective-permute-start | bytes 430088 | tf_op jit(solution)/shard_map/ppermute | solution.py:542
  11.4 8.8 %collective-permute-start.3 = (bf16[560,128]{1,0:T(8,128)(2,1)S(1)}, bf16[560,128]{1,0:T(8,128)(2,1)S(1)}, u32[]{:S(2)}, u32[]{:S(2)}) collective-permute-start(bf16[560,128]{1,0:T(8,128)(2,1)S(1)} %collective-permute-done.2.refs_1_), channel_id=1, source_target_pairs={{0,4},{4,0},{1,5},{5,1},{2,6},{6,2},{3,7},{7,3},{8,12},{12,8},{9,1... | collective-permute-start | bytes 430088 | tf_op jit(solution)/shard_map/ppermute | solution.py:549
  12.0 8.2 %collective-permute-start.5 = (bf16[560,128]{1,0:T(8,128)(2,1)S(1)}, bf16[560,128]{1,0:T(8,128)(2,1)S(1)}, u32[]{:S(2)}, u32[]{:S(2)}) collective-permute-start(bf16[560,128]{1,0:T(8,128)(2,1)S(1)} %collective-permute-done.4.refs_3_), channel_id=1, source_target_pairs={{0,4},{4,0},{1,5},{5,1},{2,6},{6,2},{3,7},{7,3},{8,12},{12,8},{9,1... | collective-permute-start | bytes 430088 | tf_op jit(solution)/shard_map/ppermute | solution.py:549
  20.2 6.1 %collective-permute-start.8 = (bf16[832,128]{1,0:T(8,128)(2,1)S(1)}, bf16[832,128]{1,0:T(8,128)(2,1)S(1)}, u32[]{:S(2)}, u32[]{:S(2)}) collective-permute-start(bf16[832,128]{1,0:T(8,128)(2,1)S(1)} %collective-permute-done.refs_0_), channel_id=1, source_target_pairs={{0,1},{1,0},{2,3},{3,2},{4,5},{5,4},{6,7},{7,6},{8,9},{9,8},{10,11... | collective-permute-start | bytes 638984 | tf_op jit(solution)/shard_map/ppermute | solution.py:555
  20.9 1.4 %collective-permute-start.7 = (bf16[560,128]{1,0:T(8,128)(2,1)S(1)}, bf16[560,128]{1,0:T(8,128)(2,1)S(1)}, u32[]{:S(2)}, u32[]{:S(2)}) collective-permute-start(bf16[560,128]{1,0:T(8,128)(2,1)S(1)} %collective-permute-done.6.refs_5_), channel_id=1, source_target_pairs={{0,4},{4,0},{1,5},{5,1},{2,6},{6,2},{3,7},{7,3},{8,12},{12,8},{9,1... | collective-permute-start | bytes 430088 | tf_op jit(solution)/shard_map/ppermute | solution.py:549
  24.7 1.2 %collective-permute-start.9 = (f32[8,256]{1,0:T(8,128)S(1)}, f32[8,256]{1,0:T(8,128)S(1)}, u32[]{:S(2)}, u32[]{:S(2)}) collective-permute-start(f32[8,256]{1,0:T(8,128)S(1)} %get-tuple-element.82.refs_7_), channel_id=1, source_target_pairs={{0,4},{4,0},{1,5},{5,1},{2,6},{6,2},{3,7},{7,3},{8,12},{12,8},{9,1... | collective-permute-start | bytes 24584 | tf_op jit(solution)/shard_map/ppermute | solution.py:580
  26.4 13.3 %collective-permute-start.10 = (bf16[2,832,128]{2,1,0:T(8,128)(2,1)S(1)}, bf16[2,832,128]{2,1,0:T(8,128)(2,1)S(1)}, u32[]{:S(2)}, u32[]{:S(2)}) collective-permute-start(bf16[2,832,128]{2,1,0:T(8,128)(2,1)S(1)} %get-tuple-element.72), channel_id=1, source_target_pairs={{0,1},{1,0},{2,3},{3,2},{4,5},{5,4},{6,7},{7,6},{8,9},{9,8},{10,11... | collective-permute-start | bytes 1277960 | tf_op jit(solution)/shard_map/ppermute | solution.py:586
  28.1 3.7 %collective-permute-start.11 = (f32[16,256]{1,0:T(8,128)S(1)}, f32[16,256]{1,0:T(8,128)S(1)}, u32[]{:S(2)}, u32[]{:S(2)}) collective-permute-start(f32[16,256]{1,0:T(8,128)S(1)} %pad_maximum_fusion.1), channel_id=1, source_target_pairs={{0,8},{8,0},{1,9},{9,1},{2,10},{10,2},{3,11},{11,3},{4,12},{12,4},... | collective-permute-start | bytes 49160 | tf_op jit(solution)/shard_map/ppermute | solution.py:580
  31.8 4.1 %collective-permute-start.12 = (f32[32,256]{1,0:T(8,128)S(1)}, f32[32,256]{1,0:T(8,128)S(1)}, u32[]{:S(2)}, u32[]{:S(2)}) collective-permute-start(f32[32,256]{1,0:T(8,128)S(1)} %pad_maximum_fusion), channel_id=1, source_target_pairs={{0,16},{16,0},{1,17},{17,1},{2,18},{18,2},{3,19},{19,3},{4,20},{20... | collective-permute-start | bytes 98312 | tf_op jit(solution)/shard_map/ppermute | solution.py:580
  36.0 29.2 %collective-permute-start.15 = (bf16[2,832,128]{2,1,0:T(8,128)(2,1)S(1)}, bf16[2,832,128]{2,1,0:T(8,128)(2,1)S(1)}, u32[]{:S(2)}, u32[]{:S(2)}) collective-permute-start(bf16[2,832,128]{2,1,0:T(8,128)(2,1)S(1)} %stack.1.rest_0_), channel_id=1, source_target_pairs={{0,24},{8,16},{16,8},{24,0},{1,25},{9,17},{17,9},{25,1},{2,26},{10... | collective-permute-start | bytes 1277960 | tf_op jit(solution)/shard_map/ppermute | solution.py:601
  36.3 28.9 %collective-permute-start.14 = (bf16[2,832,128]{2,1,0:T(8,128)(2,1)S(1)}, bf16[2,832,128]{2,1,0:T(8,128)(2,1)S(1)}, u32[]{:S(2)}, u32[]{:S(2)}) collective-permute-start(bf16[2,832,128]{2,1,0:T(8,128)(2,1)S(1)} %stack.1.rest_0_), channel_id=1, source_target_pairs={{0,16},{8,24},{16,0},{24,8},{1,17},{9,25},{17,1},{25,9},{2,18},{10... | collective-permute-start | bytes 1277960 | tf_op jit(solution)/shard_map/ppermute | solution.py:601
  37.9 27.4 %collective-permute-start.13 = (bf16[2,832,128]{2,1,0:T(8,128)(2,1)S(1)}, bf16[2,832,128]{2,1,0:T(8,128)(2,1)S(1)}, u32[]{:S(2)}, u32[]{:S(2)}) collective-permute-start(bf16[2,832,128]{2,1,0:T(8,128)(2,1)S(1)} %stack.1.rest_0_), channel_id=1, source_target_pairs={{0,8},{8,0},{16,24},{24,16},{1,9},{9,1},{17,25},{25,17},{2,10},{10... | collective-permute-start | bytes 1277960 | tf_op jit(solution)/shard_map/ppermute | solution.py:601
  39.5 25.8 %collective-permute-start.16 = (bf16[2,832,128]{2,1,0:T(8,128)(2,1)S(1)}, bf16[2,832,128]{2,1,0:T(8,128)(2,1)S(1)}, u32[]{:S(2)}, u32[]{:S(2)}) collective-permute-start(bf16[2,832,128]{2,1,0:T(8,128)(2,1)S(1)} %get-tuple-element.97), channel_id=1, source_target_pairs={{0,1},{1,0},{2,3},{3,2},{4,5},{5,4},{6,7},{7,6},{8,9},{9,8},{10,11... | collective-permute-start | bytes 1277960 | tf_op jit(solution)/shard_map/ppermute | solution.py:586
  39.6 26.7 %collective-permute-start.22 = (bf16[2,832,128]{2,1,0:T(8,128)(2,1)S(1)}, bf16[2,832,128]{2,1,0:T(8,128)(2,1)S(1)}, u32[]{:S(2)}, u32[]{:S(2)}) collective-permute-start(bf16[2,832,128]{2,1,0:T(8,128)(2,1)S(1)} %stack.1.rest_0_), channel_id=1, source_target_pairs={{0,4},{4,0},{1,5},{5,1},{2,6},{6,2},{3,7},{7,3},{8,12},{12,8},{9,1... | collective-permute-start | bytes 1277960 | tf_op jit(solution)/shard_map/ppermute | solution.py:621
  65.2 1.8 %collective-permute-start.20 = (bf16[2,832,128]{2,1,0:T(8,128)(2,1)S(1)}, bf16[2,832,128]{2,1,0:T(8,128)(2,1)S(1)}, u32[]{:S(2)}, u32[]{:S(2)}) collective-permute-start(bf16[2,832,128]{2,1,0:T(8,128)(2,1)S(1)} %collective-permute-done.10.rest_5_.rest_3_), channel_id=1, source_target_pairs={{0,4},{4,0},{1,5},{5,1},{2,6},{6,2},{3,7},{7,3},{8,12},{12,8},{9,1... | collective-permute-start | bytes 1277960 | tf_op jit(solution)/shard_map/ppermute | solution.py:622
  65.3 3.8 %collective-permute-start.17 = (bf16[2,832,128]{2,1,0:T(8,128)(2,1)S(1)}, bf16[2,832,128]{2,1,0:T(8,128)(2,1)S(1)}, u32[]{:S(2)}, u32[]{:S(2)}) collective-permute-start(bf16[2,832,128]{2,1,0:T(8,128)(2,1)S(1)} %collective-permute-done.13.rest_2_), channel_id=1, source_target_pairs={{0,4},{4,0},{1,5},{5,1},{2,6},{6,2},{3,7},{7,3},{8,12},{12,8},{9,1... | collective-permute-start | bytes 1277960 | tf_op jit(solution)/shard_map/ppermute | solution.py:638
  65.8 3.3 %collective-permute-start.18 = (bf16[2,832,128]{2,1,0:T(8,128)(2,1)S(1)}, bf16[2,832,128]{2,1,0:T(8,128)(2,1)S(1)}, u32[]{:S(2)}, u32[]{:S(2)}) collective-permute-start(bf16[2,832,128]{2,1,0:T(8,128)(2,1)S(1)} %collective-permute-done.14.rest_3_), channel_id=1, source_target_pairs={{0,4},{4,0},{1,5},{5,1},{2,6},{6,2},{3,7},{7,3},{8,12},{12,8},{9,1... | collective-permute-start | bytes 1277960 | tf_op jit(solution)/shard_map/ppermute | solution.py:638
  65.9 3.2 %collective-permute-start.19 = (bf16[2,832,128]{2,1,0:T(8,128)(2,1)S(1)}, bf16[2,832,128]{2,1,0:T(8,128)(2,1)S(1)}, u32[]{:S(2)}, u32[]{:S(2)}) collective-permute-start(bf16[2,832,128]{2,1,0:T(8,128)(2,1)S(1)} %collective-permute-done.15.rest_4_), channel_id=1, source_target_pairs={{0,4},{4,0},{1,5},{5,1},{2,6},{6,2},{3,7},{7,3},{8,12},{12,8},{9,1... | collective-permute-start | bytes 1277960 | tf_op jit(solution)/shard_map/ppermute | solution.py:638
  66.3 3.1 %collective-permute-start.21 = (bf16[2,832,128]{2,1,0:T(8,128)(2,1)S(1)}, bf16[2,832,128]{2,1,0:T(8,128)(2,1)S(1)}, u32[]{:S(2)}, u32[]{:S(2)}) collective-permute-start(bf16[2,832,128]{2,1,0:T(8,128)(2,1)S(1)} %collective-permute-done.16.rest_6_.rest_4_), channel_id=1, source_target_pairs={{0,4},{4,0},{1,5},{5,1},{2,6},{6,2},{3,7},{7,3},{8,12},{12,8},{9,1... | collective-permute-start | bytes 1277960 | tf_op jit(solution)/shard_map/ppermute | solution.py:637

commit v20 on v19

--- a/solution.py
+++ b/solution.py
@@ -418,7 +418,7 @@
 
 
 def columns_kernel(ctx, distances, cat_ref, feat_ref, ww_ref, vw_ref, fw_ref, *rest):
-    pieces, firsts = rest[: len(distances)], rest[len(distances) : len(distances) + 4]
+    pieces, firsts = rest[: len(distances)], rest[len(distances) : len(distances) + 2]
     out_ref, tile_ref, sems = rest[-3:]
     nf2 = fw_ref.shape[0]
     heads = feat_ref.shape[1] // nf2
@@ -427,7 +427,7 @@
     copies = []
     for n, (e, ref) in enumerate(zip(distances, pieces)):
         part = pl.ds(pl.multiple_of(jnp.bitwise_xor(me, e) * tile, tile), tile)
-        views = [firsts[2 * (e % 2) + e // 4].at[e // 2 % 2]]
+        views = [firsts[e // 4].at[e // 2 % 2]]
         views += [ref.at[t] for t in range(heads - 2)]
         main = [ww_ref[part, :], vw_ref[part, :]]
         main += [v[m * tile : (m + 1) * tile, :] for v in views for m in range(3)]
@@ -545,13 +545,14 @@
         across = lax.ppermute(outs[0], "tp", [(z, z ^ 2) for z in range(heads)])
     for d in range(1, chips):
         if spread and d == chips - 1:
-            across, recv = lax.optimization_barrier((across, recv))
+            across, recv[2 * d] = lax.optimization_barrier((across, recv[2 * d]))
         recv[2 * d + 1] = lax.ppermute(recv[2 * d], "core", swap)
     recv = [recv[d] for d in range(1, count)]
     if count > 8:
         recv = [jnp.stack(recv)]
 
     if spread:
+        across, recv = lax.optimization_barrier((across, recv))
         near = [across, lax.ppermute(across, "tp", [(z, z ^ 1) for z in range(heads)])]
 
     attended, stat, sheet = pl.pallas_call(
@@ -618,8 +619,6 @@
         return (attended, merge(lax.all_gather(grads, "tp"), weights, rows, dim))
 
     first[0], grads = lax.optimization_barrier((first[0], grads))
-    swapped = [lax.ppermute(pieces[0], "core", swap)]
-    firsts = [lax.ppermute(first[0], "core", swap)]
     grads = lax.all_gather(grads, "tp")
     cat, feats = pl.pallas_call(
         cat_kernel,
@@ -633,19 +632,19 @@
         cost_estimate=cost(1, 1024),
         name="cat",
     )(grads)
-    pieces, first[1], _ = lax.optimization_barrier((pieces, first[1], cat))
-    firsts = [*first, *firsts, lax.ppermute(first[1], "core", swap)]
-    swapped += [lax.ppermute(p, "core", swap) for p in pieces[1:]]
+    pieces, first, _ = lax.optimization_barrier((pieces, first, cat))
+    other_first = [lax.ppermute(p, "core", swap) for p in first]
+    swapped = [lax.ppermute(p, "core", swap) for p in pieces]
 
     total = []
-    for distances in ((0, 1, 2, 4, 6), (3, 5, 7)):
+    for distances in ((0, 2, 4, 6), (1, 3, 5, 7)):
         parts = [(swapped if e % 2 else pieces)[e // 2] for e in distances]
-        args = [cat, feats, ww, vw, fw, *parts, *firsts[:3], firsts[3 if total else 2], *total]
+        args = [cat, feats, ww, vw, fw, *parts, *(other_first if total else first), *total]
         total = [
             pl.pallas_call(
                 partial(columns_kernel, ctx, distances),
                 out_shape=jax.ShapeDtypeStruct((rows, dim), bf16),
-                in_specs=[VMEM] * (9 + len(parts)) + [ANY] * len(total),
+                in_specs=[VMEM] * (7 + len(parts)) + [ANY] * len(total),
                 out_specs=ANY,
                 scratch_shapes=[
                     pltpu.VMEM((len(parts), rows, tile), bf16),

time: 71.2 us -> 72.5 us (1.018)
  starting transfers between devices: 16.3 us -> 18.5 us
  waiting for transfers between devices: 19.2 us -> 18.1 us
    ppermute x1, waiting for transfers between devices: 2.25 us -> 0.17 us  [per_device(): across = lax.ppermute(outs[0], 'tp', [(z, z ^ 2) for z in range(heads)])]
    ppermute x1, waiting for transfers between devices: 0.51 us -> 2.34 us  [per_device(): lax.ppermute(across, 'tp', [(z, z ^ 1) for z in range(heads)])]
    ppermute x3, starting transfers between devices: 5.01 us -> 3.49 us  [per_device(): lax.ppermute(sends[d], ctx[:-1], [(i, i ^ d) for i in range(chips)])]
    ppermute x1, starting transfers between devices: 2.59 us -> 4.11 us  [per_device(): across = lax.ppermute(outs[0], 'tp', [(z, z ^ 2) for z in range(heads)])]
    ppermute x3, waiting for transfers between devices: 7.8 us -> 6.68 us  [per_device(): stats.append(lax.ppermute(held, name, swap))]
    ppermute x3, starting transfers between devices: 1.19 us -> 2.14 us  [per_device(): stats.append(lax.ppermute(held, name, swap))]
    ppermute x1, starting transfers between devices: 0.68 us -> 1.57 us  [per_device(): lax.ppermute(across, 'tp', [(z, z ^ 1) for z in range(heads)])]
    ppermute x6, waiting for transfers between devices: 0.91 us -> 1.69 us  [the longest x2 1.01 us: per_device(): other_first = [lax.ppermute(p, 'core', swap) for p in first]]
  transfers between devices with their start and end apart: 23 -> 23, of which waited for: 11 -> 12; matrix products, arithmetic and copies ran while one was open for 0% -> 0% of each run, Pallas kernels for 12% -> 11%
where the time goes in v20:
time: 72.5 us; the launch traced here: 72.4 us
  blocking collectives  21.8 us (30%)
  starting transfers between devices  18.5 us (26%)
  waiting for transfers between devices  18.1 us (25%)
  Pallas kernels  13.1 us (18%)
  between operations  0.75 us (1%)
    all_gather x1, blocking collectives, per_device(): grads = lax.all_gather(grads, 'tp')  21.8 us
    ppermute x3, waiting for transfers between devices, per_device(): stats.append(lax.ppermute(held, name, swap))  6.68 us
    ppermute x3, waiting for transfers between devices, per_device(): lax.ppermute(sends[d], ctx[:-1], [(i, i ^ d) for i in range(chips)])  6.17 us
    ppermute x1, starting transfers between devices, per_device(): across = lax.ppermute(outs[0], 'tp', [(z, z ^ 2) for z in range(heads)])  4.11 us
    pallas_call x2, Pallas kernels, per_device(): pl.pallas_call(partial(columns_kernel, ctx, distances), out_shape=jax.Sha...  3.71 us
    pallas_call x1, Pallas kernels, per_device(): pl.pallas_call(lambda *refs: gradient_kernel(ctx, count, len(recv), len(s...  3.65 us
    ppermute x3, starting transfers between devices, per_device(): lax.ppermute(pieces[0], ctx[:-1], [(i, i ^ d) for i in range(chips)])  3.55 us
    ppermute x3, starting transfers between devices, per_device(): lax.ppermute(sends[d], ctx[:-1], [(i, i ^ d) for i in range(chips)])  3.49 us
  transfers between devices with their start and end apart: 23, of which 12 were waited for; matrix products, arithmetic and copies ran while one was open for 0% of the time, Pallas kernels for 11%

profile of v20, /device:TPU:0, one launch (start us, length us, event | category | flops | bytes accessed | tf_op | source)
XLA Modules:
  0.0 72.4 jit_solution(8692398497394752550)
XLA Ops:
  0.6 3.2 %project.1 = (bf16[832,128]{1,0:T(8,128)(2,1)S(1)}, bf16[2,832,128]{2,1,0:T(8,128)(2,1)S(1)}, bf16[2,832,128]{2,1,0:T(8,128)(2,1)S(1)}, bf16[560,128]{1,0:T(8,12...) custom-call(bf16[256,2048]{1,0:T(8,128)(2,1)} %tok_hbm.1, ...), custom_call_target="tpu_custom_call" | custom-call | flops 1 | bytes 1024 | tf_op jit(solution)/shard_map/project/pallas_call | solution.py:513
  3.8 4.1 %collective-permute-start = (bf16[832,128]{1,0:T(8,128)(2,1)S(1)}, bf16[832,128]{1,0:T(8,128)(2,1)S(1)}, u32[]{:S(2)}, u32[]{:S(2)}) collective-permute-start(bf16[832,128]{1,0:T(8,128)(2,1)S(1)} %get-tuple-element.57), channel_id=1, source_target_pairs={{0,2},{1,3},{2,0},{3,1},{4,6},{5,7},{6,4},{7,5},{8,10},{9,11},{10,... | collective-permute-start | bytes 638984 | tf_op jit(solution)/shard_map/ppermute | solution.py:545
  7.9 1.5 %collective-permute-start.3 = (bf16[560,128]{1,0:T(8,128)(2,1)S(1)}, bf16[560,128]{1,0:T(8,128)(2,1)S(1)}, u32[]{:S(2)}, u32[]{:S(2)}) collective-permute-start(bf16[560,128]{1,0:T(8,128)(2,1)S(1)} %get-tuple-element.61), channel_id=1, source_target_pairs={{0,8},{8,0},{16,24},{24,16},{1,9},{9,1},{17,25},{25,17},{2,10},{10... | collective-permute-start | bytes 430088 | tf_op jit(solution)/shard_map/ppermute | solution.py:542
  9.4 1.5 %collective-permute-start.5 = (bf16[560,128]{1,0:T(8,128)(2,1)S(1)}, bf16[560,128]{1,0:T(8,128)(2,1)S(1)}, u32[]{:S(2)}, u32[]{:S(2)}) collective-permute-start(bf16[560,128]{1,0:T(8,128)(2,1)S(1)} %get-tuple-element.62), channel_id=1, source_target_pairs={{0,16},{8,24},{16,0},{24,8},{1,17},{9,25},{17,1},{25,9},{2,18},{10... | collective-permute-start | bytes 430088 | tf_op jit(solution)/shard_map/ppermute | solution.py:542
  10.9 0.5 collective-permute-start.1
  11.4 0.0 collective-permute-start.2
  11.4 2.4 %collective-permute-done.3.refs_1_ = bf16[560,128]{1,0:T(8,128)(2,1)S(1)} collective-permute-done((bf16[560,128]{1,0:T(8,128)(2,1)S(1)}, bf16[560,128]{1,0:T(8,128)(2,1)S(1)}, u32[]{:S(2)}, u32[]{:S(2)}) %collective-permute-start.3) | collective-permute-done | bytes 143392 | tf_op jit(solution)/shard_map/ppermute | solution.py:542
  13.8 0.0 collective-permute-start.4
  13.8 3.7 %collective-permute-done.5.refs_3_ = bf16[560,128]{1,0:T(8,128)(2,1)S(1)} collective-permute-done((bf16[560,128]{1,0:T(8,128)(2,1)S(1)}, bf16[560,128]{1,0:T(8,128)(2,1)S(1)}, u32[]{:S(2)}, u32[]{:S(2)}) %collective-permute-start.5) | collective-permute-done | bytes 143392 | tf_op jit(solution)/shard_map/ppermute | solution.py:542
  17.6 0.0 collective-permute-start.6
  17.6 0.0 collective-permute-done.1.refs_5_
  17.6 0.2 collective-permute-done.refs_0_
  17.7 0.3 collective-permute-start.7
  18.1 0.8 %collective-permute-done.6.refs_4_ = bf16[560,128]{1,0:T(8,128)(2,1)S(1)} collective-permute-done((bf16[560,128]{1,0:T(8,128)(2,1)S(1)}, bf16[560,128]{1,0:T(8,128)(2,1)S(1)}, u32[]{:S(2)}, u32[]{:S(2)}) %collective-permute-start.6) | collective-permute-done | bytes 143392 | tf_op jit(solution)/shard_map/ppermute | solution.py:549
  18.9 0.2 collective-permute-done.7.refs_6_
  19.1 1.6 %collective-permute-start.8 = (bf16[832,128]{1,0:T(8,128)(2,1)S(1)}, bf16[832,128]{1,0:T(8,128)(2,1)S(1)}, u32[]{:S(2)}, u32[]{:S(2)}) collective-permute-start(bf16[832,128]{1,0:T(8,128)(2,1)S(1)} %collective-permute-done.refs_0_), channel_id=1, source_target_pairs={{0,1},{1,0},{2,3},{3,2},{4,5},{5,4},{6,7},{7,6},{8,9},{9,8},{10,11... | collective-permute-start | bytes 638984 | tf_op jit(solution)/shard_map/ppermute | solution.py:556
  20.7 2.4 %query_side.1 = (bf16[256,128]{1,0:T(8,128)(2,1)}, f32[8,256]{1,0:T(8,128)S(1)}, f32[256,128]{1,0:T(8,128)S(1)}) custom-call(bf16[560,128]{1,0:T(8,128)(2,1)S(1)} %collective-permute-done.2.refs_0_, bf16[560,128]{1,0:T(8,128)(2,1)S(1)} %collective-permute-done.3.refs_1_, bf16[560,128]{1,0:T(8,128)(2,1)S(1)} %collective-permute-done.4.refs_2_, ...), custom_call_target="tpu_custom_call" | custom-call | flops 1 | bytes 1024 | tf_op jit(solution)/shard_map/query_side/pallas_call | solution.py:558
  23.1 0.0 collective-permute-start.9
  23.1 1.1 %collective-permute-done.9.refs_8_ = f32[8,256]{1,0:T(8,128)S(1)} collective-permute-done((f32[8,256]{1,0:T(8,128)S(1)}, f32[8,256]{1,0:T(8,128)S(1)}, u32[]{:S(2)}, u32[]{:S(2)}) %collective-permute-start.9) | collective-permute-done | bytes 8224 | tf_op jit(solution)/shard_map/ppermute | solution.py:581
  24.3 2.3 %collective-permute-done.8.refs_1_ = bf16[832,128]{1,0:T(8,128)(2,1)S(1)} collective-permute-done((bf16[832,128]{1,0:T(8,128)(2,1)S(1)}, bf16[832,128]{1,0:T(8,128)(2,1)S(1)}, u32[]{:S(2)}, u32[]{:S(2)}) %collective-permute-start.8) | collective-permute-done | bytes 213024 | tf_op jit(solution)/shard_map/ppermute | solution.py:556
  26.6 1.6 %collective-permute-start.10 = (bf16[2,832,128]{2,1,0:T(8,128)(2,1)S(1)}, bf16[2,832,128]{2,1,0:T(8,128)(2,1)S(1)}, u32[]{:S(2)}, u32[]{:S(2)}) collective-permute-start(bf16[2,832,128]{2,1,0:T(8,128)(2,1)S(1)} %get-tuple-element.79), channel_id=1, source_target_pairs={{0,1},{1,0},{2,3},{3,2},{4,5},{5,4},{6,7},{7,6},{8,9},{9,8},{10,11... | collective-permute-start | bytes 1277960 | tf_op jit(solution)/shard_map/ppermute | solution.py:587
  28.2 0.7 %collective-permute-start.11 = (f32[16,256]{1,0:T(8,128)S(1)}, f32[16,256]{1,0:T(8,128)S(1)}, u32[]{:S(2)}, u32[]{:S(2)}) collective-permute-start(f32[16,256]{1,0:T(8,128)S(1)} %pad_maximum_fusion.1), channel_id=1, source_target_pairs={{0,8},{8,0},{1,9},{9,1},{2,10},{10,2},{3,11},{11,3},{4,12},{12,4},... | collective-permute-start | bytes 49160 | tf_op jit(solution)/shard_map/ppermute | solution.py:581
  28.9 3.0 %collective-permute-done.11.refs_9_ = f32[16,256]{1,0:T(8,128)S(1)} collective-permute-done((f32[16,256]{1,0:T(8,128)S(1)}, f32[16,256]{1,0:T(8,128)S(1)}, u32[]{:S(2)}, u32[]{:S(2)}) %collective-permute-start.11) | collective-permute-done | bytes 16416 | tf_op jit(solution)/shard_map/ppermute | solution.py:581
  31.9 1.4 %collective-permute-start.12 = (f32[32,256]{1,0:T(8,128)S(1)}, f32[32,256]{1,0:T(8,128)S(1)}, u32[]{:S(2)}, u32[]{:S(2)}) collective-permute-start(f32[32,256]{1,0:T(8,128)S(1)} %pad_maximum_fusion), channel_id=1, source_target_pairs={{0,16},{16,0},{1,17},{17,1},{2,18},{18,2},{3,19},{19,3},{4,20},{20... | collective-permute-start | bytes 98312 | tf_op jit(solution)/shard_map/ppermute | solution.py:581
  33.3 2.5 %collective-permute-done.12.refs_10_ = f32[32,256]{1,0:T(8,128)S(1)} collective-permute-done((f32[32,256]{1,0:T(8,128)S(1)}, f32[32,256]{1,0:T(8,128)S(1)}, u32[]{:S(2)}, u32[]{:S(2)}) %collective-permute-start.12) | collective-permute-done | bytes 32800 | tf_op jit(solution)/shard_map/ppermute | solution.py:581
  35.9 0.8 %collective-permute-start.13 = (bf16[2,832,128]{2,1,0:T(8,128)(2,1)S(1)}, bf16[2,832,128]{2,1,0:T(8,128)(2,1)S(1)}, u32[]{:S(2)}, u32[]{:S(2)}) collective-permute-start(bf16[2,832,128]{2,1,0:T(8,128)(2,1)S(1)} %stack.1.rest_0_), channel_id=1, source_target_pairs={{0,8},{8,0},{16,24},{24,16},{1,9},{9,1},{17,25},{25,17},{2,10},{10... | collective-permute-start | bytes 1277960 | tf_op jit(solution)/shard_map/ppermute | solution.py:602
  36.7 1.2 %collective-permute-start.14 = (bf16[2,832,128]{2,1,0:T(8,128)(2,1)S(1)}, bf16[2,832,128]{2,1,0:T(8,128)(2,1)S(1)}, u32[]{:S(2)}, u32[]{:S(2)}) collective-permute-start(bf16[2,832,128]{2,1,0:T(8,128)(2,1)S(1)} %stack.1.rest_0_), channel_id=1, source_target_pairs={{0,16},{8,24},{16,0},{24,8},{1,17},{9,25},{17,1},{25,9},{2,18},{10... | collective-permute-start | bytes 1277960 | tf_op jit(solution)/shard_map/ppermute | solution.py:602
  37.9 1.5 %collective-permute-start.15 = (bf16[2,832,128]{2,1,0:T(8,128)(2,1)S(1)}, bf16[2,832,128]{2,1,0:T(8,128)(2,1)S(1)}, u32[]{:S(2)}, u32[]{:S(2)}) collective-permute-start(bf16[2,832,128]{2,1,0:T(8,128)(2,1)S(1)} %stack.1.rest_0_), channel_id=1, source_target_pairs={{0,24},{8,16},{16,8},{24,0},{1,25},{9,17},{17,9},{25,1},{2,26},{10... | collective-permute-start | bytes 1277960 | tf_op jit(solution)/shard_map/ppermute | solution.py:602
  39.4 0.5 collective-permute-start.16
  39.9 3.6 %gradients.1 = bf16[832,128]{1,0:T(8,128)(2,1)S(1)} custom-call(bf16[560,128]{1,0:T(8,128)(2,1)S(1)} %collective-permute-done.2.refs_0_, bf16[560,128]{1,0:T(8,128)(2,1)S(1)} %collective-permute-done.3.refs_1_, bf16[560,128]{1,0:T(8,128)(2,1)S(1)} %collective-permute-done.4.refs_2_, bf16[560,128]{1,0:T(8,128)(2,1)S(1)} %collective-permute-done.5.refs_3_, ...), custom_call_target="tpu_custom_call" | custom-call | flops 1 | bytes 1024 | tf_op jit(solution)/shard_map/gradients/pallas_call | solution.py:606
  43.5 0.0 collective-permute-done.10.rest_4_
  43.6 21.8 %all-gather = bf16[3328,128]{1,0:T(8,128)(2,1)S(1)} all-gather(bf16[832,128]{1,0:T(8,128)(2,1)S(1)} %gradients.1), channel_id=2, replica_groups=mesh['half0'=2,'half1'=2,'core'=2,'tp'=4] {'tp'}, dimensions={0}, use_global_device_ids=true | all-gather | bytes 1064960 | tf_op jit(solution)/shard_map/all_gather | solution.py:622
  65.4 0.2 cat.1
  65.6 0.0 collective-permute-done.13.rest_1_
  65.6 0.0 collective-permute-done.14.rest_2_
  65.6 0.0 collective-permute-done.15.rest_3_
  65.6 0.1 collective-permute-start.17
  65.7 0.5 collective-permute-start.18
  66.2 0.1 collective-permute-start.19
  66.3 0.4 collective-permute-start.20
  66.7 0.1 collective-permute-start.21
  66.8 0.7 collective-permute-done.17.rest_0_
  67.5 0.1 collective-permute-start.22
  67.6 1.9 %columns.2.rest_6_ = bf16[256,2048]{1,0:T(8,128)(2,1)} custom-call(bf16[256,1536]{1,0:T(8,128)(2,1)S(1)} %get-tuple-element.98.cat_ref, bf16[256,128]{1,0:T(8,128)(2,1)S(1)} %get-tuple-element.99.feat_ref, bf16[2048,256]{1,0:T(8,128)(2,1)S(1)} %get-tuple-element.100.ww_ref, bf16[2048,128]{1,0:T(8,128)(2,1)S(1)} %get-tuple-element.101.vw_ref, ...), custom_call_target="tpu_custom_call" | custom-call | flops 1 | bytes 1024 | tf_op jit(solution)/shard_map/columns/pallas_call | solution.py:644
  69.5 0.0 collective-permute-done.18.rest_1_
  69.5 0.4 collective-permute-done.21.rest_4_
  69.9 0.6 collective-permute-done.22.rest_5_
  70.5 1.9 %columns.3 = bf16[256,2048]{1,0:T(8,128)(2,1)} custom-call(bf16[256,1536]{1,0:T(8,128)(2,1)S(1)} %get-tuple-element.98.cat_ref, bf16[256,128]{1,0:T(8,128)(2,1)S(1)} %get-tuple-element.99.feat_ref, bf16[2048,256]{1,0:T(8,128)(2,1)S(1)} %get-tuple-element.100.ww_ref, ...), custom_call_target="tpu_custom_call", output_to_operand_aliasing={{}: (11, {})} | custom-call | flops 1 | bytes 1024 | tf_op jit(solution)/shard_map/columns/pallas_call | solution.py:644
  (8 shorter events, 0.0 us)
Async XLA Ops:
  3.8 13.9 %collective-permute-start = (bf16[832,128]{1,0:T(8,128)(2,1)S(1)}, bf16[832,128]{1,0:T(8,128)(2,1)S(1)}, u32[]{:S(2)}, u32[]{:S(2)}) collective-permute-start(bf16[832,128]{1,0:T(8,128)(2,1)S(1)} %get-tuple-element.57), channel_id=1, source_target_pairs={{0,2},{1,3},{2,0},{3,1},{4,6},{5,7},{6,4},{7,5},{8,10},{9,11},{10,... | collective-permute-start | bytes 638984 | tf_op jit(solution)/shard_map/ppermute | solution.py:545
  7.9 5.9 %collective-permute-start.3 = (bf16[560,128]{1,0:T(8,128)(2,1)S(1)}, bf16[560,128]{1,0:T(8,128)(2,1)S(1)}, u32[]{:S(2)}, u32[]{:S(2)}) collective-permute-start(bf16[560,128]{1,0:T(8,128)(2,1)S(1)} %get-tuple-element.61), channel_id=1, source_target_pairs={{0,8},{8,0},{16,24},{24,16},{1,9},{9,1},{17,25},{25,17},{2,10},{10... | collective-permute-start | bytes 430088 | tf_op jit(solution)/shard_map/ppermute | solution.py:542
  9.4 8.2 %collective-permute-start.5 = (bf16[560,128]{1,0:T(8,128)(2,1)S(1)}, bf16[560,128]{1,0:T(8,128)(2,1)S(1)}, u32[]{:S(2)}, u32[]{:S(2)}) collective-permute-start(bf16[560,128]{1,0:T(8,128)(2,1)S(1)} %get-tuple-element.62), channel_id=1, source_target_pairs={{0,16},{8,24},{16,0},{24,8},{1,17},{9,25},{17,1},{25,9},{2,18},{10... | collective-permute-start | bytes 430088 | tf_op jit(solution)/shard_map/ppermute | solution.py:542
  10.9 6.7 %collective-permute-start.1 = (bf16[560,128]{1,0:T(8,128)(2,1)S(1)}, bf16[560,128]{1,0:T(8,128)(2,1)S(1)}, u32[]{:S(2)}, u32[]{:S(2)}) collective-permute-start(bf16[560,128]{1,0:T(8,128)(2,1)S(1)} %get-tuple-element.58), channel_id=1, source_target_pairs={{0,24},{8,16},{16,8},{24,0},{1,25},{9,17},{17,9},{25,1},{2,26},{10... | collective-permute-start | bytes 430088 | tf_op jit(solution)/shard_map/ppermute | solution.py:542
  11.4 6.7 %collective-permute-start.2 = (bf16[560,128]{1,0:T(8,128)(2,1)S(1)}, bf16[560,128]{1,0:T(8,128)(2,1)S(1)}, u32[]{:S(2)}, u32[]{:S(2)}) collective-permute-start(bf16[560,128]{1,0:T(8,128)(2,1)S(1)} %get-tuple-element.60), channel_id=1, source_target_pairs={{0,4},{4,0},{1,5},{5,1},{2,6},{6,2},{3,7},{7,3},{8,12},{12,8},{9,1... | collective-permute-start | bytes 430088 | tf_op jit(solution)/shard_map/ppermute | solution.py:543
  13.8 4.3 %collective-permute-start.4 = (bf16[560,128]{1,0:T(8,128)(2,1)S(1)}, bf16[560,128]{1,0:T(8,128)(2,1)S(1)}, u32[]{:S(2)}, u32[]{:S(2)}) collective-permute-start(bf16[560,128]{1,0:T(8,128)(2,1)S(1)} %collective-permute-done.3.refs_1_), channel_id=1, source_target_pairs={{0,4},{4,0},{1,5},{5,1},{2,6},{6,2},{3,7},{7,3},{8,12},{12,8},{9,1... | collective-permute-start | bytes 430088 | tf_op jit(solution)/shard_map/ppermute | solution.py:549
  17.6 1.4 %collective-permute-start.6 = (bf16[560,128]{1,0:T(8,128)(2,1)S(1)}, bf16[560,128]{1,0:T(8,128)(2,1)S(1)}, u32[]{:S(2)}, u32[]{:S(2)}) collective-permute-start(bf16[560,128]{1,0:T(8,128)(2,1)S(1)} %collective-permute-done.5.refs_3_), channel_id=1, source_target_pairs={{0,4},{4,0},{1,5},{5,1},{2,6},{6,2},{3,7},{7,3},{8,12},{12,8},{9,1... | collective-permute-start | bytes 430088 | tf_op jit(solution)/shard_map/ppermute | solution.py:549
  17.7 1.4 %collective-permute-start.7 = (bf16[560,128]{1,0:T(8,128)(2,1)S(1)}, bf16[560,128]{1,0:T(8,128)(2,1)S(1)}, u32[]{:S(2)}, u32[]{:S(2)}) collective-permute-start(bf16[560,128]{1,0:T(8,128)(2,1)S(1)} %collective-permute-done.1.refs_5_), channel_id=1, source_target_pairs={{0,4},{4,0},{1,5},{5,1},{2,6},{6,2},{3,7},{7,3},{8,12},{12,8},{9,1... | collective-permute-start | bytes 430088 | tf_op jit(solution)/shard_map/ppermute | solution.py:549
  19.1 7.5 %collective-permute-start.8 = (bf16[832,128]{1,0:T(8,128)(2,1)S(1)}, bf16[832,128]{1,0:T(8,128)(2,1)S(1)}, u32[]{:S(2)}, u32[]{:S(2)}) collective-permute-start(bf16[832,128]{1,0:T(8,128)(2,1)S(1)} %collective-permute-done.refs_0_), channel_id=1, source_target_pairs={{0,1},{1,0},{2,3},{3,2},{4,5},{5,4},{6,7},{7,6},{8,9},{9,8},{10,11... | collective-permute-start | bytes 638984 | tf_op jit(solution)/shard_map/ppermute | solution.py:556
  23.1 1.2 %collective-permute-start.9 = (f32[8,256]{1,0:T(8,128)S(1)}, f32[8,256]{1,0:T(8,128)S(1)}, u32[]{:S(2)}, u32[]{:S(2)}) collective-permute-start(f32[8,256]{1,0:T(8,128)S(1)} %get-tuple-element.89.refs_7_), channel_id=1, source_target_pairs={{0,4},{4,0},{1,5},{5,1},{2,6},{6,2},{3,7},{7,3},{8,12},{12,8},{9,1... | collective-permute-start | bytes 24584 | tf_op jit(solution)/shard_map/ppermute | solution.py:581
  26.6 16.9 %collective-permute-start.10 = (bf16[2,832,128]{2,1,0:T(8,128)(2,1)S(1)}, bf16[2,832,128]{2,1,0:T(8,128)(2,1)S(1)}, u32[]{:S(2)}, u32[]{:S(2)}) collective-permute-start(bf16[2,832,128]{2,1,0:T(8,128)(2,1)S(1)} %get-tuple-element.79), channel_id=1, source_target_pairs={{0,1},{1,0},{2,3},{3,2},{4,5},{5,4},{6,7},{7,6},{8,9},{9,8},{10,11... | collective-permute-start | bytes 1277960 | tf_op jit(solution)/shard_map/ppermute | solution.py:587
  28.2 3.7 %collective-permute-start.11 = (f32[16,256]{1,0:T(8,128)S(1)}, f32[16,256]{1,0:T(8,128)S(1)}, u32[]{:S(2)}, u32[]{:S(2)}) collective-permute-start(f32[16,256]{1,0:T(8,128)S(1)} %pad_maximum_fusion.1), channel_id=1, source_target_pairs={{0,8},{8,0},{1,9},{9,1},{2,10},{10,2},{3,11},{11,3},{4,12},{12,4},... | collective-permute-start | bytes 49160 | tf_op jit(solution)/shard_map/ppermute | solution.py:581
  31.9 3.9 %collective-permute-start.12 = (f32[32,256]{1,0:T(8,128)S(1)}, f32[32,256]{1,0:T(8,128)S(1)}, u32[]{:S(2)}, u32[]{:S(2)}) collective-permute-start(f32[32,256]{1,0:T(8,128)S(1)} %pad_maximum_fusion), channel_id=1, source_target_pairs={{0,16},{16,0},{1,17},{17,1},{2,18},{18,2},{3,19},{19,3},{4,20},{20... | collective-permute-start | bytes 98312 | tf_op jit(solution)/shard_map/ppermute | solution.py:581
  35.9 29.7 %collective-permute-start.13 = (bf16[2,832,128]{2,1,0:T(8,128)(2,1)S(1)}, bf16[2,832,128]{2,1,0:T(8,128)(2,1)S(1)}, u32[]{:S(2)}, u32[]{:S(2)}) collective-permute-start(bf16[2,832,128]{2,1,0:T(8,128)(2,1)S(1)} %stack.1.rest_0_), channel_id=1, source_target_pairs={{0,8},{8,0},{16,24},{24,16},{1,9},{9,1},{17,25},{25,17},{2,10},{10... | collective-permute-start | bytes 1277960 | tf_op jit(solution)/shard_map/ppermute | solution.py:602
  36.7 28.9 %collective-permute-start.14 = (bf16[2,832,128]{2,1,0:T(8,128)(2,1)S(1)}, bf16[2,832,128]{2,1,0:T(8,128)(2,1)S(1)}, u32[]{:S(2)}, u32[]{:S(2)}) collective-permute-start(bf16[2,832,128]{2,1,0:T(8,128)(2,1)S(1)} %stack.1.rest_0_), channel_id=1, source_target_pairs={{0,16},{8,24},{16,0},{24,8},{1,17},{9,25},{17,1},{25,9},{2,18},{10... | collective-permute-start | bytes 1277960 | tf_op jit(solution)/shard_map/ppermute | solution.py:602
  37.9 27.7 %collective-permute-start.15 = (bf16[2,832,128]{2,1,0:T(8,128)(2,1)S(1)}, bf16[2,832,128]{2,1,0:T(8,128)(2,1)S(1)}, u32[]{:S(2)}, u32[]{:S(2)}) collective-permute-start(bf16[2,832,128]{2,1,0:T(8,128)(2,1)S(1)} %stack.1.rest_0_), channel_id=1, source_target_pairs={{0,24},{8,16},{16,8},{24,0},{1,25},{9,17},{17,9},{25,1},{2,26},{10... | collective-permute-start | bytes 1277960 | tf_op jit(solution)/shard_map/ppermute | solution.py:602
  39.4 26.2 %collective-permute-start.16 = (bf16[2,832,128]{2,1,0:T(8,128)(2,1)S(1)}, bf16[2,832,128]{2,1,0:T(8,128)(2,1)S(1)}, u32[]{:S(2)}, u32[]{:S(2)}) collective-permute-start(bf16[2,832,128]{2,1,0:T(8,128)(2,1)S(1)} %get-tuple-element.105), channel_id=1, source_target_pairs={{0,1},{1,0},{2,3},{3,2},{4,5},{5,4},{6,7},{7,6},{8,9},{9,8},{10,11... | collective-permute-start | bytes 1277960 | tf_op jit(solution)/shard_map/ppermute | solution.py:587
  65.6 1.8 %collective-permute-start.17 = (bf16[2,832,128]{2,1,0:T(8,128)(2,1)S(1)}, bf16[2,832,128]{2,1,0:T(8,128)(2,1)S(1)}, u32[]{:S(2)}, u32[]{:S(2)}) collective-permute-start(bf16[2,832,128]{2,1,0:T(8,128)(2,1)S(1)} %stack.1.rest_0_), channel_id=1, source_target_pairs={{0,4},{4,0},{1,5},{5,1},{2,6},{6,2},{3,7},{7,3},{8,12},{12,8},{9,1... | collective-permute-start | bytes 1277960 | tf_op jit(solution)/shard_map/ppermute | solution.py:637
  65.7 3.8 %collective-permute-start.18 = (bf16[2,832,128]{2,1,0:T(8,128)(2,1)S(1)}, bf16[2,832,128]{2,1,0:T(8,128)(2,1)S(1)}, u32[]{:S(2)}, u32[]{:S(2)}) collective-permute-start(bf16[2,832,128]{2,1,0:T(8,128)(2,1)S(1)} %collective-permute-done.13.rest_1_), channel_id=1, source_target_pairs={{0,4},{4,0},{1,5},{5,1},{2,6},{6,2},{3,7},{7,3},{8,12},{12,8},{9,1... | collective-permute-start | bytes 1277960 | tf_op jit(solution)/shard_map/ppermute | solution.py:637
  66.2 3.3 %collective-permute-start.19 = (bf16[2,832,128]{2,1,0:T(8,128)(2,1)S(1)}, bf16[2,832,128]{2,1,0:T(8,128)(2,1)S(1)}, u32[]{:S(2)}, u32[]{:S(2)}) collective-permute-start(bf16[2,832,128]{2,1,0:T(8,128)(2,1)S(1)} %collective-permute-done.14.rest_2_), channel_id=1, source_target_pairs={{0,4},{4,0},{1,5},{5,1},{2,6},{6,2},{3,7},{7,3},{8,12},{12,8},{9,1... | collective-permute-start | bytes 1277960 | tf_op jit(solution)/shard_map/ppermute | solution.py:637
  66.3 3.2 %collective-permute-start.20 = (bf16[2,832,128]{2,1,0:T(8,128)(2,1)S(1)}, bf16[2,832,128]{2,1,0:T(8,128)(2,1)S(1)}, u32[]{:S(2)}, u32[]{:S(2)}) collective-permute-start(bf16[2,832,128]{2,1,0:T(8,128)(2,1)S(1)} %collective-permute-done.15.rest_3_), channel_id=1, source_target_pairs={{0,4},{4,0},{1,5},{5,1},{2,6},{6,2},{3,7},{7,3},{8,12},{12,8},{9,1... | collective-permute-start | bytes 1277960 | tf_op jit(solution)/shard_map/ppermute | solution.py:637
  66.7 3.2 %collective-permute-start.21 = (bf16[2,832,128]{2,1,0:T(8,128)(2,1)S(1)}, bf16[2,832,128]{2,1,0:T(8,128)(2,1)S(1)}, u32[]{:S(2)}, u32[]{:S(2)}) collective-permute-start(bf16[2,832,128]{2,1,0:T(8,128)(2,1)S(1)} %collective-permute-done.10.rest_4_), channel_id=1, source_target_pairs={{0,4},{4,0},{1,5},{5,1},{2,6},{6,2},{3,7},{7,3},{8,12},{12,8},{9,1... | collective-permute-start | bytes 1277960 | tf_op jit(solution)/shard_map/ppermute | solution.py:636
  67.5 3.0 %collective-permute-start.22 = (bf16[2,832,128]{2,1,0:T(8,128)(2,1)S(1)}, bf16[2,832,128]{2,1,0:T(8,128)(2,1)S(1)}, u32[]{:S(2)}, u32[]{:S(2)}) collective-permute-start(bf16[2,832,128]{2,1,0:T(8,128)(2,1)S(1)} %collective-permute-done.16.rest_5_), channel_id=1, source_target_pairs={{0,4},{4,0},{1,5},{5,1},{2,6},{6,2},{3,7},{7,3},{8,12},{12,8},{9,1... | collective-permute-start | bytes 1277960 | tf_op jit(solution)/shard_map/ppermute | solution.py:636

commit v21 on v20

--- a/solution.py
+++ b/solution.py
@@ -152,12 +152,11 @@
         pl.when(later)(lambda ref=ref: put_keys(ref))
         pl.when(jnp.logical_not(later))(lambda ref=ref: put_query(ref))
     if packs:
-        own_pack, *first_packs = rest[:packs]
+        own_pack, other_pack = rest[:packs]
         pack(me, ww_ref, vw_ref, fw_ref, own_pack)
-        for n, ref in enumerate(first_packs):
-            for d in range(2):
-                piece = jnp.bitwise_xor(me, 4 * n + 2 * d)
-                pack(piece, ww_ref, vw_ref, fw_ref, ref.at[d])
+        for d in range(other_pack.shape[0]):
+            piece = jnp.bitwise_xor(me, 2 * d + 2)
+            pack(piece, ww_ref, vw_ref, fw_ref, other_pack.at[d])
 
 def stack_kernel(*refs):
     *parts, out_ref = refs
@@ -427,7 +426,7 @@
     copies = []
     for n, (e, ref) in enumerate(zip(distances, pieces)):
         part = pl.ds(pl.multiple_of(jnp.bitwise_xor(me, e) * tile, tile), tile)
-        views = [firsts[e // 4].at[e // 2 % 2]]
+        views = [firsts[1].at[e // 2 - 1] if e > 1 else firsts[0]]
         views += [ref.at[t] for t in range(heads - 2)]
         main = [ww_ref[part, :], vw_ref[part, :]]
         main += [v[m * tile : (m + 1) * tile, :] for v in views for m in range(3)]
@@ -506,7 +505,7 @@
     packs = []
     if spread:
         packs = [jax.ShapeDtypeStruct((columns * tile // LANES, LANES), bf16)]
-        packs += [jax.ShapeDtypeStruct((2, *packs[0].shape), bf16)] * (chips // 2)
+        packs += [jax.ShapeDtypeStruct((chips - 1, *packs[0].shape), bf16)]
 
     payload = 2 * rows + 2 * nf + 16
     block = jax.ShapeDtypeStruct((payload, LANES), bf16)
@@ -552,7 +551,8 @@
         recv = [jnp.stack(recv)]
 
     if spread:
-        across, recv = lax.optimization_barrier((across, recv))
+        early = lax.ppermute(outs[0], "tp", [(z, z ^ 1) for z in range(heads)])
+        across, early, recv = lax.optimization_barrier((across, early, recv))
         near = [across, lax.ppermute(across, "tp", [(z, z ^ 1) for z in range(heads)])]
 
     attended, stat, sheet = pl.pallas_call(
@@ -583,8 +583,7 @@
         stats = [jnp.concatenate(stats, axis=0)]
 
     if spread:
-        later, stats = lax.optimization_barrier((outs[2], stats))
-        first = [lax.ppermute(p, "tp", [(z, z ^ 1) for z in range(heads)]) for p in (sent, later)]
+        first = [early, lax.ppermute(sent, "tp", [(z, z ^ 1) for z in range(heads)])]
         near, stats = lax.optimization_barrier((near, stats))
         pieces = [
             pl.pallas_call(
@@ -618,7 +617,7 @@
         weights = lax.all_gather(weights, "tp")
         return (attended, merge(lax.all_gather(grads, "tp"), weights, rows, dim))
 
-    first[0], grads = lax.optimization_barrier((first[0], grads))
+    first[1], grads = lax.optimization_barrier((first[1], grads))
     grads = lax.all_gather(grads, "tp")
     cat, feats = pl.pallas_call(
         cat_kernel,

time: 72.5 us -> 68.4 us (0.943)
  blocking collectives: 21.8 us -> 18.4 us
  waiting for transfers between devices: 18.1 us -> 17.2 us
    all_gather x1, blocking collectives: 21.8 us -> 18.4 us  [per_device(): grads = lax.all_gather(grads, 'tp')]
    ppermute x2, waiting for transfers between devices: 0.01 us -> 2.83 us  [the longest x1 2.83 us: per_device(): early = lax.ppermute(outs[0], 'tp', [(z, z ^ 1) for z in range(heads)])]
    ppermute x3, waiting for transfers between devices: 6.17 us -> 4.2 us  [per_device(): lax.ppermute(sends[d], ctx[:-1], [(i, i ^ d) for i in range(chips)])]
    ppermute x1, starting transfers between devices: 1.57 us -> 0.07 us  [per_device(): lax.ppermute(across, 'tp', [(z, z ^ 1) for z in range(heads)])]
    ppermute x3, waiting for transfers between devices: 1.05 us -> 0.01 us  [per_device(): recv[2 * d + 1] = lax.ppermute(recv[2 * d], 'core', swap)]
    ppermute x2, starting transfers between devices: 2.03 us -> 2.97 us  [the longest x1 1.58 us: per_device(): early = lax.ppermute(outs[0], 'tp', [(z, z ^ 1) for z in range(heads)])]
  transfers between devices with their start and end apart: 23 -> 23, of which waited for: 12 -> 12; matrix products, arithmetic and copies ran while one was open for 0% -> 0% of each run, Pallas kernels for 11% -> 12%
where the time goes in v21:
time: 68.4 us; the launch traced here: 68.3 us
  starting transfers between devices  18.7 us (27%)
  blocking collectives  18.4 us (27%)
  waiting for transfers between devices  17.2 us (25%)
  Pallas kernels  13.1 us (19%)
  between operations  0.74 us (1%)
    all_gather x1, blocking collectives, per_device(): grads = lax.all_gather(grads, 'tp')  18.4 us
    ppermute x3, waiting for transfers between devices, per_device(): stats.append(lax.ppermute(held, name, swap))  6.07 us
    ppermute x3, waiting for transfers between devices, per_device(): lax.ppermute(sends[d], ctx[:-1], [(i, i ^ d) for i in range(chips)])  4.2 us
    ppermute x1, starting transfers between devices, per_device(): across = lax.ppermute(outs[0], 'tp', [(z, z ^ 2) for z in range(heads)])  4.1 us
    pallas_call x2, Pallas kernels, per_device(): pl.pallas_call(partial(columns_kernel, ctx, distances), out_shape=jax.Sha...  3.71 us
    pallas_call x1, Pallas kernels, per_device(): pl.pallas_call(lambda *refs: gradient_kernel(ctx, count, len(recv), len(s...  3.62 us
    ppermute x3, starting transfers between devices, per_device(): lax.ppermute(pieces[0], ctx[:-1], [(i, i ^ d) for i in range(chips)])  3.55 us
    ppermute x3, starting transfers between devices, per_device(): lax.ppermute(sends[d], ctx[:-1], [(i, i ^ d) for i in range(chips)])  3.49 us
  transfers between devices with their start and end apart: 23, of which 12 were waited for; matrix products, arithmetic and copies ran while one was open for 0% of the time, Pallas kernels for 12%

profile of v21, /device:TPU:0, one launch (start us, length us, event | category | flops | bytes accessed | tf_op | source)
XLA Modules:
  0.0 68.3 jit_solution(11628212938983112686)
XLA Ops:
  0.6 3.1 %project.1 = (bf16[832,128]{1,0:T(8,128)(2,1)S(1)}, bf16[3,832,128]{2,1,0:T(8,128)(2,1)S(1)}, bf16[560,128]{1,0:T(8,128)(2,1)S(1)}, bf16[560,128]{1,0:T(8,128)(2...) custom-call(bf16[256,2048]{1,0:T(8,128)(2,1)} %tok_hbm.1, ...), custom_call_target="tpu_custom_call" | custom-call | flops 1 | bytes 1024 | tf_op jit(solution)/shard_map/project/pallas_call | solution.py:512
  3.8 4.1 %collective-permute-start = (bf16[832,128]{1,0:T(8,128)(2,1)S(1)}, bf16[832,128]{1,0:T(8,128)(2,1)S(1)}, u32[]{:S(2)}, u32[]{:S(2)}) collective-permute-start(bf16[832,128]{1,0:T(8,128)(2,1)S(1)} %get-tuple-element.52), channel_id=1, source_target_pairs={{0,2},{1,3},{2,0},{3,1},{4,6},{5,7},{6,4},{7,5},{8,10},{9,11},{10,... | collective-permute-start | bytes 638984 | tf_op jit(solution)/shard_map/ppermute | solution.py:544
  7.9 2.4 %collective-permute-start.1 = (bf16[560,128]{1,0:T(8,128)(2,1)S(1)}, bf16[560,128]{1,0:T(8,128)(2,1)S(1)}, u32[]{:S(2)}, u32[]{:S(2)}) collective-permute-start(bf16[560,128]{1,0:T(8,128)(2,1)S(1)} %get-tuple-element.53), channel_id=1, source_target_pairs={{0,24},{8,16},{16,8},{24,0},{1,25},{9,17},{17,9},{25,1},{2,26},{10... | collective-permute-start | bytes 430088 | tf_op jit(solution)/shard_map/ppermute | solution.py:541
  10.3 0.5 collective-permute-start.4
  10.9 0.5 collective-permute-start.6
  11.4 1.6 %collective-permute-start.2 = (bf16[832,128]{1,0:T(8,128)(2,1)S(1)}, bf16[832,128]{1,0:T(8,128)(2,1)S(1)}, u32[]{:S(2)}, u32[]{:S(2)}) collective-permute-start(bf16[832,128]{1,0:T(8,128)(2,1)S(1)} %get-tuple-element.52), channel_id=1, source_target_pairs={{0,1},{1,0},{2,3},{3,2},{4,5},{5,4},{6,7},{7,6},{8,9},{9,8},{10,11... | collective-permute-start | bytes 638984 | tf_op jit(solution)/shard_map/ppermute | solution.py:554
  13.0 2.5 %collective-permute-done.1.refs_5_ = bf16[560,128]{1,0:T(8,128)(2,1)S(1)} collective-permute-done((bf16[560,128]{1,0:T(8,128)(2,1)S(1)}, bf16[560,128]{1,0:T(8,128)(2,1)S(1)}, u32[]{:S(2)}, u32[]{:S(2)}) %collective-permute-start.1) | collective-permute-done | bytes 143392 | tf_op jit(solution)/shard_map/ppermute | solution.py:541
  15.5 1.7 %collective-permute-done.4.refs_1_ = bf16[560,128]{1,0:T(8,128)(2,1)S(1)} collective-permute-done((bf16[560,128]{1,0:T(8,128)(2,1)S(1)}, bf16[560,128]{1,0:T(8,128)(2,1)S(1)}, u32[]{:S(2)}, u32[]{:S(2)}) %collective-permute-start.4) | collective-permute-done | bytes 143392 | tf_op jit(solution)/shard_map/ppermute | solution.py:541
  17.2 0.0 collective-permute-start.5
  17.2 0.0 collective-permute-done.6.refs_3_
  17.2 0.5 collective-permute-start.7
  17.7 0.2 collective-permute-done.refs_0_
  17.8 0.0 collective-permute-start.8
  17.8 0.0 collective-permute-done.3.refs_0_
  17.8 2.8 %collective-permute-done.2.rest_4_ = bf16[832,128]{1,0:T(8,128)(2,1)S(1)} collective-permute-done((bf16[832,128]{1,0:T(8,128)(2,1)S(1)}, bf16[832,128]{1,0:T(8,128)(2,1)S(1)}, u32[]{:S(2)}, u32[]{:S(2)}) %collective-permute-start.2) | collective-permute-done | bytes 213024 | tf_op jit(solution)/shard_map/ppermute | solution.py:554
  20.7 0.0 collective-permute-done.5.refs_2_
  20.7 0.0 collective-permute-done.7.refs_4_
  20.7 0.1 collective-permute-start.9
  20.8 2.4 %query_side.1 = (bf16[256,128]{1,0:T(8,128)(2,1)}, f32[8,256]{1,0:T(8,128)S(1)}, f32[256,128]{1,0:T(8,128)S(1)}) custom-call(bf16[560,128]{1,0:T(8,128)(2,1)S(1)} %collective-permute-done.3.refs_0_, bf16[560,128]{1,0:T(8,128)(2,1)S(1)} %collective-permute-done.4.refs_1_, bf16[560,128]{1,0:T(8,128)(2,1)S(1)} %collective-permute-done.5.refs_2_, ...), custom_call_target="tpu_custom_call" | custom-call | flops 1 | bytes 1024 | tf_op jit(solution)/shard_map/query_side/pallas_call | solution.py:558
  23.1 1.2 %collective-permute-done.10.refs_8_ = f32[8,256]{1,0:T(8,128)S(1)} collective-permute-done((f32[8,256]{1,0:T(8,128)S(1)}, f32[8,256]{1,0:T(8,128)S(1)}, u32[]{:S(2)}, u32[]{:S(2)}) %collective-permute-start.10) | collective-permute-done | bytes 8224 | tf_op jit(solution)/shard_map/ppermute | solution.py:581
  24.3 2.3 %collective-permute-done.9.refs_1_ = bf16[832,128]{1,0:T(8,128)(2,1)S(1)} collective-permute-done((bf16[832,128]{1,0:T(8,128)(2,1)S(1)}, bf16[832,128]{1,0:T(8,128)(2,1)S(1)}, u32[]{:S(2)}, u32[]{:S(2)}) %collective-permute-start.9) | collective-permute-done | bytes 213024 | tf_op jit(solution)/shard_map/ppermute | solution.py:556
  26.6 1.4 %collective-permute-start.11 = (bf16[3,832,128]{2,1,0:T(8,128)(2,1)S(1)}, bf16[3,832,128]{2,1,0:T(8,128)(2,1)S(1)}, u32[]{:S(2)}, u32[]{:S(2)}) collective-permute-start(bf16[3,832,128]{2,1,0:T(8,128)(2,1)S(1)} %get-tuple-element.74), channel_id=1, source_target_pairs={{0,1},{1,0},{2,3},{3,2},{4,5},{5,4},{6,7},{7,6},{8,9},{9,8},{10,11... | collective-permute-start | bytes 1916936 | tf_op jit(solution)/shard_map/ppermute | solution.py:586
  28.0 1.5 %collective-permute-start.12 = (f32[16,256]{1,0:T(8,128)S(1)}, f32[16,256]{1,0:T(8,128)S(1)}, u32[]{:S(2)}, u32[]{:S(2)}) collective-permute-start(f32[16,256]{1,0:T(8,128)S(1)} %pad_maximum_fusion.1), channel_id=1, source_target_pairs={{0,8},{8,0},{1,9},{9,1},{2,10},{10,2},{3,11},{11,3},{4,12},{12,4},... | collective-permute-start | bytes 49160 | tf_op jit(solution)/shard_map/ppermute | solution.py:581
  29.5 2.2 %collective-permute-done.12.refs_9_ = f32[16,256]{1,0:T(8,128)S(1)} collective-permute-done((f32[16,256]{1,0:T(8,128)S(1)}, f32[16,256]{1,0:T(8,128)S(1)}, u32[]{:S(2)}, u32[]{:S(2)}) %collective-permute-start.12) | collective-permute-done | bytes 16416 | tf_op jit(solution)/shard_map/ppermute | solution.py:581
  31.7 1.3 %collective-permute-start.13 = (f32[32,256]{1,0:T(8,128)S(1)}, f32[32,256]{1,0:T(8,128)S(1)}, u32[]{:S(2)}, u32[]{:S(2)}) collective-permute-start(f32[32,256]{1,0:T(8,128)S(1)} %pad_maximum_fusion), channel_id=1, source_target_pairs={{0,16},{16,0},{1,17},{17,1},{2,18},{18,2},{3,19},{19,3},{4,20},{20... | collective-permute-start | bytes 98312 | tf_op jit(solution)/shard_map/ppermute | solution.py:581
  33.0 2.7 %collective-permute-done.13.refs_10_ = f32[32,256]{1,0:T(8,128)S(1)} collective-permute-done((f32[32,256]{1,0:T(8,128)S(1)}, f32[32,256]{1,0:T(8,128)S(1)}, u32[]{:S(2)}, u32[]{:S(2)}) %collective-permute-start.13) | collective-permute-done | bytes 32800 | tf_op jit(solution)/shard_map/ppermute | solution.py:581
  35.7 1.7 %collective-permute-start.14 = (bf16[2,832,128]{2,1,0:T(8,128)(2,1)S(1)}, bf16[2,832,128]{2,1,0:T(8,128)(2,1)S(1)}, u32[]{:S(2)}, u32[]{:S(2)}) collective-permute-start(bf16[2,832,128]{2,1,0:T(8,128)(2,1)S(1)} %stack.1.rest_0_), channel_id=1, source_target_pairs={{0,8},{8,0},{16,24},{24,16},{1,9},{9,1},{17,25},{25,17},{2,10},{10... | collective-permute-start | bytes 1277960 | tf_op jit(solution)/shard_map/ppermute | solution.py:601
  37.3 1.5 %collective-permute-start.15 = (bf16[2,832,128]{2,1,0:T(8,128)(2,1)S(1)}, bf16[2,832,128]{2,1,0:T(8,128)(2,1)S(1)}, u32[]{:S(2)}, u32[]{:S(2)}) collective-permute-start(bf16[2,832,128]{2,1,0:T(8,128)(2,1)S(1)} %stack.1.rest_0_), channel_id=1, source_target_pairs={{0,16},{8,24},{16,0},{24,8},{1,17},{9,25},{17,1},{25,9},{2,18},{10... | collective-permute-start | bytes 1277960 | tf_op jit(solution)/shard_map/ppermute | solution.py:601
  38.8 0.4 collective-permute-start.16
  39.2 3.6 %gradients.1 = bf16[832,128]{1,0:T(8,128)(2,1)S(1)} custom-call(bf16[560,128]{1,0:T(8,128)(2,1)S(1)} %collective-permute-done.3.refs_0_, bf16[560,128]{1,0:T(8,128)(2,1)S(1)} %collective-permute-done.4.refs_1_, bf16[560,128]{1,0:T(8,128)(2,1)S(1)} %collective-permute-done.5.refs_2_, bf16[560,128]{1,0:T(8,128)(2,1)S(1)} %collective-permute-done.6.refs_3_, ...), custom_call_target="tpu_custom_call" | custom-call | flops 1 | bytes 1024 | tf_op jit(solution)/shard_map/gradients/pallas_call | solution.py:605
  42.8 0.0 collective-permute-done.11.rest_5_
  42.9 18.4 %all-gather = bf16[3328,128]{1,0:T(8,128)(2,1)S(1)} all-gather(bf16[832,128]{1,0:T(8,128)(2,1)S(1)} %gradients.1), channel_id=2, replica_groups=mesh['half0'=2,'half1'=2,'core'=2,'tp'=4] {'tp'}, dimensions={0}, use_global_device_ids=true | all-gather | bytes 1064960 | tf_op jit(solution)/shard_map/all_gather | solution.py:621
  61.3 0.2 cat.1
  61.5 0.0 collective-permute-done.14.rest_1_
  61.5 0.0 collective-permute-done.15.rest_2_
  61.5 0.1 collective-permute-start.21
  61.6 0.5 collective-permute-start.22
  62.1 0.1 collective-permute-start.17
  62.2 0.4 collective-permute-start.18
  62.6 0.1 collective-permute-start.19
  62.7 0.4 collective-permute-done.21.rest_4_
  63.1 0.1 collective-permute-start.20
  63.2 1.9 %columns.2.rest_6_ = bf16[256,2048]{1,0:T(8,128)(2,1)} custom-call(bf16[256,1536]{1,0:T(8,128)(2,1)S(1)} %get-tuple-element.88.cat_ref, bf16[256,128]{1,0:T(8,128)(2,1)S(1)} %get-tuple-element.89.feat_ref, bf16[2048,256]{1,0:T(8,128)(2,1)S(1)} %get-tuple-element.90.ww_ref, bf16[2048,128]{1,0:T(8,128)(2,1)S(1)} %get-tuple-element.91.vw_ref, ...), custom_call_target="tpu_custom_call" | custom-call | flops 1 | bytes 1024 | tf_op jit(solution)/shard_map/columns/pallas_call | solution.py:643
  65.0 0.0 collective-permute-done.17.rest_0_
  65.1 0.1 collective-permute-done.18.rest_1_
  65.2 0.6 collective-permute-done.19.rest_2_
  65.8 0.6 collective-permute-done.20.rest_3_
  66.4 1.9 %columns.3 = bf16[256,2048]{1,0:T(8,128)(2,1)} custom-call(bf16[256,1536]{1,0:T(8,128)(2,1)S(1)} %get-tuple-element.88.cat_ref, bf16[256,128]{1,0:T(8,128)(2,1)S(1)} %get-tuple-element.89.feat_ref, bf16[2048,256]{1,0:T(8,128)(2,1)S(1)} %get-tuple-element.90.ww_ref, bf16[2048,128]{1,0:T(8,128)(2,1)S(1)} %get-tuple-element.91.vw_ref, ...), custom_call_target="tpu_custom_call", output_to_operand_aliasing={{}: (11, {})} | custom-call | flops 1 | bytes 1024 | tf_op jit(solution)/shard_map/columns/pallas_call | solution.py:643
  (8 shorter events, 0.0 us)
Async XLA Ops:
  3.8 14.0 %collective-permute-start = (bf16[832,128]{1,0:T(8,128)(2,1)S(1)}, bf16[832,128]{1,0:T(8,128)(2,1)S(1)}, u32[]{:S(2)}, u32[]{:S(2)}) collective-permute-start(bf16[832,128]{1,0:T(8,128)(2,1)S(1)} %get-tuple-element.52), channel_id=1, source_target_pairs={{0,2},{1,3},{2,0},{3,1},{4,6},{5,7},{6,4},{7,5},{8,10},{9,11},{10,... | collective-permute-start | bytes 638984 | tf_op jit(solution)/shard_map/ppermute | solution.py:544
  7.9 7.6 %collective-permute-start.1 = (bf16[560,128]{1,0:T(8,128)(2,1)S(1)}, bf16[560,128]{1,0:T(8,128)(2,1)S(1)}, u32[]{:S(2)}, u32[]{:S(2)}) collective-permute-start(bf16[560,128]{1,0:T(8,128)(2,1)S(1)} %get-tuple-element.53), channel_id=1, source_target_pairs={{0,24},{8,16},{16,8},{24,0},{1,25},{9,17},{17,9},{25,1},{2,26},{10... | collective-permute-start | bytes 430088 | tf_op jit(solution)/shard_map/ppermute | solution.py:541
  10.3 6.8 %collective-permute-start.4 = (bf16[560,128]{1,0:T(8,128)(2,1)S(1)}, bf16[560,128]{1,0:T(8,128)(2,1)S(1)}, u32[]{:S(2)}, u32[]{:S(2)}) collective-permute-start(bf16[560,128]{1,0:T(8,128)(2,1)S(1)} %get-tuple-element.56), channel_id=1, source_target_pairs={{0,8},{8,0},{16,24},{24,16},{1,9},{9,1},{17,25},{25,17},{2,10},{10... | collective-permute-start | bytes 430088 | tf_op jit(solution)/shard_map/ppermute | solution.py:541
  10.9 6.3 %collective-permute-start.6 = (bf16[560,128]{1,0:T(8,128)(2,1)S(1)}, bf16[560,128]{1,0:T(8,128)(2,1)S(1)}, u32[]{:S(2)}, u32[]{:S(2)}) collective-permute-start(bf16[560,128]{1,0:T(8,128)(2,1)S(1)} %get-tuple-element.57), channel_id=1, source_target_pairs={{0,16},{8,24},{16,0},{24,8},{1,17},{9,25},{17,1},{25,9},{2,18},{10... | collective-permute-start | bytes 430088 | tf_op jit(solution)/shard_map/ppermute | solution.py:541
  11.4 9.3 %collective-permute-start.2 = (bf16[832,128]{1,0:T(8,128)(2,1)S(1)}, bf16[832,128]{1,0:T(8,128)(2,1)S(1)}, u32[]{:S(2)}, u32[]{:S(2)}) collective-permute-start(bf16[832,128]{1,0:T(8,128)(2,1)S(1)} %get-tuple-element.52), channel_id=1, source_target_pairs={{0,1},{1,0},{2,3},{3,2},{4,5},{5,4},{6,7},{7,6},{8,9},{9,8},{10,11... | collective-permute-start | bytes 638984 | tf_op jit(solution)/shard_map/ppermute | solution.py:554
  15.5 2.4 %collective-permute-start.3 = (bf16[560,128]{1,0:T(8,128)(2,1)S(1)}, bf16[560,128]{1,0:T(8,128)(2,1)S(1)}, u32[]{:S(2)}, u32[]{:S(2)}) collective-permute-start(bf16[560,128]{1,0:T(8,128)(2,1)S(1)} %get-tuple-element.55), channel_id=1, source_target_pairs={{0,4},{4,0},{1,5},{5,1},{2,6},{6,2},{3,7},{7,3},{8,12},{12,8},{9,1... | collective-permute-start | bytes 430088 | tf_op jit(solution)/shard_map/ppermute | solution.py:542
  17.2 3.5 %collective-permute-start.5 = (bf16[560,128]{1,0:T(8,128)(2,1)S(1)}, bf16[560,128]{1,0:T(8,128)(2,1)S(1)}, u32[]{:S(2)}, u32[]{:S(2)}) collective-permute-start(bf16[560,128]{1,0:T(8,128)(2,1)S(1)} %collective-permute-done.4.refs_1_), channel_id=1, source_target_pairs={{0,4},{4,0},{1,5},{5,1},{2,6},{6,2},{3,7},{7,3},{8,12},{12,8},{9,1... | collective-permute-start | bytes 430088 | tf_op jit(solution)/shard_map/ppermute | solution.py:548
  17.2 3.5 %collective-permute-start.7 = (bf16[560,128]{1,0:T(8,128)(2,1)S(1)}, bf16[560,128]{1,0:T(8,128)(2,1)S(1)}, u32[]{:S(2)}, u32[]{:S(2)}) collective-permute-start(bf16[560,128]{1,0:T(8,128)(2,1)S(1)} %collective-permute-done.6.refs_3_), channel_id=1, source_target_pairs={{0,4},{4,0},{1,5},{5,1},{2,6},{6,2},{3,7},{7,3},{8,12},{12,8},{9,1... | collective-permute-start | bytes 430088 | tf_op jit(solution)/shard_map/ppermute | solution.py:548
  17.8 2.8 %collective-permute-start.8 = (bf16[560,128]{1,0:T(8,128)(2,1)S(1)}, bf16[560,128]{1,0:T(8,128)(2,1)S(1)}, u32[]{:S(2)}, u32[]{:S(2)}) collective-permute-start(bf16[560,128]{1,0:T(8,128)(2,1)S(1)} %collective-permute-done.1.refs_5_), channel_id=1, source_target_pairs={{0,4},{4,0},{1,5},{5,1},{2,6},{6,2},{3,7},{7,3},{8,12},{12,8},{9,1... | collective-permute-start | bytes 430088 | tf_op jit(solution)/shard_map/ppermute | solution.py:548
  20.7 5.9 %collective-permute-start.9 = (bf16[832,128]{1,0:T(8,128)(2,1)S(1)}, bf16[832,128]{1,0:T(8,128)(2,1)S(1)}, u32[]{:S(2)}, u32[]{:S(2)}) collective-permute-start(bf16[832,128]{1,0:T(8,128)(2,1)S(1)} %collective-permute-done.refs_0_), channel_id=1, source_target_pairs={{0,1},{1,0},{2,3},{3,2},{4,5},{5,4},{6,7},{7,6},{8,9},{9,8},{10,11... | collective-permute-start | bytes 638984 | tf_op jit(solution)/shard_map/ppermute | solution.py:556
  23.1 1.2 %collective-permute-start.10 = (f32[8,256]{1,0:T(8,128)S(1)}, f32[8,256]{1,0:T(8,128)S(1)}, u32[]{:S(2)}, u32[]{:S(2)}) collective-permute-start(f32[8,256]{1,0:T(8,128)S(1)} %get-tuple-element.79.refs_7_), channel_id=1, source_target_pairs={{0,4},{4,0},{1,5},{5,1},{2,6},{6,2},{3,7},{7,3},{8,12},{12,8},{9,1... | collective-permute-start | bytes 24584 | tf_op jit(solution)/shard_map/ppermute | solution.py:581
  26.6 16.3 %collective-permute-start.11 = (bf16[3,832,128]{2,1,0:T(8,128)(2,1)S(1)}, bf16[3,832,128]{2,1,0:T(8,128)(2,1)S(1)}, u32[]{:S(2)}, u32[]{:S(2)}) collective-permute-start(bf16[3,832,128]{2,1,0:T(8,128)(2,1)S(1)} %get-tuple-element.74), channel_id=1, source_target_pairs={{0,1},{1,0},{2,3},{3,2},{4,5},{5,4},{6,7},{7,6},{8,9},{9,8},{10,11... | collective-permute-start | bytes 1916936 | tf_op jit(solution)/shard_map/ppermute | solution.py:586
  28.0 3.7 %collective-permute-start.12 = (f32[16,256]{1,0:T(8,128)S(1)}, f32[16,256]{1,0:T(8,128)S(1)}, u32[]{:S(2)}, u32[]{:S(2)}) collective-permute-start(f32[16,256]{1,0:T(8,128)S(1)} %pad_maximum_fusion.1), channel_id=1, source_target_pairs={{0,8},{8,0},{1,9},{9,1},{2,10},{10,2},{3,11},{11,3},{4,12},{12,4},... | collective-permute-start | bytes 49160 | tf_op jit(solution)/shard_map/ppermute | solution.py:581
  31.7 3.9 %collective-permute-start.13 = (f32[32,256]{1,0:T(8,128)S(1)}, f32[32,256]{1,0:T(8,128)S(1)}, u32[]{:S(2)}, u32[]{:S(2)}) collective-permute-start(f32[32,256]{1,0:T(8,128)S(1)} %pad_maximum_fusion), channel_id=1, source_target_pairs={{0,16},{16,0},{1,17},{17,1},{2,18},{18,2},{3,19},{19,3},{4,20},{20... | collective-permute-start | bytes 98312 | tf_op jit(solution)/shard_map/ppermute | solution.py:581
  35.7 25.8 %collective-permute-start.14 = (bf16[2,832,128]{2,1,0:T(8,128)(2,1)S(1)}, bf16[2,832,128]{2,1,0:T(8,128)(2,1)S(1)}, u32[]{:S(2)}, u32[]{:S(2)}) collective-permute-start(bf16[2,832,128]{2,1,0:T(8,128)(2,1)S(1)} %stack.1.rest_0_), channel_id=1, source_target_pairs={{0,8},{8,0},{16,24},{24,16},{1,9},{9,1},{17,25},{25,17},{2,10},{10... | collective-permute-start | bytes 1277960 | tf_op jit(solution)/shard_map/ppermute | solution.py:601
  37.3 24.2 %collective-permute-start.15 = (bf16[2,832,128]{2,1,0:T(8,128)(2,1)S(1)}, bf16[2,832,128]{2,1,0:T(8,128)(2,1)S(1)}, u32[]{:S(2)}, u32[]{:S(2)}) collective-permute-start(bf16[2,832,128]{2,1,0:T(8,128)(2,1)S(1)} %stack.1.rest_0_), channel_id=1, source_target_pairs={{0,16},{8,24},{16,0},{24,8},{1,17},{9,25},{17,1},{25,9},{2,18},{10... | collective-permute-start | bytes 1277960 | tf_op jit(solution)/shard_map/ppermute | solution.py:601
  38.8 22.7 %collective-permute-start.16 = (bf16[2,832,128]{2,1,0:T(8,128)(2,1)S(1)}, bf16[2,832,128]{2,1,0:T(8,128)(2,1)S(1)}, u32[]{:S(2)}, u32[]{:S(2)}) collective-permute-start(bf16[2,832,128]{2,1,0:T(8,128)(2,1)S(1)} %stack.1.rest_0_), channel_id=1, source_target_pairs={{0,24},{8,16},{16,8},{24,0},{1,25},{9,17},{17,9},{25,1},{2,26},{10... | collective-permute-start | bytes 1277960 | tf_op jit(solution)/shard_map/ppermute | solution.py:601
  61.5 1.5 %collective-permute-start.21 = (bf16[832,128]{1,0:T(8,128)(2,1)S(1)}, bf16[832,128]{1,0:T(8,128)(2,1)S(1)}, u32[]{:S(2)}, u32[]{:S(2)}) collective-permute-start(bf16[832,128]{1,0:T(8,128)(2,1)S(1)} %collective-permute-done.2.rest_4_), channel_id=1, source_target_pairs={{0,4},{4,0},{1,5},{5,1},{2,6},{6,2},{3,7},{7,3},{8,12},{12,8},{9,1... | collective-permute-start | bytes 638984 | tf_op jit(solution)/shard_map/ppermute | solution.py:635
  61.6 4.8 %collective-permute-start.22 = (bf16[3,832,128]{2,1,0:T(8,128)(2,1)S(1)}, bf16[3,832,128]{2,1,0:T(8,128)(2,1)S(1)}, u32[]{:S(2)}, u32[]{:S(2)}) collective-permute-start(bf16[3,832,128]{2,1,0:T(8,128)(2,1)S(1)} %collective-permute-done.11.rest_5_), channel_id=1, source_target_pairs={{0,4},{4,0},{1,5},{5,1},{2,6},{6,2},{3,7},{7,3},{8,12},{12,8},{9,1... | collective-permute-start | bytes 1916936 | tf_op jit(solution)/shard_map/ppermute | solution.py:635
  62.1 3.0 %collective-permute-start.17 = (bf16[2,832,128]{2,1,0:T(8,128)(2,1)S(1)}, bf16[2,832,128]{2,1,0:T(8,128)(2,1)S(1)}, u32[]{:S(2)}, u32[]{:S(2)}) collective-permute-start(bf16[2,832,128]{2,1,0:T(8,128)(2,1)S(1)} %stack.1.rest_0_), channel_id=1, source_target_pairs={{0,4},{4,0},{1,5},{5,1},{2,6},{6,2},{3,7},{7,3},{8,12},{12,8},{9,1... | collective-permute-start | bytes 1277960 | tf_op jit(solution)/shard_map/ppermute | solution.py:636
  62.2 3.0 %collective-permute-start.18 = (bf16[2,832,128]{2,1,0:T(8,128)(2,1)S(1)}, bf16[2,832,128]{2,1,0:T(8,128)(2,1)S(1)}, u32[]{:S(2)}, u32[]{:S(2)}) collective-permute-start(bf16[2,832,128]{2,1,0:T(8,128)(2,1)S(1)} %collective-permute-done.14.rest_1_), channel_id=1, source_target_pairs={{0,4},{4,0},{1,5},{5,1},{2,6},{6,2},{3,7},{7,3},{8,12},{12,8},{9,1... | collective-permute-start | bytes 1277960 | tf_op jit(solution)/shard_map/ppermute | solution.py:636
  62.6 3.2 %collective-permute-start.19 = (bf16[2,832,128]{2,1,0:T(8,128)(2,1)S(1)}, bf16[2,832,128]{2,1,0:T(8,128)(2,1)S(1)}, u32[]{:S(2)}, u32[]{:S(2)}) collective-permute-start(bf16[2,832,128]{2,1,0:T(8,128)(2,1)S(1)} %collective-permute-done.15.rest_2_), channel_id=1, source_target_pairs={{0,4},{4,0},{1,5},{5,1},{2,6},{6,2},{3,7},{7,3},{8,12},{12,8},{9,1... | collective-permute-start | bytes 1277960 | tf_op jit(solution)/shard_map/ppermute | solution.py:636
  63.1 3.4 %collective-permute-start.20 = (bf16[2,832,128]{2,1,0:T(8,128)(2,1)S(1)}, bf16[2,832,128]{2,1,0:T(8,128)(2,1)S(1)}, u32[]{:S(2)}, u32[]{:S(2)}) collective-permute-start(bf16[2,832,128]{2,1,0:T(8,128)(2,1)S(1)} %collective-permute-done.16.rest_3_), channel_id=1, source_target_pairs={{0,4},{4,0},{1,5},{5,1},{2,6},{6,2},{3,7},{7,3},{8,12},{12,8},{9,1... | collective-permute-start | bytes 1277960 | tf_op jit(solution)/shard_map/ppermute | solution.py:636

commit v22 on v21

--- a/solution.py
+++ b/solution.py
@@ -335,7 +335,7 @@
     x = nn(q, wide(own_ref, feat_at, nf)) * feat_scale
     e = jnp.where(causal, jnp.exp(jnp.minimum(cum_c - own_cum, 0.0)), 0.0) * rden_c
     dx = (dp - dl_c) * e * (1.0 + x)
-    dqt = nt(wide(own_ref, feat_at, nf), dx.astype(bf16))
+    dq_f = nt(dx.astype(bf16), wide(own_ref, feat_at, nf))
 
     s = nt(wk, wq) * scale
     causal = at_row <= at_col
@@ -345,11 +345,11 @@
     x = nn(k, wide(query_ref, feat_at, nf)) * feat_scale
     e = jnp.where(causal, jnp.exp(jnp.minimum(own_cum - cum_c, 0.0)), 0.0) * mine_ref[2:3, :]
     dx = (dp - mine_ref[3:4, :]) * e * (1.0 + x)
-    dkt = nt(wide(query_ref, feat_at, nf), dx.astype(bf16))
+    dk_f = nt(dx.astype(bf16), wide(query_ref, feat_at, nf))
     dv = nn((p + (1.0 + x + 0.5 * x * x) * e).astype(bf16), do)
 
     def step(d, carry):
-        dwq, dqt, dwk, dkt, dv = carry
+        dwq, dq_f, dwk, dk_f, dv = carry
         j = partner(me, d, count)
         view = recv(d)
         mine = j < me
@@ -378,19 +378,20 @@
         x = nn(rows_f, other_f) * feat_scale
         e = e_r * e_c
         dx = (dp - pick(mine, dl_c, 0.0) - pick(mine, zero, st[3:4, :])) * e * (1.0 + x)
-        more_f = nt(other_f, dx.astype(bf16))
+        more_f = nt(dx.astype(bf16), other_f)
         more_v = nn((p + (1.0 + x + 0.5 * x * x) * e).astype(bf16), other_v)
         dwq = dwq + pick(mine, more_w, 0.0)
         dwk = dwk + pick(mine, 0.0, more_w)
-        dqt = dqt + pick(mine, more_f, 0.0)
-        dkt = dkt + pick(mine, 0.0, more_f)
+        dq_f = dq_f + pick(mine, more_f, 0.0)
+        dk_f = dk_f + pick(mine, 0.0, more_f)
         dv = dv + pick(mine, 0.0, more_v)
-        return dwq, dqt, dwk, dkt, dv
-
-    dwq, dqt, dwk, dkt, dv = over_partners(count, step, (dwq, dqt, dwk, dkt, dv))
+        return dwq, dq_f, dwk, dk_f, dv
+
+    dwq, dq_f, dwk, dk_f, dv = over_partners(count, step, (dwq, dq_f, dwk, dk_f, dv))
     dwq, dwk = (dwq * scale).astype(bf16), (dwk * scale).astype(bf16)
     dv = dv.astype(bf16)
-    dft = (jnp.concatenate([dqt, dkt], axis=0) * feat_scale).astype(bf16)
+    padded = jnp.concatenate([dq_f, dk_f, jnp.zeros((rows, LANES - 2 * nf), f32)], axis=1)
+    dft = (jnp.transpose(padded)[: 2 * nf] * feat_scale).astype(bf16)
     (grad_ref,) = rest
     grad_ref[0:rows, :] = dwq
     grad_ref[rows : 2 * rows, :] = dwk
@@ -416,25 +417,49 @@
     gather_rows(grad_ref, order, cat_ref, feat_ref)
 
 
-def columns_kernel(ctx, distances, cat_ref, feat_ref, ww_ref, vw_ref, fw_ref, *rest):
-    pieces, firsts = rest[: len(distances)], rest[len(distances) : len(distances) + 2]
-    out_ref, tile_ref, sems = rest[-3:]
+def column_sums(ctx, e, cat_ref, feat_ref, ww_ref, vw_ref, fw_ref, piece_ref, firsts):
     nf2 = fw_ref.shape[0]
     heads = feat_ref.shape[1] // nf2
     tile = 2 * LANES
-    me = block_index(ctx)
+    part = pl.ds(pl.multiple_of(jnp.bitwise_xor(block_index(ctx), e) * tile, tile), tile)
+    views = [firsts[1].at[e // 2 - 1] if e > 1 else firsts[0]]
+    views += [piece_ref.at[t] for t in range(heads - 2)]
+    main = [ww_ref[part, :], vw_ref[part, :]]
+    main += [v[m * tile : (m + 1) * tile, :] for v in views for m in range(3)]
+    feats = [fw_ref[:, part]] + [wide(v, 3 * tile, nf2) for v in views]
+    total = nt(cat_ref[...], jnp.concatenate(main, axis=1))
+    total += nn(feat_ref[...], jnp.concatenate(feats, axis=0))
+    return total.astype(bf16), part
+
+
+def columns_kernel(ctx, distances, *rest):
+    operands, rest = rest[:5], rest[5:]
+    pieces, firsts = rest[: len(distances)], rest[len(distances) : len(distances) + 2]
+    out_ref, tile_ref, sems = rest[-3:]
     copies = []
     for n, (e, ref) in enumerate(zip(distances, pieces)):
-        part = pl.ds(pl.multiple_of(jnp.bitwise_xor(me, e) * tile, tile), tile)
-        views = [firsts[1].at[e // 2 - 1] if e > 1 else firsts[0]]
-        views += [ref.at[t] for t in range(heads - 2)]
-        main = [ww_ref[part, :], vw_ref[part, :]]
-        main += [v[m * tile : (m + 1) * tile, :] for v in views for m in range(3)]
-        feats = [fw_ref[:, part]] + [wide(v, 3 * tile, nf2) for v in views]
-        total = nt(cat_ref[...], jnp.concatenate(main, axis=1))
-        total += nn(feat_ref[...], jnp.concatenate(feats, axis=0))
-        tile_ref[n] = total.astype(bf16)
+        tile_ref[n], part = column_sums(ctx, e, *operands, ref, firsts)
         copies.append(pltpu.make_async_copy(tile_ref.at[n], out_ref.at[:, part], sems.at[n]))
+        copies[-1].start()
+    for copy in copies:
+        copy.wait()
+
+
+def passed_kernel(ctx, distances, *rest):
+    operands, rest = rest[:5], rest[5:]
+    pieces, firsts = rest[: len(distances)], rest[len(distances) : len(distances) + 2]
+    for n, (e, ref) in enumerate(zip(distances, pieces)):
+        rest[-1][n], _ = column_sums(ctx, e, *operands, ref, firsts)
+
+
+def lay_kernel(ctx, tiles_ref, before_hbm, out_ref, sems):
+    del before_hbm
+    count, _, tile = tiles_ref.shape
+    copies = []
+    for d in range(count):
+        at = jnp.bitwise_xor(block_index(ctx), 2 * d + 1) * tile
+        part = pl.ds(pl.multiple_of(at, tile), tile)
+        copies.append(pltpu.make_async_copy(tiles_ref.at[d], out_ref.at[:, part], sems.at[d]))
         copies[-1].start()
     for copy in copies:
         copy.wait()
@@ -619,27 +644,29 @@
 
     first[1], grads = lax.optimization_barrier((first[1], grads))
     grads = lax.all_gather(grads, "tp")
-    cat, feats = pl.pallas_call(
-        cat_kernel,
-        out_shape=[
-            jax.ShapeDtypeStruct((rows, 3 * LANES * heads), bf16),
-            jax.ShapeDtypeStruct((rows, nf2 * heads), bf16),
-        ],
-        in_specs=[VMEM],
-        out_specs=[VMEM] * 2,
-        compiler_params=params,
-        cost_estimate=cost(1, 1024),
-        name="cat",
-    )(grads)
-    pieces, first, _ = lax.optimization_barrier((pieces, first, cat))
-    other_first = [lax.ppermute(p, "core", swap) for p in first]
-    swapped = [lax.ppermute(p, "core", swap) for p in pieces]
-
-    total = []
-    for distances in ((0, 2, 4, 6), (1, 3, 5, 7)):
-        parts = [(swapped if e % 2 else pieces)[e // 2] for e in distances]
-        args = [cat, feats, ww, vw, fw, *parts, *(other_first if total else first), *total]
-        total = [
+    pieces, first, grads = lax.optimization_barrier((pieces, first, grads))
+    sibling_grads = lax.ppermute(grads, "core", swap)
+
+    def operands_of(grads):
+        return pl.pallas_call(
+            cat_kernel,
+            out_shape=[
+                jax.ShapeDtypeStruct((rows, 3 * LANES * heads), bf16),
+                jax.ShapeDtypeStruct((rows, nf2 * heads), bf16),
+            ],
+            in_specs=[VMEM],
+            out_specs=[VMEM] * 2,
+            compiler_params=params,
+            cost_estimate=cost(1, 1024),
+            name="cat",
+        )(grads)
+
+    mine = operands_of(grads)
+
+    def columns_of(distances, total):
+        parts = [pieces[e // 2] for e in distances]
+        args = [*mine, ww, vw, fw, *parts, *first, *total]
+        return [
             pl.pallas_call(
                 partial(columns_kernel, ctx, distances),
                 out_shape=jax.ShapeDtypeStruct((rows, dim), bf16),
@@ -655,7 +682,33 @@
                 name="columns",
             )(*args)
         ]
-    return (attended, total[0])
+
+    total = columns_of((0, 2), [])
+    sibling_grads, total = lax.optimization_barrier((sibling_grads, total))
+    passed = pl.pallas_call(
+        partial(passed_kernel, ctx, (0, 2, 4, 6)),
+        out_shape=jax.ShapeDtypeStruct((chips, rows, tile), bf16),
+        in_specs=[VMEM] * (7 + chips),
+        out_specs=VMEM,
+        compiler_params=params,
+        cost_estimate=cost(1, 1024),
+        name="passed",
+    )(*operands_of(sibling_grads), ww, vw, fw, *pieces, *first)
+    passed, total = lax.optimization_barrier((passed, total))
+    received = lax.ppermute(passed, "core", swap)
+    total = columns_of((4, 6), total)
+    total = pl.pallas_call(
+        partial(lay_kernel, ctx),
+        out_shape=jax.ShapeDtypeStruct((rows, dim), bf16),
+        in_specs=[VMEM, ANY],
+        out_specs=ANY,
+        scratch_shapes=[pltpu.SemaphoreType.DMA((chips,))],
+        input_output_aliases={1: 0},
+        compiler_params=params,
+        cost_estimate=cost(1, 1024),
+        name="lay",
+    )(received, *total)
+    return (attended, total)
 
 
 def solution(mesh):

time: 68.4 us -> 70.5 us (1.031)
  blocking collectives: 18.4 us -> 21 us
  Pallas kernels: 13.1 us -> 14.1 us
  starting transfers between devices: 18.7 us -> 17.7 us
    all_gather x1, blocking collectives: 18.4 us -> 21 us  [per_device(): grads = lax.all_gather(grads, 'tp')]
    pallas_call x3 -> x6, Pallas kernels: 3.92 us -> 5.1 us  [the longest x2 2.73 us: columns_of(): pl.pallas_call(partial(columns_kernel, ctx, distances), out_shape=jax.Sha...]
    ppermute x6 -> x2, starting transfers between devices: 1.29 us -> 0.27 us  [the longest x1 0.2 us: per_device(): received = lax.ppermute(passed, 'core', swap)]
    ppermute x6 -> x2, waiting for transfers between devices: 1.71 us -> 1.18 us  [the longest x1 0.77 us: per_device(): sibling_grads = lax.ppermute(grads, 'core', swap)]
  transfers between devices with their start and end apart: 23 -> 19, of which waited for: 12 -> 10; matrix products, arithmetic and copies ran while one was open for 0% -> 0% of each run, Pallas kernels for 12% -> 13%
where the time goes in v22:
time: 70.5 us; the launch traced here: 70.3 us
  blocking collectives  21 us (30%)
  starting transfers between devices  17.7 us (25%)
  waiting for transfers between devices  16.7 us (24%)
  Pallas kernels  14.1 us (20%)
  between operations  0.71 us (1%)
    all_gather x1, blocking collectives, per_device(): grads = lax.all_gather(grads, 'tp')  21 us
    ppermute x3, waiting for transfers between devices, per_device(): stats.append(lax.ppermute(held, name, swap))  6.06 us
    ppermute x3, waiting for transfers between devices, per_device(): lax.ppermute(sends[d], ctx[:-1], [(i, i ^ d) for i in range(chips)])  4.2 us
    ppermute x1, starting transfers between devices, per_device(): across = lax.ppermute(outs[0], 'tp', [(z, z ^ 2) for z in range(heads)])  4.1 us
    ppermute x3, starting transfers between devices, per_device(): lax.ppermute(pieces[0], ctx[:-1], [(i, i ^ d) for i in range(chips)])  3.55 us
    pallas_call x1, Pallas kernels, per_device(): pl.pallas_call(lambda *refs: gradient_kernel(ctx, count, len(recv), len(s...  3.5 us
    ppermute x3, starting transfers between devices, per_device(): lax.ppermute(sends[d], ctx[:-1], [(i, i ^ d) for i in range(chips)])  3.49 us
    pallas_call x1, Pallas kernels, per_device(): pl.pallas_call(partial(project_kernel, ctx, len(packs)), out_shape=packs...  3.13 us
  transfers between devices with their start and end apart: 19, of which 10 were waited for; matrix products, arithmetic and copies ran while one was open for 0% of the time, Pallas kernels for 13%

profile of v22, /device:TPU:0, one launch (start us, length us, event | category | flops | bytes accessed | tf_op | source)
XLA Modules:
  0.0 70.3 jit_solution(6955156692815469782)
XLA Ops:
  0.6 3.1 %project.1 = (bf16[832,128]{1,0:T(8,128)(2,1)S(1)}, bf16[3,832,128]{2,1,0:T(8,128)(2,1)S(1)}, bf16[560,128]{1,0:T(8,128)(2,1)S(1)}, bf16[560,128]{1,0:T(8,128)(2...) custom-call(bf16[256,2048]{1,0:T(8,128)(2,1)} %tok_hbm.1, ...), custom_call_target="tpu_custom_call" | custom-call | flops 1 | bytes 1024 | tf_op jit(solution)/shard_map/project/pallas_call | solution.py:537
  3.8 4.1 %collective-permute-start = (bf16[832,128]{1,0:T(8,128)(2,1)S(1)}, bf16[832,128]{1,0:T(8,128)(2,1)S(1)}, u32[]{:S(2)}, u32[]{:S(2)}) collective-permute-start(bf16[832,128]{1,0:T(8,128)(2,1)S(1)} %get-tuple-element.59), channel_id=1, source_target_pairs={{0,2},{1,3},{2,0},{3,1},{4,6},{5,7},{6,4},{7,5},{8,10},{9,11},{10,... | collective-permute-start | bytes 638984 | tf_op jit(solution)/shard_map/ppermute | solution.py:569
  7.9 2.4 %collective-permute-start.1 = (bf16[560,128]{1,0:T(8,128)(2,1)S(1)}, bf16[560,128]{1,0:T(8,128)(2,1)S(1)}, u32[]{:S(2)}, u32[]{:S(2)}) collective-permute-start(bf16[560,128]{1,0:T(8,128)(2,1)S(1)} %get-tuple-element.60), channel_id=1, source_target_pairs={{0,24},{8,16},{16,8},{24,0},{1,25},{9,17},{17,9},{25,1},{2,26},{10... | collective-permute-start | bytes 430088 | tf_op jit(solution)/shard_map/ppermute | solution.py:566
  10.3 0.5 collective-permute-start.4
  10.9 0.5 collective-permute-start.6
  11.4 1.6 %collective-permute-start.2 = (bf16[832,128]{1,0:T(8,128)(2,1)S(1)}, bf16[832,128]{1,0:T(8,128)(2,1)S(1)}, u32[]{:S(2)}, u32[]{:S(2)}) collective-permute-start(bf16[832,128]{1,0:T(8,128)(2,1)S(1)} %get-tuple-element.59), channel_id=1, source_target_pairs={{0,1},{1,0},{2,3},{3,2},{4,5},{5,4},{6,7},{7,6},{8,9},{9,8},{10,11... | collective-permute-start | bytes 638984 | tf_op jit(solution)/shard_map/ppermute | solution.py:579
  12.9 2.5 %collective-permute-done.1.refs_5_ = bf16[560,128]{1,0:T(8,128)(2,1)S(1)} collective-permute-done((bf16[560,128]{1,0:T(8,128)(2,1)S(1)}, bf16[560,128]{1,0:T(8,128)(2,1)S(1)}, u32[]{:S(2)}, u32[]{:S(2)}) %collective-permute-start.1) | collective-permute-done | bytes 143392 | tf_op jit(solution)/shard_map/ppermute | solution.py:566
  15.5 0.0 collective-permute-start.3
  15.5 1.7 %collective-permute-done.4.refs_1_ = bf16[560,128]{1,0:T(8,128)(2,1)S(1)} collective-permute-done((bf16[560,128]{1,0:T(8,128)(2,1)S(1)}, bf16[560,128]{1,0:T(8,128)(2,1)S(1)}, u32[]{:S(2)}, u32[]{:S(2)}) %collective-permute-start.4) | collective-permute-done | bytes 143392 | tf_op jit(solution)/shard_map/ppermute | solution.py:566
  17.1 0.0 collective-permute-start.5
  17.1 0.0 collective-permute-done.6.refs_3_
  17.1 0.5 collective-permute-start.7
  17.7 0.2 collective-permute-done.refs_0_
  17.8 0.0 collective-permute-start.8
  17.8 0.0 collective-permute-done.3.refs_0_
  17.8 2.8 %collective-permute-done.2.rest_7_.rest_9_ = bf16[832,128]{1,0:T(8,128)(2,1)S(1)} collective-permute-done((bf16[832,128]{1,0:T(8,128)(2,1)S(1)}, bf16[832,128]{1,0:T(8,128)(2,1)S(1)}, u32[]{:S(2)}, u32[]{:S(2)}) %collective-permute-start.2) | collective-permute-done | bytes 213024 | tf_op jit(solution)/shard_map/ppermute | solution.py:579
  20.6 0.0 collective-permute-done.5.refs_2_
  20.6 0.0 collective-permute-done.7.refs_4_
  20.7 0.0 collective-permute-done.8.refs_6_
  20.7 0.1 collective-permute-start.9
  20.7 2.4 %query_side.1 = (bf16[256,128]{1,0:T(8,128)(2,1)}, f32[8,256]{1,0:T(8,128)S(1)}, f32[256,128]{1,0:T(8,128)S(1)}) custom-call(bf16[560,128]{1,0:T(8,128)(2,1)S(1)} %collective-permute-done.3.refs_0_, bf16[560,128]{1,0:T(8,128)(2,1)S(1)} %collective-permute-done.4.refs_1_, bf16[560,128]{1,0:T(8,128)(2,1)S(1)} %collective-permute-done.5.refs_2_, ...), custom_call_target="tpu_custom_call" | custom-call | flops 1 | bytes 1024 | tf_op jit(solution)/shard_map/query_side/pallas_call | solution.py:583
  23.1 0.0 collective-permute-start.10
  23.1 1.2 %collective-permute-done.10.refs_8_ = f32[8,256]{1,0:T(8,128)S(1)} collective-permute-done((f32[8,256]{1,0:T(8,128)S(1)}, f32[8,256]{1,0:T(8,128)S(1)}, u32[]{:S(2)}, u32[]{:S(2)}) %collective-permute-start.10) | collective-permute-done | bytes 8224 | tf_op jit(solution)/shard_map/ppermute | solution.py:606
  24.3 2.3 %collective-permute-done.9.refs_1_ = bf16[832,128]{1,0:T(8,128)(2,1)S(1)} collective-permute-done((bf16[832,128]{1,0:T(8,128)(2,1)S(1)}, bf16[832,128]{1,0:T(8,128)(2,1)S(1)}, u32[]{:S(2)}, u32[]{:S(2)}) %collective-permute-start.9) | collective-permute-done | bytes 213024 | tf_op jit(solution)/shard_map/ppermute | solution.py:581
  26.6 1.4 %collective-permute-start.16 = (bf16[3,832,128]{2,1,0:T(8,128)(2,1)S(1)}, bf16[3,832,128]{2,1,0:T(8,128)(2,1)S(1)}, u32[]{:S(2)}, u32[]{:S(2)}) collective-permute-start(bf16[3,832,128]{2,1,0:T(8,128)(2,1)S(1)} %get-tuple-element.90), channel_id=1, source_target_pairs={{0,1},{1,0},{2,3},{3,2},{4,5},{5,4},{6,7},{7,6},{8,9},{9,8},{10,11... | collective-permute-start | bytes 1916936 | tf_op jit(solution)/shard_map/ppermute | solution.py:611
  28.0 1.5 %collective-permute-start.11 = (f32[16,256]{1,0:T(8,128)S(1)}, f32[16,256]{1,0:T(8,128)S(1)}, u32[]{:S(2)}, u32[]{:S(2)}) collective-permute-start(f32[16,256]{1,0:T(8,128)S(1)} %pad_maximum_fusion.1), channel_id=1, source_target_pairs={{0,8},{8,0},{1,9},{9,1},{2,10},{10,2},{3,11},{11,3},{4,12},{12,4},... | collective-permute-start | bytes 49160 | tf_op jit(solution)/shard_map/ppermute | solution.py:606
  29.5 2.2 %collective-permute-done.11.refs_9_ = f32[16,256]{1,0:T(8,128)S(1)} collective-permute-done((f32[16,256]{1,0:T(8,128)S(1)}, f32[16,256]{1,0:T(8,128)S(1)}, u32[]{:S(2)}, u32[]{:S(2)}) %collective-permute-start.11) | collective-permute-done | bytes 16416 | tf_op jit(solution)/shard_map/ppermute | solution.py:606
  31.7 1.3 %collective-permute-start.12 = (f32[32,256]{1,0:T(8,128)S(1)}, f32[32,256]{1,0:T(8,128)S(1)}, u32[]{:S(2)}, u32[]{:S(2)}) collective-permute-start(f32[32,256]{1,0:T(8,128)S(1)} %pad_maximum_fusion), channel_id=1, source_target_pairs={{0,16},{16,0},{1,17},{17,1},{2,18},{18,2},{3,19},{19,3},{4,20},{20... | collective-permute-start | bytes 98312 | tf_op jit(solution)/shard_map/ppermute | solution.py:606
  33.0 2.7 %collective-permute-done.12.refs_10_ = f32[32,256]{1,0:T(8,128)S(1)} collective-permute-done((f32[32,256]{1,0:T(8,128)S(1)}, f32[32,256]{1,0:T(8,128)S(1)}, u32[]{:S(2)}, u32[]{:S(2)}) %collective-permute-start.12) | collective-permute-done | bytes 32800 | tf_op jit(solution)/shard_map/ppermute | solution.py:606
  35.7 2.3 %collective-permute-start.15 = (bf16[2,832,128]{2,1,0:T(8,128)(2,1)S(1)}, bf16[2,832,128]{2,1,0:T(8,128)(2,1)S(1)}, u32[]{:S(2)}, u32[]{:S(2)}) collective-permute-start(bf16[2,832,128]{2,1,0:T(8,128)(2,1)S(1)} %stack.1.rest_5_), channel_id=1, source_target_pairs={{0,24},{8,16},{16,8},{24,0},{1,25},{9,17},{17,9},{25,1},{2,26},{10... | collective-permute-start | bytes 1277960 | tf_op jit(solution)/shard_map/ppermute | solution.py:626
  37.9 0.8 %collective-permute-start.14 = (bf16[2,832,128]{2,1,0:T(8,128)(2,1)S(1)}, bf16[2,832,128]{2,1,0:T(8,128)(2,1)S(1)}, u32[]{:S(2)}, u32[]{:S(2)}) collective-permute-start(bf16[2,832,128]{2,1,0:T(8,128)(2,1)S(1)} %stack.1.rest_5_), channel_id=1, source_target_pairs={{0,16},{8,24},{16,0},{24,8},{1,17},{9,25},{17,1},{25,9},{2,18},{10... | collective-permute-start | bytes 1277960 | tf_op jit(solution)/shard_map/ppermute | solution.py:626
  38.7 0.5 collective-permute-start.13
  39.2 3.5 %gradients.1 = bf16[832,128]{1,0:T(8,128)(2,1)S(1)} custom-call(bf16[560,128]{1,0:T(8,128)(2,1)S(1)} %collective-permute-done.3.refs_0_, bf16[560,128]{1,0:T(8,128)(2,1)S(1)} %collective-permute-done.4.refs_1_, bf16[560,128]{1,0:T(8,128)(2,1)S(1)} %collective-permute-done.5.refs_2_, bf16[560,128]{1,0:T(8,128)(2,1)S(1)} %collective-permute-done.6.refs_3_, ...), custom_call_target="tpu_custom_call" | custom-call | flops 1 | bytes 1024 | tf_op jit(solution)/shard_map/gradients/pallas_call | solution.py:630
  42.7 0.0 collective-permute-done.16.rest_8_.rest_10_
  42.7 21.0 %all-gather = bf16[3328,128]{1,0:T(8,128)(2,1)S(1)} all-gather(bf16[832,128]{1,0:T(8,128)(2,1)S(1)} %gradients.1), channel_id=2, replica_groups=mesh['half0'=2,'half1'=2,'core'=2,'tp'=4] {'tp'}, dimensions={0}, use_global_device_ids=true | all-gather | bytes 1064960 | tf_op jit(solution)/shard_map/all_gather | solution.py:646
  63.7 0.0 collective-permute-done.15.rest_8_.rest_6_
  63.7 0.0 collective-permute-done.14.rest_7_.rest_5_
  63.8 0.0 collective-permute-done.13.rest_6_
  63.8 0.1 collective-permute-start.17
  63.8 0.2 cat.2
  64.1 1.4 %columns.2.rest_9_ = bf16[256,2048]{1,0:T(8,128)(2,1)} custom-call(bf16[256,1536]{1,0:T(8,128)(2,1)S(1)} %get-tuple-element.99.rest_0_, bf16[256,128]{1,0:T(8,128)(2,1)S(1)} %get-tuple-element.100.rest_1_, bf16[2048,256]{1,0:T(8,128)(2,1)S(1)} %get-tuple-element.101.rest_2_, bf16[2048,128]{1,0:T(8,128)(2,1)S(1)} %get-tuple-element.102.rest_3_, ...), custom_call_target="tpu_custom_call" | custom-call | flops 1 | bytes 1024 | tf_op jit(solution)/shard_map/columns/pallas_call | solution.py:670
  65.4 0.8 %collective-permute-done.17.grad_ref = bf16[4,832,128]{2,1,0:T(8,128)(2,1)S(1)} collective-permute-done((bf16[4,832,128]{2,1,0:T(8,128)(2,1)S(1)}, bf16[4,832,128]{2,1,0:T(8,128)(2,1)S(1)}, u32[]{:S(2)}, u32[]{:S(2)}) %collective-permute-start.17) | collective-permute-done | bytes 852000 | tf_op jit(solution)/shard_map/ppermute | solution.py:648
  66.2 0.2 cat.3
  66.4 1.1 %passed.1 = bf16[4,256,256]{2,1,0:T(8,128)(2,1)S(1)} custom-call(bf16[256,1536]{1,0:T(8,128)(2,1)S(1)} %get-tuple-element.109.rest_0_, bf16[256,128]{1,0:T(8,128)(2,1)S(1)} %get-tuple-element.110.rest_1_, bf16[2048,256]{1,0:T(8,128)(2,1)S(1)} %get-tuple-element.101.rest_2_, bf16[2048,128]{1,0:T(8,128)(2,1)S(1)} %get-tuple-element.102.rest_3_, ...), custom_call_target="tpu_custom_call" | custom-call | flops 1 | bytes 1024 | tf_op jit(solution)/shard_map/passed/pallas_call | solution.py:688
  67.5 0.2 collective-permute-start.18
  67.8 1.4 %columns.3.before_hbm = bf16[256,2048]{1,0:T(8,128)(2,1)} custom-call(bf16[256,1536]{1,0:T(8,128)(2,1)S(1)} %get-tuple-element.99.rest_0_, bf16[256,128]{1,0:T(8,128)(2,1)S(1)} %get-tuple-element.100.rest_1_, bf16[2048,256]{1,0:T(8,128)(2,1)S(1)} %get-tuple-element.101.rest_2_, ...), custom_call_target="tpu_custom_call", output_to_operand_aliasing={{}: (9, {})} | custom-call | flops 1 | bytes 1024 | tf_op jit(solution)/shard_map/columns/pallas_call | solution.py:670
  69.1 0.4 collective-permute-done.18.tiles_ref
  69.5 0.8 %lay.1 = bf16[256,2048]{1,0:T(8,128)(2,1)} custom-call(bf16[4,256,256]{2,1,0:T(8,128)(2,1)S(1)} %collective-permute-done.18.tiles_ref, bf16[256,2048]{1,0:T(8,128)(2,1)} %columns.3.before_hbm), custom_call_target="tpu_custom_call", output_to_operand_aliasing={{}: (1, {})} | custom-call | flops 1 | bytes 1024 | tf_op jit(solution)/shard_map/lay/pallas_call | solution.py:700
  (3 shorter events, 0.0 us)
Async XLA Ops:
  3.8 14.0 %collective-permute-start = (bf16[832,128]{1,0:T(8,128)(2,1)S(1)}, bf16[832,128]{1,0:T(8,128)(2,1)S(1)}, u32[]{:S(2)}, u32[]{:S(2)}) collective-permute-start(bf16[832,128]{1,0:T(8,128)(2,1)S(1)} %get-tuple-element.59), channel_id=1, source_target_pairs={{0,2},{1,3},{2,0},{3,1},{4,6},{5,7},{6,4},{7,5},{8,10},{9,11},{10,... | collective-permute-start | bytes 638984 | tf_op jit(solution)/shard_map/ppermute | solution.py:569
  7.9 7.6 %collective-permute-start.1 = (bf16[560,128]{1,0:T(8,128)(2,1)S(1)}, bf16[560,128]{1,0:T(8,128)(2,1)S(1)}, u32[]{:S(2)}, u32[]{:S(2)}) collective-permute-start(bf16[560,128]{1,0:T(8,128)(2,1)S(1)} %get-tuple-element.60), channel_id=1, source_target_pairs={{0,24},{8,16},{16,8},{24,0},{1,25},{9,17},{17,9},{25,1},{2,26},{10... | collective-permute-start | bytes 430088 | tf_op jit(solution)/shard_map/ppermute | solution.py:566
  10.3 6.8 %collective-permute-start.4 = (bf16[560,128]{1,0:T(8,128)(2,1)S(1)}, bf16[560,128]{1,0:T(8,128)(2,1)S(1)}, u32[]{:S(2)}, u32[]{:S(2)}) collective-permute-start(bf16[560,128]{1,0:T(8,128)(2,1)S(1)} %get-tuple-element.63), channel_id=1, source_target_pairs={{0,8},{8,0},{16,24},{24,16},{1,9},{9,1},{17,25},{25,17},{2,10},{10... | collective-permute-start | bytes 430088 | tf_op jit(solution)/shard_map/ppermute | solution.py:566
  10.9 6.3 %collective-permute-start.6 = (bf16[560,128]{1,0:T(8,128)(2,1)S(1)}, bf16[560,128]{1,0:T(8,128)(2,1)S(1)}, u32[]{:S(2)}, u32[]{:S(2)}) collective-permute-start(bf16[560,128]{1,0:T(8,128)(2,1)S(1)} %get-tuple-element.64), channel_id=1, source_target_pairs={{0,16},{8,24},{16,0},{24,8},{1,17},{9,25},{17,1},{25,9},{2,18},{10... | collective-permute-start | bytes 430088 | tf_op jit(solution)/shard_map/ppermute | solution.py:566
  11.4 9.3 %collective-permute-start.2 = (bf16[832,128]{1,0:T(8,128)(2,1)S(1)}, bf16[832,128]{1,0:T(8,128)(2,1)S(1)}, u32[]{:S(2)}, u32[]{:S(2)}) collective-permute-start(bf16[832,128]{1,0:T(8,128)(2,1)S(1)} %get-tuple-element.59), channel_id=1, source_target_pairs={{0,1},{1,0},{2,3},{3,2},{4,5},{5,4},{6,7},{7,6},{8,9},{9,8},{10,11... | collective-permute-start | bytes 638984 | tf_op jit(solution)/shard_map/ppermute | solution.py:579
  15.5 2.4 %collective-permute-start.3 = (bf16[560,128]{1,0:T(8,128)(2,1)S(1)}, bf16[560,128]{1,0:T(8,128)(2,1)S(1)}, u32[]{:S(2)}, u32[]{:S(2)}) collective-permute-start(bf16[560,128]{1,0:T(8,128)(2,1)S(1)} %get-tuple-element.62), channel_id=1, source_target_pairs={{0,4},{4,0},{1,5},{5,1},{2,6},{6,2},{3,7},{7,3},{8,12},{12,8},{9,1... | collective-permute-start | bytes 430088 | tf_op jit(solution)/shard_map/ppermute | solution.py:567
  17.1 3.5 %collective-permute-start.5 = (bf16[560,128]{1,0:T(8,128)(2,1)S(1)}, bf16[560,128]{1,0:T(8,128)(2,1)S(1)}, u32[]{:S(2)}, u32[]{:S(2)}) collective-permute-start(bf16[560,128]{1,0:T(8,128)(2,1)S(1)} %collective-permute-done.4.refs_1_), channel_id=1, source_target_pairs={{0,4},{4,0},{1,5},{5,1},{2,6},{6,2},{3,7},{7,3},{8,12},{12,8},{9,1... | collective-permute-start | bytes 430088 | tf_op jit(solution)/shard_map/ppermute | solution.py:573
  17.1 3.5 %collective-permute-start.7 = (bf16[560,128]{1,0:T(8,128)(2,1)S(1)}, bf16[560,128]{1,0:T(8,128)(2,1)S(1)}, u32[]{:S(2)}, u32[]{:S(2)}) collective-permute-start(bf16[560,128]{1,0:T(8,128)(2,1)S(1)} %collective-permute-done.6.refs_3_), channel_id=1, source_target_pairs={{0,4},{4,0},{1,5},{5,1},{2,6},{6,2},{3,7},{7,3},{8,12},{12,8},{9,1... | collective-permute-start | bytes 430088 | tf_op jit(solution)/shard_map/ppermute | solution.py:573
  17.8 2.8 %collective-permute-start.8 = (bf16[560,128]{1,0:T(8,128)(2,1)S(1)}, bf16[560,128]{1,0:T(8,128)(2,1)S(1)}, u32[]{:S(2)}, u32[]{:S(2)}) collective-permute-start(bf16[560,128]{1,0:T(8,128)(2,1)S(1)} %collective-permute-done.1.refs_5_), channel_id=1, source_target_pairs={{0,4},{4,0},{1,5},{5,1},{2,6},{6,2},{3,7},{7,3},{8,12},{12,8},{9,1... | collective-permute-start | bytes 430088 | tf_op jit(solution)/shard_map/ppermute | solution.py:573
  20.7 5.9 %collective-permute-start.9 = (bf16[832,128]{1,0:T(8,128)(2,1)S(1)}, bf16[832,128]{1,0:T(8,128)(2,1)S(1)}, u32[]{:S(2)}, u32[]{:S(2)}) collective-permute-start(bf16[832,128]{1,0:T(8,128)(2,1)S(1)} %collective-permute-done.refs_0_), channel_id=1, source_target_pairs={{0,1},{1,0},{2,3},{3,2},{4,5},{5,4},{6,7},{7,6},{8,9},{9,8},{10,11... | collective-permute-start | bytes 638984 | tf_op jit(solution)/shard_map/ppermute | solution.py:581
  23.1 1.2 %collective-permute-start.10 = (f32[8,256]{1,0:T(8,128)S(1)}, f32[8,256]{1,0:T(8,128)S(1)}, u32[]{:S(2)}, u32[]{:S(2)}) collective-permute-start(f32[8,256]{1,0:T(8,128)S(1)} %get-tuple-element.91.refs_7_), channel_id=1, source_target_pairs={{0,4},{4,0},{1,5},{5,1},{2,6},{6,2},{3,7},{7,3},{8,12},{12,8},{9,1... | collective-permute-start | bytes 24584 | tf_op jit(solution)/shard_map/ppermute | solution.py:606
  26.6 16.1 %collective-permute-start.16 = (bf16[3,832,128]{2,1,0:T(8,128)(2,1)S(1)}, bf16[3,832,128]{2,1,0:T(8,128)(2,1)S(1)}, u32[]{:S(2)}, u32[]{:S(2)}) collective-permute-start(bf16[3,832,128]{2,1,0:T(8,128)(2,1)S(1)} %get-tuple-element.90), channel_id=1, source_target_pairs={{0,1},{1,0},{2,3},{3,2},{4,5},{5,4},{6,7},{7,6},{8,9},{9,8},{10,11... | collective-permute-start | bytes 1916936 | tf_op jit(solution)/shard_map/ppermute | solution.py:611
  28.0 3.7 %collective-permute-start.11 = (f32[16,256]{1,0:T(8,128)S(1)}, f32[16,256]{1,0:T(8,128)S(1)}, u32[]{:S(2)}, u32[]{:S(2)}) collective-permute-start(f32[16,256]{1,0:T(8,128)S(1)} %pad_maximum_fusion.1), channel_id=1, source_target_pairs={{0,8},{8,0},{1,9},{9,1},{2,10},{10,2},{3,11},{11,3},{4,12},{12,4},... | collective-permute-start | bytes 49160 | tf_op jit(solution)/shard_map/ppermute | solution.py:606
  31.7 3.9 %collective-permute-start.12 = (f32[32,256]{1,0:T(8,128)S(1)}, f32[32,256]{1,0:T(8,128)S(1)}, u32[]{:S(2)}, u32[]{:S(2)}) collective-permute-start(f32[32,256]{1,0:T(8,128)S(1)} %pad_maximum_fusion), channel_id=1, source_target_pairs={{0,16},{16,0},{1,17},{17,1},{2,18},{18,2},{3,19},{19,3},{4,20},{20... | collective-permute-start | bytes 98312 | tf_op jit(solution)/shard_map/ppermute | solution.py:606
  35.7 28.1 %collective-permute-start.15 = (bf16[2,832,128]{2,1,0:T(8,128)(2,1)S(1)}, bf16[2,832,128]{2,1,0:T(8,128)(2,1)S(1)}, u32[]{:S(2)}, u32[]{:S(2)}) collective-permute-start(bf16[2,832,128]{2,1,0:T(8,128)(2,1)S(1)} %stack.1.rest_5_), channel_id=1, source_target_pairs={{0,24},{8,16},{16,8},{24,0},{1,25},{9,17},{17,9},{25,1},{2,26},{10... | collective-permute-start | bytes 1277960 | tf_op jit(solution)/shard_map/ppermute | solution.py:626
  37.9 25.8 %collective-permute-start.14 = (bf16[2,832,128]{2,1,0:T(8,128)(2,1)S(1)}, bf16[2,832,128]{2,1,0:T(8,128)(2,1)S(1)}, u32[]{:S(2)}, u32[]{:S(2)}) collective-permute-start(bf16[2,832,128]{2,1,0:T(8,128)(2,1)S(1)} %stack.1.rest_5_), channel_id=1, source_target_pairs={{0,16},{8,24},{16,0},{24,8},{1,17},{9,25},{17,1},{25,9},{2,18},{10... | collective-permute-start | bytes 1277960 | tf_op jit(solution)/shard_map/ppermute | solution.py:626
  38.7 25.1 %collective-permute-start.13 = (bf16[2,832,128]{2,1,0:T(8,128)(2,1)S(1)}, bf16[2,832,128]{2,1,0:T(8,128)(2,1)S(1)}, u32[]{:S(2)}, u32[]{:S(2)}) collective-permute-start(bf16[2,832,128]{2,1,0:T(8,128)(2,1)S(1)} %stack.1.rest_5_), channel_id=1, source_target_pairs={{0,8},{8,0},{16,24},{24,16},{1,9},{9,1},{17,25},{25,17},{2,10},{10... | collective-permute-start | bytes 1277960 | tf_op jit(solution)/shard_map/ppermute | solution.py:626
  63.8 2.4 %collective-permute-start.17 = (bf16[4,832,128]{2,1,0:T(8,128)(2,1)S(1)}, bf16[4,832,128]{2,1,0:T(8,128)(2,1)S(1)}, u32[]{:S(2)}, u32[]{:S(2)}) collective-permute-start(bf16[4,832,128]{2,1,0:T(8,128)(2,1)S(1)} %bitcast.3), channel_id=1, source_target_pairs={{0,4},{4,0},{1,5},{5,1},{2,6},{6,2},{3,7},{7,3},{8,12},{12,8},{9,1... | collective-permute-start | bytes 2555912 | tf_op jit(solution)/shard_map/ppermute | solution.py:648
  67.5 2.0 %collective-permute-start.18 = (bf16[4,256,256]{2,1,0:T(8,128)(2,1)S(1)}, bf16[4,256,256]{2,1,0:T(8,128)(2,1)S(1)}, u32[]{:S(2)}, u32[]{:S(2)}) collective-permute-start(bf16[4,256,256]{2,1,0:T(8,128)(2,1)S(1)} %passed.1), channel_id=1, source_target_pairs={{0,4},{4,0},{1,5},{5,1},{2,6},{6,2},{3,7},{7,3},{8,12},{12,8},{9,1... | collective-permute-start | bytes 1572872 | tf_op jit(solution)/shard_map/ppermute | solution.py:698

commit v23 on v22

--- a/solution.py
+++ b/solution.py
@@ -435,31 +435,20 @@
 def columns_kernel(ctx, distances, *rest):
     operands, rest = rest[:5], rest[5:]
     pieces, firsts = rest[: len(distances)], rest[len(distances) : len(distances) + 2]
-    out_ref, tile_ref, sems = rest[-3:]
-    copies = []
-    for n, (e, ref) in enumerate(zip(distances, pieces)):
-        tile_ref[n], part = column_sums(ctx, e, *operands, ref, firsts)
-        copies.append(pltpu.make_async_copy(tile_ref.at[n], out_ref.at[:, part], sems.at[n]))
-        copies[-1].start()
-    for copy in copies:
-        copy.wait()
-
-
-def passed_kernel(ctx, distances, *rest):
-    operands, rest = rest[:5], rest[5:]
-    pieces, firsts = rest[: len(distances)], rest[len(distances) : len(distances) + 2]
     for n, (e, ref) in enumerate(zip(distances, pieces)):
         rest[-1][n], _ = column_sums(ctx, e, *operands, ref, firsts)
 
 
-def lay_kernel(ctx, tiles_ref, before_hbm, out_ref, sems):
-    del before_hbm
-    count, _, tile = tiles_ref.shape
+def lay_kernel(ctx, *refs):
+    *tiles, received_ref, out_ref, sems = refs
+    views = [(ref.at[n], 2 * (2 * m + n)) for m, ref in enumerate(tiles) for n in range(2)]
+    views += [(received_ref.at[d], 2 * d + 1) for d in range(received_ref.shape[0])]
     copies = []
-    for d in range(count):
-        at = jnp.bitwise_xor(block_index(ctx), 2 * d + 1) * tile
+    for n, (view, e) in enumerate(views):
+        tile = view.shape[1]
+        at = jnp.bitwise_xor(block_index(ctx), e) * tile
         part = pl.ds(pl.multiple_of(at, tile), tile)
-        copies.append(pltpu.make_async_copy(tiles_ref.at[d], out_ref.at[:, part], sems.at[d]))
+        copies.append(pltpu.make_async_copy(view, out_ref.at[:, part], sems.at[n]))
         copies[-1].start()
     for copy in copies:
         copy.wait()
@@ -621,7 +610,7 @@
                 name="stack",
             )(*near)
         ]
-        for d in range(1, chips):
+        for d in (1, 2):
             pieces.append(
                 lax.ppermute(pieces[0], ctx[:-1], [(i, i ^ d) for i in range(chips)])
             )
@@ -642,6 +631,8 @@
         weights = lax.all_gather(weights, "tp")
         return (attended, merge(lax.all_gather(grads, "tp"), weights, rows, dim))
 
+    diagonal, grads = lax.optimization_barrier((pieces[0], grads))
+    pieces.append(lax.ppermute(diagonal, ctx[:-1], [(i, i ^ 3) for i in range(chips)]))
     first[1], grads = lax.optimization_barrier((first[1], grads))
     grads = lax.all_gather(grads, "tp")
     pieces, first, grads = lax.optimization_barrier((pieces, first, grads))
@@ -663,51 +654,35 @@
 
     mine = operands_of(grads)
 
-    def columns_of(distances, total):
+    def columns_of(distances, operands):
         parts = [pieces[e // 2] for e in distances]
-        args = [*mine, ww, vw, fw, *parts, *first, *total]
-        return [
-            pl.pallas_call(
-                partial(columns_kernel, ctx, distances),
-                out_shape=jax.ShapeDtypeStruct((rows, dim), bf16),
-                in_specs=[VMEM] * (7 + len(parts)) + [ANY] * len(total),
-                out_specs=ANY,
-                scratch_shapes=[
-                    pltpu.VMEM((len(parts), rows, tile), bf16),
-                    pltpu.SemaphoreType.DMA((len(parts),)),
-                ],
-                input_output_aliases={len(args) - 1: 0} if total else {},
-                compiler_params=params,
-                cost_estimate=cost(1, 1024),
-                name="columns",
-            )(*args)
-        ]
-
-    total = columns_of((0, 2), [])
-    sibling_grads, total = lax.optimization_barrier((sibling_grads, total))
-    passed = pl.pallas_call(
-        partial(passed_kernel, ctx, (0, 2, 4, 6)),
-        out_shape=jax.ShapeDtypeStruct((chips, rows, tile), bf16),
-        in_specs=[VMEM] * (7 + chips),
-        out_specs=VMEM,
-        compiler_params=params,
-        cost_estimate=cost(1, 1024),
-        name="passed",
-    )(*operands_of(sibling_grads), ww, vw, fw, *pieces, *first)
-    passed, total = lax.optimization_barrier((passed, total))
+        return pl.pallas_call(
+            partial(columns_kernel, ctx, distances),
+            out_shape=jax.ShapeDtypeStruct((len(parts), rows, tile), bf16),
+            in_specs=[VMEM] * (7 + len(parts)),
+            out_specs=VMEM,
+            compiler_params=params,
+            cost_estimate=cost(1, 1024),
+            name="columns",
+        )(*operands, ww, vw, fw, *parts, *first)
+
+    early_tiles = columns_of((0, 2), mine)
+    sibling_grads, early_tiles = lax.optimization_barrier((sibling_grads, early_tiles))
+    passed = columns_of((0, 2, 4, 6), operands_of(sibling_grads))
+    passed, mine = lax.optimization_barrier((passed, mine))
     received = lax.ppermute(passed, "core", swap)
-    total = columns_of((4, 6), total)
+    late_tiles = columns_of((4, 6), mine)
+    late_tiles, received = lax.optimization_barrier((late_tiles, received))
     total = pl.pallas_call(
         partial(lay_kernel, ctx),
         out_shape=jax.ShapeDtypeStruct((rows, dim), bf16),
-        in_specs=[VMEM, ANY],
+        in_specs=[VMEM] * 3,
         out_specs=ANY,
-        scratch_shapes=[pltpu.SemaphoreType.DMA((chips,))],
-        input_output_aliases={1: 0},
+        scratch_shapes=[pltpu.SemaphoreType.DMA((count,))],
         compiler_params=params,
         cost_estimate=cost(1, 1024),
         name="lay",
-    )(received, *total)
+    )(early_tiles, late_tiles, received)
     return (attended, total)
 
 

time: 70.5 us -> 68.2 us (0.967)
  blocking collectives: 21 us -> 18.4 us
  waiting for transfers between devices: 16.7 us -> 18.1 us
  Pallas kernels: 14.1 us -> 13 us
    all_gather x1, blocking collectives: 21 us -> 18.4 us  [per_device(): grads = lax.all_gather(grads, 'tp')]
    pallas_call x1 -> x0, Pallas kernels: 1.13 us -> none  [per_device(): pl.pallas_call(partial(passed_kernel, ctx, (0, 2, 4, 6)), out_shape=jax.S...]
    ppermute x1, waiting for transfers between devices: 0.77 us -> 1.48 us  [per_device(): sibling_grads = lax.ppermute(grads, 'core', swap)]
    ppermute x1, waiting for transfers between devices: 0.41 us -> 1.12 us  [per_device(): received = lax.ppermute(passed, 'core', swap)]
    ppermute x3 -> x2, starting transfers between devices: 3.55 us -> 3.18 us  [per_device(): lax.ppermute(pieces[0], ctx[:-1], [(i, i ^ d) for i in range(chips)])]
    pallas_call x2 -> x3, Pallas kernels: 2.73 us -> 2.43 us  [columns_of(): pl.pallas_call(partial(columns_kernel, ctx, distances), out_shape=jax.Sha...]
  transfers between devices with their start and end apart: 19 -> 19, of which waited for: 10 -> 10; matrix products, arithmetic and copies ran while one was open for 0% -> 0% of each run, Pallas kernels for 13% -> 11%
where the time goes in v23:
time: 68.2 us; the launch traced here: 68.1 us
  blocking collectives  18.4 us (27%)
  waiting for transfers between devices  18.1 us (27%)
  starting transfers between devices  17.8 us (26%)
  Pallas kernels  13 us (19%)
  between operations  0.71 us (1%)
    all_gather x1, blocking collectives, per_device(): grads = lax.all_gather(grads, 'tp')  18.4 us
    ppermute x3, waiting for transfers between devices, per_device(): stats.append(lax.ppermute(held, name, swap))  6.06 us
    ppermute x3, waiting for transfers between devices, per_device(): lax.ppermute(sends[d], ctx[:-1], [(i, i ^ d) for i in range(chips)])  4.2 us
    ppermute x1, starting transfers between devices, per_device(): across = lax.ppermute(outs[0], 'tp', [(z, z ^ 2) for z in range(heads)])  4.1 us
    pallas_call x1, Pallas kernels, per_device(): pl.pallas_call(lambda *refs: gradient_kernel(ctx, count, len(recv), len(s...  3.6 us
    ppermute x3, starting transfers between devices, per_device(): lax.ppermute(sends[d], ctx[:-1], [(i, i ^ d) for i in range(chips)])  3.49 us
    ppermute x2, starting transfers between devices, per_device(): lax.ppermute(pieces[0], ctx[:-1], [(i, i ^ d) for i in range(chips)])  3.18 us
    pallas_call x1, Pallas kernels, per_device(): pl.pallas_call(partial(project_kernel, ctx, len(packs)), out_shape=packs...  3.13 us
  transfers between devices with their start and end apart: 19, of which 10 were waited for; matrix products, arithmetic and copies ran while one was open for 0% of the time, Pallas kernels for 11%

profile of v23, /device:TPU:0, one launch (start us, length us, event | category | flops | bytes accessed | tf_op | source)
XLA Modules:
  0.0 68.1 jit_solution(9822463229413470497)
XLA Ops:
  0.6 3.1 %project.1 = (bf16[832,128]{1,0:T(8,128)(2,1)S(1)}, bf16[3,832,128]{2,1,0:T(8,128)(2,1)S(1)}, bf16[560,128]{1,0:T(8,128)(2,1)S(1)}, bf16[560,128]{1,0:T(8,128)(2...) custom-call(bf16[256,2048]{1,0:T(8,128)(2,1)} %tok_hbm.1, ...), custom_call_target="tpu_custom_call" | custom-call | flops 1 | bytes 1024 | tf_op jit(solution)/shard_map/project/pallas_call | solution.py:526
  3.8 4.1 %collective-permute-start = (bf16[832,128]{1,0:T(8,128)(2,1)S(1)}, bf16[832,128]{1,0:T(8,128)(2,1)S(1)}, u32[]{:S(2)}, u32[]{:S(2)}) collective-permute-start(bf16[832,128]{1,0:T(8,128)(2,1)S(1)} %get-tuple-element.64), channel_id=1, source_target_pairs={{0,2},{1,3},{2,0},{3,1},{4,6},{5,7},{6,4},{7,5},{8,10},{9,11},{10,... | collective-permute-start | bytes 638984 | tf_op jit(solution)/shard_map/ppermute | solution.py:558
  7.9 2.4 %collective-permute-start.1 = (bf16[560,128]{1,0:T(8,128)(2,1)S(1)}, bf16[560,128]{1,0:T(8,128)(2,1)S(1)}, u32[]{:S(2)}, u32[]{:S(2)}) collective-permute-start(bf16[560,128]{1,0:T(8,128)(2,1)S(1)} %get-tuple-element.65), channel_id=1, source_target_pairs={{0,24},{8,16},{16,8},{24,0},{1,25},{9,17},{17,9},{25,1},{2,26},{10... | collective-permute-start | bytes 430088 | tf_op jit(solution)/shard_map/ppermute | solution.py:555
  10.3 0.5 collective-permute-start.4
  10.9 0.5 collective-permute-start.6
  11.4 1.6 %collective-permute-start.2 = (bf16[832,128]{1,0:T(8,128)(2,1)S(1)}, bf16[832,128]{1,0:T(8,128)(2,1)S(1)}, u32[]{:S(2)}, u32[]{:S(2)}) collective-permute-start(bf16[832,128]{1,0:T(8,128)(2,1)S(1)} %get-tuple-element.64), channel_id=1, source_target_pairs={{0,1},{1,0},{2,3},{3,2},{4,5},{5,4},{6,7},{7,6},{8,9},{9,8},{10,11... | collective-permute-start | bytes 638984 | tf_op jit(solution)/shard_map/ppermute | solution.py:568
  12.9 2.5 %collective-permute-done.1.refs_5_ = bf16[560,128]{1,0:T(8,128)(2,1)S(1)} collective-permute-done((bf16[560,128]{1,0:T(8,128)(2,1)S(1)}, bf16[560,128]{1,0:T(8,128)(2,1)S(1)}, u32[]{:S(2)}, u32[]{:S(2)}) %collective-permute-start.1) | collective-permute-done | bytes 143392 | tf_op jit(solution)/shard_map/ppermute | solution.py:555
  15.5 0.0 collective-permute-start.3
  15.5 1.7 %collective-permute-done.4.refs_1_ = bf16[560,128]{1,0:T(8,128)(2,1)S(1)} collective-permute-done((bf16[560,128]{1,0:T(8,128)(2,1)S(1)}, bf16[560,128]{1,0:T(8,128)(2,1)S(1)}, u32[]{:S(2)}, u32[]{:S(2)}) %collective-permute-start.4) | collective-permute-done | bytes 143392 | tf_op jit(solution)/shard_map/ppermute | solution.py:555
  17.1 0.0 collective-permute-start.5
  17.1 0.0 collective-permute-done.6.refs_3_
  17.1 0.5 collective-permute-start.7
  17.7 0.2 collective-permute-done.refs_0_
  17.8 0.0 collective-permute-start.8
  17.8 0.0 collective-permute-done.3.refs_0_
  17.8 2.8 %collective-permute-done.2.rest_7_.rest_9_ = bf16[832,128]{1,0:T(8,128)(2,1)S(1)} collective-permute-done((bf16[832,128]{1,0:T(8,128)(2,1)S(1)}, bf16[832,128]{1,0:T(8,128)(2,1)S(1)}, u32[]{:S(2)}, u32[]{:S(2)}) %collective-permute-start.2) | collective-permute-done | bytes 213024 | tf_op jit(solution)/shard_map/ppermute | solution.py:568
  20.6 0.0 collective-permute-done.5.refs_2_
  20.6 0.0 collective-permute-done.7.refs_4_
  20.7 0.0 collective-permute-done.8.refs_6_
  20.7 0.1 collective-permute-start.9
  20.7 2.4 %query_side.1 = (bf16[256,128]{1,0:T(8,128)(2,1)}, f32[8,256]{1,0:T(8,128)S(1)}, f32[256,128]{1,0:T(8,128)S(1)}) custom-call(bf16[560,128]{1,0:T(8,128)(2,1)S(1)} %collective-permute-done.3.refs_0_, bf16[560,128]{1,0:T(8,128)(2,1)S(1)} %collective-permute-done.4.refs_1_, bf16[560,128]{1,0:T(8,128)(2,1)S(1)} %collective-permute-done.5.refs_2_, ...), custom_call_target="tpu_custom_call" | custom-call | flops 1 | bytes 1024 | tf_op jit(solution)/shard_map/query_side/pallas_call | solution.py:572
  23.1 0.0 collective-permute-start.10
  23.1 1.2 %collective-permute-done.10.refs_8_ = f32[8,256]{1,0:T(8,128)S(1)} collective-permute-done((f32[8,256]{1,0:T(8,128)S(1)}, f32[8,256]{1,0:T(8,128)S(1)}, u32[]{:S(2)}, u32[]{:S(2)}) %collective-permute-start.10) | collective-permute-done | bytes 8224 | tf_op jit(solution)/shard_map/ppermute | solution.py:595
  24.3 2.3 %collective-permute-done.9.refs_1_ = bf16[832,128]{1,0:T(8,128)(2,1)S(1)} collective-permute-done((bf16[832,128]{1,0:T(8,128)(2,1)S(1)}, bf16[832,128]{1,0:T(8,128)(2,1)S(1)}, u32[]{:S(2)}, u32[]{:S(2)}) %collective-permute-start.9) | collective-permute-done | bytes 213024 | tf_op jit(solution)/shard_map/ppermute | solution.py:570
  26.6 1.4 %collective-permute-start.16 = (bf16[3,832,128]{2,1,0:T(8,128)(2,1)S(1)}, bf16[3,832,128]{2,1,0:T(8,128)(2,1)S(1)}, u32[]{:S(2)}, u32[]{:S(2)}) collective-permute-start(bf16[3,832,128]{2,1,0:T(8,128)(2,1)S(1)} %get-tuple-element.101), channel_id=1, source_target_pairs={{0,1},{1,0},{2,3},{3,2},{4,5},{5,4},{6,7},{7,6},{8,9},{9,8},{10,11... | collective-permute-start | bytes 1916936 | tf_op jit(solution)/shard_map/ppermute | solution.py:600
  28.0 1.5 %collective-permute-start.11 = (f32[16,256]{1,0:T(8,128)S(1)}, f32[16,256]{1,0:T(8,128)S(1)}, u32[]{:S(2)}, u32[]{:S(2)}) collective-permute-start(f32[16,256]{1,0:T(8,128)S(1)} %pad_maximum_fusion.1), channel_id=1, source_target_pairs={{0,8},{8,0},{1,9},{9,1},{2,10},{10,2},{3,11},{11,3},{4,12},{12,4},... | collective-permute-start | bytes 49160 | tf_op jit(solution)/shard_map/ppermute | solution.py:595
  29.5 2.2 %collective-permute-done.11.refs_9_ = f32[16,256]{1,0:T(8,128)S(1)} collective-permute-done((f32[16,256]{1,0:T(8,128)S(1)}, f32[16,256]{1,0:T(8,128)S(1)}, u32[]{:S(2)}, u32[]{:S(2)}) %collective-permute-start.11) | collective-permute-done | bytes 16416 | tf_op jit(solution)/shard_map/ppermute | solution.py:595
  31.7 1.3 %collective-permute-start.12 = (f32[32,256]{1,0:T(8,128)S(1)}, f32[32,256]{1,0:T(8,128)S(1)}, u32[]{:S(2)}, u32[]{:S(2)}) collective-permute-start(f32[32,256]{1,0:T(8,128)S(1)} %pad_maximum_fusion), channel_id=1, source_target_pairs={{0,16},{16,0},{1,17},{17,1},{2,18},{18,2},{3,19},{19,3},{4,20},{20... | collective-permute-start | bytes 98312 | tf_op jit(solution)/shard_map/ppermute | solution.py:595
  33.0 2.7 %collective-permute-done.12.refs_10_ = f32[32,256]{1,0:T(8,128)S(1)} collective-permute-done((f32[32,256]{1,0:T(8,128)S(1)}, f32[32,256]{1,0:T(8,128)S(1)}, u32[]{:S(2)}, u32[]{:S(2)}) %collective-permute-start.12) | collective-permute-done | bytes 32800 | tf_op jit(solution)/shard_map/ppermute | solution.py:595
  35.7 1.7 %collective-permute-start.13 = (bf16[2,832,128]{2,1,0:T(8,128)(2,1)S(1)}, bf16[2,832,128]{2,1,0:T(8,128)(2,1)S(1)}, u32[]{:S(2)}, u32[]{:S(2)}) collective-permute-start(bf16[2,832,128]{2,1,0:T(8,128)(2,1)S(1)} %stack.1.rest_5_), channel_id=1, source_target_pairs={{0,8},{8,0},{16,24},{24,16},{1,9},{9,1},{17,25},{25,17},{2,10},{10... | collective-permute-start | bytes 1277960 | tf_op jit(solution)/shard_map/ppermute | solution.py:615
  37.3 1.5 %collective-permute-start.14 = (bf16[2,832,128]{2,1,0:T(8,128)(2,1)S(1)}, bf16[2,832,128]{2,1,0:T(8,128)(2,1)S(1)}, u32[]{:S(2)}, u32[]{:S(2)}) collective-permute-start(bf16[2,832,128]{2,1,0:T(8,128)(2,1)S(1)} %stack.1.rest_5_), channel_id=1, source_target_pairs={{0,16},{8,24},{16,0},{24,8},{1,17},{9,25},{17,1},{25,9},{2,18},{10... | collective-permute-start | bytes 1277960 | tf_op jit(solution)/shard_map/ppermute | solution.py:615
  38.8 3.6 %gradients.1 = bf16[832,128]{1,0:T(8,128)(2,1)S(1)} custom-call(bf16[560,128]{1,0:T(8,128)(2,1)S(1)} %collective-permute-done.3.refs_0_, bf16[560,128]{1,0:T(8,128)(2,1)S(1)} %collective-permute-done.4.refs_1_, bf16[560,128]{1,0:T(8,128)(2,1)S(1)} %collective-permute-done.5.refs_2_, bf16[560,128]{1,0:T(8,128)(2,1)S(1)} %collective-permute-done.6.refs_3_, ...), custom_call_target="tpu_custom_call" | custom-call | flops 1 | bytes 1024 | tf_op jit(solution)/shard_map/gradients/pallas_call | solution.py:619
  42.4 0.4 collective-permute-start.15
  42.8 0.0 collective-permute-done.16.rest_8_.rest_10_
  42.9 18.4 %all-gather = bf16[3328,128]{1,0:T(8,128)(2,1)S(1)} all-gather(bf16[832,128]{1,0:T(8,128)(2,1)S(1)} %gradients.1), channel_id=2, replica_groups=mesh['half0'=2,'half1'=2,'core'=2,'tp'=4] {'tp'}, dimensions={0}, use_global_device_ids=true | all-gather | bytes 1064960 | tf_op jit(solution)/shard_map/all_gather | solution.py:637
  61.3 0.0 collective-permute-done.13.rest_6_
  61.3 0.0 collective-permute-done.14.rest_7_.rest_5_
  61.3 0.0 collective-permute-done.15.rest_8_.rest_6_
  61.3 0.1 collective-permute-start.17
  61.4 0.2 cat.2
  61.6 0.7 columns.3.refs_0_
  62.2 1.5 %collective-permute-done.17.grad_ref = bf16[4,832,128]{2,1,0:T(8,128)(2,1)S(1)} collective-permute-done((bf16[4,832,128]{2,1,0:T(8,128)(2,1)S(1)}, bf16[4,832,128]{2,1,0:T(8,128)(2,1)S(1)}, u32[]{:S(2)}, u32[]{:S(2)}) %collective-permute-start.17) | collective-permute-done | bytes 852000 | tf_op jit(solution)/shard_map/ppermute | solution.py:639
  63.7 0.2 cat.3
  63.9 1.1 %columns.4 = bf16[4,256,256]{2,1,0:T(8,128)(2,1)S(1)} custom-call(bf16[256,1536]{1,0:T(8,128)(2,1)S(1)} %get-tuple-element.117.rest_0_, bf16[256,128]{1,0:T(8,128)(2,1)S(1)} %get-tuple-element.118.rest_1_, bf16[2048,256]{1,0:T(8,128)(2,1)S(1)} %get-tuple-element.108.rest_2_, bf16[2048,128]{1,0:T(8,128)(2,1)S(1)} %get-tuple-element.109.rest_3_, ...), custom_call_target="tpu_custom_call" | custom-call | flops 1 | bytes 1024 | tf_op jit(solution)/shard_map/columns/pallas_call | solution.py:659
  65.1 0.2 collective-permute-start.18
  65.3 0.6 columns.5.refs_1_
  65.9 1.1 %collective-permute-done.18.refs_2_ = bf16[4,256,256]{2,1,0:T(8,128)(2,1)S(1)} collective-permute-done((bf16[4,256,256]{2,1,0:T(8,128)(2,1)S(1)}, bf16[4,256,256]{2,1,0:T(8,128)(2,1)S(1)}, u32[]{:S(2)}, u32[]{:S(2)}) %collective-permute-start.18) | collective-permute-done | bytes 524320 | tf_op jit(solution)/shard_map/ppermute | solution.py:673
  67.0 1.0 %lay.1 = bf16[256,2048]{1,0:T(8,128)(2,1)} custom-call(bf16[2,256,256]{2,1,0:T(8,128)(2,1)S(1)} %columns.3.refs_0_, bf16[2,256,256]{2,1,0:T(8,128)(2,1)S(1)} %columns.5.refs_1_, bf16[4,256,256]{2,1,0:T(8,128)(2,1)S(1)} %collective-permute-done.18.refs_2_), custom_call_target="tpu_custom_call" | custom-call | flops 1 | bytes 1024 | tf_op jit(solution)/shard_map/lay/pallas_call | solution.py:676
  (3 shorter events, 0.0 us)
Async XLA Ops:
  3.8 14.0 %collective-permute-start = (bf16[832,128]{1,0:T(8,128)(2,1)S(1)}, bf16[832,128]{1,0:T(8,128)(2,1)S(1)}, u32[]{:S(2)}, u32[]{:S(2)}) collective-permute-start(bf16[832,128]{1,0:T(8,128)(2,1)S(1)} %get-tuple-element.64), channel_id=1, source_target_pairs={{0,2},{1,3},{2,0},{3,1},{4,6},{5,7},{6,4},{7,5},{8,10},{9,11},{10,... | collective-permute-start | bytes 638984 | tf_op jit(solution)/shard_map/ppermute | solution.py:558
  7.9 7.6 %collective-permute-start.1 = (bf16[560,128]{1,0:T(8,128)(2,1)S(1)}, bf16[560,128]{1,0:T(8,128)(2,1)S(1)}, u32[]{:S(2)}, u32[]{:S(2)}) collective-permute-start(bf16[560,128]{1,0:T(8,128)(2,1)S(1)} %get-tuple-element.65), channel_id=1, source_target_pairs={{0,24},{8,16},{16,8},{24,0},{1,25},{9,17},{17,9},{25,1},{2,26},{10... | collective-permute-start | bytes 430088 | tf_op jit(solution)/shard_map/ppermute | solution.py:555
  10.3 6.8 %collective-permute-start.4 = (bf16[560,128]{1,0:T(8,128)(2,1)S(1)}, bf16[560,128]{1,0:T(8,128)(2,1)S(1)}, u32[]{:S(2)}, u32[]{:S(2)}) collective-permute-start(bf16[560,128]{1,0:T(8,128)(2,1)S(1)} %get-tuple-element.68), channel_id=1, source_target_pairs={{0,8},{8,0},{16,24},{24,16},{1,9},{9,1},{17,25},{25,17},{2,10},{10... | collective-permute-start | bytes 430088 | tf_op jit(solution)/shard_map/ppermute | solution.py:555
  10.9 6.3 %collective-permute-start.6 = (bf16[560,128]{1,0:T(8,128)(2,1)S(1)}, bf16[560,128]{1,0:T(8,128)(2,1)S(1)}, u32[]{:S(2)}, u32[]{:S(2)}) collective-permute-start(bf16[560,128]{1,0:T(8,128)(2,1)S(1)} %get-tuple-element.69), channel_id=1, source_target_pairs={{0,16},{8,24},{16,0},{24,8},{1,17},{9,25},{17,1},{25,9},{2,18},{10... | collective-permute-start | bytes 430088 | tf_op jit(solution)/shard_map/ppermute | solution.py:555
  11.4 9.3 %collective-permute-start.2 = (bf16[832,128]{1,0:T(8,128)(2,1)S(1)}, bf16[832,128]{1,0:T(8,128)(2,1)S(1)}, u32[]{:S(2)}, u32[]{:S(2)}) collective-permute-start(bf16[832,128]{1,0:T(8,128)(2,1)S(1)} %get-tuple-element.64), channel_id=1, source_target_pairs={{0,1},{1,0},{2,3},{3,2},{4,5},{5,4},{6,7},{7,6},{8,9},{9,8},{10,11... | collective-permute-start | bytes 638984 | tf_op jit(solution)/shard_map/ppermute | solution.py:568
  15.5 2.4 %collective-permute-start.3 = (bf16[560,128]{1,0:T(8,128)(2,1)S(1)}, bf16[560,128]{1,0:T(8,128)(2,1)S(1)}, u32[]{:S(2)}, u32[]{:S(2)}) collective-permute-start(bf16[560,128]{1,0:T(8,128)(2,1)S(1)} %get-tuple-element.67), channel_id=1, source_target_pairs={{0,4},{4,0},{1,5},{5,1},{2,6},{6,2},{3,7},{7,3},{8,12},{12,8},{9,1... | collective-permute-start | bytes 430088 | tf_op jit(solution)/shard_map/ppermute | solution.py:556
  17.1 3.5 %collective-permute-start.5 = (bf16[560,128]{1,0:T(8,128)(2,1)S(1)}, bf16[560,128]{1,0:T(8,128)(2,1)S(1)}, u32[]{:S(2)}, u32[]{:S(2)}) collective-permute-start(bf16[560,128]{1,0:T(8,128)(2,1)S(1)} %collective-permute-done.4.refs_1_), channel_id=1, source_target_pairs={{0,4},{4,0},{1,5},{5,1},{2,6},{6,2},{3,7},{7,3},{8,12},{12,8},{9,1... | collective-permute-start | bytes 430088 | tf_op jit(solution)/shard_map/ppermute | solution.py:562
  17.1 3.5 %collective-permute-start.7 = (bf16[560,128]{1,0:T(8,128)(2,1)S(1)}, bf16[560,128]{1,0:T(8,128)(2,1)S(1)}, u32[]{:S(2)}, u32[]{:S(2)}) collective-permute-start(bf16[560,128]{1,0:T(8,128)(2,1)S(1)} %collective-permute-done.6.refs_3_), channel_id=1, source_target_pairs={{0,4},{4,0},{1,5},{5,1},{2,6},{6,2},{3,7},{7,3},{8,12},{12,8},{9,1... | collective-permute-start | bytes 430088 | tf_op jit(solution)/shard_map/ppermute | solution.py:562
  17.8 2.8 %collective-permute-start.8 = (bf16[560,128]{1,0:T(8,128)(2,1)S(1)}, bf16[560,128]{1,0:T(8,128)(2,1)S(1)}, u32[]{:S(2)}, u32[]{:S(2)}) collective-permute-start(bf16[560,128]{1,0:T(8,128)(2,1)S(1)} %collective-permute-done.1.refs_5_), channel_id=1, source_target_pairs={{0,4},{4,0},{1,5},{5,1},{2,6},{6,2},{3,7},{7,3},{8,12},{12,8},{9,1... | collective-permute-start | bytes 430088 | tf_op jit(solution)/shard_map/ppermute | solution.py:562
  20.7 5.9 %collective-permute-start.9 = (bf16[832,128]{1,0:T(8,128)(2,1)S(1)}, bf16[832,128]{1,0:T(8,128)(2,1)S(1)}, u32[]{:S(2)}, u32[]{:S(2)}) collective-permute-start(bf16[832,128]{1,0:T(8,128)(2,1)S(1)} %collective-permute-done.refs_0_), channel_id=1, source_target_pairs={{0,1},{1,0},{2,3},{3,2},{4,5},{5,4},{6,7},{7,6},{8,9},{9,8},{10,11... | collective-permute-start | bytes 638984 | tf_op jit(solution)/shard_map/ppermute | solution.py:570
  23.1 1.2 %collective-permute-start.10 = (f32[8,256]{1,0:T(8,128)S(1)}, f32[8,256]{1,0:T(8,128)S(1)}, u32[]{:S(2)}, u32[]{:S(2)}) collective-permute-start(f32[8,256]{1,0:T(8,128)S(1)} %get-tuple-element.94.refs_7_), channel_id=1, source_target_pairs={{0,4},{4,0},{1,5},{5,1},{2,6},{6,2},{3,7},{7,3},{8,12},{12,8},{9,1... | collective-permute-start | bytes 24584 | tf_op jit(solution)/shard_map/ppermute | solution.py:595
  26.6 16.3 %collective-permute-start.16 = (bf16[3,832,128]{2,1,0:T(8,128)(2,1)S(1)}, bf16[3,832,128]{2,1,0:T(8,128)(2,1)S(1)}, u32[]{:S(2)}, u32[]{:S(2)}) collective-permute-start(bf16[3,832,128]{2,1,0:T(8,128)(2,1)S(1)} %get-tuple-element.101), channel_id=1, source_target_pairs={{0,1},{1,0},{2,3},{3,2},{4,5},{5,4},{6,7},{7,6},{8,9},{9,8},{10,11... | collective-permute-start | bytes 1916936 | tf_op jit(solution)/shard_map/ppermute | solution.py:600
  28.0 3.7 %collective-permute-start.11 = (f32[16,256]{1,0:T(8,128)S(1)}, f32[16,256]{1,0:T(8,128)S(1)}, u32[]{:S(2)}, u32[]{:S(2)}) collective-permute-start(f32[16,256]{1,0:T(8,128)S(1)} %pad_maximum_fusion.1), channel_id=1, source_target_pairs={{0,8},{8,0},{1,9},{9,1},{2,10},{10,2},{3,11},{11,3},{4,12},{12,4},... | collective-permute-start | bytes 49160 | tf_op jit(solution)/shard_map/ppermute | solution.py:595
  31.7 3.9 %collective-permute-start.12 = (f32[32,256]{1,0:T(8,128)S(1)}, f32[32,256]{1,0:T(8,128)S(1)}, u32[]{:S(2)}, u32[]{:S(2)}) collective-permute-start(f32[32,256]{1,0:T(8,128)S(1)} %pad_maximum_fusion), channel_id=1, source_target_pairs={{0,16},{16,0},{1,17},{17,1},{2,18},{18,2},{3,19},{19,3},{4,20},{20... | collective-permute-start | bytes 98312 | tf_op jit(solution)/shard_map/ppermute | solution.py:595
  35.7 25.6 %collective-permute-start.13 = (bf16[2,832,128]{2,1,0:T(8,128)(2,1)S(1)}, bf16[2,832,128]{2,1,0:T(8,128)(2,1)S(1)}, u32[]{:S(2)}, u32[]{:S(2)}) collective-permute-start(bf16[2,832,128]{2,1,0:T(8,128)(2,1)S(1)} %stack.1.rest_5_), channel_id=1, source_target_pairs={{0,8},{8,0},{16,24},{24,16},{1,9},{9,1},{17,25},{25,17},{2,10},{10... | collective-permute-start | bytes 1277960 | tf_op jit(solution)/shard_map/ppermute | solution.py:615
  37.3 23.9 %collective-permute-start.14 = (bf16[2,832,128]{2,1,0:T(8,128)(2,1)S(1)}, bf16[2,832,128]{2,1,0:T(8,128)(2,1)S(1)}, u32[]{:S(2)}, u32[]{:S(2)}) collective-permute-start(bf16[2,832,128]{2,1,0:T(8,128)(2,1)S(1)} %stack.1.rest_5_), channel_id=1, source_target_pairs={{0,16},{8,24},{16,0},{24,8},{1,17},{9,25},{17,1},{25,9},{2,18},{10... | collective-permute-start | bytes 1277960 | tf_op jit(solution)/shard_map/ppermute | solution.py:615
  42.4 18.9 %collective-permute-start.15 = (bf16[2,832,128]{2,1,0:T(8,128)(2,1)S(1)}, bf16[2,832,128]{2,1,0:T(8,128)(2,1)S(1)}, u32[]{:S(2)}, u32[]{:S(2)}) collective-permute-start(bf16[2,832,128]{2,1,0:T(8,128)(2,1)S(1)} %stack.1.rest_5_), channel_id=1, source_target_pairs={{0,24},{8,16},{16,8},{24,0},{1,25},{9,17},{17,9},{25,1},{2,26},{10... | collective-permute-start | bytes 1277960 | tf_op jit(solution)/shard_map/ppermute | solution.py:635
  61.3 2.4 %collective-permute-start.17 = (bf16[4,832,128]{2,1,0:T(8,128)(2,1)S(1)}, bf16[4,832,128]{2,1,0:T(8,128)(2,1)S(1)}, u32[]{:S(2)}, u32[]{:S(2)}) collective-permute-start(bf16[4,832,128]{2,1,0:T(8,128)(2,1)S(1)} %bitcast.3), channel_id=1, source_target_pairs={{0,4},{4,0},{1,5},{5,1},{2,6},{6,2},{3,7},{7,3},{8,12},{12,8},{9,1... | collective-permute-start | bytes 2555912 | tf_op jit(solution)/shard_map/ppermute | solution.py:639
  65.1 2.0 %collective-permute-start.18 = (bf16[4,256,256]{2,1,0:T(8,128)(2,1)S(1)}, bf16[4,256,256]{2,1,0:T(8,128)(2,1)S(1)}, u32[]{:S(2)}, u32[]{:S(2)}) collective-permute-start(bf16[4,256,256]{2,1,0:T(8,128)(2,1)S(1)} %columns.4), channel_id=1, source_target_pairs={{0,4},{4,0},{1,5},{5,1},{2,6},{6,2},{3,7},{7,3},{8,12},{12,8},{9,1... | collective-permute-start | bytes 1572872 | tf_op jit(solution)/shard_map/ppermute | solution.py:673

commit v24 on v23

--- a/solution.py
+++ b/solution.py
@@ -598,7 +598,6 @@
 
     if spread:
         first = [early, lax.ppermute(sent, "tp", [(z, z ^ 1) for z in range(heads)])]
-        near, stats = lax.optimization_barrier((near, stats))
         pieces = [
             pl.pallas_call(
                 stack_kernel,
@@ -611,9 +610,8 @@
             )(*near)
         ]
         for d in (1, 2):
-            pieces.append(
-                lax.ppermute(pieces[0], ctx[:-1], [(i, i ^ d) for i in range(chips)])
-            )
+            free, _ = lax.optimization_barrier((pieces[0], stats[d + 1]))
+            pieces.append(lax.ppermute(free, ctx[:-1], [(i, i ^ d) for i in range(chips)]))
         pieces[0], sheet = lax.optimization_barrier((pieces[0], sheet))
 
     grads = pl.pallas_call(

time: 68.2 us -> 68.2 us (level)
  waiting for transfers between devices: 18.1 us -> 16.9 us
  starting transfers between devices: 17.8 us -> 18.8 us
    ppermute x1, starting transfers between devices: 0.42 us -> 1.85 us  [per_device(): lax.ppermute(diagonal, ctx[:-1], [(i, i ^ 3) for i in range(chips)])]
    ppermute x3, waiting for transfers between devices: 6.06 us -> 4.8 us  [per_device(): stats.append(lax.ppermute(held, name, swap))]
where the time goes in v24:
time: 68.2 us; the launch traced here: 68.1 us
  starting transfers between devices  18.8 us (28%)
  blocking collectives  18.7 us (27%)
  waiting for transfers between devices  16.9 us (25%)
  Pallas kernels  13 us (19%)
  between operations  0.71 us (1%)
    all_gather x1, blocking collectives, per_device(): grads = lax.all_gather(grads, 'tp')  18.7 us
    ppermute x3, waiting for transfers between devices, per_device(): stats.append(lax.ppermute(held, name, swap))  4.8 us
    ppermute x3, waiting for transfers between devices, per_device(): lax.ppermute(sends[d], ctx[:-1], [(i, i ^ d) for i in range(chips)])  4.2 us
    ppermute x1, starting transfers between devices, per_device(): across = lax.ppermute(outs[0], 'tp', [(z, z ^ 2) for z in range(heads)])  4.1 us
    pallas_call x1, Pallas kernels, per_device(): pl.pallas_call(lambda *refs: gradient_kernel(ctx, count, len(recv), len(s...  3.59 us
    ppermute x3, starting transfers between devices, per_device(): lax.ppermute(sends[d], ctx[:-1], [(i, i ^ d) for i in range(chips)])  3.49 us
    pallas_call x1, Pallas kernels, per_device(): pl.pallas_call(partial(project_kernel, ctx, len(packs)), out_shape=packs...  3.13 us
    ppermute x1, waiting for transfers between devices, per_device(): early = lax.ppermute(outs[0], 'tp', [(z, z ^ 1) for z in range(heads)])  2.83 us
  transfers between devices with their start and end apart: 19, of which 10 were waited for; matrix products, arithmetic and copies ran while one was open for 0% of the time, Pallas kernels for 11%

profile of v24, /device:TPU:0, one launch (start us, length us, event | category | flops | bytes accessed | tf_op | source)
XLA Modules:
  0.0 68.1 jit_solution(15701393758298511552)
XLA Ops:
  0.6 3.1 %project.1 = (bf16[832,128]{1,0:T(8,128)(2,1)S(1)}, bf16[3,832,128]{2,1,0:T(8,128)(2,1)S(1)}, bf16[560,128]{1,0:T(8,128)(2,1)S(1)}, bf16[560,128]{1,0:T(8,128)(2...) custom-call(bf16[256,2048]{1,0:T(8,128)(2,1)} %tok_hbm.1, ...), custom_call_target="tpu_custom_call" | custom-call | flops 1 | bytes 1024 | tf_op jit(solution)/shard_map/project/pallas_call | solution.py:526
  3.8 4.1 %collective-permute-start = (bf16[832,128]{1,0:T(8,128)(2,1)S(1)}, bf16[832,128]{1,0:T(8,128)(2,1)S(1)}, u32[]{:S(2)}, u32[]{:S(2)}) collective-permute-start(bf16[832,128]{1,0:T(8,128)(2,1)S(1)} %get-tuple-element.60), channel_id=1, source_target_pairs={{0,2},{1,3},{2,0},{3,1},{4,6},{5,7},{6,4},{7,5},{8,10},{9,11},{10,... | collective-permute-start | bytes 638984 | tf_op jit(solution)/shard_map/ppermute | solution.py:558
  7.9 2.4 %collective-permute-start.1 = (bf16[560,128]{1,0:T(8,128)(2,1)S(1)}, bf16[560,128]{1,0:T(8,128)(2,1)S(1)}, u32[]{:S(2)}, u32[]{:S(2)}) collective-permute-start(bf16[560,128]{1,0:T(8,128)(2,1)S(1)} %get-tuple-element.61), channel_id=1, source_target_pairs={{0,24},{8,16},{16,8},{24,0},{1,25},{9,17},{17,9},{25,1},{2,26},{10... | collective-permute-start | bytes 430088 | tf_op jit(solution)/shard_map/ppermute | solution.py:555
  10.3 0.5 collective-permute-start.4
  10.9 0.5 collective-permute-start.6
  11.4 1.6 %collective-permute-start.2 = (bf16[832,128]{1,0:T(8,128)(2,1)S(1)}, bf16[832,128]{1,0:T(8,128)(2,1)S(1)}, u32[]{:S(2)}, u32[]{:S(2)}) collective-permute-start(bf16[832,128]{1,0:T(8,128)(2,1)S(1)} %get-tuple-element.60), channel_id=1, source_target_pairs={{0,1},{1,0},{2,3},{3,2},{4,5},{5,4},{6,7},{7,6},{8,9},{9,8},{10,11... | collective-permute-start | bytes 638984 | tf_op jit(solution)/shard_map/ppermute | solution.py:568
  12.9 2.5 %collective-permute-done.1.refs_5_ = bf16[560,128]{1,0:T(8,128)(2,1)S(1)} collective-permute-done((bf16[560,128]{1,0:T(8,128)(2,1)S(1)}, bf16[560,128]{1,0:T(8,128)(2,1)S(1)}, u32[]{:S(2)}, u32[]{:S(2)}) %collective-permute-start.1) | collective-permute-done | bytes 143392 | tf_op jit(solution)/shard_map/ppermute | solution.py:555
  15.5 0.0 collective-permute-start.3
  15.5 1.7 %collective-permute-done.4.refs_1_ = bf16[560,128]{1,0:T(8,128)(2,1)S(1)} collective-permute-done((bf16[560,128]{1,0:T(8,128)(2,1)S(1)}, bf16[560,128]{1,0:T(8,128)(2,1)S(1)}, u32[]{:S(2)}, u32[]{:S(2)}) %collective-permute-start.4) | collective-permute-done | bytes 143392 | tf_op jit(solution)/shard_map/ppermute | solution.py:555
  17.1 0.0 collective-permute-start.5
  17.1 0.0 collective-permute-done.6.refs_3_
  17.1 0.5 collective-permute-start.7
  17.7 0.2 collective-permute-done.refs_0_
  17.8 0.0 collective-permute-start.8
  17.8 0.0 collective-permute-done.3.refs_0_
  17.8 2.8 %collective-permute-done.2.rest_7_.rest_9_ = bf16[832,128]{1,0:T(8,128)(2,1)S(1)} collective-permute-done((bf16[832,128]{1,0:T(8,128)(2,1)S(1)}, bf16[832,128]{1,0:T(8,128)(2,1)S(1)}, u32[]{:S(2)}, u32[]{:S(2)}) %collective-permute-start.2) | collective-permute-done | bytes 213024 | tf_op jit(solution)/shard_map/ppermute | solution.py:568
  20.6 0.0 collective-permute-done.5.refs_2_
  20.6 0.0 collective-permute-done.7.refs_4_
  20.7 0.0 collective-permute-done.8.refs_6_
  20.7 0.1 collective-permute-start.9
  20.7 2.4 %query_side.1 = (bf16[256,128]{1,0:T(8,128)(2,1)}, f32[8,256]{1,0:T(8,128)S(1)}, f32[256,128]{1,0:T(8,128)S(1)}) custom-call(bf16[560,128]{1,0:T(8,128)(2,1)S(1)} %collective-permute-done.3.refs_0_, bf16[560,128]{1,0:T(8,128)(2,1)S(1)} %collective-permute-done.4.refs_1_, bf16[560,128]{1,0:T(8,128)(2,1)S(1)} %collective-permute-done.5.refs_2_, ...), custom_call_target="tpu_custom_call" | custom-call | flops 1 | bytes 1024 | tf_op jit(solution)/shard_map/query_side/pallas_call | solution.py:572
  23.1 0.0 collective-permute-start.10
  23.1 1.2 %collective-permute-done.10.refs_8_ = f32[8,256]{1,0:T(8,128)S(1)} collective-permute-done((f32[8,256]{1,0:T(8,128)S(1)}, f32[8,256]{1,0:T(8,128)S(1)}, u32[]{:S(2)}, u32[]{:S(2)}) %collective-permute-start.10) | collective-permute-done | bytes 8224 | tf_op jit(solution)/shard_map/ppermute | solution.py:595
  24.3 2.3 %collective-permute-done.9.refs_1_ = bf16[832,128]{1,0:T(8,128)(2,1)S(1)} collective-permute-done((bf16[832,128]{1,0:T(8,128)(2,1)S(1)}, bf16[832,128]{1,0:T(8,128)(2,1)S(1)}, u32[]{:S(2)}, u32[]{:S(2)}) %collective-permute-start.9) | collective-permute-done | bytes 213024 | tf_op jit(solution)/shard_map/ppermute | solution.py:570
  26.6 1.4 %collective-permute-start.16 = (bf16[3,832,128]{2,1,0:T(8,128)(2,1)S(1)}, bf16[3,832,128]{2,1,0:T(8,128)(2,1)S(1)}, u32[]{:S(2)}, u32[]{:S(2)}) collective-permute-start(bf16[3,832,128]{2,1,0:T(8,128)(2,1)S(1)} %get-tuple-element.93), channel_id=1, source_target_pairs={{0,1},{1,0},{2,3},{3,2},{4,5},{5,4},{6,7},{7,6},{8,9},{9,8},{10,11... | collective-permute-start | bytes 1916936 | tf_op jit(solution)/shard_map/ppermute | solution.py:600
  28.0 1.5 %collective-permute-start.11 = (f32[16,256]{1,0:T(8,128)S(1)}, f32[16,256]{1,0:T(8,128)S(1)}, u32[]{:S(2)}, u32[]{:S(2)}) collective-permute-start(f32[16,256]{1,0:T(8,128)S(1)} %pad_maximum_fusion.1), channel_id=1, source_target_pairs={{0,8},{8,0},{1,9},{9,1},{2,10},{10,2},{3,11},{11,3},{4,12},{12,4},... | collective-permute-start | bytes 49160 | tf_op jit(solution)/shard_map/ppermute | solution.py:595
  29.5 2.2 %collective-permute-done.11.refs_9_ = f32[16,256]{1,0:T(8,128)S(1)} collective-permute-done((f32[16,256]{1,0:T(8,128)S(1)}, f32[16,256]{1,0:T(8,128)S(1)}, u32[]{:S(2)}, u32[]{:S(2)}) %collective-permute-start.11) | collective-permute-done | bytes 16416 | tf_op jit(solution)/shard_map/ppermute | solution.py:595
  31.7 1.3 %collective-permute-start.13 = (f32[32,256]{1,0:T(8,128)S(1)}, f32[32,256]{1,0:T(8,128)S(1)}, u32[]{:S(2)}, u32[]{:S(2)}) collective-permute-start(f32[32,256]{1,0:T(8,128)S(1)} %pad_maximum_fusion), channel_id=1, source_target_pairs={{0,16},{16,0},{1,17},{17,1},{2,18},{18,2},{3,19},{19,3},{4,20},{20... | collective-permute-start | bytes 98312 | tf_op jit(solution)/shard_map/ppermute | solution.py:595
  33.0 1.6 %collective-permute-start.12 = (bf16[2,832,128]{2,1,0:T(8,128)(2,1)S(1)}, bf16[2,832,128]{2,1,0:T(8,128)(2,1)S(1)}, u32[]{:S(2)}, u32[]{:S(2)}) collective-permute-start(bf16[2,832,128]{2,1,0:T(8,128)(2,1)S(1)} %stack.1.rest_5_), channel_id=1, source_target_pairs={{0,8},{8,0},{16,24},{24,16},{1,9},{9,1},{17,25},{25,17},{2,10},{10... | collective-permute-start | bytes 1277960 | tf_op jit(solution)/shard_map/ppermute | solution.py:614
  34.6 1.4 %collective-permute-done.13.refs_10_ = f32[32,256]{1,0:T(8,128)S(1)} collective-permute-done((f32[32,256]{1,0:T(8,128)S(1)}, f32[32,256]{1,0:T(8,128)S(1)}, u32[]{:S(2)}, u32[]{:S(2)}) %collective-permute-start.13) | collective-permute-done | bytes 32800 | tf_op jit(solution)/shard_map/ppermute | solution.py:595
  36.0 1.2 %collective-permute-start.14 = (bf16[2,832,128]{2,1,0:T(8,128)(2,1)S(1)}, bf16[2,832,128]{2,1,0:T(8,128)(2,1)S(1)}, u32[]{:S(2)}, u32[]{:S(2)}) collective-permute-start(bf16[2,832,128]{2,1,0:T(8,128)(2,1)S(1)} %stack.1.rest_5_), channel_id=1, source_target_pairs={{0,16},{8,24},{16,0},{24,8},{1,17},{9,25},{17,1},{25,9},{2,18},{10... | collective-permute-start | bytes 1277960 | tf_op jit(solution)/shard_map/ppermute | solution.py:614
  37.1 3.6 %gradients.1 = bf16[832,128]{1,0:T(8,128)(2,1)S(1)} custom-call(bf16[560,128]{1,0:T(8,128)(2,1)S(1)} %collective-permute-done.3.refs_0_, bf16[560,128]{1,0:T(8,128)(2,1)S(1)} %collective-permute-done.4.refs_1_, bf16[560,128]{1,0:T(8,128)(2,1)S(1)} %collective-permute-done.5.refs_2_, bf16[560,128]{1,0:T(8,128)(2,1)S(1)} %collective-permute-done.6.refs_3_, ...), custom_call_target="tpu_custom_call" | custom-call | flops 1 | bytes 1024 | tf_op jit(solution)/shard_map/gradients/pallas_call | solution.py:617
  40.7 1.8 %collective-permute-start.15 = (bf16[2,832,128]{2,1,0:T(8,128)(2,1)S(1)}, bf16[2,832,128]{2,1,0:T(8,128)(2,1)S(1)}, u32[]{:S(2)}, u32[]{:S(2)}) collective-permute-start(bf16[2,832,128]{2,1,0:T(8,128)(2,1)S(1)} %stack.1.rest_5_), channel_id=1, source_target_pairs={{0,24},{8,16},{16,8},{24,0},{1,25},{9,17},{17,9},{25,1},{2,26},{10... | collective-permute-start | bytes 1277960 | tf_op jit(solution)/shard_map/ppermute | solution.py:633
  42.6 0.0 collective-permute-done.16.rest_8_.rest_10_
  42.6 18.7 %all-gather = bf16[3328,128]{1,0:T(8,128)(2,1)S(1)} all-gather(bf16[832,128]{1,0:T(8,128)(2,1)S(1)} %gradients.1), channel_id=2, replica_groups=mesh['half0'=2,'half1'=2,'core'=2,'tp'=4] {'tp'}, dimensions={0}, use_global_device_ids=true | all-gather | bytes 1064960 | tf_op jit(solution)/shard_map/all_gather | solution.py:635
  61.3 0.0 collective-permute-done.12.rest_6_
  61.3 0.0 collective-permute-done.14.rest_7_.rest_5_
  61.3 0.0 collective-permute-done.15.rest_8_.rest_6_
  61.3 0.1 collective-permute-start.17
  61.4 0.2 cat.2
  61.6 0.7 columns.3.refs_0_
  62.3 1.5 %collective-permute-done.17.grad_ref = bf16[4,832,128]{2,1,0:T(8,128)(2,1)S(1)} collective-permute-done((bf16[4,832,128]{2,1,0:T(8,128)(2,1)S(1)}, bf16[4,832,128]{2,1,0:T(8,128)(2,1)S(1)}, u32[]{:S(2)}, u32[]{:S(2)}) %collective-permute-start.17) | collective-permute-done | bytes 852000 | tf_op jit(solution)/shard_map/ppermute | solution.py:637
  63.7 0.2 cat.3
  63.9 1.1 %columns.4 = bf16[4,256,256]{2,1,0:T(8,128)(2,1)S(1)} custom-call(bf16[256,1536]{1,0:T(8,128)(2,1)S(1)} %get-tuple-element.109.rest_0_, bf16[256,128]{1,0:T(8,128)(2,1)S(1)} %get-tuple-element.110.rest_1_, bf16[2048,256]{1,0:T(8,128)(2,1)S(1)} %get-tuple-element.100.rest_2_, bf16[2048,128]{1,0:T(8,128)(2,1)S(1)} %get-tuple-element.101.rest_3_, ...), custom_call_target="tpu_custom_call" | custom-call | flops 1 | bytes 1024 | tf_op jit(solution)/shard_map/columns/pallas_call | solution.py:657
  65.1 0.2 collective-permute-start.18
  65.3 0.6 columns.5.refs_1_
  65.9 1.1 %collective-permute-done.18.refs_2_ = bf16[4,256,256]{2,1,0:T(8,128)(2,1)S(1)} collective-permute-done((bf16[4,256,256]{2,1,0:T(8,128)(2,1)S(1)}, bf16[4,256,256]{2,1,0:T(8,128)(2,1)S(1)}, u32[]{:S(2)}, u32[]{:S(2)}) %collective-permute-start.18) | collective-permute-done | bytes 524320 | tf_op jit(solution)/shard_map/ppermute | solution.py:671
  67.1 1.0 %lay.1 = bf16[256,2048]{1,0:T(8,128)(2,1)} custom-call(bf16[2,256,256]{2,1,0:T(8,128)(2,1)S(1)} %columns.3.refs_0_, bf16[2,256,256]{2,1,0:T(8,128)(2,1)S(1)} %columns.5.refs_1_, bf16[4,256,256]{2,1,0:T(8,128)(2,1)S(1)} %collective-permute-done.18.refs_2_), custom_call_target="tpu_custom_call" | custom-call | flops 1 | bytes 1024 | tf_op jit(solution)/shard_map/lay/pallas_call | solution.py:674
  (3 shorter events, 0.0 us)
Async XLA Ops:
  3.8 14.0 %collective-permute-start = (bf16[832,128]{1,0:T(8,128)(2,1)S(1)}, bf16[832,128]{1,0:T(8,128)(2,1)S(1)}, u32[]{:S(2)}, u32[]{:S(2)}) collective-permute-start(bf16[832,128]{1,0:T(8,128)(2,1)S(1)} %get-tuple-element.60), channel_id=1, source_target_pairs={{0,2},{1,3},{2,0},{3,1},{4,6},{5,7},{6,4},{7,5},{8,10},{9,11},{10,... | collective-permute-start | bytes 638984 | tf_op jit(solution)/shard_map/ppermute | solution.py:558
  7.9 7.6 %collective-permute-start.1 = (bf16[560,128]{1,0:T(8,128)(2,1)S(1)}, bf16[560,128]{1,0:T(8,128)(2,1)S(1)}, u32[]{:S(2)}, u32[]{:S(2)}) collective-permute-start(bf16[560,128]{1,0:T(8,128)(2,1)S(1)} %get-tuple-element.61), channel_id=1, source_target_pairs={{0,24},{8,16},{16,8},{24,0},{1,25},{9,17},{17,9},{25,1},{2,26},{10... | collective-permute-start | bytes 430088 | tf_op jit(solution)/shard_map/ppermute | solution.py:555
  10.3 6.8 %collective-permute-start.4 = (bf16[560,128]{1,0:T(8,128)(2,1)S(1)}, bf16[560,128]{1,0:T(8,128)(2,1)S(1)}, u32[]{:S(2)}, u32[]{:S(2)}) collective-permute-start(bf16[560,128]{1,0:T(8,128)(2,1)S(1)} %get-tuple-element.64), channel_id=1, source_target_pairs={{0,8},{8,0},{16,24},{24,16},{1,9},{9,1},{17,25},{25,17},{2,10},{10... | collective-permute-start | bytes 430088 | tf_op jit(solution)/shard_map/ppermute | solution.py:555
  10.9 6.3 %collective-permute-start.6 = (bf16[560,128]{1,0:T(8,128)(2,1)S(1)}, bf16[560,128]{1,0:T(8,128)(2,1)S(1)}, u32[]{:S(2)}, u32[]{:S(2)}) collective-permute-start(bf16[560,128]{1,0:T(8,128)(2,1)S(1)} %get-tuple-element.65), channel_id=1, source_target_pairs={{0,16},{8,24},{16,0},{24,8},{1,17},{9,25},{17,1},{25,9},{2,18},{10... | collective-permute-start | bytes 430088 | tf_op jit(solution)/shard_map/ppermute | solution.py:555
  11.4 9.3 %collective-permute-start.2 = (bf16[832,128]{1,0:T(8,128)(2,1)S(1)}, bf16[832,128]{1,0:T(8,128)(2,1)S(1)}, u32[]{:S(2)}, u32[]{:S(2)}) collective-permute-start(bf16[832,128]{1,0:T(8,128)(2,1)S(1)} %get-tuple-element.60), channel_id=1, source_target_pairs={{0,1},{1,0},{2,3},{3,2},{4,5},{5,4},{6,7},{7,6},{8,9},{9,8},{10,11... | collective-permute-start | bytes 638984 | tf_op jit(solution)/shard_map/ppermute | solution.py:568
  15.5 2.4 %collective-permute-start.3 = (bf16[560,128]{1,0:T(8,128)(2,1)S(1)}, bf16[560,128]{1,0:T(8,128)(2,1)S(1)}, u32[]{:S(2)}, u32[]{:S(2)}) collective-permute-start(bf16[560,128]{1,0:T(8,128)(2,1)S(1)} %get-tuple-element.63), channel_id=1, source_target_pairs={{0,4},{4,0},{1,5},{5,1},{2,6},{6,2},{3,7},{7,3},{8,12},{12,8},{9,1... | collective-permute-start | bytes 430088 | tf_op jit(solution)/shard_map/ppermute | solution.py:556
  17.1 3.5 %collective-permute-start.5 = (bf16[560,128]{1,0:T(8,128)(2,1)S(1)}, bf16[560,128]{1,0:T(8,128)(2,1)S(1)}, u32[]{:S(2)}, u32[]{:S(2)}) collective-permute-start(bf16[560,128]{1,0:T(8,128)(2,1)S(1)} %collective-permute-done.4.refs_1_), channel_id=1, source_target_pairs={{0,4},{4,0},{1,5},{5,1},{2,6},{6,2},{3,7},{7,3},{8,12},{12,8},{9,1... | collective-permute-start | bytes 430088 | tf_op jit(solution)/shard_map/ppermute | solution.py:562
  17.1 3.5 %collective-permute-start.7 = (bf16[560,128]{1,0:T(8,128)(2,1)S(1)}, bf16[560,128]{1,0:T(8,128)(2,1)S(1)}, u32[]{:S(2)}, u32[]{:S(2)}) collective-permute-start(bf16[560,128]{1,0:T(8,128)(2,1)S(1)} %collective-permute-done.6.refs_3_), channel_id=1, source_target_pairs={{0,4},{4,0},{1,5},{5,1},{2,6},{6,2},{3,7},{7,3},{8,12},{12,8},{9,1... | collective-permute-start | bytes 430088 | tf_op jit(solution)/shard_map/ppermute | solution.py:562
  17.8 2.8 %collective-permute-start.8 = (bf16[560,128]{1,0:T(8,128)(2,1)S(1)}, bf16[560,128]{1,0:T(8,128)(2,1)S(1)}, u32[]{:S(2)}, u32[]{:S(2)}) collective-permute-start(bf16[560,128]{1,0:T(8,128)(2,1)S(1)} %collective-permute-done.1.refs_5_), channel_id=1, source_target_pairs={{0,4},{4,0},{1,5},{5,1},{2,6},{6,2},{3,7},{7,3},{8,12},{12,8},{9,1... | collective-permute-start | bytes 430088 | tf_op jit(solution)/shard_map/ppermute | solution.py:562
  20.7 5.9 %collective-permute-start.9 = (bf16[832,128]{1,0:T(8,128)(2,1)S(1)}, bf16[832,128]{1,0:T(8,128)(2,1)S(1)}, u32[]{:S(2)}, u32[]{:S(2)}) collective-permute-start(bf16[832,128]{1,0:T(8,128)(2,1)S(1)} %collective-permute-done.refs_0_), channel_id=1, source_target_pairs={{0,1},{1,0},{2,3},{3,2},{4,5},{5,4},{6,7},{7,6},{8,9},{9,8},{10,11... | collective-permute-start | bytes 638984 | tf_op jit(solution)/shard_map/ppermute | solution.py:570
  23.1 1.2 %collective-permute-start.10 = (f32[8,256]{1,0:T(8,128)S(1)}, f32[8,256]{1,0:T(8,128)S(1)}, u32[]{:S(2)}, u32[]{:S(2)}) collective-permute-start(f32[8,256]{1,0:T(8,128)S(1)} %get-tuple-element.86.refs_7_), channel_id=1, source_target_pairs={{0,4},{4,0},{1,5},{5,1},{2,6},{6,2},{3,7},{7,3},{8,12},{12,8},{9,1... | collective-permute-start | bytes 24584 | tf_op jit(solution)/shard_map/ppermute | solution.py:595
  26.6 16.0 %collective-permute-start.16 = (bf16[3,832,128]{2,1,0:T(8,128)(2,1)S(1)}, bf16[3,832,128]{2,1,0:T(8,128)(2,1)S(1)}, u32[]{:S(2)}, u32[]{:S(2)}) collective-permute-start(bf16[3,832,128]{2,1,0:T(8,128)(2,1)S(1)} %get-tuple-element.93), channel_id=1, source_target_pairs={{0,1},{1,0},{2,3},{3,2},{4,5},{5,4},{6,7},{7,6},{8,9},{9,8},{10,11... | collective-permute-start | bytes 1916936 | tf_op jit(solution)/shard_map/ppermute | solution.py:600
  28.0 3.7 %collective-permute-start.11 = (f32[16,256]{1,0:T(8,128)S(1)}, f32[16,256]{1,0:T(8,128)S(1)}, u32[]{:S(2)}, u32[]{:S(2)}) collective-permute-start(f32[16,256]{1,0:T(8,128)S(1)} %pad_maximum_fusion.1), channel_id=1, source_target_pairs={{0,8},{8,0},{1,9},{9,1},{2,10},{10,2},{3,11},{11,3},{4,12},{12,4},... | collective-permute-start | bytes 49160 | tf_op jit(solution)/shard_map/ppermute | solution.py:595
  31.7 4.3 %collective-permute-start.13 = (f32[32,256]{1,0:T(8,128)S(1)}, f32[32,256]{1,0:T(8,128)S(1)}, u32[]{:S(2)}, u32[]{:S(2)}) collective-permute-start(f32[32,256]{1,0:T(8,128)S(1)} %pad_maximum_fusion), channel_id=1, source_target_pairs={{0,16},{16,0},{1,17},{17,1},{2,18},{18,2},{3,19},{19,3},{4,20},{20... | collective-permute-start | bytes 98312 | tf_op jit(solution)/shard_map/ppermute | solution.py:595
  33.0 28.3 %collective-permute-start.12 = (bf16[2,832,128]{2,1,0:T(8,128)(2,1)S(1)}, bf16[2,832,128]{2,1,0:T(8,128)(2,1)S(1)}, u32[]{:S(2)}, u32[]{:S(2)}) collective-permute-start(bf16[2,832,128]{2,1,0:T(8,128)(2,1)S(1)} %stack.1.rest_5_), channel_id=1, source_target_pairs={{0,8},{8,0},{16,24},{24,16},{1,9},{9,1},{17,25},{25,17},{2,10},{10... | collective-permute-start | bytes 1277960 | tf_op jit(solution)/shard_map/ppermute | solution.py:614
  36.0 25.3 %collective-permute-start.14 = (bf16[2,832,128]{2,1,0:T(8,128)(2,1)S(1)}, bf16[2,832,128]{2,1,0:T(8,128)(2,1)S(1)}, u32[]{:S(2)}, u32[]{:S(2)}) collective-permute-start(bf16[2,832,128]{2,1,0:T(8,128)(2,1)S(1)} %stack.1.rest_5_), channel_id=1, source_target_pairs={{0,16},{8,24},{16,0},{24,8},{1,17},{9,25},{17,1},{25,9},{2,18},{10... | collective-permute-start | bytes 1277960 | tf_op jit(solution)/shard_map/ppermute | solution.py:614
  40.7 20.5 %collective-permute-start.15 = (bf16[2,832,128]{2,1,0:T(8,128)(2,1)S(1)}, bf16[2,832,128]{2,1,0:T(8,128)(2,1)S(1)}, u32[]{:S(2)}, u32[]{:S(2)}) collective-permute-start(bf16[2,832,128]{2,1,0:T(8,128)(2,1)S(1)} %stack.1.rest_5_), channel_id=1, source_target_pairs={{0,24},{8,16},{16,8},{24,0},{1,25},{9,17},{17,9},{25,1},{2,26},{10... | collective-permute-start | bytes 1277960 | tf_op jit(solution)/shard_map/ppermute | solution.py:633
  61.3 2.4 %collective-permute-start.17 = (bf16[4,832,128]{2,1,0:T(8,128)(2,1)S(1)}, bf16[4,832,128]{2,1,0:T(8,128)(2,1)S(1)}, u32[]{:S(2)}, u32[]{:S(2)}) collective-permute-start(bf16[4,832,128]{2,1,0:T(8,128)(2,1)S(1)} %bitcast.3), channel_id=1, source_target_pairs={{0,4},{4,0},{1,5},{5,1},{2,6},{6,2},{3,7},{7,3},{8,12},{12,8},{9,1... | collective-permute-start | bytes 2555912 | tf_op jit(solution)/shard_map/ppermute | solution.py:637
  65.1 2.0 %collective-permute-start.18 = (bf16[4,256,256]{2,1,0:T(8,128)(2,1)S(1)}, bf16[4,256,256]{2,1,0:T(8,128)(2,1)S(1)}, u32[]{:S(2)}, u32[]{:S(2)}) collective-permute-start(bf16[4,256,256]{2,1,0:T(8,128)(2,1)S(1)} %columns.4), channel_id=1, source_target_pairs={{0,4},{4,0},{1,5},{5,1},{2,6},{6,2},{3,7},{7,3},{8,12},{12,8},{9,1... | collective-permute-start | bytes 1572872 | tf_op jit(solution)/shard_map/ppermute | solution.py:671

commit v25 on v24

--- a/solution.py
+++ b/solution.py
@@ -155,7 +155,7 @@
         own_pack, other_pack = rest[:packs]
         pack(me, ww_ref, vw_ref, fw_ref, own_pack)
         for d in range(other_pack.shape[0]):
-            piece = jnp.bitwise_xor(me, 2 * d + 2)
+            piece = jnp.bitwise_xor(me, 2 * d + 4)
             pack(piece, ww_ref, vw_ref, fw_ref, other_pack.at[d])
 
 def stack_kernel(*refs):
@@ -422,7 +422,10 @@
     heads = feat_ref.shape[1] // nf2
     tile = 2 * LANES
     part = pl.ds(pl.multiple_of(jnp.bitwise_xor(block_index(ctx), e) * tile, tile), tile)
-    views = [firsts[1].at[e // 2 - 1] if e > 1 else firsts[0]]
+    if e // 2 == 1:
+        views = [piece_ref.at[heads - 2]]
+    else:
+        views = [firsts[1].at[e // 2 - 2] if e > 1 else firsts[0]]
     views += [piece_ref.at[t] for t in range(heads - 2)]
     main = [ww_ref[part, :], vw_ref[part, :]]
     main += [v[m * tile : (m + 1) * tile, :] for v in views for m in range(3)]
@@ -519,7 +522,7 @@
     packs = []
     if spread:
         packs = [jax.ShapeDtypeStruct((columns * tile // LANES, LANES), bf16)]
-        packs += [jax.ShapeDtypeStruct((chips - 1, *packs[0].shape), bf16)]
+        packs += [jax.ShapeDtypeStruct((chips - 2, *packs[0].shape), bf16)]
 
     payload = 2 * rows + 2 * nf + 16
     block = jax.ShapeDtypeStruct((payload, LANES), bf16)
@@ -598,19 +601,22 @@
 
     if spread:
         first = [early, lax.ppermute(sent, "tp", [(z, z ^ 1) for z in range(heads)])]
-        pieces = [
-            pl.pallas_call(
+
+        def stacked(parts):
+            return pl.pallas_call(
                 stack_kernel,
-                out_shape=jax.ShapeDtypeStruct((heads - 2, *packs[0].shape), bf16),
-                in_specs=[VMEM] * (heads - 2),
+                out_shape=jax.ShapeDtypeStruct((len(parts), *packs[0].shape), bf16),
+                in_specs=[VMEM] * len(parts),
                 out_specs=VMEM,
                 compiler_params=params,
                 cost_estimate=cost(1, 1024),
                 name="stack",
-            )(*near)
-        ]
+            )(*parts)
+
+        pieces = [stacked(near)]
         for d in (1, 2):
-            free, _ = lax.optimization_barrier((pieces[0], stats[d + 1]))
+            whole = stacked([*near, early]) if d == 1 else pieces[0]
+            free, _ = lax.optimization_barrier((whole, stats[d + 1]))
             pieces.append(lax.ppermute(free, ctx[:-1], [(i, i ^ d) for i in range(chips)]))
         pieces[0], sheet = lax.optimization_barrier((pieces[0], sheet))
 

time: 68.2 us -> 68.3 us (level)
  waiting for transfers between devices: 16.9 us -> 18.3 us
  starting transfers between devices: 18.8 us -> 17.7 us
    ppermute x3, waiting for transfers between devices: 4.8 us -> 6.25 us  [per_device(): stats.append(lax.ppermute(held, name, swap))]
    ppermute x1, starting transfers between devices: 1.85 us -> 0.73 us  [per_device(): lax.ppermute(diagonal, ctx[:-1], [(i, i ^ 3) for i in range(chips)])]
where the time goes in v25:
time: 68.3 us; the launch traced here: 68.1 us
  waiting for transfers between devices  18.3 us (27%)
  blocking collectives  18.3 us (27%)
  starting transfers between devices  17.7 us (26%)
  Pallas kernels  13 us (19%)
  between operations  0.71 us (1%)
    all_gather x1, blocking collectives, per_device(): grads = lax.all_gather(grads, 'tp')  18.3 us
    ppermute x3, waiting for transfers between devices, per_device(): stats.append(lax.ppermute(held, name, swap))  6.25 us
    ppermute x3, waiting for transfers between devices, per_device(): lax.ppermute(sends[d], ctx[:-1], [(i, i ^ d) for i in range(chips)])  4.2 us
    ppermute x1, starting transfers between devices, per_device(): across = lax.ppermute(outs[0], 'tp', [(z, z ^ 2) for z in range(heads)])  4.1 us
    pallas_call x1, Pallas kernels, per_device(): pl.pallas_call(lambda *refs: gradient_kernel(ctx, count, len(recv), len(s...  3.58 us
    ppermute x3, starting transfers between devices, per_device(): lax.ppermute(sends[d], ctx[:-1], [(i, i ^ d) for i in range(chips)])  3.49 us
    pallas_call x1, Pallas kernels, per_device(): pl.pallas_call(partial(project_kernel, ctx, len(packs)), out_shape=packs...  3.1 us
    ppermute x1, waiting for transfers between devices, per_device(): early = lax.ppermute(outs[0], 'tp', [(z, z ^ 1) for z in range(heads)])  2.83 us
  transfers between devices with their start and end apart: 19, of which 10 were waited for; matrix products, arithmetic and copies ran while one was open for 0% of the time, Pallas kernels for 11%

profile of v25, /device:TPU:0, one launch (start us, length us, event | category | flops | bytes accessed | tf_op | source)
XLA Modules:
  0.0 68.1 jit_solution(14297337438561218726)
XLA Ops:
  0.6 3.1 %project.1 = (bf16[832,128]{1,0:T(8,128)(2,1)S(1)}, bf16[2,832,128]{2,1,0:T(8,128)(2,1)S(1)}, bf16[560,128]{1,0:T(8,128)(2,1)S(1)}, bf16[560,128]{1,0:T(8,128)(2...) custom-call(bf16[256,2048]{1,0:T(8,128)(2,1)} %tok_hbm.1, ...), custom_call_target="tpu_custom_call" | custom-call | flops 1 | bytes 1024 | tf_op jit(solution)/shard_map/project/pallas_call | solution.py:529
  3.7 4.1 %collective-permute-start = (bf16[832,128]{1,0:T(8,128)(2,1)S(1)}, bf16[832,128]{1,0:T(8,128)(2,1)S(1)}, u32[]{:S(2)}, u32[]{:S(2)}) collective-permute-start(bf16[832,128]{1,0:T(8,128)(2,1)S(1)} %get-tuple-element.60), channel_id=1, source_target_pairs={{0,2},{1,3},{2,0},{3,1},{4,6},{5,7},{6,4},{7,5},{8,10},{9,11},{10,... | collective-permute-start | bytes 638984 | tf_op jit(solution)/shard_map/ppermute | solution.py:561
  7.8 2.4 %collective-permute-start.1 = (bf16[560,128]{1,0:T(8,128)(2,1)S(1)}, bf16[560,128]{1,0:T(8,128)(2,1)S(1)}, u32[]{:S(2)}, u32[]{:S(2)}) collective-permute-start(bf16[560,128]{1,0:T(8,128)(2,1)S(1)} %get-tuple-element.61), channel_id=1, source_target_pairs={{0,24},{8,16},{16,8},{24,0},{1,25},{9,17},{17,9},{25,1},{2,26},{10... | collective-permute-start | bytes 430088 | tf_op jit(solution)/shard_map/ppermute | solution.py:558
  10.3 0.5 collective-permute-start.4
  10.8 0.5 collective-permute-start.6
  11.3 1.6 %collective-permute-start.2 = (bf16[832,128]{1,0:T(8,128)(2,1)S(1)}, bf16[832,128]{1,0:T(8,128)(2,1)S(1)}, u32[]{:S(2)}, u32[]{:S(2)}) collective-permute-start(bf16[832,128]{1,0:T(8,128)(2,1)S(1)} %get-tuple-element.60), channel_id=1, source_target_pairs={{0,1},{1,0},{2,3},{3,2},{4,5},{5,4},{6,7},{7,6},{8,9},{9,8},{10,11... | collective-permute-start | bytes 638984 | tf_op jit(solution)/shard_map/ppermute | solution.py:571
  12.9 2.5 %collective-permute-done.1.refs_5_ = bf16[560,128]{1,0:T(8,128)(2,1)S(1)} collective-permute-done((bf16[560,128]{1,0:T(8,128)(2,1)S(1)}, bf16[560,128]{1,0:T(8,128)(2,1)S(1)}, u32[]{:S(2)}, u32[]{:S(2)}) %collective-permute-start.1) | collective-permute-done | bytes 143392 | tf_op jit(solution)/shard_map/ppermute | solution.py:558
  15.4 0.0 collective-permute-start.3
  15.4 1.7 %collective-permute-done.4.refs_1_ = bf16[560,128]{1,0:T(8,128)(2,1)S(1)} collective-permute-done((bf16[560,128]{1,0:T(8,128)(2,1)S(1)}, bf16[560,128]{1,0:T(8,128)(2,1)S(1)}, u32[]{:S(2)}, u32[]{:S(2)}) %collective-permute-start.4) | collective-permute-done | bytes 143392 | tf_op jit(solution)/shard_map/ppermute | solution.py:558
  17.1 0.0 collective-permute-start.5
  17.1 0.0 collective-permute-done.6.refs_3_
  17.1 0.5 collective-permute-start.7
  17.6 0.2 collective-permute-done.refs_0_
  17.8 0.0 collective-permute-start.8
  17.8 0.0 collective-permute-done.3.refs_0_
  17.8 2.8 %collective-permute-done.2.refs_2_.rest_7_.rest_9_ = bf16[832,128]{1,0:T(8,128)(2,1)S(1)} collective-permute-done((bf16[832,128]{1,0:T(8,128)(2,1)S(1)}, bf16[832,128]{1,0:T(8,128)(2,1)S(1)}, u32[]{:S(2)}, u32[]{:S(2)}) %collective-permute-start.2) | collective-permute-done | bytes 213024 | tf_op jit(solution)/shard_map/ppermute | solution.py:571
  20.6 0.0 collective-permute-done.5.refs_2_
  20.6 0.0 collective-permute-done.7.refs_4_
  20.6 0.0 collective-permute-done.8.refs_6_
  20.6 0.1 collective-permute-start.9
  20.7 2.4 %query_side.1 = (bf16[256,128]{1,0:T(8,128)(2,1)}, f32[8,256]{1,0:T(8,128)S(1)}, f32[256,128]{1,0:T(8,128)S(1)}) custom-call(bf16[560,128]{1,0:T(8,128)(2,1)S(1)} %collective-permute-done.3.refs_0_, bf16[560,128]{1,0:T(8,128)(2,1)S(1)} %collective-permute-done.4.refs_1_, bf16[560,128]{1,0:T(8,128)(2,1)S(1)} %collective-permute-done.5.refs_2_, ...), custom_call_target="tpu_custom_call" | custom-call | flops 1 | bytes 1024 | tf_op jit(solution)/shard_map/query_side/pallas_call | solution.py:575
  23.1 0.0 collective-permute-start.10
  23.1 1.2 %collective-permute-done.10.refs_8_ = f32[8,256]{1,0:T(8,128)S(1)} collective-permute-done((f32[8,256]{1,0:T(8,128)S(1)}, f32[8,256]{1,0:T(8,128)S(1)}, u32[]{:S(2)}, u32[]{:S(2)}) %collective-permute-start.10) | collective-permute-done | bytes 8224 | tf_op jit(solution)/shard_map/ppermute | solution.py:598
  24.3 2.3 %collective-permute-done.9.refs_1_ = bf16[832,128]{1,0:T(8,128)(2,1)S(1)} collective-permute-done((bf16[832,128]{1,0:T(8,128)(2,1)S(1)}, bf16[832,128]{1,0:T(8,128)(2,1)S(1)}, u32[]{:S(2)}, u32[]{:S(2)}) %collective-permute-start.9) | collective-permute-done | bytes 213024 | tf_op jit(solution)/shard_map/ppermute | solution.py:573
  26.5 1.4 %collective-permute-start.16 = (bf16[2,832,128]{2,1,0:T(8,128)(2,1)S(1)}, bf16[2,832,128]{2,1,0:T(8,128)(2,1)S(1)}, u32[]{:S(2)}, u32[]{:S(2)}) collective-permute-start(bf16[2,832,128]{2,1,0:T(8,128)(2,1)S(1)} %get-tuple-element.93), channel_id=1, source_target_pairs={{0,1},{1,0},{2,3},{3,2},{4,5},{5,4},{6,7},{7,6},{8,9},{9,8},{10,11... | collective-permute-start | bytes 1277960 | tf_op jit(solution)/shard_map/ppermute | solution.py:603
  27.9 1.5 %collective-permute-start.11 = (f32[16,256]{1,0:T(8,128)S(1)}, f32[16,256]{1,0:T(8,128)S(1)}, u32[]{:S(2)}, u32[]{:S(2)}) collective-permute-start(f32[16,256]{1,0:T(8,128)S(1)} %pad_maximum_fusion.1), channel_id=1, source_target_pairs={{0,8},{8,0},{1,9},{9,1},{2,10},{10,2},{3,11},{11,3},{4,12},{12,4},... | collective-permute-start | bytes 49160 | tf_op jit(solution)/shard_map/ppermute | solution.py:598
  29.5 2.2 %collective-permute-done.11.refs_9_ = f32[16,256]{1,0:T(8,128)S(1)} collective-permute-done((f32[16,256]{1,0:T(8,128)S(1)}, f32[16,256]{1,0:T(8,128)S(1)}, u32[]{:S(2)}, u32[]{:S(2)}) %collective-permute-start.11) | collective-permute-done | bytes 16416 | tf_op jit(solution)/shard_map/ppermute | solution.py:598
  31.7 1.5 %collective-permute-start.12 = (bf16[3,832,128]{2,1,0:T(8,128)(2,1)S(1)}, bf16[3,832,128]{2,1,0:T(8,128)(2,1)S(1)}, u32[]{:S(2)}, u32[]{:S(2)}) collective-permute-start(bf16[3,832,128]{2,1,0:T(8,128)(2,1)S(1)} %stack.3), channel_id=1, source_target_pairs={{0,8},{8,0},{16,24},{24,16},{1,9},{9,1},{17,25},{25,17},{2,10},{10... | collective-permute-start | bytes 1916936 | tf_op jit(solution)/shard_map/ppermute | solution.py:620
  33.2 1.3 %collective-permute-start.13 = (f32[32,256]{1,0:T(8,128)S(1)}, f32[32,256]{1,0:T(8,128)S(1)}, u32[]{:S(2)}, u32[]{:S(2)}) collective-permute-start(f32[32,256]{1,0:T(8,128)S(1)} %pad_maximum_fusion), channel_id=1, source_target_pairs={{0,16},{16,0},{1,17},{17,1},{2,18},{18,2},{3,19},{19,3},{4,20},{20... | collective-permute-start | bytes 98312 | tf_op jit(solution)/shard_map/ppermute | solution.py:598
  34.5 2.9 %collective-permute-done.13.refs_10_ = f32[32,256]{1,0:T(8,128)S(1)} collective-permute-done((f32[32,256]{1,0:T(8,128)S(1)}, f32[32,256]{1,0:T(8,128)S(1)}, u32[]{:S(2)}, u32[]{:S(2)}) %collective-permute-start.13) | collective-permute-done | bytes 32800 | tf_op jit(solution)/shard_map/ppermute | solution.py:598
  37.4 1.3 %collective-permute-start.14 = (bf16[2,832,128]{2,1,0:T(8,128)(2,1)S(1)}, bf16[2,832,128]{2,1,0:T(8,128)(2,1)S(1)}, u32[]{:S(2)}, u32[]{:S(2)}) collective-permute-start(bf16[2,832,128]{2,1,0:T(8,128)(2,1)S(1)} %stack.2.rest_5_), channel_id=1, source_target_pairs={{0,16},{8,24},{16,0},{24,8},{1,17},{9,25},{17,1},{25,9},{2,18},{10... | collective-permute-start | bytes 1277960 | tf_op jit(solution)/shard_map/ppermute | solution.py:620
  38.7 3.6 %gradients.1 = bf16[832,128]{1,0:T(8,128)(2,1)S(1)} custom-call(bf16[560,128]{1,0:T(8,128)(2,1)S(1)} %collective-permute-done.3.refs_0_, bf16[560,128]{1,0:T(8,128)(2,1)S(1)} %collective-permute-done.4.refs_1_, bf16[560,128]{1,0:T(8,128)(2,1)S(1)} %collective-permute-done.5.refs_2_, bf16[560,128]{1,0:T(8,128)(2,1)S(1)} %collective-permute-done.6.refs_3_, ...), custom_call_target="tpu_custom_call" | custom-call | flops 1 | bytes 1024 | tf_op jit(solution)/shard_map/gradients/pallas_call | solution.py:623
  42.2 0.7 %collective-permute-start.15 = (bf16[2,832,128]{2,1,0:T(8,128)(2,1)S(1)}, bf16[2,832,128]{2,1,0:T(8,128)(2,1)S(1)}, u32[]{:S(2)}, u32[]{:S(2)}) collective-permute-start(bf16[2,832,128]{2,1,0:T(8,128)(2,1)S(1)} %stack.2.rest_5_), channel_id=1, source_target_pairs={{0,24},{8,16},{16,8},{24,0},{1,25},{9,17},{17,9},{25,1},{2,26},{10... | collective-permute-start | bytes 1277960 | tf_op jit(solution)/shard_map/ppermute | solution.py:639
  43.0 0.0 collective-permute-done.16.rest_8_.rest_10_
  43.0 18.3 %all-gather = bf16[3328,128]{1,0:T(8,128)(2,1)S(1)} all-gather(bf16[832,128]{1,0:T(8,128)(2,1)S(1)} %gradients.1), channel_id=2, replica_groups=mesh['half0'=2,'half1'=2,'core'=2,'tp'=4] {'tp'}, dimensions={0}, use_global_device_ids=true | all-gather | bytes 1064960 | tf_op jit(solution)/shard_map/all_gather | solution.py:641
  61.3 0.0 collective-permute-done.14.rest_7_.rest_5_
  61.3 0.0 collective-permute-done.15.rest_8_.rest_6_
  61.3 0.0 collective-permute-done.12.rest_6_
  61.3 0.1 collective-permute-start.17
  61.4 0.2 cat.2
  61.6 0.7 columns.3.refs_0_
  62.3 1.5 %collective-permute-done.17.grad_ref = bf16[4,832,128]{2,1,0:T(8,128)(2,1)S(1)} collective-permute-done((bf16[4,832,128]{2,1,0:T(8,128)(2,1)S(1)}, bf16[4,832,128]{2,1,0:T(8,128)(2,1)S(1)}, u32[]{:S(2)}, u32[]{:S(2)}) %collective-permute-start.17) | collective-permute-done | bytes 852000 | tf_op jit(solution)/shard_map/ppermute | solution.py:643
  63.8 0.2 cat.3
  64.0 1.1 %columns.4 = bf16[4,256,256]{2,1,0:T(8,128)(2,1)S(1)} custom-call(bf16[256,1536]{1,0:T(8,128)(2,1)S(1)} %get-tuple-element.109.rest_0_, bf16[256,128]{1,0:T(8,128)(2,1)S(1)} %get-tuple-element.110.rest_1_, bf16[2048,256]{1,0:T(8,128)(2,1)S(1)} %get-tuple-element.100.rest_2_, bf16[2048,128]{1,0:T(8,128)(2,1)S(1)} %get-tuple-element.101.rest_3_, ...), custom_call_target="tpu_custom_call" | custom-call | flops 1 | bytes 1024 | tf_op jit(solution)/shard_map/columns/pallas_call | solution.py:663
  65.1 0.2 collective-permute-start.18
  65.3 0.6 columns.5.refs_1_
  65.9 1.1 %collective-permute-done.18.refs_2_ = bf16[4,256,256]{2,1,0:T(8,128)(2,1)S(1)} collective-permute-done((bf16[4,256,256]{2,1,0:T(8,128)(2,1)S(1)}, bf16[4,256,256]{2,1,0:T(8,128)(2,1)S(1)}, u32[]{:S(2)}, u32[]{:S(2)}) %collective-permute-start.18) | collective-permute-done | bytes 524320 | tf_op jit(solution)/shard_map/ppermute | solution.py:677
  67.1 1.0 %lay.1 = bf16[256,2048]{1,0:T(8,128)(2,1)} custom-call(bf16[2,256,256]{2,1,0:T(8,128)(2,1)S(1)} %columns.3.refs_0_, bf16[2,256,256]{2,1,0:T(8,128)(2,1)S(1)} %columns.5.refs_1_, bf16[4,256,256]{2,1,0:T(8,128)(2,1)S(1)} %collective-permute-done.18.refs_2_), custom_call_target="tpu_custom_call" | custom-call | flops 1 | bytes 1024 | tf_op jit(solution)/shard_map/lay/pallas_call | solution.py:680
  (4 shorter events, 0.1 us)
Async XLA Ops:
  3.7 14.0 %collective-permute-start = (bf16[832,128]{1,0:T(8,128)(2,1)S(1)}, bf16[832,128]{1,0:T(8,128)(2,1)S(1)}, u32[]{:S(2)}, u32[]{:S(2)}) collective-permute-start(bf16[832,128]{1,0:T(8,128)(2,1)S(1)} %get-tuple-element.60), channel_id=1, source_target_pairs={{0,2},{1,3},{2,0},{3,1},{4,6},{5,7},{6,4},{7,5},{8,10},{9,11},{10,... | collective-permute-start | bytes 638984 | tf_op jit(solution)/shard_map/ppermute | solution.py:561
  7.8 7.6 %collective-permute-start.1 = (bf16[560,128]{1,0:T(8,128)(2,1)S(1)}, bf16[560,128]{1,0:T(8,128)(2,1)S(1)}, u32[]{:S(2)}, u32[]{:S(2)}) collective-permute-start(bf16[560,128]{1,0:T(8,128)(2,1)S(1)} %get-tuple-element.61), channel_id=1, source_target_pairs={{0,24},{8,16},{16,8},{24,0},{1,25},{9,17},{17,9},{25,1},{2,26},{10... | collective-permute-start | bytes 430088 | tf_op jit(solution)/shard_map/ppermute | solution.py:558
  10.3 6.8 %collective-permute-start.4 = (bf16[560,128]{1,0:T(8,128)(2,1)S(1)}, bf16[560,128]{1,0:T(8,128)(2,1)S(1)}, u32[]{:S(2)}, u32[]{:S(2)}) collective-permute-start(bf16[560,128]{1,0:T(8,128)(2,1)S(1)} %get-tuple-element.64), channel_id=1, source_target_pairs={{0,8},{8,0},{16,24},{24,16},{1,9},{9,1},{17,25},{25,17},{2,10},{10... | collective-permute-start | bytes 430088 | tf_op jit(solution)/shard_map/ppermute | solution.py:558
  10.8 6.3 %collective-permute-start.6 = (bf16[560,128]{1,0:T(8,128)(2,1)S(1)}, bf16[560,128]{1,0:T(8,128)(2,1)S(1)}, u32[]{:S(2)}, u32[]{:S(2)}) collective-permute-start(bf16[560,128]{1,0:T(8,128)(2,1)S(1)} %get-tuple-element.65), channel_id=1, source_target_pairs={{0,16},{8,24},{16,0},{24,8},{1,17},{9,25},{17,1},{25,9},{2,18},{10... | collective-permute-start | bytes 430088 | tf_op jit(solution)/shard_map/ppermute | solution.py:558
  11.3 9.3 %collective-permute-start.2 = (bf16[832,128]{1,0:T(8,128)(2,1)S(1)}, bf16[832,128]{1,0:T(8,128)(2,1)S(1)}, u32[]{:S(2)}, u32[]{:S(2)}) collective-permute-start(bf16[832,128]{1,0:T(8,128)(2,1)S(1)} %get-tuple-element.60), channel_id=1, source_target_pairs={{0,1},{1,0},{2,3},{3,2},{4,5},{5,4},{6,7},{7,6},{8,9},{9,8},{10,11... | collective-permute-start | bytes 638984 | tf_op jit(solution)/shard_map/ppermute | solution.py:571
  15.4 2.4 %collective-permute-start.3 = (bf16[560,128]{1,0:T(8,128)(2,1)S(1)}, bf16[560,128]{1,0:T(8,128)(2,1)S(1)}, u32[]{:S(2)}, u32[]{:S(2)}) collective-permute-start(bf16[560,128]{1,0:T(8,128)(2,1)S(1)} %get-tuple-element.63), channel_id=1, source_target_pairs={{0,4},{4,0},{1,5},{5,1},{2,6},{6,2},{3,7},{7,3},{8,12},{12,8},{9,1... | collective-permute-start | bytes 430088 | tf_op jit(solution)/shard_map/ppermute | solution.py:559
  17.1 3.5 %collective-permute-start.5 = (bf16[560,128]{1,0:T(8,128)(2,1)S(1)}, bf16[560,128]{1,0:T(8,128)(2,1)S(1)}, u32[]{:S(2)}, u32[]{:S(2)}) collective-permute-start(bf16[560,128]{1,0:T(8,128)(2,1)S(1)} %collective-permute-done.4.refs_1_), channel_id=1, source_target_pairs={{0,4},{4,0},{1,5},{5,1},{2,6},{6,2},{3,7},{7,3},{8,12},{12,8},{9,1... | collective-permute-start | bytes 430088 | tf_op jit(solution)/shard_map/ppermute | solution.py:565
  17.1 3.5 %collective-permute-start.7 = (bf16[560,128]{1,0:T(8,128)(2,1)S(1)}, bf16[560,128]{1,0:T(8,128)(2,1)S(1)}, u32[]{:S(2)}, u32[]{:S(2)}) collective-permute-start(bf16[560,128]{1,0:T(8,128)(2,1)S(1)} %collective-permute-done.6.refs_3_), channel_id=1, source_target_pairs={{0,4},{4,0},{1,5},{5,1},{2,6},{6,2},{3,7},{7,3},{8,12},{12,8},{9,1... | collective-permute-start | bytes 430088 | tf_op jit(solution)/shard_map/ppermute | solution.py:565
  17.8 2.8 %collective-permute-start.8 = (bf16[560,128]{1,0:T(8,128)(2,1)S(1)}, bf16[560,128]{1,0:T(8,128)(2,1)S(1)}, u32[]{:S(2)}, u32[]{:S(2)}) collective-permute-start(bf16[560,128]{1,0:T(8,128)(2,1)S(1)} %collective-permute-done.1.refs_5_), channel_id=1, source_target_pairs={{0,4},{4,0},{1,5},{5,1},{2,6},{6,2},{3,7},{7,3},{8,12},{12,8},{9,1... | collective-permute-start | bytes 430088 | tf_op jit(solution)/shard_map/ppermute | solution.py:565
  20.6 5.9 %collective-permute-start.9 = (bf16[832,128]{1,0:T(8,128)(2,1)S(1)}, bf16[832,128]{1,0:T(8,128)(2,1)S(1)}, u32[]{:S(2)}, u32[]{:S(2)}) collective-permute-start(bf16[832,128]{1,0:T(8,128)(2,1)S(1)} %collective-permute-done.refs_0_), channel_id=1, source_target_pairs={{0,1},{1,0},{2,3},{3,2},{4,5},{5,4},{6,7},{7,6},{8,9},{9,8},{10,11... | collective-permute-start | bytes 638984 | tf_op jit(solution)/shard_map/ppermute | solution.py:573
  23.1 1.2 %collective-permute-start.10 = (f32[8,256]{1,0:T(8,128)S(1)}, f32[8,256]{1,0:T(8,128)S(1)}, u32[]{:S(2)}, u32[]{:S(2)}) collective-permute-start(f32[8,256]{1,0:T(8,128)S(1)} %get-tuple-element.87.refs_7_), channel_id=1, source_target_pairs={{0,4},{4,0},{1,5},{5,1},{2,6},{6,2},{3,7},{7,3},{8,12},{12,8},{9,1... | collective-permute-start | bytes 24584 | tf_op jit(solution)/shard_map/ppermute | solution.py:598
  26.5 16.4 %collective-permute-start.16 = (bf16[2,832,128]{2,1,0:T(8,128)(2,1)S(1)}, bf16[2,832,128]{2,1,0:T(8,128)(2,1)S(1)}, u32[]{:S(2)}, u32[]{:S(2)}) collective-permute-start(bf16[2,832,128]{2,1,0:T(8,128)(2,1)S(1)} %get-tuple-element.93), channel_id=1, source_target_pairs={{0,1},{1,0},{2,3},{3,2},{4,5},{5,4},{6,7},{7,6},{8,9},{9,8},{10,11... | collective-permute-start | bytes 1277960 | tf_op jit(solution)/shard_map/ppermute | solution.py:603
  27.9 3.7 %collective-permute-start.11 = (f32[16,256]{1,0:T(8,128)S(1)}, f32[16,256]{1,0:T(8,128)S(1)}, u32[]{:S(2)}, u32[]{:S(2)}) collective-permute-start(f32[16,256]{1,0:T(8,128)S(1)} %pad_maximum_fusion.1), channel_id=1, source_target_pairs={{0,8},{8,0},{1,9},{9,1},{2,10},{10,2},{3,11},{11,3},{4,12},{12,4},... | collective-permute-start | bytes 49160 | tf_op jit(solution)/shard_map/ppermute | solution.py:598
  31.7 29.6 %collective-permute-start.12 = (bf16[3,832,128]{2,1,0:T(8,128)(2,1)S(1)}, bf16[3,832,128]{2,1,0:T(8,128)(2,1)S(1)}, u32[]{:S(2)}, u32[]{:S(2)}) collective-permute-start(bf16[3,832,128]{2,1,0:T(8,128)(2,1)S(1)} %stack.3), channel_id=1, source_target_pairs={{0,8},{8,0},{16,24},{24,16},{1,9},{9,1},{17,25},{25,17},{2,10},{10... | collective-permute-start | bytes 1916936 | tf_op jit(solution)/shard_map/ppermute | solution.py:620
  33.2 4.2 %collective-permute-start.13 = (f32[32,256]{1,0:T(8,128)S(1)}, f32[32,256]{1,0:T(8,128)S(1)}, u32[]{:S(2)}, u32[]{:S(2)}) collective-permute-start(f32[32,256]{1,0:T(8,128)S(1)} %pad_maximum_fusion), channel_id=1, source_target_pairs={{0,16},{16,0},{1,17},{17,1},{2,18},{18,2},{3,19},{19,3},{4,20},{20... | collective-permute-start | bytes 98312 | tf_op jit(solution)/shard_map/ppermute | solution.py:598
  37.4 23.9 %collective-permute-start.14 = (bf16[2,832,128]{2,1,0:T(8,128)(2,1)S(1)}, bf16[2,832,128]{2,1,0:T(8,128)(2,1)S(1)}, u32[]{:S(2)}, u32[]{:S(2)}) collective-permute-start(bf16[2,832,128]{2,1,0:T(8,128)(2,1)S(1)} %stack.2.rest_5_), channel_id=1, source_target_pairs={{0,16},{8,24},{16,0},{24,8},{1,17},{9,25},{17,1},{25,9},{2,18},{10... | collective-permute-start | bytes 1277960 | tf_op jit(solution)/shard_map/ppermute | solution.py:620
  42.2 19.1 %collective-permute-start.15 = (bf16[2,832,128]{2,1,0:T(8,128)(2,1)S(1)}, bf16[2,832,128]{2,1,0:T(8,128)(2,1)S(1)}, u32[]{:S(2)}, u32[]{:S(2)}) collective-permute-start(bf16[2,832,128]{2,1,0:T(8,128)(2,1)S(1)} %stack.2.rest_5_), channel_id=1, source_target_pairs={{0,24},{8,16},{16,8},{24,0},{1,25},{9,17},{17,9},{25,1},{2,26},{10... | collective-permute-start | bytes 1277960 | tf_op jit(solution)/shard_map/ppermute | solution.py:639
  61.3 2.4 %collective-permute-start.17 = (bf16[4,832,128]{2,1,0:T(8,128)(2,1)S(1)}, bf16[4,832,128]{2,1,0:T(8,128)(2,1)S(1)}, u32[]{:S(2)}, u32[]{:S(2)}) collective-permute-start(bf16[4,832,128]{2,1,0:T(8,128)(2,1)S(1)} %bitcast.3), channel_id=1, source_target_pairs={{0,4},{4,0},{1,5},{5,1},{2,6},{6,2},{3,7},{7,3},{8,12},{12,8},{9,1... | collective-permute-start | bytes 2555912 | tf_op jit(solution)/shard_map/ppermute | solution.py:643
  65.1 2.0 %collective-permute-start.18 = (bf16[4,256,256]{2,1,0:T(8,128)(2,1)S(1)}, bf16[4,256,256]{2,1,0:T(8,128)(2,1)S(1)}, u32[]{:S(2)}, u32[]{:S(2)}) collective-permute-start(bf16[4,256,256]{2,1,0:T(8,128)(2,1)S(1)} %columns.4), channel_id=1, source_target_pairs={{0,4},{4,0},{1,5},{5,1},{2,6},{6,2},{3,7},{7,3},{8,12},{12,8},{9,1... | collective-permute-start | bytes 1572872 | tf_op jit(solution)/shard_map/ppermute | solution.py:677

commit v26 on v25

--- a/solution.py
+++ b/solution.py
@@ -443,9 +443,9 @@
 
 
 def lay_kernel(ctx, *refs):
-    *tiles, received_ref, out_ref, sems = refs
-    views = [(ref.at[n], 2 * (2 * m + n)) for m, ref in enumerate(tiles) for n in range(2)]
-    views += [(received_ref.at[d], 2 * d + 1) for d in range(received_ref.shape[0])]
+    own_ref, *received, out_ref, sems = refs
+    views = [(own_ref.at[n], 2 * n) for n in range(own_ref.shape[0])]
+    views += [(ref.at[n], 4 * m + 2 * n + 1) for m, ref in enumerate(received) for n in range(2)]
     copies = []
     for n, (view, e) in enumerate(views):
         tile = view.shape[1]
@@ -670,13 +670,14 @@
             name="columns",
         )(*operands, ww, vw, fw, *parts, *first)
 
-    early_tiles = columns_of((0, 2), mine)
-    sibling_grads, early_tiles = lax.optimization_barrier((sibling_grads, early_tiles))
-    passed = columns_of((0, 2, 4, 6), operands_of(sibling_grads))
-    passed, mine = lax.optimization_barrier((passed, mine))
-    received = lax.ppermute(passed, "core", swap)
-    late_tiles = columns_of((4, 6), mine)
-    late_tiles, received = lax.optimization_barrier((late_tiles, received))
+    own_tiles = columns_of((0, 2, 4, 6), mine)
+    sibling_grads, own_tiles = lax.optimization_barrier((sibling_grads, own_tiles))
+    sibling = operands_of(sibling_grads)
+    received = []
+    for distances in ((0, 2), (4, 6)):
+        passed = columns_of(distances, sibling)
+        passed, sibling = lax.optimization_barrier((passed, sibling))
+        received.append(lax.ppermute(passed, "core", swap))
     total = pl.pallas_call(
         partial(lay_kernel, ctx),
         out_shape=jax.ShapeDtypeStruct((rows, dim), bf16),
@@ -686,7 +687,7 @@
         compiler_params=params,
         cost_estimate=cost(1, 1024),
         name="lay",
-    )(early_tiles, late_tiles, received)
+    )(own_tiles, *received)
     return (attended, total)
 
 

time: 68.3 us -> 67.9 us (level)
    ppermute x1 -> x2, waiting for transfers between devices: 1.13 us -> 1.4 us  [per_device(): received.append(lax.ppermute(passed, 'core', swap))]
  transfers between devices with their start and end apart: 19 -> 20, of which waited for: 10 -> 11; matrix products, arithmetic and copies ran while one was open for 0% -> 0% of each run, Pallas kernels for 11% -> 11%
where the time goes in v26:
time: 67.9 us; the launch traced here: 67.8 us
  starting transfers between devices  18.1 us (27%)
  blocking collectives  18.1 us (27%)
  waiting for transfers between devices  17.9 us (26%)
  Pallas kernels  13 us (19%)
  between operations  0.71 us (1%)
    all_gather x1, blocking collectives, per_device(): grads = lax.all_gather(grads, 'tp')  18.1 us
    ppermute x3, waiting for transfers between devices, per_device(): stats.append(lax.ppermute(held, name, swap))  5.98 us
    ppermute x3, waiting for transfers between devices, per_device(): lax.ppermute(sends[d], ctx[:-1], [(i, i ^ d) for i in range(chips)])  4.2 us
    ppermute x1, starting transfers between devices, per_device(): across = lax.ppermute(outs[0], 'tp', [(z, z ^ 2) for z in range(heads)])  4.1 us
    pallas_call x1, Pallas kernels, per_device(): pl.pallas_call(lambda *refs: gradient_kernel(ctx, count, len(recv), len(s...  3.56 us
    ppermute x3, starting transfers between devices, per_device(): lax.ppermute(sends[d], ctx[:-1], [(i, i ^ d) for i in range(chips)])  3.49 us
    pallas_call x1, Pallas kernels, per_device(): pl.pallas_call(partial(project_kernel, ctx, len(packs)), out_shape=packs...  3.1 us
    ppermute x1, waiting for transfers between devices, per_device(): early = lax.ppermute(outs[0], 'tp', [(z, z ^ 1) for z in range(heads)])  2.83 us
  transfers between devices with their start and end apart: 20, of which 11 were waited for; matrix products, arithmetic and copies ran while one was open for 0% of the time, Pallas kernels for 11%

profile of v26, /device:TPU:0, one launch (start us, length us, event | category | flops | bytes accessed | tf_op | source)
XLA Modules:
  0.0 67.8 jit_solution(9088899644935417071)
XLA Ops:
  0.6 3.1 %project.1 = (bf16[832,128]{1,0:T(8,128)(2,1)S(1)}, bf16[2,832,128]{2,1,0:T(8,128)(2,1)S(1)}, bf16[560,128]{1,0:T(8,128)(2,1)S(1)}, bf16[560,128]{1,0:T(8,128)(2...) custom-call(bf16[256,2048]{1,0:T(8,128)(2,1)} %tok_hbm.1, ...), custom_call_target="tpu_custom_call" | custom-call | flops 1 | bytes 1024 | tf_op jit(solution)/shard_map/project/pallas_call | solution.py:529
  3.7 4.1 %collective-permute-start = (bf16[832,128]{1,0:T(8,128)(2,1)S(1)}, bf16[832,128]{1,0:T(8,128)(2,1)S(1)}, u32[]{:S(2)}, u32[]{:S(2)}) collective-permute-start(bf16[832,128]{1,0:T(8,128)(2,1)S(1)} %get-tuple-element.59), channel_id=1, source_target_pairs={{0,2},{1,3},{2,0},{3,1},{4,6},{5,7},{6,4},{7,5},{8,10},{9,11},{10,... | collective-permute-start | bytes 638984 | tf_op jit(solution)/shard_map/ppermute | solution.py:561
  7.8 2.4 %collective-permute-start.1 = (bf16[560,128]{1,0:T(8,128)(2,1)S(1)}, bf16[560,128]{1,0:T(8,128)(2,1)S(1)}, u32[]{:S(2)}, u32[]{:S(2)}) collective-permute-start(bf16[560,128]{1,0:T(8,128)(2,1)S(1)} %get-tuple-element.60), channel_id=1, source_target_pairs={{0,24},{8,16},{16,8},{24,0},{1,25},{9,17},{17,9},{25,1},{2,26},{10... | collective-permute-start | bytes 430088 | tf_op jit(solution)/shard_map/ppermute | solution.py:558
  10.3 0.5 collective-permute-start.4
  10.8 0.5 collective-permute-start.6
  11.3 1.6 %collective-permute-start.2 = (bf16[832,128]{1,0:T(8,128)(2,1)S(1)}, bf16[832,128]{1,0:T(8,128)(2,1)S(1)}, u32[]{:S(2)}, u32[]{:S(2)}) collective-permute-start(bf16[832,128]{1,0:T(8,128)(2,1)S(1)} %get-tuple-element.59), channel_id=1, source_target_pairs={{0,1},{1,0},{2,3},{3,2},{4,5},{5,4},{6,7},{7,6},{8,9},{9,8},{10,11... | collective-permute-start | bytes 638984 | tf_op jit(solution)/shard_map/ppermute | solution.py:571
  12.9 2.5 %collective-permute-done.1.refs_5_ = bf16[560,128]{1,0:T(8,128)(2,1)S(1)} collective-permute-done((bf16[560,128]{1,0:T(8,128)(2,1)S(1)}, bf16[560,128]{1,0:T(8,128)(2,1)S(1)}, u32[]{:S(2)}, u32[]{:S(2)}) %collective-permute-start.1) | collective-permute-done | bytes 143392 | tf_op jit(solution)/shard_map/ppermute | solution.py:558
  15.4 0.0 collective-permute-start.3
  15.4 1.7 %collective-permute-done.4.refs_1_ = bf16[560,128]{1,0:T(8,128)(2,1)S(1)} collective-permute-done((bf16[560,128]{1,0:T(8,128)(2,1)S(1)}, bf16[560,128]{1,0:T(8,128)(2,1)S(1)}, u32[]{:S(2)}, u32[]{:S(2)}) %collective-permute-start.4) | collective-permute-done | bytes 143392 | tf_op jit(solution)/shard_map/ppermute | solution.py:558
  17.1 0.0 collective-permute-start.5
  17.1 0.0 collective-permute-done.6.refs_3_
  17.1 0.5 collective-permute-start.7
  17.6 0.2 collective-permute-done.refs_0_
  17.8 0.0 collective-permute-start.8
  17.8 0.0 collective-permute-done.3.refs_0_
  17.8 2.8 %collective-permute-done.2.refs_2_.rest_9_.rest_7_ = bf16[832,128]{1,0:T(8,128)(2,1)S(1)} collective-permute-done((bf16[832,128]{1,0:T(8,128)(2,1)S(1)}, bf16[832,128]{1,0:T(8,128)(2,1)S(1)}, u32[]{:S(2)}, u32[]{:S(2)}) %collective-permute-start.2) | collective-permute-done | bytes 213024 | tf_op jit(solution)/shard_map/ppermute | solution.py:571
  20.6 0.0 collective-permute-done.5.refs_2_
  20.6 0.0 collective-permute-done.7.refs_4_
  20.6 0.0 collective-permute-done.8.refs_6_
  20.6 0.1 collective-permute-start.9
  20.7 2.4 %query_side.1 = (bf16[256,128]{1,0:T(8,128)(2,1)}, f32[8,256]{1,0:T(8,128)S(1)}, f32[256,128]{1,0:T(8,128)S(1)}) custom-call(bf16[560,128]{1,0:T(8,128)(2,1)S(1)} %collective-permute-done.3.refs_0_, bf16[560,128]{1,0:T(8,128)(2,1)S(1)} %collective-permute-done.4.refs_1_, bf16[560,128]{1,0:T(8,128)(2,1)S(1)} %collective-permute-done.5.refs_2_, ...), custom_call_target="tpu_custom_call" | custom-call | flops 1 | bytes 1024 | tf_op jit(solution)/shard_map/query_side/pallas_call | solution.py:575
  23.1 0.0 collective-permute-start.10
  23.1 1.2 %collective-permute-done.10.refs_8_ = f32[8,256]{1,0:T(8,128)S(1)} collective-permute-done((f32[8,256]{1,0:T(8,128)S(1)}, f32[8,256]{1,0:T(8,128)S(1)}, u32[]{:S(2)}, u32[]{:S(2)}) %collective-permute-start.10) | collective-permute-done | bytes 8224 | tf_op jit(solution)/shard_map/ppermute | solution.py:598
  24.3 2.3 %collective-permute-done.9.refs_1_ = bf16[832,128]{1,0:T(8,128)(2,1)S(1)} collective-permute-done((bf16[832,128]{1,0:T(8,128)(2,1)S(1)}, bf16[832,128]{1,0:T(8,128)(2,1)S(1)}, u32[]{:S(2)}, u32[]{:S(2)}) %collective-permute-start.9) | collective-permute-done | bytes 213024 | tf_op jit(solution)/shard_map/ppermute | solution.py:573
  26.5 1.4 %collective-permute-start.16 = (bf16[2,832,128]{2,1,0:T(8,128)(2,1)S(1)}, bf16[2,832,128]{2,1,0:T(8,128)(2,1)S(1)}, u32[]{:S(2)}, u32[]{:S(2)}) collective-permute-start(bf16[2,832,128]{2,1,0:T(8,128)(2,1)S(1)} %get-tuple-element.92), channel_id=1, source_target_pairs={{0,1},{1,0},{2,3},{3,2},{4,5},{5,4},{6,7},{7,6},{8,9},{9,8},{10,11... | collective-permute-start | bytes 1277960 | tf_op jit(solution)/shard_map/ppermute | solution.py:603
  27.9 1.5 %collective-permute-start.11 = (f32[16,256]{1,0:T(8,128)S(1)}, f32[16,256]{1,0:T(8,128)S(1)}, u32[]{:S(2)}, u32[]{:S(2)}) collective-permute-start(f32[16,256]{1,0:T(8,128)S(1)} %pad_maximum_fusion.1), channel_id=1, source_target_pairs={{0,8},{8,0},{1,9},{9,1},{2,10},{10,2},{3,11},{11,3},{4,12},{12,4},... | collective-permute-start | bytes 49160 | tf_op jit(solution)/shard_map/ppermute | solution.py:598
  29.5 2.2 %collective-permute-done.11.refs_9_ = f32[16,256]{1,0:T(8,128)S(1)} collective-permute-done((f32[16,256]{1,0:T(8,128)S(1)}, f32[16,256]{1,0:T(8,128)S(1)}, u32[]{:S(2)}, u32[]{:S(2)}) %collective-permute-start.11) | collective-permute-done | bytes 16416 | tf_op jit(solution)/shard_map/ppermute | solution.py:598
  31.7 1.5 %collective-permute-start.12 = (bf16[3,832,128]{2,1,0:T(8,128)(2,1)S(1)}, bf16[3,832,128]{2,1,0:T(8,128)(2,1)S(1)}, u32[]{:S(2)}, u32[]{:S(2)}) collective-permute-start(bf16[3,832,128]{2,1,0:T(8,128)(2,1)S(1)} %stack.3), channel_id=1, source_target_pairs={{0,8},{8,0},{16,24},{24,16},{1,9},{9,1},{17,25},{25,17},{2,10},{10... | collective-permute-start | bytes 1916936 | tf_op jit(solution)/shard_map/ppermute | solution.py:620
  33.2 1.3 %collective-permute-start.13 = (f32[32,256]{1,0:T(8,128)S(1)}, f32[32,256]{1,0:T(8,128)S(1)}, u32[]{:S(2)}, u32[]{:S(2)}) collective-permute-start(f32[32,256]{1,0:T(8,128)S(1)} %pad_maximum_fusion), channel_id=1, source_target_pairs={{0,16},{16,0},{1,17},{17,1},{2,18},{18,2},{3,19},{19,3},{4,20},{20... | collective-permute-start | bytes 98312 | tf_op jit(solution)/shard_map/ppermute | solution.py:598
  34.5 2.6 %collective-permute-done.13.refs_10_ = f32[32,256]{1,0:T(8,128)S(1)} collective-permute-done((f32[32,256]{1,0:T(8,128)S(1)}, f32[32,256]{1,0:T(8,128)S(1)}, u32[]{:S(2)}, u32[]{:S(2)}) %collective-permute-start.13) | collective-permute-done | bytes 32800 | tf_op jit(solution)/shard_map/ppermute | solution.py:598
  37.1 3.6 %gradients.1 = bf16[832,128]{1,0:T(8,128)(2,1)S(1)} custom-call(bf16[560,128]{1,0:T(8,128)(2,1)S(1)} %collective-permute-done.3.refs_0_, bf16[560,128]{1,0:T(8,128)(2,1)S(1)} %collective-permute-done.4.refs_1_, bf16[560,128]{1,0:T(8,128)(2,1)S(1)} %collective-permute-done.5.refs_2_, bf16[560,128]{1,0:T(8,128)(2,1)S(1)} %collective-permute-done.6.refs_3_, ...), custom_call_target="tpu_custom_call" | custom-call | flops 1 | bytes 1024 | tf_op jit(solution)/shard_map/gradients/pallas_call | solution.py:623
  40.7 1.3 %collective-permute-start.15 = (bf16[2,832,128]{2,1,0:T(8,128)(2,1)S(1)}, bf16[2,832,128]{2,1,0:T(8,128)(2,1)S(1)}, u32[]{:S(2)}, u32[]{:S(2)}) collective-permute-start(bf16[2,832,128]{2,1,0:T(8,128)(2,1)S(1)} %stack.2.rest_5_), channel_id=1, source_target_pairs={{0,24},{8,16},{16,8},{24,0},{1,25},{9,17},{17,9},{25,1},{2,26},{10... | collective-permute-start | bytes 1277960 | tf_op jit(solution)/shard_map/ppermute | solution.py:639
  41.9 0.8 %collective-permute-start.14 = (bf16[2,832,128]{2,1,0:T(8,128)(2,1)S(1)}, bf16[2,832,128]{2,1,0:T(8,128)(2,1)S(1)}, u32[]{:S(2)}, u32[]{:S(2)}) collective-permute-start(bf16[2,832,128]{2,1,0:T(8,128)(2,1)S(1)} %stack.2.rest_5_), channel_id=1, source_target_pairs={{0,16},{8,24},{16,0},{24,8},{1,17},{9,25},{17,1},{25,9},{2,18},{10... | collective-permute-start | bytes 1277960 | tf_op jit(solution)/shard_map/ppermute | solution.py:620
  42.7 0.0 collective-permute-done.16.rest_10_.rest_8_
  42.7 18.1 %all-gather = bf16[3328,128]{1,0:T(8,128)(2,1)S(1)} all-gather(bf16[832,128]{1,0:T(8,128)(2,1)S(1)} %gradients.1), channel_id=2, replica_groups=mesh['half0'=2,'half1'=2,'core'=2,'tp'=4] {'tp'}, dimensions={0}, use_global_device_ids=true | all-gather | bytes 1064960 | tf_op jit(solution)/shard_map/all_gather | solution.py:641
  60.8 0.0 collective-permute-done.15.rest_8_.rest_6_
  60.8 0.1 collective-permute-start.17
  60.9 0.2 cat.2
  61.1 1.1 %columns.3.refs_0_ = bf16[4,256,256]{2,1,0:T(8,128)(2,1)S(1)} custom-call(bf16[256,1536]{1,0:T(8,128)(2,1)S(1)} %get-tuple-element.97.rest_0_, bf16[256,128]{1,0:T(8,128)(2,1)S(1)} %get-tuple-element.98.rest_1_, bf16[2048,256]{1,0:T(8,128)(2,1)S(1)} %get-tuple-element.99.rest_2_, bf16[2048,128]{1,0:T(8,128)(2,1)S(1)} %get-tuple-element.100.rest_3_, ...), custom_call_target="tpu_custom_call" | custom-call | flops 1 | bytes 1024 | tf_op jit(solution)/shard_map/columns/pallas_call | solution.py:663
  62.2 1.0 %collective-permute-done.17.grad_ref = bf16[4,832,128]{2,1,0:T(8,128)(2,1)S(1)} collective-permute-done((bf16[4,832,128]{2,1,0:T(8,128)(2,1)S(1)}, bf16[4,832,128]{2,1,0:T(8,128)(2,1)S(1)}, u32[]{:S(2)}, u32[]{:S(2)}) %collective-permute-start.17) | collective-permute-done | bytes 852000 | tf_op jit(solution)/shard_map/ppermute | solution.py:643
  63.2 0.2 cat.3
  63.5 0.7 columns.4
  64.1 0.7 columns.5
  64.8 0.2 collective-permute-start.19
  65.0 0.4 collective-permute-start.18
  65.4 1.0 %collective-permute-done.19.refs_2_ = bf16[2,256,256]{2,1,0:T(8,128)(2,1)S(1)} collective-permute-done((bf16[2,256,256]{2,1,0:T(8,128)(2,1)S(1)}, bf16[2,256,256]{2,1,0:T(8,128)(2,1)S(1)}, u32[]{:S(2)}, u32[]{:S(2)}) %collective-permute-start.19) | collective-permute-done | bytes 262176 | tf_op jit(solution)/shard_map/ppermute | solution.py:680
  66.4 0.4 collective-permute-done.18.refs_1_
  66.8 1.0 %lay.1 = bf16[256,2048]{1,0:T(8,128)(2,1)} custom-call(bf16[4,256,256]{2,1,0:T(8,128)(2,1)S(1)} %columns.3.refs_0_, bf16[2,256,256]{2,1,0:T(8,128)(2,1)S(1)} %collective-permute-done.18.refs_1_, bf16[2,256,256]{2,1,0:T(8,128)(2,1)S(1)} %collective-permute-done.19.refs_2_), custom_call_target="tpu_custom_call" | custom-call | flops 1 | bytes 1024 | tf_op jit(solution)/shard_map/lay/pallas_call | solution.py:681
  (6 shorter events, 0.1 us)
Async XLA Ops:
  3.7 14.0 %collective-permute-start = (bf16[832,128]{1,0:T(8,128)(2,1)S(1)}, bf16[832,128]{1,0:T(8,128)(2,1)S(1)}, u32[]{:S(2)}, u32[]{:S(2)}) collective-permute-start(bf16[832,128]{1,0:T(8,128)(2,1)S(1)} %get-tuple-element.59), channel_id=1, source_target_pairs={{0,2},{1,3},{2,0},{3,1},{4,6},{5,7},{6,4},{7,5},{8,10},{9,11},{10,... | collective-permute-start | bytes 638984 | tf_op jit(solution)/shard_map/ppermute | solution.py:561
  7.8 7.6 %collective-permute-start.1 = (bf16[560,128]{1,0:T(8,128)(2,1)S(1)}, bf16[560,128]{1,0:T(8,128)(2,1)S(1)}, u32[]{:S(2)}, u32[]{:S(2)}) collective-permute-start(bf16[560,128]{1,0:T(8,128)(2,1)S(1)} %get-tuple-element.60), channel_id=1, source_target_pairs={{0,24},{8,16},{16,8},{24,0},{1,25},{9,17},{17,9},{25,1},{2,26},{10... | collective-permute-start | bytes 430088 | tf_op jit(solution)/shard_map/ppermute | solution.py:558
  10.3 6.8 %collective-permute-start.4 = (bf16[560,128]{1,0:T(8,128)(2,1)S(1)}, bf16[560,128]{1,0:T(8,128)(2,1)S(1)}, u32[]{:S(2)}, u32[]{:S(2)}) collective-permute-start(bf16[560,128]{1,0:T(8,128)(2,1)S(1)} %get-tuple-element.63), channel_id=1, source_target_pairs={{0,8},{8,0},{16,24},{24,16},{1,9},{9,1},{17,25},{25,17},{2,10},{10... | collective-permute-start | bytes 430088 | tf_op jit(solution)/shard_map/ppermute | solution.py:558
  10.8 6.3 %collective-permute-start.6 = (bf16[560,128]{1,0:T(8,128)(2,1)S(1)}, bf16[560,128]{1,0:T(8,128)(2,1)S(1)}, u32[]{:S(2)}, u32[]{:S(2)}) collective-permute-start(bf16[560,128]{1,0:T(8,128)(2,1)S(1)} %get-tuple-element.64), channel_id=1, source_target_pairs={{0,16},{8,24},{16,0},{24,8},{1,17},{9,25},{17,1},{25,9},{2,18},{10... | collective-permute-start | bytes 430088 | tf_op jit(solution)/shard_map/ppermute | solution.py:558
  11.3 9.3 %collective-permute-start.2 = (bf16[832,128]{1,0:T(8,128)(2,1)S(1)}, bf16[832,128]{1,0:T(8,128)(2,1)S(1)}, u32[]{:S(2)}, u32[]{:S(2)}) collective-permute-start(bf16[832,128]{1,0:T(8,128)(2,1)S(1)} %get-tuple-element.59), channel_id=1, source_target_pairs={{0,1},{1,0},{2,3},{3,2},{4,5},{5,4},{6,7},{7,6},{8,9},{9,8},{10,11... | collective-permute-start | bytes 638984 | tf_op jit(solution)/shard_map/ppermute | solution.py:571
  15.4 2.4 %collective-permute-start.3 = (bf16[560,128]{1,0:T(8,128)(2,1)S(1)}, bf16[560,128]{1,0:T(8,128)(2,1)S(1)}, u32[]{:S(2)}, u32[]{:S(2)}) collective-permute-start(bf16[560,128]{1,0:T(8,128)(2,1)S(1)} %get-tuple-element.62), channel_id=1, source_target_pairs={{0,4},{4,0},{1,5},{5,1},{2,6},{6,2},{3,7},{7,3},{8,12},{12,8},{9,1... | collective-permute-start | bytes 430088 | tf_op jit(solution)/shard_map/ppermute | solution.py:559
  17.1 3.5 %collective-permute-start.5 = (bf16[560,128]{1,0:T(8,128)(2,1)S(1)}, bf16[560,128]{1,0:T(8,128)(2,1)S(1)}, u32[]{:S(2)}, u32[]{:S(2)}) collective-permute-start(bf16[560,128]{1,0:T(8,128)(2,1)S(1)} %collective-permute-done.4.refs_1_), channel_id=1, source_target_pairs={{0,4},{4,0},{1,5},{5,1},{2,6},{6,2},{3,7},{7,3},{8,12},{12,8},{9,1... | collective-permute-start | bytes 430088 | tf_op jit(solution)/shard_map/ppermute | solution.py:565
  17.1 3.5 %collective-permute-start.7 = (bf16[560,128]{1,0:T(8,128)(2,1)S(1)}, bf16[560,128]{1,0:T(8,128)(2,1)S(1)}, u32[]{:S(2)}, u32[]{:S(2)}) collective-permute-start(bf16[560,128]{1,0:T(8,128)(2,1)S(1)} %collective-permute-done.6.refs_3_), channel_id=1, source_target_pairs={{0,4},{4,0},{1,5},{5,1},{2,6},{6,2},{3,7},{7,3},{8,12},{12,8},{9,1... | collective-permute-start | bytes 430088 | tf_op jit(solution)/shard_map/ppermute | solution.py:565
  17.8 2.8 %collective-permute-start.8 = (bf16[560,128]{1,0:T(8,128)(2,1)S(1)}, bf16[560,128]{1,0:T(8,128)(2,1)S(1)}, u32[]{:S(2)}, u32[]{:S(2)}) collective-permute-start(bf16[560,128]{1,0:T(8,128)(2,1)S(1)} %collective-permute-done.1.refs_5_), channel_id=1, source_target_pairs={{0,4},{4,0},{1,5},{5,1},{2,6},{6,2},{3,7},{7,3},{8,12},{12,8},{9,1... | collective-permute-start | bytes 430088 | tf_op jit(solution)/shard_map/ppermute | solution.py:565
  20.6 5.9 %collective-permute-start.9 = (bf16[832,128]{1,0:T(8,128)(2,1)S(1)}, bf16[832,128]{1,0:T(8,128)(2,1)S(1)}, u32[]{:S(2)}, u32[]{:S(2)}) collective-permute-start(bf16[832,128]{1,0:T(8,128)(2,1)S(1)} %collective-permute-done.refs_0_), channel_id=1, source_target_pairs={{0,1},{1,0},{2,3},{3,2},{4,5},{5,4},{6,7},{7,6},{8,9},{9,8},{10,11... | collective-permute-start | bytes 638984 | tf_op jit(solution)/shard_map/ppermute | solution.py:573
  23.1 1.2 %collective-permute-start.10 = (f32[8,256]{1,0:T(8,128)S(1)}, f32[8,256]{1,0:T(8,128)S(1)}, u32[]{:S(2)}, u32[]{:S(2)}) collective-permute-start(f32[8,256]{1,0:T(8,128)S(1)} %get-tuple-element.86.refs_7_), channel_id=1, source_target_pairs={{0,4},{4,0},{1,5},{5,1},{2,6},{6,2},{3,7},{7,3},{8,12},{12,8},{9,1... | collective-permute-start | bytes 24584 | tf_op jit(solution)/shard_map/ppermute | solution.py:598
  26.5 16.2 %collective-permute-start.16 = (bf16[2,832,128]{2,1,0:T(8,128)(2,1)S(1)}, bf16[2,832,128]{2,1,0:T(8,128)(2,1)S(1)}, u32[]{:S(2)}, u32[]{:S(2)}) collective-permute-start(bf16[2,832,128]{2,1,0:T(8,128)(2,1)S(1)} %get-tuple-element.92), channel_id=1, source_target_pairs={{0,1},{1,0},{2,3},{3,2},{4,5},{5,4},{6,7},{7,6},{8,9},{9,8},{10,11... | collective-permute-start | bytes 1277960 | tf_op jit(solution)/shard_map/ppermute | solution.py:603
  27.9 3.7 %collective-permute-start.11 = (f32[16,256]{1,0:T(8,128)S(1)}, f32[16,256]{1,0:T(8,128)S(1)}, u32[]{:S(2)}, u32[]{:S(2)}) collective-permute-start(f32[16,256]{1,0:T(8,128)S(1)} %pad_maximum_fusion.1), channel_id=1, source_target_pairs={{0,8},{8,0},{1,9},{9,1},{2,10},{10,2},{3,11},{11,3},{4,12},{12,4},... | collective-permute-start | bytes 49160 | tf_op jit(solution)/shard_map/ppermute | solution.py:598
  31.7 29.1 %collective-permute-start.12 = (bf16[3,832,128]{2,1,0:T(8,128)(2,1)S(1)}, bf16[3,832,128]{2,1,0:T(8,128)(2,1)S(1)}, u32[]{:S(2)}, u32[]{:S(2)}) collective-permute-start(bf16[3,832,128]{2,1,0:T(8,128)(2,1)S(1)} %stack.3), channel_id=1, source_target_pairs={{0,8},{8,0},{16,24},{24,16},{1,9},{9,1},{17,25},{25,17},{2,10},{10... | collective-permute-start | bytes 1916936 | tf_op jit(solution)/shard_map/ppermute | solution.py:620
  33.2 3.9 %collective-permute-start.13 = (f32[32,256]{1,0:T(8,128)S(1)}, f32[32,256]{1,0:T(8,128)S(1)}, u32[]{:S(2)}, u32[]{:S(2)}) collective-permute-start(f32[32,256]{1,0:T(8,128)S(1)} %pad_maximum_fusion), channel_id=1, source_target_pairs={{0,16},{16,0},{1,17},{17,1},{2,18},{18,2},{3,19},{19,3},{4,20},{20... | collective-permute-start | bytes 98312 | tf_op jit(solution)/shard_map/ppermute | solution.py:598
  40.7 20.1 %collective-permute-start.15 = (bf16[2,832,128]{2,1,0:T(8,128)(2,1)S(1)}, bf16[2,832,128]{2,1,0:T(8,128)(2,1)S(1)}, u32[]{:S(2)}, u32[]{:S(2)}) collective-permute-start(bf16[2,832,128]{2,1,0:T(8,128)(2,1)S(1)} %stack.2.rest_5_), channel_id=1, source_target_pairs={{0,24},{8,16},{16,8},{24,0},{1,25},{9,17},{17,9},{25,1},{2,26},{10... | collective-permute-start | bytes 1277960 | tf_op jit(solution)/shard_map/ppermute | solution.py:639
  41.9 18.9 %collective-permute-start.14 = (bf16[2,832,128]{2,1,0:T(8,128)(2,1)S(1)}, bf16[2,832,128]{2,1,0:T(8,128)(2,1)S(1)}, u32[]{:S(2)}, u32[]{:S(2)}) collective-permute-start(bf16[2,832,128]{2,1,0:T(8,128)(2,1)S(1)} %stack.2.rest_5_), channel_id=1, source_target_pairs={{0,16},{8,24},{16,0},{24,8},{1,17},{9,25},{17,1},{25,9},{2,18},{10... | collective-permute-start | bytes 1277960 | tf_op jit(solution)/shard_map/ppermute | solution.py:620
  60.8 2.4 %collective-permute-start.17 = (bf16[4,832,128]{2,1,0:T(8,128)(2,1)S(1)}, bf16[4,832,128]{2,1,0:T(8,128)(2,1)S(1)}, u32[]{:S(2)}, u32[]{:S(2)}) collective-permute-start(bf16[4,832,128]{2,1,0:T(8,128)(2,1)S(1)} %bitcast.3), channel_id=1, source_target_pairs={{0,4},{4,0},{1,5},{5,1},{2,6},{6,2},{3,7},{7,3},{8,12},{12,8},{9,1... | collective-permute-start | bytes 2555912 | tf_op jit(solution)/shard_map/ppermute | solution.py:643
  64.8 1.6 %collective-permute-start.19 = (bf16[2,256,256]{2,1,0:T(8,128)(2,1)S(1)}, bf16[2,256,256]{2,1,0:T(8,128)(2,1)S(1)}, u32[]{:S(2)}, u32[]{:S(2)}) collective-permute-start(bf16[2,256,256]{2,1,0:T(8,128)(2,1)S(1)} %columns.5), channel_id=1, source_target_pairs={{0,4},{4,0},{1,5},{5,1},{2,6},{6,2},{3,7},{7,3},{8,12},{12,8},{9,1... | collective-permute-start | bytes 786440 | tf_op jit(solution)/shard_map/ppermute | solution.py:680
  65.0 1.8 %collective-permute-start.18 = (bf16[2,256,256]{2,1,0:T(8,128)(2,1)S(1)}, bf16[2,256,256]{2,1,0:T(8,128)(2,1)S(1)}, u32[]{:S(2)}, u32[]{:S(2)}) collective-permute-start(bf16[2,256,256]{2,1,0:T(8,128)(2,1)S(1)} %columns.4), channel_id=1, source_target_pairs={{0,4},{4,0},{1,5},{5,1},{2,6},{6,2},{3,7},{7,3},{8,12},{12,8},{9,1... | collective-permute-start | bytes 786440 | tf_op jit(solution)/shard_map/ppermute | solution.py:680
